TPU v7x, 32 devices: a whole 2x2x4 slice. The times are simulated.
32 devices in a mesh: groups: 2 (over x), op: 16 (over z, y, core).
Axes of the slice: x: 2, y: 2, z: 4, core: 2. Of those that a mesh axis runs over, the one named last changes fastest.
Arguments:
- trial: bfloat16 [32, 2, 128, 128], P(('groups', 'op')), parts along dimension 0, may hold values from -8 to 8
- left_ops: bfloat16 [8192, 128, 128], P(('groups', 'op')), parts along dimension 0, may hold values from -0.03125 to 0.03125
- right_ops: bfloat16 [128, 128, 128], P(('groups', 'op')), parts along dimension 0, may hold values from -0.5 to 0.5
- task_list: int32 [8192, 4], P(('groups', 'op')), parts along dimension 0, may hold values from 0 to 63, as said below
Outputs:
- product: float32 [32, 2, 128, 128], P(('groups', 'op')), parts along dimension 0
- correlation: float32 [4, 2], P('groups'), parts along dimension 0
- projected: float32 [4, 2], P('groups'), parts along dimension 0
There are 2 independent parts, one for each index of `groups`. A program takes and returns all parts, laid end to end along the dimension named above; each array names one. Nothing has to cross between parts.
Inputs may be any that keep to these rules, and one draw needn't show every extreme that they name: `task_list`: column 0 and 1 are sectors below 16, column 2 a term below 64, column 3 is 0 or 1; the live slots of one device's 256 rows come first, and some device has all 256 slots live.
All inputs are finite; a program needn't handle non-finite values.
Results may differ from a plain program's by a relative error of at most 0.005.
Values may be sent and summed in bfloat16 or wider, within the bound.
No kernel may reach another device: no remote copies, remote signals or barrier semaphores. Data moves between devices by JAX's collectives and lax.ppermute only.
A program may use at most 128 MiB of HBM per device.

v0:
```python
import jax
import jax.numpy as jnp
from jax import lax
from jax.sharding import PartitionSpec as P


def slot_terms(task_ops, task_rows, whole_trial, whole_right):
    sources = jnp.take(whole_trial, task_rows[:, 0], axis=0)
    rights = jnp.take(whole_right, task_rows[:, 2], axis=0)
    half = jnp.einsum(
        "nab,nvbc->nvac", task_ops, sources, preferred_element_type=jnp.float32
    ).astype(jnp.bfloat16)
    return jnp.einsum("nvac,ndc->nvad", half, rights, preferred_element_type=jnp.float32)


def target_weights(task_rows, sectors):
    columns = jnp.arange(sectors, dtype=jnp.int32)
    match = (task_rows[:, 1][:, None] == columns[None, :]).astype(jnp.float32)
    return match * task_rows[:, 3][:, None].astype(jnp.float32)


def body(trial, left_ops, right_ops, task_list):
    whole_trial, whole_right = (
        lax.all_gather(trial, "op", axis=0, tiled=True),
        lax.all_gather(right_ops, "op", axis=0, tiled=True),
    )
    task_ops, task_rows = (left_ops, task_list)
    slots = task_ops.shape[0]
    sectors = whole_trial.shape[0]
    tile = min(64, slots)
    turns = slots // tile

    def accumulate(index, acc):
        ops = lax.dynamic_slice_in_dim(task_ops, index * tile, tile, 0)
        rows = lax.dynamic_slice_in_dim(task_rows, index * tile, tile, 0)
        terms = slot_terms(ops, rows, whole_trial, whole_right)
        weights = target_weights(rows, sectors)
        return acc + jnp.einsum("ns,nvad->svad", weights, terms, precision=lax.Precision.HIGHEST)

    partial_sums = lax.fori_loop(0, turns, accumulate, jnp.zeros(whole_trial.shape, jnp.float32))
    product = lax.psum_scatter(partial_sums, "op", scatter_dimension=0, tiled=True)
    own = trial.astype(jnp.float32)
    projected_terms = jnp.einsum("sibc,sjbc->ij", own, product)
    correlation_terms = jnp.einsum("sibc,sjbc->ij", own, own)
    correlation, projected = lax.psum((correlation_terms, projected_terms), "op")
    return (product, correlation, projected)


def solution(mesh):
    return jax.shard_map(
        body,
        mesh=mesh,
        in_specs=(
            P(("groups", "op"), None, None, None),
            P(("groups", "op"), None, None),
            P(("groups", "op"), None, None),
            P(("groups", "op"), None),
        ),
        out_specs=(P(("groups", "op"), None, None, None), P("groups", None), P("groups", None)),
        check_vma=False,
    )
```

profile of v0, /device:TPU:0, one launch (start us, length us, event | category | flops | bytes accessed | tf_op | source)
XLA Modules:
  0.0 307.7 jit_solution(4056680570818270990)
XLA Ops:
  7.2 0.0 all-gather.3.cloned.1.call-start
  7.2 0.7 all-gather.3.cloned.1.call-update
  7.9 0.0 all-gather.5.cloned.1.call-start
  7.9 0.7 all-gather.5.cloned.1.call-update
  8.6 0.0 reduce-scatter.2.cloned.1.call-start
  8.7 42.1 %all-gather.3.cloned.1.call-done = bf16[16,2,128,128]{3,2,1,0:T(8,128)(2,1)} async-done(((bf16[1,2,128,128]{3,2,1,0:T(8,128)(2,1)}), bf16[16,2,128,128]{3,2,1,0:T(8,128)(2,1)}) %all-gather.3.cloned.1.call-update) | async-done | bytes 1048592 | tf_op jit(solution)/shard_map/all_gather | solution.py:24
  50.8 42.5 %all-gather.5.cloned.1.call-done = bf16[64,128,128]{2,1,0:T(8,128)(2,1)} async-done(((bf16[4,128,128]{2,1,0:T(8,128)(2,1)}), bf16[64,128,128]{2,1,0:T(8,128)(2,1)}) %all-gather.5.cloned.1.call-update) | async-done | bytes 2097168 | tf_op jit(solution)/shard_map/all_gather | solution.py:25
  93.3 111.7 %while.14 = (s32[]{:T(128)}, f32[16,2,128,128]{3,0,2,1:T(8,128)}, s32[256,4]{0,1:T(4,128)}, bf16[16,2,128,128]{3,2,1,0:T(8,128)(2,1)}, bf16[256,128,128]{2,1,0:T...) while((s32[]{:T(128)}, f32[16,2,128,128]{3,0,2,1:T(8,128)}, ...), condition=%wide.region_1.0_spmd.clone, body=%wide.region_0.1_spmd.clone.sunk | while | flops 1482691840 | bytes 41957796 | solution.py:40
  93.3 0.8 constant_dynamic-slice_fusion.2
  94.1 4.3 %gather_fusion = bf16[64,2,128,128]{3,2,1,0:T(8,128)(2,1)} fusion(bf16[16,2,128,128]{3,2,1,0:T(8,128)(2,1)} %get-tuple-element.238, s32[1024]{0:T(1024)S(1)} %get-tuple-element.209), kind=kCustom, calls=%fused_computation.clone.clone.1 | custom fusion | bytes 8388864 | tf_op jit(solution)/shard_map/while/body/eval_jaxpr/jit(_take)/gather | solution.py:8
  98.4 2.5 gather_fusion.1
  101.0 6.8 %fusion.52 = f32[64,2,128,128]{3,2,1,0:T(8,128)} fusion(bf16[64,2,128,128]{3,2,1,0:T(8,128)(2,1)} %gather_fusion, pred[64]{0:T(512)(128)(4,1)S(1)} %get-tuple-element.210, bf16[64,128,128]{2,1,0:T(8,128)(2,1)S(1)} %gather_fusion.1, bf16[256,128,128]{2,1,0:T(8,128)(2,1)} %get-tuple-element.239, s32[]{:T(128)S(6)} %select_n.81, ...), kind=kOutput, calls=%fused_computation.4.clone.1 | convolution fusion | flops 1078984704 | bytes 16777348 | tf_op jit(solution)/shard_map/while/body/eval_jaxpr/nvac,ndc->nvad/dot_general | solution.py:13
  107.8 13.3 %select_add_fusion.2 = f32[16,2,128,128]{3,0,2,1:T(8,128)} fusion(f32[16,2,128,128]{3,0,2,1:T(8,128)} %get-tuple-element.226, f32[64,2,128,128]{3,2,1,0:T(8,128)} %fusion.52, pred[]{:T(512)S(6)} %compare.3, f32[64]{0:T(128)S(1)} %get-tuple-element.213, s32[64]{0:T(128)S(1)} %get-tuple-element.214), kind=kOutput, calls=%fused_computation.12.clone.1 | convolution fusion | flops 403703808 | bytes 12583425 | tf_op jit(solution)/shard_map/while/body/eval_jaxpr/ns,nvad->svad/dot_general | solution.py:38
  121.1 0.8 constant_dynamic-slice_fusion.2
  121.8 4.3 %gather_fusion = bf16[64,2,128,128]{3,2,1,0:T(8,128)(2,1)} fusion(bf16[16,2,128,128]{3,2,1,0:T(8,128)(2,1)} %get-tuple-element.238, s32[1024]{0:T(1024)S(1)} %get-tuple-element.209), kind=kCustom, calls=%fused_computation.clone.clone.1 | custom fusion | bytes 8388864 | tf_op jit(solution)/shard_map/while/body/eval_jaxpr/jit(_take)/gather | solution.py:8
  126.1 2.5 gather_fusion.1
  128.7 6.8 %fusion.52 = f32[64,2,128,128]{3,2,1,0:T(8,128)} fusion(bf16[64,2,128,128]{3,2,1,0:T(8,128)(2,1)} %gather_fusion, pred[64]{0:T(512)(128)(4,1)S(1)} %get-tuple-element.210, bf16[64,128,128]{2,1,0:T(8,128)(2,1)S(1)} %gather_fusion.1, bf16[256,128,128]{2,1,0:T(8,128)(2,1)} %get-tuple-element.239, s32[]{:T(128)S(6)} %select_n.81, ...), kind=kOutput, calls=%fused_computation.4.clone.1 | convolution fusion | flops 1078984704 | bytes 16777348 | tf_op jit(solution)/shard_map/while/body/eval_jaxpr/nvac,ndc->nvad/dot_general | solution.py:13
  135.5 13.6 %select_add_fusion.2 = f32[16,2,128,128]{3,0,2,1:T(8,128)} fusion(f32[16,2,128,128]{3,0,2,1:T(8,128)} %get-tuple-element.226, f32[64,2,128,128]{3,2,1,0:T(8,128)} %fusion.52, pred[]{:T(512)S(6)} %compare.3, f32[64]{0:T(128)S(1)} %get-tuple-element.213, s32[64]{0:T(128)S(1)} %get-tuple-element.214), kind=kOutput, calls=%fused_computation.12.clone.1 | convolution fusion | flops 403703808 | bytes 12583425 | tf_op jit(solution)/shard_map/while/body/eval_jaxpr/ns,nvad->svad/dot_general | solution.py:38
  149.1 0.8 constant_dynamic-slice_fusion.2
  149.8 4.3 %gather_fusion = bf16[64,2,128,128]{3,2,1,0:T(8,128)(2,1)} fusion(bf16[16,2,128,128]{3,2,1,0:T(8,128)(2,1)} %get-tuple-element.238, s32[1024]{0:T(1024)S(1)} %get-tuple-element.209), kind=kCustom, calls=%fused_computation.clone.clone.1 | custom fusion | bytes 8388864 | tf_op jit(solution)/shard_map/while/body/eval_jaxpr/jit(_take)/gather | solution.py:8
  154.1 2.5 gather_fusion.1
  156.7 6.8 %fusion.52 = f32[64,2,128,128]{3,2,1,0:T(8,128)} fusion(bf16[64,2,128,128]{3,2,1,0:T(8,128)(2,1)} %gather_fusion, pred[64]{0:T(512)(128)(4,1)S(1)} %get-tuple-element.210, bf16[64,128,128]{2,1,0:T(8,128)(2,1)S(1)} %gather_fusion.1, bf16[256,128,128]{2,1,0:T(8,128)(2,1)} %get-tuple-element.239, s32[]{:T(128)S(6)} %select_n.81, ...), kind=kOutput, calls=%fused_computation.4.clone.1 | convolution fusion | flops 1078984704 | bytes 16777348 | tf_op jit(solution)/shard_map/while/body/eval_jaxpr/nvac,ndc->nvad/dot_general | solution.py:13
  163.5 13.6 %select_add_fusion.2 = f32[16,2,128,128]{3,0,2,1:T(8,128)} fusion(f32[16,2,128,128]{3,0,2,1:T(8,128)} %get-tuple-element.226, f32[64,2,128,128]{3,2,1,0:T(8,128)} %fusion.52, pred[]{:T(512)S(6)} %compare.3, f32[64]{0:T(128)S(1)} %get-tuple-element.213, s32[64]{0:T(128)S(1)} %get-tuple-element.214), kind=kOutput, calls=%fused_computation.12.clone.1 | convolution fusion | flops 403703808 | bytes 12583425 | tf_op jit(solution)/shard_map/while/body/eval_jaxpr/ns,nvad->svad/dot_general | solution.py:38
  177.1 0.8 constant_dynamic-slice_fusion.2
  177.8 4.3 %gather_fusion = bf16[64,2,128,128]{3,2,1,0:T(8,128)(2,1)} fusion(bf16[16,2,128,128]{3,2,1,0:T(8,128)(2,1)} %get-tuple-element.238, s32[1024]{0:T(1024)S(1)} %get-tuple-element.209), kind=kCustom, calls=%fused_computation.clone.clone.1 | custom fusion | bytes 8388864 | tf_op jit(solution)/shard_map/while/body/eval_jaxpr/jit(_take)/gather | solution.py:8
  182.1 2.5 gather_fusion.1
  184.7 6.8 %fusion.52 = f32[64,2,128,128]{3,2,1,0:T(8,128)} fusion(bf16[64,2,128,128]{3,2,1,0:T(8,128)(2,1)} %gather_fusion, pred[64]{0:T(512)(128)(4,1)S(1)} %get-tuple-element.210, bf16[64,128,128]{2,1,0:T(8,128)(2,1)S(1)} %gather_fusion.1, bf16[256,128,128]{2,1,0:T(8,128)(2,1)} %get-tuple-element.239, s32[]{:T(128)S(6)} %select_n.81, ...), kind=kOutput, calls=%fused_computation.4.clone.1 | convolution fusion | flops 1078984704 | bytes 16777348 | tf_op jit(solution)/shard_map/while/body/eval_jaxpr/nvac,ndc->nvad/dot_general | solution.py:13
  191.5 13.6 %select_add_fusion.2 = f32[16,2,128,128]{3,0,2,1:T(8,128)} fusion(f32[16,2,128,128]{3,0,2,1:T(8,128)} %get-tuple-element.226, f32[64,2,128,128]{3,2,1,0:T(8,128)} %fusion.52, pred[]{:T(512)S(6)} %compare.3, f32[64]{0:T(128)S(1)} %get-tuple-element.213, s32[64]{0:T(128)S(1)} %get-tuple-element.214), kind=kOutput, calls=%fused_computation.12.clone.1 | convolution fusion | flops 403703808 | bytes 12583425 | tf_op jit(solution)/shard_map/while/body/eval_jaxpr/ns,nvad->svad/dot_general | solution.py:38
  205.1 3.6 %copy.13 = f32[16,2,128,128]{3,2,1,0:T(8,128)} copy(f32[16,2,128,128]{3,0,2,1:T(8,128)} %get-tuple-element.112) | data formatting | bytes 4194304 | tf_op jit(solution)/shard_map/while | solution.py:40
  208.7 0.0 copy-start
  208.7 0.0 reduce-scatter.2.cloned.1.call-update
  208.7 0.8 copy-done
  209.5 0.3 convolution_bitcast_fusion.1
  209.8 59.4 %reduce-scatter.2.cloned.1.call-done = f32[1,2,128,128]{3,2,1,0:T(8,128)} async-done(((f32[16,2,128,128]{3,2,1,0:T(8,128)}), f32[1,2,128,128]{3,2,1,0:T(8,128)}) %reduce-scatter.2.cloned.1.call-update) | async-done | bytes 131088 | tf_op jit(solution)/shard_map/reduce_scatter | solution.py:41
  269.2 1.2 convolution_bitcast_fusion
  270.4 30.1 %all-reduce = (f32[2,2]{1,0:T(2,128)}, f32[2,2]{0,1:T(2,128)S(1)}) all-reduce(f32[2,2]{1,0:T(2,128)S(1)} %convolution_bitcast_fusion.1, f32[2,2]{0,1:T(2,128)S(1)} %convolution_bitcast_fusion), channel_id=1, replica_groups=mesh['groups'=2,'op'=16] {'op'}, use_global_device_ids=true, to_apply=%region_3.4 | all-reduce | flops 8 | bytes 64 | tf_op jit(solution)/shard_map/psum | solution.py:45
  300.5 0.6 copy.18
  (13 shorter events, 0.1 us)
Async XLA Ops:
  7.2 43.7 %all-gather.3.cloned.1.call-start = ((), (), s32[]{:S(2)}) async-start(), calls=%async_computation.1 | async-start | bytes 1114112 | tf_op jit(solution)/shard_map/all_gather | solution.py:24
  7.9 85.4 %all-gather.5.cloned.1.call-start = ((), (), s32[]{:S(2)}) async-start(), calls=%async_computation.2 | async-start | bytes 2228224 | tf_op jit(solution)/shard_map/all_gather | solution.py:25
  8.6 260.5 %reduce-scatter.2.cloned.1.call-start = ((), (), s32[]{:S(2)}) async-start(), calls=%async_computation.3 | async-start | bytes 2228224 | tf_op jit(solution)/shard_map/reduce_scatter | solution.py:41
  208.7 0.8 copy-start
Sparse Core Ops, SparseCore 0:
  10.2 40.6 all-gather.2
  53.0 40.3 all-gather.4
  208.8 60.3 reduce-scatter.1
where the time goes:
time: 308 us
  waiting for transfers between devices  145 us (47%)
  matrix products  82.8 us (27%)
  local copies, waits for them, and re-layouts  35.3 us (11%)
  blocking collectives  30.1 us (10%)
  between operations  13.8 us (4%)
    reduce_scatter x1, waiting for transfers between devices, body(): lax.psum_scatter(partial_sums, 'op', scatter_dimension=0, tiled=True)  59.4 us
    dot_general x4, matrix products, accumulate(): jnp.einsum('ns,nvad->svad', weights, terms, precision=lax.Precision.HIGHEST)  54 us
    all_gather x1, waiting for transfers between devices, body(): lax.all_gather(right_ops, 'op', axis=0, tiled=True)  42.5 us
    all_gather x1, waiting for transfers between devices, body(): lax.all_gather(trial, 'op', axis=0, tiled=True)  42.1 us
    psum x1, blocking collectives, body(): lax.psum((correlation_terms, projected_terms), 'op')  30.1 us
    dot_general x4, matrix products, slot_terms(): jnp.einsum('nvac,ndc->nvad', half, rights, preferred_element_type=jnp.flo...  27.3 us
    gather x4, local copies, waits for them, and re-layouts, slot_terms(): sources = jnp.take(whole_trial, task_rows[:, 0], axis=0)  17.1 us
    gather x4, local copies, waits for them, and re-layouts, slot_terms(): rights = jnp.take(whole_right, task_rows[:, 2], axis=0)  10.2 us
  transfers between devices with their start and end apart: 3, of which 3 were waited for; matrix products, arithmetic and copies ran while one was open for 0% of the time, Pallas kernels for 0%

commit v1 on v0

v1 whole, which is shorter than its diff:
```python
import functools

import jax
import jax.numpy as jnp
from jax import lax
from jax.experimental import pallas as pl
from jax.experimental.pallas import tpu as pltpu
from jax.sharding import PartitionSpec as P

VMEM_LIMIT = 56 * 1024 * 1024
TAIL = 32
LEFT_CHUNK = 16
UNROLL = 4


def exchange(value, n, mask):
    return lax.ppermute(value, "op", [(i, i ^ mask) for i in range(n)])


def gather(block, n):
    have = {0: block}
    for r in range(4, n, 4):
        have[r] = exchange(block, n, r)
    for r in sorted(have):
        have[r ^ 2] = exchange(have[r], n, 2)
    for r in sorted(have):
        have[r ^ 1] = exchange(have[r], n, 1)
    return [have[r] for r in range(n)]


def split3(value):
    high = value.astype(jnp.bfloat16)
    rest = value - high.astype(jnp.float32)
    middle = rest.astype(jnp.bfloat16)
    low = (rest - middle.astype(jnp.float32)).astype(jnp.bfloat16)
    zero = jnp.zeros_like(value)
    return jnp.concatenate(
        [high.astype(jnp.float32), middle.astype(jnp.float32), low.astype(jnp.float32), zero], axis=0
    ).astype(jnp.bfloat16)


def join3(tail):
    wide = tail.astype(jnp.float32)
    return wide[0:8] + wide[8:16] + wide[16:24]


def matrix_of(values):
    rows = lax.broadcasted_iota(jnp.int32, (8, 128), 0)
    lanes = lax.broadcasted_iota(jnp.int32, (8, 128), 1)
    total = jnp.zeros((8, 128), jnp.float32)
    for (i, j), value in values.items():
        total = total + jnp.where((rows == i) & (lanes == j), value, 0.0)
    return total


def fold(value):
    return value.reshape(16, 8, 128).sum(axis=0)


def tasks_kernel(n, terms_per, tasks_ref, left_ref, *refs):
    blocks = refs[:n]
    send_ref, keep_ref, own_ref, corr_ref = refs[n : n + 4]
    trial, right, left, acc, block_sem, left_sem = refs[n + 4 :]
    slots = left_ref.shape[0]
    me = lax.axis_index("op")
    chunks = slots // LEFT_CHUNK

    def left_copy(chunk):
        rows = pl.ds(chunk * LEFT_CHUNK, LEFT_CHUNK)
        return pltpu.make_async_copy(left_ref.at[rows], left.at[rows], left_sem.at[chunk])

    def block_copies(r):
        owner = jnp.bitwise_xor(me, r)
        return (
            pltpu.make_async_copy(blocks[r].at[pl.ds(0, 2)], trial.at[owner], block_sem.at[r, 0]),
            pltpu.make_async_copy(
                blocks[r].at[pl.ds(2, terms_per)],
                right.at[pl.ds(owner * terms_per, terms_per)],
                block_sem.at[r, 1],
            ),
        )

    for r in range(n):
        for copy in block_copies(r):
            copy.start()
    for chunk in range(chunks):
        left_copy(chunk).start()

    def clear(s, carry):
        acc[s] = jnp.zeros((256, 128), jnp.float32)
        return carry

    lax.fori_loop(0, n + 1, clear, 0)
    for r in range(n):
        for copy in block_copies(r):
            copy.wait()

    def group(first):
        halves = []
        for u in range(UNROLL):
            slot = first + u
            source = tasks_ref[0, slot]
            vectors = jnp.concatenate([trial[source, 0], trial[source, 1]], axis=1)
            half = jnp.dot(left[slot], vectors, preferred_element_type=jnp.float32)
            halves.append(half.astype(jnp.bfloat16))
        for u in range(UNROLL):
            slot = first + u
            half = jnp.concatenate([halves[u][:, :128], halves[u][:, 128:]], axis=0)
            term = lax.dot_general(
                half, right[tasks_ref[2, slot]], (((1,), (1,)), ((), ())), preferred_element_type=jnp.float32
            )
            target = jnp.where(tasks_ref[3, slot] > 0, tasks_ref[1, slot], n)
            acc[target] = acc[target] + term

    def chunk_step(chunk, carry):
        left_copy(chunk).wait()
        for part in range(LEFT_CHUNK // UNROLL):
            first = chunk * LEFT_CHUNK + part * UNROLL

            @pl.when(tasks_ref[3, first] > 0)
            def _():
                group(first)

        return carry

    lax.fori_loop(0, chunks, chunk_step, 0)

    def dots(s, carry):
        c00, c01, c11, p00, p01, p10, p11 = carry
        t0 = trial[s, 0].astype(jnp.float32)
        t1 = trial[s, 1].astype(jnp.float32)
        a0 = acc[s, 0:128, :]
        a1 = acc[s, 128:256, :]
        return (
            c00 + fold(t0 * t0),
            c01 + fold(t0 * t1),
            c11 + fold(t1 * t1),
            p00 + fold(t0 * a0),
            p01 + fold(t0 * a1),
            p10 + fold(t1 * a0),
            p11 + fold(t1 * a1),
        )

    zero = jnp.zeros((8, 128), jnp.float32)
    c00, c01, c11, p00, p01, p10, p11 = [jnp.sum(x) for x in lax.fori_loop(0, n, dots, (zero,) * 7)]
    corr_ref[...] = matrix_of({(0, 0): c00, (0, 1): c01, (1, 0): c01, (1, 1): c11})[0:2, 0:2]
    own = matrix_of({(0, 0): p00, (0, 1): p01, (1, 0): p10, (1, 1): p11})
    own_ref[...] = own

    def pack(j, carry):
        mine = jnp.bitwise_xor(me, 2 * j)
        keep_ref[j] = acc[mine]
        send_ref[pl.ds(pl.multiple_of(j * 256, 256), 256), :] = acc[jnp.bitwise_xor(mine, 1)].astype(jnp.bfloat16)
        return carry

    lax.fori_loop(0, n // 2, pack, 0)
    send_ref[n // 2 * 256 :, :] = split3(own)


def run_tasks(tasks, left_ops, blocks):
    n = len(blocks)
    terms_per = blocks[0].shape[0] - 2
    slots = left_ops.shape[0]
    return pl.pallas_call(
        functools.partial(tasks_kernel, n, terms_per),
        out_shape=(
            jax.ShapeDtypeStruct((n // 2 * 256 + TAIL, 128), jnp.bfloat16),
            jax.ShapeDtypeStruct((n // 2, 256, 128), jnp.float32),
            jax.ShapeDtypeStruct((8, 128), jnp.float32),
            jax.ShapeDtypeStruct((2, 2), jnp.float32),
        ),
        in_specs=[pl.BlockSpec(memory_space=pltpu.SMEM)] + [pl.BlockSpec(memory_space=pl.ANY)] * (1 + n),
        scratch_shapes=[
            pltpu.VMEM((n, 2, 128, 128), jnp.bfloat16),
            pltpu.VMEM((n * terms_per, 128, 128), jnp.bfloat16),
            pltpu.VMEM((slots, 128, 128), jnp.bfloat16),
            pltpu.VMEM((n + 1, 256, 128), jnp.float32),
            pltpu.SemaphoreType.DMA((n, 2)),
            pltpu.SemaphoreType.DMA((slots // LEFT_CHUNK,)),
        ],
        compiler_params=pltpu.CompilerParams(vmem_limit_bytes=VMEM_LIMIT),
        cost_estimate=pl.CostEstimate(
            flops=slots * 8 * 128**3, bytes_accessed=slots * 32768 + n * 200000, transcendentals=0
        ),
    )(tasks, left_ops, *blocks)


def chip_kernel(chips, keep_ref, own_ref, received_ref, mine_ref, total_ref, *sends):
    total = own_ref[...] + join3(received_ref[chips * 256 :, :])
    total_ref[...] = total
    tail = split3(total)
    for j in range(chips):
        value = keep_ref[j] + received_ref[j * 256 : (j + 1) * 256, :].astype(jnp.float32)
        if j == 0:
            mine_ref[...] = value
        else:
            sends[j - 1][0:256, :] = value.astype(jnp.bfloat16)
            sends[j - 1][256:, :] = tail


def add_chip(keep, own, received):
    chips = keep.shape[0]
    return pl.pallas_call(
        functools.partial(chip_kernel, chips),
        out_shape=(jax.ShapeDtypeStruct((256, 128), jnp.float32), jax.ShapeDtypeStruct((8, 128), jnp.float32))
        + (jax.ShapeDtypeStruct((256 + TAIL, 128), jnp.bfloat16),) * (chips - 1),
        compiler_params=pltpu.CompilerParams(vmem_limit_bytes=VMEM_LIMIT),
    )(keep, own, received)


def last_kernel(mine_ref, total_ref, *refs):
    received, (product_ref, projected_ref) = refs[:-2], refs[-2:]
    value, total = mine_ref[...], total_ref[...]
    for ref in received:
        value = value + ref[0:256, :].astype(jnp.float32)
        total = total + join3(ref[256:, :])
    product_ref[0, 0] = value[0:128]
    product_ref[0, 1] = value[128:256]
    projected_ref[...] = total[0:2, 0:2]


def add_all(mine, total, received):
    return pl.pallas_call(
        last_kernel,
        out_shape=(
            jax.ShapeDtypeStruct((1, 2, 128, 128), jnp.float32),
            jax.ShapeDtypeStruct((2, 2), jnp.float32),
        ),
        compiler_params=pltpu.CompilerParams(vmem_limit_bytes=VMEM_LIMIT),
    )(mine, total, *received)


def body(n, trial, left_ops, right_ops, task_list):
    blocks = gather(jnp.concatenate([trial[0], right_ops], axis=0), n)
    send, keep, own, correlation = run_tasks(task_list.T, left_ops, blocks)
    mine, total, *sends = add_chip(keep, own, exchange(send, n, 1))
    received = [exchange(value, n, 2 * (j + 1)) for j, value in enumerate(sends)]
    product, projected = add_all(mine, total, received)
    return product, correlation, projected


def solution(mesh):
    return jax.shard_map(
        functools.partial(body, mesh.shape["op"]),
        mesh=mesh,
        in_specs=(
            P(("groups", "op"), None, None, None),
            P(("groups", "op"), None, None),
            P(("groups", "op"), None, None),
            P(("groups", "op"), None),
        ),
        out_specs=(P(("groups", "op"), None, None, None), P("groups", None), P("groups", None)),
        check_vma=False,
    )
```

time: 308 us -> 94.2 us (0.31)
  waiting for transfers between devices: 145 us -> 31.4 us
  matrix products: 82.8 us -> 0 us
  local copies, waits for them, and re-layouts: 35.3 us -> 2.03 us
  blocking collectives: 30.1 us -> 0 us
  Pallas kernels: 0 us -> 29.2 us
  starting transfers between devices: 0.11 us -> 28.9 us
  between operations: 13.8 us -> 0.92 us
    all_gather x2 -> x0, waiting for transfers between devices: 84.6 us -> none  [the longest x1 42.5 us: body(): lax.all_gather(right_ops, 'op', axis=0, tiled=True)]
    dot_general x10 -> x0, matrix products: 82.8 us -> none  [the longest x4 54 us: accumulate(): jnp.einsum('ns,nvad->svad', weights, terms, precision=lax.Precision.HIGHEST)]
    reduce_scatter x1 -> x0, waiting for transfers between devices: 59.4 us -> none  [body(): lax.psum_scatter(partial_sums, 'op', scatter_dimension=0, tiled=True)]
    ppermute x0 -> x23, waiting for transfers between devices: none -> 31.4 us  [exchange(): return lax.ppermute(value, 'op', [(i, i ^ mask) for i in range(n)])]
    psum x1 -> x0, blocking collectives: 30.1 us -> none  [body(): lax.psum((correlation_terms, projected_terms), 'op')]
    pallas_call x0 -> x3, Pallas kernels: none -> 29.2 us  [the longest x1 25.1 us: run_tasks(): pl.pallas_call(functools.partial(tasks_kernel, n, terms_per), out_shape=(...]
    ppermute x0 -> x23, starting transfers between devices: none -> 28.9 us  [exchange(): return lax.ppermute(value, 'op', [(i, i ^ mask) for i in range(n)])]
    gather x8 -> x0, local copies, waits for them, and re-layouts: 27.3 us -> none  [the longest x4 17.1 us: slot_terms(): sources = jnp.take(whole_trial, task_rows[:, 0], axis=0)]
  transfers between devices with their start and end apart: 3 -> 23, of which waited for: 3 -> 8; matrix products, arithmetic and copies ran while one was open for 0% -> 0% of each run, Pallas kernels for 0% -> 0%
where the time goes in v1:
time: 94.2 us; the launch traced here: 93.3 us
  waiting for transfers between devices  31.4 us (33%)
  Pallas kernels  29.2 us (31%)
  starting transfers between devices  28.9 us (31%)
  local copies, waits for them, and re-layouts  2.03 us (2%)
    ppermute x23, waiting for transfers between devices, exchange(): return lax.ppermute(value, 'op', [(i, i ^ mask) for i in range(n)])  31.4 us
    ppermute x23, starting transfers between devices, exchange(): return lax.ppermute(value, 'op', [(i, i ^ mask) for i in range(n)])  28.9 us
    pallas_call x1, Pallas kernels, run_tasks(): pl.pallas_call(functools.partial(tasks_kernel, n, terms_per), out_shape=(...  25.1 us
    pallas_call x1, Pallas kernels, add_chip(): pl.pallas_call(functools.partial(chip_kernel, chips), out_shape=(jax.Shap...  2.2 us
    unnamed x48, local copies, waits for them, and re-layouts  2.03 us
    pallas_call x1, Pallas kernels, add_all(): pl.pallas_call(last_kernel, out_shape=(jax.ShapeDtypeStruct((1, 2, 128, 1...  1.89 us
  transfers between devices with their start and end apart: 23, of which 8 were waited for; matrix products, arithmetic and copies ran while one was open for 0% of the time, Pallas kernels for 0%

profile of v1, /device:TPU:0, one launch (start us, length us, event | category | flops | bytes accessed | tf_op | source)
XLA Modules:
  0.0 93.3 jit_solution(2183514074274000319)
XLA Ops:
  0.6 0.9 pad_maximum_fusion.refs_0_
  1.6 0.0 copy-start.1
  1.6 5.1 %collective-permute-start.11 = (bf16[6,128,128]{2,1,0:T(8,128)(2,1)S(1)}, bf16[6,128,128]{2,1,0:T(8,128)(2,1)S(1)}, u32[]{:S(2)}, u32[]{:S(2)}) collective-permute-start(bf16[6,128,128]{2,1,0:T(8,128)(2,1)S(1)} %pad_maximum_fusion.refs_0_), channel_id=1, source_target_pairs={{0,12},{1,13},{2,14},{3,15},{4,8},{5,9},{6,10},{7,11},{8,4},{9,5},... | collective-permute-start | bytes 589832 | tf_op jit(solution)/shard_map/ppermute | solution.py:17
  6.7 0.0 collective-permute-start.7
  6.7 0.6 collective-permute-start.3
  7.3 1.7 %collective-permute-start.1 = (bf16[6,128,128]{2,1,0:T(8,128)(2,1)S(1)}, bf16[6,128,128]{2,1,0:T(8,128)(2,1)S(1)}, u32[]{:S(2)}, u32[]{:S(2)}) collective-permute-start(bf16[6,128,128]{2,1,0:T(8,128)(2,1)S(1)} %pad_maximum_fusion.refs_0_), channel_id=1, source_target_pairs={{0,2},{1,3},{2,0},{3,1},{4,6},{5,7},{6,4},{7,5},{8,10},{9,11},{10,... | collective-permute-start | bytes 589832 | tf_op jit(solution)/shard_map/ppermute | solution.py:17
  9.0 0.0 collective-permute-start
  9.0 3.6 %collective-permute-done.11.refs_12_ = bf16[6,128,128]{2,1,0:T(8,128)(2,1)S(1)} collective-permute-done((bf16[6,128,128]{2,1,0:T(8,128)(2,1)S(1)}, bf16[6,128,128]{2,1,0:T(8,128)(2,1)S(1)}, u32[]{:S(2)}, u32[]{:S(2)}) %collective-permute-start.11) | collective-permute-done | bytes 196640 | tf_op jit(solution)/shard_map/ppermute | solution.py:17
  12.6 1.7 %collective-permute-start.13 = (bf16[6,128,128]{2,1,0:T(8,128)(2,1)S(1)}, bf16[6,128,128]{2,1,0:T(8,128)(2,1)S(1)}, u32[]{:S(2)}, u32[]{:S(2)}) collective-permute-start(bf16[6,128,128]{2,1,0:T(8,128)(2,1)S(1)} %collective-permute-done.11.refs_12_), channel_id=1, source_target_pairs={{0,2},{1,3},{2,0},{3,1},{4,6},{5,7},{6,4},{7,5},{8,10},{9,11},{10,... | collective-permute-start | bytes 589832 | tf_op jit(solution)/shard_map/ppermute | solution.py:17
  14.3 9.1 %collective-permute-done.7.refs_8_ = bf16[6,128,128]{2,1,0:T(8,128)(2,1)S(1)} collective-permute-done((bf16[6,128,128]{2,1,0:T(8,128)(2,1)S(1)}, bf16[6,128,128]{2,1,0:T(8,128)(2,1)S(1)}, u32[]{:S(2)}, u32[]{:S(2)}) %collective-permute-start.7) | collective-permute-done | bytes 196640 | tf_op jit(solution)/shard_map/ppermute | solution.py:17
  23.4 0.0 collective-permute-start.12
  23.4 0.0 collective-permute-done.3.refs_4_
  23.4 0.0 copy-start.11
  23.4 1.6 %collective-permute-start.9 = (bf16[6,128,128]{2,1,0:T(8,128)(2,1)S(1)}, bf16[6,128,128]{2,1,0:T(8,128)(2,1)S(1)}, u32[]{:S(2)}, u32[]{:S(2)}) collective-permute-start(bf16[6,128,128]{2,1,0:T(8,128)(2,1)S(1)} %collective-permute-done.7.refs_8_), channel_id=1, source_target_pairs={{0,2},{1,3},{2,0},{3,1},{4,6},{5,7},{6,4},{7,5},{8,10},{9,11},{10,... | collective-permute-start | bytes 589832 | tf_op jit(solution)/shard_map/ppermute | solution.py:17
  25.0 0.0 collective-permute-done.1.refs_2_
  25.0 0.2 collective-permute-start.8
  25.2 0.0 collective-permute-done.refs_1_
  25.2 0.5 collective-permute-start.5
  25.7 0.0 collective-permute-done.13.refs_14_
  25.7 0.1 collective-permute-start.4
  25.7 0.0 collective-permute-done.12.refs_13_
  25.7 0.4 collective-permute-start.2
  26.2 5.0 %collective-permute-done.9.refs_10_ = bf16[6,128,128]{2,1,0:T(8,128)(2,1)S(1)} collective-permute-done((bf16[6,128,128]{2,1,0:T(8,128)(2,1)S(1)}, bf16[6,128,128]{2,1,0:T(8,128)(2,1)S(1)}, u32[]{:S(2)}, u32[]{:S(2)}) %collective-permute-start.9) | collective-permute-done | bytes 196640 | tf_op jit(solution)/shard_map/ppermute | solution.py:17
  31.2 0.0 collective-permute-start.14
  31.2 0.0 collective-permute-done.8.refs_9_
  31.2 0.0 copy-start.17
  31.2 0.5 collective-permute-start.10
  31.7 3.2 %collective-permute-done.5.refs_6_ = bf16[6,128,128]{2,1,0:T(8,128)(2,1)S(1)} collective-permute-done((bf16[6,128,128]{2,1,0:T(8,128)(2,1)S(1)}, bf16[6,128,128]{2,1,0:T(8,128)(2,1)S(1)}, u32[]{:S(2)}, u32[]{:S(2)}) %collective-permute-start.5) | collective-permute-done | bytes 196640 | tf_op jit(solution)/shard_map/ppermute | solution.py:17
  34.9 0.0 collective-permute-start.6
  34.9 0.0 collective-permute-done.4.refs_5_
  34.9 0.0 copy-start.19
  35.0 0.0 collective-permute-done.2.refs_3_
  35.0 0.0 copy-start.20
  35.0 0.0 collective-permute-done.14.refs_15_
  35.0 0.0 copy-start.21
  35.0 0.0 collective-permute-done.10.refs_11_
  35.0 0.0 copy-start.22
  35.0 1.4 %collective-permute-done.6.refs_7_ = bf16[6,128,128]{2,1,0:T(8,128)(2,1)S(1)} collective-permute-done((bf16[6,128,128]{2,1,0:T(8,128)(2,1)S(1)}, bf16[6,128,128]{2,1,0:T(8,128)(2,1)S(1)}, u32[]{:S(2)}, u32[]{:S(2)}) %collective-permute-start.6) | collective-permute-done | bytes 196640 | tf_op jit(solution)/shard_map/ppermute | solution.py:17
  36.4 0.0 copy-done.1
  36.4 0.0 copy-done.9
  36.4 0.0 copy-done.10
  36.5 0.6 copy-done.23
  37.1 25.1 %shard_map.67 = (bf16[2080,128]{1,0:T(8,128)(2,1)}, f32[8,256,128]{2,1,0:T(8,128)}, f32[8,128]{1,0:T(8,128)}, f32[2,2]{1,0:T(2,128)}) custom-call(s32[4,256]{1,0:T(4,128)} %bitcast.3, bf16[256,128,128]{2,1,0:T(8,128)(2,1)} %left_ref.1, bf16[6,128,128]{2,1,0:T(8,128)(2,1)} %copy-done.1, bf16[6,128,128]{2,1,0:T(8,128)(2,1)} %copy-done.13, ...), custom_call_target="tpu_custom_call" | custom-call | flops 4294967296 | bytes 11588608 | tf_op jit(solution)/shard_map/pallas_call | solution.py:164
  62.1 3.9 %collective-permute-start.15 = (bf16[2080,128]{1,0:T(8,128)(2,1)}, bf16[2080,128]{1,0:T(8,128)(2,1)S(1)}, u32[]{:S(2)}, u32[]{:S(2)}) collective-permute-start(bf16[2080,128]{1,0:T(8,128)(2,1)} %get-tuple-element.20), channel_id=1, source_target_pairs={{0,1},{1,0},{2,3},{3,2},{4,5},{5,4},{6,7},{7,6},{8,9},{9,8},{10,11... | collective-permute-start | bytes 1597448 | tf_op jit(solution)/shard_map/ppermute | solution.py:17
  66.0 1.8 %collective-permute-done.15.received_ref = bf16[2080,128]{1,0:T(8,128)(2,1)S(1)} collective-permute-done((bf16[2080,128]{1,0:T(8,128)(2,1)}, bf16[2080,128]{1,0:T(8,128)(2,1)S(1)}, u32[]{:S(2)}, u32[]{:S(2)}) %collective-permute-start.15) | collective-permute-done | bytes 532512 | tf_op jit(solution)/shard_map/ppermute | solution.py:17
  67.8 0.8 copy-done
  68.6 2.2 %shard_map.68 = (f32[256,128]{1,0:T(8,128)}, f32[8,128]{1,0:T(8,128)}, bf16[288,128]{1,0:T(8,128)(2,1)}, bf16[288,128]{1,0:T(8,128)(2,1)}, bf16[288,128]{1,0:T(8...) custom-call(f32[8,256,128]{2,1,0:T(8,128)} %get-tuple-element.18.kee, ...), custom_call_target="tpu_custom_call" | custom-call | tf_op jit(solution)/shard_map/pallas_call | solution.py:203
  70.8 2.8 %collective-permute-start.16 = (bf16[288,128]{1,0:T(8,128)(2,1)}, bf16[288,128]{1,0:T(8,128)(2,1)S(1)}, u32[]{:S(2)}, u32[]{:S(2)}) collective-permute-start(bf16[288,128]{1,0:T(8,128)(2,1)} %get-tuple-element.23), channel_id=1, source_target_pairs={{0,2},{1,3},{2,0},{3,1},{4,6},{5,7},{6,4},{7,5},{8,10},{9,11},{10,... | collective-permute-start | bytes 221192 | tf_op jit(solution)/shard_map/ppermute | solution.py:17
  73.6 1.5 %collective-permute-start.17 = (bf16[288,128]{1,0:T(8,128)(2,1)}, bf16[288,128]{1,0:T(8,128)(2,1)S(1)}, u32[]{:S(2)}, u32[]{:S(2)}) collective-permute-start(bf16[288,128]{1,0:T(8,128)(2,1)} %get-tuple-element.24), channel_id=1, source_target_pairs={{0,4},{1,5},{2,6},{3,7},{4,0},{5,1},{6,2},{7,3},{8,12},{9,13},{10,... | collective-permute-start | bytes 221192 | tf_op jit(solution)/shard_map/ppermute | solution.py:17
  75.1 0.0 collective-permute-start.18
  75.1 3.0 %collective-permute-start.19 = (bf16[288,128]{1,0:T(8,128)(2,1)}, bf16[288,128]{1,0:T(8,128)(2,1)S(1)}, u32[]{:S(2)}, u32[]{:S(2)}) collective-permute-start(bf16[288,128]{1,0:T(8,128)(2,1)} %get-tuple-element.26), channel_id=1, source_target_pairs={{0,8},{1,9},{2,10},{3,11},{4,12},{5,13},{6,14},{7,15},{8,0},{9,1},... | collective-permute-start | bytes 221192 | tf_op jit(solution)/shard_map/ppermute | solution.py:17
  78.1 1.3 %collective-permute-start.20 = (bf16[288,128]{1,0:T(8,128)(2,1)}, bf16[288,128]{1,0:T(8,128)(2,1)S(1)}, u32[]{:S(2)}, u32[]{:S(2)}) collective-permute-start(bf16[288,128]{1,0:T(8,128)(2,1)} %get-tuple-element.27), channel_id=1, source_target_pairs={{0,10},{1,11},{2,8},{3,9},{4,14},{5,15},{6,12},{7,13},{8,2},{9,3},... | collective-permute-start | bytes 221192 | tf_op jit(solution)/shard_map/ppermute | solution.py:17
  79.5 0.0 collective-permute-done.16.refs_0_
  79.5 3.9 %collective-permute-start.21 = (bf16[288,128]{1,0:T(8,128)(2,1)}, bf16[288,128]{1,0:T(8,128)(2,1)S(1)}, u32[]{:S(2)}, u32[]{:S(2)}) collective-permute-start(bf16[288,128]{1,0:T(8,128)(2,1)} %get-tuple-element.28), channel_id=1, source_target_pairs={{0,12},{1,13},{2,14},{3,15},{4,8},{5,9},{6,10},{7,11},{8,4},{9,5},... | collective-permute-start | bytes 221192 | tf_op jit(solution)/shard_map/ppermute | solution.py:17
  83.4 0.0 collective-permute-done.17.refs_1_
  83.4 0.0 collective-permute-start.22
  83.4 0.0 collective-permute-done.18.refs_2_
  83.4 0.0 copy-start.4
  83.5 0.0 collective-permute-done.19.refs_3_
  83.5 6.1 %collective-permute-done.20.refs_4_ = bf16[288,128]{1,0:T(8,128)(2,1)S(1)} collective-permute-done((bf16[288,128]{1,0:T(8,128)(2,1)}, bf16[288,128]{1,0:T(8,128)(2,1)S(1)}, u32[]{:S(2)}, u32[]{:S(2)}) %collective-permute-start.20) | collective-permute-done | bytes 73760 | tf_op jit(solution)/shard_map/ppermute | solution.py:17
  89.6 0.0 collective-permute-done.21.refs_5_
  89.6 1.2 %collective-permute-done.22.refs_6_ = bf16[288,128]{1,0:T(8,128)(2,1)S(1)} collective-permute-done((bf16[288,128]{1,0:T(8,128)(2,1)}, bf16[288,128]{1,0:T(8,128)(2,1)S(1)}, u32[]{:S(2)}, u32[]{:S(2)}) %collective-permute-start.22) | collective-permute-done | bytes 73760 | tf_op jit(solution)/shard_map/ppermute | solution.py:17
  90.8 0.6 copy-done.8
  91.4 1.9 %shard_map.69 = (f32[1,2,128,128]{3,2,1,0:T(8,128)}, f32[2,2]{1,0:T(2,128)}) custom-call(f32[256,128]{1,0:T(8,128)} %get-tuple-element.21.mine_ref, f32[8,128]{1,0:T(8,128)} %get-tuple-element.22.total_ref, bf16[288,128]{1,0:T(8,128)(2,1)} %copy-done.2, bf16[288,128]{1,0:T(8,128)(2,1)} %copy-done.3, bf16[288,128]{1,0:T(8,128)(2,1)} %copy-done.4, ...), custom_call_target="tpu_custom_call" | custom-call | tf_op jit(solution)/shard_map/pallas_call | solution.py:223
  (34 shorter events, 0.1 us)
Async XLA Ops:
  1.6 34.8 %copy-start.1 = (bf16[6,128,128]{2,1,0:T(8,128)(2,1)}, bf16[6,128,128]{2,1,0:T(8,128)(2,1)S(1)}, u32[]{:S(2)}) copy-start(bf16[6,128,128]{2,1,0:T(8,128)(2,1)S(1)} %pad_maximum_fusion.refs_0_) | copy-start | bytes 589828
  1.6 11.0 %collective-permute-start.11 = (bf16[6,128,128]{2,1,0:T(8,128)(2,1)S(1)}, bf16[6,128,128]{2,1,0:T(8,128)(2,1)S(1)}, u32[]{:S(2)}, u32[]{:S(2)}) collective-permute-start(bf16[6,128,128]{2,1,0:T(8,128)(2,1)S(1)} %pad_maximum_fusion.refs_0_), channel_id=1, source_target_pairs={{0,12},{1,13},{2,14},{3,15},{4,8},{5,9},{6,10},{7,11},{8,4},{9,5},... | collective-permute-start | bytes 589832 | tf_op jit(solution)/shard_map/ppermute | solution.py:17
  6.7 16.7 %collective-permute-start.7 = (bf16[6,128,128]{2,1,0:T(8,128)(2,1)S(1)}, bf16[6,128,128]{2,1,0:T(8,128)(2,1)S(1)}, u32[]{:S(2)}, u32[]{:S(2)}) collective-permute-start(bf16[6,128,128]{2,1,0:T(8,128)(2,1)S(1)} %pad_maximum_fusion.refs_0_), channel_id=1, source_target_pairs={{0,8},{1,9},{2,10},{3,11},{4,12},{5,13},{6,14},{7,15},{8,0},{9,1},... | collective-permute-start | bytes 589832 | tf_op jit(solution)/shard_map/ppermute | solution.py:17
  6.7 16.7 %collective-permute-start.3 = (bf16[6,128,128]{2,1,0:T(8,128)(2,1)S(1)}, bf16[6,128,128]{2,1,0:T(8,128)(2,1)S(1)}, u32[]{:S(2)}, u32[]{:S(2)}) collective-permute-start(bf16[6,128,128]{2,1,0:T(8,128)(2,1)S(1)} %pad_maximum_fusion.refs_0_), channel_id=1, source_target_pairs={{0,4},{1,5},{2,6},{3,7},{4,0},{5,1},{6,2},{7,3},{8,12},{9,13},{10,... | collective-permute-start | bytes 589832 | tf_op jit(solution)/shard_map/ppermute | solution.py:17
  7.3 17.7 %collective-permute-start.1 = (bf16[6,128,128]{2,1,0:T(8,128)(2,1)S(1)}, bf16[6,128,128]{2,1,0:T(8,128)(2,1)S(1)}, u32[]{:S(2)}, u32[]{:S(2)}) collective-permute-start(bf16[6,128,128]{2,1,0:T(8,128)(2,1)S(1)} %pad_maximum_fusion.refs_0_), channel_id=1, source_target_pairs={{0,2},{1,3},{2,0},{3,1},{4,6},{5,7},{6,4},{7,5},{8,10},{9,11},{10,... | collective-permute-start | bytes 589832 | tf_op jit(solution)/shard_map/ppermute | solution.py:17
  9.0 16.2 %collective-permute-start = (bf16[6,128,128]{2,1,0:T(8,128)(2,1)S(1)}, bf16[6,128,128]{2,1,0:T(8,128)(2,1)S(1)}, u32[]{:S(2)}, u32[]{:S(2)}) collective-permute-start(bf16[6,128,128]{2,1,0:T(8,128)(2,1)S(1)} %pad_maximum_fusion.refs_0_), channel_id=1, source_target_pairs={{0,1},{1,0},{2,3},{3,2},{4,5},{5,4},{6,7},{7,6},{8,9},{9,8},{10,11... | collective-permute-start | bytes 589832 | tf_op jit(solution)/shard_map/ppermute | solution.py:17
  12.6 23.8 %copy-start.9 = (bf16[6,128,128]{2,1,0:T(8,128)(2,1)}, bf16[6,128,128]{2,1,0:T(8,128)(2,1)S(1)}, u32[]{:S(2)}) copy-start(bf16[6,128,128]{2,1,0:T(8,128)(2,1)S(1)} %collective-permute-done.11.refs_12_) | copy-start | bytes 589828
  12.6 13.1 %collective-permute-start.13 = (bf16[6,128,128]{2,1,0:T(8,128)(2,1)S(1)}, bf16[6,128,128]{2,1,0:T(8,128)(2,1)S(1)}, u32[]{:S(2)}, u32[]{:S(2)}) collective-permute-start(bf16[6,128,128]{2,1,0:T(8,128)(2,1)S(1)} %collective-permute-done.11.refs_12_), channel_id=1, source_target_pairs={{0,2},{1,3},{2,0},{3,1},{4,6},{5,7},{6,4},{7,5},{8,10},{9,11},{10,... | collective-permute-start | bytes 589832 | tf_op jit(solution)/shard_map/ppermute | solution.py:17
  23.4 13.0 %copy-start.10 = (bf16[6,128,128]{2,1,0:T(8,128)(2,1)}, bf16[6,128,128]{2,1,0:T(8,128)(2,1)S(1)}, u32[]{:S(2)}) copy-start(bf16[6,128,128]{2,1,0:T(8,128)(2,1)S(1)} %collective-permute-done.7.refs_8_) | copy-start | bytes 589828
  23.4 2.4 %collective-permute-start.12 = (bf16[6,128,128]{2,1,0:T(8,128)(2,1)S(1)}, bf16[6,128,128]{2,1,0:T(8,128)(2,1)S(1)}, u32[]{:S(2)}, u32[]{:S(2)}) collective-permute-start(bf16[6,128,128]{2,1,0:T(8,128)(2,1)S(1)} %collective-permute-done.11.refs_12_), channel_id=1, source_target_pairs={{0,1},{1,0},{2,3},{3,2},{4,5},{5,4},{6,7},{7,6},{8,9},{9,8},{10,11... | collective-permute-start | bytes 589832 | tf_op jit(solution)/shard_map/ppermute | solution.py:17
  23.4 13.0 %copy-start.11 = (bf16[6,128,128]{2,1,0:T(8,128)(2,1)}, bf16[6,128,128]{2,1,0:T(8,128)(2,1)S(1)}, u32[]{:S(2)}) copy-start(bf16[6,128,128]{2,1,0:T(8,128)(2,1)S(1)} %collective-permute-done.3.refs_4_) | copy-start | bytes 589828
  23.4 7.8 %collective-permute-start.9 = (bf16[6,128,128]{2,1,0:T(8,128)(2,1)S(1)}, bf16[6,128,128]{2,1,0:T(8,128)(2,1)S(1)}, u32[]{:S(2)}, u32[]{:S(2)}) collective-permute-start(bf16[6,128,128]{2,1,0:T(8,128)(2,1)S(1)} %collective-permute-done.7.refs_8_), channel_id=1, source_target_pairs={{0,2},{1,3},{2,0},{3,1},{4,6},{5,7},{6,4},{7,5},{8,10},{9,11},{10,... | collective-permute-start | bytes 589832 | tf_op jit(solution)/shard_map/ppermute | solution.py:17
  25.0 11.4 %copy-start.12 = (bf16[6,128,128]{2,1,0:T(8,128)(2,1)}, bf16[6,128,128]{2,1,0:T(8,128)(2,1)S(1)}, u32[]{:S(2)}) copy-start(bf16[6,128,128]{2,1,0:T(8,128)(2,1)S(1)} %collective-permute-done.1.refs_2_) | copy-start | bytes 589828
  25.0 6.2 %collective-permute-start.8 = (bf16[6,128,128]{2,1,0:T(8,128)(2,1)S(1)}, bf16[6,128,128]{2,1,0:T(8,128)(2,1)S(1)}, u32[]{:S(2)}, u32[]{:S(2)}) collective-permute-start(bf16[6,128,128]{2,1,0:T(8,128)(2,1)S(1)} %collective-permute-done.7.refs_8_), channel_id=1, source_target_pairs={{0,1},{1,0},{2,3},{3,2},{4,5},{5,4},{6,7},{7,6},{8,9},{9,8},{10,11... | collective-permute-start | bytes 589832 | tf_op jit(solution)/shard_map/ppermute | solution.py:17
  25.2 11.3 %copy-start.13 = (bf16[6,128,128]{2,1,0:T(8,128)(2,1)}, bf16[6,128,128]{2,1,0:T(8,128)(2,1)S(1)}, u32[]{:S(2)}) copy-start(bf16[6,128,128]{2,1,0:T(8,128)(2,1)S(1)} %collective-permute-done.refs_1_) | copy-start | bytes 589828
  25.2 9.8 %collective-permute-start.5 = (bf16[6,128,128]{2,1,0:T(8,128)(2,1)S(1)}, bf16[6,128,128]{2,1,0:T(8,128)(2,1)S(1)}, u32[]{:S(2)}, u32[]{:S(2)}) collective-permute-start(bf16[6,128,128]{2,1,0:T(8,128)(2,1)S(1)} %collective-permute-done.3.refs_4_), channel_id=1, source_target_pairs={{0,2},{1,3},{2,0},{3,1},{4,6},{5,7},{6,4},{7,5},{8,10},{9,11},{10,... | collective-permute-start | bytes 589832 | tf_op jit(solution)/shard_map/ppermute | solution.py:17
  25.7 10.7 %copy-start.14 = (bf16[6,128,128]{2,1,0:T(8,128)(2,1)}, bf16[6,128,128]{2,1,0:T(8,128)(2,1)S(1)}, u32[]{:S(2)}) copy-start(bf16[6,128,128]{2,1,0:T(8,128)(2,1)S(1)} %collective-permute-done.13.refs_14_) | copy-start | bytes 589828
  25.7 9.3 %collective-permute-start.4 = (bf16[6,128,128]{2,1,0:T(8,128)(2,1)S(1)}, bf16[6,128,128]{2,1,0:T(8,128)(2,1)S(1)}, u32[]{:S(2)}, u32[]{:S(2)}) collective-permute-start(bf16[6,128,128]{2,1,0:T(8,128)(2,1)S(1)} %collective-permute-done.3.refs_4_), channel_id=1, source_target_pairs={{0,1},{1,0},{2,3},{3,2},{4,5},{5,4},{6,7},{7,6},{8,9},{9,8},{10,11... | collective-permute-start | bytes 589832 | tf_op jit(solution)/shard_map/ppermute | solution.py:17
  25.7 10.7 %copy-start.15 = (bf16[6,128,128]{2,1,0:T(8,128)(2,1)}, bf16[6,128,128]{2,1,0:T(8,128)(2,1)S(1)}, u32[]{:S(2)}) copy-start(bf16[6,128,128]{2,1,0:T(8,128)(2,1)S(1)} %collective-permute-done.12.refs_13_) | copy-start | bytes 589828
  25.7 9.2 %collective-permute-start.2 = (bf16[6,128,128]{2,1,0:T(8,128)(2,1)S(1)}, bf16[6,128,128]{2,1,0:T(8,128)(2,1)S(1)}, u32[]{:S(2)}, u32[]{:S(2)}) collective-permute-start(bf16[6,128,128]{2,1,0:T(8,128)(2,1)S(1)} %collective-permute-done.1.refs_2_), channel_id=1, source_target_pairs={{0,1},{1,0},{2,3},{3,2},{4,5},{5,4},{6,7},{7,6},{8,9},{9,8},{10,11... | collective-permute-start | bytes 589832 | tf_op jit(solution)/shard_map/ppermute | solution.py:17
  31.2 5.3 %copy-start.16 = (bf16[6,128,128]{2,1,0:T(8,128)(2,1)}, bf16[6,128,128]{2,1,0:T(8,128)(2,1)S(1)}, u32[]{:S(2)}) copy-start(bf16[6,128,128]{2,1,0:T(8,128)(2,1)S(1)} %collective-permute-done.9.refs_10_) | copy-start | bytes 589828
  31.2 3.8 %collective-permute-start.14 = (bf16[6,128,128]{2,1,0:T(8,128)(2,1)S(1)}, bf16[6,128,128]{2,1,0:T(8,128)(2,1)S(1)}, u32[]{:S(2)}, u32[]{:S(2)}) collective-permute-start(bf16[6,128,128]{2,1,0:T(8,128)(2,1)S(1)} %collective-permute-done.13.refs_14_), channel_id=1, source_target_pairs={{0,1},{1,0},{2,3},{3,2},{4,5},{5,4},{6,7},{7,6},{8,9},{9,8},{10,11... | collective-permute-start | bytes 589832 | tf_op jit(solution)/shard_map/ppermute | solution.py:17
  31.2 5.3 %copy-start.17 = (bf16[6,128,128]{2,1,0:T(8,128)(2,1)}, bf16[6,128,128]{2,1,0:T(8,128)(2,1)S(1)}, u32[]{:S(2)}) copy-start(bf16[6,128,128]{2,1,0:T(8,128)(2,1)S(1)} %collective-permute-done.8.refs_9_) | copy-start | bytes 589828
  31.2 3.8 %collective-permute-start.10 = (bf16[6,128,128]{2,1,0:T(8,128)(2,1)S(1)}, bf16[6,128,128]{2,1,0:T(8,128)(2,1)S(1)}, u32[]{:S(2)}, u32[]{:S(2)}) collective-permute-start(bf16[6,128,128]{2,1,0:T(8,128)(2,1)S(1)} %collective-permute-done.9.refs_10_), channel_id=1, source_target_pairs={{0,1},{1,0},{2,3},{3,2},{4,5},{5,4},{6,7},{7,6},{8,9},{9,8},{10,11... | collective-permute-start | bytes 589832 | tf_op jit(solution)/shard_map/ppermute | solution.py:17
  34.9 1.5 %copy-start.18 = (bf16[6,128,128]{2,1,0:T(8,128)(2,1)}, bf16[6,128,128]{2,1,0:T(8,128)(2,1)S(1)}, u32[]{:S(2)}) copy-start(bf16[6,128,128]{2,1,0:T(8,128)(2,1)S(1)} %collective-permute-done.5.refs_6_) | copy-start | bytes 589828
  34.9 1.4 %collective-permute-start.6 = (bf16[6,128,128]{2,1,0:T(8,128)(2,1)S(1)}, bf16[6,128,128]{2,1,0:T(8,128)(2,1)S(1)}, u32[]{:S(2)}, u32[]{:S(2)}) collective-permute-start(bf16[6,128,128]{2,1,0:T(8,128)(2,1)S(1)} %collective-permute-done.5.refs_6_), channel_id=1, source_target_pairs={{0,1},{1,0},{2,3},{3,2},{4,5},{5,4},{6,7},{7,6},{8,9},{9,8},{10,11... | collective-permute-start | bytes 589832 | tf_op jit(solution)/shard_map/ppermute | solution.py:17
  34.9 1.5 %copy-start.19 = (bf16[6,128,128]{2,1,0:T(8,128)(2,1)}, bf16[6,128,128]{2,1,0:T(8,128)(2,1)S(1)}, u32[]{:S(2)}) copy-start(bf16[6,128,128]{2,1,0:T(8,128)(2,1)S(1)} %collective-permute-done.4.refs_5_) | copy-start | bytes 589828
  35.0 1.5 %copy-start.20 = (bf16[6,128,128]{2,1,0:T(8,128)(2,1)}, bf16[6,128,128]{2,1,0:T(8,128)(2,1)S(1)}, u32[]{:S(2)}) copy-start(bf16[6,128,128]{2,1,0:T(8,128)(2,1)S(1)} %collective-permute-done.2.refs_3_) | copy-start | bytes 589828
  35.0 1.5 %copy-start.21 = (bf16[6,128,128]{2,1,0:T(8,128)(2,1)}, bf16[6,128,128]{2,1,0:T(8,128)(2,1)S(1)}, u32[]{:S(2)}) copy-start(bf16[6,128,128]{2,1,0:T(8,128)(2,1)S(1)} %collective-permute-done.14.refs_15_) | copy-start | bytes 589828
  35.0 1.5 %copy-start.22 = (bf16[6,128,128]{2,1,0:T(8,128)(2,1)}, bf16[6,128,128]{2,1,0:T(8,128)(2,1)S(1)}, u32[]{:S(2)}) copy-start(bf16[6,128,128]{2,1,0:T(8,128)(2,1)S(1)} %collective-permute-done.10.refs_11_) | copy-start | bytes 589828
  36.4 0.7 copy-start.23
  62.1 5.6 %collective-permute-start.15 = (bf16[2080,128]{1,0:T(8,128)(2,1)}, bf16[2080,128]{1,0:T(8,128)(2,1)S(1)}, u32[]{:S(2)}, u32[]{:S(2)}) collective-permute-start(bf16[2080,128]{1,0:T(8,128)(2,1)} %get-tuple-element.20), channel_id=1, source_target_pairs={{0,1},{1,0},{2,3},{3,2},{4,5},{5,4},{6,7},{7,6},{8,9},{9,8},{10,11... | collective-permute-start | bytes 1597448 | tf_op jit(solution)/shard_map/ppermute | solution.py:17
  67.8 0.8 copy-start
  70.8 8.7 %collective-permute-start.16 = (bf16[288,128]{1,0:T(8,128)(2,1)}, bf16[288,128]{1,0:T(8,128)(2,1)S(1)}, u32[]{:S(2)}, u32[]{:S(2)}) collective-permute-start(bf16[288,128]{1,0:T(8,128)(2,1)} %get-tuple-element.23), channel_id=1, source_target_pairs={{0,2},{1,3},{2,0},{3,1},{4,6},{5,7},{6,4},{7,5},{8,10},{9,11},{10,... | collective-permute-start | bytes 221192 | tf_op jit(solution)/shard_map/ppermute | solution.py:17
  73.6 9.8 %collective-permute-start.17 = (bf16[288,128]{1,0:T(8,128)(2,1)}, bf16[288,128]{1,0:T(8,128)(2,1)S(1)}, u32[]{:S(2)}, u32[]{:S(2)}) collective-permute-start(bf16[288,128]{1,0:T(8,128)(2,1)} %get-tuple-element.24), channel_id=1, source_target_pairs={{0,4},{1,5},{2,6},{3,7},{4,0},{5,1},{6,2},{7,3},{8,12},{9,13},{10,... | collective-permute-start | bytes 221192 | tf_op jit(solution)/shard_map/ppermute | solution.py:17
  75.1 8.3 %collective-permute-start.18 = (bf16[288,128]{1,0:T(8,128)(2,1)}, bf16[288,128]{1,0:T(8,128)(2,1)S(1)}, u32[]{:S(2)}, u32[]{:S(2)}) collective-permute-start(bf16[288,128]{1,0:T(8,128)(2,1)} %get-tuple-element.25), channel_id=1, source_target_pairs={{0,6},{1,7},{2,4},{3,5},{4,2},{5,3},{6,0},{7,1},{8,14},{9,15},{10,... | collective-permute-start | bytes 221192 | tf_op jit(solution)/shard_map/ppermute | solution.py:17
  75.1 8.3 %collective-permute-start.19 = (bf16[288,128]{1,0:T(8,128)(2,1)}, bf16[288,128]{1,0:T(8,128)(2,1)S(1)}, u32[]{:S(2)}, u32[]{:S(2)}) collective-permute-start(bf16[288,128]{1,0:T(8,128)(2,1)} %get-tuple-element.26), channel_id=1, source_target_pairs={{0,8},{1,9},{2,10},{3,11},{4,12},{5,13},{6,14},{7,15},{8,0},{9,1},... | collective-permute-start | bytes 221192 | tf_op jit(solution)/shard_map/ppermute | solution.py:17
  78.1 11.5 %collective-permute-start.20 = (bf16[288,128]{1,0:T(8,128)(2,1)}, bf16[288,128]{1,0:T(8,128)(2,1)S(1)}, u32[]{:S(2)}, u32[]{:S(2)}) collective-permute-start(bf16[288,128]{1,0:T(8,128)(2,1)} %get-tuple-element.27), channel_id=1, source_target_pairs={{0,10},{1,11},{2,8},{3,9},{4,14},{5,15},{6,12},{7,13},{8,2},{9,3},... | collective-permute-start | bytes 221192 | tf_op jit(solution)/shard_map/ppermute | solution.py:17
  79.5 11.3 %copy-start.2 = (bf16[288,128]{1,0:T(8,128)(2,1)}, bf16[288,128]{1,0:T(8,128)(2,1)S(1)}, u32[]{:S(2)}) copy-start(bf16[288,128]{1,0:T(8,128)(2,1)S(1)} %collective-permute-done.16.refs_0_) | copy-start | bytes 221188
  79.5 10.1 %collective-permute-start.21 = (bf16[288,128]{1,0:T(8,128)(2,1)}, bf16[288,128]{1,0:T(8,128)(2,1)S(1)}, u32[]{:S(2)}, u32[]{:S(2)}) collective-permute-start(bf16[288,128]{1,0:T(8,128)(2,1)} %get-tuple-element.28), channel_id=1, source_target_pairs={{0,12},{1,13},{2,14},{3,15},{4,8},{5,9},{6,10},{7,11},{8,4},{9,5},... | collective-permute-start | bytes 221192 | tf_op jit(solution)/shard_map/ppermute | solution.py:17
  83.4 7.4 %copy-start.3 = (bf16[288,128]{1,0:T(8,128)(2,1)}, bf16[288,128]{1,0:T(8,128)(2,1)S(1)}, u32[]{:S(2)}) copy-start(bf16[288,128]{1,0:T(8,128)(2,1)S(1)} %collective-permute-done.17.refs_1_) | copy-start | bytes 221188
  83.4 7.4 %collective-permute-start.22 = (bf16[288,128]{1,0:T(8,128)(2,1)}, bf16[288,128]{1,0:T(8,128)(2,1)S(1)}, u32[]{:S(2)}, u32[]{:S(2)}) collective-permute-start(bf16[288,128]{1,0:T(8,128)(2,1)} %get-tuple-element.29), channel_id=1, source_target_pairs={{0,14},{1,15},{2,12},{3,13},{4,10},{5,11},{6,8},{7,9},{8,6},{9,7},... | collective-permute-start | bytes 221192 | tf_op jit(solution)/shard_map/ppermute | solution.py:17
  83.4 7.4 %copy-start.4 = (bf16[288,128]{1,0:T(8,128)(2,1)}, bf16[288,128]{1,0:T(8,128)(2,1)S(1)}, u32[]{:S(2)}) copy-start(bf16[288,128]{1,0:T(8,128)(2,1)S(1)} %collective-permute-done.18.refs_2_) | copy-start | bytes 221188
  83.5 7.3 %copy-start.5 = (bf16[288,128]{1,0:T(8,128)(2,1)}, bf16[288,128]{1,0:T(8,128)(2,1)S(1)}, u32[]{:S(2)}) copy-start(bf16[288,128]{1,0:T(8,128)(2,1)S(1)} %collective-permute-done.19.refs_3_) | copy-start | bytes 221188
  89.6 1.2 %copy-start.6 = (bf16[288,128]{1,0:T(8,128)(2,1)}, bf16[288,128]{1,0:T(8,128)(2,1)S(1)}, u32[]{:S(2)}) copy-start(bf16[288,128]{1,0:T(8,128)(2,1)S(1)} %collective-permute-done.20.refs_4_) | copy-start | bytes 221188
  89.6 1.2 %copy-start.7 = (bf16[288,128]{1,0:T(8,128)(2,1)}, bf16[288,128]{1,0:T(8,128)(2,1)S(1)}, u32[]{:S(2)}) copy-start(bf16[288,128]{1,0:T(8,128)(2,1)S(1)} %collective-permute-done.21.refs_5_) | copy-start | bytes 221188
  90.8 0.6 copy-start.8

commit v2 on v0

v2 whole, which is shorter than its diff:
```python
import functools

import jax
import jax.numpy as jnp
from jax import lax
from jax.experimental import pallas as pl
from jax.experimental.pallas import tpu as pltpu
from jax.sharding import PartitionSpec as P

VMEM_LIMIT = 56 * 1024 * 1024
TAIL = 32
CHUNK = 32
UNROLL = 16
PAIRS = 8


def exchange(value, n, mask):
    return lax.ppermute(value, "op", [(i, i ^ mask) for i in range(n)])


def ring_step(value, n):
    return lax.ppermute(value, "op", [(i, (i + 4) % n) for i in range(n)])


def gather(block, n):
    blocks = []
    for step in range(n // 4):
        if step:
            block = ring_step(block, n)
        across = exchange(block, n, 2)
        blocks += [block, exchange(block, n, 1), across, exchange(across, n, 1)]
    return blocks


def owner_of(place, n):
    me = lax.axis_index("op")
    step, mask = divmod(place, 4)
    return lax.rem(me // 4 - step + n // 4, n // 4) * 4 + jnp.bitwise_xor(lax.rem(me, 4), mask)


def split3(value):
    high = value.astype(jnp.bfloat16)
    rest = value - high.astype(jnp.float32)
    middle = rest.astype(jnp.bfloat16)
    low = (rest - middle.astype(jnp.float32)).astype(jnp.bfloat16)
    zero = jnp.zeros_like(value)
    return jnp.concatenate(
        [high.astype(jnp.float32), middle.astype(jnp.float32), low.astype(jnp.float32), zero], axis=0
    ).astype(jnp.bfloat16)


def join3(tail):
    wide = tail.astype(jnp.float32)
    return wide[0:8] + wide[8:16] + wide[16:24]


def matrix_of(values):
    rows = lax.broadcasted_iota(jnp.int32, (8, 128), 0)
    lanes = lax.broadcasted_iota(jnp.int32, (8, 128), 1)
    total = jnp.zeros((8, 128), jnp.float32)
    for (i, j), value in values.items():
        total = total + jnp.where((rows == i) & (lanes == j), value, 0.0)
    return total


def fold(value):
    return value.reshape(16, 8, 128).sum(axis=0)


def plan_kernel(sectors, terms, tasks_ref, plan_ref):
    slots = tasks_ref.shape[1]
    places = plan_ref.shape[1]
    rows = tasks_ref[...].astype(jnp.float32)
    source, target, term, live = rows[0:1], rows[1:2], rows[2:3], rows[3:4]
    key = jnp.where(live > 0, target, float(sectors))
    lane = lax.broadcasted_iota(jnp.int32, (1, slots), 1).astype(jnp.float32)

    def column(*values):
        pad = [jnp.zeros((8 - len(values), slots), jnp.float32)]
        return jnp.transpose(jnp.concatenate(list(values) + pad, axis=0))

    columns = column(key, lane, source, term)
    key_column, lane_column = columns[:, 0:1], columns[:, 1:2]
    earlier = jnp.where((key_column == key) & (lane_column < lane), 1.0, 0.0)
    within = jnp.sum(earlier, axis=0, keepdims=True)
    sector = lax.broadcasted_iota(jnp.int32, (sectors, slots), 0).astype(jnp.float32)
    count = jnp.sum(jnp.where(sector == key, 1.0, 0.0), axis=1, keepdims=True)
    padded = 2.0 * jnp.floor((count + 1.0) * 0.5)
    start = jnp.sum(jnp.where(sector < key, padded, 0.0), axis=0, keepdims=True)
    place = jnp.where(live > 0, start + within, -1.0)
    place_column = column(place)[:, 0:1]
    at = lax.broadcasted_iota(jnp.int32, (slots, places), 1).astype(jnp.float32)
    hit = place_column == at

    def pick(values, other):
        found = jnp.sum(jnp.where(hit, values - other, 0.0), axis=0, keepdims=True)
        return (found + other).astype(jnp.int32)

    plan_ref[0:1] = pick(lane_column, 0.0)
    plan_ref[1:2] = pick(columns[:, 2:3], 0.0)
    plan_ref[2:3] = pick(columns[:, 3:4], float(terms))
    plan_ref[3:4] = pick(key_column, float(sectors))
    plan_ref[4:8] = jnp.zeros((4, places), jnp.int32)


def make_plan(tasks, sectors, terms):
    places = -(-(tasks.shape[1] + sectors) // CHUNK) * CHUNK
    return pl.pallas_call(
        functools.partial(plan_kernel, sectors, terms),
        out_shape=jax.ShapeDtypeStruct((8, places), jnp.int32),
        compiler_params=pltpu.CompilerParams(vmem_limit_bytes=VMEM_LIMIT),
    )(tasks)


def half_kernel(n, plan_ref, left_ref, *refs):
    blocks = refs[:n]
    half_ref, corr_ref, trial, left, trial_sem, left_sem = refs[n:]
    step, steps = pl.program_id(0), pl.num_programs(0)

    def fetch(chunk):
        def one(u, carry):
            slot = plan_ref[0, chunk * CHUNK + u]
            pltpu.make_async_copy(
                left_ref.at[slot], left.at[lax.rem(chunk, 2), u], left_sem.at[lax.rem(chunk, 2)]
            ).start()
            return carry

        lax.fori_loop(0, CHUNK, one, 0)

    def trial_copy(place):
        return pltpu.make_async_copy(
            blocks[place].at[pl.ds(0, 2)], trial.at[owner_of(place, n)], trial_sem.at[place]
        )

    @pl.when(step == 0)
    def _():
        for place in range(n):
            trial_copy(place).start()
        fetch(0)

    @pl.when(step + 1 < steps)
    def _():
        fetch(step + 1)

    @pl.when(step == 0)
    def _():
        for place in range(n):
            trial_copy(place).wait()

        def dots(s, carry):
            t0 = trial[s, 0].astype(jnp.float32)
            t1 = trial[s, 1].astype(jnp.float32)
            return carry[0] + fold(t0 * t0), carry[1] + fold(t0 * t1), carry[2] + fold(t1 * t1)

        zero = jnp.zeros((8, 128), jnp.float32)
        c00, c01, c11 = [jnp.sum(x) for x in lax.fori_loop(0, n, dots, (zero,) * 3)]
        corr_ref[...] = matrix_of({(0, 0): c00, (0, 1): c01, (1, 0): c01, (1, 1): c11})[0:2, 0:2]

    now = lax.rem(step, 2)
    pltpu.make_async_copy(left_ref.at[pl.ds(0, CHUNK)], left.at[now], left_sem.at[now]).wait()

    def some(part, carry):
        for u in range(UNROLL):
            at = part * UNROLL + u
            source = plan_ref[1, step * CHUNK + at]
            vectors = jnp.concatenate([trial[source, 0], trial[source, 1]], axis=1)
            half = jnp.dot(left[now, at], vectors, preferred_element_type=jnp.float32).astype(jnp.bfloat16)
            half_ref[at, 0:128, :] = half[:, :128]
            half_ref[at, 128:256, :] = half[:, 128:]
        return carry

    lax.fori_loop(0, CHUNK // UNROLL, some, 0)


def make_halves(plan, left_ops, blocks):
    n = len(blocks)
    places = plan.shape[1]
    return pl.pallas_call(
        functools.partial(half_kernel, n),
        grid=(places // CHUNK,),
        out_shape=(
            jax.ShapeDtypeStruct((places, 256, 128), jnp.bfloat16),
            jax.ShapeDtypeStruct((2, 2), jnp.float32),
        ),
        in_specs=[pl.BlockSpec(memory_space=pltpu.SMEM)] + [pl.BlockSpec(memory_space=pl.ANY)] * (1 + n),
        out_specs=(
            pl.BlockSpec((CHUNK, 256, 128), lambda i: (i, 0, 0)),
            pl.BlockSpec((2, 2), lambda i: (0, 0)),
        ),
        scratch_shapes=[
            pltpu.VMEM((n, 2, 128, 128), jnp.bfloat16),
            pltpu.VMEM((2, CHUNK, 128, 128), jnp.bfloat16),
            pltpu.SemaphoreType.DMA((n,)),
            pltpu.SemaphoreType.DMA((2,)),
        ],
        compiler_params=pltpu.CompilerParams(vmem_limit_bytes=VMEM_LIMIT),
        cost_estimate=pl.CostEstimate(
            flops=places * 4 * 128**3, bytes_accessed=places * 98304 + n * 65536, transcendentals=0
        ),
    )(plan, left_ops, *blocks)


def term_kernel(n, terms_per, plan_ref, half_ref, *refs):
    blocks = refs[:n]
    send_ref, keep_ref, own_ref, trial, right, acc, block_sem = refs[n:]
    step, steps = pl.program_id(0), pl.num_programs(0)

    def block_copies(place):
        owner = owner_of(place, n)
        return (
            pltpu.make_async_copy(blocks[place].at[pl.ds(0, 2)], trial.at[owner], block_sem.at[place, 0]),
            pltpu.make_async_copy(
                blocks[place].at[pl.ds(2, terms_per)],
                right.at[pl.ds(owner * terms_per, terms_per)],
                block_sem.at[place, 1],
            ),
        )

    @pl.when(step == 0)
    def _():
        for place in range(n):
            for copy in block_copies(place):
                copy.start()
        right[n * terms_per] = jnp.zeros((128, 128), jnp.bfloat16)

        def clear(s, carry):
            acc[s] = jnp.zeros((256, 128), jnp.float32)
            return carry

        lax.fori_loop(0, n + 1, clear, 0)
        for place in range(n):
            for copy in block_copies(place):
                copy.wait()

    for part in range(CHUNK // 2 // PAIRS):
        first = step * CHUNK + part * 2 * PAIRS

        @pl.when(plan_ref[3, first] < n)
        def _():
            for u in range(PAIRS):
                at = part * 2 * PAIRS + 2 * u
                place = first + 2 * u
                halves = jnp.concatenate([half_ref[at], half_ref[at + 1]], axis=1)
                rights = jnp.concatenate([right[plan_ref[2, place]], right[plan_ref[2, place + 1]]], axis=1)
                term = lax.dot_general(
                    halves, rights, (((1,), (1,)), ((), ())), preferred_element_type=jnp.float32
                )
                target = plan_ref[3, place]
                acc[target] = acc[target] + term

    @pl.when(step == steps - 1)
    def _():
        def dots(s, carry):
            t0 = trial[s, 0].astype(jnp.float32)
            t1 = trial[s, 1].astype(jnp.float32)
            a0 = acc[s, 0:128, :]
            a1 = acc[s, 128:256, :]
            p00, p01, p10, p11 = carry
            return p00 + fold(t0 * a0), p01 + fold(t0 * a1), p10 + fold(t1 * a0), p11 + fold(t1 * a1)

        zero = jnp.zeros((8, 128), jnp.float32)
        p00, p01, p10, p11 = [jnp.sum(x) for x in lax.fori_loop(0, n, dots, (zero,) * 4)]
        own = matrix_of({(0, 0): p00, (0, 1): p01, (1, 0): p10, (1, 1): p11})
        own_ref[...] = own
        core = lax.rem(lax.axis_index("op"), 2)

        def pack(j, carry):
            keep_ref[j] = acc[2 * j + core]
            send_ref[pl.ds(pl.multiple_of(j * 256, 256), 256), :] = acc[2 * j + 1 - core].astype(jnp.bfloat16)
            return carry

        lax.fori_loop(0, n // 2, pack, 0)
        send_ref[n // 2 * 256 :, :] = split3(own)


def add_terms(plan, halves, blocks):
    n = len(blocks)
    terms_per = blocks[0].shape[0] - 2
    places = plan.shape[1]
    return pl.pallas_call(
        functools.partial(term_kernel, n, terms_per),
        grid=(places // CHUNK,),
        out_shape=(
            jax.ShapeDtypeStruct((n // 2 * 256 + TAIL, 128), jnp.bfloat16),
            jax.ShapeDtypeStruct((n // 2, 256, 128), jnp.float32),
            jax.ShapeDtypeStruct((8, 128), jnp.float32),
        ),
        in_specs=[
            pl.BlockSpec(memory_space=pltpu.SMEM),
            pl.BlockSpec((CHUNK, 256, 128), lambda i: (i, 0, 0)),
        ]
        + [pl.BlockSpec(memory_space=pl.ANY)] * n,
        out_specs=(
            pl.BlockSpec((n // 2 * 256 + TAIL, 128), lambda i: (0, 0)),
            pl.BlockSpec((n // 2, 256, 128), lambda i: (0, 0, 0)),
            pl.BlockSpec((8, 128), lambda i: (0, 0)),
        ),
        scratch_shapes=[
            pltpu.VMEM((n, 2, 128, 128), jnp.bfloat16),
            pltpu.VMEM((n * terms_per + 1, 128, 128), jnp.bfloat16),
            pltpu.VMEM((n + 1, 256, 128), jnp.float32),
            pltpu.SemaphoreType.DMA((n, 2)),
        ],
        compiler_params=pltpu.CompilerParams(vmem_limit_bytes=VMEM_LIMIT),
        cost_estimate=pl.CostEstimate(
            flops=places * 4 * 128**3, bytes_accessed=places * 65536 + n * 200000, transcendentals=0
        ),
    )(plan, halves, *blocks)


def chip_kernel(chips, keep_ref, own_ref, received_ref, mine_ref, total_ref, send_ref):
    total = own_ref[...] + join3(received_ref[chips * 256 :, :])
    total_ref[...] = total
    tail = split3(total)
    here = lax.axis_index("op") // 2
    for j in range(chips):
        value = keep_ref[j] + received_ref[j * 256 : (j + 1) * 256, :].astype(jnp.float32)
        send_ref[j, 0:256, :] = value.astype(jnp.bfloat16)
        send_ref[j, 256:, :] = tail

    mine_ref[...] = keep_ref[here] + received_ref[
        pl.ds(pl.multiple_of(here * 256, 256), 256), :
    ].astype(jnp.float32)
    send_ref[here] = jnp.zeros((256 + TAIL, 128), jnp.bfloat16)


def add_chip(keep, own, received):
    chips = keep.shape[0]
    return pl.pallas_call(
        functools.partial(chip_kernel, chips),
        out_shape=(
            jax.ShapeDtypeStruct((256, 128), jnp.float32),
            jax.ShapeDtypeStruct((8, 128), jnp.float32),
            jax.ShapeDtypeStruct((chips, 256 + TAIL, 128), jnp.bfloat16),
        ),
        compiler_params=pltpu.CompilerParams(vmem_limit_bytes=VMEM_LIMIT),
    )(keep, own, received)


def last_kernel(mine_ref, total_ref, received_ref, product_ref, projected_ref):
    value, total = mine_ref[...], total_ref[...]
    for j in range(received_ref.shape[0]):
        value = value + received_ref[j, 0:256, :].astype(jnp.float32)
        total = total + join3(received_ref[j, 256:, :])
    product_ref[0, 0] = value[0:128]
    product_ref[0, 1] = value[128:256]
    projected_ref[...] = total[0:2, 0:2]


def add_all(mine, total, received):
    return pl.pallas_call(
        last_kernel,
        out_shape=(
            jax.ShapeDtypeStruct((1, 2, 128, 128), jnp.float32),
            jax.ShapeDtypeStruct((2, 2), jnp.float32),
        ),
        compiler_params=pltpu.CompilerParams(vmem_limit_bytes=VMEM_LIMIT),
    )(mine, total, received)


def body(n, trial, left_ops, right_ops, task_list):
    blocks = gather(jnp.concatenate([trial[0], right_ops], axis=0), n)
    plan = make_plan(task_list.T, n, n * right_ops.shape[0])
    halves, correlation = make_halves(plan, left_ops, blocks)
    send, keep, own = add_terms(plan, halves, blocks)
    mine, total, send = add_chip(keep, own, exchange(send, n, 1))
    same_core = [list(range(core, n, 2)) for core in range(2)]
    received = lax.all_to_all(send, "op", 0, 0, axis_index_groups=same_core, tiled=True)
    product, projected = add_all(mine, total, received)
    return product, correlation, projected


def solution(mesh):
    return jax.shard_map(
        functools.partial(body, mesh.shape["op"]),
        mesh=mesh,
        in_specs=(
            P(("groups", "op"), None, None, None),
            P(("groups", "op"), None, None),
            P(("groups", "op"), None, None),
            P(("groups", "op"), None),
        ),
        out_specs=(P(("groups", "op"), None, None, None), P("groups", None), P("groups", None)),
        check_vma=False,
    )
```

time: 308 us -> 102 us (0.33)
  waiting for transfers between devices: 145 us -> 24.7 us
  matrix products: 82.8 us -> 0 us
  Pallas kernels: 0 us -> 37.8 us
  local copies, waits for them, and re-layouts: 35.3 us -> 2.29 us
  between operations: 13.8 us -> 0.84 us
  starting transfers between devices: 0.11 us -> 10.3 us
  blocking collectives: 30.1 us -> 23 us
    all_gather x2 -> x0, waiting for transfers between devices: 84.6 us -> none  [the longest x1 42.5 us: body(): lax.all_gather(right_ops, 'op', axis=0, tiled=True)]
    dot_general x10 -> x0, matrix products: 82.8 us -> none  [the longest x4 54 us: accumulate(): jnp.einsum('ns,nvad->svad', weights, terms, precision=lax.Precision.HIGHEST)]
    reduce_scatter x1 -> x0, waiting for transfers between devices: 59.4 us -> none  [body(): lax.psum_scatter(partial_sums, 'op', scatter_dimension=0, tiled=True)]
    pallas_call x0 -> x5, Pallas kernels: none -> 37.8 us  [the longest x1 16.2 us: make_halves(): pl.pallas_call(functools.partial(half_kernel, n), grid=(places // CHUNK,)...]
    psum x1 -> x0, blocking collectives: 30.1 us -> none  [body(): lax.psum((correlation_terms, projected_terms), 'op')]
    gather x8 -> x0, local copies, waits for them, and re-layouts: 27.3 us -> none  [the longest x4 17.1 us: slot_terms(): sources = jnp.take(whole_trial, task_rows[:, 0], axis=0)]
    ppermute x0 -> x16, waiting for transfers between devices: none -> 24.7 us  [the longest x3 18.2 us: ring_step(): return lax.ppermute(value, 'op', [(i, (i + 4) % n) for i in range(n)])]
    all_to_all x0 -> x1, blocking collectives: none -> 23 us  [body(): lax.all_to_all(send, 'op', 0, 0, axis_index_groups=same_core, tiled=True)]
  transfers between devices with their start and end apart: 3 -> 16, of which waited for: 3 -> 6; matrix products, arithmetic and copies ran while one was open for 0% -> 0% of each run, Pallas kernels for 0% -> 2%
where the time goes in v2:
time: 102 us; the launch traced here: 99.9 us
  Pallas kernels  37.8 us (37%)
  waiting for transfers between devices  24.7 us (24%)
  blocking collectives  23 us (23%)
  starting transfers between devices  10.3 us (10%)
  local copies, waits for them, and re-layouts  2.29 us (2%)
    all_to_all x1, blocking collectives, body(): lax.all_to_all(send, 'op', 0, 0, axis_index_groups=same_core, tiled=True)  23 us
    ppermute x3, waiting for transfers between devices, ring_step(): return lax.ppermute(value, 'op', [(i, (i + 4) % n) for i in range(n)])  18.2 us
    pallas_call x1, Pallas kernels, make_halves(): pl.pallas_call(functools.partial(half_kernel, n), grid=(places // CHUNK,)...  16.2 us
    pallas_call x1, Pallas kernels, add_terms(): pl.pallas_call(functools.partial(term_kernel, n, terms_per), grid=(places...  15.4 us
    ppermute x13, starting transfers between devices, exchange(): return lax.ppermute(value, 'op', [(i, i ^ mask) for i in range(n)])  7.21 us
    ppermute x13, waiting for transfers between devices, exchange(): return lax.ppermute(value, 'op', [(i, i ^ mask) for i in range(n)])  6.52 us
    ppermute x3, starting transfers between devices, ring_step(): return lax.ppermute(value, 'op', [(i, (i + 4) % n) for i in range(n)])  3.08 us
    pallas_call x1, Pallas kernels, add_chip(): pl.pallas_call(functools.partial(chip_kernel, chips), out_shape=(jax.Shap...  2.34 us
  transfers between devices with their start and end apart: 16, of which 6 were waited for; matrix products, arithmetic and copies ran while one was open for 0% of the time, Pallas kernels for 2%

profile of v2, /device:TPU:0, one launch (start us, length us, event | category | flops | bytes accessed | tf_op | source)
XLA Modules:
  0.0 99.9 jit_solution(2774468254960841438)
XLA Ops:
  0.6 0.9 pad_maximum_fusion.refs_0_
  1.6 0.0 copy-start
  1.6 3.1 %collective-permute-start.3 = (bf16[6,128,128]{2,1,0:T(8,128)(2,1)S(1)}, bf16[6,128,128]{2,1,0:T(8,128)(2,1)S(1)}, u32[]{:S(2)}, u32[]{:S(2)}) collective-permute-start(bf16[6,128,128]{2,1,0:T(8,128)(2,1)S(1)} %pad_maximum_fusion.refs_0_), channel_id=1, source_target_pairs={{0,4},{1,5},{2,6},{3,7},{4,8},{5,9},{6,10},{7,11},{8,12},{9,13},{1... | collective-permute-start | bytes 589832 | tf_op jit(solution)/shard_map/ppermute | solution.py:22
  4.6 6.9 %collective-permute-done.3.refs_4_ = bf16[6,128,128]{2,1,0:T(8,128)(2,1)S(1)} collective-permute-done((bf16[6,128,128]{2,1,0:T(8,128)(2,1)S(1)}, bf16[6,128,128]{2,1,0:T(8,128)(2,1)S(1)}, u32[]{:S(2)}, u32[]{:S(2)}) %collective-permute-start.3) | collective-permute-done | bytes 196640 | tf_op jit(solution)/shard_map/ppermute | solution.py:22
  11.6 0.0 copy-start.1
  11.6 0.0 collective-permute-start.7
  11.6 1.5 %collective-permute-start.1 = (bf16[6,128,128]{2,1,0:T(8,128)(2,1)S(1)}, bf16[6,128,128]{2,1,0:T(8,128)(2,1)S(1)}, u32[]{:S(2)}, u32[]{:S(2)}) collective-permute-start(bf16[6,128,128]{2,1,0:T(8,128)(2,1)S(1)} %pad_maximum_fusion.refs_0_), channel_id=1, source_target_pairs={{0,2},{1,3},{2,0},{3,1},{4,6},{5,7},{6,4},{7,5},{8,10},{9,11},{10,... | collective-permute-start | bytes 589832 | tf_op jit(solution)/shard_map/ppermute | solution.py:18
  13.1 0.0 collective-permute-start
  13.1 6.4 %collective-permute-done.7.refs_8_ = bf16[6,128,128]{2,1,0:T(8,128)(2,1)S(1)} collective-permute-done((bf16[6,128,128]{2,1,0:T(8,128)(2,1)S(1)}, bf16[6,128,128]{2,1,0:T(8,128)(2,1)S(1)}, u32[]{:S(2)}, u32[]{:S(2)}) %collective-permute-start.7) | collective-permute-done | bytes 196640 | tf_op jit(solution)/shard_map/ppermute | solution.py:22
  19.5 0.0 copy-start.2
  19.5 0.0 collective-permute-start.11
  19.5 1.3 %collective-permute-start.5 = (bf16[6,128,128]{2,1,0:T(8,128)(2,1)S(1)}, bf16[6,128,128]{2,1,0:T(8,128)(2,1)S(1)}, u32[]{:S(2)}, u32[]{:S(2)}) collective-permute-start(bf16[6,128,128]{2,1,0:T(8,128)(2,1)S(1)} %collective-permute-done.3.refs_4_), channel_id=1, source_target_pairs={{0,2},{1,3},{2,0},{3,1},{4,6},{5,7},{6,4},{7,5},{8,10},{9,11},{10,... | collective-permute-start | bytes 589832 | tf_op jit(solution)/shard_map/ppermute | solution.py:18
  20.7 0.0 collective-permute-start.4
  20.7 0.0 collective-permute-done.1.refs_2_
  20.7 0.0 copy-start.3
  20.8 0.5 collective-permute-start.2
  21.3 0.0 collective-permute-done.refs_1_
  21.3 0.8 collective-permute-start.9
  22.0 4.9 %collective-permute-done.11.refs_12_ = bf16[6,128,128]{2,1,0:T(8,128)(2,1)S(1)} collective-permute-done((bf16[6,128,128]{2,1,0:T(8,128)(2,1)S(1)}, bf16[6,128,128]{2,1,0:T(8,128)(2,1)S(1)}, u32[]{:S(2)}, u32[]{:S(2)}) %collective-permute-start.11) | collective-permute-done | bytes 196640 | tf_op jit(solution)/shard_map/ppermute | solution.py:22
  26.9 1.3 %collective-permute-start.13 = (bf16[6,128,128]{2,1,0:T(8,128)(2,1)S(1)}, bf16[6,128,128]{2,1,0:T(8,128)(2,1)S(1)}, u32[]{:S(2)}, u32[]{:S(2)}) collective-permute-start(bf16[6,128,128]{2,1,0:T(8,128)(2,1)S(1)} %collective-permute-done.11.refs_12_), channel_id=1, source_target_pairs={{0,2},{1,3},{2,0},{3,1},{4,6},{5,7},{6,4},{7,5},{8,10},{9,11},{10,... | collective-permute-start | bytes 589832 | tf_op jit(solution)/shard_map/ppermute | solution.py:18
  28.2 0.0 collective-permute-done.5.refs_6_
  28.2 0.0 collective-permute-start.8
  28.2 0.0 collective-permute-done.4.refs_5_
  28.2 0.0 copy-start.7
  28.2 0.5 collective-permute-start.6
  28.7 0.0 collective-permute-done.2.refs_3_
  28.7 0.1 collective-permute-start.12
  28.8 1.7 %collective-permute-done.9.refs_10_ = bf16[6,128,128]{2,1,0:T(8,128)(2,1)S(1)} collective-permute-done((bf16[6,128,128]{2,1,0:T(8,128)(2,1)S(1)}, bf16[6,128,128]{2,1,0:T(8,128)(2,1)S(1)}, u32[]{:S(2)}, u32[]{:S(2)}) %collective-permute-start.9) | collective-permute-done | bytes 196640 | tf_op jit(solution)/shard_map/ppermute | solution.py:18
  30.6 0.0 collective-permute-start.10
  30.6 3.0 %collective-permute-done.13.refs_14_ = bf16[6,128,128]{2,1,0:T(8,128)(2,1)S(1)} collective-permute-done((bf16[6,128,128]{2,1,0:T(8,128)(2,1)S(1)}, bf16[6,128,128]{2,1,0:T(8,128)(2,1)S(1)}, u32[]{:S(2)}, u32[]{:S(2)}) %collective-permute-start.13) | collective-permute-done | bytes 196640 | tf_op jit(solution)/shard_map/ppermute | solution.py:18
  33.6 0.0 collective-permute-start.14
  33.6 2.0 %shard_map.67.plan_ref = s32[8,288]{1,0:T(8,128)} custom-call(s32[4,256]{1,0:T(4,128)} %bitcast.3), custom_call_target="tpu_custom_call" | custom-call | tf_op jit(solution)/shard_map/pallas_call | solution.py:108
  35.6 0.0 collective-permute-done.8.refs_9_
  35.6 0.0 collective-permute-done.6.refs_7_
  35.6 0.0 copy-start.12
  35.6 0.0 collective-permute-done.12.refs_13_
  35.6 0.0 copy-start.13
  35.6 0.0 collective-permute-done.10.refs_11_
  35.6 0.0 copy-start.14
  35.6 0.0 collective-permute-done.14.refs_15_
  35.6 0.0 copy-done
  35.6 0.0 copy-done.1
  35.7 0.0 copy-done.2
  35.7 0.0 copy-done.3
  35.7 0.0 copy-done.4
  35.7 0.0 copy-done.5
  35.7 0.0 copy-done.6
  35.7 0.0 copy-done.7
  35.7 0.0 copy-done.8
  35.7 0.0 copy-done.9
  35.7 0.0 copy-done.10
  35.7 0.5 copy-done.11
  36.3 0.1 copy-done.12
  36.3 0.1 copy-done.13
  36.4 0.1 copy-done.14
  36.5 0.7 copy-done.15
  37.2 16.2 %shard_map.68 = (bf16[288,256,128]{2,1,0:T(8,128)(2,1)}, f32[2,2]{1,0:T(2,128)}) custom-call(s32[8,288]{1,0:T(8,128)} %shard_map.67.plan_ref, bf16[256,128,128]{2,1,0:T(8,128)(2,1)} %left_ref.1, bf16[6,128,128]{2,1,0:T(8,128)(2,1)} %copy-done, bf16[6,128,128]{2,1,0:T(8,128)(2,1)} %copy-done.4, bf16[6,128,128]{2,1,0:T(8,128)(2,1)} %copy-done.3, ...), custom_call_target="tpu_custom_call" | custom-call | flops 2415919104 | bytes 29360128 | tf_op jit(solution)/shard_map/pallas_call | solution.py:178
  53.4 15.4 %shard_map.69 = (bf16[2080,128]{1,0:T(8,128)(2,1)}, f32[8,256,128]{2,1,0:T(8,128)}, f32[8,128]{1,0:T(8,128)}) custom-call(s32[8,288]{1,0:T(8,128)} %shard_map.67.plan_ref, bf16[288,256,128]{2,1,0:T(8,128)(2,1)} %get-tuple-element.13.half_ref, bf16[6,128,128]{2,1,0:T(8,128)(2,1)} %copy-done, bf16[6,128,128]{2,1,0:T(8,128)(2,1)} %copy-done.4, ...), custom_call_target="tpu_custom_call" | custom-call | flops 2415919104 | bytes 22074368 | tf_op jit(solution)/shard_map/pallas_call | solution.py:280
  68.8 1.3 %collective-permute-start.15 = (bf16[2080,128]{1,0:T(8,128)(2,1)}, bf16[2080,128]{1,0:T(8,128)(2,1)S(1)}, u32[]{:S(2)}, u32[]{:S(2)}) collective-permute-start(bf16[2080,128]{1,0:T(8,128)(2,1)} %get-tuple-element.16), channel_id=1, source_target_pairs={{0,1},{1,0},{2,3},{3,2},{4,5},{5,4},{6,7},{7,6},{8,9},{9,8},{10,11... | collective-permute-start | bytes 1597448 | tf_op jit(solution)/shard_map/ppermute | solution.py:18
  70.1 1.8 %collective-permute-done.15.received_ref = bf16[2080,128]{1,0:T(8,128)(2,1)S(1)} collective-permute-done((bf16[2080,128]{1,0:T(8,128)(2,1)}, bf16[2080,128]{1,0:T(8,128)(2,1)S(1)}, u32[]{:S(2)}, u32[]{:S(2)}) %collective-permute-start.15) | collective-permute-done | bytes 532512 | tf_op jit(solution)/shard_map/ppermute | solution.py:18
  71.8 0.8 copy-done.16
  72.6 2.3 %shard_map.70 = (f32[256,128]{1,0:T(8,128)}, f32[8,128]{1,0:T(8,128)}, bf16[8,288,128]{2,1,0:T(8,128)(2,1)}) custom-call(f32[8,256,128]{2,1,0:T(8,128)} %get-tuple-element.14.keep_ref, f32[8,128]{1,0:T(8,128)} %get-tuple-element.15.own_ref, bf16[2080,128]{1,0:T(8,128)(2,1)} %copy-done.16), custom_call_target="tpu_custom_call" | custom-call | tf_op jit(solution)/shard_map/pallas_call | solution.py:329
  75.0 23.0 %all_to_all.5.received_ref = bf16[8,288,128]{2,1,0:T(8,128)(2,1)} all-to-all(bf16[8,288,128]{2,1,0:T(8,128)(2,1)} %get-tuple-element.19), channel_id=1, replica_groups={{0,2,4,6,8,10,12,14},{1,3,5,7,9,11,13,15},{16,18,20,22,24,26,28,30},{17..., dimensions={0} | all-to-all | bytes 1179648 | tf_op jit(solution)/shard_map/all_to_all | solution.py:368
  98.0 1.9 %shard_map.71 = (f32[1,2,128,128]{3,2,1,0:T(8,128)}, f32[2,2]{1,0:T(2,128)}) custom-call(f32[256,128]{1,0:T(8,128)} %get-tuple-element.17.mine_ref, f32[8,128]{1,0:T(8,128)} %get-tuple-element.18.total_ref, bf16[8,288,128]{2,1,0:T(8,128)(2,1)} %all_to_all.5.received_ref), custom_call_target="tpu_custom_call" | custom-call | tf_op jit(solution)/shard_map/pallas_call | solution.py:351
  (9 shorter events, 0.0 us)
Async XLA Ops:
  1.6 34.1 %copy-start = (bf16[6,128,128]{2,1,0:T(8,128)(2,1)}, bf16[6,128,128]{2,1,0:T(8,128)(2,1)S(1)}, u32[]{:S(2)}) copy-start(bf16[6,128,128]{2,1,0:T(8,128)(2,1)S(1)} %pad_maximum_fusion.refs_0_) | copy-start | bytes 589828
  1.6 10.0 %collective-permute-start.3 = (bf16[6,128,128]{2,1,0:T(8,128)(2,1)S(1)}, bf16[6,128,128]{2,1,0:T(8,128)(2,1)S(1)}, u32[]{:S(2)}, u32[]{:S(2)}) collective-permute-start(bf16[6,128,128]{2,1,0:T(8,128)(2,1)S(1)} %pad_maximum_fusion.refs_0_), channel_id=1, source_target_pairs={{0,4},{1,5},{2,6},{3,7},{4,8},{5,9},{6,10},{7,11},{8,12},{9,13},{1... | collective-permute-start | bytes 589832 | tf_op jit(solution)/shard_map/ppermute | solution.py:22
  11.6 24.1 %copy-start.1 = (bf16[6,128,128]{2,1,0:T(8,128)(2,1)}, bf16[6,128,128]{2,1,0:T(8,128)(2,1)S(1)}, u32[]{:S(2)}) copy-start(bf16[6,128,128]{2,1,0:T(8,128)(2,1)S(1)} %collective-permute-done.3.refs_4_) | copy-start | bytes 589828
  11.6 7.9 %collective-permute-start.7 = (bf16[6,128,128]{2,1,0:T(8,128)(2,1)S(1)}, bf16[6,128,128]{2,1,0:T(8,128)(2,1)S(1)}, u32[]{:S(2)}, u32[]{:S(2)}) collective-permute-start(bf16[6,128,128]{2,1,0:T(8,128)(2,1)S(1)} %collective-permute-done.3.refs_4_), channel_id=1, source_target_pairs={{0,4},{1,5},{2,6},{3,7},{4,8},{5,9},{6,10},{7,11},{8,12},{9,13},{1... | collective-permute-start | bytes 589832 | tf_op jit(solution)/shard_map/ppermute | solution.py:22
  11.6 9.2 %collective-permute-start.1 = (bf16[6,128,128]{2,1,0:T(8,128)(2,1)S(1)}, bf16[6,128,128]{2,1,0:T(8,128)(2,1)S(1)}, u32[]{:S(2)}, u32[]{:S(2)}) collective-permute-start(bf16[6,128,128]{2,1,0:T(8,128)(2,1)S(1)} %pad_maximum_fusion.refs_0_), channel_id=1, source_target_pairs={{0,2},{1,3},{2,0},{3,1},{4,6},{5,7},{6,4},{7,5},{8,10},{9,11},{10,... | collective-permute-start | bytes 589832 | tf_op jit(solution)/shard_map/ppermute | solution.py:18
  13.1 8.2 %collective-permute-start = (bf16[6,128,128]{2,1,0:T(8,128)(2,1)S(1)}, bf16[6,128,128]{2,1,0:T(8,128)(2,1)S(1)}, u32[]{:S(2)}, u32[]{:S(2)}) collective-permute-start(bf16[6,128,128]{2,1,0:T(8,128)(2,1)S(1)} %pad_maximum_fusion.refs_0_), channel_id=1, source_target_pairs={{0,1},{1,0},{2,3},{3,2},{4,5},{5,4},{6,7},{7,6},{8,9},{9,8},{10,11... | collective-permute-start | bytes 589832 | tf_op jit(solution)/shard_map/ppermute | solution.py:18
  19.5 16.2 %copy-start.2 = (bf16[6,128,128]{2,1,0:T(8,128)(2,1)}, bf16[6,128,128]{2,1,0:T(8,128)(2,1)S(1)}, u32[]{:S(2)}) copy-start(bf16[6,128,128]{2,1,0:T(8,128)(2,1)S(1)} %collective-permute-done.7.refs_8_) | copy-start | bytes 589828
  19.5 7.5 %collective-permute-start.11 = (bf16[6,128,128]{2,1,0:T(8,128)(2,1)S(1)}, bf16[6,128,128]{2,1,0:T(8,128)(2,1)S(1)}, u32[]{:S(2)}, u32[]{:S(2)}) collective-permute-start(bf16[6,128,128]{2,1,0:T(8,128)(2,1)S(1)} %collective-permute-done.7.refs_8_), channel_id=1, source_target_pairs={{0,4},{1,5},{2,6},{3,7},{4,8},{5,9},{6,10},{7,11},{8,12},{9,13},{1... | collective-permute-start | bytes 589832 | tf_op jit(solution)/shard_map/ppermute | solution.py:22
  19.5 8.7 %collective-permute-start.5 = (bf16[6,128,128]{2,1,0:T(8,128)(2,1)S(1)}, bf16[6,128,128]{2,1,0:T(8,128)(2,1)S(1)}, u32[]{:S(2)}, u32[]{:S(2)}) collective-permute-start(bf16[6,128,128]{2,1,0:T(8,128)(2,1)S(1)} %collective-permute-done.3.refs_4_), channel_id=1, source_target_pairs={{0,2},{1,3},{2,0},{3,1},{4,6},{5,7},{6,4},{7,5},{8,10},{9,11},{10,... | collective-permute-start | bytes 589832 | tf_op jit(solution)/shard_map/ppermute | solution.py:18
  20.7 7.5 %collective-permute-start.4 = (bf16[6,128,128]{2,1,0:T(8,128)(2,1)S(1)}, bf16[6,128,128]{2,1,0:T(8,128)(2,1)S(1)}, u32[]{:S(2)}, u32[]{:S(2)}) collective-permute-start(bf16[6,128,128]{2,1,0:T(8,128)(2,1)S(1)} %collective-permute-done.3.refs_4_), channel_id=1, source_target_pairs={{0,1},{1,0},{2,3},{3,2},{4,5},{5,4},{6,7},{7,6},{8,9},{9,8},{10,11... | collective-permute-start | bytes 589832 | tf_op jit(solution)/shard_map/ppermute | solution.py:18
  20.7 14.9 %copy-start.3 = (bf16[6,128,128]{2,1,0:T(8,128)(2,1)}, bf16[6,128,128]{2,1,0:T(8,128)(2,1)S(1)}, u32[]{:S(2)}) copy-start(bf16[6,128,128]{2,1,0:T(8,128)(2,1)S(1)} %collective-permute-done.1.refs_2_) | copy-start | bytes 589828
  20.8 8.0 %collective-permute-start.2 = (bf16[6,128,128]{2,1,0:T(8,128)(2,1)S(1)}, bf16[6,128,128]{2,1,0:T(8,128)(2,1)S(1)}, u32[]{:S(2)}, u32[]{:S(2)}) collective-permute-start(bf16[6,128,128]{2,1,0:T(8,128)(2,1)S(1)} %collective-permute-done.1.refs_2_), channel_id=1, source_target_pairs={{0,1},{1,0},{2,3},{3,2},{4,5},{5,4},{6,7},{7,6},{8,9},{9,8},{10,11... | collective-permute-start | bytes 589832 | tf_op jit(solution)/shard_map/ppermute | solution.py:18
  21.3 14.4 %copy-start.4 = (bf16[6,128,128]{2,1,0:T(8,128)(2,1)}, bf16[6,128,128]{2,1,0:T(8,128)(2,1)S(1)}, u32[]{:S(2)}) copy-start(bf16[6,128,128]{2,1,0:T(8,128)(2,1)S(1)} %collective-permute-done.refs_1_) | copy-start | bytes 589828
  21.3 9.3 %collective-permute-start.9 = (bf16[6,128,128]{2,1,0:T(8,128)(2,1)S(1)}, bf16[6,128,128]{2,1,0:T(8,128)(2,1)S(1)}, u32[]{:S(2)}, u32[]{:S(2)}) collective-permute-start(bf16[6,128,128]{2,1,0:T(8,128)(2,1)S(1)} %collective-permute-done.7.refs_8_), channel_id=1, source_target_pairs={{0,2},{1,3},{2,0},{3,1},{4,6},{5,7},{6,4},{7,5},{8,10},{9,11},{10,... | collective-permute-start | bytes 589832 | tf_op jit(solution)/shard_map/ppermute | solution.py:18
  26.9 8.8 %copy-start.5 = (bf16[6,128,128]{2,1,0:T(8,128)(2,1)}, bf16[6,128,128]{2,1,0:T(8,128)(2,1)S(1)}, u32[]{:S(2)}) copy-start(bf16[6,128,128]{2,1,0:T(8,128)(2,1)S(1)} %collective-permute-done.11.refs_12_) | copy-start | bytes 589828
  26.9 6.6 %collective-permute-start.13 = (bf16[6,128,128]{2,1,0:T(8,128)(2,1)S(1)}, bf16[6,128,128]{2,1,0:T(8,128)(2,1)S(1)}, u32[]{:S(2)}, u32[]{:S(2)}) collective-permute-start(bf16[6,128,128]{2,1,0:T(8,128)(2,1)S(1)} %collective-permute-done.11.refs_12_), channel_id=1, source_target_pairs={{0,2},{1,3},{2,0},{3,1},{4,6},{5,7},{6,4},{7,5},{8,10},{9,11},{10,... | collective-permute-start | bytes 589832 | tf_op jit(solution)/shard_map/ppermute | solution.py:18
  28.2 7.5 %copy-start.6 = (bf16[6,128,128]{2,1,0:T(8,128)(2,1)}, bf16[6,128,128]{2,1,0:T(8,128)(2,1)S(1)}, u32[]{:S(2)}) copy-start(bf16[6,128,128]{2,1,0:T(8,128)(2,1)S(1)} %collective-permute-done.5.refs_6_) | copy-start | bytes 589828
  28.2 7.4 %collective-permute-start.8 = (bf16[6,128,128]{2,1,0:T(8,128)(2,1)S(1)}, bf16[6,128,128]{2,1,0:T(8,128)(2,1)S(1)}, u32[]{:S(2)}, u32[]{:S(2)}) collective-permute-start(bf16[6,128,128]{2,1,0:T(8,128)(2,1)S(1)} %collective-permute-done.7.refs_8_), channel_id=1, source_target_pairs={{0,1},{1,0},{2,3},{3,2},{4,5},{5,4},{6,7},{7,6},{8,9},{9,8},{10,11... | collective-permute-start | bytes 589832 | tf_op jit(solution)/shard_map/ppermute | solution.py:18
  28.2 7.5 %copy-start.7 = (bf16[6,128,128]{2,1,0:T(8,128)(2,1)}, bf16[6,128,128]{2,1,0:T(8,128)(2,1)S(1)}, u32[]{:S(2)}) copy-start(bf16[6,128,128]{2,1,0:T(8,128)(2,1)S(1)} %collective-permute-done.4.refs_5_) | copy-start | bytes 589828
  28.2 7.3 %collective-permute-start.6 = (bf16[6,128,128]{2,1,0:T(8,128)(2,1)S(1)}, bf16[6,128,128]{2,1,0:T(8,128)(2,1)S(1)}, u32[]{:S(2)}, u32[]{:S(2)}) collective-permute-start(bf16[6,128,128]{2,1,0:T(8,128)(2,1)S(1)} %collective-permute-done.5.refs_6_), channel_id=1, source_target_pairs={{0,1},{1,0},{2,3},{3,2},{4,5},{5,4},{6,7},{7,6},{8,9},{9,8},{10,11... | collective-permute-start | bytes 589832 | tf_op jit(solution)/shard_map/ppermute | solution.py:18
  28.7 7.0 %copy-start.8 = (bf16[6,128,128]{2,1,0:T(8,128)(2,1)}, bf16[6,128,128]{2,1,0:T(8,128)(2,1)S(1)}, u32[]{:S(2)}) copy-start(bf16[6,128,128]{2,1,0:T(8,128)(2,1)S(1)} %collective-permute-done.2.refs_3_) | copy-start | bytes 589828
  28.7 6.9 %collective-permute-start.12 = (bf16[6,128,128]{2,1,0:T(8,128)(2,1)S(1)}, bf16[6,128,128]{2,1,0:T(8,128)(2,1)S(1)}, u32[]{:S(2)}, u32[]{:S(2)}) collective-permute-start(bf16[6,128,128]{2,1,0:T(8,128)(2,1)S(1)} %collective-permute-done.11.refs_12_), channel_id=1, source_target_pairs={{0,1},{1,0},{2,3},{3,2},{4,5},{5,4},{6,7},{7,6},{8,9},{9,8},{10,11... | collective-permute-start | bytes 589832 | tf_op jit(solution)/shard_map/ppermute | solution.py:18
  30.6 5.2 %copy-start.9 = (bf16[6,128,128]{2,1,0:T(8,128)(2,1)}, bf16[6,128,128]{2,1,0:T(8,128)(2,1)S(1)}, u32[]{:S(2)}) copy-start(bf16[6,128,128]{2,1,0:T(8,128)(2,1)S(1)} %collective-permute-done.9.refs_10_) | copy-start | bytes 589828
  30.6 5.0 %collective-permute-start.10 = (bf16[6,128,128]{2,1,0:T(8,128)(2,1)S(1)}, bf16[6,128,128]{2,1,0:T(8,128)(2,1)S(1)}, u32[]{:S(2)}, u32[]{:S(2)}) collective-permute-start(bf16[6,128,128]{2,1,0:T(8,128)(2,1)S(1)} %collective-permute-done.9.refs_10_), channel_id=1, source_target_pairs={{0,1},{1,0},{2,3},{3,2},{4,5},{5,4},{6,7},{7,6},{8,9},{9,8},{10,11... | collective-permute-start | bytes 589832 | tf_op jit(solution)/shard_map/ppermute | solution.py:18
  33.6 2.2 %copy-start.10 = (bf16[6,128,128]{2,1,0:T(8,128)(2,1)}, bf16[6,128,128]{2,1,0:T(8,128)(2,1)S(1)}, u32[]{:S(2)}) copy-start(bf16[6,128,128]{2,1,0:T(8,128)(2,1)S(1)} %collective-permute-done.13.refs_14_) | copy-start | bytes 589828
  33.6 2.1 %collective-permute-start.14 = (bf16[6,128,128]{2,1,0:T(8,128)(2,1)S(1)}, bf16[6,128,128]{2,1,0:T(8,128)(2,1)S(1)}, u32[]{:S(2)}, u32[]{:S(2)}) collective-permute-start(bf16[6,128,128]{2,1,0:T(8,128)(2,1)S(1)} %collective-permute-done.13.refs_14_), channel_id=1, source_target_pairs={{0,1},{1,0},{2,3},{3,2},{4,5},{5,4},{6,7},{7,6},{8,9},{9,8},{10,11... | collective-permute-start | bytes 589832 | tf_op jit(solution)/shard_map/ppermute | solution.py:18
  35.6 0.7 copy-start.11
  35.6 0.7 copy-start.12
  35.6 0.8 copy-start.13
  35.6 0.9 copy-start.14
  36.5 0.7 copy-start.15
  68.8 3.1 %collective-permute-start.15 = (bf16[2080,128]{1,0:T(8,128)(2,1)}, bf16[2080,128]{1,0:T(8,128)(2,1)S(1)}, u32[]{:S(2)}, u32[]{:S(2)}) collective-permute-start(bf16[2080,128]{1,0:T(8,128)(2,1)} %get-tuple-element.16), channel_id=1, source_target_pairs={{0,1},{1,0},{2,3},{3,2},{4,5},{5,4},{6,7},{7,6},{8,9},{9,8},{10,11... | collective-permute-start | bytes 1597448 | tf_op jit(solution)/shard_map/ppermute | solution.py:18
  71.8 0.8 copy-start.16

commit v3 on v0

v3 whole, which is shorter than its diff:
```python
import functools

import jax
import jax.numpy as jnp
from jax import lax
from jax.experimental import pallas as pl
from jax.experimental.pallas import tpu as pltpu
from jax.sharding import PartitionSpec as P

TAIL = 32
PAIRS = 4
GROUP = 2 * PAIRS
SLOTS_AHEAD = 4
TRIALS = 2


def exchange(value, n, mask):
    return lax.ppermute(value, "op", [(i, i ^ mask) for i in range(n)])


def chip_at(place, chips):
    return 2 * place if place < chips // 2 else 2 * (chips - place) - 1


def ring_step(value, n):
    chips = n // 2
    order = [chip_at(place, chips) for place in range(chips)]
    pairs = []
    for place, chip in enumerate(order):
        pairs.append((2 * chip, 2 * order[(place + 1) % chips]))
        pairs.append((2 * chip + 1, 2 * order[(place - 1) % chips] + 1))
    return lax.ppermute(value, "op", pairs)


def place_of(chip, chips):
    half = jnp.floor(chip * 0.5)
    return jnp.where(chip == 2.0 * half, half, chips - 1.0 - half)


def owner_of(step, swapped, half, n):
    chips = n // 2
    me = lax.axis_index("op")
    chip, core = me // 2, lax.rem(me, 2)
    odd = lax.rem(chip, 2)
    mine = jnp.where(odd == 0, chip // 2, chips - 1 - chip // 2)
    line = 1 - core if swapped else core
    place = lax.rem(mine + (2 * line - 1) * step + 2 * chips, chips)
    there = jnp.where(place < chips // 2, 2 * place, 2 * (chips - place) - 1)
    return 2 * there + (line if half == 0 else 1 - line)


def split3(value):
    high = value.astype(jnp.bfloat16)
    rest = value - high.astype(jnp.float32)
    middle = rest.astype(jnp.bfloat16)
    low = (rest - middle.astype(jnp.float32)).astype(jnp.bfloat16)
    zero = jnp.zeros_like(value)
    return jnp.concatenate(
        [high.astype(jnp.float32), middle.astype(jnp.float32), low.astype(jnp.float32), zero], axis=0
    ).astype(jnp.bfloat16)


def join3(tail):
    wide = tail.astype(jnp.float32)
    return wide[0:8] + wide[8:16] + wide[16:24]


def matrix_of(values):
    rows = lax.broadcasted_iota(jnp.int32, (8, 128), 0)
    lanes = lax.broadcasted_iota(jnp.int32, (8, 128), 1)
    total = jnp.zeros((8, 128), jnp.float32)
    for (i, j), value in values.items():
        total = total + jnp.where((rows == i) & (lanes == j), value, 0.0)
    return total


def fold(value):
    return value.reshape(16, 8, 128).sum(axis=0)


def phases_of(n):
    return min(4, n // 4)


def plan_kernel(n, terms, tasks_ref, plan_ref):
    slots = tasks_ref.shape[1]
    places = plan_ref.shape[1]
    chips = n // 2
    phases = phases_of(n)
    steps = chips // 2
    rows = tasks_ref[...].astype(jnp.float32)
    source, target, term, live = rows[0:1], rows[1:2], rows[2:3], rows[3:4]
    me = lax.axis_index("op")
    mine = place_of((jnp.zeros((1, slots), jnp.int32) + me // 2).astype(jnp.float32), float(chips))

    def distance(owner):
        gap = place_of(jnp.floor(owner * 0.5), float(chips)) - mine
        up = jnp.where(gap < 0, gap + chips, gap)
        return jnp.minimum(up, chips - up)

    far = jnp.maximum(distance(source), distance(jnp.floor(term * (n / terms))))
    phase = jnp.maximum(jnp.ceil(far * (phases / steps)), 1.0) - 1.0
    keys = phases * n
    key = jnp.where(live > 0, phase * n + target, float(keys))
    lane = lax.broadcasted_iota(jnp.int32, (1, slots), 1).astype(jnp.float32)

    def column(*values):
        pad = [jnp.zeros((8 - len(values), slots), jnp.float32)]
        return jnp.transpose(jnp.concatenate(list(values) + pad, axis=0))

    columns = column(key, lane, source, term, target)
    key_column, lane_column = columns[:, 0:1], columns[:, 1:2]
    earlier = jnp.where((key_column == key) & (lane_column < lane), 1.0, 0.0)
    place = jnp.sum(earlier, axis=0, keepdims=True)
    index = lax.broadcasted_iota(jnp.int32, (keys, slots), 0).astype(jnp.float32)
    count = jnp.sum(jnp.where(index == key, 1.0, 0.0), axis=1, keepdims=True)
    padded = 2.0 * jnp.floor((count + 1.0) * 0.5)
    number = lax.broadcasted_iota(jnp.int32, (1, places), 1).astype(jnp.float32)
    starts = jnp.zeros((1, places), jnp.float32)
    start = jnp.zeros((1, 1), jnp.float32)
    for p in range(phases):
        part = padded[p * n : (p + 1) * n]
        before = jnp.sum(jnp.where(index[p * n : (p + 1) * n] < key, part, 0.0), axis=0, keepdims=True)
        place = place + jnp.where(phase == p, start + before, 0.0)
        groups = jnp.ceil(jnp.sum(part, axis=0, keepdims=True) / GROUP)
        start = start + groups * GROUP
        starts = starts + jnp.where(number > p, groups, 0.0)
    place = jnp.where(live > 0, place, -1.0)
    place_column = column(place)[:, 0:1]
    at = lax.broadcasted_iota(jnp.int32, (slots, places), 1).astype(jnp.float32)
    hit = place_column == at

    def pick(values, other):
        found = jnp.sum(jnp.where(hit, values - other, 0.0), axis=0, keepdims=True)
        return (found + other).astype(jnp.int32)

    own = (jnp.zeros((1, 1), jnp.int32) + me).astype(jnp.float32)
    plan_ref[0:1] = pick(lane_column, 0.0)
    plan_ref[1:2] = pick(columns[:, 2:3], own)
    plan_ref[2:3] = pick(columns[:, 3:4], float(terms))
    plan_ref[3:4] = pick(columns[:, 4:5], float(n))
    plan_ref[4:5] = starts.astype(jnp.int32)
    plan_ref[5:8] = jnp.zeros((3, places), jnp.int32)


def make_plan(tasks, n, terms):
    slots = tasks.shape[1]
    phases = phases_of(n)
    most = slots + min(slots, phases * n) + phases * GROUP
    return pl.pallas_call(
        functools.partial(plan_kernel, n, terms),
        out_shape=jax.ShapeDtypeStruct((8, -(-most // 128) * 128), jnp.int32),
    )(tasks)


def tasks_kernel(n, terms_per, phase, last, kinds, plan_ref, left_ref, *refs):
    if phase:
        acc_in, corr_in, *refs = refs
    blocks, refs = refs[: len(kinds)], refs[len(kinds) :]
    if last:
        send_ref, keep_ref, own_ref, corr_ref, *refs = refs
    else:
        acc_out, corr_out, *refs = refs
    trial, right, acc, left, block_sem, left_sem, acc_sem = refs
    first, count = plan_ref[4, phase], plan_ref[4, phase + 1] - plan_ref[4, phase]
    per = TRIALS + terms_per

    def block_copies(b):
        step, swapped, unused = kinds[b]
        copies = []
        for half in range(2):
            owner = owner_of(step, swapped, half, n)
            copies.append(
                pltpu.make_async_copy(
                    blocks[b].at[pl.ds(half * per, TRIALS)], trial.at[owner], block_sem.at[b, 2 * half]
                )
            )
            copies.append(
                pltpu.make_async_copy(
                    blocks[b].at[pl.ds(half * per + TRIALS, terms_per)],
                    right.at[pl.ds(owner * terms_per, terms_per)],
                    block_sem.at[b, 2 * half + 1],
                )
            )
        return copies

    def fetch(group):
        at = lax.rem(group, SLOTS_AHEAD)
        for u in range(GROUP):
            slot = plan_ref[0, (first + group) * GROUP + u]
            pltpu.make_async_copy(left_ref.at[slot], left.at[at, u], left_sem.at[at]).start()

    for b in range(len(kinds)):
        for copy in block_copies(b):
            copy.start()
    for group in range(SLOTS_AHEAD - 1):

        @pl.when(group < count)
        def _():
            fetch(group)

    if phase:
        acc_copy = pltpu.make_async_copy(acc_in, acc.at[pl.ds(0, n)], acc_sem)
        acc_copy.start()
    else:

        def clear(s, carry):
            acc[s] = jnp.zeros((256, 128), jnp.float32)
            return carry

        lax.fori_loop(0, n, clear, 0)
    right[n * terms_per] = jnp.zeros((128, 128), jnp.bfloat16)
    for b in range(len(kinds)):
        for copy in block_copies(b):
            copy.wait()
    if phase:
        acc_copy.wait()

    corr = [corr_in[8 * i : 8 * i + 8, :] if phase else jnp.zeros((8, 128), jnp.float32) for i in range(3)]
    for step, swapped, new in kinds:
        for half in range(2) if new else ():
            owner = owner_of(step, swapped, half, n)
            t0, t1 = trial[owner, 0].astype(jnp.float32), trial[owner, 1].astype(jnp.float32)
            corr = [corr[0] + fold(t0 * t0), corr[1] + fold(t0 * t1), corr[2] + fold(t1 * t1)]

    def turn(group, carry):
        @pl.when(group + SLOTS_AHEAD - 1 < count)
        def _():
            fetch(group + SLOTS_AHEAD - 1)

        at = lax.rem(group, SLOTS_AHEAD)
        pltpu.make_async_copy(left_ref.at[pl.ds(0, GROUP)], left.at[at], left_sem.at[at]).wait()
        place = (first + group) * GROUP
        halves = []
        for u in range(GROUP):
            source = plan_ref[1, place + u]
            vectors = jnp.concatenate([trial[source, 0], trial[source, 1]], axis=1)
            half = jnp.dot(left[at, u], vectors, preferred_element_type=jnp.float32)
            halves.append(half.astype(jnp.bfloat16))
        for u in range(0, GROUP, 2):
            one, two = halves[u], halves[u + 1]
            pair = jnp.concatenate(
                [
                    jnp.concatenate([one[:, :128], two[:, :128]], axis=1),
                    jnp.concatenate([one[:, 128:], two[:, 128:]], axis=1),
                ],
                axis=0,
            )
            rights = jnp.concatenate(
                [right[plan_ref[2, place + u]], right[plan_ref[2, place + u + 1]]], axis=1
            )
            term = lax.dot_general(
                pair, rights, (((1,), (1,)), ((), ())), preferred_element_type=jnp.float32
            )
            target = plan_ref[3, place + u]
            acc[target] = acc[target] + term
        return carry

    lax.fori_loop(0, count, turn, 0)
    if not last:
        for i in range(3):
            corr_out[8 * i : 8 * i + 8, :] = corr[i]
        acc_copy = pltpu.make_async_copy(acc.at[pl.ds(0, n)], acc_out, acc_sem)
        acc_copy.start()
        acc_copy.wait()
        return
    c00, c01, c11 = [jnp.sum(x) for x in corr]
    corr_ref[...] = matrix_of({(0, 0): c00, (0, 1): c01, (1, 0): c01, (1, 1): c11})[0:2, 0:2]

    def dots(s, carry):
        t0 = trial[s, 0].astype(jnp.float32)
        t1 = trial[s, 1].astype(jnp.float32)
        a0 = acc[s, 0:128, :]
        a1 = acc[s, 128:256, :]
        p00, p01, p10, p11 = carry
        return p00 + fold(t0 * a0), p01 + fold(t0 * a1), p10 + fold(t1 * a0), p11 + fold(t1 * a1)

    zero = jnp.zeros((8, 128), jnp.float32)
    p00, p01, p10, p11 = [jnp.sum(x) for x in lax.fori_loop(0, n, dots, (zero,) * 4)]
    own = matrix_of({(0, 0): p00, (0, 1): p01, (1, 0): p10, (1, 1): p11})
    own_ref[...] = own
    core = lax.rem(lax.axis_index("op"), 2)

    def pack(j, carry):
        keep_ref[j] = acc[2 * j + core]
        send_ref[pl.ds(pl.multiple_of(j * 256, 256), 256), :] = acc[2 * j + 1 - core].astype(jnp.bfloat16)
        return carry

    lax.fori_loop(0, n // 2, pack, 0)
    send_ref[n // 2 * 256 :, :] = split3(own)


def run_phase(n, phase, plan, left_ops, state, blocks):
    last = phase == phases_of(n) - 1
    slots = left_ops.shape[0]
    terms_per = blocks[0][0].shape[0] // 2 - TRIALS
    kinds = tuple(block[1:] for block in blocks)
    hbm = pl.BlockSpec(memory_space=pltpu.HBM)
    vmem = pl.BlockSpec(memory_space=pltpu.VMEM)
    if last:
        out_shape = (
            jax.ShapeDtypeStruct((n // 2 * 256 + TAIL, 128), jnp.bfloat16),
            jax.ShapeDtypeStruct((n // 2, 256, 128), jnp.float32),
            jax.ShapeDtypeStruct((8, 128), jnp.float32),
            jax.ShapeDtypeStruct((2, 2), jnp.float32),
        )
        out_specs = (vmem,) * 4
    else:
        out_shape = (
            jax.ShapeDtypeStruct((n, 256, 128), jnp.float32),
            jax.ShapeDtypeStruct((24, 128), jnp.float32),
        )
        out_specs = (hbm, vmem)
    share = 4 * slots // (4 * phases_of(n))
    return pl.pallas_call(
        functools.partial(tasks_kernel, n, terms_per, phase, last, kinds),
        out_shape=out_shape,
        in_specs=[pl.BlockSpec(memory_space=pltpu.SMEM), hbm]
        + ([hbm, vmem] if phase else [])
        + [hbm] * len(blocks),
        out_specs=out_specs,
        scratch_shapes=[
            pltpu.VMEM((n, TRIALS, 128, 128), jnp.bfloat16),
            pltpu.VMEM((n * terms_per + 1, 128, 128), jnp.bfloat16),
            pltpu.VMEM((n + 1, 256, 128), jnp.float32),
            pltpu.VMEM((SLOTS_AHEAD, GROUP, 128, 128), jnp.bfloat16),
            pltpu.SemaphoreType.DMA((len(blocks), 4)),
            pltpu.SemaphoreType.DMA((SLOTS_AHEAD,)),
            pltpu.SemaphoreType.DMA,
        ],
        compiler_params=pltpu.CompilerParams(vmem_limit_bytes=n * 640 * 1024 + 10 * 1024 * 1024),
        cost_estimate=pl.CostEstimate(
            flops=share * 8 * 128**3, bytes_accessed=share * 32768 + n * 450000, transcendentals=0
        ),
    )(plan, left_ops, *state, *[block[0] for block in blocks])


def add_kernel(keep_ref, total_ref, received_ref, *outs):
    levels = keep_ref.shape[0] // 2
    send_ref, rest_ref, sum_ref = outs
    total = total_ref[...] + join3(received_ref[2 * levels * 256 :, :])
    sum_ref[...] = total
    y = lax.rem(lax.axis_index("op") // 2, 2)

    def level(z, carry):
        def at(chip):
            rows = pl.ds(pl.multiple_of(chip * 256, 256), 256)
            return keep_ref[chip] + received_ref[rows, :].astype(jnp.float32)

        rest_ref[z] = at(2 * z + y)
        send_ref[pl.ds(pl.multiple_of(z * 256, 256), 256), :] = at(2 * z + 1 - y).astype(jnp.bfloat16)
        return carry

    lax.fori_loop(0, levels, level, 0)
    send_ref[levels * 256 :, :] = split3(total)


def add_core(keep, total, received):
    levels = keep.shape[0] // 2
    return pl.pallas_call(
        add_kernel,
        out_shape=(
            jax.ShapeDtypeStruct((levels * 256 + TAIL, 128), jnp.bfloat16),
            jax.ShapeDtypeStruct((levels, 256, 128), jnp.float32),
            jax.ShapeDtypeStruct((8, 128), jnp.float32),
        ),
    )(keep, total, received)


def level_kernel(rest_ref, total_ref, received_ref, mine_ref, sum_ref, *sends):
    levels = rest_ref.shape[0]
    total = total_ref[...] + join3(received_ref[levels * 256 :, :])
    sum_ref[...] = total
    tail = split3(total)
    here = lax.axis_index("op") // 4
    for r in range(levels):
        z = jnp.bitwise_xor(here, r)
        rows = pl.ds(pl.multiple_of(z * 256, 256), 256)
        value = rest_ref[z] + received_ref[rows, :].astype(jnp.float32)
        if r == 0:
            mine_ref[...] = value
        else:
            sends[r - 1][0:256, :] = value.astype(jnp.bfloat16)
            sends[r - 1][256:, :] = tail


def add_level(rest, total, received):
    levels = rest.shape[0]
    return pl.pallas_call(
        level_kernel,
        out_shape=(jax.ShapeDtypeStruct((256, 128), jnp.float32), jax.ShapeDtypeStruct((8, 128), jnp.float32))
        + (jax.ShapeDtypeStruct((256 + TAIL, 128), jnp.bfloat16),) * (levels - 1),
    )(rest, total, received)


def last_kernel(mine_ref, total_ref, *refs):
    received, (product_ref, projected_ref) = refs[:-2], refs[-2:]
    value, total = mine_ref[...], total_ref[...]
    for ref in received:
        value = value + ref[0:256, :].astype(jnp.float32)
        total = total + join3(ref[256:, :])
    product_ref[0, 0] = value[0:128]
    product_ref[0, 1] = value[128:256]
    projected_ref[...] = total[0:2, 0:2]


def add_all(mine, total, received):
    return pl.pallas_call(
        last_kernel,
        out_shape=(
            jax.ShapeDtypeStruct((1, 2, 128, 128), jnp.float32),
            jax.ShapeDtypeStruct((2, 2), jnp.float32),
        ),
    )(mine, total, *received)


def body(n, trial, left_ops, right_ops, task_list):
    steps = n // 4
    phases = phases_of(n)
    own = (trial[0], right_ops)
    other = [exchange(value, n, 1) for value in own]
    block = jnp.concatenate([*own, *other], axis=0)
    plan = make_plan(task_list.T, n, n * right_ops.shape[0])
    blocks = [(block, 0, False)]
    seen = 0
    state = ()
    phase = 0
    for step in range(1, steps + 1):
        block = ring_step(block, n)
        blocks.append((block, step, False))
        if step < steps:
            blocks.append((exchange(block, n, 1), step, True))
        if step * phases // steps > phase:
            these = [(*entry, b >= seen) for b, entry in enumerate(blocks)]
            state = run_phase(n, phase, plan, left_ops, state, these)
            seen = len(blocks)
            phase += 1
    send, keep, total, correlation = state
    send, rest, total = add_core(keep, total, exchange(send, n, 1))
    mine, total, *sends = add_level(rest, total, exchange(send, n, 2))
    received = [exchange(value, n, 4 * (r + 1)) for r, value in enumerate(sends)]
    product, projected = add_all(mine, total, received)
    return product, correlation, projected


def solution(mesh):
    return jax.shard_map(
        functools.partial(body, mesh.shape["op"]),
        mesh=mesh,
        in_specs=(
            P(("groups", "op"), None, None, None),
            P(("groups", "op"), None, None),
            P(("groups", "op"), None, None),
            P(("groups", "op"), None),
        ),
        out_specs=(P(("groups", "op"), None, None, None), P("groups", None), P("groups", None)),
        check_vma=False,
    )
```

time: 308 us -> 117 us (0.38)
  waiting for transfers between devices: 145 us -> 34.3 us
  matrix products: 82.8 us -> 0 us
  Pallas kernels: 0 us -> 46.1 us
  blocking collectives: 30.1 us -> 0 us
  local copies, waits for them, and re-layouts: 35.3 us -> 7.81 us
  starting transfers between devices: 0.11 us -> 26.6 us
  between operations: 13.8 us -> 0.72 us
    all_gather x2 -> x0, waiting for transfers between devices: 84.6 us -> none  [the longest x1 42.5 us: body(): lax.all_gather(right_ops, 'op', axis=0, tiled=True)]
    dot_general x10 -> x0, matrix products: 82.8 us -> none  [the longest x4 54 us: accumulate(): jnp.einsum('ns,nvad->svad', weights, terms, precision=lax.Precision.HIGHEST)]
    reduce_scatter x1 -> x0, waiting for transfers between devices: 59.4 us -> none  [body(): lax.psum_scatter(partial_sums, 'op', scatter_dimension=0, tiled=True)]
    pallas_call x0 -> x8, Pallas kernels: none -> 46.1 us  [the longest x4 38.1 us: run_phase(): pl.pallas_call(functools.partial(tasks_kernel, n, terms_per, phase, last,...]
    ppermute x0 -> x14, waiting for transfers between devices: none -> 34.3 us  [the longest x10 17.7 us: exchange(): return lax.ppermute(value, 'op', [(i, i ^ mask) for i in range(n)])]
    psum x1 -> x0, blocking collectives: 30.1 us -> none  [body(): lax.psum((correlation_terms, projected_terms), 'op')]
    gather x8 -> x0, local copies, waits for them, and re-layouts: 27.3 us -> none  [the longest x4 17.1 us: slot_terms(): sources = jnp.take(whole_trial, task_rows[:, 0], axis=0)]
    ppermute x0 -> x14, starting transfers between devices: none -> 26.6 us  [the longest x10 17.6 us: exchange(): return lax.ppermute(value, 'op', [(i, i ^ mask) for i in range(n)])]
  transfers between devices with their start and end apart: 3 -> 14, of which waited for: 3 -> 8; matrix products, arithmetic and copies ran while one was open for 0% -> 0% of each run, Pallas kernels for 0% -> 26%
where the time goes in v3:
time: 117 us; the launch traced here: 116 us
  Pallas kernels  46.1 us (39%)
  waiting for transfers between devices  34.3 us (29%)
  starting transfers between devices  26.6 us (23%)
  local copies, waits for them, and re-layouts  7.81 us (7%)
    pallas_call x4, Pallas kernels, run_phase(): pl.pallas_call(functools.partial(tasks_kernel, n, terms_per, phase, last,...  38.1 us
    ppermute x10, waiting for transfers between devices, exchange(): return lax.ppermute(value, 'op', [(i, i ^ mask) for i in range(n)])  17.7 us
    ppermute x10, starting transfers between devices, exchange(): return lax.ppermute(value, 'op', [(i, i ^ mask) for i in range(n)])  17.6 us
    ppermute x4, waiting for transfers between devices, ring_step(): return lax.ppermute(value, 'op', pairs)  16.6 us
    ppermute x4, starting transfers between devices, ring_step(): return lax.ppermute(value, 'op', pairs)  9.04 us
    unnamed x18, local copies, waits for them, and re-layouts  7.81 us
    pallas_call x1, Pallas kernels, add_core(): pl.pallas_call(add_kernel, out_shape=(jax.ShapeDtypeStruct((levels * 256...  2.41 us
  transfers between devices with their start and end apart: 14, of which 8 were waited for; matrix products, arithmetic and copies ran while one was open for 0% of the time, Pallas kernels for 26%

profile of v3, /device:TPU:0, one launch (start us, length us, event | category | flops | bytes accessed | tf_op | source)
XLA Modules:
  0.0 116.4 jit_solution(13740822802485751109)
XLA Ops:
  0.6 0.5 collective-permute-start.1
  1.1 0.1 collective-permute-start
  1.2 1.4 %collective-permute-done = bf16[2,128,128]{2,1,0:T(8,128)(2,1)S(1)} collective-permute-done((bf16[2,128,128]{2,1,0:T(8,128)(2,1)}, bf16[2,128,128]{2,1,0:T(8,128)(2,1)S(1)}, u32[]{:S(2)}, u32[]{:S(2)}) %collective-permute-start) | collective-permute-done | bytes 65568 | tf_op jit(solution)/shard_map/ppermute | solution.py:18
  2.6 0.0 collective-permute-done.1
  2.6 1.0 pad_maximum_fusion.refs_0_.refs_2_
  3.6 2.8 %collective-permute-start.2 = (bf16[12,128,128]{2,1,0:T(8,128)(2,1)S(1)}, bf16[12,128,128]{2,1,0:T(8,128)(2,1)S(1)}, u32[]{:S(2)}, u32[]{:S(2)}) collective-permute-start(bf16[12,128,128]{2,1,0:T(8,128)(2,1)S(1)} %pad_maximum_fusion.refs_0_.refs_2_), channel_id=1, source_target_pairs={{0,4},{1,3},{4,8},{5,1},{8,12},{9,5},{12,14},{13,9},{14,10},{15,13... | collective-permute-start | bytes 1179656 | tf_op jit(solution)/shard_map/ppermute | solution.py:32
  6.4 5.7 %collective-permute-done.2.refs_1_.refs_3_ = bf16[12,128,128]{2,1,0:T(8,128)(2,1)S(1)} collective-permute-done((bf16[12,128,128]{2,1,0:T(8,128)(2,1)S(1)}, bf16[12,128,128]{2,1,0:T(8,128)(2,1)S(1)}, u32[]{:S(2)}, u32[]{:S(2)}) %collective-permute-start.2) | collective-permute-done | bytes 393248 | tf_op jit(solution)/shard_map/ppermute | solution.py:32
  12.1 2.1 %collective-permute-start.4 = (bf16[12,128,128]{2,1,0:T(8,128)(2,1)S(1)}, bf16[12,128,128]{2,1,0:T(8,128)(2,1)S(1)}, u32[]{:S(2)}, u32[]{:S(2)}) collective-permute-start(bf16[12,128,128]{2,1,0:T(8,128)(2,1)S(1)} %collective-permute-done.2.refs_1_.refs_3_), channel_id=1, source_target_pairs={{0,4},{1,3},{4,8},{5,1},{8,12},{9,5},{12,14},{13,9},{14,10},{15,13... | collective-permute-start | bytes 1179656 | tf_op jit(solution)/shard_map/ppermute | solution.py:32
  14.2 5.7 %collective-permute-done.4.refs_5_ = bf16[12,128,128]{2,1,0:T(8,128)(2,1)S(1)} collective-permute-done((bf16[12,128,128]{2,1,0:T(8,128)(2,1)S(1)}, bf16[12,128,128]{2,1,0:T(8,128)(2,1)S(1)}, u32[]{:S(2)}, u32[]{:S(2)}) %collective-permute-start.4) | collective-permute-done | bytes 393248 | tf_op jit(solution)/shard_map/ppermute | solution.py:32
  19.9 2.1 %collective-permute-start.6 = (bf16[12,128,128]{2,1,0:T(8,128)(2,1)S(1)}, bf16[12,128,128]{2,1,0:T(8,128)(2,1)S(1)}, u32[]{:S(2)}, u32[]{:S(2)}) collective-permute-start(bf16[12,128,128]{2,1,0:T(8,128)(2,1)S(1)} %collective-permute-done.4.refs_5_), channel_id=1, source_target_pairs={{0,4},{1,3},{4,8},{5,1},{8,12},{9,5},{12,14},{13,9},{14,10},{15,13... | collective-permute-start | bytes 1179656 | tf_op jit(solution)/shard_map/ppermute | solution.py:32
  21.9 0.0 collective-permute-start.3
  21.9 0.5 collective-permute-start.5
  22.5 5.2 %collective-permute-done.6.refs_7_ = bf16[12,128,128]{2,1,0:T(8,128)(2,1)S(1)} collective-permute-done((bf16[12,128,128]{2,1,0:T(8,128)(2,1)S(1)}, bf16[12,128,128]{2,1,0:T(8,128)(2,1)S(1)}, u32[]{:S(2)}, u32[]{:S(2)}) %collective-permute-start.6) | collective-permute-done | bytes 393248 | tf_op jit(solution)/shard_map/ppermute | solution.py:32
  27.6 0.0 collective-permute-start.7
  27.6 2.1 %collective-permute-start.8 = (bf16[12,128,128]{2,1,0:T(8,128)(2,1)S(1)}, bf16[12,128,128]{2,1,0:T(8,128)(2,1)S(1)}, u32[]{:S(2)}, u32[]{:S(2)}) collective-permute-start(bf16[12,128,128]{2,1,0:T(8,128)(2,1)S(1)} %collective-permute-done.6.refs_7_), channel_id=1, source_target_pairs={{0,4},{1,3},{4,8},{5,1},{8,12},{9,5},{12,14},{13,9},{14,10},{15,13... | collective-permute-start | bytes 1179656 | tf_op jit(solution)/shard_map/ppermute | solution.py:32
  29.7 2.0 %shard_map.67.plan_ref = s32[8,384]{1,0:T(8,128)} custom-call(s32[4,256]{1,0:T(4,128)} %bitcast.4), custom_call_target="tpu_custom_call" | custom-call | tf_op jit(solution)/shard_map/pallas_call | solution.py:150
  31.7 0.0 collective-permute-done.3.refs_2_.refs_4_
  31.7 0.0 copy-start
  31.7 3.4 %copy-done = bf16[256,128,128]{2,1,0:T(8,128)(2,1)S(1)} copy-done((bf16[256,128,128]{2,1,0:T(8,128)(2,1)S(1)}, bf16[256,128,128]{2,1,0:T(8,128)(2,1)}, u32[]{:S(2)}) %copy-start) | copy-done | bytes 8388632
  35.1 0.0 copy-start.2
  35.1 0.7 copy-done.2
  35.8 6.2 %shard_map.68 = (f32[16,256,128]{2,1,0:T(8,128)S(1)}, f32[24,128]{1,0:T(8,128)S(1)}) custom-call(s32[8,384]{1,0:T(8,128)S(1)} %copy-done.2, bf16[256,128,128]{2,1,0:T(8,128)(2,1)S(1)} %copy-done, bf16[12,128,128]{2,1,0:T(8,128)(2,1)S(1)} %pad_maximum_fusion.refs_0_.refs_2_, bf16[12,128,128]{2,1,0:T(8,128)(2,1)S(1)} %collective-permute-done.2.refs_1_.refs_3_, ...), custom_call_target="tpu_custom_call" | custom-call | flops 1073741824 | bytes 9297152 | tf_op jit(solution)/shard_map/pallas_call | solution.py:315
  42.1 0.0 collective-permute-done.5.refs_6_
  42.1 9.0 %shard_map.69 = (f32[16,256,128]{2,1,0:T(8,128)S(1)}, f32[24,128]{1,0:T(8,128)S(1)}) custom-call(s32[8,384]{1,0:T(8,128)S(1)} %copy-done.2, bf16[256,128,128]{2,1,0:T(8,128)(2,1)S(1)} %copy-done, f32[16,256,128]{2,1,0:T(8,128)S(1)} %get-tuple-element.23.refs_0_, f32[24,128]{1,0:T(8,128)S(1)} %get-tuple-element.24.refs_1_, ...), custom_call_target="tpu_custom_call" | custom-call | flops 1073741824 | bytes 9297152 | tf_op jit(solution)/shard_map/pallas_call | solution.py:315
  51.1 0.0 collective-permute-done.7.refs_8_
  51.1 12.6 %shard_map.70 = (f32[16,256,128]{2,1,0:T(8,128)S(1)}, f32[24,128]{1,0:T(8,128)S(1)}) custom-call(s32[8,384]{1,0:T(8,128)S(1)} %copy-done.2, bf16[256,128,128]{2,1,0:T(8,128)(2,1)S(1)} %copy-done, f32[16,256,128]{2,1,0:T(8,128)S(1)} %get-tuple-element.25.refs_0_, f32[24,128]{1,0:T(8,128)S(1)} %get-tuple-element.26.refs_1_, ...), custom_call_target="tpu_custom_call" | custom-call | flops 1073741824 | bytes 9297152 | tf_op jit(solution)/shard_map/pallas_call | solution.py:315
  63.7 0.0 collective-permute-done.8.refs_9_
  63.7 10.2 %shard_map.71 = (bf16[2080,128]{1,0:T(8,128)(2,1)S(1)}, f32[8,256,128]{2,1,0:T(8,128)S(1)}, f32[8,128]{1,0:T(8,128)S(1)}, f32[2,2]{1,0:T(2,128)}) custom-call(s32[8,384]{1,0:T(8,128)S(1)} %copy-done.2, bf16[256,128,128]{2,1,0:T(8,128)(2,1)S(1)} %copy-done, f32[16,256,128]{2,1,0:T(8,128)S(1)} %get-tuple-element.27.refs_0_, ...), custom_call_target="tpu_custom_call" | custom-call | flops 1073741824 | bytes 9297152 | tf_op jit(solution)/shard_map/pallas_call | solution.py:315
  73.9 0.0 copy-start.1
  74.0 1.0 copy-done.1
  74.9 0.0 copy-start.3
  74.9 0.6 copy-done.3
  75.5 5.2 %collective-permute-start.9 = (bf16[2080,128]{1,0:T(8,128)(2,1)S(1)}, bf16[2080,128]{1,0:T(8,128)(2,1)S(1)}, u32[]{:S(2)}, u32[]{:S(2)}) collective-permute-start(bf16[2080,128]{1,0:T(8,128)(2,1)S(1)} %get-tuple-element.31), channel_id=1, source_target_pairs={{0,1},{1,0},{2,3},{3,2},{4,5},{5,4},{6,7},{7,6},{8,9},{9,8},{10,11... | collective-permute-start | bytes 1597448 | tf_op jit(solution)/shard_map/ppermute | solution.py:18
  80.7 1.5 %collective-permute-done.9.received_ref = bf16[2080,128]{1,0:T(8,128)(2,1)S(1)} collective-permute-done((bf16[2080,128]{1,0:T(8,128)(2,1)S(1)}, bf16[2080,128]{1,0:T(8,128)(2,1)S(1)}, u32[]{:S(2)}, u32[]{:S(2)}) %collective-permute-start.9) | collective-permute-done | bytes 532512 | tf_op jit(solution)/shard_map/ppermute | solution.py:18
  82.2 0.0 copy-start.4
  82.2 0.8 copy-done.4
  83.0 2.4 %shard_map.72 = (bf16[1056,128]{1,0:T(8,128)(2,1)}, f32[4,256,128]{2,1,0:T(8,128)}, f32[8,128]{1,0:T(8,128)}) custom-call(f32[8,256,128]{2,1,0:T(8,128)} %copy-done.1, f32[8,128]{1,0:T(8,128)} %copy-done.3, bf16[2080,128]{1,0:T(8,128)(2,1)} %copy-done.4), custom_call_target="tpu_custom_call" | custom-call | tf_op jit(solution)/shard_map/pallas_call | solution.py:360
  85.5 0.0 collective-permute-start.10
  85.5 9.0 %collective-permute-done.10.received_ref = bf16[1056,128]{1,0:T(8,128)(2,1)S(1)} collective-permute-done((bf16[1056,128]{1,0:T(8,128)(2,1)}, bf16[1056,128]{1,0:T(8,128)(2,1)S(1)}, u32[]{:S(2)}, u32[]{:S(2)}) %collective-permute-start.10) | collective-permute-done | bytes 270368 | tf_op jit(solution)/shard_map/ppermute | solution.py:18
  94.4 0.0 copy-start.5
  94.4 0.7 copy-done.5
  95.1 1.9 %shard_map.73 = (f32[256,128]{1,0:T(8,128)}, f32[8,128]{1,0:T(8,128)}, bf16[288,128]{1,0:T(8,128)(2,1)}, bf16[288,128]{1,0:T(8,128)(2,1)}, bf16[288,128]{1,0:T(8,128)(2,1)}) custom-call(f32[4,256,128]{2,1,0:T(8,128)} %get-tuple-element.32.rest_ref, f32[8,128]{1,0:T(8,128)} %get-tuple-element.33.total_ref, bf16[1056,128]{1,0:T(8,128)(2,1)} %copy-done.5), custom_call_target="tpu_custom_call" | custom-call | tf_op jit(solution)/shard_map/pallas_call | solution.py:389
  97.0 8.9 %collective-permute-start.11 = (bf16[288,128]{1,0:T(8,128)(2,1)}, bf16[288,128]{1,0:T(8,128)(2,1)S(1)}, u32[]{:S(2)}, u32[]{:S(2)}) collective-permute-start(bf16[288,128]{1,0:T(8,128)(2,1)} %get-tuple-element.37), channel_id=1, source_target_pairs={{0,4},{1,5},{2,6},{3,7},{4,0},{5,1},{6,2},{7,3},{8,12},{9,13},{10,... | collective-permute-start | bytes 221192 | tf_op jit(solution)/shard_map/ppermute | solution.py:18
  105.9 0.0 collective-permute-start.12
  105.9 2.4 %collective-permute-start.13 = (bf16[288,128]{1,0:T(8,128)(2,1)}, bf16[288,128]{1,0:T(8,128)(2,1)S(1)}, u32[]{:S(2)}, u32[]{:S(2)}) collective-permute-start(bf16[288,128]{1,0:T(8,128)(2,1)} %get-tuple-element.39), channel_id=1, source_target_pairs={{0,12},{1,13},{2,14},{3,15},{4,8},{5,9},{6,10},{7,11},{8,4},{9,5},... | collective-permute-start | bytes 221192 | tf_op jit(solution)/shard_map/ppermute | solution.py:18
  108.3 0.5 collective-permute-done.11.refs_0_
  108.8 0.0 copy-start.6
  108.8 5.2 %collective-permute-done.12.refs_1_ = bf16[288,128]{1,0:T(8,128)(2,1)S(1)} collective-permute-done((bf16[288,128]{1,0:T(8,128)(2,1)}, bf16[288,128]{1,0:T(8,128)(2,1)S(1)}, u32[]{:S(2)}, u32[]{:S(2)}) %collective-permute-start.12) | collective-permute-done | bytes 73760 | tf_op jit(solution)/shard_map/ppermute | solution.py:18
  114.1 0.0 copy-start.7
  114.1 0.0 collective-permute-done.13.refs_2_
  114.1 0.0 copy-start.8
  114.1 0.0 copy-done.6
  114.1 0.6 copy-done.7
  114.7 0.0 copy-done.8
  114.7 1.7 %shard_map.74 = (f32[1,2,128,128]{3,2,1,0:T(8,128)}, f32[2,2]{1,0:T(2,128)}) custom-call(f32[256,128]{1,0:T(8,128)} %get-tuple-element.35.mine_ref, f32[8,128]{1,0:T(8,128)} %get-tuple-element.36.total_ref, bf16[288,128]{1,0:T(8,128)(2,1)} %copy-done.6, bf16[288,128]{1,0:T(8,128)(2,1)} %copy-done.7, bf16[288,128]{1,0:T(8,128)(2,1)} %copy-done.8), custom_call_target="tpu_custom_call" | custom-call | tf_op jit(solution)/shard_map/pallas_call | solution.py:408
Async XLA Ops:
  0.6 2.0 %collective-permute-start.1 = (bf16[4,128,128]{2,1,0:T(8,128)(2,1)}, bf16[4,128,128]{2,1,0:T(8,128)(2,1)S(1)}, u32[]{:S(2)}, u32[]{:S(2)}) collective-permute-start(bf16[4,128,128]{2,1,0:T(8,128)(2,1)} %param.6), channel_id=1, source_target_pairs={{0,1},{1,0},{2,3},{3,2},{4,5},{5,4},{6,7},{7,6},{8,9},{9,8},{10,11... | collective-permute-start | bytes 393224 | tf_op jit(solution)/shard_map/ppermute | solution.py:18
  1.1 1.5 %collective-permute-start = (bf16[2,128,128]{2,1,0:T(8,128)(2,1)}, bf16[2,128,128]{2,1,0:T(8,128)(2,1)S(1)}, u32[]{:S(2)}, u32[]{:S(2)}) collective-permute-start(bf16[2,128,128]{2,1,0:T(8,128)(2,1)} %bitcast.2), channel_id=1, source_target_pairs={{0,1},{1,0},{2,3},{3,2},{4,5},{5,4},{6,7},{7,6},{8,9},{9,8},{10,11... | collective-permute-start | bytes 196616 | tf_op jit(solution)/shard_map/ppermute | solution.py:18
  3.6 8.5 %collective-permute-start.2 = (bf16[12,128,128]{2,1,0:T(8,128)(2,1)S(1)}, bf16[12,128,128]{2,1,0:T(8,128)(2,1)S(1)}, u32[]{:S(2)}, u32[]{:S(2)}) collective-permute-start(bf16[12,128,128]{2,1,0:T(8,128)(2,1)S(1)} %pad_maximum_fusion.refs_0_.refs_2_), channel_id=1, source_target_pairs={{0,4},{1,3},{4,8},{5,1},{8,12},{9,5},{12,14},{13,9},{14,10},{15,13... | collective-permute-start | bytes 1179656 | tf_op jit(solution)/shard_map/ppermute | solution.py:32
  12.1 7.8 %collective-permute-start.4 = (bf16[12,128,128]{2,1,0:T(8,128)(2,1)S(1)}, bf16[12,128,128]{2,1,0:T(8,128)(2,1)S(1)}, u32[]{:S(2)}, u32[]{:S(2)}) collective-permute-start(bf16[12,128,128]{2,1,0:T(8,128)(2,1)S(1)} %collective-permute-done.2.refs_1_.refs_3_), channel_id=1, source_target_pairs={{0,4},{1,3},{4,8},{5,1},{8,12},{9,5},{12,14},{13,9},{14,10},{15,13... | collective-permute-start | bytes 1179656 | tf_op jit(solution)/shard_map/ppermute | solution.py:32
  19.9 7.8 %collective-permute-start.6 = (bf16[12,128,128]{2,1,0:T(8,128)(2,1)S(1)}, bf16[12,128,128]{2,1,0:T(8,128)(2,1)S(1)}, u32[]{:S(2)}, u32[]{:S(2)}) collective-permute-start(bf16[12,128,128]{2,1,0:T(8,128)(2,1)S(1)} %collective-permute-done.4.refs_5_), channel_id=1, source_target_pairs={{0,4},{1,3},{4,8},{5,1},{8,12},{9,5},{12,14},{13,9},{14,10},{15,13... | collective-permute-start | bytes 1179656 | tf_op jit(solution)/shard_map/ppermute | solution.py:32
  21.9 9.8 %collective-permute-start.3 = (bf16[12,128,128]{2,1,0:T(8,128)(2,1)S(1)}, bf16[12,128,128]{2,1,0:T(8,128)(2,1)S(1)}, u32[]{:S(2)}, u32[]{:S(2)}) collective-permute-start(bf16[12,128,128]{2,1,0:T(8,128)(2,1)S(1)} %collective-permute-done.2.refs_1_.refs_3_), channel_id=1, source_target_pairs={{0,1},{1,0},{2,3},{3,2},{4,5},{5,4},{6,7},{7,6},{8,9},{9,8},{10,11... | collective-permute-start | bytes 1179656 | tf_op jit(solution)/shard_map/ppermute | solution.py:18
  21.9 20.1 %collective-permute-start.5 = (bf16[12,128,128]{2,1,0:T(8,128)(2,1)S(1)}, bf16[12,128,128]{2,1,0:T(8,128)(2,1)S(1)}, u32[]{:S(2)}, u32[]{:S(2)}) collective-permute-start(bf16[12,128,128]{2,1,0:T(8,128)(2,1)S(1)} %collective-permute-done.4.refs_5_), channel_id=1, source_target_pairs={{0,1},{1,0},{2,3},{3,2},{4,5},{5,4},{6,7},{7,6},{8,9},{9,8},{10,11... | collective-permute-start | bytes 1179656 | tf_op jit(solution)/shard_map/ppermute | solution.py:18
  27.6 23.4 %collective-permute-start.7 = (bf16[12,128,128]{2,1,0:T(8,128)(2,1)S(1)}, bf16[12,128,128]{2,1,0:T(8,128)(2,1)S(1)}, u32[]{:S(2)}, u32[]{:S(2)}) collective-permute-start(bf16[12,128,128]{2,1,0:T(8,128)(2,1)S(1)} %collective-permute-done.6.refs_7_), channel_id=1, source_target_pairs={{0,1},{1,0},{2,3},{3,2},{4,5},{5,4},{6,7},{7,6},{8,9},{9,8},{10,11... | collective-permute-start | bytes 1179656 | tf_op jit(solution)/shard_map/ppermute | solution.py:18
  27.6 36.0 %collective-permute-start.8 = (bf16[12,128,128]{2,1,0:T(8,128)(2,1)S(1)}, bf16[12,128,128]{2,1,0:T(8,128)(2,1)S(1)}, u32[]{:S(2)}, u32[]{:S(2)}) collective-permute-start(bf16[12,128,128]{2,1,0:T(8,128)(2,1)S(1)} %collective-permute-done.6.refs_7_), channel_id=1, source_target_pairs={{0,4},{1,3},{4,8},{5,1},{8,12},{9,5},{12,14},{13,9},{14,10},{15,13... | collective-permute-start | bytes 1179656 | tf_op jit(solution)/shard_map/ppermute | solution.py:32
  31.7 3.4 %copy-start = (bf16[256,128,128]{2,1,0:T(8,128)(2,1)S(1)}, bf16[256,128,128]{2,1,0:T(8,128)(2,1)}, u32[]{:S(2)}) copy-start(bf16[256,128,128]{2,1,0:T(8,128)(2,1)} %left_ref.7) | copy-start | bytes 25165828
  35.1 0.7 copy-start.2
  73.9 1.0 copy-start.1
  74.9 0.6 copy-start.3
  75.5 6.7 %collective-permute-start.9 = (bf16[2080,128]{1,0:T(8,128)(2,1)S(1)}, bf16[2080,128]{1,0:T(8,128)(2,1)S(1)}, u32[]{:S(2)}, u32[]{:S(2)}) collective-permute-start(bf16[2080,128]{1,0:T(8,128)(2,1)S(1)} %get-tuple-element.31), channel_id=1, source_target_pairs={{0,1},{1,0},{2,3},{3,2},{4,5},{5,4},{6,7},{7,6},{8,9},{9,8},{10,11... | collective-permute-start | bytes 1597448 | tf_op jit(solution)/shard_map/ppermute | solution.py:18
  82.2 0.8 copy-start.4
  85.5 9.0 %collective-permute-start.10 = (bf16[1056,128]{1,0:T(8,128)(2,1)}, bf16[1056,128]{1,0:T(8,128)(2,1)S(1)}, u32[]{:S(2)}, u32[]{:S(2)}) collective-permute-start(bf16[1056,128]{1,0:T(8,128)(2,1)} %get-tuple-element.34), channel_id=1, source_target_pairs={{0,2},{1,3},{2,0},{3,1},{4,6},{5,7},{6,4},{7,5},{8,10},{9,11},{10,... | collective-permute-start | bytes 811016 | tf_op jit(solution)/shard_map/ppermute | solution.py:18
  94.4 0.7 copy-start.5
  97.0 11.8 %collective-permute-start.11 = (bf16[288,128]{1,0:T(8,128)(2,1)}, bf16[288,128]{1,0:T(8,128)(2,1)S(1)}, u32[]{:S(2)}, u32[]{:S(2)}) collective-permute-start(bf16[288,128]{1,0:T(8,128)(2,1)} %get-tuple-element.37), channel_id=1, source_target_pairs={{0,4},{1,5},{2,6},{3,7},{4,0},{5,1},{6,2},{7,3},{8,12},{9,13},{10,... | collective-permute-start | bytes 221192 | tf_op jit(solution)/shard_map/ppermute | solution.py:18
  105.9 8.1 %collective-permute-start.12 = (bf16[288,128]{1,0:T(8,128)(2,1)}, bf16[288,128]{1,0:T(8,128)(2,1)S(1)}, u32[]{:S(2)}, u32[]{:S(2)}) collective-permute-start(bf16[288,128]{1,0:T(8,128)(2,1)} %get-tuple-element.38), channel_id=1, source_target_pairs={{0,8},{1,9},{2,10},{3,11},{4,12},{5,13},{6,14},{7,15},{8,0},{9,1},... | collective-permute-start | bytes 221192 | tf_op jit(solution)/shard_map/ppermute | solution.py:18
  105.9 8.1 %collective-permute-start.13 = (bf16[288,128]{1,0:T(8,128)(2,1)}, bf16[288,128]{1,0:T(8,128)(2,1)S(1)}, u32[]{:S(2)}, u32[]{:S(2)}) collective-permute-start(bf16[288,128]{1,0:T(8,128)(2,1)} %get-tuple-element.39), channel_id=1, source_target_pairs={{0,12},{1,13},{2,14},{3,15},{4,8},{5,9},{6,10},{7,11},{8,4},{9,5},... | collective-permute-start | bytes 221192 | tf_op jit(solution)/shard_map/ppermute | solution.py:18
  108.8 5.2 %copy-start.6 = (bf16[288,128]{1,0:T(8,128)(2,1)}, bf16[288,128]{1,0:T(8,128)(2,1)S(1)}, u32[]{:S(2)}) copy-start(bf16[288,128]{1,0:T(8,128)(2,1)S(1)} %collective-permute-done.11.refs_0_) | copy-start | bytes 221188
  114.1 0.6 copy-start.7
  114.1 0.6 copy-start.8

commit v4 on v1

v4 whole, which is shorter than its diff:
```python
import functools

import jax
import jax.numpy as jnp
from jax import lax
from jax.experimental import pallas as pl
from jax.experimental.pallas import tpu as pltpu
from jax.sharding import PartitionSpec as P

VMEM_LIMIT = 56 * 1024 * 1024
TAIL = 32
TRIALS = 2
CHUNK = 16
PAIRS = 8
AHEAD = 3


def exchange(value, n, mask):
    return lax.ppermute(value, "op", [(i, i ^ mask) for i in range(n)])


def chip_at(place, chips):
    return 2 * place if place < chips // 2 else 2 * (chips - place) - 1


def ring_step(value, n):
    chips = n // 2
    order = [chip_at(place, chips) for place in range(chips)]
    pairs = []
    for place, chip in enumerate(order):
        pairs.append((2 * chip, 2 * order[(place + 1) % chips]))
        pairs.append((2 * chip + 1, 2 * order[(place - 1) % chips] + 1))
    return lax.ppermute(value, "op", pairs)


def owner_of(step, swapped, half, n):
    chips = n // 2
    me = lax.axis_index("op")
    chip, core = me // 2, lax.rem(me, 2)
    odd = lax.rem(chip, 2)
    mine = jnp.where(odd == 0, chip // 2, chips - 1 - chip // 2)
    line = 1 - core if swapped else core
    place = lax.rem(mine + (2 * line - 1) * step + 2 * chips, chips)
    there = jnp.where(place < chips // 2, 2 * place, 2 * (chips - place) - 1)
    return 2 * there + (line if half == 0 else 1 - line)


def split3(value):
    high = value.astype(jnp.bfloat16)
    rest = value - high.astype(jnp.float32)
    middle = rest.astype(jnp.bfloat16)
    low = (rest - middle.astype(jnp.float32)).astype(jnp.bfloat16)
    zero = jnp.zeros_like(value)
    return jnp.concatenate(
        [high.astype(jnp.float32), middle.astype(jnp.float32), low.astype(jnp.float32), zero], axis=0
    ).astype(jnp.bfloat16)


def join3(tail):
    wide = tail.astype(jnp.float32)
    return wide[0:8] + wide[8:16] + wide[16:24]


def matrix_of(values):
    rows = lax.broadcasted_iota(jnp.int32, (8, 128), 0)
    lanes = lax.broadcasted_iota(jnp.int32, (8, 128), 1)
    total = jnp.zeros((8, 128), jnp.float32)
    for (i, j), value in values.items():
        total = total + jnp.where((rows == i) & (lanes == j), value, 0.0)
    return total


def fold(value):
    return value.reshape(16, 8, 128).sum(axis=0)


def run_of(slots, n):
    return 4 if slots >= 8 * n else 2


def plan_kernel(n, terms, tasks_ref, plan_ref):
    slots = tasks_ref.shape[1]
    places = plan_ref.shape[1]
    rows = tasks_ref[...].astype(jnp.float32)
    source, target, term, live = rows[0:1], rows[1:2], rows[2:3], rows[3:4]
    lane = lax.broadcasted_iota(jnp.int32, (1, slots), 1).astype(jnp.float32)
    number = lax.broadcasted_iota(jnp.int32, (1, places), 1).astype(jnp.float32)
    at = lax.broadcasted_iota(jnp.int32, (slots, places), 1).astype(jnp.float32)
    index = lax.broadcasted_iota(jnp.int32, (n, slots), 0).astype(jnp.float32)

    def column(*values):
        pad = [jnp.zeros((8 - len(values), slots), jnp.float32)]
        return jnp.transpose(jnp.concatenate(list(values) + pad, axis=0))

    def sort(sector, unit):
        key = jnp.where(live > 0, sector, float(n))
        columns = column(key, lane)
        earlier = jnp.where((columns[:, 0:1] == key) & (columns[:, 1:2] < lane), 1.0, 0.0)
        count = jnp.sum(jnp.where(index == key, 1.0, 0.0), axis=1, keepdims=True)
        padded = jnp.ceil(count / unit) * unit
        before = jnp.sum(jnp.where(index < key, padded, 0.0), axis=0, keepdims=True)
        place = before + jnp.sum(earlier, axis=0, keepdims=True)
        return jnp.where(live > 0, place, -1.0), jnp.sum(padded, axis=0, keepdims=True)

    by_source, source_places = sort(source, float(run_of(slots, n)))
    by_target, target_places = sort(target, 2.0)
    columns = column(by_source, by_target, lane, source, term, target)

    def picker(places_column):
        hit = places_column == at

        def pick(values, other):
            found = jnp.sum(jnp.where(hit, values - other, 0.0), axis=0, keepdims=True)
            return (found + other).astype(jnp.int32)

        return pick

    pick = picker(columns[:, 0:1])
    plan_ref[0:1] = pick(columns[:, 2:3], 0.0)
    plan_ref[1:2] = pick(columns[:, 3:4], 0.0)
    pick = picker(columns[:, 1:2])
    plan_ref[2:3] = pick(columns[:, 0:1], 0.0)
    plan_ref[3:4] = pick(columns[:, 4:5], float(terms))
    plan_ref[4:5] = pick(columns[:, 5:6], float(n))
    turns = jnp.where(
        number == 0, jnp.ceil(source_places / CHUNK), jnp.ceil(target_places / (2 * PAIRS))
    )
    plan_ref[5:6] = turns.astype(jnp.int32)
    plan_ref[6:8] = jnp.zeros((2, places), jnp.int32)


def make_plan(tasks, n, terms):
    slots = tasks.shape[1]
    most = slots + min(slots, n) * (run_of(slots, n) - 1) + CHUNK
    return pl.pallas_call(
        functools.partial(plan_kernel, n, terms),
        out_shape=jax.ShapeDtypeStruct((8, -(-most // 128) * 128), jnp.int32),
    )(tasks)


def tasks_kernel(n, terms_per, kinds, plan_ref, left_ref, *refs):
    blocks, refs = refs[: len(kinds)], refs[len(kinds) :]
    send_ref, keep_ref, own_ref, trial, right, acc, left, halves, block_sem, left_sem = refs
    per = TRIALS + terms_per
    run = run_of(left_ref.shape[0], n)
    source_turns, target_turns = plan_ref[5, 0], plan_ref[5, 1]

    def block_copies(b, which):
        step, swapped = kinds[b]
        copies = []
        for half in range(2):
            owner = owner_of(step, swapped, half, n)
            if which == 0:
                source, to = blocks[b].at[pl.ds(half * per, TRIALS)], trial.at[owner]
            else:
                source = blocks[b].at[pl.ds(half * per + TRIALS, terms_per)]
                to = right.at[pl.ds(owner * terms_per, terms_per)]
            copies.append(pltpu.make_async_copy(source, to, block_sem.at[b, 2 * half + which]))
        return copies

    def fetch(turn):
        at = lax.rem(turn, AHEAD)
        for u in range(CHUNK):
            slot = plan_ref[0, turn * CHUNK + u]
            pltpu.make_async_copy(left_ref.at[slot], left.at[at, u], left_sem.at[at]).start()

    for b in range(len(kinds)):
        for copy in block_copies(b, 0):
            copy.start()
    for turn in range(AHEAD - 1):

        @pl.when(turn < source_turns)
        def _():
            fetch(turn)

    for b in range(len(kinds)):
        for copy in block_copies(b, 1):
            copy.start()
    right[n * terms_per] = jnp.zeros((128, 128), jnp.bfloat16)

    def clear(s, carry):
        acc[s] = jnp.zeros((256, 128), jnp.float32)
        return carry

    lax.fori_loop(0, n, clear, 0)
    for b in range(len(kinds)):
        for copy in block_copies(b, 0):
            copy.wait()

    def source_turn(turn, carry):
        @pl.when(turn + AHEAD - 1 < source_turns)
        def _():
            fetch(turn + AHEAD - 1)

        at = lax.rem(turn, AHEAD)
        pltpu.make_async_copy(left_ref.at[pl.ds(0, CHUNK)], left.at[at], left_sem.at[at]).wait()
        first = turn * CHUNK
        for r in range(CHUNK // run):
            source = plan_ref[1, first + r * run]
            vectors = jnp.concatenate([trial[source, 0], trial[source, 1]], axis=1)
            rows = left[at, r * run : (r + 1) * run].reshape(run * 128, 128)
            half = jnp.dot(rows, vectors, preferred_element_type=jnp.float32).astype(jnp.bfloat16)
            for u in range(run):
                halves[first + r * run + u, 0] = half[u * 128 : (u + 1) * 128, :128]
                halves[first + r * run + u, 1] = half[u * 128 : (u + 1) * 128, 128:]
        return carry

    lax.fori_loop(0, source_turns, source_turn, 0)
    for b in range(len(kinds)):
        for copy in block_copies(b, 1):
            copy.wait()

    def target_turn(turn, carry):
        first = turn * 2 * PAIRS
        for u in range(0, 2 * PAIRS, 2):
            place = first + u
            one, two = plan_ref[2, place], plan_ref[2, place + 1]
            pair = jnp.concatenate(
                [
                    jnp.concatenate([halves[one, 0], halves[two, 0]], axis=1),
                    jnp.concatenate([halves[one, 1], halves[two, 1]], axis=1),
                ],
                axis=0,
            )
            rights = jnp.concatenate([right[plan_ref[3, place]], right[plan_ref[3, place + 1]]], axis=1)
            term = lax.dot_general(
                pair, rights, (((1,), (1,)), ((), ())), preferred_element_type=jnp.float32
            )
            target = plan_ref[4, place]
            acc[target] = acc[target] + term
        return carry

    lax.fori_loop(0, target_turns, target_turn, 0)

    def dots(s, carry):
        t0 = trial[s, 0].astype(jnp.float32)
        t1 = trial[s, 1].astype(jnp.float32)
        a0 = acc[s, 0:128, :]
        a1 = acc[s, 128:256, :]
        p00, p01, p10, p11 = carry
        return p00 + fold(t0 * a0), p01 + fold(t0 * a1), p10 + fold(t1 * a0), p11 + fold(t1 * a1)

    zero = jnp.zeros((8, 128), jnp.float32)
    p00, p01, p10, p11 = [jnp.sum(x) for x in lax.fori_loop(0, n, dots, (zero,) * 4)]
    own = matrix_of({(0, 0): p00, (0, 1): p01, (1, 0): p10, (1, 1): p11})
    own_ref[...] = own
    me = lax.axis_index("op")

    def pack(j, carry):
        mine = jnp.bitwise_xor(me, 2 * j)
        keep_ref[j] = acc[mine]
        send_ref[pl.ds(pl.multiple_of(j * 256, 256), 256), :] = acc[jnp.bitwise_xor(mine, 1)].astype(jnp.bfloat16)
        return carry

    lax.fori_loop(0, n // 2, pack, 0)
    send_ref[n // 2 * 256 :, :] = split3(own)


def run_tasks(n, plan, left_ops, blocks):
    slots = left_ops.shape[0]
    places = plan.shape[1]
    terms_per = blocks[0][0].shape[0] // 2 - TRIALS
    kinds = tuple(block[1:] for block in blocks)
    hbm = pl.BlockSpec(memory_space=pltpu.HBM)
    return pl.pallas_call(
        functools.partial(tasks_kernel, n, terms_per, kinds),
        out_shape=(
            jax.ShapeDtypeStruct((n // 2 * 256 + TAIL, 128), jnp.bfloat16),
            jax.ShapeDtypeStruct((n // 2, 256, 128), jnp.float32),
            jax.ShapeDtypeStruct((8, 128), jnp.float32),
        ),
        in_specs=[pl.BlockSpec(memory_space=pltpu.SMEM), hbm] + [hbm] * len(blocks),
        scratch_shapes=[
            pltpu.VMEM((n, TRIALS, 128, 128), jnp.bfloat16),
            pltpu.VMEM((n * terms_per + 1, 128, 128), jnp.bfloat16),
            pltpu.VMEM((n + 1, 256, 128), jnp.float32),
            pltpu.VMEM((AHEAD, CHUNK, 128, 128), jnp.bfloat16),
            pltpu.VMEM((places, 2, 128, 128), jnp.bfloat16),
            pltpu.SemaphoreType.DMA((len(blocks), 4)),
            pltpu.SemaphoreType.DMA((AHEAD,)),
        ],
        compiler_params=pltpu.CompilerParams(vmem_limit_bytes=VMEM_LIMIT),
        cost_estimate=pl.CostEstimate(
            flops=slots * 8 * 128**3, bytes_accessed=slots * 32768 + n * 450000, transcendentals=0
        ),
    )(plan, left_ops, *[block[0] for block in blocks])


def corr_kernel(spans, *refs):
    blocks, corr_ref = refs[:-1], refs[-1]
    total = [jnp.zeros((8, 128), jnp.float32)] * 3
    for ref, span in zip(blocks, spans):
        for start in (0, span):
            t0, t1 = ref[start].astype(jnp.float32), ref[start + 1].astype(jnp.float32)
            total = [total[0] + fold(t0 * t0), total[1] + fold(t0 * t1), total[2] + fold(t1 * t1)]
    c00, c01, c11 = [jnp.sum(x) for x in total]
    corr_ref[...] = matrix_of({(0, 0): c00, (0, 1): c01, (1, 0): c01, (1, 1): c11})[0:2, 0:2]


def correlate(blocks):
    return pl.pallas_call(
        functools.partial(corr_kernel, [block.shape[0] // 2 for block in blocks]),
        out_shape=jax.ShapeDtypeStruct((2, 2), jnp.float32),
        compiler_params=pltpu.CompilerParams(vmem_limit_bytes=VMEM_LIMIT),
    )(*blocks)


def chip_kernel(chips, keep_ref, own_ref, received_ref, mine_ref, total_ref, *sends):
    total = own_ref[...] + join3(received_ref[chips * 256 :, :])
    total_ref[...] = total
    tail = split3(total)
    for j in range(chips):
        value = keep_ref[j] + received_ref[j * 256 : (j + 1) * 256, :].astype(jnp.float32)
        if j == 0:
            mine_ref[...] = value
        else:
            sends[j - 1][0:256, :] = value.astype(jnp.bfloat16)
            sends[j - 1][256:, :] = tail


def add_chip(keep, own, received):
    chips = keep.shape[0]
    return pl.pallas_call(
        functools.partial(chip_kernel, chips),
        out_shape=(jax.ShapeDtypeStruct((256, 128), jnp.float32), jax.ShapeDtypeStruct((8, 128), jnp.float32))
        + (jax.ShapeDtypeStruct((256 + TAIL, 128), jnp.bfloat16),) * (chips - 1),
        compiler_params=pltpu.CompilerParams(vmem_limit_bytes=VMEM_LIMIT),
    )(keep, own, received)


def last_kernel(mine_ref, total_ref, *refs):
    received, (product_ref, projected_ref) = refs[:-2], refs[-2:]
    value, total = mine_ref[...], total_ref[...]
    for ref in received:
        value = value + ref[0:256, :].astype(jnp.float32)
        total = total + join3(ref[256:, :])
    product_ref[0, 0] = value[0:128]
    product_ref[0, 1] = value[128:256]
    projected_ref[...] = total[0:2, 0:2]


def add_all(mine, total, received):
    return pl.pallas_call(
        last_kernel,
        out_shape=(
            jax.ShapeDtypeStruct((1, 2, 128, 128), jnp.float32),
            jax.ShapeDtypeStruct((2, 2), jnp.float32),
        ),
        compiler_params=pltpu.CompilerParams(vmem_limit_bytes=VMEM_LIMIT),
    )(mine, total, *received)


def body(n, trial, left_ops, right_ops, task_list):
    steps = n // 4
    own = (trial[0], right_ops)
    other = [exchange(value, n, 1) for value in own]
    block = jnp.concatenate([*own, *other], axis=0)
    plan = make_plan(task_list.T, n, n * right_ops.shape[0])
    blocks = [(block, 0, False)]
    for step in range(1, steps + 1):
        block = ring_step(block, n)
        blocks.append((block, step, False))
        if step < steps:
            blocks.append((exchange(block, n, 1), step, True))
    send, keep, own = run_tasks(n, plan, left_ops, blocks)
    send, arrays = lax.optimization_barrier((send, [block[0] for block in blocks]))
    correlation = correlate(arrays)
    mine, total, *sends = add_chip(keep, own, exchange(send, n, 1))
    received = [exchange(value, n, 2 * (j + 1)) for j, value in enumerate(sends)]
    product, projected = add_all(mine, total, received)
    return product, correlation, projected


def solution(mesh):
    return jax.shard_map(
        functools.partial(body, mesh.shape["op"]),
        mesh=mesh,
        in_specs=(
            P(("groups", "op"), None, None, None),
            P(("groups", "op"), None, None),
            P(("groups", "op"), None, None),
            P(("groups", "op"), None),
        ),
        out_specs=(P(("groups", "op"), None, None, None), P("groups", None), P("groups", None)),
        check_vma=False,
    )
```

time: 94.2 us -> 85.1 us (0.903)
  starting transfers between devices: 28.9 us -> 22.7 us
  waiting for transfers between devices: 31.4 us -> 27.3 us
    ppermute x23 -> x13, waiting for transfers between devices: 31.4 us -> 7.17 us  [exchange(): return lax.ppermute(value, 'op', [(i, i ^ mask) for i in range(n)])]
    ppermute x0 -> x4, waiting for transfers between devices: none -> 20.1 us  [ring_step(): return lax.ppermute(value, 'op', pairs)]
    ppermute x23 -> x13, starting transfers between devices: 28.9 us -> 13.6 us  [exchange(): return lax.ppermute(value, 'op', [(i, i ^ mask) for i in range(n)])]
    ppermute x0 -> x4, starting transfers between devices: none -> 9.04 us  [ring_step(): return lax.ppermute(value, 'op', pairs)]
    unnamed x48 -> x32, local copies, waits for them, and re-layouts: 2.03 us -> 2.87 us
    pallas_call x1 -> x3, Pallas kernels: 25.1 us -> 25.1 us  [the longest x1 20.1 us: run_tasks(): pl.pallas_call(functools.partial(tasks_kernel, n, terms_per, kinds), out_...]
  transfers between devices with their start and end apart: 23 -> 17, of which waited for: 8 -> 9; matrix products, arithmetic and copies ran while one was open for 0% -> 0% of each run, Pallas kernels for 0% -> 6%
where the time goes in v4:
time: 85.1 us; the launch traced here: 83.7 us
  Pallas kernels  29.2 us (34%)
  waiting for transfers between devices  27.3 us (32%)
  starting transfers between devices  22.7 us (27%)
  local copies, waits for them, and re-layouts  2.87 us (3%)
  other arithmetic  0.96 us (1%)
    pallas_call x1, Pallas kernels, run_tasks(): pl.pallas_call(functools.partial(tasks_kernel, n, terms_per, kinds), out_...  20.1 us
    ppermute x4, waiting for transfers between devices, ring_step(): return lax.ppermute(value, 'op', pairs)  20.1 us
    ppermute x13, starting transfers between devices, exchange(): return lax.ppermute(value, 'op', [(i, i ^ mask) for i in range(n)])  13.6 us
    ppermute x4, starting transfers between devices, ring_step(): return lax.ppermute(value, 'op', pairs)  9.04 us
    ppermute x13, waiting for transfers between devices, exchange(): return lax.ppermute(value, 'op', [(i, i ^ mask) for i in range(n)])  7.17 us
    unnamed x32, local copies, waits for them, and re-layouts  2.87 us
    pallas_call x1, Pallas kernels, correlate(): pl.pallas_call(functools.partial(corr_kernel, [block.shape[0] // 2 for bl...  2.8 us
    pallas_call x1, Pallas kernels, add_chip(): pl.pallas_call(functools.partial(chip_kernel, chips), out_shape=(jax.Shap...  2.2 us
  transfers between devices with their start and end apart: 17, of which 9 were waited for; matrix products, arithmetic and copies ran while one was open for 0% of the time, Pallas kernels for 6%

profile of v4, /device:TPU:0, one launch (start us, length us, event | category | flops | bytes accessed | tf_op | source)
XLA Modules:
  0.0 83.7 jit_solution(2361274521479451974)
XLA Ops:
  0.6 0.5 collective-permute-start.1
  1.1 0.1 collective-permute-start
  1.2 1.4 %collective-permute-done = bf16[2,128,128]{2,1,0:T(8,128)(2,1)S(1)} collective-permute-done((bf16[2,128,128]{2,1,0:T(8,128)(2,1)}, bf16[2,128,128]{2,1,0:T(8,128)(2,1)S(1)}, u32[]{:S(2)}, u32[]{:S(2)}) %collective-permute-start) | collective-permute-done | bytes 65568 | tf_op jit(solution)/shard_map/ppermute | solution.py:19
  2.6 0.0 collective-permute-done.1
  2.6 1.0 %pad_maximum_fusion.refs_0_ = bf16[12,128,128]{2,1,0:T(8,128)(2,1)S(1)} fusion(bf16[4,128,128]{2,1,0:T(8,128)(2,1)S(1)} %collective-permute-done.1, bf16[2,128,128]{2,1,0:T(8,128)(2,1)S(1)} %collective-permute-done, bf16[4,128,128]{2,1,0:T(8,128)(2,1)} %param.6, bf16[2,128,128]{2,1,0:T(8,128)(2,1)} %bitcast.3), kind=kLoop, calls=%fused_computation | loop fusion | flops 589824 | bytes 786432 | tf_op jit(solution)/shard_map/concatenate | solution.py:357
  3.6 0.0 copy-start
  3.6 2.8 %collective-permute-start.2 = (bf16[12,128,128]{2,1,0:T(8,128)(2,1)S(1)}, bf16[12,128,128]{2,1,0:T(8,128)(2,1)S(1)}, u32[]{:S(2)}, u32[]{:S(2)}) collective-permute-start(bf16[12,128,128]{2,1,0:T(8,128)(2,1)S(1)} %pad_maximum_fusion.refs_0_), channel_id=1, source_target_pairs={{0,4},{1,3},{4,8},{5,1},{8,12},{9,5},{12,14},{13,9},{14,10},{15,13... | collective-permute-start | bytes 1179656 | tf_op jit(solution)/shard_map/ppermute | solution.py:33
  6.4 5.7 %collective-permute-done.2.refs_1_ = bf16[12,128,128]{2,1,0:T(8,128)(2,1)S(1)} collective-permute-done((bf16[12,128,128]{2,1,0:T(8,128)(2,1)S(1)}, bf16[12,128,128]{2,1,0:T(8,128)(2,1)S(1)}, u32[]{:S(2)}, u32[]{:S(2)}) %collective-permute-start.2) | collective-permute-done | bytes 393248 | tf_op jit(solution)/shard_map/ppermute | solution.py:33
  12.1 2.1 %collective-permute-start.4 = (bf16[12,128,128]{2,1,0:T(8,128)(2,1)S(1)}, bf16[12,128,128]{2,1,0:T(8,128)(2,1)S(1)}, u32[]{:S(2)}, u32[]{:S(2)}) collective-permute-start(bf16[12,128,128]{2,1,0:T(8,128)(2,1)S(1)} %collective-permute-done.2.refs_1_), channel_id=1, source_target_pairs={{0,4},{1,3},{4,8},{5,1},{8,12},{9,5},{12,14},{13,9},{14,10},{15,13... | collective-permute-start | bytes 1179656 | tf_op jit(solution)/shard_map/ppermute | solution.py:33
  14.2 5.7 %collective-permute-done.4.refs_3_ = bf16[12,128,128]{2,1,0:T(8,128)(2,1)S(1)} collective-permute-done((bf16[12,128,128]{2,1,0:T(8,128)(2,1)S(1)}, bf16[12,128,128]{2,1,0:T(8,128)(2,1)S(1)}, u32[]{:S(2)}, u32[]{:S(2)}) %collective-permute-start.4) | collective-permute-done | bytes 393248 | tf_op jit(solution)/shard_map/ppermute | solution.py:33
  19.9 0.0 copy-start.3
  19.9 2.1 %collective-permute-start.6 = (bf16[12,128,128]{2,1,0:T(8,128)(2,1)S(1)}, bf16[12,128,128]{2,1,0:T(8,128)(2,1)S(1)}, u32[]{:S(2)}, u32[]{:S(2)}) collective-permute-start(bf16[12,128,128]{2,1,0:T(8,128)(2,1)S(1)} %collective-permute-done.4.refs_3_), channel_id=1, source_target_pairs={{0,4},{1,3},{4,8},{5,1},{8,12},{9,5},{12,14},{13,9},{14,10},{15,13... | collective-permute-start | bytes 1179656 | tf_op jit(solution)/shard_map/ppermute | solution.py:33
  22.0 0.0 collective-permute-start.3
  22.0 0.5 collective-permute-start.5
  22.5 5.2 %collective-permute-done.6.refs_5_ = bf16[12,128,128]{2,1,0:T(8,128)(2,1)S(1)} collective-permute-done((bf16[12,128,128]{2,1,0:T(8,128)(2,1)S(1)}, bf16[12,128,128]{2,1,0:T(8,128)(2,1)S(1)}, u32[]{:S(2)}, u32[]{:S(2)}) %collective-permute-start.6) | collective-permute-done | bytes 393248 | tf_op jit(solution)/shard_map/ppermute | solution.py:33
  27.7 0.0 copy-start.4
  27.7 2.1 %collective-permute-start.8 = (bf16[12,128,128]{2,1,0:T(8,128)(2,1)S(1)}, bf16[12,128,128]{2,1,0:T(8,128)(2,1)S(1)}, u32[]{:S(2)}, u32[]{:S(2)}) collective-permute-start(bf16[12,128,128]{2,1,0:T(8,128)(2,1)S(1)} %collective-permute-done.6.refs_5_), channel_id=1, source_target_pairs={{0,4},{1,3},{4,8},{5,1},{8,12},{9,5},{12,14},{13,9},{14,10},{15,13... | collective-permute-start | bytes 1179656 | tf_op jit(solution)/shard_map/ppermute | solution.py:33
  29.7 0.0 collective-permute-start.7
  29.7 2.2 %shard_map.67.plan_ref = s32[8,384]{1,0:T(8,128)} custom-call(s32[4,256]{1,0:T(4,128)} %bitcast.4), custom_call_target="tpu_custom_call" | custom-call | tf_op jit(solution)/shard_map/pallas_call | solution.py:135
  31.9 0.0 collective-permute-done.3.refs_2_
  31.9 0.0 copy-start.5
  31.9 0.0 collective-permute-done.5.refs_4_
  31.9 0.0 copy-start.6
  31.9 3.5 %collective-permute-done.8.refs_7_ = bf16[12,128,128]{2,1,0:T(8,128)(2,1)S(1)} collective-permute-done((bf16[12,128,128]{2,1,0:T(8,128)(2,1)S(1)}, bf16[12,128,128]{2,1,0:T(8,128)(2,1)S(1)}, u32[]{:S(2)}, u32[]{:S(2)}) %collective-permute-start.8) | collective-permute-done | bytes 393248 | tf_op jit(solution)/shard_map/ppermute | solution.py:33
  35.4 0.0 copy-start.7
  35.4 0.0 collective-permute-done.7.refs_6_
  35.4 0.0 copy-done
  35.4 0.0 copy-done.2
  35.5 0.0 copy-done.3
  35.5 0.0 copy-done.4
  35.5 0.0 copy-done.5
  35.5 0.0 copy-done.6
  35.5 0.7 copy-done.7
  36.2 0.0 copy-start.8
  36.2 0.7 copy-done.8
  36.9 20.1 %shard_map.68 = (bf16[2080,128]{1,0:T(8,128)(2,1)}, f32[8,256,128]{2,1,0:T(8,128)}, f32[8,128]{1,0:T(8,128)}) custom-call(s32[8,384]{1,0:T(8,128)} %shard_map.67.plan_ref, bf16[256,128,128]{2,1,0:T(8,128)(2,1)} %left_ref.1, bf16[12,128,128]{2,1,0:T(8,128)(2,1)} %copy-done, bf16[12,128,128]{2,1,0:T(8,128)(2,1)} %copy-done.2, bf16[12,128,128]{2,1,0:T(8,128)(2,1)} %copy-done.5, ...), custom_call_target="tpu_custom_call" | custom-call | flops 4294967296 | bytes 15588608 | tf_op jit(solution)/shard_map/pallas_call | solution.py:265
  57.1 0.1 collective-permute-start.9
  57.2 2.1 %collective-permute-done.9.received_ref = bf16[2080,128]{1,0:T(8,128)(2,1)S(1)} collective-permute-done((bf16[2080,128]{1,0:T(8,128)(2,1)}, bf16[2080,128]{1,0:T(8,128)(2,1)S(1)}, u32[]{:S(2)}, u32[]{:S(2)}) %collective-permute-start.9) | collective-permute-done | bytes 532512 | tf_op jit(solution)/shard_map/ppermute | solution.py:19
  59.3 0.0 copy-start.1
  59.3 0.8 copy-done.1
  60.1 2.2 %shard_map.69 = (f32[256,128]{1,0:T(8,128)}, f32[8,128]{1,0:T(8,128)}, bf16[288,128]{1,0:T(8,128)(2,1)}, bf16[288,128]{1,0:T(8,128)(2,1)}, bf16[288,128]{1,0:T(8...) custom-call(f32[8,256,128]{2,1,0:T(8,128)} %get-tuple-element.26.kee, ...), custom_call_target="tpu_custom_call" | custom-call | tf_op jit(solution)/shard_map/pallas_call | solution.py:323
  62.3 1.2 %collective-permute-start.10 = (bf16[288,128]{1,0:T(8,128)(2,1)}, bf16[288,128]{1,0:T(8,128)(2,1)S(1)}, u32[]{:S(2)}, u32[]{:S(2)}) collective-permute-start(bf16[288,128]{1,0:T(8,128)(2,1)} %get-tuple-element.32), channel_id=1, source_target_pairs={{0,2},{1,3},{2,0},{3,1},{4,6},{5,7},{6,4},{7,5},{8,10},{9,11},{10,... | collective-permute-start | bytes 221192 | tf_op jit(solution)/shard_map/ppermute | solution.py:19
  63.5 2.1 %collective-permute-start.11 = (bf16[288,128]{1,0:T(8,128)(2,1)}, bf16[288,128]{1,0:T(8,128)(2,1)S(1)}, u32[]{:S(2)}, u32[]{:S(2)}) collective-permute-start(bf16[288,128]{1,0:T(8,128)(2,1)} %get-tuple-element.33), channel_id=1, source_target_pairs={{0,4},{1,5},{2,6},{3,7},{4,0},{5,1},{6,2},{7,3},{8,12},{9,13},{10,... | collective-permute-start | bytes 221192 | tf_op jit(solution)/shard_map/ppermute | solution.py:19
  65.7 1.4 %collective-permute-start.12 = (bf16[288,128]{1,0:T(8,128)(2,1)}, bf16[288,128]{1,0:T(8,128)(2,1)S(1)}, u32[]{:S(2)}, u32[]{:S(2)}) collective-permute-start(bf16[288,128]{1,0:T(8,128)(2,1)} %get-tuple-element.34), channel_id=1, source_target_pairs={{0,6},{1,7},{2,4},{3,5},{4,2},{5,3},{6,0},{7,1},{8,14},{9,15},{10,... | collective-permute-start | bytes 221192 | tf_op jit(solution)/shard_map/ppermute | solution.py:19
  67.1 1.5 %collective-permute-start.13 = (bf16[288,128]{1,0:T(8,128)(2,1)}, bf16[288,128]{1,0:T(8,128)(2,1)S(1)}, u32[]{:S(2)}, u32[]{:S(2)}) collective-permute-start(bf16[288,128]{1,0:T(8,128)(2,1)} %get-tuple-element.35), channel_id=1, source_target_pairs={{0,8},{1,9},{2,10},{3,11},{4,12},{5,13},{6,14},{7,15},{8,0},{9,1},... | collective-permute-start | bytes 221192 | tf_op jit(solution)/shard_map/ppermute | solution.py:19
  68.5 1.5 %collective-permute-start.14 = (bf16[288,128]{1,0:T(8,128)(2,1)}, bf16[288,128]{1,0:T(8,128)(2,1)S(1)}, u32[]{:S(2)}, u32[]{:S(2)}) collective-permute-start(bf16[288,128]{1,0:T(8,128)(2,1)} %get-tuple-element.36), channel_id=1, source_target_pairs={{0,10},{1,11},{2,8},{3,9},{4,14},{5,15},{6,12},{7,13},{8,2},{9,3},... | collective-permute-start | bytes 221192 | tf_op jit(solution)/shard_map/ppermute | solution.py:19
  70.0 0.0 collective-permute-done.10.refs_0_
  70.0 3.8 %collective-permute-start.15 = (bf16[288,128]{1,0:T(8,128)(2,1)}, bf16[288,128]{1,0:T(8,128)(2,1)S(1)}, u32[]{:S(2)}, u32[]{:S(2)}) collective-permute-start(bf16[288,128]{1,0:T(8,128)(2,1)} %get-tuple-element.37), channel_id=1, source_target_pairs={{0,12},{1,13},{2,14},{3,15},{4,8},{5,9},{6,10},{7,11},{8,4},{9,5},... | collective-permute-start | bytes 221192 | tf_op jit(solution)/shard_map/ppermute | solution.py:19
  73.8 0.0 collective-permute-done.11.refs_1_
  73.8 0.9 %collective-permute-start.16 = (bf16[288,128]{1,0:T(8,128)(2,1)}, bf16[288,128]{1,0:T(8,128)(2,1)S(1)}, u32[]{:S(2)}, u32[]{:S(2)}) collective-permute-start(bf16[288,128]{1,0:T(8,128)(2,1)} %get-tuple-element.38), channel_id=1, source_target_pairs={{0,14},{1,15},{2,12},{3,13},{4,10},{5,11},{6,8},{7,9},{8,6},{9,7},... | collective-permute-start | bytes 221192 | tf_op jit(solution)/shard_map/ppermute | solution.py:19
  74.7 2.8 %shard_map.71 = f32[2,2]{1,0:T(2,128)} custom-call(bf16[12,128,128]{2,1,0:T(8,128)(2,1)} %copy-done, bf16[12,128,128]{2,1,0:T(8,128)(2,1)} %copy-done.2, bf16[12,128,128]{2,1,0:T(8,128)(2,1)} %copy-done.5, bf16[12,128,128]{2,1,0:T(8,128)(2,1)} %copy-done.3, bf16[12,128,128]{2,1,0:T(8,128)(2,1)} %copy-done.6, bf16[12,128,128]{2,1,0:T(8,128)(2,1)} %copy-done.4, ...), custom_call_target="tpu_custom_call" | custom-call | tf_op jit(solution)/shard_map/pallas_call | solution.py:301
  77.5 0.0 collective-permute-done.12.refs_2_
  77.5 0.9 %collective-permute-done.13.refs_3_ = bf16[288,128]{1,0:T(8,128)(2,1)S(1)} collective-permute-done((bf16[288,128]{1,0:T(8,128)(2,1)}, bf16[288,128]{1,0:T(8,128)(2,1)S(1)}, u32[]{:S(2)}, u32[]{:S(2)}) %collective-permute-start.13) | collective-permute-done | bytes 73760 | tf_op jit(solution)/shard_map/ppermute | solution.py:19
  78.4 1.7 %collective-permute-done.14.refs_4_ = bf16[288,128]{1,0:T(8,128)(2,1)S(1)} collective-permute-done((bf16[288,128]{1,0:T(8,128)(2,1)}, bf16[288,128]{1,0:T(8,128)(2,1)S(1)}, u32[]{:S(2)}, u32[]{:S(2)}) %collective-permute-start.14) | collective-permute-done | bytes 73760 | tf_op jit(solution)/shard_map/ppermute | solution.py:19
  80.1 0.0 collective-permute-done.15.refs_5_
  80.1 1.1 %collective-permute-done.16.refs_6_ = bf16[288,128]{1,0:T(8,128)(2,1)S(1)} collective-permute-done((bf16[288,128]{1,0:T(8,128)(2,1)}, bf16[288,128]{1,0:T(8,128)(2,1)S(1)}, u32[]{:S(2)}, u32[]{:S(2)}) %collective-permute-start.16) | collective-permute-done | bytes 73760 | tf_op jit(solution)/shard_map/ppermute | solution.py:19
  81.2 0.0 copy-done.9
  81.2 0.0 copy-done.10
  81.2 0.0 copy-done.11
  81.2 0.0 copy-done.12
  81.2 0.0 copy-done.13
  81.2 0.0 copy-done.14
  81.2 0.6 copy-done.15
  81.8 1.9 %shard_map.70 = (f32[1,2,128,128]{3,2,1,0:T(8,128)}, f32[2,2]{1,0:T(2,128)}) custom-call(f32[256,128]{1,0:T(8,128)} %get-tuple-element.30.mine_ref, f32[8,128]{1,0:T(8,128)} %get-tuple-element.31.total_ref, bf16[288,128]{1,0:T(8,128)(2,1)} %copy-done.9, bf16[288,128]{1,0:T(8,128)(2,1)} %copy-done.10, bf16[288,128]{1,0:T(8,128)(2,1)} %copy-done.11, ...), custom_call_target="tpu_custom_call" | custom-call | tf_op jit(solution)/shard_map/pallas_call | solution.py:343
  (8 shorter events, 0.0 us)
Async XLA Ops:
  0.6 2.0 %collective-permute-start.1 = (bf16[4,128,128]{2,1,0:T(8,128)(2,1)}, bf16[4,128,128]{2,1,0:T(8,128)(2,1)S(1)}, u32[]{:S(2)}, u32[]{:S(2)}) collective-permute-start(bf16[4,128,128]{2,1,0:T(8,128)(2,1)} %param.6), channel_id=1, source_target_pairs={{0,1},{1,0},{2,3},{3,2},{4,5},{5,4},{6,7},{7,6},{8,9},{9,8},{10,11... | collective-permute-start | bytes 393224 | tf_op jit(solution)/shard_map/ppermute | solution.py:19
  1.1 1.5 %collective-permute-start = (bf16[2,128,128]{2,1,0:T(8,128)(2,1)}, bf16[2,128,128]{2,1,0:T(8,128)(2,1)S(1)}, u32[]{:S(2)}, u32[]{:S(2)}) collective-permute-start(bf16[2,128,128]{2,1,0:T(8,128)(2,1)} %bitcast.2), channel_id=1, source_target_pairs={{0,1},{1,0},{2,3},{3,2},{4,5},{5,4},{6,7},{7,6},{8,9},{9,8},{10,11... | collective-permute-start | bytes 196616 | tf_op jit(solution)/shard_map/ppermute | solution.py:19
  3.6 31.9 %copy-start = (bf16[12,128,128]{2,1,0:T(8,128)(2,1)}, bf16[12,128,128]{2,1,0:T(8,128)(2,1)S(1)}, u32[]{:S(2)}) copy-start(bf16[12,128,128]{2,1,0:T(8,128)(2,1)S(1)} %pad_maximum_fusion.refs_0_) | copy-start | bytes 1179652
  3.6 8.5 %collective-permute-start.2 = (bf16[12,128,128]{2,1,0:T(8,128)(2,1)S(1)}, bf16[12,128,128]{2,1,0:T(8,128)(2,1)S(1)}, u32[]{:S(2)}, u32[]{:S(2)}) collective-permute-start(bf16[12,128,128]{2,1,0:T(8,128)(2,1)S(1)} %pad_maximum_fusion.refs_0_), channel_id=1, source_target_pairs={{0,4},{1,3},{4,8},{5,1},{8,12},{9,5},{12,14},{13,9},{14,10},{15,13... | collective-permute-start | bytes 1179656 | tf_op jit(solution)/shard_map/ppermute | solution.py:33
  12.1 23.4 %copy-start.2 = (bf16[12,128,128]{2,1,0:T(8,128)(2,1)}, bf16[12,128,128]{2,1,0:T(8,128)(2,1)S(1)}, u32[]{:S(2)}) copy-start(bf16[12,128,128]{2,1,0:T(8,128)(2,1)S(1)} %collective-permute-done.2.refs_1_) | copy-start | bytes 1179652
  12.1 7.8 %collective-permute-start.4 = (bf16[12,128,128]{2,1,0:T(8,128)(2,1)S(1)}, bf16[12,128,128]{2,1,0:T(8,128)(2,1)S(1)}, u32[]{:S(2)}, u32[]{:S(2)}) collective-permute-start(bf16[12,128,128]{2,1,0:T(8,128)(2,1)S(1)} %collective-permute-done.2.refs_1_), channel_id=1, source_target_pairs={{0,4},{1,3},{4,8},{5,1},{8,12},{9,5},{12,14},{13,9},{14,10},{15,13... | collective-permute-start | bytes 1179656 | tf_op jit(solution)/shard_map/ppermute | solution.py:33
  19.9 15.6 %copy-start.3 = (bf16[12,128,128]{2,1,0:T(8,128)(2,1)}, bf16[12,128,128]{2,1,0:T(8,128)(2,1)S(1)}, u32[]{:S(2)}) copy-start(bf16[12,128,128]{2,1,0:T(8,128)(2,1)S(1)} %collective-permute-done.4.refs_3_) | copy-start | bytes 1179652
  19.9 7.8 %collective-permute-start.6 = (bf16[12,128,128]{2,1,0:T(8,128)(2,1)S(1)}, bf16[12,128,128]{2,1,0:T(8,128)(2,1)S(1)}, u32[]{:S(2)}, u32[]{:S(2)}) collective-permute-start(bf16[12,128,128]{2,1,0:T(8,128)(2,1)S(1)} %collective-permute-done.4.refs_3_), channel_id=1, source_target_pairs={{0,4},{1,3},{4,8},{5,1},{8,12},{9,5},{12,14},{13,9},{14,10},{15,13... | collective-permute-start | bytes 1179656 | tf_op jit(solution)/shard_map/ppermute | solution.py:33
  22.0 9.9 %collective-permute-start.3 = (bf16[12,128,128]{2,1,0:T(8,128)(2,1)S(1)}, bf16[12,128,128]{2,1,0:T(8,128)(2,1)S(1)}, u32[]{:S(2)}, u32[]{:S(2)}) collective-permute-start(bf16[12,128,128]{2,1,0:T(8,128)(2,1)S(1)} %collective-permute-done.2.refs_1_), channel_id=1, source_target_pairs={{0,1},{1,0},{2,3},{3,2},{4,5},{5,4},{6,7},{7,6},{8,9},{9,8},{10,11... | collective-permute-start | bytes 1179656 | tf_op jit(solution)/shard_map/ppermute | solution.py:19
  22.0 9.9 %collective-permute-start.5 = (bf16[12,128,128]{2,1,0:T(8,128)(2,1)S(1)}, bf16[12,128,128]{2,1,0:T(8,128)(2,1)S(1)}, u32[]{:S(2)}, u32[]{:S(2)}) collective-permute-start(bf16[12,128,128]{2,1,0:T(8,128)(2,1)S(1)} %collective-permute-done.4.refs_3_), channel_id=1, source_target_pairs={{0,1},{1,0},{2,3},{3,2},{4,5},{5,4},{6,7},{7,6},{8,9},{9,8},{10,11... | collective-permute-start | bytes 1179656 | tf_op jit(solution)/shard_map/ppermute | solution.py:19
  27.7 7.8 %copy-start.4 = (bf16[12,128,128]{2,1,0:T(8,128)(2,1)}, bf16[12,128,128]{2,1,0:T(8,128)(2,1)S(1)}, u32[]{:S(2)}) copy-start(bf16[12,128,128]{2,1,0:T(8,128)(2,1)S(1)} %collective-permute-done.6.refs_5_) | copy-start | bytes 1179652
  27.7 7.8 %collective-permute-start.8 = (bf16[12,128,128]{2,1,0:T(8,128)(2,1)S(1)}, bf16[12,128,128]{2,1,0:T(8,128)(2,1)S(1)}, u32[]{:S(2)}, u32[]{:S(2)}) collective-permute-start(bf16[12,128,128]{2,1,0:T(8,128)(2,1)S(1)} %collective-permute-done.6.refs_5_), channel_id=1, source_target_pairs={{0,4},{1,3},{4,8},{5,1},{8,12},{9,5},{12,14},{13,9},{14,10},{15,13... | collective-permute-start | bytes 1179656 | tf_op jit(solution)/shard_map/ppermute | solution.py:33
  29.7 5.7 %collective-permute-start.7 = (bf16[12,128,128]{2,1,0:T(8,128)(2,1)S(1)}, bf16[12,128,128]{2,1,0:T(8,128)(2,1)S(1)}, u32[]{:S(2)}, u32[]{:S(2)}) collective-permute-start(bf16[12,128,128]{2,1,0:T(8,128)(2,1)S(1)} %collective-permute-done.6.refs_5_), channel_id=1, source_target_pairs={{0,1},{1,0},{2,3},{3,2},{4,5},{5,4},{6,7},{7,6},{8,9},{9,8},{10,11... | collective-permute-start | bytes 1179656 | tf_op jit(solution)/shard_map/ppermute | solution.py:19
  31.9 3.6 %copy-start.5 = (bf16[12,128,128]{2,1,0:T(8,128)(2,1)}, bf16[12,128,128]{2,1,0:T(8,128)(2,1)S(1)}, u32[]{:S(2)}) copy-start(bf16[12,128,128]{2,1,0:T(8,128)(2,1)S(1)} %collective-permute-done.3.refs_2_) | copy-start | bytes 1179652
  31.9 3.6 %copy-start.6 = (bf16[12,128,128]{2,1,0:T(8,128)(2,1)}, bf16[12,128,128]{2,1,0:T(8,128)(2,1)S(1)}, u32[]{:S(2)}) copy-start(bf16[12,128,128]{2,1,0:T(8,128)(2,1)S(1)} %collective-permute-done.5.refs_4_) | copy-start | bytes 1179652
  35.4 0.8 copy-start.7
  36.2 0.7 copy-start.8
  57.1 2.2 %collective-permute-start.9 = (bf16[2080,128]{1,0:T(8,128)(2,1)}, bf16[2080,128]{1,0:T(8,128)(2,1)S(1)}, u32[]{:S(2)}, u32[]{:S(2)}) collective-permute-start(bf16[2080,128]{1,0:T(8,128)(2,1)} %get-tuple-element.29), channel_id=1, source_target_pairs={{0,1},{1,0},{2,3},{3,2},{4,5},{5,4},{6,7},{7,6},{8,9},{9,8},{10,11... | collective-permute-start | bytes 1597448 | tf_op jit(solution)/shard_map/ppermute | solution.py:19
  59.3 0.8 copy-start.1
  62.3 7.7 %collective-permute-start.10 = (bf16[288,128]{1,0:T(8,128)(2,1)}, bf16[288,128]{1,0:T(8,128)(2,1)S(1)}, u32[]{:S(2)}, u32[]{:S(2)}) collective-permute-start(bf16[288,128]{1,0:T(8,128)(2,1)} %get-tuple-element.32), channel_id=1, source_target_pairs={{0,2},{1,3},{2,0},{3,1},{4,6},{5,7},{6,4},{7,5},{8,10},{9,11},{10,... | collective-permute-start | bytes 221192 | tf_op jit(solution)/shard_map/ppermute | solution.py:19
  63.5 10.3 %collective-permute-start.11 = (bf16[288,128]{1,0:T(8,128)(2,1)}, bf16[288,128]{1,0:T(8,128)(2,1)S(1)}, u32[]{:S(2)}, u32[]{:S(2)}) collective-permute-start(bf16[288,128]{1,0:T(8,128)(2,1)} %get-tuple-element.33), channel_id=1, source_target_pairs={{0,4},{1,5},{2,6},{3,7},{4,0},{5,1},{6,2},{7,3},{8,12},{9,13},{10,... | collective-permute-start | bytes 221192 | tf_op jit(solution)/shard_map/ppermute | solution.py:19
  65.7 11.9 %collective-permute-start.12 = (bf16[288,128]{1,0:T(8,128)(2,1)}, bf16[288,128]{1,0:T(8,128)(2,1)S(1)}, u32[]{:S(2)}, u32[]{:S(2)}) collective-permute-start(bf16[288,128]{1,0:T(8,128)(2,1)} %get-tuple-element.34), channel_id=1, source_target_pairs={{0,6},{1,7},{2,4},{3,5},{4,2},{5,3},{6,0},{7,1},{8,14},{9,15},{10,... | collective-permute-start | bytes 221192 | tf_op jit(solution)/shard_map/ppermute | solution.py:19
  67.1 11.3 %collective-permute-start.13 = (bf16[288,128]{1,0:T(8,128)(2,1)}, bf16[288,128]{1,0:T(8,128)(2,1)S(1)}, u32[]{:S(2)}, u32[]{:S(2)}) collective-permute-start(bf16[288,128]{1,0:T(8,128)(2,1)} %get-tuple-element.35), channel_id=1, source_target_pairs={{0,8},{1,9},{2,10},{3,11},{4,12},{5,13},{6,14},{7,15},{8,0},{9,1},... | collective-permute-start | bytes 221192 | tf_op jit(solution)/shard_map/ppermute | solution.py:19
  68.5 11.6 %collective-permute-start.14 = (bf16[288,128]{1,0:T(8,128)(2,1)}, bf16[288,128]{1,0:T(8,128)(2,1)S(1)}, u32[]{:S(2)}, u32[]{:S(2)}) collective-permute-start(bf16[288,128]{1,0:T(8,128)(2,1)} %get-tuple-element.36), channel_id=1, source_target_pairs={{0,10},{1,11},{2,8},{3,9},{4,14},{5,15},{6,12},{7,13},{8,2},{9,3},... | collective-permute-start | bytes 221192 | tf_op jit(solution)/shard_map/ppermute | solution.py:19
  70.0 11.2 %copy-start.9 = (bf16[288,128]{1,0:T(8,128)(2,1)}, bf16[288,128]{1,0:T(8,128)(2,1)S(1)}, u32[]{:S(2)}) copy-start(bf16[288,128]{1,0:T(8,128)(2,1)S(1)} %collective-permute-done.10.refs_0_) | copy-start | bytes 221188
  70.0 10.1 %collective-permute-start.15 = (bf16[288,128]{1,0:T(8,128)(2,1)}, bf16[288,128]{1,0:T(8,128)(2,1)S(1)}, u32[]{:S(2)}, u32[]{:S(2)}) collective-permute-start(bf16[288,128]{1,0:T(8,128)(2,1)} %get-tuple-element.37), channel_id=1, source_target_pairs={{0,12},{1,13},{2,14},{3,15},{4,8},{5,9},{6,10},{7,11},{8,4},{9,5},... | collective-permute-start | bytes 221192 | tf_op jit(solution)/shard_map/ppermute | solution.py:19
  73.8 7.4 %copy-start.10 = (bf16[288,128]{1,0:T(8,128)(2,1)}, bf16[288,128]{1,0:T(8,128)(2,1)S(1)}, u32[]{:S(2)}) copy-start(bf16[288,128]{1,0:T(8,128)(2,1)S(1)} %collective-permute-done.11.refs_1_) | copy-start | bytes 221188
  73.8 7.4 %collective-permute-start.16 = (bf16[288,128]{1,0:T(8,128)(2,1)}, bf16[288,128]{1,0:T(8,128)(2,1)S(1)}, u32[]{:S(2)}, u32[]{:S(2)}) collective-permute-start(bf16[288,128]{1,0:T(8,128)(2,1)} %get-tuple-element.38), channel_id=1, source_target_pairs={{0,14},{1,15},{2,12},{3,13},{4,10},{5,11},{6,8},{7,9},{8,6},{9,7},... | collective-permute-start | bytes 221192 | tf_op jit(solution)/shard_map/ppermute | solution.py:19
  77.5 3.7 %copy-start.11 = (bf16[288,128]{1,0:T(8,128)(2,1)}, bf16[288,128]{1,0:T(8,128)(2,1)S(1)}, u32[]{:S(2)}) copy-start(bf16[288,128]{1,0:T(8,128)(2,1)S(1)} %collective-permute-done.12.refs_2_) | copy-start | bytes 221188
  78.4 2.8 %copy-start.12 = (bf16[288,128]{1,0:T(8,128)(2,1)}, bf16[288,128]{1,0:T(8,128)(2,1)S(1)}, u32[]{:S(2)}) copy-start(bf16[288,128]{1,0:T(8,128)(2,1)S(1)} %collective-permute-done.13.refs_3_) | copy-start | bytes 221188
  80.1 1.1 %copy-start.13 = (bf16[288,128]{1,0:T(8,128)(2,1)}, bf16[288,128]{1,0:T(8,128)(2,1)S(1)}, u32[]{:S(2)}) copy-start(bf16[288,128]{1,0:T(8,128)(2,1)S(1)} %collective-permute-done.14.refs_4_) | copy-start | bytes 221188
  80.1 1.1 %copy-start.14 = (bf16[288,128]{1,0:T(8,128)(2,1)}, bf16[288,128]{1,0:T(8,128)(2,1)S(1)}, u32[]{:S(2)}) copy-start(bf16[288,128]{1,0:T(8,128)(2,1)S(1)} %collective-permute-done.15.refs_5_) | copy-start | bytes 221188
  81.2 0.6 copy-start.15

commit v5 on v4

--- a/solution.py
+++ b/solution.py
@@ -7,11 +7,11 @@
 from jax.experimental.pallas import tpu as pltpu
 from jax.sharding import PartitionSpec as P
 
-VMEM_LIMIT = 56 * 1024 * 1024
+MIB = 1024 * 1024
 TAIL = 32
 TRIALS = 2
-CHUNK = 16
-PAIRS = 8
+CHUNK = 32
+PAIRS = 16
 AHEAD = 3
 
 
@@ -222,9 +222,9 @@
                 ],
                 axis=0,
             )
-            rights = jnp.concatenate([right[plan_ref[3, place]], right[plan_ref[3, place + 1]]], axis=1)
+            rights = jnp.concatenate([right[plan_ref[3, place]], right[plan_ref[3, place + 1]]], axis=0)
             term = lax.dot_general(
-                pair, rights, (((1,), (1,)), ((), ())), preferred_element_type=jnp.float32
+                pair, rights, (((1,), (0,)), ((), ())), preferred_element_type=jnp.float32
             )
             target = plan_ref[4, place]
             acc[target] = acc[target] + term
@@ -279,7 +279,7 @@
             pltpu.SemaphoreType.DMA((len(blocks), 4)),
             pltpu.SemaphoreType.DMA((AHEAD,)),
         ],
-        compiler_params=pltpu.CompilerParams(vmem_limit_bytes=VMEM_LIMIT),
+        compiler_params=pltpu.CompilerParams(vmem_limit_bytes=(53 if n <= 16 else 57) * MIB),
         cost_estimate=pl.CostEstimate(
             flops=slots * 8 * 128**3, bytes_accessed=slots * 32768 + n * 450000, transcendentals=0
         ),
@@ -301,7 +301,7 @@
     return pl.pallas_call(
         functools.partial(corr_kernel, [block.shape[0] // 2 for block in blocks]),
         out_shape=jax.ShapeDtypeStruct((2, 2), jnp.float32),
-        compiler_params=pltpu.CompilerParams(vmem_limit_bytes=VMEM_LIMIT),
+        compiler_params=pltpu.CompilerParams(vmem_limit_bytes=16 * MIB),
     )(*blocks)
 
 
@@ -324,7 +324,7 @@
         functools.partial(chip_kernel, chips),
         out_shape=(jax.ShapeDtypeStruct((256, 128), jnp.float32), jax.ShapeDtypeStruct((8, 128), jnp.float32))
         + (jax.ShapeDtypeStruct((256 + TAIL, 128), jnp.bfloat16),) * (chips - 1),
-        compiler_params=pltpu.CompilerParams(vmem_limit_bytes=VMEM_LIMIT),
+        compiler_params=pltpu.CompilerParams(vmem_limit_bytes=16 * MIB),
     )(keep, own, received)
 
 
@@ -346,13 +346,13 @@
             jax.ShapeDtypeStruct((1, 2, 128, 128), jnp.float32),
             jax.ShapeDtypeStruct((2, 2), jnp.float32),
         ),
-        compiler_params=pltpu.CompilerParams(vmem_limit_bytes=VMEM_LIMIT),
+        compiler_params=pltpu.CompilerParams(vmem_limit_bytes=16 * MIB),
     )(mine, total, *received)
 
 
 def body(n, trial, left_ops, right_ops, task_list):
     steps = n // 4
-    own = (trial[0], right_ops)
+    own = (trial[0], right_ops.swapaxes(1, 2))
     other = [exchange(value, n, 1) for value in own]
     block = jnp.concatenate([*own, *other], axis=0)
     plan = make_plan(task_list.T, n, n * right_ops.shape[0])

time: 85.1 us -> 80.9 us (0.951)
  Pallas kernels: 29.2 us -> 21.1 us
  local copies, waits for them, and re-layouts: 2.87 us -> 10.4 us
  waiting for transfers between devices: 27.3 us -> 23.8 us
    unnamed x32 -> x29, local copies, waits for them, and re-layouts: 2.87 us -> 10.4 us
    ppermute x13, waiting for transfers between devices: 7.17 us -> 3.7 us  [exchange(): return lax.ppermute(value, 'op', [(i, i ^ mask) for i in range(n)])]
    pallas_call x1, Pallas kernels: 20.1 us -> 17.1 us  [run_tasks(): pl.pallas_call(functools.partial(tasks_kernel, n, terms_per, kinds), out_...]
    pallas_call x1, Pallas kernels: 2.2 us -> 0.12 us  [add_chip(): pl.pallas_call(functools.partial(chip_kernel, chips), out_shape=(jax.Shap...]
    pallas_call x1, Pallas kernels: 2.8 us -> 0.98 us  [correlate(): pl.pallas_call(functools.partial(corr_kernel, [block.shape[0] // 2 for bl...]
    pallas_call x1, Pallas kernels: 1.89 us -> 0.73 us  [add_all(): pl.pallas_call(last_kernel, out_shape=(jax.ShapeDtypeStruct((1, 2, 128, 1...]
  transfers between devices with their start and end apart: 17 -> 17, of which waited for: 9 -> 7; matrix products, arithmetic and copies ran while one was open for 0% -> 0% of each run, Pallas kernels for 6% -> 4%
where the time goes in v5:
time: 80.9 us; the launch traced here: 80.3 us
  waiting for transfers between devices  23.8 us (29%)
  starting transfers between devices  23.4 us (29%)
  Pallas kernels  21.1 us (26%)
  local copies, waits for them, and re-layouts  10.4 us (13%)
  other arithmetic  0.89 us (1%)
    ppermute x4, waiting for transfers between devices, ring_step(): return lax.ppermute(value, 'op', pairs)  20.1 us
    pallas_call x1, Pallas kernels, run_tasks(): pl.pallas_call(functools.partial(tasks_kernel, n, terms_per, kinds), out_...  17.1 us
    ppermute x13, starting transfers between devices, exchange(): return lax.ppermute(value, 'op', [(i, i ^ mask) for i in range(n)])  14.4 us
    unnamed x29, local copies, waits for them, and re-layouts  10.4 us
    ppermute x4, starting transfers between devices, ring_step(): return lax.ppermute(value, 'op', pairs)  9.04 us
    ppermute x13, waiting for transfers between devices, exchange(): return lax.ppermute(value, 'op', [(i, i ^ mask) for i in range(n)])  3.7 us
    pallas_call x1, Pallas kernels, make_plan(): pl.pallas_call(functools.partial(plan_kernel, n, terms), out_shape=jax.Sh...  2.15 us
  transfers between devices with their start and end apart: 17, of which 7 were waited for; matrix products, arithmetic and copies ran while one was open for 0% of the time, Pallas kernels for 4%

profile of v5, /device:TPU:0, one launch (start us, length us, event | category | flops | bytes accessed | tf_op | source)
XLA Modules:
  0.0 80.3 jit_solution(1786002000585569392)
XLA Ops:
  0.6 1.0 %copy.7 = bf16[4,128,128]{1,2,0:T(8,128)(2,1)S(1)} copy(bf16[4,128,128]{2,1,0:T(8,128)(2,1)} %param.6) | data formatting | bytes 262144 | tf_op args[2]
  1.7 0.5 collective-permute-start.1
  2.2 0.1 collective-permute-start
  2.3 1.4 %collective-permute-done = bf16[2,128,128]{2,1,0:T(8,128)(2,1)S(1)} collective-permute-done((bf16[2,128,128]{2,1,0:T(8,128)(2,1)}, bf16[2,128,128]{2,1,0:T(8,128)(2,1)S(1)}, u32[]{:S(2)}, u32[]{:S(2)}) %collective-permute-start) | collective-permute-done | bytes 65568 | tf_op jit(solution)/shard_map/ppermute | solution.py:19
  3.6 0.0 collective-permute-done.1
  3.6 0.9 %pad_maximum_fusion.refs_0_ = bf16[12,128,128]{2,1,0:T(8,128)(2,1)S(1)} fusion(bf16[4,128,128]{2,1,0:T(8,128)(2,1)S(1)} %collective-permute-done.1, bf16[2,128,128]{2,1,0:T(8,128)(2,1)S(1)} %collective-permute-done, bf16[4,128,128]{2,1,0:T(8,128)(2,1)S(1)} %bitcast.4, bf16[2,128,128]{2,1,0:T(8,128)(2,1)} %bitcast.6), kind=kLoop, calls=%fused_computation | loop fusion | flops 589824 | bytes 786432 | tf_op jit(solution)/shard_map/concatenate | solution.py:357
  4.5 2.8 %collective-permute-start.2 = (bf16[12,128,128]{2,1,0:T(8,128)(2,1)S(1)}, bf16[12,128,128]{2,1,0:T(8,128)(2,1)S(1)}, u32[]{:S(2)}, u32[]{:S(2)}) collective-permute-start(bf16[12,128,128]{2,1,0:T(8,128)(2,1)S(1)} %pad_maximum_fusion.refs_0_), channel_id=1, source_target_pairs={{0,4},{1,3},{4,8},{5,1},{8,12},{9,5},{12,14},{13,9},{14,10},{15,13... | collective-permute-start | bytes 1179656 | tf_op jit(solution)/shard_map/ppermute | solution.py:33
  7.4 5.7 %collective-permute-done.2.refs_1_ = bf16[12,128,128]{2,1,0:T(8,128)(2,1)S(1)} collective-permute-done((bf16[12,128,128]{2,1,0:T(8,128)(2,1)S(1)}, bf16[12,128,128]{2,1,0:T(8,128)(2,1)S(1)}, u32[]{:S(2)}, u32[]{:S(2)}) %collective-permute-start.2) | collective-permute-done | bytes 393248 | tf_op jit(solution)/shard_map/ppermute | solution.py:33
  13.1 2.1 %collective-permute-start.4 = (bf16[12,128,128]{2,1,0:T(8,128)(2,1)S(1)}, bf16[12,128,128]{2,1,0:T(8,128)(2,1)S(1)}, u32[]{:S(2)}, u32[]{:S(2)}) collective-permute-start(bf16[12,128,128]{2,1,0:T(8,128)(2,1)S(1)} %collective-permute-done.2.refs_1_), channel_id=1, source_target_pairs={{0,4},{1,3},{4,8},{5,1},{8,12},{9,5},{12,14},{13,9},{14,10},{15,13... | collective-permute-start | bytes 1179656 | tf_op jit(solution)/shard_map/ppermute | solution.py:33
  15.1 5.7 %collective-permute-done.4.refs_3_ = bf16[12,128,128]{2,1,0:T(8,128)(2,1)S(1)} collective-permute-done((bf16[12,128,128]{2,1,0:T(8,128)(2,1)S(1)}, bf16[12,128,128]{2,1,0:T(8,128)(2,1)S(1)}, u32[]{:S(2)}, u32[]{:S(2)}) %collective-permute-start.4) | collective-permute-done | bytes 393248 | tf_op jit(solution)/shard_map/ppermute | solution.py:33
  20.8 0.0 copy-start.1
  20.8 2.1 %collective-permute-start.6 = (bf16[12,128,128]{2,1,0:T(8,128)(2,1)S(1)}, bf16[12,128,128]{2,1,0:T(8,128)(2,1)S(1)}, u32[]{:S(2)}, u32[]{:S(2)}) collective-permute-start(bf16[12,128,128]{2,1,0:T(8,128)(2,1)S(1)} %collective-permute-done.4.refs_3_), channel_id=1, source_target_pairs={{0,4},{1,3},{4,8},{5,1},{8,12},{9,5},{12,14},{13,9},{14,10},{15,13... | collective-permute-start | bytes 1179656 | tf_op jit(solution)/shard_map/ppermute | solution.py:33
  22.9 0.0 collective-permute-start.3
  22.9 0.5 collective-permute-start.5
  23.4 5.2 %collective-permute-done.6.refs_5_ = bf16[12,128,128]{2,1,0:T(8,128)(2,1)S(1)} collective-permute-done((bf16[12,128,128]{2,1,0:T(8,128)(2,1)S(1)}, bf16[12,128,128]{2,1,0:T(8,128)(2,1)S(1)}, u32[]{:S(2)}, u32[]{:S(2)}) %collective-permute-start.6) | collective-permute-done | bytes 393248 | tf_op jit(solution)/shard_map/ppermute | solution.py:33
  28.6 0.0 copy-start.3
  28.6 2.1 %collective-permute-start.8 = (bf16[12,128,128]{2,1,0:T(8,128)(2,1)S(1)}, bf16[12,128,128]{2,1,0:T(8,128)(2,1)S(1)}, u32[]{:S(2)}, u32[]{:S(2)}) collective-permute-start(bf16[12,128,128]{2,1,0:T(8,128)(2,1)S(1)} %collective-permute-done.6.refs_5_), channel_id=1, source_target_pairs={{0,4},{1,3},{4,8},{5,1},{8,12},{9,5},{12,14},{13,9},{14,10},{15,13... | collective-permute-start | bytes 1179656 | tf_op jit(solution)/shard_map/ppermute | solution.py:33
  30.7 0.0 collective-permute-start.7
  30.7 2.2 %shard_map.67.plan_ref = s32[8,384]{1,0:T(8,128)} custom-call(s32[4,256]{1,0:T(4,128)} %bitcast.7), custom_call_target="tpu_custom_call" | custom-call | tf_op jit(solution)/shard_map/pallas_call | solution.py:135
  32.8 0.0 collective-permute-done.3.refs_2_
  32.8 0.0 copy-start.5
  32.8 0.0 collective-permute-done.5.refs_4_
  32.9 0.0 copy-start.7
  32.9 3.5 %collective-permute-done.8.refs_7_ = bf16[12,128,128]{2,1,0:T(8,128)(2,1)S(1)} collective-permute-done((bf16[12,128,128]{2,1,0:T(8,128)(2,1)S(1)}, bf16[12,128,128]{2,1,0:T(8,128)(2,1)S(1)}, u32[]{:S(2)}, u32[]{:S(2)}) %collective-permute-start.8) | collective-permute-done | bytes 393248 | tf_op jit(solution)/shard_map/ppermute | solution.py:33
  36.4 0.0 copy-start.9
  36.4 0.0 collective-permute-done.7.refs_6_
  36.4 0.0 copy-done.1
  36.4 0.0 copy-done.3
  36.4 0.0 copy-done.5
  36.4 0.0 copy-done.7
  36.4 0.7 copy-done.9
  37.1 0.0 copy-start.11
  37.1 0.7 copy-done.11
  37.9 0.0 copy-start.13
  37.9 0.7 copy-done.13
  38.6 17.1 %shard_map.68 = (bf16[2080,128]{1,0:T(8,128)(2,1)}, f32[8,256,128]{2,1,0:T(8,128)}, f32[8,128]{1,0:T(8,128)S(1)}) custom-call(s32[8,384]{1,0:T(8,128)S(1)} %copy-done.13, bf16[256,128,128]{2,1,0:T(8,128)(2,1)} %left_ref.1, bf16[12,128,128]{2,1,0:T(8,128)(2,1)S(1)} %pad_maximum_fusion.refs_0_, bf16[12,128,128]{2,1,0:T(8,128)(2,1)S(1)} %collective-permute-done.2.refs_1_, ...), custom_call_target="tpu_custom_call" | custom-call | flops 4294967296 | bytes 15588608 | tf_op jit(solution)/shard_map/pallas_call | solution.py:265
  55.7 0.1 collective-permute-start.9
  55.8 2.1 %collective-permute-done.9.received_ref = bf16[2080,128]{1,0:T(8,128)(2,1)S(1)} collective-permute-done((bf16[2080,128]{1,0:T(8,128)(2,1)}, bf16[2080,128]{1,0:T(8,128)(2,1)S(1)}, u32[]{:S(2)}, u32[]{:S(2)}) %collective-permute-start.9) | collective-permute-done | bytes 532512 | tf_op jit(solution)/shard_map/ppermute | solution.py:19
  57.9 0.0 copy-start
  57.9 1.2 %copy-done = f32[8,256,128]{2,1,0:T(8,128)S(1)} copy-done((f32[8,256,128]{2,1,0:T(8,128)S(1)}, f32[8,256,128]{2,1,0:T(8,128)}, u32[]{:S(2)}) %copy-start) | copy-done | bytes 1048600
  59.1 0.1 shard_map.69
  59.3 0.2 collective-permute-start.10
  59.5 0.4 collective-permute-start.11
  59.8 3.0 %collective-permute-start.12 = (bf16[288,128]{1,0:T(8,128)(2,1)S(1)}, bf16[288,128]{1,0:T(8,128)(2,1)S(1)}, u32[]{:S(2)}, u32[]{:S(2)}) collective-permute-start(bf16[288,128]{1,0:T(8,128)(2,1)S(1)} %get-tuple-element.34), channel_id=1, source_target_pairs={{0,6},{1,7},{2,4},{3,5},{4,2},{5,3},{6,0},{7,1},{8,14},{9,15},{10,... | collective-permute-start | bytes 221192 | tf_op jit(solution)/shard_map/ppermute | solution.py:19
  62.8 4.3 %collective-permute-start.13 = (bf16[288,128]{1,0:T(8,128)(2,1)S(1)}, bf16[288,128]{1,0:T(8,128)(2,1)S(1)}, u32[]{:S(2)}, u32[]{:S(2)}) collective-permute-start(bf16[288,128]{1,0:T(8,128)(2,1)S(1)} %get-tuple-element.35), channel_id=1, source_target_pairs={{0,8},{1,9},{2,10},{3,11},{4,12},{5,13},{6,14},{7,15},{8,0},{9,1},... | collective-permute-start | bytes 221192 | tf_op jit(solution)/shard_map/ppermute | solution.py:19
  67.2 0.9 %collective-permute-start.14 = (bf16[288,128]{1,0:T(8,128)(2,1)S(1)}, bf16[288,128]{1,0:T(8,128)(2,1)S(1)}, u32[]{:S(2)}, u32[]{:S(2)}) collective-permute-start(bf16[288,128]{1,0:T(8,128)(2,1)S(1)} %get-tuple-element.36), channel_id=1, source_target_pairs={{0,10},{1,11},{2,8},{3,9},{4,14},{5,15},{6,12},{7,13},{8,2},{9,3},... | collective-permute-start | bytes 221192 | tf_op jit(solution)/shard_map/ppermute | solution.py:19
  68.1 0.0 collective-permute-done.10.refs_0_
  68.1 4.4 %collective-permute-start.15 = (bf16[288,128]{1,0:T(8,128)(2,1)S(1)}, bf16[288,128]{1,0:T(8,128)(2,1)S(1)}, u32[]{:S(2)}, u32[]{:S(2)}) collective-permute-start(bf16[288,128]{1,0:T(8,128)(2,1)S(1)} %get-tuple-element.37), channel_id=1, source_target_pairs={{0,12},{1,13},{2,14},{3,15},{4,8},{5,9},{6,10},{7,11},{8,4},{9,5},... | collective-permute-start | bytes 221192 | tf_op jit(solution)/shard_map/ppermute | solution.py:19
  72.4 0.0 collective-permute-done.11.refs_1_
  72.5 0.0 collective-permute-start.16
  72.5 0.0 copy-start.2
  72.5 1.0 %copy-done.2 = bf16[12,128,128]{2,1,0:T(8,128)(2,1)S(1)} copy-done((bf16[12,128,128]{2,1,0:T(8,128)(2,1)S(1)}, bf16[12,128,128]{2,1,0:T(8,128)(2,1)}, u32[]{:S(2)}) %copy-start.2) | copy-done | bytes 393240
  73.5 1.0 %copy-done.4 = bf16[12,128,128]{2,1,0:T(8,128)(2,1)S(1)} copy-done((bf16[12,128,128]{2,1,0:T(8,128)(2,1)S(1)}, bf16[12,128,128]{2,1,0:T(8,128)(2,1)}, u32[]{:S(2)}) %copy-start.4) | copy-done | bytes 393240
  74.4 1.0 %copy-done.6 = bf16[12,128,128]{2,1,0:T(8,128)(2,1)S(1)} copy-done((bf16[12,128,128]{2,1,0:T(8,128)(2,1)S(1)}, bf16[12,128,128]{2,1,0:T(8,128)(2,1)}, u32[]{:S(2)}) %copy-start.6) | copy-done | bytes 393240
  75.4 1.0 %copy-done.8 = bf16[12,128,128]{2,1,0:T(8,128)(2,1)S(1)} copy-done((bf16[12,128,128]{2,1,0:T(8,128)(2,1)S(1)}, bf16[12,128,128]{2,1,0:T(8,128)(2,1)}, u32[]{:S(2)}) %copy-start.8) | copy-done | bytes 393240
  76.4 1.0 %copy-done.10 = bf16[12,128,128]{2,1,0:T(8,128)(2,1)S(1)} copy-done((bf16[12,128,128]{2,1,0:T(8,128)(2,1)S(1)}, bf16[12,128,128]{2,1,0:T(8,128)(2,1)}, u32[]{:S(2)}) %copy-start.10) | copy-done | bytes 393240
  77.4 1.0 %copy-done.12 = bf16[12,128,128]{2,1,0:T(8,128)(2,1)S(1)} copy-done((bf16[12,128,128]{2,1,0:T(8,128)(2,1)S(1)}, bf16[12,128,128]{2,1,0:T(8,128)(2,1)}, u32[]{:S(2)}) %copy-start.12) | copy-done | bytes 393240
  78.4 1.0 %shard_map.71 = f32[2,2]{1,0:T(2,128)} custom-call(bf16[12,128,128]{2,1,0:T(8,128)(2,1)S(1)} %pad_maximum_fusion.refs_0_, bf16[12,128,128]{2,1,0:T(8,128)(2,1)S(1)} %collective-permute-done.2.refs_1_, bf16[12,128,128]{2,1,0:T(8,128)(2,1)S(1)} %copy-done.6, bf16[12,128,128]{2,1,0:T(8,128)(2,1)S(1)} %copy-done.2, bf16[12,128,128]{2,1,0:T(8,128)(2,1)S(1)} %copy-done.8, ...), custom_call_target="tpu_custom_call" | custom-call | tf_op jit(solution)/shard_map/pallas_call | solution.py:301
  79.4 0.0 collective-permute-done.12.refs_2_
  79.4 0.0 collective-permute-done.13.refs_3_
  79.4 0.0 collective-permute-done.14.refs_4_
  79.4 0.0 collective-permute-done.15.refs_5_
  79.4 0.2 collective-permute-done.16.refs_6_
  79.6 0.7 shard_map.70
  (5 shorter events, 0.0 us)
Async XLA Ops:
  1.7 2.0 %collective-permute-start.1 = (bf16[4,128,128]{2,1,0:T(8,128)(2,1)S(1)}, bf16[4,128,128]{2,1,0:T(8,128)(2,1)S(1)}, u32[]{:S(2)}, u32[]{:S(2)}) collective-permute-start(bf16[4,128,128]{2,1,0:T(8,128)(2,1)S(1)} %bitcast.3), channel_id=1, source_target_pairs={{0,1},{1,0},{2,3},{3,2},{4,5},{5,4},{6,7},{7,6},{8,9},{9,8},{10,11... | collective-permute-start | bytes 393224 | tf_op jit(solution)/shard_map/ppermute | solution.py:19
  2.2 1.5 %collective-permute-start = (bf16[2,128,128]{2,1,0:T(8,128)(2,1)}, bf16[2,128,128]{2,1,0:T(8,128)(2,1)S(1)}, u32[]{:S(2)}, u32[]{:S(2)}) collective-permute-start(bf16[2,128,128]{2,1,0:T(8,128)(2,1)} %bitcast.5), channel_id=1, source_target_pairs={{0,1},{1,0},{2,3},{3,2},{4,5},{5,4},{6,7},{7,6},{8,9},{9,8},{10,11... | collective-permute-start | bytes 196616 | tf_op jit(solution)/shard_map/ppermute | solution.py:19
  4.5 8.5 %collective-permute-start.2 = (bf16[12,128,128]{2,1,0:T(8,128)(2,1)S(1)}, bf16[12,128,128]{2,1,0:T(8,128)(2,1)S(1)}, u32[]{:S(2)}, u32[]{:S(2)}) collective-permute-start(bf16[12,128,128]{2,1,0:T(8,128)(2,1)S(1)} %pad_maximum_fusion.refs_0_), channel_id=1, source_target_pairs={{0,4},{1,3},{4,8},{5,1},{8,12},{9,5},{12,14},{13,9},{14,10},{15,13... | collective-permute-start | bytes 1179656 | tf_op jit(solution)/shard_map/ppermute | solution.py:33
  13.1 7.8 %collective-permute-start.4 = (bf16[12,128,128]{2,1,0:T(8,128)(2,1)S(1)}, bf16[12,128,128]{2,1,0:T(8,128)(2,1)S(1)}, u32[]{:S(2)}, u32[]{:S(2)}) collective-permute-start(bf16[12,128,128]{2,1,0:T(8,128)(2,1)S(1)} %collective-permute-done.2.refs_1_), channel_id=1, source_target_pairs={{0,4},{1,3},{4,8},{5,1},{8,12},{9,5},{12,14},{13,9},{14,10},{15,13... | collective-permute-start | bytes 1179656 | tf_op jit(solution)/shard_map/ppermute | solution.py:33
  20.8 15.6 %copy-start.1 = (bf16[12,128,128]{2,1,0:T(8,128)(2,1)}, bf16[12,128,128]{2,1,0:T(8,128)(2,1)S(1)}, u32[]{:S(2)}) copy-start(bf16[12,128,128]{2,1,0:T(8,128)(2,1)S(1)} %collective-permute-done.4.refs_3_) | copy-start | bytes 1179652
  20.8 7.8 %collective-permute-start.6 = (bf16[12,128,128]{2,1,0:T(8,128)(2,1)S(1)}, bf16[12,128,128]{2,1,0:T(8,128)(2,1)S(1)}, u32[]{:S(2)}, u32[]{:S(2)}) collective-permute-start(bf16[12,128,128]{2,1,0:T(8,128)(2,1)S(1)} %collective-permute-done.4.refs_3_), channel_id=1, source_target_pairs={{0,4},{1,3},{4,8},{5,1},{8,12},{9,5},{12,14},{13,9},{14,10},{15,13... | collective-permute-start | bytes 1179656 | tf_op jit(solution)/shard_map/ppermute | solution.py:33
  22.9 9.9 %collective-permute-start.3 = (bf16[12,128,128]{2,1,0:T(8,128)(2,1)S(1)}, bf16[12,128,128]{2,1,0:T(8,128)(2,1)S(1)}, u32[]{:S(2)}, u32[]{:S(2)}) collective-permute-start(bf16[12,128,128]{2,1,0:T(8,128)(2,1)S(1)} %collective-permute-done.2.refs_1_), channel_id=1, source_target_pairs={{0,1},{1,0},{2,3},{3,2},{4,5},{5,4},{6,7},{7,6},{8,9},{9,8},{10,11... | collective-permute-start | bytes 1179656 | tf_op jit(solution)/shard_map/ppermute | solution.py:19
  22.9 9.9 %collective-permute-start.5 = (bf16[12,128,128]{2,1,0:T(8,128)(2,1)S(1)}, bf16[12,128,128]{2,1,0:T(8,128)(2,1)S(1)}, u32[]{:S(2)}, u32[]{:S(2)}) collective-permute-start(bf16[12,128,128]{2,1,0:T(8,128)(2,1)S(1)} %collective-permute-done.4.refs_3_), channel_id=1, source_target_pairs={{0,1},{1,0},{2,3},{3,2},{4,5},{5,4},{6,7},{7,6},{8,9},{9,8},{10,11... | collective-permute-start | bytes 1179656 | tf_op jit(solution)/shard_map/ppermute | solution.py:19
  28.6 7.8 %copy-start.3 = (bf16[12,128,128]{2,1,0:T(8,128)(2,1)}, bf16[12,128,128]{2,1,0:T(8,128)(2,1)S(1)}, u32[]{:S(2)}) copy-start(bf16[12,128,128]{2,1,0:T(8,128)(2,1)S(1)} %collective-permute-done.6.refs_5_) | copy-start | bytes 1179652
  28.6 7.8 %collective-permute-start.8 = (bf16[12,128,128]{2,1,0:T(8,128)(2,1)S(1)}, bf16[12,128,128]{2,1,0:T(8,128)(2,1)S(1)}, u32[]{:S(2)}, u32[]{:S(2)}) collective-permute-start(bf16[12,128,128]{2,1,0:T(8,128)(2,1)S(1)} %collective-permute-done.6.refs_5_), channel_id=1, source_target_pairs={{0,4},{1,3},{4,8},{5,1},{8,12},{9,5},{12,14},{13,9},{14,10},{15,13... | collective-permute-start | bytes 1179656 | tf_op jit(solution)/shard_map/ppermute | solution.py:33
  30.7 5.7 %collective-permute-start.7 = (bf16[12,128,128]{2,1,0:T(8,128)(2,1)S(1)}, bf16[12,128,128]{2,1,0:T(8,128)(2,1)S(1)}, u32[]{:S(2)}, u32[]{:S(2)}) collective-permute-start(bf16[12,128,128]{2,1,0:T(8,128)(2,1)S(1)} %collective-permute-done.6.refs_5_), channel_id=1, source_target_pairs={{0,1},{1,0},{2,3},{3,2},{4,5},{5,4},{6,7},{7,6},{8,9},{9,8},{10,11... | collective-permute-start | bytes 1179656 | tf_op jit(solution)/shard_map/ppermute | solution.py:19
  32.8 3.6 %copy-start.5 = (bf16[12,128,128]{2,1,0:T(8,128)(2,1)}, bf16[12,128,128]{2,1,0:T(8,128)(2,1)S(1)}, u32[]{:S(2)}) copy-start(bf16[12,128,128]{2,1,0:T(8,128)(2,1)S(1)} %collective-permute-done.3.refs_2_) | copy-start | bytes 1179652
  32.9 3.6 %copy-start.7 = (bf16[12,128,128]{2,1,0:T(8,128)(2,1)}, bf16[12,128,128]{2,1,0:T(8,128)(2,1)S(1)}, u32[]{:S(2)}) copy-start(bf16[12,128,128]{2,1,0:T(8,128)(2,1)S(1)} %collective-permute-done.5.refs_4_) | copy-start | bytes 1179652
  36.4 0.8 copy-start.9
  37.1 0.8 copy-start.11
  37.9 0.7 copy-start.13
  55.7 2.2 %collective-permute-start.9 = (bf16[2080,128]{1,0:T(8,128)(2,1)}, bf16[2080,128]{1,0:T(8,128)(2,1)S(1)}, u32[]{:S(2)}, u32[]{:S(2)}) collective-permute-start(bf16[2080,128]{1,0:T(8,128)(2,1)} %get-tuple-element.29), channel_id=1, source_target_pairs={{0,1},{1,0},{2,3},{3,2},{4,5},{5,4},{6,7},{7,6},{8,9},{9,8},{10,11... | collective-permute-start | bytes 1597448 | tf_op jit(solution)/shard_map/ppermute | solution.py:19
  57.9 1.2 %copy-start = (f32[8,256,128]{2,1,0:T(8,128)S(1)}, f32[8,256,128]{2,1,0:T(8,128)}, u32[]{:S(2)}) copy-start(f32[8,256,128]{2,1,0:T(8,128)} %get-tuple-element.26.keep_ref) | copy-start | bytes 3145732
  59.3 8.8 %collective-permute-start.10 = (bf16[288,128]{1,0:T(8,128)(2,1)S(1)}, bf16[288,128]{1,0:T(8,128)(2,1)S(1)}, u32[]{:S(2)}, u32[]{:S(2)}) collective-permute-start(bf16[288,128]{1,0:T(8,128)(2,1)S(1)} %get-tuple-element.32), channel_id=1, source_target_pairs={{0,2},{1,3},{2,0},{3,1},{4,6},{5,7},{6,4},{7,5},{8,10},{9,11},{10,... | collective-permute-start | bytes 221192 | tf_op jit(solution)/shard_map/ppermute | solution.py:19
  59.5 13.0 %collective-permute-start.11 = (bf16[288,128]{1,0:T(8,128)(2,1)S(1)}, bf16[288,128]{1,0:T(8,128)(2,1)S(1)}, u32[]{:S(2)}, u32[]{:S(2)}) collective-permute-start(bf16[288,128]{1,0:T(8,128)(2,1)S(1)} %get-tuple-element.33), channel_id=1, source_target_pairs={{0,4},{1,5},{2,6},{3,7},{4,0},{5,1},{6,2},{7,3},{8,12},{9,13},{10,... | collective-permute-start | bytes 221192 | tf_op jit(solution)/shard_map/ppermute | solution.py:19
  59.8 19.6 %collective-permute-start.12 = (bf16[288,128]{1,0:T(8,128)(2,1)S(1)}, bf16[288,128]{1,0:T(8,128)(2,1)S(1)}, u32[]{:S(2)}, u32[]{:S(2)}) collective-permute-start(bf16[288,128]{1,0:T(8,128)(2,1)S(1)} %get-tuple-element.34), channel_id=1, source_target_pairs={{0,6},{1,7},{2,4},{3,5},{4,2},{5,3},{6,0},{7,1},{8,14},{9,15},{10,... | collective-permute-start | bytes 221192 | tf_op jit(solution)/shard_map/ppermute | solution.py:19
  62.8 16.6 %collective-permute-start.13 = (bf16[288,128]{1,0:T(8,128)(2,1)S(1)}, bf16[288,128]{1,0:T(8,128)(2,1)S(1)}, u32[]{:S(2)}, u32[]{:S(2)}) collective-permute-start(bf16[288,128]{1,0:T(8,128)(2,1)S(1)} %get-tuple-element.35), channel_id=1, source_target_pairs={{0,8},{1,9},{2,10},{3,11},{4,12},{5,13},{6,14},{7,15},{8,0},{9,1},... | collective-permute-start | bytes 221192 | tf_op jit(solution)/shard_map/ppermute | solution.py:19
  67.2 12.3 %collective-permute-start.14 = (bf16[288,128]{1,0:T(8,128)(2,1)S(1)}, bf16[288,128]{1,0:T(8,128)(2,1)S(1)}, u32[]{:S(2)}, u32[]{:S(2)}) collective-permute-start(bf16[288,128]{1,0:T(8,128)(2,1)S(1)} %get-tuple-element.36), channel_id=1, source_target_pairs={{0,10},{1,11},{2,8},{3,9},{4,14},{5,15},{6,12},{7,13},{8,2},{9,3},... | collective-permute-start | bytes 221192 | tf_op jit(solution)/shard_map/ppermute | solution.py:19
  68.1 11.4 %collective-permute-start.15 = (bf16[288,128]{1,0:T(8,128)(2,1)S(1)}, bf16[288,128]{1,0:T(8,128)(2,1)S(1)}, u32[]{:S(2)}, u32[]{:S(2)}) collective-permute-start(bf16[288,128]{1,0:T(8,128)(2,1)S(1)} %get-tuple-element.37), channel_id=1, source_target_pairs={{0,12},{1,13},{2,14},{3,15},{4,8},{5,9},{6,10},{7,11},{8,4},{9,5},... | collective-permute-start | bytes 221192 | tf_op jit(solution)/shard_map/ppermute | solution.py:19
  72.5 7.2 %collective-permute-start.16 = (bf16[288,128]{1,0:T(8,128)(2,1)S(1)}, bf16[288,128]{1,0:T(8,128)(2,1)S(1)}, u32[]{:S(2)}, u32[]{:S(2)}) collective-permute-start(bf16[288,128]{1,0:T(8,128)(2,1)S(1)} %get-tuple-element.38), channel_id=1, source_target_pairs={{0,14},{1,15},{2,12},{3,13},{4,10},{5,11},{6,8},{7,9},{8,6},{9,7},... | collective-permute-start | bytes 221192 | tf_op jit(solution)/shard_map/ppermute | solution.py:19
  72.5 1.0 %copy-start.2 = (bf16[12,128,128]{2,1,0:T(8,128)(2,1)S(1)}, bf16[12,128,128]{2,1,0:T(8,128)(2,1)}, u32[]{:S(2)}) copy-start(bf16[12,128,128]{2,1,0:T(8,128)(2,1)} %copy-done.1) | copy-start | bytes 1179652
  73.5 1.0 %copy-start.4 = (bf16[12,128,128]{2,1,0:T(8,128)(2,1)S(1)}, bf16[12,128,128]{2,1,0:T(8,128)(2,1)}, u32[]{:S(2)}) copy-start(bf16[12,128,128]{2,1,0:T(8,128)(2,1)} %copy-done.3) | copy-start | bytes 1179652
  74.4 1.0 %copy-start.6 = (bf16[12,128,128]{2,1,0:T(8,128)(2,1)S(1)}, bf16[12,128,128]{2,1,0:T(8,128)(2,1)}, u32[]{:S(2)}) copy-start(bf16[12,128,128]{2,1,0:T(8,128)(2,1)} %copy-done.5) | copy-start | bytes 1179652
  75.4 1.0 %copy-start.8 = (bf16[12,128,128]{2,1,0:T(8,128)(2,1)S(1)}, bf16[12,128,128]{2,1,0:T(8,128)(2,1)}, u32[]{:S(2)}) copy-start(bf16[12,128,128]{2,1,0:T(8,128)(2,1)} %copy-done.7) | copy-start | bytes 1179652
  76.4 1.0 %copy-start.10 = (bf16[12,128,128]{2,1,0:T(8,128)(2,1)S(1)}, bf16[12,128,128]{2,1,0:T(8,128)(2,1)}, u32[]{:S(2)}) copy-start(bf16[12,128,128]{2,1,0:T(8,128)(2,1)} %copy-done.9) | copy-start | bytes 1179652
  77.4 1.0 %copy-start.12 = (bf16[12,128,128]{2,1,0:T(8,128)(2,1)S(1)}, bf16[12,128,128]{2,1,0:T(8,128)(2,1)}, u32[]{:S(2)}) copy-start(bf16[12,128,128]{2,1,0:T(8,128)(2,1)} %copy-done.11) | copy-start | bytes 1179652

commit v6 on v5

--- a/solution.py
+++ b/solution.py
@@ -8,11 +8,11 @@
 from jax.sharding import PartitionSpec as P
 
 MIB = 1024 * 1024
+AHEAD = 3
 TAIL = 32
 TRIALS = 2
 CHUNK = 32
 PAIRS = 16
-AHEAD = 3
 
 
 def exchange(value, n, mask):
@@ -74,11 +74,16 @@
     return value.reshape(16, 8, 128).sum(axis=0)
 
 
+def fits(n):
+    return n <= 16
+
+
 def run_of(slots, n):
     return 4 if slots >= 8 * n else 2
 
 
-def plan_kernel(n, terms, tasks_ref, plan_ref):
+def plan_kernel(n, terms, tasks_ref, *refs):
+    plan_ref = refs[-1]
     slots = tasks_ref.shape[1]
     places = plan_ref.shape[1]
     rows = tasks_ref[...].astype(jnp.float32)
@@ -129,53 +134,54 @@
     plan_ref[6:8] = jnp.zeros((2, places), jnp.int32)
 
 
-def make_plan(tasks, n, terms):
-    slots = tasks.shape[1]
-    most = slots + min(slots, n) * (run_of(slots, n) - 1) + CHUNK
+def source_places(slots, n):
+    most = slots + min(slots, n) * (run_of(slots, n) - 1)
+    return -(-most // CHUNK) * CHUNK
+
+
+def make_plan(tasks, left_ops, n, terms):
+    most = source_places(tasks.shape[1], n) + 2 * PAIRS
+    given = [tasks, left_ops] if fits(n) else [tasks]
     return pl.pallas_call(
         functools.partial(plan_kernel, n, terms),
+        in_specs=[pl.BlockSpec(memory_space=pltpu.VMEM)] * len(given),
         out_shape=jax.ShapeDtypeStruct((8, -(-most // 128) * 128), jnp.int32),
-    )(tasks)
+        compiler_params=pltpu.CompilerParams(vmem_limit_bytes=16 * MIB),
+    )(*given)
 
 
 def tasks_kernel(n, terms_per, kinds, plan_ref, left_ref, *refs):
     blocks, refs = refs[: len(kinds)], refs[len(kinds) :]
-    send_ref, keep_ref, own_ref, trial, right, acc, left, halves, block_sem, left_sem = refs
-    per = TRIALS + terms_per
+    send_ref, keep_ref, own_ref, trial, right, acc, halves, block_sem, *refs = refs
     run = run_of(left_ref.shape[0], n)
     source_turns, target_turns = plan_ref[5, 0], plan_ref[5, 1]
 
-    def block_copies(b, which):
-        step, swapped = kinds[b]
-        copies = []
-        for half in range(2):
-            owner = owner_of(step, swapped, half, n)
-            if which == 0:
-                source, to = blocks[b].at[pl.ds(half * per, TRIALS)], trial.at[owner]
-            else:
-                source = blocks[b].at[pl.ds(half * per + TRIALS, terms_per)]
-                to = right.at[pl.ds(owner * terms_per, terms_per)]
-            copies.append(pltpu.make_async_copy(source, to, block_sem.at[b, 2 * half + which]))
-        return copies
+    def block_copy(b, which):
+        owner = owner_of(*kinds[b], n)
+        if which == 0:
+            source, to = blocks[b].at[pl.ds(0, TRIALS)], trial.at[owner]
+        else:
+            source = blocks[b].at[pl.ds(TRIALS, terms_per)]
+            to = right.at[pl.ds(owner * terms_per, terms_per)]
+        return pltpu.make_async_copy(source, to, block_sem.at[b, which])
 
     def fetch(turn):
+        left, left_sem = refs
         at = lax.rem(turn, AHEAD)
         for u in range(CHUNK):
             slot = plan_ref[0, turn * CHUNK + u]
             pltpu.make_async_copy(left_ref.at[slot], left.at[at, u], left_sem.at[at]).start()
 
     for b in range(len(kinds)):
-        for copy in block_copies(b, 0):
-            copy.start()
-    for turn in range(AHEAD - 1):
+        block_copy(b, 0).start()
+    for turn in range(AHEAD - 1) if refs else ():
 
         @pl.when(turn < source_turns)
         def _():
             fetch(turn)
 
     for b in range(len(kinds)):
-        for copy in block_copies(b, 1):
-            copy.start()
+        block_copy(b, 1).start()
     right[n * terms_per] = jnp.zeros((128, 128), jnp.bfloat16)
 
     def clear(s, carry):
@@ -184,31 +190,35 @@
 
     lax.fori_loop(0, n, clear, 0)
     for b in range(len(kinds)):
-        for copy in block_copies(b, 0):
-            copy.wait()
+        block_copy(b, 0).wait()
 
     def source_turn(turn, carry):
-        @pl.when(turn + AHEAD - 1 < source_turns)
-        def _():
-            fetch(turn + AHEAD - 1)
-
-        at = lax.rem(turn, AHEAD)
-        pltpu.make_async_copy(left_ref.at[pl.ds(0, CHUNK)], left.at[at], left_sem.at[at]).wait()
         first = turn * CHUNK
-        for r in range(CHUNK // run):
-            source = plan_ref[1, first + r * run]
+        if refs:
+            left, left_sem = refs
+
+            @pl.when(turn + AHEAD - 1 < source_turns)
+            def _():
+                fetch(turn + AHEAD - 1)
+
+            at = lax.rem(turn, AHEAD)
+            pltpu.make_async_copy(left_ref.at[pl.ds(0, CHUNK)], left.at[at], left_sem.at[at]).wait()
+        for r in range(0, CHUNK, run):
+            source = plan_ref[1, first + r]
             vectors = jnp.concatenate([trial[source, 0], trial[source, 1]], axis=1)
-            rows = left[at, r * run : (r + 1) * run].reshape(run * 128, 128)
+            if refs:
+                rows = left[at, r : r + run].reshape(run * 128, 128)
+            else:
+                rows = jnp.concatenate([left_ref[plan_ref[0, first + r + u]] for u in range(run)], axis=0)
             half = jnp.dot(rows, vectors, preferred_element_type=jnp.float32).astype(jnp.bfloat16)
             for u in range(run):
-                halves[first + r * run + u, 0] = half[u * 128 : (u + 1) * 128, :128]
-                halves[first + r * run + u, 1] = half[u * 128 : (u + 1) * 128, 128:]
+                halves[first + r + u, 0] = half[u * 128 : (u + 1) * 128, :128]
+                halves[first + r + u, 1] = half[u * 128 : (u + 1) * 128, 128:]
         return carry
 
     lax.fori_loop(0, source_turns, source_turn, 0)
     for b in range(len(kinds)):
-        for copy in block_copies(b, 1):
-            copy.wait()
+        block_copy(b, 1).wait()
 
     def target_turn(turn, carry):
         first = turn * 2 * PAIRS
@@ -258,10 +268,14 @@
 
 def run_tasks(n, plan, left_ops, blocks):
     slots = left_ops.shape[0]
-    places = plan.shape[1]
-    terms_per = blocks[0][0].shape[0] // 2 - TRIALS
+    terms_per = blocks[0][0].shape[0] - TRIALS
     kinds = tuple(block[1:] for block in blocks)
-    hbm = pl.BlockSpec(memory_space=pltpu.HBM)
+    small = fits(n)
+    given = pl.BlockSpec(memory_space=pltpu.VMEM if small else pltpu.HBM)
+    fetched = [] if small else [
+        pltpu.VMEM((AHEAD, CHUNK, 128, 128), jnp.bfloat16),
+        pltpu.SemaphoreType.DMA((AHEAD,)),
+    ]
     return pl.pallas_call(
         functools.partial(tasks_kernel, n, terms_per, kinds),
         out_shape=(
@@ -269,37 +283,35 @@
             jax.ShapeDtypeStruct((n // 2, 256, 128), jnp.float32),
             jax.ShapeDtypeStruct((8, 128), jnp.float32),
         ),
-        in_specs=[pl.BlockSpec(memory_space=pltpu.SMEM), hbm] + [hbm] * len(blocks),
+        in_specs=[pl.BlockSpec(memory_space=pltpu.SMEM)] + [given] * (1 + len(blocks)),
         scratch_shapes=[
             pltpu.VMEM((n, TRIALS, 128, 128), jnp.bfloat16),
             pltpu.VMEM((n * terms_per + 1, 128, 128), jnp.bfloat16),
             pltpu.VMEM((n + 1, 256, 128), jnp.float32),
-            pltpu.VMEM((AHEAD, CHUNK, 128, 128), jnp.bfloat16),
-            pltpu.VMEM((places, 2, 128, 128), jnp.bfloat16),
-            pltpu.SemaphoreType.DMA((len(blocks), 4)),
-            pltpu.SemaphoreType.DMA((AHEAD,)),
-        ],
-        compiler_params=pltpu.CompilerParams(vmem_limit_bytes=(53 if n <= 16 else 57) * MIB),
+            pltpu.VMEM((source_places(slots, n), 2, 128, 128), jnp.bfloat16),
+            pltpu.SemaphoreType.DMA((len(blocks), 2)),
+        ]
+        + fetched,
+        compiler_params=pltpu.CompilerParams(vmem_limit_bytes=(34 if small else 58) * MIB),
         cost_estimate=pl.CostEstimate(
             flops=slots * 8 * 128**3, bytes_accessed=slots * 32768 + n * 450000, transcendentals=0
         ),
     )(plan, left_ops, *[block[0] for block in blocks])
 
 
-def corr_kernel(spans, *refs):
+def corr_kernel(*refs):
     blocks, corr_ref = refs[:-1], refs[-1]
     total = [jnp.zeros((8, 128), jnp.float32)] * 3
-    for ref, span in zip(blocks, spans):
-        for start in (0, span):
-            t0, t1 = ref[start].astype(jnp.float32), ref[start + 1].astype(jnp.float32)
-            total = [total[0] + fold(t0 * t0), total[1] + fold(t0 * t1), total[2] + fold(t1 * t1)]
+    for ref in blocks:
+        t0, t1 = ref[0].astype(jnp.float32), ref[1].astype(jnp.float32)
+        total = [total[0] + fold(t0 * t0), total[1] + fold(t0 * t1), total[2] + fold(t1 * t1)]
     c00, c01, c11 = [jnp.sum(x) for x in total]
     corr_ref[...] = matrix_of({(0, 0): c00, (0, 1): c01, (1, 0): c01, (1, 1): c11})[0:2, 0:2]
 
 
 def correlate(blocks):
     return pl.pallas_call(
-        functools.partial(corr_kernel, [block.shape[0] // 2 for block in blocks]),
+        corr_kernel,
         out_shape=jax.ShapeDtypeStruct((2, 2), jnp.float32),
         compiler_params=pltpu.CompilerParams(vmem_limit_bytes=16 * MIB),
     )(*blocks)
@@ -350,23 +362,27 @@
     )(mine, total, *received)
 
 
+def gather(own, n):
+    steps = n // 4
+    lines = [own, exchange(own, n, 1)]
+    blocks = [(value, 0, False, half) for half, value in enumerate(lines)]
+    for step in range(1, steps + 1):
+        for half in range(2):
+            lines[half] = ring_step(lines[half], n)
+            blocks.append((lines[half], step, False, half))
+        if step < steps:
+            blocks += [(exchange(value, n, 1), step, True, half) for half, value in enumerate(lines)]
+    return blocks
+
+
 def body(n, trial, left_ops, right_ops, task_list):
-    steps = n // 4
-    own = (trial[0], right_ops.swapaxes(1, 2))
-    other = [exchange(value, n, 1) for value in own]
-    block = jnp.concatenate([*own, *other], axis=0)
-    plan = make_plan(task_list.T, n, n * right_ops.shape[0])
-    blocks = [(block, 0, False)]
-    for step in range(1, steps + 1):
-        block = ring_step(block, n)
-        blocks.append((block, step, False))
-        if step < steps:
-            blocks.append((exchange(block, n, 1), step, True))
+    blocks = gather(jnp.concatenate([trial[0], right_ops.swapaxes(1, 2)], axis=0), n)
+    plan = make_plan(task_list.T, left_ops, n, n * right_ops.shape[0])
     send, keep, own = run_tasks(n, plan, left_ops, blocks)
     send, arrays = lax.optimization_barrier((send, [block[0] for block in blocks]))
     correlation = correlate(arrays)
     mine, total, *sends = add_chip(keep, own, exchange(send, n, 1))
-    received = [exchange(value, n, 2 * (j + 1)) for j, value in enumerate(sends)]
+    received = [exchange(sends[j - 1], n, 2 * j) for j in reversed(range(1, n // 2))]
     product, projected = add_all(mine, total, received)
     return product, correlation, projected
 

time: 80.9 us -> 71.4 us (0.88)
  waiting for transfers between devices: 23.8 us -> 9.91 us
  starting transfers between devices: 23.4 us -> 31.1 us
  local copies, waits for them, and re-layouts: 10.4 us -> 7.55 us
    ppermute x4 -> x8, waiting for transfers between devices: 20.1 us -> 5.02 us  [ring_step(): return lax.ppermute(value, 'op', pairs)]
    ppermute x4 -> x8, starting transfers between devices: 9.04 us -> 15.7 us  [ring_step(): return lax.ppermute(value, 'op', pairs)]
    unnamed x29 -> x7, local copies, waits for them, and re-layouts: 10.4 us -> 7.55 us
    pallas_call x2, Pallas kernels: 3.13 us -> 1.84 us  [the longest x1 0.98 us: correlate(): pl.pallas_call(corr_kernel, out_shape=jax.ShapeDtypeStruct((2, 2), jnp.fl...]
    ppermute x13 -> x15, waiting for transfers between devices: 3.7 us -> 4.9 us  [exchange(): return lax.ppermute(value, 'op', [(i, i ^ mask) for i in range(n)])]
    ppermute x13 -> x15, starting transfers between devices: 14.4 us -> 15.4 us  [exchange(): return lax.ppermute(value, 'op', [(i, i ^ mask) for i in range(n)])]
    pallas_call x1, Pallas kernels: 17.1 us -> 17.9 us  [run_tasks(): pl.pallas_call(functools.partial(tasks_kernel, n, terms_per, kinds), out_...]
  transfers between devices with their start and end apart: 17 -> 23, of which waited for: 7 -> 7; matrix products, arithmetic and copies ran while one was open for 0% -> 0% of each run, Pallas kernels for 4% -> 3%
where the time goes in v6:
time: 71.4 us; the launch traced here: 70.7 us
  starting transfers between devices  31.1 us (44%)
  Pallas kernels  20.6 us (29%)
  waiting for transfers between devices  9.91 us (14%)
  local copies, waits for them, and re-layouts  7.55 us (11%)
  other arithmetic  0.86 us (1%)
  between operations  0.73 us (1%)
    pallas_call x1, Pallas kernels, run_tasks(): pl.pallas_call(functools.partial(tasks_kernel, n, terms_per, kinds), out_...  17.9 us
    ppermute x8, starting transfers between devices, ring_step(): return lax.ppermute(value, 'op', pairs)  15.7 us
    ppermute x15, starting transfers between devices, exchange(): return lax.ppermute(value, 'op', [(i, i ^ mask) for i in range(n)])  15.4 us
    unnamed x7, local copies, waits for them, and re-layouts  7.55 us
    ppermute x8, waiting for transfers between devices, ring_step(): return lax.ppermute(value, 'op', pairs)  5.02 us
    ppermute x15, waiting for transfers between devices, exchange(): return lax.ppermute(value, 'op', [(i, i ^ mask) for i in range(n)])  4.9 us
  transfers between devices with their start and end apart: 23, of which 7 were waited for; matrix products, arithmetic and copies ran while one was open for 0% of the time, Pallas kernels for 3%

profile of v6, /device:TPU:0, one launch (start us, length us, event | category | flops | bytes accessed | tf_op | source)
XLA Modules:
  0.0 70.7 jit_solution(16018640919742490655)
XLA Ops:
  0.6 1.0 %copy.7 = bf16[4,128,128]{1,2,0:T(8,128)(2,1)S(1)} copy(bf16[4,128,128]{2,1,0:T(8,128)(2,1)} %param.6) | data formatting | bytes 262144 | tf_op args[2]
  1.7 0.9 %pad_maximum_fusion.refs_0_ = bf16[6,128,128]{2,1,0:T(8,128)(2,1)S(1)} fusion(bf16[4,128,128]{2,1,0:T(8,128)(2,1)S(1)} %bitcast.4, bf16[2,128,128]{2,1,0:T(8,128)(2,1)} %bitcast.5), kind=kLoop, calls=%fused_computation | loop fusion | flops 98304 | bytes 393216 | tf_op jit(solution)/shard_map/concatenate | solution.py:379
  2.5 0.5 collective-permute-start
  3.0 2.6 %collective-permute-start.1 = (bf16[6,128,128]{2,1,0:T(8,128)(2,1)S(1)}, bf16[6,128,128]{2,1,0:T(8,128)(2,1)S(1)}, u32[]{:S(2)}, u32[]{:S(2)}) collective-permute-start(bf16[6,128,128]{2,1,0:T(8,128)(2,1)S(1)} %pad_maximum_fusion.refs_0_), channel_id=1, source_target_pairs={{0,4},{1,3},{4,8},{5,1},{8,12},{9,5},{12,14},{13,9},{14,10},{15,13... | collective-permute-start | bytes 589832 | tf_op jit(solution)/shard_map/ppermute | solution.py:33
  5.7 0.0 collective-permute-done.refs_1_
  5.7 1.6 %collective-permute-start.2 = (bf16[6,128,128]{2,1,0:T(8,128)(2,1)S(1)}, bf16[6,128,128]{2,1,0:T(8,128)(2,1)S(1)}, u32[]{:S(2)}, u32[]{:S(2)}) collective-permute-start(bf16[6,128,128]{2,1,0:T(8,128)(2,1)S(1)} %collective-permute-done.refs_1_), channel_id=1, source_target_pairs={{0,4},{1,3},{4,8},{5,1},{8,12},{9,5},{12,14},{13,9},{14,10},{15,13... | collective-permute-start | bytes 589832 | tf_op jit(solution)/shard_map/ppermute | solution.py:33
  7.3 2.0 %collective-permute-done.1.refs_2_ = bf16[6,128,128]{2,1,0:T(8,128)(2,1)S(1)} collective-permute-done((bf16[6,128,128]{2,1,0:T(8,128)(2,1)S(1)}, bf16[6,128,128]{2,1,0:T(8,128)(2,1)S(1)}, u32[]{:S(2)}, u32[]{:S(2)}) %collective-permute-start.1) | collective-permute-done | bytes 196640 | tf_op jit(solution)/shard_map/ppermute | solution.py:33
  9.3 2.1 %collective-permute-start.5 = (bf16[6,128,128]{2,1,0:T(8,128)(2,1)S(1)}, bf16[6,128,128]{2,1,0:T(8,128)(2,1)S(1)}, u32[]{:S(2)}, u32[]{:S(2)}) collective-permute-start(bf16[6,128,128]{2,1,0:T(8,128)(2,1)S(1)} %collective-permute-done.1.refs_2_), channel_id=1, source_target_pairs={{0,4},{1,3},{4,8},{5,1},{8,12},{9,5},{12,14},{13,9},{14,10},{15,13... | collective-permute-start | bytes 589832 | tf_op jit(solution)/shard_map/ppermute | solution.py:33
  11.3 0.0 collective-permute-done.2.refs_3_
  11.4 2.1 %collective-permute-start.6 = (bf16[6,128,128]{2,1,0:T(8,128)(2,1)S(1)}, bf16[6,128,128]{2,1,0:T(8,128)(2,1)S(1)}, u32[]{:S(2)}, u32[]{:S(2)}) collective-permute-start(bf16[6,128,128]{2,1,0:T(8,128)(2,1)S(1)} %collective-permute-done.2.refs_3_), channel_id=1, source_target_pairs={{0,4},{1,3},{4,8},{5,1},{8,12},{9,5},{12,14},{13,9},{14,10},{15,13... | collective-permute-start | bytes 589832 | tf_op jit(solution)/shard_map/ppermute | solution.py:33
  13.5 1.5 %collective-permute-done.5.refs_6_ = bf16[6,128,128]{2,1,0:T(8,128)(2,1)S(1)} collective-permute-done((bf16[6,128,128]{2,1,0:T(8,128)(2,1)S(1)}, bf16[6,128,128]{2,1,0:T(8,128)(2,1)S(1)}, u32[]{:S(2)}, u32[]{:S(2)}) %collective-permute-start.5) | collective-permute-done | bytes 196640 | tf_op jit(solution)/shard_map/ppermute | solution.py:33
  14.9 2.1 %collective-permute-start.9 = (bf16[6,128,128]{2,1,0:T(8,128)(2,1)S(1)}, bf16[6,128,128]{2,1,0:T(8,128)(2,1)S(1)}, u32[]{:S(2)}, u32[]{:S(2)}) collective-permute-start(bf16[6,128,128]{2,1,0:T(8,128)(2,1)S(1)} %collective-permute-done.5.refs_6_), channel_id=1, source_target_pairs={{0,4},{1,3},{4,8},{5,1},{8,12},{9,5},{12,14},{13,9},{14,10},{15,13... | collective-permute-start | bytes 589832 | tf_op jit(solution)/shard_map/ppermute | solution.py:33
  17.0 0.0 collective-permute-start.3
  17.0 0.5 collective-permute-start.7
  17.5 0.0 collective-permute-done.6.refs_7_
  17.5 1.6 %collective-permute-start.10 = (bf16[6,128,128]{2,1,0:T(8,128)(2,1)S(1)}, bf16[6,128,128]{2,1,0:T(8,128)(2,1)S(1)}, u32[]{:S(2)}, u32[]{:S(2)}) collective-permute-start(bf16[6,128,128]{2,1,0:T(8,128)(2,1)S(1)} %collective-permute-done.6.refs_7_), channel_id=1, source_target_pairs={{0,4},{1,3},{4,8},{5,1},{8,12},{9,5},{12,14},{13,9},{14,10},{15,13... | collective-permute-start | bytes 589832 | tf_op jit(solution)/shard_map/ppermute | solution.py:33
  19.1 0.0 collective-permute-start.4
  19.1 1.5 %collective-permute-done.9.refs_10_ = bf16[6,128,128]{2,1,0:T(8,128)(2,1)S(1)} collective-permute-done((bf16[6,128,128]{2,1,0:T(8,128)(2,1)S(1)}, bf16[6,128,128]{2,1,0:T(8,128)(2,1)S(1)}, u32[]{:S(2)}, u32[]{:S(2)}) %collective-permute-start.9) | collective-permute-done | bytes 196640 | tf_op jit(solution)/shard_map/ppermute | solution.py:33
  20.6 2.1 %collective-permute-start.13 = (bf16[6,128,128]{2,1,0:T(8,128)(2,1)S(1)}, bf16[6,128,128]{2,1,0:T(8,128)(2,1)S(1)}, u32[]{:S(2)}, u32[]{:S(2)}) collective-permute-start(bf16[6,128,128]{2,1,0:T(8,128)(2,1)S(1)} %collective-permute-done.9.refs_10_), channel_id=1, source_target_pairs={{0,4},{1,3},{4,8},{5,1},{8,12},{9,5},{12,14},{13,9},{14,10},{15,13... | collective-permute-start | bytes 589832 | tf_op jit(solution)/shard_map/ppermute | solution.py:33
  22.7 0.0 collective-permute-done.3.refs_4_
  22.7 0.0 collective-permute-start.11
  22.7 0.0 collective-permute-done.7.refs_8_
  22.7 0.5 collective-permute-start.8
  23.2 0.0 collective-permute-done.10.refs_11_
  23.2 1.6 %collective-permute-start.14 = (bf16[6,128,128]{2,1,0:T(8,128)(2,1)S(1)}, bf16[6,128,128]{2,1,0:T(8,128)(2,1)S(1)}, u32[]{:S(2)}, u32[]{:S(2)}) collective-permute-start(bf16[6,128,128]{2,1,0:T(8,128)(2,1)S(1)} %collective-permute-done.10.refs_11_), channel_id=1, source_target_pairs={{0,4},{1,3},{4,8},{5,1},{8,12},{9,5},{12,14},{13,9},{14,10},{15,13... | collective-permute-start | bytes 589832 | tf_op jit(solution)/shard_map/ppermute | solution.py:33
  24.8 0.0 collective-permute-done.4.refs_5_
  24.8 0.0 collective-permute-start.12
  24.8 0.0 copy-start
  24.8 3.4 %copy-done = bf16[256,128,128]{2,1,0:T(8,128)(2,1)S(1)} copy-done((bf16[256,128,128]{2,1,0:T(8,128)(2,1)S(1)}, bf16[256,128,128]{2,1,0:T(8,128)(2,1)}, u32[]{:S(2)}) %copy-start) | copy-done | bytes 8388632
  28.2 0.0 copy-start.2
  28.2 0.7 copy-done.2
  28.9 0.0 copy-start.1
  28.9 0.9 %shard_map.67.plan_ref = s32[8,384]{1,0:T(8,128)S(1)} custom-call(s32[4,256]{1,0:T(4,128)S(1)} %bitcast.3, bf16[256,128,128]{2,1,0:T(8,128)(2,1)S(1)} %copy-done), custom_call_target="tpu_custom_call" | custom-call | tf_op jit(solution)/shard_map/pallas_call | solution.py:145
  29.7 0.0 collective-permute-done.13.refs_14_
  29.8 0.0 collective-permute-done.11.refs_12_
  29.8 0.0 collective-permute-done.8.refs_9_
  29.8 0.0 collective-permute-done.14.refs_15_
  29.8 0.0 collective-permute-done.12.refs_13_
  29.8 2.5 %copy-done.1 = bf16[256,128,128]{2,1,0:T(8,128)(2,1)S(1)} copy-done((bf16[256,128,128]{2,1,0:T(8,128)(2,1)S(1)}, bf16[256,128,128]{2,1,0:T(8,128)(2,1)}, u32[]{:S(2)}) %copy-start.1) | copy-done | bytes 8388632
  32.3 17.9 %shard_map.68 = (bf16[2080,128]{1,0:T(8,128)(2,1)S(1)}, f32[8,256,128]{2,1,0:T(8,128)S(1)}, f32[8,128]{1,0:T(8,128)S(1)}) custom-call(s32[8,384]{1,0:T(8,128)S(1)} %shard_map.67.plan_ref, bf16[256,128,128]{2,1,0:T(8,128)(2,1)S(1)} %copy-done.1, bf16[6,128,128]{2,1,0:T(8,128)(2,1)S(1)} %pad_maximum_fusion.refs_0_, ...), custom_call_target="tpu_custom_call" | custom-call | flops 4294967296 | bytes 15588608 | tf_op jit(solution)/shard_map/pallas_call | solution.py:279
  50.2 0.1 collective-permute-start.15
  50.3 1.9 %collective-permute-done.15.received_ref = bf16[2080,128]{1,0:T(8,128)(2,1)S(1)} collective-permute-done((bf16[2080,128]{1,0:T(8,128)(2,1)S(1)}, bf16[2080,128]{1,0:T(8,128)(2,1)S(1)}, u32[]{:S(2)}, u32[]{:S(2)}) %collective-permute-start.15) | collective-permute-done | bytes 532512 | tf_op jit(solution)/shard_map/ppermute | solution.py:19
  52.2 0.1 shard_map.69
  52.3 4.9 %collective-permute-start.16 = (bf16[288,128]{1,0:T(8,128)(2,1)S(1)}, bf16[288,128]{1,0:T(8,128)(2,1)S(1)}, u32[]{:S(2)}, u32[]{:S(2)}) collective-permute-start(bf16[288,128]{1,0:T(8,128)(2,1)S(1)} %get-tuple-element.40), channel_id=1, source_target_pairs={{0,14},{1,15},{2,12},{3,13},{4,10},{5,11},{6,8},{7,9},{8,6},{9,7},... | collective-permute-start | bytes 221192 | tf_op jit(solution)/shard_map/ppermute | solution.py:19
  57.2 0.2 collective-permute-start.17
  57.4 1.9 %collective-permute-start.18 = (bf16[288,128]{1,0:T(8,128)(2,1)S(1)}, bf16[288,128]{1,0:T(8,128)(2,1)S(1)}, u32[]{:S(2)}, u32[]{:S(2)}) collective-permute-start(bf16[288,128]{1,0:T(8,128)(2,1)S(1)} %get-tuple-element.42), channel_id=1, source_target_pairs={{0,10},{1,11},{2,8},{3,9},{4,14},{5,15},{6,12},{7,13},{8,2},{9,3},... | collective-permute-start | bytes 221192 | tf_op jit(solution)/shard_map/ppermute | solution.py:19
  59.3 1.9 %collective-permute-start.19 = (bf16[288,128]{1,0:T(8,128)(2,1)S(1)}, bf16[288,128]{1,0:T(8,128)(2,1)S(1)}, u32[]{:S(2)}, u32[]{:S(2)}) collective-permute-start(bf16[288,128]{1,0:T(8,128)(2,1)S(1)} %get-tuple-element.43), channel_id=1, source_target_pairs={{0,8},{1,9},{2,10},{3,11},{4,12},{5,13},{6,14},{7,15},{8,0},{9,1},... | collective-permute-start | bytes 221192 | tf_op jit(solution)/shard_map/ppermute | solution.py:19
  61.2 1.5 %collective-permute-start.20 = (bf16[288,128]{1,0:T(8,128)(2,1)S(1)}, bf16[288,128]{1,0:T(8,128)(2,1)S(1)}, u32[]{:S(2)}, u32[]{:S(2)}) collective-permute-start(bf16[288,128]{1,0:T(8,128)(2,1)S(1)} %get-tuple-element.44), channel_id=1, source_target_pairs={{0,6},{1,7},{2,4},{3,5},{4,2},{5,3},{6,0},{7,1},{8,14},{9,15},{10,... | collective-permute-start | bytes 221192 | tf_op jit(solution)/shard_map/ppermute | solution.py:19
  62.6 0.0 collective-permute-done.16.refs_0_
  62.6 0.6 collective-permute-start.21
  63.3 0.8 %collective-permute-done.17.refs_1_ = bf16[288,128]{1,0:T(8,128)(2,1)S(1)} collective-permute-done((bf16[288,128]{1,0:T(8,128)(2,1)S(1)}, bf16[288,128]{1,0:T(8,128)(2,1)S(1)}, u32[]{:S(2)}, u32[]{:S(2)}) %collective-permute-start.17) | collective-permute-done | bytes 73760 | tf_op jit(solution)/shard_map/ppermute | solution.py:19
  64.0 2.8 %collective-permute-start.22 = (bf16[288,128]{1,0:T(8,128)(2,1)S(1)}, bf16[288,128]{1,0:T(8,128)(2,1)S(1)}, u32[]{:S(2)}, u32[]{:S(2)}) collective-permute-start(bf16[288,128]{1,0:T(8,128)(2,1)S(1)} %get-tuple-element.46), channel_id=1, source_target_pairs={{0,2},{1,3},{2,0},{3,1},{4,6},{5,7},{6,4},{7,5},{8,10},{9,11},{10,... | collective-permute-start | bytes 221192 | tf_op jit(solution)/shard_map/ppermute | solution.py:19
  66.8 1.0 %shard_map.71 = f32[2,2]{1,0:T(2,128)} custom-call(bf16[6,128,128]{2,1,0:T(8,128)(2,1)S(1)} %pad_maximum_fusion.refs_0_, bf16[6,128,128]{2,1,0:T(8,128)(2,1)S(1)} %collective-permute-done.refs_1_, bf16[6,128,128]{2,1,0:T(8,128)(2,1)S(1)} %collective-permute-done.1.refs_2_, bf16[6,128,128]{2,1,0:T(8,128)(2,1)S(1)} %collective-permute-done.2.refs_3_, ...), custom_call_target="tpu_custom_call" | custom-call | tf_op jit(solution)/shard_map/pallas_call | solution.py:313
  67.8 1.6 %collective-permute-done.18.refs_2_ = bf16[288,128]{1,0:T(8,128)(2,1)S(1)} collective-permute-done((bf16[288,128]{1,0:T(8,128)(2,1)S(1)}, bf16[288,128]{1,0:T(8,128)(2,1)S(1)}, u32[]{:S(2)}, u32[]{:S(2)}) %collective-permute-start.18) | collective-permute-done | bytes 73760 | tf_op jit(solution)/shard_map/ppermute | solution.py:19
  69.5 0.5 collective-permute-done.19.refs_3_
  70.0 0.0 collective-permute-done.20.refs_4_
  70.0 0.0 collective-permute-done.21.refs_5_
  70.0 0.0 collective-permute-done.22.refs_6_
  70.0 0.7 %shard_map.70 = (f32[1,2,128,128]{3,2,1,0:T(8,128)}, f32[2,2]{1,0:T(2,128)}) custom-call(f32[256,128]{1,0:T(8,128)S(1)} %get-tuple-element.38.mine_ref, f32[8,128]{1,0:T(8,128)S(1)} %get-tuple-element.39.total_ref, bf16[288,128]{1,0:T(8,128)(2,1)S(1)} %collective-permute-done.16.refs_0_, bf16[288,128]{1,0:T(8,128)(2,1)S(1)} %collective-permute-done.17.refs_1_, ...), custom_call_target="tpu_custom_call" | custom-call | tf_op jit(solution)/shard_map/pallas_call | solution.py:355
Async XLA Ops:
  2.5 3.2 %collective-permute-start = (bf16[6,128,128]{2,1,0:T(8,128)(2,1)S(1)}, bf16[6,128,128]{2,1,0:T(8,128)(2,1)S(1)}, u32[]{:S(2)}, u32[]{:S(2)}) collective-permute-start(bf16[6,128,128]{2,1,0:T(8,128)(2,1)S(1)} %pad_maximum_fusion.refs_0_), channel_id=1, source_target_pairs={{0,1},{1,0},{2,3},{3,2},{4,5},{5,4},{6,7},{7,6},{8,9},{9,8},{10,11... | collective-permute-start | bytes 589832 | tf_op jit(solution)/shard_map/ppermute | solution.py:19
  3.0 6.2 %collective-permute-start.1 = (bf16[6,128,128]{2,1,0:T(8,128)(2,1)S(1)}, bf16[6,128,128]{2,1,0:T(8,128)(2,1)S(1)}, u32[]{:S(2)}, u32[]{:S(2)}) collective-permute-start(bf16[6,128,128]{2,1,0:T(8,128)(2,1)S(1)} %pad_maximum_fusion.refs_0_), channel_id=1, source_target_pairs={{0,4},{1,3},{4,8},{5,1},{8,12},{9,5},{12,14},{13,9},{14,10},{15,13... | collective-permute-start | bytes 589832 | tf_op jit(solution)/shard_map/ppermute | solution.py:33
  5.7 5.7 %collective-permute-start.2 = (bf16[6,128,128]{2,1,0:T(8,128)(2,1)S(1)}, bf16[6,128,128]{2,1,0:T(8,128)(2,1)S(1)}, u32[]{:S(2)}, u32[]{:S(2)}) collective-permute-start(bf16[6,128,128]{2,1,0:T(8,128)(2,1)S(1)} %collective-permute-done.refs_1_), channel_id=1, source_target_pairs={{0,4},{1,3},{4,8},{5,1},{8,12},{9,5},{12,14},{13,9},{14,10},{15,13... | collective-permute-start | bytes 589832 | tf_op jit(solution)/shard_map/ppermute | solution.py:33
  9.3 5.7 %collective-permute-start.5 = (bf16[6,128,128]{2,1,0:T(8,128)(2,1)S(1)}, bf16[6,128,128]{2,1,0:T(8,128)(2,1)S(1)}, u32[]{:S(2)}, u32[]{:S(2)}) collective-permute-start(bf16[6,128,128]{2,1,0:T(8,128)(2,1)S(1)} %collective-permute-done.1.refs_2_), channel_id=1, source_target_pairs={{0,4},{1,3},{4,8},{5,1},{8,12},{9,5},{12,14},{13,9},{14,10},{15,13... | collective-permute-start | bytes 589832 | tf_op jit(solution)/shard_map/ppermute | solution.py:33
  11.4 6.2 %collective-permute-start.6 = (bf16[6,128,128]{2,1,0:T(8,128)(2,1)S(1)}, bf16[6,128,128]{2,1,0:T(8,128)(2,1)S(1)}, u32[]{:S(2)}, u32[]{:S(2)}) collective-permute-start(bf16[6,128,128]{2,1,0:T(8,128)(2,1)S(1)} %collective-permute-done.2.refs_3_), channel_id=1, source_target_pairs={{0,4},{1,3},{4,8},{5,1},{8,12},{9,5},{12,14},{13,9},{14,10},{15,13... | collective-permute-start | bytes 589832 | tf_op jit(solution)/shard_map/ppermute | solution.py:33
  14.9 5.7 %collective-permute-start.9 = (bf16[6,128,128]{2,1,0:T(8,128)(2,1)S(1)}, bf16[6,128,128]{2,1,0:T(8,128)(2,1)S(1)}, u32[]{:S(2)}, u32[]{:S(2)}) collective-permute-start(bf16[6,128,128]{2,1,0:T(8,128)(2,1)S(1)} %collective-permute-done.5.refs_6_), channel_id=1, source_target_pairs={{0,4},{1,3},{4,8},{5,1},{8,12},{9,5},{12,14},{13,9},{14,10},{15,13... | collective-permute-start | bytes 589832 | tf_op jit(solution)/shard_map/ppermute | solution.py:33
  17.0 5.7 %collective-permute-start.3 = (bf16[6,128,128]{2,1,0:T(8,128)(2,1)S(1)}, bf16[6,128,128]{2,1,0:T(8,128)(2,1)S(1)}, u32[]{:S(2)}, u32[]{:S(2)}) collective-permute-start(bf16[6,128,128]{2,1,0:T(8,128)(2,1)S(1)} %collective-permute-done.1.refs_2_), channel_id=1, source_target_pairs={{0,1},{1,0},{2,3},{3,2},{4,5},{5,4},{6,7},{7,6},{8,9},{9,8},{10,11... | collective-permute-start | bytes 589832 | tf_op jit(solution)/shard_map/ppermute | solution.py:19
  17.0 5.7 %collective-permute-start.7 = (bf16[6,128,128]{2,1,0:T(8,128)(2,1)S(1)}, bf16[6,128,128]{2,1,0:T(8,128)(2,1)S(1)}, u32[]{:S(2)}, u32[]{:S(2)}) collective-permute-start(bf16[6,128,128]{2,1,0:T(8,128)(2,1)S(1)} %collective-permute-done.5.refs_6_), channel_id=1, source_target_pairs={{0,1},{1,0},{2,3},{3,2},{4,5},{5,4},{6,7},{7,6},{8,9},{9,8},{10,11... | collective-permute-start | bytes 589832 | tf_op jit(solution)/shard_map/ppermute | solution.py:19
  17.5 5.7 %collective-permute-start.10 = (bf16[6,128,128]{2,1,0:T(8,128)(2,1)S(1)}, bf16[6,128,128]{2,1,0:T(8,128)(2,1)S(1)}, u32[]{:S(2)}, u32[]{:S(2)}) collective-permute-start(bf16[6,128,128]{2,1,0:T(8,128)(2,1)S(1)} %collective-permute-done.6.refs_7_), channel_id=1, source_target_pairs={{0,4},{1,3},{4,8},{5,1},{8,12},{9,5},{12,14},{13,9},{14,10},{15,13... | collective-permute-start | bytes 589832 | tf_op jit(solution)/shard_map/ppermute | solution.py:33
  19.1 5.7 %collective-permute-start.4 = (bf16[6,128,128]{2,1,0:T(8,128)(2,1)S(1)}, bf16[6,128,128]{2,1,0:T(8,128)(2,1)S(1)}, u32[]{:S(2)}, u32[]{:S(2)}) collective-permute-start(bf16[6,128,128]{2,1,0:T(8,128)(2,1)S(1)} %collective-permute-done.2.refs_3_), channel_id=1, source_target_pairs={{0,1},{1,0},{2,3},{3,2},{4,5},{5,4},{6,7},{7,6},{8,9},{9,8},{10,11... | collective-permute-start | bytes 589832 | tf_op jit(solution)/shard_map/ppermute | solution.py:19
  20.6 9.1 %collective-permute-start.13 = (bf16[6,128,128]{2,1,0:T(8,128)(2,1)S(1)}, bf16[6,128,128]{2,1,0:T(8,128)(2,1)S(1)}, u32[]{:S(2)}, u32[]{:S(2)}) collective-permute-start(bf16[6,128,128]{2,1,0:T(8,128)(2,1)S(1)} %collective-permute-done.9.refs_10_), channel_id=1, source_target_pairs={{0,4},{1,3},{4,8},{5,1},{8,12},{9,5},{12,14},{13,9},{14,10},{15,13... | collective-permute-start | bytes 589832 | tf_op jit(solution)/shard_map/ppermute | solution.py:33
  22.7 7.1 %collective-permute-start.11 = (bf16[6,128,128]{2,1,0:T(8,128)(2,1)S(1)}, bf16[6,128,128]{2,1,0:T(8,128)(2,1)S(1)}, u32[]{:S(2)}, u32[]{:S(2)}) collective-permute-start(bf16[6,128,128]{2,1,0:T(8,128)(2,1)S(1)} %collective-permute-done.9.refs_10_), channel_id=1, source_target_pairs={{0,1},{1,0},{2,3},{3,2},{4,5},{5,4},{6,7},{7,6},{8,9},{9,8},{10,11... | collective-permute-start | bytes 589832 | tf_op jit(solution)/shard_map/ppermute | solution.py:19
  22.7 7.1 %collective-permute-start.8 = (bf16[6,128,128]{2,1,0:T(8,128)(2,1)S(1)}, bf16[6,128,128]{2,1,0:T(8,128)(2,1)S(1)}, u32[]{:S(2)}, u32[]{:S(2)}) collective-permute-start(bf16[6,128,128]{2,1,0:T(8,128)(2,1)S(1)} %collective-permute-done.6.refs_7_), channel_id=1, source_target_pairs={{0,1},{1,0},{2,3},{3,2},{4,5},{5,4},{6,7},{7,6},{8,9},{9,8},{10,11... | collective-permute-start | bytes 589832 | tf_op jit(solution)/shard_map/ppermute | solution.py:19
  23.2 6.6 %collective-permute-start.14 = (bf16[6,128,128]{2,1,0:T(8,128)(2,1)S(1)}, bf16[6,128,128]{2,1,0:T(8,128)(2,1)S(1)}, u32[]{:S(2)}, u32[]{:S(2)}) collective-permute-start(bf16[6,128,128]{2,1,0:T(8,128)(2,1)S(1)} %collective-permute-done.10.refs_11_), channel_id=1, source_target_pairs={{0,4},{1,3},{4,8},{5,1},{8,12},{9,5},{12,14},{13,9},{14,10},{15,13... | collective-permute-start | bytes 589832 | tf_op jit(solution)/shard_map/ppermute | solution.py:33
  24.8 5.0 %collective-permute-start.12 = (bf16[6,128,128]{2,1,0:T(8,128)(2,1)S(1)}, bf16[6,128,128]{2,1,0:T(8,128)(2,1)S(1)}, u32[]{:S(2)}, u32[]{:S(2)}) collective-permute-start(bf16[6,128,128]{2,1,0:T(8,128)(2,1)S(1)} %collective-permute-done.10.refs_11_), channel_id=1, source_target_pairs={{0,1},{1,0},{2,3},{3,2},{4,5},{5,4},{6,7},{7,6},{8,9},{9,8},{10,11... | collective-permute-start | bytes 589832 | tf_op jit(solution)/shard_map/ppermute | solution.py:19
  24.8 3.4 %copy-start = (bf16[256,128,128]{2,1,0:T(8,128)(2,1)S(1)}, bf16[256,128,128]{2,1,0:T(8,128)(2,1)}, u32[]{:S(2)}) copy-start(bf16[256,128,128]{2,1,0:T(8,128)(2,1)} %left_ref.1) | copy-start | bytes 25165828
  28.2 0.7 copy-start.2
  28.9 3.4 %copy-start.1 = (bf16[256,128,128]{2,1,0:T(8,128)(2,1)S(1)}, bf16[256,128,128]{2,1,0:T(8,128)(2,1)}, u32[]{:S(2)}) copy-start(bf16[256,128,128]{2,1,0:T(8,128)(2,1)} %left_ref.1) | copy-start | bytes 25165828
  50.2 2.0 %collective-permute-start.15 = (bf16[2080,128]{1,0:T(8,128)(2,1)S(1)}, bf16[2080,128]{1,0:T(8,128)(2,1)S(1)}, u32[]{:S(2)}, u32[]{:S(2)}) collective-permute-start(bf16[2080,128]{1,0:T(8,128)(2,1)S(1)} %get-tuple-element.37), channel_id=1, source_target_pairs={{0,1},{1,0},{2,3},{3,2},{4,5},{5,4},{6,7},{7,6},{8,9},{9,8},{10,11... | collective-permute-start | bytes 1597448 | tf_op jit(solution)/shard_map/ppermute | solution.py:19
  52.3 10.3 %collective-permute-start.16 = (bf16[288,128]{1,0:T(8,128)(2,1)S(1)}, bf16[288,128]{1,0:T(8,128)(2,1)S(1)}, u32[]{:S(2)}, u32[]{:S(2)}) collective-permute-start(bf16[288,128]{1,0:T(8,128)(2,1)S(1)} %get-tuple-element.40), channel_id=1, source_target_pairs={{0,14},{1,15},{2,12},{3,13},{4,10},{5,11},{6,8},{7,9},{8,6},{9,7},... | collective-permute-start | bytes 221192 | tf_op jit(solution)/shard_map/ppermute | solution.py:19
  57.2 6.8 %collective-permute-start.17 = (bf16[288,128]{1,0:T(8,128)(2,1)S(1)}, bf16[288,128]{1,0:T(8,128)(2,1)S(1)}, u32[]{:S(2)}, u32[]{:S(2)}) collective-permute-start(bf16[288,128]{1,0:T(8,128)(2,1)S(1)} %get-tuple-element.41), channel_id=1, source_target_pairs={{0,12},{1,13},{2,14},{3,15},{4,8},{5,9},{6,10},{7,11},{8,4},{9,5},... | collective-permute-start | bytes 221192 | tf_op jit(solution)/shard_map/ppermute | solution.py:19
  57.4 12.1 %collective-permute-start.18 = (bf16[288,128]{1,0:T(8,128)(2,1)S(1)}, bf16[288,128]{1,0:T(8,128)(2,1)S(1)}, u32[]{:S(2)}, u32[]{:S(2)}) collective-permute-start(bf16[288,128]{1,0:T(8,128)(2,1)S(1)} %get-tuple-element.42), channel_id=1, source_target_pairs={{0,10},{1,11},{2,8},{3,9},{4,14},{5,15},{6,12},{7,13},{8,2},{9,3},... | collective-permute-start | bytes 221192 | tf_op jit(solution)/shard_map/ppermute | solution.py:19
  59.3 10.7 %collective-permute-start.19 = (bf16[288,128]{1,0:T(8,128)(2,1)S(1)}, bf16[288,128]{1,0:T(8,128)(2,1)S(1)}, u32[]{:S(2)}, u32[]{:S(2)}) collective-permute-start(bf16[288,128]{1,0:T(8,128)(2,1)S(1)} %get-tuple-element.43), channel_id=1, source_target_pairs={{0,8},{1,9},{2,10},{3,11},{4,12},{5,13},{6,14},{7,15},{8,0},{9,1},... | collective-permute-start | bytes 221192 | tf_op jit(solution)/shard_map/ppermute | solution.py:19
  61.2 8.8 %collective-permute-start.20 = (bf16[288,128]{1,0:T(8,128)(2,1)S(1)}, bf16[288,128]{1,0:T(8,128)(2,1)S(1)}, u32[]{:S(2)}, u32[]{:S(2)}) collective-permute-start(bf16[288,128]{1,0:T(8,128)(2,1)S(1)} %get-tuple-element.44), channel_id=1, source_target_pairs={{0,6},{1,7},{2,4},{3,5},{4,2},{5,3},{6,0},{7,1},{8,14},{9,15},{10,... | collective-permute-start | bytes 221192 | tf_op jit(solution)/shard_map/ppermute | solution.py:19
  62.6 7.4 %collective-permute-start.21 = (bf16[288,128]{1,0:T(8,128)(2,1)S(1)}, bf16[288,128]{1,0:T(8,128)(2,1)S(1)}, u32[]{:S(2)}, u32[]{:S(2)}) collective-permute-start(bf16[288,128]{1,0:T(8,128)(2,1)S(1)} %get-tuple-element.45), channel_id=1, source_target_pairs={{0,4},{1,5},{2,6},{3,7},{4,0},{5,1},{6,2},{7,3},{8,12},{9,13},{10,... | collective-permute-start | bytes 221192 | tf_op jit(solution)/shard_map/ppermute | solution.py:19
  64.0 6.0 %collective-permute-start.22 = (bf16[288,128]{1,0:T(8,128)(2,1)S(1)}, bf16[288,128]{1,0:T(8,128)(2,1)S(1)}, u32[]{:S(2)}, u32[]{:S(2)}) collective-permute-start(bf16[288,128]{1,0:T(8,128)(2,1)S(1)} %get-tuple-element.46), channel_id=1, source_target_pairs={{0,2},{1,3},{2,0},{3,1},{4,6},{5,7},{6,4},{7,5},{8,10},{9,11},{10,... | collective-permute-start | bytes 221192 | tf_op jit(solution)/shard_map/ppermute | solution.py:19

commit v7 on v6

v7 whole, which is shorter than its diff:
```python
import functools

import jax
import jax.numpy as jnp
from jax import lax
from jax.experimental import pallas as pl
from jax.experimental.pallas import tpu as pltpu
from jax.sharding import PartitionSpec as P

MIB = 1024 * 1024
TAIL = 16
TRIALS = 2
CHUNK = 16
PAIRS = 8
AHEAD = 3


def exchange(value, n, mask):
    return lax.ppermute(value, "op", [(i, i ^ mask) for i in range(n)])


def chip_at(place, chips):
    return 2 * place if place < chips // 2 else 2 * (chips - place) - 1


def ring_step(value, n):
    chips = n // 2
    order = [chip_at(place, chips) for place in range(chips)]
    pairs = []
    for place, chip in enumerate(order):
        pairs.append((2 * chip, 2 * order[(place + 1) % chips]))
        pairs.append((2 * chip + 1, 2 * order[(place - 1) % chips] + 1))
    return lax.ppermute(value, "op", pairs)


def owner_of(step, swapped, half, n):
    chips = n // 2
    me = lax.axis_index("op")
    chip, core = me // 2, lax.rem(me, 2)
    odd = lax.rem(chip, 2)
    mine = jnp.where(odd == 0, chip // 2, chips - 1 - chip // 2)
    line = 1 - core if swapped else core
    place = lax.rem(mine + (2 * line - 1) * step + 2 * chips, chips)
    there = jnp.where(place < chips // 2, 2 * place, 2 * (chips - place) - 1)
    return 2 * there + (line if half == 0 else 1 - line)


def split3(value):
    lanes = lax.broadcasted_iota(jnp.int32, (8, 128), 1)
    high = value.astype(jnp.bfloat16).astype(jnp.float32)
    middle = (value - high).astype(jnp.bfloat16).astype(jnp.float32)
    low = (value - high - middle).astype(jnp.bfloat16).astype(jnp.float32)
    return jnp.where(lanes < 2, high, jnp.where(lanes < 4, middle, low))


def tail_of(first, second):
    return jnp.concatenate([first, second], axis=0).astype(jnp.bfloat16)


def matrix_of(values, repeats=1):
    rows = lax.broadcasted_iota(jnp.int32, (8, 128), 0)
    lanes = lax.broadcasted_iota(jnp.int32, (8, 128), 1)
    total = jnp.zeros((8, 128), jnp.float32)
    for (i, j), value in values.items():
        for repeat in range(repeats):
            total = total + jnp.where((rows == i) & (lanes == j + 2 * repeat), value, 0.0)
    return total


def fold(value):
    return value.reshape(16, 8, 128).sum(axis=0)


def fits(n):
    return n <= 16


def phases_of(n):
    return 1


def run_of(slots, n):
    return 4 if slots >= 8 * n else 2


def source_places(slots, n):
    most = slots + min(slots, n) * (run_of(slots, n) - 1) + phases_of(n) * CHUNK
    return -(-most // CHUNK) * CHUNK


def place_of(chip, chips):
    half = jnp.floor(chip * 0.5)
    return jnp.where(chip == 2.0 * half, half, chips - 1.0 - half)


def plan_kernel(n, terms, tasks_ref, plan_ref):
    slots = tasks_ref.shape[1]
    places = plan_ref.shape[1]
    chips = n // 2
    phases = phases_of(n)
    rows = tasks_ref[...].astype(jnp.float32)
    source, target, term, live = rows[0:1], rows[1:2], rows[2:3], rows[3:4]
    lane = lax.broadcasted_iota(jnp.int32, (1, slots), 1).astype(jnp.float32)
    number = lax.broadcasted_iota(jnp.int32, (1, places), 1).astype(jnp.float32)
    at = lax.broadcasted_iota(jnp.int32, (slots, places), 1).astype(jnp.float32)
    me = lax.axis_index("op")
    mine = place_of((jnp.zeros((1, slots), jnp.int32) + me // 2).astype(jnp.float32), float(chips))
    gap = place_of(jnp.floor(source * 0.5), float(chips)) - mine
    up = jnp.where(gap < 0, gap + chips, gap)
    far = jnp.minimum(up, chips - up)
    phase = jnp.clip(far - 1.0, 0.0, phases - 1.0)

    def column(*values):
        pad = [jnp.zeros((8 - len(values), slots), jnp.float32)]
        return jnp.transpose(jnp.concatenate(list(values) + pad, axis=0))

    def sort(sector, parts, unit, whole):
        keys = parts * n
        index = lax.broadcasted_iota(jnp.int32, (keys, slots), 0).astype(jnp.float32)
        part = phase if parts > 1 else jnp.zeros_like(phase)
        key = jnp.where(live > 0, part * n + sector, float(keys))
        columns = column(key, lane)
        earlier = jnp.where((columns[:, 0:1] == key) & (columns[:, 1:2] < lane), 1.0, 0.0)
        count = jnp.sum(jnp.where(index == key, 1.0, 0.0), axis=1, keepdims=True)
        padded = jnp.ceil(count / unit) * unit
        place = jnp.sum(earlier, axis=0, keepdims=True)
        start = jnp.zeros((1, 1), jnp.float32)
        starts = [start]
        for p in range(parts):
            lengths = padded[p * n : (p + 1) * n]
            before = jnp.where(index[p * n : (p + 1) * n] < key, lengths, 0.0)
            place = place + jnp.where(part == p, start * whole + jnp.sum(before, axis=0, keepdims=True), 0.0)
            start = start + jnp.ceil(jnp.sum(lengths, axis=0, keepdims=True) / whole)
            starts.append(start)
        return jnp.where(live > 0, place, -1.0), starts

    by_source, source_starts = sort(source, phases, float(run_of(slots, n)), float(CHUNK))
    by_target, target_starts = sort(target, 1, 2.0, 2.0 * PAIRS)
    columns = column(by_source, by_target, lane, source, term, target)

    def picker(places_column):
        hit = places_column == at

        def pick(values, other):
            found = jnp.sum(jnp.where(hit, values - other, 0.0), axis=0, keepdims=True)
            return (found + other).astype(jnp.int32)

        return pick

    own = (jnp.zeros((1, 1), jnp.int32) + me).astype(jnp.float32)
    pick = picker(columns[:, 0:1])
    plan_ref[0:1] = pick(columns[:, 2:3], 0.0)
    plan_ref[1:2] = pick(columns[:, 3:4], own)
    pick = picker(columns[:, 1:2])
    plan_ref[2:3] = pick(columns[:, 0:1], -1.0)
    plan_ref[3:4] = pick(columns[:, 4:5], float(terms))
    plan_ref[4:5] = pick(columns[:, 5:6], float(n))
    turns = jnp.zeros((1, places), jnp.float32)
    for p, start in enumerate(source_starts + [target_starts[1]]):
        turns = turns + jnp.where(number == p, start, 0.0)
    plan_ref[5:6] = turns.astype(jnp.int32)
    plan_ref[6:8] = jnp.zeros((2, places), jnp.int32)


def make_plan(tasks, n, terms):
    most = source_places(tasks.shape[1], n) + 2 * PAIRS
    return pl.pallas_call(
        functools.partial(plan_kernel, n, terms),
        out_shape=jax.ShapeDtypeStruct((8, -(-most // 128) * 128), jnp.int32),
        compiler_params=pltpu.CompilerParams(vmem_limit_bytes=16 * MIB),
    )(tasks)


def block_copies(n, kinds, blocks, trial, right, sem, which):
    copies = []
    for b, kind in enumerate(kinds):
        owner = owner_of(*kind, n)
        per = blocks[b].shape[0] - TRIALS
        if which == 0:
            source, to = blocks[b].at[pl.ds(0, TRIALS)], trial.at[owner]
        else:
            source, to = blocks[b].at[pl.ds(TRIALS, per)], right.at[pl.ds(owner * per, per)]
        copies.append(pltpu.make_async_copy(source, to, sem.at[b, which]))
    return copies


def half_steps(n, phase, plan_ref, left_ref, trial, halves, left, left_sem):
    first, last = plan_ref[5, phase], plan_ref[5, phase + 1]
    run = run_of(left_ref.shape[0], n)

    def fetch(turn):
        at = lax.rem(turn, AHEAD)
        for u in range(CHUNK):
            slot = plan_ref[0, turn * CHUNK + u]
            pltpu.make_async_copy(left_ref.at[slot], left.at[at, u], left_sem.at[at]).start()

    def start():
        for ahead in range(AHEAD - 1):

            @pl.when(first + ahead < last)
            def _():
                fetch(first + ahead)

    def turn_of(turn, carry):
        @pl.when(turn + AHEAD - 1 < last)
        def _():
            fetch(turn + AHEAD - 1)

        at = lax.rem(turn, AHEAD)
        pltpu.make_async_copy(left_ref.at[pl.ds(0, CHUNK)], left.at[at], left_sem.at[at]).wait()
        place = turn * CHUNK
        for r in range(0, CHUNK, run):
            source = plan_ref[1, place + r]
            vectors = jnp.concatenate([trial[source, 0], trial[source, 1]], axis=1)
            rows = left[at, r : r + run].reshape(run * 128, 128)
            half = jnp.dot(rows, vectors, preferred_element_type=jnp.float32).astype(jnp.bfloat16)
            for u in range(run):
                halves[place + r + u, 0] = half[u * 128 : (u + 1) * 128, :128]
                halves[place + r + u, 1] = half[u * 128 : (u + 1) * 128, 128:]
        return carry

    return start, lambda: lax.fori_loop(first, last, turn_of, 0)


def tasks_kernel(n, kinds, plan_ref, left_ref, *refs):
    blocks, refs = refs[: len(kinds)], refs[len(kinds) :]
    send_ref, keep_ref, own_ref, halves, trial, right, acc, left, block_sem, left_sem = refs
    phase = phases_of(n) - 1
    start, products = half_steps(n, phase, plan_ref, left_ref, trial, halves, left, left_sem)
    moves = [block_copies(n, kinds, blocks, trial, right, block_sem, which) for which in range(2)]
    for copy in moves[0]:
        copy.start()
    start()
    for copy in moves[1]:
        copy.start()
    right[right.shape[0] - 1] = jnp.zeros((128, 128), jnp.bfloat16)

    def clear(s, carry):
        acc[s] = jnp.zeros((256, 128), jnp.float32)
        return carry

    lax.fori_loop(0, n, clear, 0)
    for copy in moves[0]:
        copy.wait()
    products()
    for copy in moves[1]:
        copy.wait()

    def target_turn(turn, carry):
        first = turn * 2 * PAIRS
        for u in range(0, 2 * PAIRS, 2):
            place = first + u
            one = plan_ref[2, place]
            two = plan_ref[2, place + 1]
            one, two = jnp.maximum(one, 0), jnp.where(two < 0, jnp.maximum(one, 0), two)
            pair = jnp.concatenate(
                [
                    jnp.concatenate([halves[one, 0], halves[two, 0]], axis=1),
                    jnp.concatenate([halves[one, 1], halves[two, 1]], axis=1),
                ],
                axis=0,
            )
            rights = jnp.concatenate([right[plan_ref[3, place]], right[plan_ref[3, place + 1]]], axis=0)
            term = jnp.dot(pair, rights, preferred_element_type=jnp.float32)
            target = plan_ref[4, place]
            acc[target] = acc[target] + term
        return carry

    lax.fori_loop(0, plan_ref[5, phase + 2], target_turn, 0)
    me = lax.axis_index("op")

    def pack(j, carry):
        mine = jnp.bitwise_xor(me, 2 * j)
        p00, p01, p10, p11 = carry
        for other, s in enumerate((mine, jnp.bitwise_xor(mine, 1))):
            t0 = trial[s, 0].astype(jnp.float32)
            t1 = trial[s, 1].astype(jnp.float32)
            a0 = acc[s, 0:128, :]
            a1 = acc[s, 128:256, :]
            p00, p01 = p00 + fold(t0 * a0), p01 + fold(t0 * a1)
            p10, p11 = p10 + fold(t1 * a0), p11 + fold(t1 * a1)
            if other:
                rows = pl.multiple_of(j * 256, 256)
                send_ref[pl.ds(rows, 128), :] = a0.astype(jnp.bfloat16)
                send_ref[pl.ds(rows + 128, 128), :] = a1.astype(jnp.bfloat16)
            else:
                keep_ref[j, 0:128, :] = a0
                keep_ref[j, 128:256, :] = a1
        return p00, p01, p10, p11

    zero = jnp.zeros((8, 128), jnp.float32)
    sums = lax.fori_loop(0, n // 2, pack, (zero,) * 4, unroll=2)
    p00, p01, p10, p11 = [jnp.sum(x) for x in sums]
    own = split3(matrix_of({(0, 0): p00, (0, 1): p01, (1, 0): p10, (1, 1): p11}, 3))
    own_ref[...] = own
    send_ref[n // 2 * 256 :, :] = tail_of(own, jnp.zeros_like(own))


def run_tasks(n, plan, left_ops, blocks):
    slots = left_ops.shape[0]
    terms_per = blocks[0][0].shape[0] - TRIALS
    kinds = tuple(block[1:] for block in blocks)
    vmem, hbm = pl.BlockSpec(memory_space=pltpu.VMEM), pl.BlockSpec(memory_space=pltpu.HBM)
    return pl.pallas_call(
        functools.partial(tasks_kernel, n, kinds),
        out_shape=(
            jax.ShapeDtypeStruct((n // 2 * 256 + TAIL, 128), jnp.bfloat16),
            jax.ShapeDtypeStruct((n // 2, 256, 128), jnp.float32),
            jax.ShapeDtypeStruct((8, 128), jnp.float32),
        ),
        in_specs=[pl.BlockSpec(memory_space=pltpu.SMEM), hbm] + [vmem if fits(n) else hbm] * len(blocks),
        out_specs=(vmem,) * 3,
        scratch_shapes=[
            pltpu.VMEM((source_places(slots, n), 2, 128, 128), jnp.bfloat16),
            pltpu.VMEM((n, TRIALS, 128, 128), jnp.bfloat16),
            pltpu.VMEM((n * terms_per + 1, 128, 128), jnp.bfloat16),
            pltpu.VMEM((n + 1, 256, 128), jnp.float32),
            pltpu.VMEM((AHEAD, CHUNK, 128, 128), jnp.bfloat16),
            pltpu.SemaphoreType.DMA((len(blocks), 2)),
            pltpu.SemaphoreType.DMA((AHEAD,)),
        ],
        compiler_params=pltpu.CompilerParams(vmem_limit_bytes=(48 if fits(n) else 58) * MIB),
        cost_estimate=pl.CostEstimate(
            flops=slots * 8 * 128**3, bytes_accessed=slots * 32768 + n * 450000, transcendentals=0
        ),
    )(plan, left_ops, *[block[0] for block in blocks])


def join_kernel(trial_ref, right_ref, block_ref):
    block_ref[0:TRIALS] = trial_ref[0]
    for k in range(right_ref.shape[0]):
        block_ref[TRIALS + k] = jnp.transpose(right_ref[k])


def join(trial, right_ops):
    return pl.pallas_call(
        join_kernel,
        out_shape=jax.ShapeDtypeStruct((TRIALS + right_ops.shape[0], 128, 128), jnp.bfloat16),
        compiler_params=pltpu.CompilerParams(vmem_limit_bytes=16 * MIB),
    )(trial, right_ops)


def corr_kernel(*refs):
    blocks, corr_ref = refs[:-1], refs[-1]
    total = [jnp.zeros((8, 128), jnp.float32)] * 3
    for ref in blocks:
        t0, t1 = ref[0].astype(jnp.float32), ref[1].astype(jnp.float32)
        total = [total[0] + fold(t0 * t0), total[1] + fold(t0 * t1), total[2] + fold(t1 * t1)]
    c00, c01, c11 = [jnp.sum(x) for x in total]
    corr_ref[...] = matrix_of({(0, 0): c00, (0, 1): c01, (1, 0): c01, (1, 1): c11})[0:2, 0:2]


def correlate(blocks):
    return pl.pallas_call(
        corr_kernel,
        out_shape=jax.ShapeDtypeStruct((2, 2), jnp.float32),
        compiler_params=pltpu.CompilerParams(vmem_limit_bytes=16 * MIB),
    )(*blocks)


def chip_kernel(chips, keep_ref, own_ref, received_ref, mine_ref, total_ref, *sends):
    total = jnp.concatenate([own_ref[...], received_ref[chips * 256 :, :].astype(jnp.float32)[0:8]], axis=0)
    total_ref[...] = total
    tail = total.astype(jnp.bfloat16)
    for j in range(chips):
        value = keep_ref[j] + received_ref[j * 256 : (j + 1) * 256, :].astype(jnp.float32)
        if j == 0:
            mine_ref[...] = value
        else:
            sends[j - 1][0:256, :] = value.astype(jnp.bfloat16)
            sends[j - 1][256:, :] = tail


def add_chip(keep, own, received):
    chips = keep.shape[0]
    return pl.pallas_call(
        functools.partial(chip_kernel, chips),
        out_shape=(jax.ShapeDtypeStruct((256, 128), jnp.float32), jax.ShapeDtypeStruct((16, 128), jnp.float32))
        + (jax.ShapeDtypeStruct((256 + TAIL, 128), jnp.bfloat16),) * (chips - 1),
        compiler_params=pltpu.CompilerParams(vmem_limit_bytes=16 * MIB),
    )(keep, own, received)


def last_kernel(mine_ref, total_ref, *refs):
    received, (product_ref, projected_ref) = refs[:-2], refs[-2:]
    value, total = mine_ref[...], total_ref[...]
    for ref in received:
        value = value + ref[0:256, :].astype(jnp.float32)
        total = total + ref[256:, :].astype(jnp.float32)
    product_ref[0, 0] = value[0:128]
    product_ref[0, 1] = value[128:256]
    total = total[0:8] + total[8:16]
    projected_ref[...] = total[0:2, 0:2] + total[0:2, 2:4] + total[0:2, 4:6]


def add_all(mine, total, received):
    return pl.pallas_call(
        last_kernel,
        out_shape=(
            jax.ShapeDtypeStruct((1, 2, 128, 128), jnp.float32),
            jax.ShapeDtypeStruct((2, 2), jnp.float32),
        ),
        compiler_params=pltpu.CompilerParams(vmem_limit_bytes=16 * MIB),
    )(mine, total, *received)


def body(n, trial, left_ops, right_ops, task_list):
    steps = n // 4
    own = join(trial, right_ops)
    plan = make_plan(task_list.T, n, n * right_ops.shape[0])
    lines = [own, exchange(own, n, 1)]
    blocks = [(value, 0, False, half) for half, value in enumerate(lines)]
    for step in range(1, steps + 1):
        if step == steps // 2 + 1:
            lines, plan = lax.optimization_barrier((lines, plan))
        for half in range(2):
            lines[half] = ring_step(lines[half], n)
            blocks.append((lines[half], step, False, half))
        if step < steps:
            blocks += [(exchange(value, n, 1), step, True, half) for half, value in enumerate(lines)]
    send, keep, own = run_tasks(n, plan, left_ops, blocks)
    send, arrays = lax.optimization_barrier((send, [block[0] for block in blocks]))
    correlation = correlate(arrays)
    mine, total, *sends = add_chip(keep, own, exchange(send, n, 1))
    received = [exchange(sends[j - 1], n, 2 * j) for j in reversed(range(1, n // 2))]
    product, projected = add_all(mine, total, received)
    return product, correlation, projected


def solution(mesh):
    return jax.shard_map(
        functools.partial(body, mesh.shape["op"]),
        mesh=mesh,
        in_specs=(
            P(("groups", "op"), None, None, None),
            P(("groups", "op"), None, None),
            P(("groups", "op"), None, None),
            P(("groups", "op"), None),
        ),
        out_specs=(P(("groups", "op"), None, None, None), P("groups", None), P("groups", None)),
        check_vma=False,
    )
```

time: 71.4 us -> 73.8 us (1.034)
  starting transfers between devices: 31.1 us -> 37.7 us
  local copies, waits for them, and re-layouts: 7.55 us -> 2.42 us
  waiting for transfers between devices: 9.91 us -> 13.3 us
  Pallas kernels: 20.6 us -> 18.8 us
  other arithmetic: 0.86 us -> 0 us
    ppermute x15, starting transfers between devices: 15.4 us -> 21.5 us  [exchange(): return lax.ppermute(value, 'op', [(i, i ^ mask) for i in range(n)])]
    unnamed x7 -> x6, local copies, waits for them, and re-layouts: 7.55 us -> 2.42 us
    ppermute x8, waiting for transfers between devices: 5.02 us -> 9.07 us  [ring_step(): return lax.ppermute(value, 'op', pairs)]
    pallas_call x2 -> x3, Pallas kernels: 18.8 us -> 17 us  [the longest x1 16 us: run_tasks(): pl.pallas_call(functools.partial(tasks_kernel, n, kinds), out_shape=(jax....]
    concatenate x1 -> x0, other arithmetic: 0.86 us -> none  [body(): jnp.concatenate([trial[0], right_ops.swapaxes(1, 2)], axis=0)]
  transfers between devices with their start and end apart: 23 -> 23, of which waited for: 7 -> 9; matrix products, arithmetic and copies ran while one was open for 0% -> 0% of each run, Pallas kernels for 3% -> 3%
where the time goes in v7:
time: 73.8 us; the launch traced here: 73 us
  starting transfers between devices  37.7 us (51%)
  Pallas kernels  18.8 us (25%)
  waiting for transfers between devices  13.3 us (18%)
  local copies, waits for them, and re-layouts  2.42 us (3%)
    ppermute x15, starting transfers between devices, exchange(): return lax.ppermute(value, 'op', [(i, i ^ mask) for i in range(n)])  21.5 us
    ppermute x8, starting transfers between devices, ring_step(): return lax.ppermute(value, 'op', pairs)  16.2 us
    pallas_call x1, Pallas kernels, run_tasks(): pl.pallas_call(functools.partial(tasks_kernel, n, kinds), out_shape=(jax....  16 us
    ppermute x8, waiting for transfers between devices, ring_step(): return lax.ppermute(value, 'op', pairs)  9.07 us
    ppermute x15, waiting for transfers between devices, exchange(): return lax.ppermute(value, 'op', [(i, i ^ mask) for i in range(n)])  4.26 us
    unnamed x6, local copies, waits for them, and re-layouts  2.42 us
  transfers between devices with their start and end apart: 23, of which 9 were waited for; matrix products, arithmetic and copies ran while one was open for 0% of the time, Pallas kernels for 3%

profile of v7, /device:TPU:0, one launch (start us, length us, event | category | flops | bytes accessed | tf_op | source)
XLA Modules:
  0.0 73.0 jit_solution(4253880682543737766)
XLA Ops:
  0.6 0.0 copy-start
  0.6 0.9 %copy-done = bf16[4,128,128]{2,1,0:T(8,128)(2,1)S(1)} copy-done((bf16[4,128,128]{2,1,0:T(8,128)(2,1)S(1)}, bf16[4,128,128]{2,1,0:T(8,128)(2,1)}, u32[]{:S(2)}) %copy-start) | copy-done | bytes 131096
  1.5 0.0 copy-start.1
  1.5 0.8 %copy-done.1 = bf16[1,2,128,128]{3,2,1,0:T(8,128)(2,1)S(1)} copy-done((bf16[1,2,128,128]{3,2,1,0:T(8,128)(2,1)S(1)}, bf16[1,2,128,128]{3,2,1,0:T(8,128)(2,1)}, u32[]{:S(2)}) %copy-start.1) | copy-done | bytes 65560
  2.4 0.1 shard_map.67.refs_0_
  2.5 0.5 collective-permute-start.2
  3.0 2.6 %collective-permute-start = (bf16[6,128,128]{2,1,0:T(8,128)(2,1)S(1)}, bf16[6,128,128]{2,1,0:T(8,128)(2,1)S(1)}, u32[]{:S(2)}, u32[]{:S(2)}) collective-permute-start(bf16[6,128,128]{2,1,0:T(8,128)(2,1)S(1)} %shard_map.67.refs_0_), channel_id=1, source_target_pairs={{0,4},{1,3},{4,8},{5,1},{8,12},{9,5},{12,14},{13,9},{14,10},{15,13... | collective-permute-start | bytes 589832 | tf_op jit(solution)/shard_map/ppermute | solution.py:33
  5.6 0.0 collective-permute-done.2.refs_1_
  5.6 1.6 %collective-permute-start.3 = (bf16[6,128,128]{2,1,0:T(8,128)(2,1)S(1)}, bf16[6,128,128]{2,1,0:T(8,128)(2,1)S(1)}, u32[]{:S(2)}, u32[]{:S(2)}) collective-permute-start(bf16[6,128,128]{2,1,0:T(8,128)(2,1)S(1)} %collective-permute-done.2.refs_1_), channel_id=1, source_target_pairs={{0,4},{1,3},{4,8},{5,1},{8,12},{9,5},{12,14},{13,9},{14,10},{15,13... | collective-permute-start | bytes 589832 | tf_op jit(solution)/shard_map/ppermute | solution.py:33
  7.2 2.0 %collective-permute-done.refs_2_ = bf16[6,128,128]{2,1,0:T(8,128)(2,1)S(1)} collective-permute-done((bf16[6,128,128]{2,1,0:T(8,128)(2,1)S(1)}, bf16[6,128,128]{2,1,0:T(8,128)(2,1)S(1)}, u32[]{:S(2)}, u32[]{:S(2)}) %collective-permute-start) | collective-permute-done | bytes 196640 | tf_op jit(solution)/shard_map/ppermute | solution.py:33
  9.2 2.1 %collective-permute-start.1 = (bf16[6,128,128]{2,1,0:T(8,128)(2,1)S(1)}, bf16[6,128,128]{2,1,0:T(8,128)(2,1)S(1)}, u32[]{:S(2)}, u32[]{:S(2)}) collective-permute-start(bf16[6,128,128]{2,1,0:T(8,128)(2,1)S(1)} %collective-permute-done.refs_2_), channel_id=1, source_target_pairs={{0,4},{1,3},{4,8},{5,1},{8,12},{9,5},{12,14},{13,9},{14,10},{15,13... | collective-permute-start | bytes 589832 | tf_op jit(solution)/shard_map/ppermute | solution.py:33
  11.3 0.0 collective-permute-done.3.refs_3_
  11.3 2.1 %collective-permute-start.4 = (bf16[6,128,128]{2,1,0:T(8,128)(2,1)S(1)}, bf16[6,128,128]{2,1,0:T(8,128)(2,1)S(1)}, u32[]{:S(2)}, u32[]{:S(2)}) collective-permute-start(bf16[6,128,128]{2,1,0:T(8,128)(2,1)S(1)} %collective-permute-done.3.refs_3_), channel_id=1, source_target_pairs={{0,4},{1,3},{4,8},{5,1},{8,12},{9,5},{12,14},{13,9},{14,10},{15,13... | collective-permute-start | bytes 589832 | tf_op jit(solution)/shard_map/ppermute | solution.py:33
  13.4 0.0 copy-start.2
  13.4 0.7 copy-done.2
  14.1 0.9 %shard_map.68.plan_ref = s32[8,384]{1,0:T(8,128)S(1)} custom-call(s32[4,256]{1,0:T(4,128)S(1)} %bitcast.1), custom_call_target="tpu_custom_call" | custom-call | tf_op jit(solution)/shard_map/pallas_call | solution.py:167
  15.0 0.1 collective-permute-start.5
  15.1 0.0 collective-permute-done.1.refs_6_
  15.1 1.9 %collective-permute-done.4.refs_7_ = bf16[6,128,128]{2,1,0:T(8,128)(2,1)S(1)} collective-permute-done((bf16[6,128,128]{2,1,0:T(8,128)(2,1)S(1)}, bf16[6,128,128]{2,1,0:T(8,128)(2,1)S(1)}, u32[]{:S(2)}, u32[]{:S(2)}) %collective-permute-start.4) | collective-permute-done | bytes 196640 | tf_op jit(solution)/shard_map/ppermute | solution.py:33
  17.0 2.1 %collective-permute-start.9 = (bf16[6,128,128]{2,1,0:T(8,128)(2,1)S(1)}, bf16[6,128,128]{2,1,0:T(8,128)(2,1)S(1)}, u32[]{:S(2)}, u32[]{:S(2)}) collective-permute-start(bf16[6,128,128]{2,1,0:T(8,128)(2,1)S(1)} %collective-permute-done.1.refs_6_), channel_id=1, source_target_pairs={{0,4},{1,3},{4,8},{5,1},{8,12},{9,5},{12,14},{13,9},{14,10},{15,13... | collective-permute-start | bytes 589832 | tf_op jit(solution)/shard_map/ppermute | solution.py:33
  19.1 0.0 collective-permute-start.6
  19.1 1.6 %collective-permute-start.10 = (bf16[6,128,128]{2,1,0:T(8,128)(2,1)S(1)}, bf16[6,128,128]{2,1,0:T(8,128)(2,1)S(1)}, u32[]{:S(2)}, u32[]{:S(2)}) collective-permute-start(bf16[6,128,128]{2,1,0:T(8,128)(2,1)S(1)} %collective-permute-done.4.refs_7_), channel_id=1, source_target_pairs={{0,4},{1,3},{4,8},{5,1},{8,12},{9,5},{12,14},{13,9},{14,10},{15,13... | collective-permute-start | bytes 589832 | tf_op jit(solution)/shard_map/ppermute | solution.py:33
  20.7 0.0 collective-permute-start.7
  20.7 0.0 collective-permute-done.5.refs_4_
  20.7 0.5 collective-permute-start.8
  21.2 1.5 %collective-permute-done.9.refs_10_ = bf16[6,128,128]{2,1,0:T(8,128)(2,1)S(1)} collective-permute-done((bf16[6,128,128]{2,1,0:T(8,128)(2,1)S(1)}, bf16[6,128,128]{2,1,0:T(8,128)(2,1)S(1)}, u32[]{:S(2)}, u32[]{:S(2)}) %collective-permute-start.9) | collective-permute-done | bytes 196640 | tf_op jit(solution)/shard_map/ppermute | solution.py:33
  22.7 2.1 %collective-permute-start.13 = (bf16[6,128,128]{2,1,0:T(8,128)(2,1)S(1)}, bf16[6,128,128]{2,1,0:T(8,128)(2,1)S(1)}, u32[]{:S(2)}, u32[]{:S(2)}) collective-permute-start(bf16[6,128,128]{2,1,0:T(8,128)(2,1)S(1)} %collective-permute-done.9.refs_10_), channel_id=1, source_target_pairs={{0,4},{1,3},{4,8},{5,1},{8,12},{9,5},{12,14},{13,9},{14,10},{15,13... | collective-permute-start | bytes 589832 | tf_op jit(solution)/shard_map/ppermute | solution.py:33
  24.7 0.0 collective-permute-done.6.refs_5_
  24.7 0.0 collective-permute-start.11
  24.7 0.0 collective-permute-done.10.refs_11_
  24.8 2.1 %collective-permute-start.14 = (bf16[6,128,128]{2,1,0:T(8,128)(2,1)S(1)}, bf16[6,128,128]{2,1,0:T(8,128)(2,1)S(1)}, u32[]{:S(2)}, u32[]{:S(2)}) collective-permute-start(bf16[6,128,128]{2,1,0:T(8,128)(2,1)S(1)} %collective-permute-done.10.refs_11_), channel_id=1, source_target_pairs={{0,4},{1,3},{4,8},{5,1},{8,12},{9,5},{12,14},{13,9},{14,10},{15,13... | collective-permute-start | bytes 589832 | tf_op jit(solution)/shard_map/ppermute | solution.py:33
  26.8 0.0 collective-permute-done.7.refs_8_
  26.9 0.0 collective-permute-start.12
  26.9 0.0 collective-permute-done.8.refs_9_
  26.9 1.5 %collective-permute-done.13.refs_14_ = bf16[6,128,128]{2,1,0:T(8,128)(2,1)S(1)} collective-permute-done((bf16[6,128,128]{2,1,0:T(8,128)(2,1)S(1)}, bf16[6,128,128]{2,1,0:T(8,128)(2,1)S(1)}, u32[]{:S(2)}, u32[]{:S(2)}) %collective-permute-start.13) | collective-permute-done | bytes 196640 | tf_op jit(solution)/shard_map/ppermute | solution.py:33
  28.3 0.0 collective-permute-done.11.refs_12_
  28.3 2.1 %collective-permute-done.14.refs_15_ = bf16[6,128,128]{2,1,0:T(8,128)(2,1)S(1)} collective-permute-done((bf16[6,128,128]{2,1,0:T(8,128)(2,1)S(1)}, bf16[6,128,128]{2,1,0:T(8,128)(2,1)S(1)}, u32[]{:S(2)}, u32[]{:S(2)}) %collective-permute-start.14) | collective-permute-done | bytes 196640 | tf_op jit(solution)/shard_map/ppermute | solution.py:33
  30.5 0.0 collective-permute-done.12.refs_13_
  30.5 16.0 %shard_map.69 = (bf16[2064,128]{1,0:T(8,128)(2,1)S(1)}, f32[8,256,128]{2,1,0:T(8,128)S(1)}, f32[8,128]{1,0:T(8,128)S(1)}) custom-call(s32[8,384]{1,0:T(8,128)S(1)} %shard_map.68.plan_ref, bf16[256,128,128]{2,1,0:T(8,128)(2,1)} %left_ref.1, bf16[6,128,128]{2,1,0:T(8,128)(2,1)S(1)} %shard_map.67.refs_0_, ...), custom_call_target="tpu_custom_call" | custom-call | flops 4294967296 | bytes 15588608 | tf_op jit(solution)/shard_map/pallas_call | solution.py:304
  46.5 0.1 collective-permute-start.15
  46.6 1.9 %collective-permute-done.15.received_ref = bf16[2064,128]{1,0:T(8,128)(2,1)S(1)} collective-permute-done((bf16[2064,128]{1,0:T(8,128)(2,1)S(1)}, bf16[2064,128]{1,0:T(8,128)(2,1)S(1)}, u32[]{:S(2)}, u32[]{:S(2)}) %collective-permute-start.15) | collective-permute-done | bytes 528416 | tf_op jit(solution)/shard_map/ppermute | solution.py:19
  48.5 0.1 shard_map.70
  48.6 6.9 %collective-permute-start.16 = (bf16[272,128]{1,0:T(8,128)(2,1)S(1)}, bf16[272,128]{1,0:T(8,128)(2,1)S(1)}, u32[]{:S(2)}, u32[]{:S(2)}) collective-permute-start(bf16[272,128]{1,0:T(8,128)(2,1)S(1)} %get-tuple-element.46), channel_id=1, source_target_pairs={{0,14},{1,15},{2,12},{3,13},{4,10},{5,11},{6,8},{7,9},{8,6},{9,7},... | collective-permute-start | bytes 208904 | tf_op jit(solution)/shard_map/ppermute | solution.py:19
  55.4 4.8 %collective-permute-start.17 = (bf16[272,128]{1,0:T(8,128)(2,1)S(1)}, bf16[272,128]{1,0:T(8,128)(2,1)S(1)}, u32[]{:S(2)}, u32[]{:S(2)}) collective-permute-start(bf16[272,128]{1,0:T(8,128)(2,1)S(1)} %get-tuple-element.47), channel_id=1, source_target_pairs={{0,12},{1,13},{2,14},{3,15},{4,8},{5,9},{6,10},{7,11},{8,4},{9,5},... | collective-permute-start | bytes 208904 | tf_op jit(solution)/shard_map/ppermute | solution.py:19
  60.2 1.8 %collective-permute-start.18 = (bf16[272,128]{1,0:T(8,128)(2,1)S(1)}, bf16[272,128]{1,0:T(8,128)(2,1)S(1)}, u32[]{:S(2)}, u32[]{:S(2)}) collective-permute-start(bf16[272,128]{1,0:T(8,128)(2,1)S(1)} %get-tuple-element.48), channel_id=1, source_target_pairs={{0,10},{1,11},{2,8},{3,9},{4,14},{5,15},{6,12},{7,13},{8,2},{9,3},... | collective-permute-start | bytes 208904 | tf_op jit(solution)/shard_map/ppermute | solution.py:19
  62.0 1.9 %collective-permute-start.19 = (bf16[272,128]{1,0:T(8,128)(2,1)S(1)}, bf16[272,128]{1,0:T(8,128)(2,1)S(1)}, u32[]{:S(2)}, u32[]{:S(2)}) collective-permute-start(bf16[272,128]{1,0:T(8,128)(2,1)S(1)} %get-tuple-element.49), channel_id=1, source_target_pairs={{0,8},{1,9},{2,10},{3,11},{4,12},{5,13},{6,14},{7,15},{8,0},{9,1},... | collective-permute-start | bytes 208904 | tf_op jit(solution)/shard_map/ppermute | solution.py:19
  63.9 1.5 %collective-permute-start.20 = (bf16[272,128]{1,0:T(8,128)(2,1)S(1)}, bf16[272,128]{1,0:T(8,128)(2,1)S(1)}, u32[]{:S(2)}, u32[]{:S(2)}) collective-permute-start(bf16[272,128]{1,0:T(8,128)(2,1)S(1)} %get-tuple-element.50), channel_id=1, source_target_pairs={{0,6},{1,7},{2,4},{3,5},{4,2},{5,3},{6,0},{7,1},{8,14},{9,15},{10,... | collective-permute-start | bytes 208904 | tf_op jit(solution)/shard_map/ppermute | solution.py:19
  65.4 0.0 collective-permute-done.16.refs_0_
  65.4 0.6 collective-permute-start.21
  66.0 0.0 collective-permute-done.17.refs_1_
  66.0 2.9 %collective-permute-start.22 = (bf16[272,128]{1,0:T(8,128)(2,1)S(1)}, bf16[272,128]{1,0:T(8,128)(2,1)S(1)}, u32[]{:S(2)}, u32[]{:S(2)}) collective-permute-start(bf16[272,128]{1,0:T(8,128)(2,1)S(1)} %get-tuple-element.52), channel_id=1, source_target_pairs={{0,2},{1,3},{2,0},{3,1},{4,6},{5,7},{6,4},{7,5},{8,10},{9,11},{10,... | collective-permute-start | bytes 208904 | tf_op jit(solution)/shard_map/ppermute | solution.py:19
  68.9 1.0 %shard_map.72 = f32[2,2]{1,0:T(2,128)} custom-call(bf16[6,128,128]{2,1,0:T(8,128)(2,1)S(1)} %shard_map.67.refs_0_, bf16[6,128,128]{2,1,0:T(8,128)(2,1)S(1)} %collective-permute-done.2.refs_1_, bf16[6,128,128]{2,1,0:T(8,128)(2,1)S(1)} %collective-permute-done.refs_2_, bf16[6,128,128]{2,1,0:T(8,128)(2,1)S(1)} %collective-permute-done.3.refs_3_, ...), custom_call_target="tpu_custom_call" | custom-call | tf_op jit(solution)/shard_map/pallas_call | solution.py:354
  69.9 1.4 %collective-permute-done.18.refs_2_ = bf16[272,128]{1,0:T(8,128)(2,1)S(1)} collective-permute-done((bf16[272,128]{1,0:T(8,128)(2,1)S(1)}, bf16[272,128]{1,0:T(8,128)(2,1)S(1)}, u32[]{:S(2)}, u32[]{:S(2)}) %collective-permute-start.18) | collective-permute-done | bytes 69664 | tf_op jit(solution)/shard_map/ppermute | solution.py:19
  71.3 0.8 %collective-permute-done.19.refs_3_ = bf16[272,128]{1,0:T(8,128)(2,1)S(1)} collective-permute-done((bf16[272,128]{1,0:T(8,128)(2,1)S(1)}, bf16[272,128]{1,0:T(8,128)(2,1)S(1)}, u32[]{:S(2)}, u32[]{:S(2)}) %collective-permute-start.19) | collective-permute-done | bytes 69664 | tf_op jit(solution)/shard_map/ppermute | solution.py:19
  72.1 0.0 collective-permute-done.20.refs_4_
  72.1 0.1 collective-permute-done.21.refs_5_
  72.2 0.0 collective-permute-done.22.refs_6_
  72.2 0.7 %shard_map.71 = (f32[1,2,128,128]{3,2,1,0:T(8,128)}, f32[2,2]{1,0:T(2,128)}) custom-call(f32[256,128]{1,0:T(8,128)S(1)} %get-tuple-element.44.mine_ref, f32[16,128]{1,0:T(8,128)S(1)} %get-tuple-element.45.total_ref, bf16[272,128]{1,0:T(8,128)(2,1)S(1)} %collective-permute-done.16.refs_0_, bf16[272,128]{1,0:T(8,128)(2,1)S(1)} %collective-permute-done.17.refs_1_, ...), custom_call_target="tpu_custom_call" | custom-call | tf_op jit(solution)/shard_map/pallas_call | solution.py:397
Async XLA Ops:
  0.6 0.9 %copy-start = (bf16[4,128,128]{2,1,0:T(8,128)(2,1)S(1)}, bf16[4,128,128]{2,1,0:T(8,128)(2,1)}, u32[]{:S(2)}) copy-start(bf16[4,128,128]{2,1,0:T(8,128)(2,1)} %right_ref.1) | copy-start | bytes 393220
  1.5 0.8 %copy-start.1 = (bf16[1,2,128,128]{3,2,1,0:T(8,128)(2,1)S(1)}, bf16[1,2,128,128]{3,2,1,0:T(8,128)(2,1)}, u32[]{:S(2)}) copy-start(bf16[1,2,128,128]{3,2,1,0:T(8,128)(2,1)} %trial_ref.1) | copy-start | bytes 196612
  2.5 3.2 %collective-permute-start.2 = (bf16[6,128,128]{2,1,0:T(8,128)(2,1)S(1)}, bf16[6,128,128]{2,1,0:T(8,128)(2,1)S(1)}, u32[]{:S(2)}, u32[]{:S(2)}) collective-permute-start(bf16[6,128,128]{2,1,0:T(8,128)(2,1)S(1)} %shard_map.67.refs_0_), channel_id=1, source_target_pairs={{0,1},{1,0},{2,3},{3,2},{4,5},{5,4},{6,7},{7,6},{8,9},{9,8},{10,11... | collective-permute-start | bytes 589832 | tf_op jit(solution)/shard_map/ppermute | solution.py:19
  3.0 6.2 %collective-permute-start = (bf16[6,128,128]{2,1,0:T(8,128)(2,1)S(1)}, bf16[6,128,128]{2,1,0:T(8,128)(2,1)S(1)}, u32[]{:S(2)}, u32[]{:S(2)}) collective-permute-start(bf16[6,128,128]{2,1,0:T(8,128)(2,1)S(1)} %shard_map.67.refs_0_), channel_id=1, source_target_pairs={{0,4},{1,3},{4,8},{5,1},{8,12},{9,5},{12,14},{13,9},{14,10},{15,13... | collective-permute-start | bytes 589832 | tf_op jit(solution)/shard_map/ppermute | solution.py:33
  5.6 5.7 %collective-permute-start.3 = (bf16[6,128,128]{2,1,0:T(8,128)(2,1)S(1)}, bf16[6,128,128]{2,1,0:T(8,128)(2,1)S(1)}, u32[]{:S(2)}, u32[]{:S(2)}) collective-permute-start(bf16[6,128,128]{2,1,0:T(8,128)(2,1)S(1)} %collective-permute-done.2.refs_1_), channel_id=1, source_target_pairs={{0,4},{1,3},{4,8},{5,1},{8,12},{9,5},{12,14},{13,9},{14,10},{15,13... | collective-permute-start | bytes 589832 | tf_op jit(solution)/shard_map/ppermute | solution.py:33
  9.2 5.9 %collective-permute-start.1 = (bf16[6,128,128]{2,1,0:T(8,128)(2,1)S(1)}, bf16[6,128,128]{2,1,0:T(8,128)(2,1)S(1)}, u32[]{:S(2)}, u32[]{:S(2)}) collective-permute-start(bf16[6,128,128]{2,1,0:T(8,128)(2,1)S(1)} %collective-permute-done.refs_2_), channel_id=1, source_target_pairs={{0,4},{1,3},{4,8},{5,1},{8,12},{9,5},{12,14},{13,9},{14,10},{15,13... | collective-permute-start | bytes 589832 | tf_op jit(solution)/shard_map/ppermute | solution.py:33
  11.3 5.7 %collective-permute-start.4 = (bf16[6,128,128]{2,1,0:T(8,128)(2,1)S(1)}, bf16[6,128,128]{2,1,0:T(8,128)(2,1)S(1)}, u32[]{:S(2)}, u32[]{:S(2)}) collective-permute-start(bf16[6,128,128]{2,1,0:T(8,128)(2,1)S(1)} %collective-permute-done.3.refs_3_), channel_id=1, source_target_pairs={{0,4},{1,3},{4,8},{5,1},{8,12},{9,5},{12,14},{13,9},{14,10},{15,13... | collective-permute-start | bytes 589832 | tf_op jit(solution)/shard_map/ppermute | solution.py:33
  13.4 0.7 copy-start.2
  15.0 5.6 %collective-permute-start.5 = (bf16[6,128,128]{2,1,0:T(8,128)(2,1)S(1)}, bf16[6,128,128]{2,1,0:T(8,128)(2,1)S(1)}, u32[]{:S(2)}, u32[]{:S(2)}) collective-permute-start(bf16[6,128,128]{2,1,0:T(8,128)(2,1)S(1)} %collective-permute-done.refs_2_), channel_id=1, source_target_pairs={{0,1},{1,0},{2,3},{3,2},{4,5},{5,4},{6,7},{7,6},{8,9},{9,8},{10,11... | collective-permute-start | bytes 589832 | tf_op jit(solution)/shard_map/ppermute | solution.py:19
  17.0 5.7 %collective-permute-start.9 = (bf16[6,128,128]{2,1,0:T(8,128)(2,1)S(1)}, bf16[6,128,128]{2,1,0:T(8,128)(2,1)S(1)}, u32[]{:S(2)}, u32[]{:S(2)}) collective-permute-start(bf16[6,128,128]{2,1,0:T(8,128)(2,1)S(1)} %collective-permute-done.1.refs_6_), channel_id=1, source_target_pairs={{0,4},{1,3},{4,8},{5,1},{8,12},{9,5},{12,14},{13,9},{14,10},{15,13... | collective-permute-start | bytes 589832 | tf_op jit(solution)/shard_map/ppermute | solution.py:33
  19.1 5.7 %collective-permute-start.6 = (bf16[6,128,128]{2,1,0:T(8,128)(2,1)S(1)}, bf16[6,128,128]{2,1,0:T(8,128)(2,1)S(1)}, u32[]{:S(2)}, u32[]{:S(2)}) collective-permute-start(bf16[6,128,128]{2,1,0:T(8,128)(2,1)S(1)} %collective-permute-done.3.refs_3_), channel_id=1, source_target_pairs={{0,1},{1,0},{2,3},{3,2},{4,5},{5,4},{6,7},{7,6},{8,9},{9,8},{10,11... | collective-permute-start | bytes 589832 | tf_op jit(solution)/shard_map/ppermute | solution.py:19
  19.1 5.7 %collective-permute-start.10 = (bf16[6,128,128]{2,1,0:T(8,128)(2,1)S(1)}, bf16[6,128,128]{2,1,0:T(8,128)(2,1)S(1)}, u32[]{:S(2)}, u32[]{:S(2)}) collective-permute-start(bf16[6,128,128]{2,1,0:T(8,128)(2,1)S(1)} %collective-permute-done.4.refs_7_), channel_id=1, source_target_pairs={{0,4},{1,3},{4,8},{5,1},{8,12},{9,5},{12,14},{13,9},{14,10},{15,13... | collective-permute-start | bytes 589832 | tf_op jit(solution)/shard_map/ppermute | solution.py:33
  20.7 6.2 %collective-permute-start.7 = (bf16[6,128,128]{2,1,0:T(8,128)(2,1)S(1)}, bf16[6,128,128]{2,1,0:T(8,128)(2,1)S(1)}, u32[]{:S(2)}, u32[]{:S(2)}) collective-permute-start(bf16[6,128,128]{2,1,0:T(8,128)(2,1)S(1)} %collective-permute-done.1.refs_6_), channel_id=1, source_target_pairs={{0,1},{1,0},{2,3},{3,2},{4,5},{5,4},{6,7},{7,6},{8,9},{9,8},{10,11... | collective-permute-start | bytes 589832 | tf_op jit(solution)/shard_map/ppermute | solution.py:19
  20.7 6.2 %collective-permute-start.8 = (bf16[6,128,128]{2,1,0:T(8,128)(2,1)S(1)}, bf16[6,128,128]{2,1,0:T(8,128)(2,1)S(1)}, u32[]{:S(2)}, u32[]{:S(2)}) collective-permute-start(bf16[6,128,128]{2,1,0:T(8,128)(2,1)S(1)} %collective-permute-done.4.refs_7_), channel_id=1, source_target_pairs={{0,1},{1,0},{2,3},{3,2},{4,5},{5,4},{6,7},{7,6},{8,9},{9,8},{10,11... | collective-permute-start | bytes 589832 | tf_op jit(solution)/shard_map/ppermute | solution.py:19
  22.7 5.7 %collective-permute-start.13 = (bf16[6,128,128]{2,1,0:T(8,128)(2,1)S(1)}, bf16[6,128,128]{2,1,0:T(8,128)(2,1)S(1)}, u32[]{:S(2)}, u32[]{:S(2)}) collective-permute-start(bf16[6,128,128]{2,1,0:T(8,128)(2,1)S(1)} %collective-permute-done.9.refs_10_), channel_id=1, source_target_pairs={{0,4},{1,3},{4,8},{5,1},{8,12},{9,5},{12,14},{13,9},{14,10},{15,13... | collective-permute-start | bytes 589832 | tf_op jit(solution)/shard_map/ppermute | solution.py:33
  24.7 3.6 %collective-permute-start.11 = (bf16[6,128,128]{2,1,0:T(8,128)(2,1)S(1)}, bf16[6,128,128]{2,1,0:T(8,128)(2,1)S(1)}, u32[]{:S(2)}, u32[]{:S(2)}) collective-permute-start(bf16[6,128,128]{2,1,0:T(8,128)(2,1)S(1)} %collective-permute-done.9.refs_10_), channel_id=1, source_target_pairs={{0,1},{1,0},{2,3},{3,2},{4,5},{5,4},{6,7},{7,6},{8,9},{9,8},{10,11... | collective-permute-start | bytes 589832 | tf_op jit(solution)/shard_map/ppermute | solution.py:19
  24.8 5.7 %collective-permute-start.14 = (bf16[6,128,128]{2,1,0:T(8,128)(2,1)S(1)}, bf16[6,128,128]{2,1,0:T(8,128)(2,1)S(1)}, u32[]{:S(2)}, u32[]{:S(2)}) collective-permute-start(bf16[6,128,128]{2,1,0:T(8,128)(2,1)S(1)} %collective-permute-done.10.refs_11_), channel_id=1, source_target_pairs={{0,4},{1,3},{4,8},{5,1},{8,12},{9,5},{12,14},{13,9},{14,10},{15,13... | collective-permute-start | bytes 589832 | tf_op jit(solution)/shard_map/ppermute | solution.py:33
  26.9 3.6 %collective-permute-start.12 = (bf16[6,128,128]{2,1,0:T(8,128)(2,1)S(1)}, bf16[6,128,128]{2,1,0:T(8,128)(2,1)S(1)}, u32[]{:S(2)}, u32[]{:S(2)}) collective-permute-start(bf16[6,128,128]{2,1,0:T(8,128)(2,1)S(1)} %collective-permute-done.10.refs_11_), channel_id=1, source_target_pairs={{0,1},{1,0},{2,3},{3,2},{4,5},{5,4},{6,7},{7,6},{8,9},{9,8},{10,11... | collective-permute-start | bytes 589832 | tf_op jit(solution)/shard_map/ppermute | solution.py:19
  46.5 2.0 %collective-permute-start.15 = (bf16[2064,128]{1,0:T(8,128)(2,1)S(1)}, bf16[2064,128]{1,0:T(8,128)(2,1)S(1)}, u32[]{:S(2)}, u32[]{:S(2)}) collective-permute-start(bf16[2064,128]{1,0:T(8,128)(2,1)S(1)} %get-tuple-element.43), channel_id=1, source_target_pairs={{0,1},{1,0},{2,3},{3,2},{4,5},{5,4},{6,7},{7,6},{8,9},{9,8},{10,11... | collective-permute-start | bytes 1585160 | tf_op jit(solution)/shard_map/ppermute | solution.py:19
  48.6 16.8 %collective-permute-start.16 = (bf16[272,128]{1,0:T(8,128)(2,1)S(1)}, bf16[272,128]{1,0:T(8,128)(2,1)S(1)}, u32[]{:S(2)}, u32[]{:S(2)}) collective-permute-start(bf16[272,128]{1,0:T(8,128)(2,1)S(1)} %get-tuple-element.46), channel_id=1, source_target_pairs={{0,14},{1,15},{2,12},{3,13},{4,10},{5,11},{6,8},{7,9},{8,6},{9,7},... | collective-permute-start | bytes 208904 | tf_op jit(solution)/shard_map/ppermute | solution.py:19
  55.4 10.6 %collective-permute-start.17 = (bf16[272,128]{1,0:T(8,128)(2,1)S(1)}, bf16[272,128]{1,0:T(8,128)(2,1)S(1)}, u32[]{:S(2)}, u32[]{:S(2)}) collective-permute-start(bf16[272,128]{1,0:T(8,128)(2,1)S(1)} %get-tuple-element.47), channel_id=1, source_target_pairs={{0,12},{1,13},{2,14},{3,15},{4,8},{5,9},{6,10},{7,11},{8,4},{9,5},... | collective-permute-start | bytes 208904 | tf_op jit(solution)/shard_map/ppermute | solution.py:19
  60.2 11.1 %collective-permute-start.18 = (bf16[272,128]{1,0:T(8,128)(2,1)S(1)}, bf16[272,128]{1,0:T(8,128)(2,1)S(1)}, u32[]{:S(2)}, u32[]{:S(2)}) collective-permute-start(bf16[272,128]{1,0:T(8,128)(2,1)S(1)} %get-tuple-element.48), channel_id=1, source_target_pairs={{0,10},{1,11},{2,8},{3,9},{4,14},{5,15},{6,12},{7,13},{8,2},{9,3},... | collective-permute-start | bytes 208904 | tf_op jit(solution)/shard_map/ppermute | solution.py:19
  62.0 10.1 %collective-permute-start.19 = (bf16[272,128]{1,0:T(8,128)(2,1)S(1)}, bf16[272,128]{1,0:T(8,128)(2,1)S(1)}, u32[]{:S(2)}, u32[]{:S(2)}) collective-permute-start(bf16[272,128]{1,0:T(8,128)(2,1)S(1)} %get-tuple-element.49), channel_id=1, source_target_pairs={{0,8},{1,9},{2,10},{3,11},{4,12},{5,13},{6,14},{7,15},{8,0},{9,1},... | collective-permute-start | bytes 208904 | tf_op jit(solution)/shard_map/ppermute | solution.py:19
  63.9 8.2 %collective-permute-start.20 = (bf16[272,128]{1,0:T(8,128)(2,1)S(1)}, bf16[272,128]{1,0:T(8,128)(2,1)S(1)}, u32[]{:S(2)}, u32[]{:S(2)}) collective-permute-start(bf16[272,128]{1,0:T(8,128)(2,1)S(1)} %get-tuple-element.50), channel_id=1, source_target_pairs={{0,6},{1,7},{2,4},{3,5},{4,2},{5,3},{6,0},{7,1},{8,14},{9,15},{10,... | collective-permute-start | bytes 208904 | tf_op jit(solution)/shard_map/ppermute | solution.py:19
  65.4 6.8 %collective-permute-start.21 = (bf16[272,128]{1,0:T(8,128)(2,1)S(1)}, bf16[272,128]{1,0:T(8,128)(2,1)S(1)}, u32[]{:S(2)}, u32[]{:S(2)}) collective-permute-start(bf16[272,128]{1,0:T(8,128)(2,1)S(1)} %get-tuple-element.51), channel_id=1, source_target_pairs={{0,4},{1,5},{2,6},{3,7},{4,0},{5,1},{6,2},{7,3},{8,12},{9,13},{10,... | collective-permute-start | bytes 208904 | tf_op jit(solution)/shard_map/ppermute | solution.py:19
  66.0 6.2 %collective-permute-start.22 = (bf16[272,128]{1,0:T(8,128)(2,1)S(1)}, bf16[272,128]{1,0:T(8,128)(2,1)S(1)}, u32[]{:S(2)}, u32[]{:S(2)}) collective-permute-start(bf16[272,128]{1,0:T(8,128)(2,1)S(1)} %get-tuple-element.52), channel_id=1, source_target_pairs={{0,2},{1,3},{2,0},{3,1},{4,6},{5,7},{6,4},{7,5},{8,10},{9,11},{10,... | collective-permute-start | bytes 208904 | tf_op jit(solution)/shard_map/ppermute | solution.py:19

commit v8 on v7

--- a/solution.py
+++ b/solution.py
@@ -10,8 +10,8 @@
 MIB = 1024 * 1024
 TAIL = 16
 TRIALS = 2
-CHUNK = 16
-PAIRS = 8
+CHUNK = 48
+PAIRS = 24
 AHEAD = 3
 
 
@@ -91,6 +91,13 @@
 def place_of(chip, chips):
     half = jnp.floor(chip * 0.5)
     return jnp.where(chip == 2.0 * half, half, chips - 1.0 - half)
+
+
+def stage_kernel(n, terms, tasks_ref, left_ref, plan_ref, held_ref, sem):
+    copy = pltpu.make_async_copy(left_ref, held_ref, sem)
+    copy.start()
+    plan_kernel(n, terms, tasks_ref, plan_ref)
+    copy.wait()
 
 
 def plan_kernel(n, terms, tasks_ref, plan_ref):
@@ -162,13 +169,27 @@
     plan_ref[6:8] = jnp.zeros((2, places), jnp.int32)
 
 
-def make_plan(tasks, n, terms):
+def make_plan(tasks, left_ops, n, terms):
     most = source_places(tasks.shape[1], n) + 2 * PAIRS
-    return pl.pallas_call(
-        functools.partial(plan_kernel, n, terms),
-        out_shape=jax.ShapeDtypeStruct((8, -(-most // 128) * 128), jnp.int32),
-        compiler_params=pltpu.CompilerParams(vmem_limit_bytes=16 * MIB),
-    )(tasks)
+    plan = jax.ShapeDtypeStruct((8, -(-most // 128) * 128), jnp.int32)
+    vmem = pl.BlockSpec(memory_space=pltpu.VMEM)
+    if fits(n):
+        return pl.pallas_call(
+            functools.partial(stage_kernel, n, terms),
+            in_specs=[vmem, pl.BlockSpec(memory_space=pltpu.HBM)],
+            out_specs=(vmem, vmem),
+            out_shape=(plan, jax.ShapeDtypeStruct(left_ops.shape, left_ops.dtype)),
+            scratch_shapes=[pltpu.SemaphoreType.DMA],
+            compiler_params=pltpu.CompilerParams(vmem_limit_bytes=42 * MIB),
+        )(tasks, left_ops)
+    return (
+        pl.pallas_call(
+            functools.partial(plan_kernel, n, terms),
+            out_shape=plan,
+            compiler_params=pltpu.CompilerParams(vmem_limit_bytes=16 * MIB),
+        )(tasks),
+        left_ops,
+    )
 
 
 def block_copies(n, kinds, blocks, trial, right, sem, which):
@@ -184,56 +205,68 @@
     return copies
 
 
-def half_steps(n, phase, plan_ref, left_ref, trial, halves, left, left_sem):
-    first, last = plan_ref[5, phase], plan_ref[5, phase + 1]
+def make_halves(n, plan_ref, left_ref, trial, halves, fetched):
+    turns = plan_ref[5, 1]
     run = run_of(left_ref.shape[0], n)
 
     def fetch(turn):
+        left, left_sem = fetched
         at = lax.rem(turn, AHEAD)
         for u in range(CHUNK):
             slot = plan_ref[0, turn * CHUNK + u]
             pltpu.make_async_copy(left_ref.at[slot], left.at[at, u], left_sem.at[at]).start()
 
     def start():
-        for ahead in range(AHEAD - 1):
-
-            @pl.when(first + ahead < last)
+        for turn in range(AHEAD - 1) if fetched else ():
+
+            @pl.when(turn < turns)
             def _():
-                fetch(first + ahead)
+                fetch(turn)
 
     def turn_of(turn, carry):
-        @pl.when(turn + AHEAD - 1 < last)
-        def _():
-            fetch(turn + AHEAD - 1)
-
-        at = lax.rem(turn, AHEAD)
-        pltpu.make_async_copy(left_ref.at[pl.ds(0, CHUNK)], left.at[at], left_sem.at[at]).wait()
+        if fetched:
+            left, left_sem = fetched
+
+            @pl.when(turn + AHEAD - 1 < turns)
+            def _():
+                fetch(turn + AHEAD - 1)
+
+            at = lax.rem(turn, AHEAD)
+            pltpu.make_async_copy(left_ref.at[pl.ds(0, CHUNK)], left.at[at], left_sem.at[at]).wait()
         place = turn * CHUNK
         for r in range(0, CHUNK, run):
             source = plan_ref[1, place + r]
             vectors = jnp.concatenate([trial[source, 0], trial[source, 1]], axis=1)
-            rows = left[at, r : r + run].reshape(run * 128, 128)
+            if fetched:
+                rows = left[at, r : r + run].reshape(run * 128, 128)
+            else:
+                rows = jnp.concatenate([left_ref[plan_ref[0, place + r + u]] for u in range(run)], axis=0)
             half = jnp.dot(rows, vectors, preferred_element_type=jnp.float32).astype(jnp.bfloat16)
             for u in range(run):
                 halves[place + r + u, 0] = half[u * 128 : (u + 1) * 128, :128]
                 halves[place + r + u, 1] = half[u * 128 : (u + 1) * 128, 128:]
         return carry
 
-    return start, lambda: lax.fori_loop(first, last, turn_of, 0)
+    return start, lambda: lax.fori_loop(0, turns, turn_of, 0)
 
 
 def tasks_kernel(n, kinds, plan_ref, left_ref, *refs):
     blocks, refs = refs[: len(kinds)], refs[len(kinds) :]
-    send_ref, keep_ref, own_ref, halves, trial, right, acc, left, block_sem, left_sem = refs
-    phase = phases_of(n) - 1
-    start, products = half_steps(n, phase, plan_ref, left_ref, trial, halves, left, left_sem)
-    moves = [block_copies(n, kinds, blocks, trial, right, block_sem, which) for which in range(2)]
-    for copy in moves[0]:
-        copy.start()
+    send_ref, keep_ref, own_ref, halves, trial, right, acc, block_sem, *fetched = refs
+    start, products = make_halves(n, plan_ref, left_ref, trial, halves, fetched)
+    right[right.shape[0] - 1] = jnp.zeros((128, 128), jnp.bfloat16)
     start()
-    for copy in moves[1]:
-        copy.start()
-    right[right.shape[0] - 1] = jnp.zeros((128, 128), jnp.bfloat16)
+    if fits(n):
+        moves = ([], [])
+        for b, kind in enumerate(kinds):
+            owner = owner_of(*kind, n)
+            per = blocks[b].shape[0] - TRIALS
+            trial[owner] = blocks[b][0:TRIALS]
+            right[pl.ds(owner * per, per)] = blocks[b][TRIALS:]
+    else:
+        moves = [block_copies(n, kinds, blocks, trial, right, block_sem, which) for which in range(2)]
+        for copy in moves[0] + moves[1]:
+            copy.start()
 
     def clear(s, carry):
         acc[s] = jnp.zeros((256, 128), jnp.float32)
@@ -266,31 +299,28 @@
             acc[target] = acc[target] + term
         return carry
 
-    lax.fori_loop(0, plan_ref[5, phase + 2], target_turn, 0)
+    lax.fori_loop(0, plan_ref[5, 2], target_turn, 0)
     me = lax.axis_index("op")
+
+    def dots(s, carry):
+        t0 = trial[s, 0].astype(jnp.float32)
+        t1 = trial[s, 1].astype(jnp.float32)
+        a0 = acc[s, 0:128, :]
+        a1 = acc[s, 128:256, :]
+        p00, p01, p10, p11 = carry
+        return p00 + fold(t0 * a0), p01 + fold(t0 * a1), p10 + fold(t1 * a0), p11 + fold(t1 * a1)
+
+    zero = jnp.zeros((8, 128), jnp.float32)
+    sums = lax.fori_loop(0, n, dots, (zero,) * 4)
+    p00, p01, p10, p11 = [jnp.sum(x) for x in sums]
 
     def pack(j, carry):
         mine = jnp.bitwise_xor(me, 2 * j)
-        p00, p01, p10, p11 = carry
-        for other, s in enumerate((mine, jnp.bitwise_xor(mine, 1))):
-            t0 = trial[s, 0].astype(jnp.float32)
-            t1 = trial[s, 1].astype(jnp.float32)
-            a0 = acc[s, 0:128, :]
-            a1 = acc[s, 128:256, :]
-            p00, p01 = p00 + fold(t0 * a0), p01 + fold(t0 * a1)
-            p10, p11 = p10 + fold(t1 * a0), p11 + fold(t1 * a1)
-            if other:
-                rows = pl.multiple_of(j * 256, 256)
-                send_ref[pl.ds(rows, 128), :] = a0.astype(jnp.bfloat16)
-                send_ref[pl.ds(rows + 128, 128), :] = a1.astype(jnp.bfloat16)
-            else:
-                keep_ref[j, 0:128, :] = a0
-                keep_ref[j, 128:256, :] = a1
-        return p00, p01, p10, p11
-
-    zero = jnp.zeros((8, 128), jnp.float32)
-    sums = lax.fori_loop(0, n // 2, pack, (zero,) * 4, unroll=2)
-    p00, p01, p10, p11 = [jnp.sum(x) for x in sums]
+        keep_ref[j] = acc[mine]
+        send_ref[pl.ds(pl.multiple_of(j * 256, 256), 256), :] = acc[jnp.bitwise_xor(mine, 1)].astype(jnp.bfloat16)
+        return carry
+
+    lax.fori_loop(0, n // 2, pack, 0)
     own = split3(matrix_of({(0, 0): p00, (0, 1): p01, (1, 0): p10, (1, 1): p11}, 3))
     own_ref[...] = own
     send_ref[n // 2 * 256 :, :] = tail_of(own, jnp.zeros_like(own))
@@ -301,6 +331,11 @@
     terms_per = blocks[0][0].shape[0] - TRIALS
     kinds = tuple(block[1:] for block in blocks)
     vmem, hbm = pl.BlockSpec(memory_space=pltpu.VMEM), pl.BlockSpec(memory_space=pltpu.HBM)
+    given = vmem if fits(n) else hbm
+    fetched = [] if fits(n) else [
+        pltpu.VMEM((AHEAD, CHUNK, 128, 128), jnp.bfloat16),
+        pltpu.SemaphoreType.DMA((AHEAD,)),
+    ]
     return pl.pallas_call(
         functools.partial(tasks_kernel, n, kinds),
         out_shape=(
@@ -308,18 +343,17 @@
             jax.ShapeDtypeStruct((n // 2, 256, 128), jnp.float32),
             jax.ShapeDtypeStruct((8, 128), jnp.float32),
         ),
-        in_specs=[pl.BlockSpec(memory_space=pltpu.SMEM), hbm] + [vmem if fits(n) else hbm] * len(blocks),
+        in_specs=[pl.BlockSpec(memory_space=pltpu.SMEM)] + [given] * (1 + len(blocks)),
         out_specs=(vmem,) * 3,
         scratch_shapes=[
             pltpu.VMEM((source_places(slots, n), 2, 128, 128), jnp.bfloat16),
             pltpu.VMEM((n, TRIALS, 128, 128), jnp.bfloat16),
             pltpu.VMEM((n * terms_per + 1, 128, 128), jnp.bfloat16),
             pltpu.VMEM((n + 1, 256, 128), jnp.float32),
-            pltpu.VMEM((AHEAD, CHUNK, 128, 128), jnp.bfloat16),
             pltpu.SemaphoreType.DMA((len(blocks), 2)),
-            pltpu.SemaphoreType.DMA((AHEAD,)),
-        ],
-        compiler_params=pltpu.CompilerParams(vmem_limit_bytes=(48 if fits(n) else 58) * MIB),
+        ]
+        + fetched,
+        compiler_params=pltpu.CompilerParams(vmem_limit_bytes=(30 if fits(n) else 58) * MIB),
         cost_estimate=pl.CostEstimate(
             flops=slots * 8 * 128**3, bytes_accessed=slots * 32768 + n * 450000, transcendentals=0
         ),
@@ -407,12 +441,12 @@
 def body(n, trial, left_ops, right_ops, task_list):
     steps = n // 4
     own = join(trial, right_ops)
-    plan = make_plan(task_list.T, n, n * right_ops.shape[0])
+    plan, left_ops = make_plan(task_list.T, left_ops, n, n * right_ops.shape[0])
     lines = [own, exchange(own, n, 1)]
     blocks = [(value, 0, False, half) for half, value in enumerate(lines)]
     for step in range(1, steps + 1):
         if step == steps // 2 + 1:
-            lines, plan = lax.optimization_barrier((lines, plan))
+            lines, plan, left_ops = lax.optimization_barrier((lines, plan, left_ops))
         for half in range(2):
             lines[half] = ring_step(lines[half], n)
             blocks.append((lines[half], step, False, half))

time: 73.8 us -> 64.8 us (0.88)
  starting transfers between devices: 37.7 us -> 32.8 us
  Pallas kernels: 18.8 us -> 15.5 us
    pallas_call x1, Pallas kernels: 16 us -> 10.2 us  [run_tasks(): pl.pallas_call(functools.partial(tasks_kernel, n, kinds), out_shape=(jax....]
    ppermute x15, starting transfers between devices: 21.5 us -> 18.1 us  [exchange(): return lax.ppermute(value, 'op', [(i, i ^ mask) for i in range(n)])]
    pallas_call x1, Pallas kernels: 0.92 us -> 3.39 us  [make_plan(): pl.pallas_call(functools.partial(stage_kernel, n, terms), in_specs=[vmem,...]
    ppermute x8, starting transfers between devices: 16.2 us -> 14.7 us  [ring_step(): return lax.ppermute(value, 'op', pairs)]
  transfers between devices with their start and end apart: 23 -> 23, of which waited for: 9 -> 8; matrix products, arithmetic and copies ran while one was open for 0% -> 0% of each run, Pallas kernels for 3% -> 7%
where the time goes in v8:
time: 64.8 us; the launch traced here: 64.6 us
  starting transfers between devices  32.8 us (51%)
  Pallas kernels  15.5 us (24%)
  waiting for transfers between devices  13.1 us (20%)
  local copies, waits for them, and re-layouts  2.42 us (4%)
  between operations  0.72 us (1%)
    ppermute x15, starting transfers between devices, exchange(): return lax.ppermute(value, 'op', [(i, i ^ mask) for i in range(n)])  18.1 us
    ppermute x8, starting transfers between devices, ring_step(): return lax.ppermute(value, 'op', pairs)  14.7 us
    pallas_call x1, Pallas kernels, run_tasks(): pl.pallas_call(functools.partial(tasks_kernel, n, kinds), out_shape=(jax....  10.2 us
    ppermute x8, waiting for transfers between devices, ring_step(): return lax.ppermute(value, 'op', pairs)  8.64 us
    ppermute x15, waiting for transfers between devices, exchange(): return lax.ppermute(value, 'op', [(i, i ^ mask) for i in range(n)])  4.51 us
    pallas_call x1, Pallas kernels, make_plan(): pl.pallas_call(functools.partial(stage_kernel, n, terms), in_specs=[vmem,...  3.39 us
    unnamed x6, local copies, waits for them, and re-layouts  2.42 us
  transfers between devices with their start and end apart: 23, of which 8 were waited for; matrix products, arithmetic and copies ran while one was open for 0% of the time, Pallas kernels for 7%

profile of v8, /device:TPU:0, one launch (start us, length us, event | category | flops | bytes accessed | tf_op | source)
XLA Modules:
  0.0 64.6 jit_solution(15030307969075030791)
XLA Ops:
  0.6 0.0 copy-start
  0.6 0.9 %copy-done = bf16[4,128,128]{2,1,0:T(8,128)(2,1)S(1)} copy-done((bf16[4,128,128]{2,1,0:T(8,128)(2,1)S(1)}, bf16[4,128,128]{2,1,0:T(8,128)(2,1)}, u32[]{:S(2)}) %copy-start) | copy-done | bytes 131096
  1.5 0.0 copy-start.1
  1.5 0.8 %copy-done.1 = bf16[1,2,128,128]{3,2,1,0:T(8,128)(2,1)S(1)} copy-done((bf16[1,2,128,128]{3,2,1,0:T(8,128)(2,1)S(1)}, bf16[1,2,128,128]{3,2,1,0:T(8,128)(2,1)}, u32[]{:S(2)}) %copy-start.1) | copy-done | bytes 65560
  2.4 0.1 shard_map.67.refs_0_
  2.5 0.5 collective-permute-start.2
  3.0 2.6 %collective-permute-start = (bf16[6,128,128]{2,1,0:T(8,128)(2,1)S(1)}, bf16[6,128,128]{2,1,0:T(8,128)(2,1)S(1)}, u32[]{:S(2)}, u32[]{:S(2)}) collective-permute-start(bf16[6,128,128]{2,1,0:T(8,128)(2,1)S(1)} %shard_map.67.refs_0_), channel_id=1, source_target_pairs={{0,4},{1,3},{4,8},{5,1},{8,12},{9,5},{12,14},{13,9},{14,10},{15,13... | collective-permute-start | bytes 589832 | tf_op jit(solution)/shard_map/ppermute | solution.py:33
  5.6 0.0 collective-permute-done.2.refs_1_
  5.6 1.6 %collective-permute-start.3 = (bf16[6,128,128]{2,1,0:T(8,128)(2,1)S(1)}, bf16[6,128,128]{2,1,0:T(8,128)(2,1)S(1)}, u32[]{:S(2)}, u32[]{:S(2)}) collective-permute-start(bf16[6,128,128]{2,1,0:T(8,128)(2,1)S(1)} %collective-permute-done.2.refs_1_), channel_id=1, source_target_pairs={{0,4},{1,3},{4,8},{5,1},{8,12},{9,5},{12,14},{13,9},{14,10},{15,13... | collective-permute-start | bytes 589832 | tf_op jit(solution)/shard_map/ppermute | solution.py:33
  7.2 2.0 %collective-permute-done.refs_2_ = bf16[6,128,128]{2,1,0:T(8,128)(2,1)S(1)} collective-permute-done((bf16[6,128,128]{2,1,0:T(8,128)(2,1)S(1)}, bf16[6,128,128]{2,1,0:T(8,128)(2,1)S(1)}, u32[]{:S(2)}, u32[]{:S(2)}) %collective-permute-start) | collective-permute-done | bytes 196640 | tf_op jit(solution)/shard_map/ppermute | solution.py:33
  9.2 2.1 %collective-permute-start.1 = (bf16[6,128,128]{2,1,0:T(8,128)(2,1)S(1)}, bf16[6,128,128]{2,1,0:T(8,128)(2,1)S(1)}, u32[]{:S(2)}, u32[]{:S(2)}) collective-permute-start(bf16[6,128,128]{2,1,0:T(8,128)(2,1)S(1)} %collective-permute-done.refs_2_), channel_id=1, source_target_pairs={{0,4},{1,3},{4,8},{5,1},{8,12},{9,5},{12,14},{13,9},{14,10},{15,13... | collective-permute-start | bytes 589832 | tf_op jit(solution)/shard_map/ppermute | solution.py:33
  11.3 0.0 collective-permute-done.3.refs_3_
  11.3 2.1 %collective-permute-start.4 = (bf16[6,128,128]{2,1,0:T(8,128)(2,1)S(1)}, bf16[6,128,128]{2,1,0:T(8,128)(2,1)S(1)}, u32[]{:S(2)}, u32[]{:S(2)}) collective-permute-start(bf16[6,128,128]{2,1,0:T(8,128)(2,1)S(1)} %collective-permute-done.3.refs_3_), channel_id=1, source_target_pairs={{0,4},{1,3},{4,8},{5,1},{8,12},{9,5},{12,14},{13,9},{14,10},{15,13... | collective-permute-start | bytes 589832 | tf_op jit(solution)/shard_map/ppermute | solution.py:33
  13.4 0.0 copy-start.2
  13.4 0.7 %copy-done.2 = s32[256,4]{0,1:T(4,128)S(1)} copy-done((s32[256,4]{0,1:T(4,128)S(1)}, s32[256,4]{0,1:T(4,128)}, u32[]{:S(2)}) %copy-start.2) | copy-done | bytes 4120
  14.1 3.4 %shard_map.68 = (s32[8,512]{1,0:T(8,128)S(1)}, bf16[256,128,128]{2,1,0:T(8,128)(2,1)S(1)}) custom-call(s32[4,256]{1,0:T(4,128)S(1)} %bitcast.1, bf16[256,128,128]{2,1,0:T(8,128)(2,1)} %left_ref.1), custom_call_target="tpu_custom_call" | custom-call | tf_op jit(solution)/shard_map/pallas_call | solution.py:177
  17.5 0.1 collective-permute-start.5
  17.6 0.0 collective-permute-done.1.refs_6_
  17.6 0.0 collective-permute-done.4.refs_7_
  17.6 1.6 %collective-permute-start.9 = (bf16[6,128,128]{2,1,0:T(8,128)(2,1)S(1)}, bf16[6,128,128]{2,1,0:T(8,128)(2,1)S(1)}, u32[]{:S(2)}, u32[]{:S(2)}) collective-permute-start(bf16[6,128,128]{2,1,0:T(8,128)(2,1)S(1)} %collective-permute-done.1.refs_6_), channel_id=1, source_target_pairs={{0,4},{1,3},{4,8},{5,1},{8,12},{9,5},{12,14},{13,9},{14,10},{15,13... | collective-permute-start | bytes 589832 | tf_op jit(solution)/shard_map/ppermute | solution.py:33
  19.2 0.0 collective-permute-start.6
  19.2 1.6 %collective-permute-start.10 = (bf16[6,128,128]{2,1,0:T(8,128)(2,1)S(1)}, bf16[6,128,128]{2,1,0:T(8,128)(2,1)S(1)}, u32[]{:S(2)}, u32[]{:S(2)}) collective-permute-start(bf16[6,128,128]{2,1,0:T(8,128)(2,1)S(1)} %collective-permute-done.4.refs_7_), channel_id=1, source_target_pairs={{0,4},{1,3},{4,8},{5,1},{8,12},{9,5},{12,14},{13,9},{14,10},{15,13... | collective-permute-start | bytes 589832 | tf_op jit(solution)/shard_map/ppermute | solution.py:33
  20.8 0.0 collective-permute-start.7
  20.8 0.0 collective-permute-done.5.refs_4_
  20.8 0.5 collective-permute-start.8
  21.3 2.0 %collective-permute-done.9.refs_10_ = bf16[6,128,128]{2,1,0:T(8,128)(2,1)S(1)} collective-permute-done((bf16[6,128,128]{2,1,0:T(8,128)(2,1)S(1)}, bf16[6,128,128]{2,1,0:T(8,128)(2,1)S(1)}, u32[]{:S(2)}, u32[]{:S(2)}) %collective-permute-start.9) | collective-permute-done | bytes 196640 | tf_op jit(solution)/shard_map/ppermute | solution.py:33
  23.3 1.6 %collective-permute-start.13 = (bf16[6,128,128]{2,1,0:T(8,128)(2,1)S(1)}, bf16[6,128,128]{2,1,0:T(8,128)(2,1)S(1)}, u32[]{:S(2)}, u32[]{:S(2)}) collective-permute-start(bf16[6,128,128]{2,1,0:T(8,128)(2,1)S(1)} %collective-permute-done.9.refs_10_), channel_id=1, source_target_pairs={{0,4},{1,3},{4,8},{5,1},{8,12},{9,5},{12,14},{13,9},{14,10},{15,13... | collective-permute-start | bytes 589832 | tf_op jit(solution)/shard_map/ppermute | solution.py:33
  24.9 0.0 collective-permute-done.6.refs_5_
  24.9 0.0 collective-permute-start.11
  24.9 0.5 collective-permute-done.10.refs_11_
  25.4 1.6 %collective-permute-start.14 = (bf16[6,128,128]{2,1,0:T(8,128)(2,1)S(1)}, bf16[6,128,128]{2,1,0:T(8,128)(2,1)S(1)}, u32[]{:S(2)}, u32[]{:S(2)}) collective-permute-start(bf16[6,128,128]{2,1,0:T(8,128)(2,1)S(1)} %collective-permute-done.10.refs_11_), channel_id=1, source_target_pairs={{0,4},{1,3},{4,8},{5,1},{8,12},{9,5},{12,14},{13,9},{14,10},{15,13... | collective-permute-start | bytes 589832 | tf_op jit(solution)/shard_map/ppermute | solution.py:33
  27.0 0.0 collective-permute-done.7.refs_8_
  27.0 0.0 collective-permute-start.12
  27.0 0.0 collective-permute-done.8.refs_9_
  27.0 2.0 %collective-permute-done.13.refs_14_ = bf16[6,128,128]{2,1,0:T(8,128)(2,1)S(1)} collective-permute-done((bf16[6,128,128]{2,1,0:T(8,128)(2,1)S(1)}, bf16[6,128,128]{2,1,0:T(8,128)(2,1)S(1)}, u32[]{:S(2)}, u32[]{:S(2)}) %collective-permute-start.13) | collective-permute-done | bytes 196640 | tf_op jit(solution)/shard_map/ppermute | solution.py:33
  29.0 0.0 collective-permute-done.11.refs_12_
  29.0 2.1 %collective-permute-done.14.refs_15_ = bf16[6,128,128]{2,1,0:T(8,128)(2,1)S(1)} collective-permute-done((bf16[6,128,128]{2,1,0:T(8,128)(2,1)S(1)}, bf16[6,128,128]{2,1,0:T(8,128)(2,1)S(1)}, u32[]{:S(2)}, u32[]{:S(2)}) %collective-permute-start.14) | collective-permute-done | bytes 196640 | tf_op jit(solution)/shard_map/ppermute | solution.py:33
  31.1 0.0 collective-permute-done.12.refs_13_
  31.1 10.2 %shard_map.69 = (bf16[2064,128]{1,0:T(8,128)(2,1)S(1)}, f32[8,256,128]{2,1,0:T(8,128)S(1)}, f32[8,128]{1,0:T(8,128)S(1)}) custom-call(s32[8,512]{1,0:T(8,128)S(1)} %get-tuple-element.42.plan_ref, bf16[256,128,128]{2,1,0:T(8,128)(2,1)S(1)} %get-tuple-element.43.left_ref, bf16[6,128,128]{2,1,0:T(8,128)(2,1)S(1)} %shard_map.67.refs_0_, ...), custom_call_target="tpu_custom_call" | custom-call | flops 4294967296 | bytes 15588608 | tf_op jit(solution)/shard_map/pallas_call | solution.py:339
  41.3 0.1 collective-permute-start.15
  41.4 1.9 %collective-permute-done.15.received_ref = bf16[2064,128]{1,0:T(8,128)(2,1)S(1)} collective-permute-done((bf16[2064,128]{1,0:T(8,128)(2,1)S(1)}, bf16[2064,128]{1,0:T(8,128)(2,1)S(1)}, u32[]{:S(2)}, u32[]{:S(2)}) %collective-permute-start.15) | collective-permute-done | bytes 528416 | tf_op jit(solution)/shard_map/ppermute | solution.py:19
  43.3 0.1 shard_map.70
  43.4 5.5 %collective-permute-start.16 = (bf16[272,128]{1,0:T(8,128)(2,1)S(1)}, bf16[272,128]{1,0:T(8,128)(2,1)S(1)}, u32[]{:S(2)}, u32[]{:S(2)}) collective-permute-start(bf16[272,128]{1,0:T(8,128)(2,1)S(1)} %get-tuple-element.52), channel_id=1, source_target_pairs={{0,14},{1,15},{2,12},{3,13},{4,10},{5,11},{6,8},{7,9},{8,6},{9,7},... | collective-permute-start | bytes 208904 | tf_op jit(solution)/shard_map/ppermute | solution.py:19
  48.8 3.2 %collective-permute-start.17 = (bf16[272,128]{1,0:T(8,128)(2,1)S(1)}, bf16[272,128]{1,0:T(8,128)(2,1)S(1)}, u32[]{:S(2)}, u32[]{:S(2)}) collective-permute-start(bf16[272,128]{1,0:T(8,128)(2,1)S(1)} %get-tuple-element.53), channel_id=1, source_target_pairs={{0,12},{1,13},{2,14},{3,15},{4,8},{5,9},{6,10},{7,11},{8,4},{9,5},... | collective-permute-start | bytes 208904 | tf_op jit(solution)/shard_map/ppermute | solution.py:19
  52.0 0.9 %collective-permute-start.18 = (bf16[272,128]{1,0:T(8,128)(2,1)S(1)}, bf16[272,128]{1,0:T(8,128)(2,1)S(1)}, u32[]{:S(2)}, u32[]{:S(2)}) collective-permute-start(bf16[272,128]{1,0:T(8,128)(2,1)S(1)} %get-tuple-element.54), channel_id=1, source_target_pairs={{0,10},{1,11},{2,8},{3,9},{4,14},{5,15},{6,12},{7,13},{8,2},{9,3},... | collective-permute-start | bytes 208904 | tf_op jit(solution)/shard_map/ppermute | solution.py:19
  52.9 0.0 collective-permute-start.19
  52.9 1.5 %collective-permute-start.20 = (bf16[272,128]{1,0:T(8,128)(2,1)S(1)}, bf16[272,128]{1,0:T(8,128)(2,1)S(1)}, u32[]{:S(2)}, u32[]{:S(2)}) collective-permute-start(bf16[272,128]{1,0:T(8,128)(2,1)S(1)} %get-tuple-element.56), channel_id=1, source_target_pairs={{0,6},{1,7},{2,4},{3,5},{4,2},{5,3},{6,0},{7,1},{8,14},{9,15},{10,... | collective-permute-start | bytes 208904 | tf_op jit(solution)/shard_map/ppermute | solution.py:19
  54.4 0.0 collective-permute-done.16.refs_0_
  54.4 3.4 %collective-permute-start.21 = (bf16[272,128]{1,0:T(8,128)(2,1)S(1)}, bf16[272,128]{1,0:T(8,128)(2,1)S(1)}, u32[]{:S(2)}, u32[]{:S(2)}) collective-permute-start(bf16[272,128]{1,0:T(8,128)(2,1)S(1)} %get-tuple-element.57), channel_id=1, source_target_pairs={{0,4},{1,5},{2,6},{3,7},{4,0},{5,1},{6,2},{7,3},{8,12},{9,13},{10,... | collective-permute-start | bytes 208904 | tf_op jit(solution)/shard_map/ppermute | solution.py:19
  57.9 0.0 collective-permute-done.17.refs_1_
  57.9 2.4 %collective-permute-start.22 = (bf16[272,128]{1,0:T(8,128)(2,1)S(1)}, bf16[272,128]{1,0:T(8,128)(2,1)S(1)}, u32[]{:S(2)}, u32[]{:S(2)}) collective-permute-start(bf16[272,128]{1,0:T(8,128)(2,1)S(1)} %get-tuple-element.58), channel_id=1, source_target_pairs={{0,2},{1,3},{2,0},{3,1},{4,6},{5,7},{6,4},{7,5},{8,10},{9,11},{10,... | collective-permute-start | bytes 208904 | tf_op jit(solution)/shard_map/ppermute | solution.py:19
  60.3 1.0 %shard_map.72 = f32[2,2]{1,0:T(2,128)} custom-call(bf16[6,128,128]{2,1,0:T(8,128)(2,1)S(1)} %shard_map.67.refs_0_, bf16[6,128,128]{2,1,0:T(8,128)(2,1)S(1)} %collective-permute-done.2.refs_1_, bf16[6,128,128]{2,1,0:T(8,128)(2,1)S(1)} %collective-permute-done.refs_2_, bf16[6,128,128]{2,1,0:T(8,128)(2,1)S(1)} %collective-permute-done.3.refs_3_, ...), custom_call_target="tpu_custom_call" | custom-call | tf_op jit(solution)/shard_map/pallas_call | solution.py:388
  61.3 0.0 collective-permute-done.18.refs_2_
  61.3 1.7 %collective-permute-done.19.refs_3_ = bf16[272,128]{1,0:T(8,128)(2,1)S(1)} collective-permute-done((bf16[272,128]{1,0:T(8,128)(2,1)S(1)}, bf16[272,128]{1,0:T(8,128)(2,1)S(1)}, u32[]{:S(2)}, u32[]{:S(2)}) %collective-permute-start.19) | collective-permute-done | bytes 69664 | tf_op jit(solution)/shard_map/ppermute | solution.py:19
  63.0 0.0 collective-permute-done.20.refs_4_
  63.0 0.9 %collective-permute-done.21.refs_5_ = bf16[272,128]{1,0:T(8,128)(2,1)S(1)} collective-permute-done((bf16[272,128]{1,0:T(8,128)(2,1)S(1)}, bf16[272,128]{1,0:T(8,128)(2,1)S(1)}, u32[]{:S(2)}, u32[]{:S(2)}) %collective-permute-start.21) | collective-permute-done | bytes 69664 | tf_op jit(solution)/shard_map/ppermute | solution.py:19
  63.9 0.0 collective-permute-done.22.refs_6_
  63.9 0.7 %shard_map.71 = (f32[1,2,128,128]{3,2,1,0:T(8,128)}, f32[2,2]{1,0:T(2,128)}) custom-call(f32[256,128]{1,0:T(8,128)S(1)} %get-tuple-element.50.mine_ref, f32[16,128]{1,0:T(8,128)S(1)} %get-tuple-element.51.total_ref, bf16[272,128]{1,0:T(8,128)(2,1)S(1)} %collective-permute-done.16.refs_0_, bf16[272,128]{1,0:T(8,128)(2,1)S(1)} %collective-permute-done.17.refs_1_, ...), custom_call_target="tpu_custom_call" | custom-call | tf_op jit(solution)/shard_map/pallas_call | solution.py:431
Async XLA Ops:
  0.6 0.9 %copy-start = (bf16[4,128,128]{2,1,0:T(8,128)(2,1)S(1)}, bf16[4,128,128]{2,1,0:T(8,128)(2,1)}, u32[]{:S(2)}) copy-start(bf16[4,128,128]{2,1,0:T(8,128)(2,1)} %right_ref.1) | copy-start | bytes 393220
  1.5 0.8 %copy-start.1 = (bf16[1,2,128,128]{3,2,1,0:T(8,128)(2,1)S(1)}, bf16[1,2,128,128]{3,2,1,0:T(8,128)(2,1)}, u32[]{:S(2)}) copy-start(bf16[1,2,128,128]{3,2,1,0:T(8,128)(2,1)} %trial_ref.1) | copy-start | bytes 196612
  2.5 3.2 %collective-permute-start.2 = (bf16[6,128,128]{2,1,0:T(8,128)(2,1)S(1)}, bf16[6,128,128]{2,1,0:T(8,128)(2,1)S(1)}, u32[]{:S(2)}, u32[]{:S(2)}) collective-permute-start(bf16[6,128,128]{2,1,0:T(8,128)(2,1)S(1)} %shard_map.67.refs_0_), channel_id=1, source_target_pairs={{0,1},{1,0},{2,3},{3,2},{4,5},{5,4},{6,7},{7,6},{8,9},{9,8},{10,11... | collective-permute-start | bytes 589832 | tf_op jit(solution)/shard_map/ppermute | solution.py:19
  3.0 6.2 %collective-permute-start = (bf16[6,128,128]{2,1,0:T(8,128)(2,1)S(1)}, bf16[6,128,128]{2,1,0:T(8,128)(2,1)S(1)}, u32[]{:S(2)}, u32[]{:S(2)}) collective-permute-start(bf16[6,128,128]{2,1,0:T(8,128)(2,1)S(1)} %shard_map.67.refs_0_), channel_id=1, source_target_pairs={{0,4},{1,3},{4,8},{5,1},{8,12},{9,5},{12,14},{13,9},{14,10},{15,13... | collective-permute-start | bytes 589832 | tf_op jit(solution)/shard_map/ppermute | solution.py:33
  5.6 5.7 %collective-permute-start.3 = (bf16[6,128,128]{2,1,0:T(8,128)(2,1)S(1)}, bf16[6,128,128]{2,1,0:T(8,128)(2,1)S(1)}, u32[]{:S(2)}, u32[]{:S(2)}) collective-permute-start(bf16[6,128,128]{2,1,0:T(8,128)(2,1)S(1)} %collective-permute-done.2.refs_1_), channel_id=1, source_target_pairs={{0,4},{1,3},{4,8},{5,1},{8,12},{9,5},{12,14},{13,9},{14,10},{15,13... | collective-permute-start | bytes 589832 | tf_op jit(solution)/shard_map/ppermute | solution.py:33
  9.2 8.4 %collective-permute-start.1 = (bf16[6,128,128]{2,1,0:T(8,128)(2,1)S(1)}, bf16[6,128,128]{2,1,0:T(8,128)(2,1)S(1)}, u32[]{:S(2)}, u32[]{:S(2)}) collective-permute-start(bf16[6,128,128]{2,1,0:T(8,128)(2,1)S(1)} %collective-permute-done.refs_2_), channel_id=1, source_target_pairs={{0,4},{1,3},{4,8},{5,1},{8,12},{9,5},{12,14},{13,9},{14,10},{15,13... | collective-permute-start | bytes 589832 | tf_op jit(solution)/shard_map/ppermute | solution.py:33
  11.3 6.3 %collective-permute-start.4 = (bf16[6,128,128]{2,1,0:T(8,128)(2,1)S(1)}, bf16[6,128,128]{2,1,0:T(8,128)(2,1)S(1)}, u32[]{:S(2)}, u32[]{:S(2)}) collective-permute-start(bf16[6,128,128]{2,1,0:T(8,128)(2,1)S(1)} %collective-permute-done.3.refs_3_), channel_id=1, source_target_pairs={{0,4},{1,3},{4,8},{5,1},{8,12},{9,5},{12,14},{13,9},{14,10},{15,13... | collective-permute-start | bytes 589832 | tf_op jit(solution)/shard_map/ppermute | solution.py:33
  13.4 0.7 %copy-start.2 = (s32[256,4]{0,1:T(4,128)S(1)}, s32[256,4]{0,1:T(4,128)}, u32[]{:S(2)}) copy-start(s32[256,4]{0,1:T(4,128)} %param.7) | copy-start | bytes 12292
  17.5 3.3 %collective-permute-start.5 = (bf16[6,128,128]{2,1,0:T(8,128)(2,1)S(1)}, bf16[6,128,128]{2,1,0:T(8,128)(2,1)S(1)}, u32[]{:S(2)}, u32[]{:S(2)}) collective-permute-start(bf16[6,128,128]{2,1,0:T(8,128)(2,1)S(1)} %collective-permute-done.refs_2_), channel_id=1, source_target_pairs={{0,1},{1,0},{2,3},{3,2},{4,5},{5,4},{6,7},{7,6},{8,9},{9,8},{10,11... | collective-permute-start | bytes 589832 | tf_op jit(solution)/shard_map/ppermute | solution.py:19
  17.6 5.7 %collective-permute-start.9 = (bf16[6,128,128]{2,1,0:T(8,128)(2,1)S(1)}, bf16[6,128,128]{2,1,0:T(8,128)(2,1)S(1)}, u32[]{:S(2)}, u32[]{:S(2)}) collective-permute-start(bf16[6,128,128]{2,1,0:T(8,128)(2,1)S(1)} %collective-permute-done.1.refs_6_), channel_id=1, source_target_pairs={{0,4},{1,3},{4,8},{5,1},{8,12},{9,5},{12,14},{13,9},{14,10},{15,13... | collective-permute-start | bytes 589832 | tf_op jit(solution)/shard_map/ppermute | solution.py:33
  19.2 5.7 %collective-permute-start.6 = (bf16[6,128,128]{2,1,0:T(8,128)(2,1)S(1)}, bf16[6,128,128]{2,1,0:T(8,128)(2,1)S(1)}, u32[]{:S(2)}, u32[]{:S(2)}) collective-permute-start(bf16[6,128,128]{2,1,0:T(8,128)(2,1)S(1)} %collective-permute-done.3.refs_3_), channel_id=1, source_target_pairs={{0,1},{1,0},{2,3},{3,2},{4,5},{5,4},{6,7},{7,6},{8,9},{9,8},{10,11... | collective-permute-start | bytes 589832 | tf_op jit(solution)/shard_map/ppermute | solution.py:19
  19.2 6.2 %collective-permute-start.10 = (bf16[6,128,128]{2,1,0:T(8,128)(2,1)S(1)}, bf16[6,128,128]{2,1,0:T(8,128)(2,1)S(1)}, u32[]{:S(2)}, u32[]{:S(2)}) collective-permute-start(bf16[6,128,128]{2,1,0:T(8,128)(2,1)S(1)} %collective-permute-done.4.refs_7_), channel_id=1, source_target_pairs={{0,4},{1,3},{4,8},{5,1},{8,12},{9,5},{12,14},{13,9},{14,10},{15,13... | collective-permute-start | bytes 589832 | tf_op jit(solution)/shard_map/ppermute | solution.py:33
  20.8 6.2 %collective-permute-start.7 = (bf16[6,128,128]{2,1,0:T(8,128)(2,1)S(1)}, bf16[6,128,128]{2,1,0:T(8,128)(2,1)S(1)}, u32[]{:S(2)}, u32[]{:S(2)}) collective-permute-start(bf16[6,128,128]{2,1,0:T(8,128)(2,1)S(1)} %collective-permute-done.1.refs_6_), channel_id=1, source_target_pairs={{0,1},{1,0},{2,3},{3,2},{4,5},{5,4},{6,7},{7,6},{8,9},{9,8},{10,11... | collective-permute-start | bytes 589832 | tf_op jit(solution)/shard_map/ppermute | solution.py:19
  20.8 6.2 %collective-permute-start.8 = (bf16[6,128,128]{2,1,0:T(8,128)(2,1)S(1)}, bf16[6,128,128]{2,1,0:T(8,128)(2,1)S(1)}, u32[]{:S(2)}, u32[]{:S(2)}) collective-permute-start(bf16[6,128,128]{2,1,0:T(8,128)(2,1)S(1)} %collective-permute-done.4.refs_7_), channel_id=1, source_target_pairs={{0,1},{1,0},{2,3},{3,2},{4,5},{5,4},{6,7},{7,6},{8,9},{9,8},{10,11... | collective-permute-start | bytes 589832 | tf_op jit(solution)/shard_map/ppermute | solution.py:19
  23.3 5.7 %collective-permute-start.13 = (bf16[6,128,128]{2,1,0:T(8,128)(2,1)S(1)}, bf16[6,128,128]{2,1,0:T(8,128)(2,1)S(1)}, u32[]{:S(2)}, u32[]{:S(2)}) collective-permute-start(bf16[6,128,128]{2,1,0:T(8,128)(2,1)S(1)} %collective-permute-done.9.refs_10_), channel_id=1, source_target_pairs={{0,4},{1,3},{4,8},{5,1},{8,12},{9,5},{12,14},{13,9},{14,10},{15,13... | collective-permute-start | bytes 589832 | tf_op jit(solution)/shard_map/ppermute | solution.py:33
  24.9 4.1 %collective-permute-start.11 = (bf16[6,128,128]{2,1,0:T(8,128)(2,1)S(1)}, bf16[6,128,128]{2,1,0:T(8,128)(2,1)S(1)}, u32[]{:S(2)}, u32[]{:S(2)}) collective-permute-start(bf16[6,128,128]{2,1,0:T(8,128)(2,1)S(1)} %collective-permute-done.9.refs_10_), channel_id=1, source_target_pairs={{0,1},{1,0},{2,3},{3,2},{4,5},{5,4},{6,7},{7,6},{8,9},{9,8},{10,11... | collective-permute-start | bytes 589832 | tf_op jit(solution)/shard_map/ppermute | solution.py:19
  25.4 5.7 %collective-permute-start.14 = (bf16[6,128,128]{2,1,0:T(8,128)(2,1)S(1)}, bf16[6,128,128]{2,1,0:T(8,128)(2,1)S(1)}, u32[]{:S(2)}, u32[]{:S(2)}) collective-permute-start(bf16[6,128,128]{2,1,0:T(8,128)(2,1)S(1)} %collective-permute-done.10.refs_11_), channel_id=1, source_target_pairs={{0,4},{1,3},{4,8},{5,1},{8,12},{9,5},{12,14},{13,9},{14,10},{15,13... | collective-permute-start | bytes 589832 | tf_op jit(solution)/shard_map/ppermute | solution.py:33
  27.0 4.1 %collective-permute-start.12 = (bf16[6,128,128]{2,1,0:T(8,128)(2,1)S(1)}, bf16[6,128,128]{2,1,0:T(8,128)(2,1)S(1)}, u32[]{:S(2)}, u32[]{:S(2)}) collective-permute-start(bf16[6,128,128]{2,1,0:T(8,128)(2,1)S(1)} %collective-permute-done.10.refs_11_), channel_id=1, source_target_pairs={{0,1},{1,0},{2,3},{3,2},{4,5},{5,4},{6,7},{7,6},{8,9},{9,8},{10,11... | collective-permute-start | bytes 589832 | tf_op jit(solution)/shard_map/ppermute | solution.py:19
  41.3 2.0 %collective-permute-start.15 = (bf16[2064,128]{1,0:T(8,128)(2,1)S(1)}, bf16[2064,128]{1,0:T(8,128)(2,1)S(1)}, u32[]{:S(2)}, u32[]{:S(2)}) collective-permute-start(bf16[2064,128]{1,0:T(8,128)(2,1)S(1)} %get-tuple-element.49), channel_id=1, source_target_pairs={{0,1},{1,0},{2,3},{3,2},{4,5},{5,4},{6,7},{7,6},{8,9},{9,8},{10,11... | collective-permute-start | bytes 1585160 | tf_op jit(solution)/shard_map/ppermute | solution.py:19
  43.4 11.1 %collective-permute-start.16 = (bf16[272,128]{1,0:T(8,128)(2,1)S(1)}, bf16[272,128]{1,0:T(8,128)(2,1)S(1)}, u32[]{:S(2)}, u32[]{:S(2)}) collective-permute-start(bf16[272,128]{1,0:T(8,128)(2,1)S(1)} %get-tuple-element.52), channel_id=1, source_target_pairs={{0,14},{1,15},{2,12},{3,13},{4,10},{5,11},{6,8},{7,9},{8,6},{9,7},... | collective-permute-start | bytes 208904 | tf_op jit(solution)/shard_map/ppermute | solution.py:19
  48.8 9.0 %collective-permute-start.17 = (bf16[272,128]{1,0:T(8,128)(2,1)S(1)}, bf16[272,128]{1,0:T(8,128)(2,1)S(1)}, u32[]{:S(2)}, u32[]{:S(2)}) collective-permute-start(bf16[272,128]{1,0:T(8,128)(2,1)S(1)} %get-tuple-element.53), channel_id=1, source_target_pairs={{0,12},{1,13},{2,14},{3,15},{4,8},{5,9},{6,10},{7,11},{8,4},{9,5},... | collective-permute-start | bytes 208904 | tf_op jit(solution)/shard_map/ppermute | solution.py:19
  52.0 9.3 %collective-permute-start.18 = (bf16[272,128]{1,0:T(8,128)(2,1)S(1)}, bf16[272,128]{1,0:T(8,128)(2,1)S(1)}, u32[]{:S(2)}, u32[]{:S(2)}) collective-permute-start(bf16[272,128]{1,0:T(8,128)(2,1)S(1)} %get-tuple-element.54), channel_id=1, source_target_pairs={{0,10},{1,11},{2,8},{3,9},{4,14},{5,15},{6,12},{7,13},{8,2},{9,3},... | collective-permute-start | bytes 208904 | tf_op jit(solution)/shard_map/ppermute | solution.py:19
  52.9 10.1 %collective-permute-start.19 = (bf16[272,128]{1,0:T(8,128)(2,1)S(1)}, bf16[272,128]{1,0:T(8,128)(2,1)S(1)}, u32[]{:S(2)}, u32[]{:S(2)}) collective-permute-start(bf16[272,128]{1,0:T(8,128)(2,1)S(1)} %get-tuple-element.55), channel_id=1, source_target_pairs={{0,8},{1,9},{2,10},{3,11},{4,12},{5,13},{6,14},{7,15},{8,0},{9,1},... | collective-permute-start | bytes 208904 | tf_op jit(solution)/shard_map/ppermute | solution.py:19
  52.9 10.1 %collective-permute-start.20 = (bf16[272,128]{1,0:T(8,128)(2,1)S(1)}, bf16[272,128]{1,0:T(8,128)(2,1)S(1)}, u32[]{:S(2)}, u32[]{:S(2)}) collective-permute-start(bf16[272,128]{1,0:T(8,128)(2,1)S(1)} %get-tuple-element.56), channel_id=1, source_target_pairs={{0,6},{1,7},{2,4},{3,5},{4,2},{5,3},{6,0},{7,1},{8,14},{9,15},{10,... | collective-permute-start | bytes 208904 | tf_op jit(solution)/shard_map/ppermute | solution.py:19
  54.4 9.4 %collective-permute-start.21 = (bf16[272,128]{1,0:T(8,128)(2,1)S(1)}, bf16[272,128]{1,0:T(8,128)(2,1)S(1)}, u32[]{:S(2)}, u32[]{:S(2)}) collective-permute-start(bf16[272,128]{1,0:T(8,128)(2,1)S(1)} %get-tuple-element.57), channel_id=1, source_target_pairs={{0,4},{1,5},{2,6},{3,7},{4,0},{5,1},{6,2},{7,3},{8,12},{9,13},{10,... | collective-permute-start | bytes 208904 | tf_op jit(solution)/shard_map/ppermute | solution.py:19
  57.9 6.0 %collective-permute-start.22 = (bf16[272,128]{1,0:T(8,128)(2,1)S(1)}, bf16[272,128]{1,0:T(8,128)(2,1)S(1)}, u32[]{:S(2)}, u32[]{:S(2)}) collective-permute-start(bf16[272,128]{1,0:T(8,128)(2,1)S(1)} %get-tuple-element.58), channel_id=1, source_target_pairs={{0,2},{1,3},{2,0},{3,1},{4,6},{5,7},{6,4},{7,5},{8,10},{9,11},{10,... | collective-permute-start | bytes 208904 | tf_op jit(solution)/shard_map/ppermute | solution.py:19

commit v9 on v8

--- a/solution.py
+++ b/solution.py
@@ -91,13 +91,6 @@
 def place_of(chip, chips):
     half = jnp.floor(chip * 0.5)
     return jnp.where(chip == 2.0 * half, half, chips - 1.0 - half)
-
-
-def stage_kernel(n, terms, tasks_ref, left_ref, plan_ref, held_ref, sem):
-    copy = pltpu.make_async_copy(left_ref, held_ref, sem)
-    copy.start()
-    plan_kernel(n, terms, tasks_ref, plan_ref)
-    copy.wait()
 
 
 def plan_kernel(n, terms, tasks_ref, plan_ref):
@@ -169,27 +162,32 @@
     plan_ref[6:8] = jnp.zeros((2, places), jnp.int32)
 
 
-def make_plan(tasks, left_ops, n, terms):
+def make_plan(tasks, n, terms):
     most = source_places(tasks.shape[1], n) + 2 * PAIRS
-    plan = jax.ShapeDtypeStruct((8, -(-most // 128) * 128), jnp.int32)
-    vmem = pl.BlockSpec(memory_space=pltpu.VMEM)
-    if fits(n):
-        return pl.pallas_call(
-            functools.partial(stage_kernel, n, terms),
-            in_specs=[vmem, pl.BlockSpec(memory_space=pltpu.HBM)],
-            out_specs=(vmem, vmem),
-            out_shape=(plan, jax.ShapeDtypeStruct(left_ops.shape, left_ops.dtype)),
-            scratch_shapes=[pltpu.SemaphoreType.DMA],
-            compiler_params=pltpu.CompilerParams(vmem_limit_bytes=42 * MIB),
-        )(tasks, left_ops)
-    return (
-        pl.pallas_call(
-            functools.partial(plan_kernel, n, terms),
-            out_shape=plan,
-            compiler_params=pltpu.CompilerParams(vmem_limit_bytes=16 * MIB),
-        )(tasks),
-        left_ops,
-    )
+    return pl.pallas_call(
+        functools.partial(plan_kernel, n, terms),
+        out_shape=jax.ShapeDtypeStruct((8, -(-most // 128) * 128), jnp.int32),
+        compiler_params=pltpu.CompilerParams(vmem_limit_bytes=16 * MIB),
+    )(tasks)
+
+
+def stage_kernel(left_ref, held_ref, sem):
+    copy = pltpu.make_async_copy(left_ref, held_ref, sem)
+    copy.start()
+    copy.wait()
+
+
+def stage(left_ops, n):
+    if not fits(n):
+        return left_ops
+    return pl.pallas_call(
+        stage_kernel,
+        in_specs=[pl.BlockSpec(memory_space=pltpu.HBM)],
+        out_specs=pl.BlockSpec(memory_space=pltpu.VMEM),
+        out_shape=jax.ShapeDtypeStruct(left_ops.shape, left_ops.dtype),
+        scratch_shapes=[pltpu.SemaphoreType.DMA],
+        compiler_params=pltpu.CompilerParams(vmem_limit_bytes=42 * MIB),
+    )(left_ops)
 
 
 def block_copies(n, kinds, blocks, trial, right, sem, which):
@@ -360,17 +358,28 @@
     )(plan, left_ops, *[block[0] for block in blocks])
 
 
-def join_kernel(trial_ref, right_ref, block_ref):
-    block_ref[0:TRIALS] = trial_ref[0]
-    for k in range(right_ref.shape[0]):
-        block_ref[TRIALS + k] = jnp.transpose(right_ref[k])
+def join_kernel(trial_ref, right_ref, block_ref, right, sem):
+    copies = [
+        pltpu.make_async_copy(right_ref, right, sem.at[0]),
+        pltpu.make_async_copy(trial_ref.at[0], block_ref.at[pl.ds(0, TRIALS)], sem.at[1]),
+    ]
+    for copy in copies:
+        copy.start()
+    copies[0].wait()
+    for k in range(right.shape[0]):
+        block_ref[TRIALS + k] = jnp.transpose(right[k])
+    copies[1].wait()
 
 
 def join(trial, right_ops):
+    hbm = pl.BlockSpec(memory_space=pltpu.HBM)
     return pl.pallas_call(
         join_kernel,
         out_shape=jax.ShapeDtypeStruct((TRIALS + right_ops.shape[0], 128, 128), jnp.bfloat16),
-        compiler_params=pltpu.CompilerParams(vmem_limit_bytes=16 * MIB),
+        in_specs=[hbm, hbm],
+        out_specs=pl.BlockSpec(memory_space=pltpu.VMEM),
+        scratch_shapes=[pltpu.VMEM(right_ops.shape, jnp.bfloat16), pltpu.SemaphoreType.DMA((2,))],
+        compiler_params=pltpu.CompilerParams(vmem_limit_bytes=59 * MIB),
     )(trial, right_ops)
 
 
@@ -441,12 +450,13 @@
 def body(n, trial, left_ops, right_ops, task_list):
     steps = n // 4
     own = join(trial, right_ops)
-    plan, left_ops = make_plan(task_list.T, left_ops, n, n * right_ops.shape[0])
+    plan = make_plan(task_list.T, n, n * right_ops.shape[0])
+    left_ops = stage(left_ops, n)
     lines = [own, exchange(own, n, 1)]
     blocks = [(value, 0, False, half) for half, value in enumerate(lines)]
     for step in range(1, steps + 1):
-        if step == steps // 2 + 1:
-            lines, plan, left_ops = lax.optimization_barrier((lines, plan, left_ops))
+        if step == 2:
+            lines[0], plan = lax.optimization_barrier((lines[0], plan))
         for half in range(2):
             lines[half] = ring_step(lines[half], n)
             blocks.append((lines[half], step, False, half))

time: 64.8 us -> 62.5 us (0.965)
  Pallas kernels: 15.5 us -> 21 us
  waiting for transfers between devices: 13.1 us -> 8.32 us
  local copies, waits for them, and re-layouts: 2.42 us -> 0.69 us
  starting transfers between devices: 32.8 us -> 32 us
    ppermute x8, waiting for transfers between devices: 8.64 us -> 3.26 us  [ring_step(): return lax.ppermute(value, 'op', pairs)]
    pallas_call x1, Pallas kernels: 10.2 us -> 13.1 us  [run_tasks(): pl.pallas_call(functools.partial(tasks_kernel, n, kinds), out_shape=(jax....]
    ppermute x15, starting transfers between devices: 18.1 us -> 15.4 us  [exchange(): return lax.ppermute(value, 'op', [(i, i ^ mask) for i in range(n)])]
    ppermute x8, starting transfers between devices: 14.7 us -> 16.7 us  [ring_step(): return lax.ppermute(value, 'op', pairs)]
    unnamed x6 -> x4, local copies, waits for them, and re-layouts: 2.42 us -> 0.69 us
    pallas_call x1, Pallas kernels: 0.08 us -> 1.68 us  [join(): pl.pallas_call(join_kernel, out_shape=jax.ShapeDtypeStruct((TRIALS + righ...]
    pallas_call x1 -> x2, Pallas kernels: 3.39 us -> 4.37 us  [the longest x1 3.39 us: stage(): pl.pallas_call(stage_kernel, in_specs=[pl.BlockSpec(memory_space=pltpu.HB...]
  transfers between devices with their start and end apart: 23 -> 23, of which waited for: 8 -> 8; matrix products, arithmetic and copies ran while one was open for 0% -> 0% of each run, Pallas kernels for 7% -> 9%
where the time goes in v9:
time: 62.5 us; the launch traced here: 62.7 us
  starting transfers between devices  32 us (51%)
  Pallas kernels  21 us (34%)
  waiting for transfers between devices  8.32 us (13%)
  between operations  0.72 us (1%)
  local copies, waits for them, and re-layouts  0.69 us (1%)
    ppermute x8, starting transfers between devices, ring_step(): return lax.ppermute(value, 'op', pairs)  16.7 us
    ppermute x15, starting transfers between devices, exchange(): return lax.ppermute(value, 'op', [(i, i ^ mask) for i in range(n)])  15.4 us
    pallas_call x1, Pallas kernels, run_tasks(): pl.pallas_call(functools.partial(tasks_kernel, n, kinds), out_shape=(jax....  13.1 us
    ppermute x15, waiting for transfers between devices, exchange(): return lax.ppermute(value, 'op', [(i, i ^ mask) for i in range(n)])  5.06 us
    pallas_call x1, Pallas kernels, stage(): pl.pallas_call(stage_kernel, in_specs=[pl.BlockSpec(memory_space=pltpu.HB...  3.39 us
    ppermute x8, waiting for transfers between devices, ring_step(): return lax.ppermute(value, 'op', pairs)  3.26 us
    pallas_call x1, Pallas kernels, join(): pl.pallas_call(join_kernel, out_shape=jax.ShapeDtypeStruct((TRIALS + righ...  1.68 us
  transfers between devices with their start and end apart: 23, of which 8 were waited for; matrix products, arithmetic and copies ran while one was open for 0% of the time, Pallas kernels for 9%

profile of v9, /device:TPU:0, one launch (start us, length us, event | category | flops | bytes accessed | tf_op | source)
XLA Modules:
  0.0 62.7 jit_solution(10566686513253982727)
XLA Ops:
  0.6 1.7 %shard_map.67.refs_0_ = bf16[6,128,128]{2,1,0:T(8,128)(2,1)} custom-call(bf16[1,2,128,128]{3,2,1,0:T(8,128)(2,1)} %trial_ref.1, bf16[4,128,128]{2,1,0:T(8,128)(2,1)} %right_ref.1), custom_call_target="tpu_custom_call" | custom-call | tf_op jit(solution)/shard_map/pallas_call | solution.py:376
  2.3 0.5 collective-permute-start.1
  2.8 2.6 %collective-permute-start = (bf16[6,128,128]{2,1,0:T(8,128)(2,1)}, bf16[6,128,128]{2,1,0:T(8,128)(2,1)S(1)}, u32[]{:S(2)}, u32[]{:S(2)}) collective-permute-start(bf16[6,128,128]{2,1,0:T(8,128)(2,1)} %shard_map.67.refs_0_), channel_id=1, source_target_pairs={{0,4},{1,3},{4,8},{5,1},{8,12},{9,5},{12,14},{13,9},{14,10},{15,13... | collective-permute-start | bytes 589832 | tf_op jit(solution)/shard_map/ppermute | solution.py:33
  5.5 0.0 collective-permute-done.1.refs_1_
  5.5 1.6 %collective-permute-start.2 = (bf16[6,128,128]{2,1,0:T(8,128)(2,1)S(1)}, bf16[6,128,128]{2,1,0:T(8,128)(2,1)S(1)}, u32[]{:S(2)}, u32[]{:S(2)}) collective-permute-start(bf16[6,128,128]{2,1,0:T(8,128)(2,1)S(1)} %collective-permute-done.1.refs_1_), channel_id=1, source_target_pairs={{0,4},{1,3},{4,8},{5,1},{8,12},{9,5},{12,14},{13,9},{14,10},{15,13... | collective-permute-start | bytes 589832 | tf_op jit(solution)/shard_map/ppermute | solution.py:33
  7.1 0.0 copy-start.1
  7.1 0.7 %copy-done.1 = s32[256,4]{0,1:T(4,128)S(1)} copy-done((s32[256,4]{0,1:T(4,128)S(1)}, s32[256,4]{0,1:T(4,128)}, u32[]{:S(2)}) %copy-start.1) | copy-done | bytes 4120
  7.8 1.0 %shard_map.68.plan_ref = s32[8,512]{1,0:T(8,128)S(1)} custom-call(s32[4,256]{1,0:T(4,128)S(1)} %bitcast.1), custom_call_target="tpu_custom_call" | custom-call | tf_op jit(solution)/shard_map/pallas_call | solution.py:167
  8.7 0.0 copy-start
  8.7 0.5 collective-permute-done.refs_2_
  9.3 2.1 %collective-permute-start.5 = (bf16[6,128,128]{2,1,0:T(8,128)(2,1)S(1)}, bf16[6,128,128]{2,1,0:T(8,128)(2,1)S(1)}, u32[]{:S(2)}, u32[]{:S(2)}) collective-permute-start(bf16[6,128,128]{2,1,0:T(8,128)(2,1)S(1)} %collective-permute-done.refs_2_), channel_id=1, source_target_pairs={{0,4},{1,3},{4,8},{5,1},{8,12},{9,5},{12,14},{13,9},{14,10},{15,13... | collective-permute-start | bytes 589832 | tf_op jit(solution)/shard_map/ppermute | solution.py:33
  11.4 0.0 collective-permute-done.2.refs_3_
  11.4 2.1 %collective-permute-start.6 = (bf16[6,128,128]{2,1,0:T(8,128)(2,1)S(1)}, bf16[6,128,128]{2,1,0:T(8,128)(2,1)S(1)}, u32[]{:S(2)}, u32[]{:S(2)}) collective-permute-start(bf16[6,128,128]{2,1,0:T(8,128)(2,1)S(1)} %collective-permute-done.2.refs_3_), channel_id=1, source_target_pairs={{0,4},{1,3},{4,8},{5,1},{8,12},{9,5},{12,14},{13,9},{14,10},{15,13... | collective-permute-start | bytes 589832 | tf_op jit(solution)/shard_map/ppermute | solution.py:33
  13.5 0.0 collective-permute-start.3
  13.5 1.5 %collective-permute-done.5.refs_6_ = bf16[6,128,128]{2,1,0:T(8,128)(2,1)S(1)} collective-permute-done((bf16[6,128,128]{2,1,0:T(8,128)(2,1)S(1)}, bf16[6,128,128]{2,1,0:T(8,128)(2,1)S(1)}, u32[]{:S(2)}, u32[]{:S(2)}) %collective-permute-start.5) | collective-permute-done | bytes 196640 | tf_op jit(solution)/shard_map/ppermute | solution.py:33
  14.9 2.1 %collective-permute-start.9 = (bf16[6,128,128]{2,1,0:T(8,128)(2,1)S(1)}, bf16[6,128,128]{2,1,0:T(8,128)(2,1)S(1)}, u32[]{:S(2)}, u32[]{:S(2)}) collective-permute-start(bf16[6,128,128]{2,1,0:T(8,128)(2,1)S(1)} %collective-permute-done.5.refs_6_), channel_id=1, source_target_pairs={{0,4},{1,3},{4,8},{5,1},{8,12},{9,5},{12,14},{13,9},{14,10},{15,13... | collective-permute-start | bytes 589832 | tf_op jit(solution)/shard_map/ppermute | solution.py:33
  17.0 0.0 collective-permute-start.4
  17.0 0.0 collective-permute-done.6.refs_7_
  17.1 2.1 %collective-permute-start.10 = (bf16[6,128,128]{2,1,0:T(8,128)(2,1)S(1)}, bf16[6,128,128]{2,1,0:T(8,128)(2,1)S(1)}, u32[]{:S(2)}, u32[]{:S(2)}) collective-permute-start(bf16[6,128,128]{2,1,0:T(8,128)(2,1)S(1)} %collective-permute-done.6.refs_7_), channel_id=1, source_target_pairs={{0,4},{1,3},{4,8},{5,1},{8,12},{9,5},{12,14},{13,9},{14,10},{15,13... | collective-permute-start | bytes 589832 | tf_op jit(solution)/shard_map/ppermute | solution.py:33
  19.1 0.0 collective-permute-start.7
  19.1 0.0 collective-permute-done.3.refs_4_
  19.1 0.5 collective-permute-start.8
  19.6 1.0 %collective-permute-done.9.refs_10_ = bf16[6,128,128]{2,1,0:T(8,128)(2,1)S(1)} collective-permute-done((bf16[6,128,128]{2,1,0:T(8,128)(2,1)S(1)}, bf16[6,128,128]{2,1,0:T(8,128)(2,1)S(1)}, u32[]{:S(2)}, u32[]{:S(2)}) %collective-permute-start.9) | collective-permute-done | bytes 196640 | tf_op jit(solution)/shard_map/ppermute | solution.py:33
  20.6 2.1 %collective-permute-start.13 = (bf16[6,128,128]{2,1,0:T(8,128)(2,1)S(1)}, bf16[6,128,128]{2,1,0:T(8,128)(2,1)S(1)}, u32[]{:S(2)}, u32[]{:S(2)}) collective-permute-start(bf16[6,128,128]{2,1,0:T(8,128)(2,1)S(1)} %collective-permute-done.9.refs_10_), channel_id=1, source_target_pairs={{0,4},{1,3},{4,8},{5,1},{8,12},{9,5},{12,14},{13,9},{14,10},{15,13... | collective-permute-start | bytes 589832 | tf_op jit(solution)/shard_map/ppermute | solution.py:33
  22.7 0.0 collective-permute-done.4.refs_5_
  22.7 0.0 collective-permute-start.11
  22.7 0.0 collective-permute-done.10.refs_11_
  22.7 2.1 %collective-permute-start.14 = (bf16[6,128,128]{2,1,0:T(8,128)(2,1)S(1)}, bf16[6,128,128]{2,1,0:T(8,128)(2,1)S(1)}, u32[]{:S(2)}, u32[]{:S(2)}) collective-permute-start(bf16[6,128,128]{2,1,0:T(8,128)(2,1)S(1)} %collective-permute-done.10.refs_11_), channel_id=1, source_target_pairs={{0,4},{1,3},{4,8},{5,1},{8,12},{9,5},{12,14},{13,9},{14,10},{15,13... | collective-permute-start | bytes 589832 | tf_op jit(solution)/shard_map/ppermute | solution.py:33
  24.8 0.0 collective-permute-done.7.refs_8_
  24.8 0.0 collective-permute-start.12
  24.8 3.4 %shard_map.69.left_ref = bf16[256,128,128]{2,1,0:T(8,128)(2,1)S(1)} custom-call(bf16[256,128,128]{2,1,0:T(8,128)(2,1)} %left_ref.1), custom_call_target="tpu_custom_call" | custom-call | tf_op jit(solution)/shard_map/pallas_call | solution.py:183
  28.2 0.0 collective-permute-done.8.refs_9_
  28.2 0.0 collective-permute-done.13.refs_14_
  28.2 0.0 collective-permute-done.11.refs_12_
  28.2 0.2 collective-permute-done.14.refs_15_
  28.4 0.0 collective-permute-done.12.refs_13_
  28.4 0.0 copy-done
  28.4 13.1 %shard_map.70 = (bf16[2064,128]{1,0:T(8,128)(2,1)S(1)}, f32[8,256,128]{2,1,0:T(8,128)S(1)}, f32[8,128]{1,0:T(8,128)S(1)}) custom-call(s32[8,512]{1,0:T(8,128)S(1)} %shard_map.68.plan_ref, bf16[256,128,128]{2,1,0:T(8,128)(2,1)S(1)} %shard_map.69.left_ref, bf16[6,128,128]{2,1,0:T(8,128)(2,1)S(1)} %copy-done, ...), custom_call_target="tpu_custom_call" | custom-call | flops 4294967296 | bytes 15588608 | tf_op jit(solution)/shard_map/pallas_call | solution.py:337
  41.5 1.4 %collective-permute-start.15 = (bf16[2064,128]{1,0:T(8,128)(2,1)S(1)}, bf16[2064,128]{1,0:T(8,128)(2,1)S(1)}, u32[]{:S(2)}, u32[]{:S(2)}) collective-permute-start(bf16[2064,128]{1,0:T(8,128)(2,1)S(1)} %get-tuple-element.41), channel_id=1, source_target_pairs={{0,1},{1,0},{2,3},{3,2},{4,5},{5,4},{6,7},{7,6},{8,9},{9,8},{10,11... | collective-permute-start | bytes 1585160 | tf_op jit(solution)/shard_map/ppermute | solution.py:19
  42.9 1.5 %collective-permute-done.15.received_ref = bf16[2064,128]{1,0:T(8,128)(2,1)S(1)} collective-permute-done((bf16[2064,128]{1,0:T(8,128)(2,1)S(1)}, bf16[2064,128]{1,0:T(8,128)(2,1)S(1)}, u32[]{:S(2)}, u32[]{:S(2)}) %collective-permute-start.15) | collective-permute-done | bytes 528416 | tf_op jit(solution)/shard_map/ppermute | solution.py:19
  44.5 0.1 shard_map.71
  44.6 3.1 %collective-permute-start.16 = (bf16[272,128]{1,0:T(8,128)(2,1)S(1)}, bf16[272,128]{1,0:T(8,128)(2,1)S(1)}, u32[]{:S(2)}, u32[]{:S(2)}) collective-permute-start(bf16[272,128]{1,0:T(8,128)(2,1)S(1)} %get-tuple-element.44), channel_id=1, source_target_pairs={{0,14},{1,15},{2,12},{3,13},{4,10},{5,11},{6,8},{7,9},{8,6},{9,7},... | collective-permute-start | bytes 208904 | tf_op jit(solution)/shard_map/ppermute | solution.py:19
  47.7 0.2 collective-permute-start.17
  48.0 3.7 %collective-permute-start.18 = (bf16[272,128]{1,0:T(8,128)(2,1)S(1)}, bf16[272,128]{1,0:T(8,128)(2,1)S(1)}, u32[]{:S(2)}, u32[]{:S(2)}) collective-permute-start(bf16[272,128]{1,0:T(8,128)(2,1)S(1)} %get-tuple-element.46), channel_id=1, source_target_pairs={{0,10},{1,11},{2,8},{3,9},{4,14},{5,15},{6,12},{7,13},{8,2},{9,3},... | collective-permute-start | bytes 208904 | tf_op jit(solution)/shard_map/ppermute | solution.py:19
  51.6 0.7 %collective-permute-start.19 = (bf16[272,128]{1,0:T(8,128)(2,1)S(1)}, bf16[272,128]{1,0:T(8,128)(2,1)S(1)}, u32[]{:S(2)}, u32[]{:S(2)}) collective-permute-start(bf16[272,128]{1,0:T(8,128)(2,1)S(1)} %get-tuple-element.47), channel_id=1, source_target_pairs={{0,8},{1,9},{2,10},{3,11},{4,12},{5,13},{6,14},{7,15},{8,0},{9,1},... | collective-permute-start | bytes 208904 | tf_op jit(solution)/shard_map/ppermute | solution.py:19
  52.3 0.9 %collective-permute-start.20 = (bf16[272,128]{1,0:T(8,128)(2,1)S(1)}, bf16[272,128]{1,0:T(8,128)(2,1)S(1)}, u32[]{:S(2)}, u32[]{:S(2)}) collective-permute-start(bf16[272,128]{1,0:T(8,128)(2,1)S(1)} %get-tuple-element.48), channel_id=1, source_target_pairs={{0,6},{1,7},{2,4},{3,5},{4,2},{5,3},{6,0},{7,1},{8,14},{9,15},{10,... | collective-permute-start | bytes 208904 | tf_op jit(solution)/shard_map/ppermute | solution.py:19
  53.2 0.0 collective-permute-done.16.refs_0_
  53.2 4.3 %collective-permute-start.21 = (bf16[272,128]{1,0:T(8,128)(2,1)S(1)}, bf16[272,128]{1,0:T(8,128)(2,1)S(1)}, u32[]{:S(2)}, u32[]{:S(2)}) collective-permute-start(bf16[272,128]{1,0:T(8,128)(2,1)S(1)} %get-tuple-element.49), channel_id=1, source_target_pairs={{0,4},{1,5},{2,6},{3,7},{4,0},{5,1},{6,2},{7,3},{8,12},{9,13},{10,... | collective-permute-start | bytes 208904 | tf_op jit(solution)/shard_map/ppermute | solution.py:19
  57.4 0.0 collective-permute-done.17.refs_1_
  57.4 0.1 collective-permute-start.22
  57.5 1.0 %shard_map.73 = f32[2,2]{1,0:T(2,128)} custom-call(bf16[6,128,128]{2,1,0:T(8,128)(2,1)S(1)} %copy-done, bf16[6,128,128]{2,1,0:T(8,128)(2,1)S(1)} %collective-permute-done.1.refs_1_, bf16[6,128,128]{2,1,0:T(8,128)(2,1)S(1)} %collective-permute-done.refs_2_, bf16[6,128,128]{2,1,0:T(8,128)(2,1)S(1)} %collective-permute-done.2.refs_3_, ...), custom_call_target="tpu_custom_call" | custom-call | tf_op jit(solution)/shard_map/pallas_call | solution.py:397
  58.5 2.2 %collective-permute-done.18.refs_2_ = bf16[272,128]{1,0:T(8,128)(2,1)S(1)} collective-permute-done((bf16[272,128]{1,0:T(8,128)(2,1)S(1)}, bf16[272,128]{1,0:T(8,128)(2,1)S(1)}, u32[]{:S(2)}, u32[]{:S(2)}) %collective-permute-start.18) | collective-permute-done | bytes 69664 | tf_op jit(solution)/shard_map/ppermute | solution.py:19
  60.7 0.1 collective-permute-done.19.refs_3_
  60.8 0.0 collective-permute-done.20.refs_4_
  60.8 1.2 %collective-permute-done.21.refs_5_ = bf16[272,128]{1,0:T(8,128)(2,1)S(1)} collective-permute-done((bf16[272,128]{1,0:T(8,128)(2,1)S(1)}, bf16[272,128]{1,0:T(8,128)(2,1)S(1)}, u32[]{:S(2)}, u32[]{:S(2)}) %collective-permute-start.21) | collective-permute-done | bytes 69664 | tf_op jit(solution)/shard_map/ppermute | solution.py:19
  62.0 0.0 collective-permute-done.22.refs_6_
  62.0 0.7 %shard_map.72 = (f32[1,2,128,128]{3,2,1,0:T(8,128)}, f32[2,2]{1,0:T(2,128)}) custom-call(f32[256,128]{1,0:T(8,128)S(1)} %get-tuple-element.42.mine_ref, f32[16,128]{1,0:T(8,128)S(1)} %get-tuple-element.43.total_ref, bf16[272,128]{1,0:T(8,128)(2,1)S(1)} %collective-permute-done.16.refs_0_, bf16[272,128]{1,0:T(8,128)(2,1)S(1)} %collective-permute-done.17.refs_1_, ...), custom_call_target="tpu_custom_call" | custom-call | tf_op jit(solution)/shard_map/pallas_call | solution.py:440
Async XLA Ops:
  2.3 3.2 %collective-permute-start.1 = (bf16[6,128,128]{2,1,0:T(8,128)(2,1)}, bf16[6,128,128]{2,1,0:T(8,128)(2,1)S(1)}, u32[]{:S(2)}, u32[]{:S(2)}) collective-permute-start(bf16[6,128,128]{2,1,0:T(8,128)(2,1)} %shard_map.67.refs_0_), channel_id=1, source_target_pairs={{0,1},{1,0},{2,3},{3,2},{4,5},{5,4},{6,7},{7,6},{8,9},{9,8},{10,11... | collective-permute-start | bytes 589832 | tf_op jit(solution)/shard_map/ppermute | solution.py:19
  2.8 6.4 %collective-permute-start = (bf16[6,128,128]{2,1,0:T(8,128)(2,1)}, bf16[6,128,128]{2,1,0:T(8,128)(2,1)S(1)}, u32[]{:S(2)}, u32[]{:S(2)}) collective-permute-start(bf16[6,128,128]{2,1,0:T(8,128)(2,1)} %shard_map.67.refs_0_), channel_id=1, source_target_pairs={{0,4},{1,3},{4,8},{5,1},{8,12},{9,5},{12,14},{13,9},{14,10},{15,13... | collective-permute-start | bytes 589832 | tf_op jit(solution)/shard_map/ppermute | solution.py:33
  5.5 5.9 %collective-permute-start.2 = (bf16[6,128,128]{2,1,0:T(8,128)(2,1)S(1)}, bf16[6,128,128]{2,1,0:T(8,128)(2,1)S(1)}, u32[]{:S(2)}, u32[]{:S(2)}) collective-permute-start(bf16[6,128,128]{2,1,0:T(8,128)(2,1)S(1)} %collective-permute-done.1.refs_1_), channel_id=1, source_target_pairs={{0,4},{1,3},{4,8},{5,1},{8,12},{9,5},{12,14},{13,9},{14,10},{15,13... | collective-permute-start | bytes 589832 | tf_op jit(solution)/shard_map/ppermute | solution.py:33
  7.1 0.7 %copy-start.1 = (s32[256,4]{0,1:T(4,128)S(1)}, s32[256,4]{0,1:T(4,128)}, u32[]{:S(2)}) copy-start(s32[256,4]{0,1:T(4,128)} %param.7) | copy-start | bytes 12292
  8.7 19.7 %copy-start = (bf16[6,128,128]{2,1,0:T(8,128)(2,1)S(1)}, bf16[6,128,128]{2,1,0:T(8,128)(2,1)}, u32[]{:S(2)}) copy-start(bf16[6,128,128]{2,1,0:T(8,128)(2,1)} %shard_map.67.refs_0_) | copy-start | bytes 589828
  9.3 5.7 %collective-permute-start.5 = (bf16[6,128,128]{2,1,0:T(8,128)(2,1)S(1)}, bf16[6,128,128]{2,1,0:T(8,128)(2,1)S(1)}, u32[]{:S(2)}, u32[]{:S(2)}) collective-permute-start(bf16[6,128,128]{2,1,0:T(8,128)(2,1)S(1)} %collective-permute-done.refs_2_), channel_id=1, source_target_pairs={{0,4},{1,3},{4,8},{5,1},{8,12},{9,5},{12,14},{13,9},{14,10},{15,13... | collective-permute-start | bytes 589832 | tf_op jit(solution)/shard_map/ppermute | solution.py:33
  11.4 5.7 %collective-permute-start.6 = (bf16[6,128,128]{2,1,0:T(8,128)(2,1)S(1)}, bf16[6,128,128]{2,1,0:T(8,128)(2,1)S(1)}, u32[]{:S(2)}, u32[]{:S(2)}) collective-permute-start(bf16[6,128,128]{2,1,0:T(8,128)(2,1)S(1)} %collective-permute-done.2.refs_3_), channel_id=1, source_target_pairs={{0,4},{1,3},{4,8},{5,1},{8,12},{9,5},{12,14},{13,9},{14,10},{15,13... | collective-permute-start | bytes 589832 | tf_op jit(solution)/shard_map/ppermute | solution.py:33
  13.5 5.7 %collective-permute-start.3 = (bf16[6,128,128]{2,1,0:T(8,128)(2,1)S(1)}, bf16[6,128,128]{2,1,0:T(8,128)(2,1)S(1)}, u32[]{:S(2)}, u32[]{:S(2)}) collective-permute-start(bf16[6,128,128]{2,1,0:T(8,128)(2,1)S(1)} %collective-permute-done.refs_2_), channel_id=1, source_target_pairs={{0,1},{1,0},{2,3},{3,2},{4,5},{5,4},{6,7},{7,6},{8,9},{9,8},{10,11... | collective-permute-start | bytes 589832 | tf_op jit(solution)/shard_map/ppermute | solution.py:19
  14.9 5.7 %collective-permute-start.9 = (bf16[6,128,128]{2,1,0:T(8,128)(2,1)S(1)}, bf16[6,128,128]{2,1,0:T(8,128)(2,1)S(1)}, u32[]{:S(2)}, u32[]{:S(2)}) collective-permute-start(bf16[6,128,128]{2,1,0:T(8,128)(2,1)S(1)} %collective-permute-done.5.refs_6_), channel_id=1, source_target_pairs={{0,4},{1,3},{4,8},{5,1},{8,12},{9,5},{12,14},{13,9},{14,10},{15,13... | collective-permute-start | bytes 589832 | tf_op jit(solution)/shard_map/ppermute | solution.py:33
  17.0 5.7 %collective-permute-start.4 = (bf16[6,128,128]{2,1,0:T(8,128)(2,1)S(1)}, bf16[6,128,128]{2,1,0:T(8,128)(2,1)S(1)}, u32[]{:S(2)}, u32[]{:S(2)}) collective-permute-start(bf16[6,128,128]{2,1,0:T(8,128)(2,1)S(1)} %collective-permute-done.2.refs_3_), channel_id=1, source_target_pairs={{0,1},{1,0},{2,3},{3,2},{4,5},{5,4},{6,7},{7,6},{8,9},{9,8},{10,11... | collective-permute-start | bytes 589832 | tf_op jit(solution)/shard_map/ppermute | solution.py:19
  17.1 5.7 %collective-permute-start.10 = (bf16[6,128,128]{2,1,0:T(8,128)(2,1)S(1)}, bf16[6,128,128]{2,1,0:T(8,128)(2,1)S(1)}, u32[]{:S(2)}, u32[]{:S(2)}) collective-permute-start(bf16[6,128,128]{2,1,0:T(8,128)(2,1)S(1)} %collective-permute-done.6.refs_7_), channel_id=1, source_target_pairs={{0,4},{1,3},{4,8},{5,1},{8,12},{9,5},{12,14},{13,9},{14,10},{15,13... | collective-permute-start | bytes 589832 | tf_op jit(solution)/shard_map/ppermute | solution.py:33
  19.1 5.7 %collective-permute-start.7 = (bf16[6,128,128]{2,1,0:T(8,128)(2,1)S(1)}, bf16[6,128,128]{2,1,0:T(8,128)(2,1)S(1)}, u32[]{:S(2)}, u32[]{:S(2)}) collective-permute-start(bf16[6,128,128]{2,1,0:T(8,128)(2,1)S(1)} %collective-permute-done.5.refs_6_), channel_id=1, source_target_pairs={{0,1},{1,0},{2,3},{3,2},{4,5},{5,4},{6,7},{7,6},{8,9},{9,8},{10,11... | collective-permute-start | bytes 589832 | tf_op jit(solution)/shard_map/ppermute | solution.py:19
  19.1 9.1 %collective-permute-start.8 = (bf16[6,128,128]{2,1,0:T(8,128)(2,1)S(1)}, bf16[6,128,128]{2,1,0:T(8,128)(2,1)S(1)}, u32[]{:S(2)}, u32[]{:S(2)}) collective-permute-start(bf16[6,128,128]{2,1,0:T(8,128)(2,1)S(1)} %collective-permute-done.6.refs_7_), channel_id=1, source_target_pairs={{0,1},{1,0},{2,3},{3,2},{4,5},{5,4},{6,7},{7,6},{8,9},{9,8},{10,11... | collective-permute-start | bytes 589832 | tf_op jit(solution)/shard_map/ppermute | solution.py:19
  20.6 7.6 %collective-permute-start.13 = (bf16[6,128,128]{2,1,0:T(8,128)(2,1)S(1)}, bf16[6,128,128]{2,1,0:T(8,128)(2,1)S(1)}, u32[]{:S(2)}, u32[]{:S(2)}) collective-permute-start(bf16[6,128,128]{2,1,0:T(8,128)(2,1)S(1)} %collective-permute-done.9.refs_10_), channel_id=1, source_target_pairs={{0,4},{1,3},{4,8},{5,1},{8,12},{9,5},{12,14},{13,9},{14,10},{15,13... | collective-permute-start | bytes 589832 | tf_op jit(solution)/shard_map/ppermute | solution.py:33
  22.7 5.5 %collective-permute-start.11 = (bf16[6,128,128]{2,1,0:T(8,128)(2,1)S(1)}, bf16[6,128,128]{2,1,0:T(8,128)(2,1)S(1)}, u32[]{:S(2)}, u32[]{:S(2)}) collective-permute-start(bf16[6,128,128]{2,1,0:T(8,128)(2,1)S(1)} %collective-permute-done.9.refs_10_), channel_id=1, source_target_pairs={{0,1},{1,0},{2,3},{3,2},{4,5},{5,4},{6,7},{7,6},{8,9},{9,8},{10,11... | collective-permute-start | bytes 589832 | tf_op jit(solution)/shard_map/ppermute | solution.py:19
  22.7 5.7 %collective-permute-start.14 = (bf16[6,128,128]{2,1,0:T(8,128)(2,1)S(1)}, bf16[6,128,128]{2,1,0:T(8,128)(2,1)S(1)}, u32[]{:S(2)}, u32[]{:S(2)}) collective-permute-start(bf16[6,128,128]{2,1,0:T(8,128)(2,1)S(1)} %collective-permute-done.10.refs_11_), channel_id=1, source_target_pairs={{0,4},{1,3},{4,8},{5,1},{8,12},{9,5},{12,14},{13,9},{14,10},{15,13... | collective-permute-start | bytes 589832 | tf_op jit(solution)/shard_map/ppermute | solution.py:33
  24.8 3.6 %collective-permute-start.12 = (bf16[6,128,128]{2,1,0:T(8,128)(2,1)S(1)}, bf16[6,128,128]{2,1,0:T(8,128)(2,1)S(1)}, u32[]{:S(2)}, u32[]{:S(2)}) collective-permute-start(bf16[6,128,128]{2,1,0:T(8,128)(2,1)S(1)} %collective-permute-done.10.refs_11_), channel_id=1, source_target_pairs={{0,1},{1,0},{2,3},{3,2},{4,5},{5,4},{6,7},{7,6},{8,9},{9,8},{10,11... | collective-permute-start | bytes 589832 | tf_op jit(solution)/shard_map/ppermute | solution.py:19
  41.5 3.0 %collective-permute-start.15 = (bf16[2064,128]{1,0:T(8,128)(2,1)S(1)}, bf16[2064,128]{1,0:T(8,128)(2,1)S(1)}, u32[]{:S(2)}, u32[]{:S(2)}) collective-permute-start(bf16[2064,128]{1,0:T(8,128)(2,1)S(1)} %get-tuple-element.41), channel_id=1, source_target_pairs={{0,1},{1,0},{2,3},{3,2},{4,5},{5,4},{6,7},{7,6},{8,9},{9,8},{10,11... | collective-permute-start | bytes 1585160 | tf_op jit(solution)/shard_map/ppermute | solution.py:19
  44.6 8.6 %collective-permute-start.16 = (bf16[272,128]{1,0:T(8,128)(2,1)S(1)}, bf16[272,128]{1,0:T(8,128)(2,1)S(1)}, u32[]{:S(2)}, u32[]{:S(2)}) collective-permute-start(bf16[272,128]{1,0:T(8,128)(2,1)S(1)} %get-tuple-element.44), channel_id=1, source_target_pairs={{0,14},{1,15},{2,12},{3,13},{4,10},{5,11},{6,8},{7,9},{8,6},{9,7},... | collective-permute-start | bytes 208904 | tf_op jit(solution)/shard_map/ppermute | solution.py:19
  47.7 9.7 %collective-permute-start.17 = (bf16[272,128]{1,0:T(8,128)(2,1)S(1)}, bf16[272,128]{1,0:T(8,128)(2,1)S(1)}, u32[]{:S(2)}, u32[]{:S(2)}) collective-permute-start(bf16[272,128]{1,0:T(8,128)(2,1)S(1)} %get-tuple-element.45), channel_id=1, source_target_pairs={{0,12},{1,13},{2,14},{3,15},{4,8},{5,9},{6,10},{7,11},{8,4},{9,5},... | collective-permute-start | bytes 208904 | tf_op jit(solution)/shard_map/ppermute | solution.py:19
  48.0 12.7 %collective-permute-start.18 = (bf16[272,128]{1,0:T(8,128)(2,1)S(1)}, bf16[272,128]{1,0:T(8,128)(2,1)S(1)}, u32[]{:S(2)}, u32[]{:S(2)}) collective-permute-start(bf16[272,128]{1,0:T(8,128)(2,1)S(1)} %get-tuple-element.46), channel_id=1, source_target_pairs={{0,10},{1,11},{2,8},{3,9},{4,14},{5,15},{6,12},{7,13},{8,2},{9,3},... | collective-permute-start | bytes 208904 | tf_op jit(solution)/shard_map/ppermute | solution.py:19
  51.6 9.2 %collective-permute-start.19 = (bf16[272,128]{1,0:T(8,128)(2,1)S(1)}, bf16[272,128]{1,0:T(8,128)(2,1)S(1)}, u32[]{:S(2)}, u32[]{:S(2)}) collective-permute-start(bf16[272,128]{1,0:T(8,128)(2,1)S(1)} %get-tuple-element.47), channel_id=1, source_target_pairs={{0,8},{1,9},{2,10},{3,11},{4,12},{5,13},{6,14},{7,15},{8,0},{9,1},... | collective-permute-start | bytes 208904 | tf_op jit(solution)/shard_map/ppermute | solution.py:19
  52.3 8.5 %collective-permute-start.20 = (bf16[272,128]{1,0:T(8,128)(2,1)S(1)}, bf16[272,128]{1,0:T(8,128)(2,1)S(1)}, u32[]{:S(2)}, u32[]{:S(2)}) collective-permute-start(bf16[272,128]{1,0:T(8,128)(2,1)S(1)} %get-tuple-element.48), channel_id=1, source_target_pairs={{0,6},{1,7},{2,4},{3,5},{4,2},{5,3},{6,0},{7,1},{8,14},{9,15},{10,... | collective-permute-start | bytes 208904 | tf_op jit(solution)/shard_map/ppermute | solution.py:19
  53.2 8.8 %collective-permute-start.21 = (bf16[272,128]{1,0:T(8,128)(2,1)S(1)}, bf16[272,128]{1,0:T(8,128)(2,1)S(1)}, u32[]{:S(2)}, u32[]{:S(2)}) collective-permute-start(bf16[272,128]{1,0:T(8,128)(2,1)S(1)} %get-tuple-element.49), channel_id=1, source_target_pairs={{0,4},{1,5},{2,6},{3,7},{4,0},{5,1},{6,2},{7,3},{8,12},{9,13},{10,... | collective-permute-start | bytes 208904 | tf_op jit(solution)/shard_map/ppermute | solution.py:19
  57.4 4.5 %collective-permute-start.22 = (bf16[272,128]{1,0:T(8,128)(2,1)S(1)}, bf16[272,128]{1,0:T(8,128)(2,1)S(1)}, u32[]{:S(2)}, u32[]{:S(2)}) collective-permute-start(bf16[272,128]{1,0:T(8,128)(2,1)S(1)} %get-tuple-element.50), channel_id=1, source_target_pairs={{0,2},{1,3},{2,0},{3,1},{4,6},{5,7},{6,4},{7,5},{8,10},{9,11},{10,... | collective-permute-start | bytes 208904 | tf_op jit(solution)/shard_map/ppermute | solution.py:19

commit v10 on v9

--- a/solution.py
+++ b/solution.py
@@ -190,16 +190,13 @@
     )(left_ops)
 
 
-def block_copies(n, kinds, blocks, trial, right, sem, which):
-    copies = []
+def block_copies(n, kinds, trials, rights, trial, right, sem):
+    copies = ([], [])
     for b, kind in enumerate(kinds):
         owner = owner_of(*kind, n)
-        per = blocks[b].shape[0] - TRIALS
-        if which == 0:
-            source, to = blocks[b].at[pl.ds(0, TRIALS)], trial.at[owner]
-        else:
-            source, to = blocks[b].at[pl.ds(TRIALS, per)], right.at[pl.ds(owner * per, per)]
-        copies.append(pltpu.make_async_copy(source, to, sem.at[b, which]))
+        per = rights[b].shape[0]
+        copies[0].append(pltpu.make_async_copy(trials[b], trial.at[owner], sem.at[b, 0]))
+        copies[1].append(pltpu.make_async_copy(rights[b], right.at[pl.ds(owner * per, per)], sem.at[b, 1]))
     return copies
 
 
@@ -249,7 +246,8 @@
 
 
 def tasks_kernel(n, kinds, plan_ref, left_ref, *refs):
-    blocks, refs = refs[: len(kinds)], refs[len(kinds) :]
+    count = len(kinds)
+    trials, rights, refs = refs[:count], refs[count : 2 * count], refs[2 * count :]
     send_ref, keep_ref, own_ref, halves, trial, right, acc, block_sem, *fetched = refs
     start, products = make_halves(n, plan_ref, left_ref, trial, halves, fetched)
     right[right.shape[0] - 1] = jnp.zeros((128, 128), jnp.bfloat16)
@@ -258,11 +256,11 @@
         moves = ([], [])
         for b, kind in enumerate(kinds):
             owner = owner_of(*kind, n)
-            per = blocks[b].shape[0] - TRIALS
-            trial[owner] = blocks[b][0:TRIALS]
-            right[pl.ds(owner * per, per)] = blocks[b][TRIALS:]
+            per = rights[b].shape[0]
+            trial[owner] = trials[b][...]
+            right[pl.ds(owner * per, per)] = rights[b][...]
     else:
-        moves = [block_copies(n, kinds, blocks, trial, right, block_sem, which) for which in range(2)]
+        moves = block_copies(n, kinds, trials, rights, trial, right, block_sem)
         for copy in moves[0] + moves[1]:
             copy.start()
 
@@ -309,7 +307,7 @@
         return p00 + fold(t0 * a0), p01 + fold(t0 * a1), p10 + fold(t1 * a0), p11 + fold(t1 * a1)
 
     zero = jnp.zeros((8, 128), jnp.float32)
-    sums = lax.fori_loop(0, n, dots, (zero,) * 4)
+    sums = lax.fori_loop(0, n, dots, (zero,) * 4, unroll=4)
     p00, p01, p10, p11 = [jnp.sum(x) for x in sums]
 
     def pack(j, carry):
@@ -318,7 +316,7 @@
         send_ref[pl.ds(pl.multiple_of(j * 256, 256), 256), :] = acc[jnp.bitwise_xor(mine, 1)].astype(jnp.bfloat16)
         return carry
 
-    lax.fori_loop(0, n // 2, pack, 0)
+    lax.fori_loop(0, n // 2, pack, 0, unroll=2)
     own = split3(matrix_of({(0, 0): p00, (0, 1): p01, (1, 0): p10, (1, 1): p11}, 3))
     own_ref[...] = own
     send_ref[n // 2 * 256 :, :] = tail_of(own, jnp.zeros_like(own))
@@ -326,8 +324,8 @@
 
 def run_tasks(n, plan, left_ops, blocks):
     slots = left_ops.shape[0]
-    terms_per = blocks[0][0].shape[0] - TRIALS
-    kinds = tuple(block[1:] for block in blocks)
+    terms_per = blocks[0][1].shape[0]
+    kinds = tuple(block[2:] for block in blocks)
     vmem, hbm = pl.BlockSpec(memory_space=pltpu.VMEM), pl.BlockSpec(memory_space=pltpu.HBM)
     given = vmem if fits(n) else hbm
     fetched = [] if fits(n) else [
@@ -341,7 +339,7 @@
             jax.ShapeDtypeStruct((n // 2, 256, 128), jnp.float32),
             jax.ShapeDtypeStruct((8, 128), jnp.float32),
         ),
-        in_specs=[pl.BlockSpec(memory_space=pltpu.SMEM)] + [given] * (1 + len(blocks)),
+        in_specs=[pl.BlockSpec(memory_space=pltpu.SMEM)] + [given] * (1 + 2 * len(blocks)),
         out_specs=(vmem,) * 3,
         scratch_shapes=[
             pltpu.VMEM((source_places(slots, n), 2, 128, 128), jnp.bfloat16),
@@ -355,32 +353,20 @@
         cost_estimate=pl.CostEstimate(
             flops=slots * 8 * 128**3, bytes_accessed=slots * 32768 + n * 450000, transcendentals=0
         ),
-    )(plan, left_ops, *[block[0] for block in blocks])
-
-
-def join_kernel(trial_ref, right_ref, block_ref, right, sem):
-    copies = [
-        pltpu.make_async_copy(right_ref, right, sem.at[0]),
-        pltpu.make_async_copy(trial_ref.at[0], block_ref.at[pl.ds(0, TRIALS)], sem.at[1]),
-    ]
-    for copy in copies:
-        copy.start()
-    copies[0].wait()
-    for k in range(right.shape[0]):
-        block_ref[TRIALS + k] = jnp.transpose(right[k])
-    copies[1].wait()
-
-
-def join(trial, right_ops):
-    hbm = pl.BlockSpec(memory_space=pltpu.HBM)
-    return pl.pallas_call(
-        join_kernel,
-        out_shape=jax.ShapeDtypeStruct((TRIALS + right_ops.shape[0], 128, 128), jnp.bfloat16),
-        in_specs=[hbm, hbm],
-        out_specs=pl.BlockSpec(memory_space=pltpu.VMEM),
-        scratch_shapes=[pltpu.VMEM(right_ops.shape, jnp.bfloat16), pltpu.SemaphoreType.DMA((2,))],
-        compiler_params=pltpu.CompilerParams(vmem_limit_bytes=59 * MIB),
-    )(trial, right_ops)
+    )(plan, left_ops, *[block[0] for block in blocks], *[block[1] for block in blocks])
+
+
+def transpose_kernel(right_ref, result_ref):
+    for k in range(right_ref.shape[0]):
+        result_ref[k] = jnp.transpose(right_ref[k])
+
+
+def transposed(right_ops):
+    return pl.pallas_call(
+        transpose_kernel,
+        out_shape=jax.ShapeDtypeStruct(right_ops.shape, right_ops.dtype),
+        compiler_params=pltpu.CompilerParams(vmem_limit_bytes=16 * MIB),
+    )(right_ops)
 
 
 def corr_kernel(*refs):
@@ -449,19 +435,19 @@
 
 def body(n, trial, left_ops, right_ops, task_list):
     steps = n // 4
-    own = join(trial, right_ops)
     plan = make_plan(task_list.T, n, n * right_ops.shape[0])
     left_ops = stage(left_ops, n)
-    lines = [own, exchange(own, n, 1)]
-    blocks = [(value, 0, False, half) for half, value in enumerate(lines)]
+    own = [trial[0], transposed(right_ops)]
+    lines = [own, [exchange(value, n, 1) for value in own]]
+    blocks = [(*values, 0, False, half) for half, values in enumerate(lines)]
     for step in range(1, steps + 1):
         if step == 2:
-            lines[0], plan = lax.optimization_barrier((lines[0], plan))
-        for half in range(2):
-            lines[half] = ring_step(lines[half], n)
-            blocks.append((lines[half], step, False, half))
+            lines[0][0], plan = lax.optimization_barrier((lines[0][0], plan))
+        lines = [[ring_step(value, n) for value in values] for values in lines]
+        blocks += [(*values, step, False, half) for half, values in enumerate(lines)]
         if step < steps:
-            blocks += [(exchange(value, n, 1), step, True, half) for half, value in enumerate(lines)]
+            for half, values in enumerate(lines):
+                blocks.append((*[exchange(value, n, 1) for value in values], step, True, half))
     send, keep, own = run_tasks(n, plan, left_ops, blocks)
     send, arrays = lax.optimization_barrier((send, [block[0] for block in blocks]))
     correlation = correlate(arrays)

time: 62.5 us -> 73 us (1.17)
  starting transfers between devices: 32 us -> 41.4 us
  waiting for transfers between devices: 8.32 us -> 10.9 us
  Pallas kernels: 21 us -> 18.6 us
  local copies, waits for them, and re-layouts: 0.69 us -> 1.59 us
    ppermute x8 -> x16, starting transfers between devices: 16.7 us -> 24.3 us  [ring_step(): return lax.ppermute(value, 'op', pairs)]
    ppermute x8 -> x16, waiting for transfers between devices: 3.26 us -> 5.96 us  [ring_step(): return lax.ppermute(value, 'op', pairs)]
    ppermute x15 -> x22, starting transfers between devices: 15.4 us -> 17 us  [exchange(): return lax.ppermute(value, 'op', [(i, i ^ mask) for i in range(n)])]
    pallas_call x1, Pallas kernels: 1.68 us -> 0.08 us  [transposed(): pl.pallas_call(transpose_kernel, out_shape=jax.ShapeDtypeStruct(right_ops...]
    unnamed x4 -> x6, local copies, waits for them, and re-layouts: 0.69 us -> 1.59 us
    pallas_call x1, Pallas kernels: 13.1 us -> 12.3 us  [run_tasks(): pl.pallas_call(functools.partial(tasks_kernel, n, kinds), out_shape=(jax....]
    ppermute x15 -> x22, waiting for transfers between devices: 5.06 us -> 4.91 us  [exchange(): return lax.ppermute(value, 'op', [(i, i ^ mask) for i in range(n)])]
  transfers between devices with their start and end apart: 23 -> 38, of which waited for: 8 -> 10; matrix products, arithmetic and copies ran while one was open for 0% -> 0% of each run, Pallas kernels for 9% -> 7%
where the time goes in v10:
time: 73 us; the launch traced here: 73.2 us
  starting transfers between devices  41.4 us (57%)
  Pallas kernels  18.6 us (25%)
  waiting for transfers between devices  10.9 us (15%)
  local copies, waits for them, and re-layouts  1.59 us (2%)
  between operations  0.77 us (1%)
    ppermute x16, starting transfers between devices, ring_step(): return lax.ppermute(value, 'op', pairs)  24.3 us
    ppermute x22, starting transfers between devices, exchange(): return lax.ppermute(value, 'op', [(i, i ^ mask) for i in range(n)])  17 us
    pallas_call x1, Pallas kernels, run_tasks(): pl.pallas_call(functools.partial(tasks_kernel, n, kinds), out_shape=(jax....  12.3 us
    ppermute x16, waiting for transfers between devices, ring_step(): return lax.ppermute(value, 'op', pairs)  5.96 us
    ppermute x22, waiting for transfers between devices, exchange(): return lax.ppermute(value, 'op', [(i, i ^ mask) for i in range(n)])  4.91 us
    pallas_call x1, Pallas kernels, stage(): pl.pallas_call(stage_kernel, in_specs=[pl.BlockSpec(memory_space=pltpu.HB...  3.39 us
    unnamed x6, local copies, waits for them, and re-layouts  1.59 us
  transfers between devices with their start and end apart: 38, of which 10 were waited for; matrix products, arithmetic and copies ran while one was open for 0% of the time, Pallas kernels for 7%

profile of v10, /device:TPU:0, one launch (start us, length us, event | category | flops | bytes accessed | tf_op | source)
XLA Modules:
  0.0 73.2 jit_solution(3152629526841404336)
XLA Ops:
  0.6 0.9 %copy-done = bf16[4,128,128]{2,1,0:T(8,128)(2,1)S(1)} copy-done((bf16[4,128,128]{2,1,0:T(8,128)(2,1)S(1)}, bf16[4,128,128]{2,1,0:T(8,128)(2,1)}, u32[]{:S(2)}) %copy-start) | copy-done | bytes 131096
  1.5 0.1 shard_map.69.refs_16_
  1.6 0.5 collective-permute-start.15
  2.1 2.6 %collective-permute-start = (bf16[2,128,128]{2,1,0:T(8,128)(2,1)}, bf16[2,128,128]{2,1,0:T(8,128)(2,1)S(1)}, u32[]{:S(2)}, u32[]{:S(2)}) collective-permute-start(bf16[2,128,128]{2,1,0:T(8,128)(2,1)} %bitcast.2), channel_id=1, source_target_pairs={{0,4},{1,3},{4,8},{5,1},{8,12},{9,5},{12,14},{13,9},{14,10},{15,13... | collective-permute-start | bytes 196616 | tf_op jit(solution)/shard_map/ppermute | solution.py:33
  4.8 0.1 collective-permute-start.1
  4.9 1.5 %collective-permute-start.16 = (bf16[4,128,128]{2,1,0:T(8,128)(2,1)S(1)}, bf16[4,128,128]{2,1,0:T(8,128)(2,1)S(1)}, u32[]{:S(2)}, u32[]{:S(2)}) collective-permute-start(bf16[4,128,128]{2,1,0:T(8,128)(2,1)S(1)} %shard_map.69.refs_16_), channel_id=1, source_target_pairs={{0,4},{1,3},{4,8},{5,1},{8,12},{9,5},{12,14},{13,9},{14,10},{15,13... | collective-permute-start | bytes 393224 | tf_op jit(solution)/shard_map/ppermute | solution.py:33
  6.4 0.7 copy-done.2
  7.0 1.0 %shard_map.67.plan_ref = s32[8,512]{1,0:T(8,128)S(1)} custom-call(s32[4,256]{1,0:T(4,128)S(1)} %bitcast.6), custom_call_target="tpu_custom_call" | custom-call | tf_op jit(solution)/shard_map/pallas_call | solution.py:167
  8.0 0.0 copy-start.1
  8.1 1.6 %collective-permute-start.2 = (bf16[2,128,128]{2,1,0:T(8,128)(2,1)S(1)}, bf16[2,128,128]{2,1,0:T(8,128)(2,1)S(1)}, u32[]{:S(2)}, u32[]{:S(2)}) collective-permute-start(bf16[2,128,128]{2,1,0:T(8,128)(2,1)S(1)} %collective-permute-done.1.refs_1_), channel_id=1, source_target_pairs={{0,4},{1,3},{4,8},{5,1},{8,12},{9,5},{12,14},{13,9},{14,10},{15,13... | collective-permute-start | bytes 196616 | tf_op jit(solution)/shard_map/ppermute | solution.py:33
  9.7 1.5 %collective-permute-start.5 = (bf16[2,128,128]{2,1,0:T(8,128)(2,1)S(1)}, bf16[2,128,128]{2,1,0:T(8,128)(2,1)S(1)}, u32[]{:S(2)}, u32[]{:S(2)}) collective-permute-start(bf16[2,128,128]{2,1,0:T(8,128)(2,1)S(1)} %collective-permute-done.refs_2_), channel_id=1, source_target_pairs={{0,4},{1,3},{4,8},{5,1},{8,12},{9,5},{12,14},{13,9},{14,10},{15,13... | collective-permute-start | bytes 196616 | tf_op jit(solution)/shard_map/ppermute | solution.py:33
  11.2 1.2 %collective-permute-start.17 = (bf16[4,128,128]{2,1,0:T(8,128)(2,1)S(1)}, bf16[4,128,128]{2,1,0:T(8,128)(2,1)S(1)}, u32[]{:S(2)}, u32[]{:S(2)}) collective-permute-start(bf16[4,128,128]{2,1,0:T(8,128)(2,1)S(1)} %collective-permute-done.15.refs_17_), channel_id=1, source_target_pairs={{0,4},{1,3},{4,8},{5,1},{8,12},{9,5},{12,14},{13,9},{14,10},{15,13... | collective-permute-start | bytes 393224 | tf_op jit(solution)/shard_map/ppermute | solution.py:33
  12.4 0.0 collective-permute-done.2.refs_3_
  12.4 1.5 %collective-permute-start.6 = (bf16[2,128,128]{2,1,0:T(8,128)(2,1)S(1)}, bf16[2,128,128]{2,1,0:T(8,128)(2,1)S(1)}, u32[]{:S(2)}, u32[]{:S(2)}) collective-permute-start(bf16[2,128,128]{2,1,0:T(8,128)(2,1)S(1)} %collective-permute-done.2.refs_3_), channel_id=1, source_target_pairs={{0,4},{1,3},{4,8},{5,1},{8,12},{9,5},{12,14},{13,9},{14,10},{15,13... | collective-permute-start | bytes 196616 | tf_op jit(solution)/shard_map/ppermute | solution.py:33
  14.0 0.0 collective-permute-done.5.refs_6_
  14.0 0.0 collective-permute-start.4
  14.0 0.0 collective-permute-done.3.refs_4_
  14.0 1.6 %collective-permute-start.9 = (bf16[2,128,128]{2,1,0:T(8,128)(2,1)S(1)}, bf16[2,128,128]{2,1,0:T(8,128)(2,1)S(1)}, u32[]{:S(2)}, u32[]{:S(2)}) collective-permute-start(bf16[2,128,128]{2,1,0:T(8,128)(2,1)S(1)} %collective-permute-done.5.refs_6_), channel_id=1, source_target_pairs={{0,4},{1,3},{4,8},{5,1},{8,12},{9,5},{12,14},{13,9},{14,10},{15,13... | collective-permute-start | bytes 196616 | tf_op jit(solution)/shard_map/ppermute | solution.py:33
  15.5 0.0 collective-permute-done.16.refs_18_
  15.5 0.0 collective-permute-start.7
  15.6 1.3 %collective-permute-done.6.refs_7_ = bf16[2,128,128]{2,1,0:T(8,128)(2,1)S(1)} collective-permute-done((bf16[2,128,128]{2,1,0:T(8,128)(2,1)S(1)}, bf16[2,128,128]{2,1,0:T(8,128)(2,1)S(1)}, u32[]{:S(2)}, u32[]{:S(2)}) %collective-permute-start.6) | collective-permute-done | bytes 65568 | tf_op jit(solution)/shard_map/ppermute | solution.py:33
  16.9 1.3 %collective-permute-start.20 = (bf16[4,128,128]{2,1,0:T(8,128)(2,1)S(1)}, bf16[4,128,128]{2,1,0:T(8,128)(2,1)S(1)}, u32[]{:S(2)}, u32[]{:S(2)}) collective-permute-start(bf16[4,128,128]{2,1,0:T(8,128)(2,1)S(1)} %collective-permute-done.16.refs_18_), channel_id=1, source_target_pairs={{0,4},{1,3},{4,8},{5,1},{8,12},{9,5},{12,14},{13,9},{14,10},{15,13... | collective-permute-start | bytes 393224 | tf_op jit(solution)/shard_map/ppermute | solution.py:33
  18.2 0.0 collective-permute-done.4.refs_5_
  18.2 1.5 %collective-permute-start.10 = (bf16[2,128,128]{2,1,0:T(8,128)(2,1)S(1)}, bf16[2,128,128]{2,1,0:T(8,128)(2,1)S(1)}, u32[]{:S(2)}, u32[]{:S(2)}) collective-permute-start(bf16[2,128,128]{2,1,0:T(8,128)(2,1)S(1)} %collective-permute-done.6.refs_7_), channel_id=1, source_target_pairs={{0,4},{1,3},{4,8},{5,1},{8,12},{9,5},{12,14},{13,9},{14,10},{15,13... | collective-permute-start | bytes 196616 | tf_op jit(solution)/shard_map/ppermute | solution.py:33
  19.8 0.0 collective-permute-done.17.refs_19_
  19.8 1.3 %collective-permute-start.21 = (bf16[4,128,128]{2,1,0:T(8,128)(2,1)S(1)}, bf16[4,128,128]{2,1,0:T(8,128)(2,1)S(1)}, u32[]{:S(2)}, u32[]{:S(2)}) collective-permute-start(bf16[4,128,128]{2,1,0:T(8,128)(2,1)S(1)} %collective-permute-done.17.refs_19_), channel_id=1, source_target_pairs={{0,4},{1,3},{4,8},{5,1},{8,12},{9,5},{12,14},{13,9},{14,10},{15,13... | collective-permute-start | bytes 393224 | tf_op jit(solution)/shard_map/ppermute | solution.py:33
  21.0 0.0 collective-permute-done.7.refs_8_
  21.0 0.0 collective-permute-start.18
  21.0 1.5 %collective-permute-done.10.refs_11_ = bf16[2,128,128]{2,1,0:T(8,128)(2,1)S(1)} collective-permute-done((bf16[2,128,128]{2,1,0:T(8,128)(2,1)S(1)}, bf16[2,128,128]{2,1,0:T(8,128)(2,1)S(1)}, u32[]{:S(2)}, u32[]{:S(2)}) %collective-permute-start.10) | collective-permute-done | bytes 65568 | tf_op jit(solution)/shard_map/ppermute | solution.py:33
  22.6 1.5 %collective-permute-start.13 = (bf16[2,128,128]{2,1,0:T(8,128)(2,1)S(1)}, bf16[2,128,128]{2,1,0:T(8,128)(2,1)S(1)}, u32[]{:S(2)}, u32[]{:S(2)}) collective-permute-start(bf16[2,128,128]{2,1,0:T(8,128)(2,1)S(1)} %collective-permute-done.9.refs_10_), channel_id=1, source_target_pairs={{0,4},{1,3},{4,8},{5,1},{8,12},{9,5},{12,14},{13,9},{14,10},{15,13... | collective-permute-start | bytes 196616 | tf_op jit(solution)/shard_map/ppermute | solution.py:33
  24.0 0.0 collective-permute-done.8.refs_9_
  24.0 0.0 collective-permute-start.11
  24.0 0.0 collective-permute-done.20.refs_22_
  24.0 1.5 %collective-permute-start.24 = (bf16[4,128,128]{2,1,0:T(8,128)(2,1)S(1)}, bf16[4,128,128]{2,1,0:T(8,128)(2,1)S(1)}, u32[]{:S(2)}, u32[]{:S(2)}) collective-permute-start(bf16[4,128,128]{2,1,0:T(8,128)(2,1)S(1)} %collective-permute-done.20.refs_22_), channel_id=1, source_target_pairs={{0,4},{1,3},{4,8},{5,1},{8,12},{9,5},{12,14},{13,9},{14,10},{15,13... | collective-permute-start | bytes 393224 | tf_op jit(solution)/shard_map/ppermute | solution.py:33
  25.5 1.3 %collective-permute-done.13.refs_14_ = bf16[2,128,128]{2,1,0:T(8,128)(2,1)S(1)} collective-permute-done((bf16[2,128,128]{2,1,0:T(8,128)(2,1)S(1)}, bf16[2,128,128]{2,1,0:T(8,128)(2,1)S(1)}, u32[]{:S(2)}, u32[]{:S(2)}) %collective-permute-start.13) | collective-permute-done | bytes 65568 | tf_op jit(solution)/shard_map/ppermute | solution.py:33
  26.8 1.5 %collective-permute-start.14 = (bf16[2,128,128]{2,1,0:T(8,128)(2,1)S(1)}, bf16[2,128,128]{2,1,0:T(8,128)(2,1)S(1)}, u32[]{:S(2)}, u32[]{:S(2)}) collective-permute-start(bf16[2,128,128]{2,1,0:T(8,128)(2,1)S(1)} %collective-permute-done.10.refs_11_), channel_id=1, source_target_pairs={{0,4},{1,3},{4,8},{5,1},{8,12},{9,5},{12,14},{13,9},{14,10},{15,13... | collective-permute-start | bytes 196616 | tf_op jit(solution)/shard_map/ppermute | solution.py:33
  28.3 0.0 collective-permute-done.11.refs_12_
  28.3 0.0 collective-permute-start.22
  28.3 0.0 collective-permute-done.21.refs_23_
  28.3 1.5 %collective-permute-start.25 = (bf16[4,128,128]{2,1,0:T(8,128)(2,1)S(1)}, bf16[4,128,128]{2,1,0:T(8,128)(2,1)S(1)}, u32[]{:S(2)}, u32[]{:S(2)}) collective-permute-start(bf16[4,128,128]{2,1,0:T(8,128)(2,1)S(1)} %collective-permute-done.21.refs_23_), channel_id=1, source_target_pairs={{0,4},{1,3},{4,8},{5,1},{8,12},{9,5},{12,14},{13,9},{14,10},{15,13... | collective-permute-start | bytes 393224 | tf_op jit(solution)/shard_map/ppermute | solution.py:33
  29.7 0.0 collective-permute-done.18.refs_20_
  29.8 0.0 collective-permute-start.19
  29.8 1.3 %collective-permute-done.14.refs_15_ = bf16[2,128,128]{2,1,0:T(8,128)(2,1)S(1)} collective-permute-done((bf16[2,128,128]{2,1,0:T(8,128)(2,1)S(1)}, bf16[2,128,128]{2,1,0:T(8,128)(2,1)S(1)}, u32[]{:S(2)}, u32[]{:S(2)}) %collective-permute-start.14) | collective-permute-done | bytes 65568 | tf_op jit(solution)/shard_map/ppermute | solution.py:33
  31.1 1.5 %collective-permute-start.28 = (bf16[4,128,128]{2,1,0:T(8,128)(2,1)S(1)}, bf16[4,128,128]{2,1,0:T(8,128)(2,1)S(1)}, u32[]{:S(2)}, u32[]{:S(2)}) collective-permute-start(bf16[4,128,128]{2,1,0:T(8,128)(2,1)S(1)} %collective-permute-done.24.refs_26_), channel_id=1, source_target_pairs={{0,4},{1,3},{4,8},{5,1},{8,12},{9,5},{12,14},{13,9},{14,10},{15,13... | collective-permute-start | bytes 393224 | tf_op jit(solution)/shard_map/ppermute | solution.py:33
  32.6 0.5 collective-permute-start.23
  33.1 0.2 collective-permute-done.25.refs_27_
  33.3 1.4 %collective-permute-start.29 = (bf16[4,128,128]{2,1,0:T(8,128)(2,1)S(1)}, bf16[4,128,128]{2,1,0:T(8,128)(2,1)S(1)}, u32[]{:S(2)}, u32[]{:S(2)}) collective-permute-start(bf16[4,128,128]{2,1,0:T(8,128)(2,1)S(1)} %collective-permute-done.25.refs_27_), channel_id=1, source_target_pairs={{0,4},{1,3},{4,8},{5,1},{8,12},{9,5},{12,14},{13,9},{14,10},{15,13... | collective-permute-start | bytes 393224 | tf_op jit(solution)/shard_map/ppermute | solution.py:33
  34.7 3.4 %shard_map.68.left_ref = bf16[256,128,128]{2,1,0:T(8,128)(2,1)S(1)} custom-call(bf16[256,128,128]{2,1,0:T(8,128)(2,1)} %left_ref.1), custom_call_target="tpu_custom_call" | custom-call | tf_op jit(solution)/shard_map/pallas_call | solution.py:183
  38.2 0.1 collective-permute-done.29.refs_31_
  38.3 12.3 %shard_map.70 = (bf16[2064,128]{1,0:T(8,128)(2,1)S(1)}, f32[8,256,128]{2,1,0:T(8,128)S(1)}, f32[8,128]{1,0:T(8,128)S(1)}) custom-call(s32[8,512]{1,0:T(8,128)S(1)} %shard_map.67.plan_ref, bf16[256,128,128]{2,1,0:T(8,128)(2,1)S(1)} %shard_map.68.left_ref, bf16[2,128,128]{2,1,0:T(8,128)(2,1)S(1)} %bitcast.4, ...), custom_call_target="tpu_custom_call" | custom-call | flops 4294967296 | bytes 15588608 | tf_op jit(solution)/shard_map/pallas_call | solution.py:335
  50.6 2.5 %collective-permute-start.30 = (bf16[2064,128]{1,0:T(8,128)(2,1)S(1)}, bf16[2064,128]{1,0:T(8,128)(2,1)S(1)}, u32[]{:S(2)}, u32[]{:S(2)}) collective-permute-start(bf16[2064,128]{1,0:T(8,128)(2,1)S(1)} %get-tuple-element.41), channel_id=1, source_target_pairs={{0,1},{1,0},{2,3},{3,2},{4,5},{5,4},{6,7},{7,6},{8,9},{9,8},{10,11... | collective-permute-start | bytes 1585160 | tf_op jit(solution)/shard_map/ppermute | solution.py:19
  53.1 1.5 %collective-permute-done.30.received_ref = bf16[2064,128]{1,0:T(8,128)(2,1)S(1)} collective-permute-done((bf16[2064,128]{1,0:T(8,128)(2,1)S(1)}, bf16[2064,128]{1,0:T(8,128)(2,1)S(1)}, u32[]{:S(2)}, u32[]{:S(2)}) %collective-permute-start.30) | collective-permute-done | bytes 528416 | tf_op jit(solution)/shard_map/ppermute | solution.py:19
  54.7 0.1 shard_map.71
  54.8 0.7 collective-permute-start.31
  55.5 2.3 %collective-permute-start.32 = (bf16[272,128]{1,0:T(8,128)(2,1)S(1)}, bf16[272,128]{1,0:T(8,128)(2,1)S(1)}, u32[]{:S(2)}, u32[]{:S(2)}) collective-permute-start(bf16[272,128]{1,0:T(8,128)(2,1)S(1)} %get-tuple-element.45), channel_id=1, source_target_pairs={{0,12},{1,13},{2,14},{3,15},{4,8},{5,9},{6,10},{7,11},{8,4},{9,5},... | collective-permute-start | bytes 208904 | tf_op jit(solution)/shard_map/ppermute | solution.py:19
  57.8 1.0 %collective-permute-start.33 = (bf16[272,128]{1,0:T(8,128)(2,1)S(1)}, bf16[272,128]{1,0:T(8,128)(2,1)S(1)}, u32[]{:S(2)}, u32[]{:S(2)}) collective-permute-start(bf16[272,128]{1,0:T(8,128)(2,1)S(1)} %get-tuple-element.46), channel_id=1, source_target_pairs={{0,10},{1,11},{2,8},{3,9},{4,14},{5,15},{6,12},{7,13},{8,2},{9,3},... | collective-permute-start | bytes 208904 | tf_op jit(solution)/shard_map/ppermute | solution.py:19
  58.9 3.7 %collective-permute-start.34 = (bf16[272,128]{1,0:T(8,128)(2,1)S(1)}, bf16[272,128]{1,0:T(8,128)(2,1)S(1)}, u32[]{:S(2)}, u32[]{:S(2)}) collective-permute-start(bf16[272,128]{1,0:T(8,128)(2,1)S(1)} %get-tuple-element.47), channel_id=1, source_target_pairs={{0,8},{1,9},{2,10},{3,11},{4,12},{5,13},{6,14},{7,15},{8,0},{9,1},... | collective-permute-start | bytes 208904 | tf_op jit(solution)/shard_map/ppermute | solution.py:19
  62.5 5.6 %collective-permute-start.36 = (bf16[272,128]{1,0:T(8,128)(2,1)S(1)}, bf16[272,128]{1,0:T(8,128)(2,1)S(1)}, u32[]{:S(2)}, u32[]{:S(2)}) collective-permute-start(bf16[272,128]{1,0:T(8,128)(2,1)S(1)} %get-tuple-element.49), channel_id=1, source_target_pairs={{0,4},{1,5},{2,6},{3,7},{4,0},{5,1},{6,2},{7,3},{8,12},{9,13},{10,... | collective-permute-start | bytes 208904 | tf_op jit(solution)/shard_map/ppermute | solution.py:19
  68.2 1.0 %shard_map.73 = f32[2,2]{1,0:T(2,128)} custom-call(bf16[2,128,128]{2,1,0:T(8,128)(2,1)S(1)} %bitcast.5, bf16[2,128,128]{2,1,0:T(8,128)(2,1)S(1)} %collective-permute-done.1.refs_1_, bf16[2,128,128]{2,1,0:T(8,128)(2,1)S(1)} %collective-permute-done.refs_2_, bf16[2,128,128]{2,1,0:T(8,128)(2,1)S(1)} %collective-permute-done.2.refs_3_, ...), custom_call_target="tpu_custom_call" | custom-call | tf_op jit(solution)/shard_map/pallas_call | solution.py:383
  69.1 1.4 %collective-permute-done.33.refs_2_ = bf16[272,128]{1,0:T(8,128)(2,1)S(1)} collective-permute-done((bf16[272,128]{1,0:T(8,128)(2,1)S(1)}, bf16[272,128]{1,0:T(8,128)(2,1)S(1)}, u32[]{:S(2)}, u32[]{:S(2)}) %collective-permute-start.33) | collective-permute-done | bytes 69664 | tf_op jit(solution)/shard_map/ppermute | solution.py:19
  70.5 0.0 collective-permute-done.34.refs_3_
  70.6 0.7 collective-permute-done.36.refs_5_
  71.2 1.3 %collective-permute-done.37.refs_6_ = bf16[272,128]{1,0:T(8,128)(2,1)S(1)} collective-permute-done((bf16[272,128]{1,0:T(8,128)(2,1)S(1)}, bf16[272,128]{1,0:T(8,128)(2,1)S(1)}, u32[]{:S(2)}, u32[]{:S(2)}) %collective-permute-start.37) | collective-permute-done | bytes 69664 | tf_op jit(solution)/shard_map/ppermute | solution.py:19
  72.5 0.7 %shard_map.72 = (f32[1,2,128,128]{3,2,1,0:T(8,128)}, f32[2,2]{1,0:T(2,128)}) custom-call(f32[256,128]{1,0:T(8,128)S(1)} %get-tuple-element.42.mine_ref, f32[16,128]{1,0:T(8,128)S(1)} %get-tuple-element.43.total_ref, bf16[272,128]{1,0:T(8,128)(2,1)S(1)} %collective-permute-done.31.refs_0_, bf16[272,128]{1,0:T(8,128)(2,1)S(1)} %collective-permute-done.32.refs_1_, ...), custom_call_target="tpu_custom_call" | custom-call | tf_op jit(solution)/shard_map/pallas_call | solution.py:426
  (25 shorter events, 0.1 us)
Async XLA Ops:
  0.6 0.9 %copy-start = (bf16[4,128,128]{2,1,0:T(8,128)(2,1)S(1)}, bf16[4,128,128]{2,1,0:T(8,128)(2,1)}, u32[]{:S(2)}) copy-start(bf16[4,128,128]{2,1,0:T(8,128)(2,1)} %right_ref.1) | copy-start | bytes 393220
  1.6 9.6 %collective-permute-start.15 = (bf16[4,128,128]{2,1,0:T(8,128)(2,1)S(1)}, bf16[4,128,128]{2,1,0:T(8,128)(2,1)S(1)}, u32[]{:S(2)}, u32[]{:S(2)}) collective-permute-start(bf16[4,128,128]{2,1,0:T(8,128)(2,1)S(1)} %shard_map.69.refs_16_), channel_id=1, source_target_pairs={{0,1},{1,0},{2,3},{3,2},{4,5},{5,4},{6,7},{7,6},{8,9},{9,8},{10,11... | collective-permute-start | bytes 393224 | tf_op jit(solution)/shard_map/ppermute | solution.py:19
  2.1 5.9 %collective-permute-start = (bf16[2,128,128]{2,1,0:T(8,128)(2,1)}, bf16[2,128,128]{2,1,0:T(8,128)(2,1)S(1)}, u32[]{:S(2)}, u32[]{:S(2)}) collective-permute-start(bf16[2,128,128]{2,1,0:T(8,128)(2,1)} %bitcast.2), channel_id=1, source_target_pairs={{0,4},{1,3},{4,8},{5,1},{8,12},{9,5},{12,14},{13,9},{14,10},{15,13... | collective-permute-start | bytes 196616 | tf_op jit(solution)/shard_map/ppermute | solution.py:33
  4.8 3.3 %collective-permute-start.1 = (bf16[2,128,128]{2,1,0:T(8,128)(2,1)}, bf16[2,128,128]{2,1,0:T(8,128)(2,1)S(1)}, u32[]{:S(2)}, u32[]{:S(2)}) collective-permute-start(bf16[2,128,128]{2,1,0:T(8,128)(2,1)} %bitcast.3), channel_id=1, source_target_pairs={{0,1},{1,0},{2,3},{3,2},{4,5},{5,4},{6,7},{7,6},{8,9},{9,8},{10,11... | collective-permute-start | bytes 196616 | tf_op jit(solution)/shard_map/ppermute | solution.py:19
  4.9 10.7 %collective-permute-start.16 = (bf16[4,128,128]{2,1,0:T(8,128)(2,1)S(1)}, bf16[4,128,128]{2,1,0:T(8,128)(2,1)S(1)}, u32[]{:S(2)}, u32[]{:S(2)}) collective-permute-start(bf16[4,128,128]{2,1,0:T(8,128)(2,1)S(1)} %shard_map.69.refs_16_), channel_id=1, source_target_pairs={{0,4},{1,3},{4,8},{5,1},{8,12},{9,5},{12,14},{13,9},{14,10},{15,13... | collective-permute-start | bytes 393224 | tf_op jit(solution)/shard_map/ppermute | solution.py:33
  6.4 0.7 copy-start.2
  8.0 30.3 %copy-start.1 = (bf16[1,2,128,128]{3,2,1,0:T(8,128)(2,1)S(1)}, bf16[1,2,128,128]{3,2,1,0:T(8,128)(2,1)}, u32[]{:S(2)}) copy-start(bf16[1,2,128,128]{3,2,1,0:T(8,128)(2,1)} %param.4) | copy-start | bytes 196612
  8.1 4.4 %collective-permute-start.2 = (bf16[2,128,128]{2,1,0:T(8,128)(2,1)S(1)}, bf16[2,128,128]{2,1,0:T(8,128)(2,1)S(1)}, u32[]{:S(2)}, u32[]{:S(2)}) collective-permute-start(bf16[2,128,128]{2,1,0:T(8,128)(2,1)S(1)} %collective-permute-done.1.refs_1_), channel_id=1, source_target_pairs={{0,4},{1,3},{4,8},{5,1},{8,12},{9,5},{12,14},{13,9},{14,10},{15,13... | collective-permute-start | bytes 196616 | tf_op jit(solution)/shard_map/ppermute | solution.py:33
  9.7 4.3 %collective-permute-start.5 = (bf16[2,128,128]{2,1,0:T(8,128)(2,1)S(1)}, bf16[2,128,128]{2,1,0:T(8,128)(2,1)S(1)}, u32[]{:S(2)}, u32[]{:S(2)}) collective-permute-start(bf16[2,128,128]{2,1,0:T(8,128)(2,1)S(1)} %collective-permute-done.refs_2_), channel_id=1, source_target_pairs={{0,4},{1,3},{4,8},{5,1},{8,12},{9,5},{12,14},{13,9},{14,10},{15,13... | collective-permute-start | bytes 196616 | tf_op jit(solution)/shard_map/ppermute | solution.py:33
  11.2 2.8 %collective-permute-start.3 = (bf16[2,128,128]{2,1,0:T(8,128)(2,1)S(1)}, bf16[2,128,128]{2,1,0:T(8,128)(2,1)S(1)}, u32[]{:S(2)}, u32[]{:S(2)}) collective-permute-start(bf16[2,128,128]{2,1,0:T(8,128)(2,1)S(1)} %collective-permute-done.refs_2_), channel_id=1, source_target_pairs={{0,1},{1,0},{2,3},{3,2},{4,5},{5,4},{6,7},{7,6},{8,9},{9,8},{10,11... | collective-permute-start | bytes 196616 | tf_op jit(solution)/shard_map/ppermute | solution.py:19
  11.2 8.5 %collective-permute-start.17 = (bf16[4,128,128]{2,1,0:T(8,128)(2,1)S(1)}, bf16[4,128,128]{2,1,0:T(8,128)(2,1)S(1)}, u32[]{:S(2)}, u32[]{:S(2)}) collective-permute-start(bf16[4,128,128]{2,1,0:T(8,128)(2,1)S(1)} %collective-permute-done.15.refs_17_), channel_id=1, source_target_pairs={{0,4},{1,3},{4,8},{5,1},{8,12},{9,5},{12,14},{13,9},{14,10},{15,13... | collective-permute-start | bytes 393224 | tf_op jit(solution)/shard_map/ppermute | solution.py:33
  12.4 4.5 %collective-permute-start.6 = (bf16[2,128,128]{2,1,0:T(8,128)(2,1)S(1)}, bf16[2,128,128]{2,1,0:T(8,128)(2,1)S(1)}, u32[]{:S(2)}, u32[]{:S(2)}) collective-permute-start(bf16[2,128,128]{2,1,0:T(8,128)(2,1)S(1)} %collective-permute-done.2.refs_3_), channel_id=1, source_target_pairs={{0,4},{1,3},{4,8},{5,1},{8,12},{9,5},{12,14},{13,9},{14,10},{15,13... | collective-permute-start | bytes 196616 | tf_op jit(solution)/shard_map/ppermute | solution.py:33
  14.0 4.3 %collective-permute-start.4 = (bf16[2,128,128]{2,1,0:T(8,128)(2,1)S(1)}, bf16[2,128,128]{2,1,0:T(8,128)(2,1)S(1)}, u32[]{:S(2)}, u32[]{:S(2)}) collective-permute-start(bf16[2,128,128]{2,1,0:T(8,128)(2,1)S(1)} %collective-permute-done.2.refs_3_), channel_id=1, source_target_pairs={{0,1},{1,0},{2,3},{3,2},{4,5},{5,4},{6,7},{7,6},{8,9},{9,8},{10,11... | collective-permute-start | bytes 196616 | tf_op jit(solution)/shard_map/ppermute | solution.py:19
  14.0 5.8 %collective-permute-start.9 = (bf16[2,128,128]{2,1,0:T(8,128)(2,1)S(1)}, bf16[2,128,128]{2,1,0:T(8,128)(2,1)S(1)}, u32[]{:S(2)}, u32[]{:S(2)}) collective-permute-start(bf16[2,128,128]{2,1,0:T(8,128)(2,1)S(1)} %collective-permute-done.5.refs_6_), channel_id=1, source_target_pairs={{0,4},{1,3},{4,8},{5,1},{8,12},{9,5},{12,14},{13,9},{14,10},{15,13... | collective-permute-start | bytes 196616 | tf_op jit(solution)/shard_map/ppermute | solution.py:33
  15.5 5.5 %collective-permute-start.7 = (bf16[2,128,128]{2,1,0:T(8,128)(2,1)S(1)}, bf16[2,128,128]{2,1,0:T(8,128)(2,1)S(1)}, u32[]{:S(2)}, u32[]{:S(2)}) collective-permute-start(bf16[2,128,128]{2,1,0:T(8,128)(2,1)S(1)} %collective-permute-done.5.refs_6_), channel_id=1, source_target_pairs={{0,1},{1,0},{2,3},{3,2},{4,5},{5,4},{6,7},{7,6},{8,9},{9,8},{10,11... | collective-permute-start | bytes 196616 | tf_op jit(solution)/shard_map/ppermute | solution.py:19
  16.9 7.1 %collective-permute-start.20 = (bf16[4,128,128]{2,1,0:T(8,128)(2,1)S(1)}, bf16[4,128,128]{2,1,0:T(8,128)(2,1)S(1)}, u32[]{:S(2)}, u32[]{:S(2)}) collective-permute-start(bf16[4,128,128]{2,1,0:T(8,128)(2,1)S(1)} %collective-permute-done.16.refs_18_), channel_id=1, source_target_pairs={{0,4},{1,3},{4,8},{5,1},{8,12},{9,5},{12,14},{13,9},{14,10},{15,13... | collective-permute-start | bytes 393224 | tf_op jit(solution)/shard_map/ppermute | solution.py:33
  18.2 4.3 %collective-permute-start.10 = (bf16[2,128,128]{2,1,0:T(8,128)(2,1)S(1)}, bf16[2,128,128]{2,1,0:T(8,128)(2,1)S(1)}, u32[]{:S(2)}, u32[]{:S(2)}) collective-permute-start(bf16[2,128,128]{2,1,0:T(8,128)(2,1)S(1)} %collective-permute-done.6.refs_7_), channel_id=1, source_target_pairs={{0,4},{1,3},{4,8},{5,1},{8,12},{9,5},{12,14},{13,9},{14,10},{15,13... | collective-permute-start | bytes 196616 | tf_op jit(solution)/shard_map/ppermute | solution.py:33
  19.8 4.3 %collective-permute-start.8 = (bf16[2,128,128]{2,1,0:T(8,128)(2,1)S(1)}, bf16[2,128,128]{2,1,0:T(8,128)(2,1)S(1)}, u32[]{:S(2)}, u32[]{:S(2)}) collective-permute-start(bf16[2,128,128]{2,1,0:T(8,128)(2,1)S(1)} %collective-permute-done.6.refs_7_), channel_id=1, source_target_pairs={{0,1},{1,0},{2,3},{3,2},{4,5},{5,4},{6,7},{7,6},{8,9},{9,8},{10,11... | collective-permute-start | bytes 196616 | tf_op jit(solution)/shard_map/ppermute | solution.py:19
  19.8 8.5 %collective-permute-start.21 = (bf16[4,128,128]{2,1,0:T(8,128)(2,1)S(1)}, bf16[4,128,128]{2,1,0:T(8,128)(2,1)S(1)}, u32[]{:S(2)}, u32[]{:S(2)}) collective-permute-start(bf16[4,128,128]{2,1,0:T(8,128)(2,1)S(1)} %collective-permute-done.17.refs_19_), channel_id=1, source_target_pairs={{0,4},{1,3},{4,8},{5,1},{8,12},{9,5},{12,14},{13,9},{14,10},{15,13... | collective-permute-start | bytes 393224 | tf_op jit(solution)/shard_map/ppermute | solution.py:33
  21.0 8.7 %collective-permute-start.18 = (bf16[4,128,128]{2,1,0:T(8,128)(2,1)S(1)}, bf16[4,128,128]{2,1,0:T(8,128)(2,1)S(1)}, u32[]{:S(2)}, u32[]{:S(2)}) collective-permute-start(bf16[4,128,128]{2,1,0:T(8,128)(2,1)S(1)} %collective-permute-done.16.refs_18_), channel_id=1, source_target_pairs={{0,1},{1,0},{2,3},{3,2},{4,5},{5,4},{6,7},{7,6},{8,9},{9,8},{10,11... | collective-permute-start | bytes 393224 | tf_op jit(solution)/shard_map/ppermute | solution.py:19
  22.6 4.3 %collective-permute-start.13 = (bf16[2,128,128]{2,1,0:T(8,128)(2,1)S(1)}, bf16[2,128,128]{2,1,0:T(8,128)(2,1)S(1)}, u32[]{:S(2)}, u32[]{:S(2)}) collective-permute-start(bf16[2,128,128]{2,1,0:T(8,128)(2,1)S(1)} %collective-permute-done.9.refs_10_), channel_id=1, source_target_pairs={{0,4},{1,3},{4,8},{5,1},{8,12},{9,5},{12,14},{13,9},{14,10},{15,13... | collective-permute-start | bytes 196616 | tf_op jit(solution)/shard_map/ppermute | solution.py:33
  24.0 4.3 %collective-permute-start.11 = (bf16[2,128,128]{2,1,0:T(8,128)(2,1)S(1)}, bf16[2,128,128]{2,1,0:T(8,128)(2,1)S(1)}, u32[]{:S(2)}, u32[]{:S(2)}) collective-permute-start(bf16[2,128,128]{2,1,0:T(8,128)(2,1)S(1)} %collective-permute-done.9.refs_10_), channel_id=1, source_target_pairs={{0,1},{1,0},{2,3},{3,2},{4,5},{5,4},{6,7},{7,6},{8,9},{9,8},{10,11... | collective-permute-start | bytes 196616 | tf_op jit(solution)/shard_map/ppermute | solution.py:19
  24.0 7.1 %collective-permute-start.24 = (bf16[4,128,128]{2,1,0:T(8,128)(2,1)S(1)}, bf16[4,128,128]{2,1,0:T(8,128)(2,1)S(1)}, u32[]{:S(2)}, u32[]{:S(2)}) collective-permute-start(bf16[4,128,128]{2,1,0:T(8,128)(2,1)S(1)} %collective-permute-done.20.refs_22_), channel_id=1, source_target_pairs={{0,4},{1,3},{4,8},{5,1},{8,12},{9,5},{12,14},{13,9},{14,10},{15,13... | collective-permute-start | bytes 393224 | tf_op jit(solution)/shard_map/ppermute | solution.py:33
  26.8 4.3 %collective-permute-start.14 = (bf16[2,128,128]{2,1,0:T(8,128)(2,1)S(1)}, bf16[2,128,128]{2,1,0:T(8,128)(2,1)S(1)}, u32[]{:S(2)}, u32[]{:S(2)}) collective-permute-start(bf16[2,128,128]{2,1,0:T(8,128)(2,1)S(1)} %collective-permute-done.10.refs_11_), channel_id=1, source_target_pairs={{0,4},{1,3},{4,8},{5,1},{8,12},{9,5},{12,14},{13,9},{14,10},{15,13... | collective-permute-start | bytes 196616 | tf_op jit(solution)/shard_map/ppermute | solution.py:33
  28.3 4.3 %collective-permute-start.22 = (bf16[4,128,128]{2,1,0:T(8,128)(2,1)S(1)}, bf16[4,128,128]{2,1,0:T(8,128)(2,1)S(1)}, u32[]{:S(2)}, u32[]{:S(2)}) collective-permute-start(bf16[4,128,128]{2,1,0:T(8,128)(2,1)S(1)} %collective-permute-done.20.refs_22_), channel_id=1, source_target_pairs={{0,1},{1,0},{2,3},{3,2},{4,5},{5,4},{6,7},{7,6},{8,9},{9,8},{10,11... | collective-permute-start | bytes 393224 | tf_op jit(solution)/shard_map/ppermute | solution.py:19
  28.3 5.0 %collective-permute-start.25 = (bf16[4,128,128]{2,1,0:T(8,128)(2,1)S(1)}, bf16[4,128,128]{2,1,0:T(8,128)(2,1)S(1)}, u32[]{:S(2)}, u32[]{:S(2)}) collective-permute-start(bf16[4,128,128]{2,1,0:T(8,128)(2,1)S(1)} %collective-permute-done.21.refs_23_), channel_id=1, source_target_pairs={{0,4},{1,3},{4,8},{5,1},{8,12},{9,5},{12,14},{13,9},{14,10},{15,13... | collective-permute-start | bytes 393224 | tf_op jit(solution)/shard_map/ppermute | solution.py:33
  29.8 5.0 %collective-permute-start.19 = (bf16[4,128,128]{2,1,0:T(8,128)(2,1)S(1)}, bf16[4,128,128]{2,1,0:T(8,128)(2,1)S(1)}, u32[]{:S(2)}, u32[]{:S(2)}) collective-permute-start(bf16[4,128,128]{2,1,0:T(8,128)(2,1)S(1)} %collective-permute-done.17.refs_19_), channel_id=1, source_target_pairs={{0,1},{1,0},{2,3},{3,2},{4,5},{5,4},{6,7},{7,6},{8,9},{9,8},{10,11... | collective-permute-start | bytes 393224 | tf_op jit(solution)/shard_map/ppermute | solution.py:19
  31.1 1.5 %collective-permute-start.12 = (bf16[2,128,128]{2,1,0:T(8,128)(2,1)S(1)}, bf16[2,128,128]{2,1,0:T(8,128)(2,1)S(1)}, u32[]{:S(2)}, u32[]{:S(2)}) collective-permute-start(bf16[2,128,128]{2,1,0:T(8,128)(2,1)S(1)} %collective-permute-done.10.refs_11_), channel_id=1, source_target_pairs={{0,1},{1,0},{2,3},{3,2},{4,5},{5,4},{6,7},{7,6},{8,9},{9,8},{10,11... | collective-permute-start | bytes 196616 | tf_op jit(solution)/shard_map/ppermute | solution.py:19
  31.1 7.0 %collective-permute-start.28 = (bf16[4,128,128]{2,1,0:T(8,128)(2,1)S(1)}, bf16[4,128,128]{2,1,0:T(8,128)(2,1)S(1)}, u32[]{:S(2)}, u32[]{:S(2)}) collective-permute-start(bf16[4,128,128]{2,1,0:T(8,128)(2,1)S(1)} %collective-permute-done.24.refs_26_), channel_id=1, source_target_pairs={{0,4},{1,3},{4,8},{5,1},{8,12},{9,5},{12,14},{13,9},{14,10},{15,13... | collective-permute-start | bytes 393224 | tf_op jit(solution)/shard_map/ppermute | solution.py:33
  32.6 5.6 %collective-permute-start.26 = (bf16[4,128,128]{2,1,0:T(8,128)(2,1)S(1)}, bf16[4,128,128]{2,1,0:T(8,128)(2,1)S(1)}, u32[]{:S(2)}, u32[]{:S(2)}) collective-permute-start(bf16[4,128,128]{2,1,0:T(8,128)(2,1)S(1)} %collective-permute-done.24.refs_26_), channel_id=1, source_target_pairs={{0,1},{1,0},{2,3},{3,2},{4,5},{5,4},{6,7},{7,6},{8,9},{9,8},{10,11... | collective-permute-start | bytes 393224 | tf_op jit(solution)/shard_map/ppermute | solution.py:19
  32.6 5.6 %collective-permute-start.23 = (bf16[4,128,128]{2,1,0:T(8,128)(2,1)S(1)}, bf16[4,128,128]{2,1,0:T(8,128)(2,1)S(1)}, u32[]{:S(2)}, u32[]{:S(2)}) collective-permute-start(bf16[4,128,128]{2,1,0:T(8,128)(2,1)S(1)} %collective-permute-done.21.refs_23_), channel_id=1, source_target_pairs={{0,1},{1,0},{2,3},{3,2},{4,5},{5,4},{6,7},{7,6},{8,9},{9,8},{10,11... | collective-permute-start | bytes 393224 | tf_op jit(solution)/shard_map/ppermute | solution.py:19
  33.3 5.0 %collective-permute-start.29 = (bf16[4,128,128]{2,1,0:T(8,128)(2,1)S(1)}, bf16[4,128,128]{2,1,0:T(8,128)(2,1)S(1)}, u32[]{:S(2)}, u32[]{:S(2)}) collective-permute-start(bf16[4,128,128]{2,1,0:T(8,128)(2,1)S(1)} %collective-permute-done.25.refs_27_), channel_id=1, source_target_pairs={{0,4},{1,3},{4,8},{5,1},{8,12},{9,5},{12,14},{13,9},{14,10},{15,13... | collective-permute-start | bytes 393224 | tf_op jit(solution)/shard_map/ppermute | solution.py:33
  34.7 3.6 %collective-permute-start.27 = (bf16[4,128,128]{2,1,0:T(8,128)(2,1)S(1)}, bf16[4,128,128]{2,1,0:T(8,128)(2,1)S(1)}, u32[]{:S(2)}, u32[]{:S(2)}) collective-permute-start(bf16[4,128,128]{2,1,0:T(8,128)(2,1)S(1)} %collective-permute-done.25.refs_27_), channel_id=1, source_target_pairs={{0,1},{1,0},{2,3},{3,2},{4,5},{5,4},{6,7},{7,6},{8,9},{9,8},{10,11... | collective-permute-start | bytes 393224 | tf_op jit(solution)/shard_map/ppermute | solution.py:19
  50.6 4.0 %collective-permute-start.30 = (bf16[2064,128]{1,0:T(8,128)(2,1)S(1)}, bf16[2064,128]{1,0:T(8,128)(2,1)S(1)}, u32[]{:S(2)}, u32[]{:S(2)}) collective-permute-start(bf16[2064,128]{1,0:T(8,128)(2,1)S(1)} %get-tuple-element.41), channel_id=1, source_target_pairs={{0,1},{1,0},{2,3},{3,2},{4,5},{5,4},{6,7},{7,6},{8,9},{9,8},{10,11... | collective-permute-start | bytes 1585160 | tf_op jit(solution)/shard_map/ppermute | solution.py:19
  54.8 7.7 %collective-permute-start.31 = (bf16[272,128]{1,0:T(8,128)(2,1)S(1)}, bf16[272,128]{1,0:T(8,128)(2,1)S(1)}, u32[]{:S(2)}, u32[]{:S(2)}) collective-permute-start(bf16[272,128]{1,0:T(8,128)(2,1)S(1)} %get-tuple-element.44), channel_id=1, source_target_pairs={{0,14},{1,15},{2,12},{3,13},{4,10},{5,11},{6,8},{7,9},{8,6},{9,7},... | collective-permute-start | bytes 208904 | tf_op jit(solution)/shard_map/ppermute | solution.py:19
  55.5 12.7 %collective-permute-start.32 = (bf16[272,128]{1,0:T(8,128)(2,1)S(1)}, bf16[272,128]{1,0:T(8,128)(2,1)S(1)}, u32[]{:S(2)}, u32[]{:S(2)}) collective-permute-start(bf16[272,128]{1,0:T(8,128)(2,1)S(1)} %get-tuple-element.45), channel_id=1, source_target_pairs={{0,12},{1,13},{2,14},{3,15},{4,8},{5,9},{6,10},{7,11},{8,4},{9,5},... | collective-permute-start | bytes 208904 | tf_op jit(solution)/shard_map/ppermute | solution.py:19
  57.8 12.7 %collective-permute-start.33 = (bf16[272,128]{1,0:T(8,128)(2,1)S(1)}, bf16[272,128]{1,0:T(8,128)(2,1)S(1)}, u32[]{:S(2)}, u32[]{:S(2)}) collective-permute-start(bf16[272,128]{1,0:T(8,128)(2,1)S(1)} %get-tuple-element.46), channel_id=1, source_target_pairs={{0,10},{1,11},{2,8},{3,9},{4,14},{5,15},{6,12},{7,13},{8,2},{9,3},... | collective-permute-start | bytes 208904 | tf_op jit(solution)/shard_map/ppermute | solution.py:19
  58.9 11.7 %collective-permute-start.34 = (bf16[272,128]{1,0:T(8,128)(2,1)S(1)}, bf16[272,128]{1,0:T(8,128)(2,1)S(1)}, u32[]{:S(2)}, u32[]{:S(2)}) collective-permute-start(bf16[272,128]{1,0:T(8,128)(2,1)S(1)} %get-tuple-element.47), channel_id=1, source_target_pairs={{0,8},{1,9},{2,10},{3,11},{4,12},{5,13},{6,14},{7,15},{8,0},{9,1},... | collective-permute-start | bytes 208904 | tf_op jit(solution)/shard_map/ppermute | solution.py:19
  62.5 8.0 %collective-permute-start.35 = (bf16[272,128]{1,0:T(8,128)(2,1)S(1)}, bf16[272,128]{1,0:T(8,128)(2,1)S(1)}, u32[]{:S(2)}, u32[]{:S(2)}) collective-permute-start(bf16[272,128]{1,0:T(8,128)(2,1)S(1)} %get-tuple-element.48), channel_id=1, source_target_pairs={{0,6},{1,7},{2,4},{3,5},{4,2},{5,3},{6,0},{7,1},{8,14},{9,15},{10,... | collective-permute-start | bytes 208904 | tf_op jit(solution)/shard_map/ppermute | solution.py:19
  62.5 8.7 %collective-permute-start.36 = (bf16[272,128]{1,0:T(8,128)(2,1)S(1)}, bf16[272,128]{1,0:T(8,128)(2,1)S(1)}, u32[]{:S(2)}, u32[]{:S(2)}) collective-permute-start(bf16[272,128]{1,0:T(8,128)(2,1)S(1)} %get-tuple-element.49), channel_id=1, source_target_pairs={{0,4},{1,5},{2,6},{3,7},{4,0},{5,1},{6,2},{7,3},{8,12},{9,13},{10,... | collective-permute-start | bytes 208904 | tf_op jit(solution)/shard_map/ppermute | solution.py:19
  68.2 4.3 %collective-permute-start.37 = (bf16[272,128]{1,0:T(8,128)(2,1)S(1)}, bf16[272,128]{1,0:T(8,128)(2,1)S(1)}, u32[]{:S(2)}, u32[]{:S(2)}) collective-permute-start(bf16[272,128]{1,0:T(8,128)(2,1)S(1)} %get-tuple-element.50), channel_id=1, source_target_pairs={{0,2},{1,3},{2,0},{3,1},{4,6},{5,7},{6,4},{7,5},{8,10},{9,11},{10,... | collective-permute-start | bytes 208904 | tf_op jit(solution)/shard_map/ppermute | solution.py:19

commit v11 on v9

--- a/solution.py
+++ b/solution.py
@@ -250,7 +250,7 @@
 
 def tasks_kernel(n, kinds, plan_ref, left_ref, *refs):
     blocks, refs = refs[: len(kinds)], refs[len(kinds) :]
-    send_ref, keep_ref, own_ref, halves, trial, right, acc, block_sem, *fetched = refs
+    send_ref, acc, own_ref, halves, trial, right, block_sem, *fetched = refs
     start, products = make_halves(n, plan_ref, left_ref, trial, halves, fetched)
     right[right.shape[0] - 1] = jnp.zeros((128, 128), jnp.bfloat16)
     start()
@@ -291,8 +291,10 @@
                 ],
                 axis=0,
             )
-            rights = jnp.concatenate([right[plan_ref[3, place]], right[plan_ref[3, place + 1]]], axis=0)
-            term = jnp.dot(pair, rights, preferred_element_type=jnp.float32)
+            rights = jnp.concatenate([right[plan_ref[3, place]], right[plan_ref[3, place + 1]]], axis=1)
+            term = lax.dot_general(
+                pair, rights, (((1,), (1,)), ((), ())), preferred_element_type=jnp.float32
+            )
             target = plan_ref[4, place]
             acc[target] = acc[target] + term
         return carry
@@ -309,16 +311,15 @@
         return p00 + fold(t0 * a0), p01 + fold(t0 * a1), p10 + fold(t1 * a0), p11 + fold(t1 * a1)
 
     zero = jnp.zeros((8, 128), jnp.float32)
-    sums = lax.fori_loop(0, n, dots, (zero,) * 4)
+    sums = lax.fori_loop(0, n, dots, (zero,) * 4, unroll=4)
     p00, p01, p10, p11 = [jnp.sum(x) for x in sums]
 
     def pack(j, carry):
         mine = jnp.bitwise_xor(me, 2 * j)
-        keep_ref[j] = acc[mine]
         send_ref[pl.ds(pl.multiple_of(j * 256, 256), 256), :] = acc[jnp.bitwise_xor(mine, 1)].astype(jnp.bfloat16)
         return carry
 
-    lax.fori_loop(0, n // 2, pack, 0)
+    lax.fori_loop(0, n // 2, pack, 0, unroll=2)
     own = split3(matrix_of({(0, 0): p00, (0, 1): p01, (1, 0): p10, (1, 1): p11}, 3))
     own_ref[...] = own
     send_ref[n // 2 * 256 :, :] = tail_of(own, jnp.zeros_like(own))
@@ -338,7 +339,7 @@
         functools.partial(tasks_kernel, n, kinds),
         out_shape=(
             jax.ShapeDtypeStruct((n // 2 * 256 + TAIL, 128), jnp.bfloat16),
-            jax.ShapeDtypeStruct((n // 2, 256, 128), jnp.float32),
+            jax.ShapeDtypeStruct((n + 1, 256, 128), jnp.float32),
             jax.ShapeDtypeStruct((8, 128), jnp.float32),
         ),
         in_specs=[pl.BlockSpec(memory_space=pltpu.SMEM)] + [given] * (1 + len(blocks)),
@@ -347,7 +348,6 @@
             pltpu.VMEM((source_places(slots, n), 2, 128, 128), jnp.bfloat16),
             pltpu.VMEM((n, TRIALS, 128, 128), jnp.bfloat16),
             pltpu.VMEM((n * terms_per + 1, 128, 128), jnp.bfloat16),
-            pltpu.VMEM((n + 1, 256, 128), jnp.float32),
             pltpu.SemaphoreType.DMA((len(blocks), 2)),
         ]
         + fetched,
@@ -358,31 +358,6 @@
     )(plan, left_ops, *[block[0] for block in blocks])
 
 
-def join_kernel(trial_ref, right_ref, block_ref, right, sem):
-    copies = [
-        pltpu.make_async_copy(right_ref, right, sem.at[0]),
-        pltpu.make_async_copy(trial_ref.at[0], block_ref.at[pl.ds(0, TRIALS)], sem.at[1]),
-    ]
-    for copy in copies:
-        copy.start()
-    copies[0].wait()
-    for k in range(right.shape[0]):
-        block_ref[TRIALS + k] = jnp.transpose(right[k])
-    copies[1].wait()
-
-
-def join(trial, right_ops):
-    hbm = pl.BlockSpec(memory_space=pltpu.HBM)
-    return pl.pallas_call(
-        join_kernel,
-        out_shape=jax.ShapeDtypeStruct((TRIALS + right_ops.shape[0], 128, 128), jnp.bfloat16),
-        in_specs=[hbm, hbm],
-        out_specs=pl.BlockSpec(memory_space=pltpu.VMEM),
-        scratch_shapes=[pltpu.VMEM(right_ops.shape, jnp.bfloat16), pltpu.SemaphoreType.DMA((2,))],
-        compiler_params=pltpu.CompilerParams(vmem_limit_bytes=59 * MIB),
-    )(trial, right_ops)
-
-
 def corr_kernel(*refs):
     blocks, corr_ref = refs[:-1], refs[-1]
     total = [jnp.zeros((8, 128), jnp.float32)] * 3
@@ -405,8 +380,9 @@
     total = jnp.concatenate([own_ref[...], received_ref[chips * 256 :, :].astype(jnp.float32)[0:8]], axis=0)
     total_ref[...] = total
     tail = total.astype(jnp.bfloat16)
+    me = lax.axis_index("op")
     for j in range(chips):
-        value = keep_ref[j] + received_ref[j * 256 : (j + 1) * 256, :].astype(jnp.float32)
+        value = keep_ref[jnp.bitwise_xor(me, 2 * j)] + received_ref[j * 256 : (j + 1) * 256, :].astype(jnp.float32)
         if j == 0:
             mine_ref[...] = value
         else:
@@ -415,7 +391,7 @@
 
 
 def add_chip(keep, own, received):
-    chips = keep.shape[0]
+    chips = keep.shape[0] // 2
     return pl.pallas_call(
         functools.partial(chip_kernel, chips),
         out_shape=(jax.ShapeDtypeStruct((256, 128), jnp.float32), jax.ShapeDtypeStruct((16, 128), jnp.float32))
@@ -449,7 +425,7 @@
 
 def body(n, trial, left_ops, right_ops, task_list):
     steps = n // 4
-    own = join(trial, right_ops)
+    own = jnp.concatenate([trial[0], right_ops], axis=0)
     plan = make_plan(task_list.T, n, n * right_ops.shape[0])
     left_ops = stage(left_ops, n)
     lines = [own, exchange(own, n, 1)]

time: 62.5 us -> 61.9 us (level); the launches traced: 62.7 us -> 61.2 us
  Pallas kernels: 21 us -> 18.4 us
  starting transfers between devices: 32 us -> 33.1 us
  other arithmetic: 0 us -> 0.93 us
  waiting for transfers between devices: 8.32 us -> 7.41 us
    pallas_call x1 -> x0, Pallas kernels: 1.68 us -> none  [join(): pl.pallas_call(join_kernel, out_shape=jax.ShapeDtypeStruct((TRIALS + righ...]
    ppermute x15, starting transfers between devices: 15.4 us -> 16.5 us  [exchange(): return lax.ppermute(value, 'op', [(i, i ^ mask) for i in range(n)])]
    concatenate x0 -> x1, other arithmetic: none -> 0.93 us  [body(): own = jnp.concatenate([trial[0], right_ops], axis=0)]
    pallas_call x1, Pallas kernels: 13.1 us -> 12.2 us  [run_tasks(): pl.pallas_call(functools.partial(tasks_kernel, n, kinds), out_shape=(jax....]
    ppermute x15, waiting for transfers between devices: 5.06 us -> 4.35 us  [exchange(): return lax.ppermute(value, 'op', [(i, i ^ mask) for i in range(n)])]
  transfers between devices with their start and end apart: 23 -> 23, of which waited for: 8 -> 7; matrix products, arithmetic and copies ran while one was open for 0% -> 0% of each run, Pallas kernels for 9% -> 9%
where the time goes in v11:
time: 61.9 us; the launch traced here: 61.2 us
  starting transfers between devices  33.1 us (53%)
  Pallas kernels  18.4 us (30%)
  waiting for transfers between devices  7.41 us (12%)
  other arithmetic  0.93 us (2%)
  between operations  0.71 us (1%)
  local copies, waits for them, and re-layouts  0.69 us (1%)
    ppermute x8, starting transfers between devices, ring_step(): return lax.ppermute(value, 'op', pairs)  16.7 us
    ppermute x15, starting transfers between devices, exchange(): return lax.ppermute(value, 'op', [(i, i ^ mask) for i in range(n)])  16.5 us
    pallas_call x1, Pallas kernels, run_tasks(): pl.pallas_call(functools.partial(tasks_kernel, n, kinds), out_shape=(jax....  12.2 us
    ppermute x15, waiting for transfers between devices, exchange(): return lax.ppermute(value, 'op', [(i, i ^ mask) for i in range(n)])  4.35 us
    pallas_call x1, Pallas kernels, stage(): pl.pallas_call(stage_kernel, in_specs=[pl.BlockSpec(memory_space=pltpu.HB...  3.39 us
    ppermute x8, waiting for transfers between devices, ring_step(): return lax.ppermute(value, 'op', pairs)  3.07 us
  transfers between devices with their start and end apart: 23, of which 7 were waited for; matrix products, arithmetic and copies ran while one was open for 0% of the time, Pallas kernels for 9%

profile of v11, /device:TPU:0, one launch (start us, length us, event | category | flops | bytes accessed | tf_op | source)
XLA Modules:
  0.0 61.2 jit_solution(3944633903306239367)
XLA Ops:
  0.6 0.9 %pad_maximum_fusion.refs_0_ = bf16[6,128,128]{2,1,0:T(8,128)(2,1)S(1)} fusion(bf16[4,128,128]{2,1,0:T(8,128)(2,1)} %param.6, bf16[2,128,128]{2,1,0:T(8,128)(2,1)} %bitcast.3), kind=kLoop, calls=%fused_computation | loop fusion | flops 98304 | bytes 393216 | tf_op jit(solution)/shard_map/concatenate | solution.py:428
  1.6 0.5 collective-permute-start.1
  2.1 2.6 %collective-permute-start = (bf16[6,128,128]{2,1,0:T(8,128)(2,1)S(1)}, bf16[6,128,128]{2,1,0:T(8,128)(2,1)S(1)}, u32[]{:S(2)}, u32[]{:S(2)}) collective-permute-start(bf16[6,128,128]{2,1,0:T(8,128)(2,1)S(1)} %pad_maximum_fusion.refs_0_), channel_id=1, source_target_pairs={{0,4},{1,3},{4,8},{5,1},{8,12},{9,5},{12,14},{13,9},{14,10},{15,13... | collective-permute-start | bytes 589832 | tf_op jit(solution)/shard_map/ppermute | solution.py:33
  4.7 0.0 collective-permute-done.1.refs_1_
  4.7 1.6 %collective-permute-start.2 = (bf16[6,128,128]{2,1,0:T(8,128)(2,1)S(1)}, bf16[6,128,128]{2,1,0:T(8,128)(2,1)S(1)}, u32[]{:S(2)}, u32[]{:S(2)}) collective-permute-start(bf16[6,128,128]{2,1,0:T(8,128)(2,1)S(1)} %collective-permute-done.1.refs_1_), channel_id=1, source_target_pairs={{0,4},{1,3},{4,8},{5,1},{8,12},{9,5},{12,14},{13,9},{14,10},{15,13... | collective-permute-start | bytes 589832 | tf_op jit(solution)/shard_map/ppermute | solution.py:33
  6.3 0.0 copy-start
  6.3 0.7 %copy-done = s32[256,4]{0,1:T(4,128)S(1)} copy-done((s32[256,4]{0,1:T(4,128)S(1)}, s32[256,4]{0,1:T(4,128)}, u32[]{:S(2)}) %copy-start) | copy-done | bytes 4120
  7.0 1.0 %shard_map.67.plan_ref = s32[8,512]{1,0:T(8,128)S(1)} custom-call(s32[4,256]{1,0:T(4,128)S(1)} %bitcast.2), custom_call_target="tpu_custom_call" | custom-call | tf_op jit(solution)/shard_map/pallas_call | solution.py:167
  8.0 0.3 collective-permute-done.refs_2_
  8.3 2.1 %collective-permute-start.5 = (bf16[6,128,128]{2,1,0:T(8,128)(2,1)S(1)}, bf16[6,128,128]{2,1,0:T(8,128)(2,1)S(1)}, u32[]{:S(2)}, u32[]{:S(2)}) collective-permute-start(bf16[6,128,128]{2,1,0:T(8,128)(2,1)S(1)} %collective-permute-done.refs_2_), channel_id=1, source_target_pairs={{0,4},{1,3},{4,8},{5,1},{8,12},{9,5},{12,14},{13,9},{14,10},{15,13... | collective-permute-start | bytes 589832 | tf_op jit(solution)/shard_map/ppermute | solution.py:33
  10.4 0.0 collective-permute-done.2.refs_3_
  10.4 2.1 %collective-permute-start.6 = (bf16[6,128,128]{2,1,0:T(8,128)(2,1)S(1)}, bf16[6,128,128]{2,1,0:T(8,128)(2,1)S(1)}, u32[]{:S(2)}, u32[]{:S(2)}) collective-permute-start(bf16[6,128,128]{2,1,0:T(8,128)(2,1)S(1)} %collective-permute-done.2.refs_3_), channel_id=1, source_target_pairs={{0,4},{1,3},{4,8},{5,1},{8,12},{9,5},{12,14},{13,9},{14,10},{15,13... | collective-permute-start | bytes 589832 | tf_op jit(solution)/shard_map/ppermute | solution.py:33
  12.5 0.0 collective-permute-start.3
  12.5 1.5 %collective-permute-done.5.refs_6_ = bf16[6,128,128]{2,1,0:T(8,128)(2,1)S(1)} collective-permute-done((bf16[6,128,128]{2,1,0:T(8,128)(2,1)S(1)}, bf16[6,128,128]{2,1,0:T(8,128)(2,1)S(1)}, u32[]{:S(2)}, u32[]{:S(2)}) %collective-permute-start.5) | collective-permute-done | bytes 196640 | tf_op jit(solution)/shard_map/ppermute | solution.py:33
  14.0 2.1 %collective-permute-start.9 = (bf16[6,128,128]{2,1,0:T(8,128)(2,1)S(1)}, bf16[6,128,128]{2,1,0:T(8,128)(2,1)S(1)}, u32[]{:S(2)}, u32[]{:S(2)}) collective-permute-start(bf16[6,128,128]{2,1,0:T(8,128)(2,1)S(1)} %collective-permute-done.5.refs_6_), channel_id=1, source_target_pairs={{0,4},{1,3},{4,8},{5,1},{8,12},{9,5},{12,14},{13,9},{14,10},{15,13... | collective-permute-start | bytes 589832 | tf_op jit(solution)/shard_map/ppermute | solution.py:33
  16.1 0.0 collective-permute-start.4
  16.1 0.0 collective-permute-done.6.refs_7_
  16.1 2.1 %collective-permute-start.10 = (bf16[6,128,128]{2,1,0:T(8,128)(2,1)S(1)}, bf16[6,128,128]{2,1,0:T(8,128)(2,1)S(1)}, u32[]{:S(2)}, u32[]{:S(2)}) collective-permute-start(bf16[6,128,128]{2,1,0:T(8,128)(2,1)S(1)} %collective-permute-done.6.refs_7_), channel_id=1, source_target_pairs={{0,4},{1,3},{4,8},{5,1},{8,12},{9,5},{12,14},{13,9},{14,10},{15,13... | collective-permute-start | bytes 589832 | tf_op jit(solution)/shard_map/ppermute | solution.py:33
  18.2 0.0 collective-permute-start.7
  18.2 0.0 collective-permute-done.3.refs_4_
  18.2 0.5 collective-permute-start.8
  18.7 1.0 %collective-permute-done.9.refs_10_ = bf16[6,128,128]{2,1,0:T(8,128)(2,1)S(1)} collective-permute-done((bf16[6,128,128]{2,1,0:T(8,128)(2,1)S(1)}, bf16[6,128,128]{2,1,0:T(8,128)(2,1)S(1)}, u32[]{:S(2)}, u32[]{:S(2)}) %collective-permute-start.9) | collective-permute-done | bytes 196640 | tf_op jit(solution)/shard_map/ppermute | solution.py:33
  19.6 2.1 %collective-permute-start.13 = (bf16[6,128,128]{2,1,0:T(8,128)(2,1)S(1)}, bf16[6,128,128]{2,1,0:T(8,128)(2,1)S(1)}, u32[]{:S(2)}, u32[]{:S(2)}) collective-permute-start(bf16[6,128,128]{2,1,0:T(8,128)(2,1)S(1)} %collective-permute-done.9.refs_10_), channel_id=1, source_target_pairs={{0,4},{1,3},{4,8},{5,1},{8,12},{9,5},{12,14},{13,9},{14,10},{15,13... | collective-permute-start | bytes 589832 | tf_op jit(solution)/shard_map/ppermute | solution.py:33
  21.7 0.0 collective-permute-done.4.refs_5_
  21.7 0.0 collective-permute-start.11
  21.7 0.0 collective-permute-done.10.refs_11_
  21.8 2.1 %collective-permute-start.14 = (bf16[6,128,128]{2,1,0:T(8,128)(2,1)S(1)}, bf16[6,128,128]{2,1,0:T(8,128)(2,1)S(1)}, u32[]{:S(2)}, u32[]{:S(2)}) collective-permute-start(bf16[6,128,128]{2,1,0:T(8,128)(2,1)S(1)} %collective-permute-done.10.refs_11_), channel_id=1, source_target_pairs={{0,4},{1,3},{4,8},{5,1},{8,12},{9,5},{12,14},{13,9},{14,10},{15,13... | collective-permute-start | bytes 589832 | tf_op jit(solution)/shard_map/ppermute | solution.py:33
  23.8 0.0 collective-permute-done.7.refs_8_
  23.8 0.0 collective-permute-start.12
  23.8 3.4 %shard_map.68.left_ref = bf16[256,128,128]{2,1,0:T(8,128)(2,1)S(1)} custom-call(bf16[256,128,128]{2,1,0:T(8,128)(2,1)} %left_ref.1), custom_call_target="tpu_custom_call" | custom-call | tf_op jit(solution)/shard_map/pallas_call | solution.py:183
  27.2 0.0 collective-permute-done.8.refs_9_
  27.2 0.0 collective-permute-done.13.refs_14_
  27.3 0.0 collective-permute-done.11.refs_12_
  27.3 0.2 collective-permute-done.14.refs_15_
  27.5 0.0 collective-permute-done.12.refs_13_
  27.5 12.2 %shard_map.69 = (bf16[2064,128]{1,0:T(8,128)(2,1)S(1)}, f32[17,256,128]{2,1,0:T(8,128)S(1)}, f32[8,128]{1,0:T(8,128)S(1)}) custom-call(s32[8,512]{1,0:T(8,128)S(1)} %shard_map.67.plan_ref, bf16[256,128,128]{2,1,0:T(8,128)(2,1)S(1)} %shard_map.68.left_ref, bf16[6,128,128]{2,1,0:T(8,128)(2,1)S(1)} %pad_maximum_fusion.refs_0_, ...), custom_call_target="tpu_custom_call" | custom-call | flops 4294967296 | bytes 15588608 | tf_op jit(solution)/shard_map/pallas_call | solution.py:338
  39.6 0.4 collective-permute-start.15
  40.0 1.6 %collective-permute-done.15.received_ref = bf16[2064,128]{1,0:T(8,128)(2,1)S(1)} collective-permute-done((bf16[2064,128]{1,0:T(8,128)(2,1)S(1)}, bf16[2064,128]{1,0:T(8,128)(2,1)S(1)}, u32[]{:S(2)}, u32[]{:S(2)}) %collective-permute-start.15) | collective-permute-done | bytes 528416 | tf_op jit(solution)/shard_map/ppermute | solution.py:19
  41.6 0.1 shard_map.70
  41.7 3.5 %collective-permute-start.16 = (bf16[272,128]{1,0:T(8,128)(2,1)S(1)}, bf16[272,128]{1,0:T(8,128)(2,1)S(1)}, u32[]{:S(2)}, u32[]{:S(2)}) collective-permute-start(bf16[272,128]{1,0:T(8,128)(2,1)S(1)} %get-tuple-element.44), channel_id=1, source_target_pairs={{0,14},{1,15},{2,12},{3,13},{4,10},{5,11},{6,8},{7,9},{8,6},{9,7},... | collective-permute-start | bytes 208904 | tf_op jit(solution)/shard_map/ppermute | solution.py:19
  45.2 2.2 %collective-permute-start.17 = (bf16[272,128]{1,0:T(8,128)(2,1)S(1)}, bf16[272,128]{1,0:T(8,128)(2,1)S(1)}, u32[]{:S(2)}, u32[]{:S(2)}) collective-permute-start(bf16[272,128]{1,0:T(8,128)(2,1)S(1)} %get-tuple-element.45), channel_id=1, source_target_pairs={{0,12},{1,13},{2,14},{3,15},{4,8},{5,9},{6,10},{7,11},{8,4},{9,5},... | collective-permute-start | bytes 208904 | tf_op jit(solution)/shard_map/ppermute | solution.py:19
  47.4 1.9 %collective-permute-start.18 = (bf16[272,128]{1,0:T(8,128)(2,1)S(1)}, bf16[272,128]{1,0:T(8,128)(2,1)S(1)}, u32[]{:S(2)}, u32[]{:S(2)}) collective-permute-start(bf16[272,128]{1,0:T(8,128)(2,1)S(1)} %get-tuple-element.46), channel_id=1, source_target_pairs={{0,10},{1,11},{2,8},{3,9},{4,14},{5,15},{6,12},{7,13},{8,2},{9,3},... | collective-permute-start | bytes 208904 | tf_op jit(solution)/shard_map/ppermute | solution.py:19
  49.3 1.9 %collective-permute-start.19 = (bf16[272,128]{1,0:T(8,128)(2,1)S(1)}, bf16[272,128]{1,0:T(8,128)(2,1)S(1)}, u32[]{:S(2)}, u32[]{:S(2)}) collective-permute-start(bf16[272,128]{1,0:T(8,128)(2,1)S(1)} %get-tuple-element.47), channel_id=1, source_target_pairs={{0,8},{1,9},{2,10},{3,11},{4,12},{5,13},{6,14},{7,15},{8,0},{9,1},... | collective-permute-start | bytes 208904 | tf_op jit(solution)/shard_map/ppermute | solution.py:19
  51.2 1.5 %collective-permute-start.20 = (bf16[272,128]{1,0:T(8,128)(2,1)S(1)}, bf16[272,128]{1,0:T(8,128)(2,1)S(1)}, u32[]{:S(2)}, u32[]{:S(2)}) collective-permute-start(bf16[272,128]{1,0:T(8,128)(2,1)S(1)} %get-tuple-element.48), channel_id=1, source_target_pairs={{0,6},{1,7},{2,4},{3,5},{4,2},{5,3},{6,0},{7,1},{8,14},{9,15},{10,... | collective-permute-start | bytes 208904 | tf_op jit(solution)/shard_map/ppermute | solution.py:19
  52.6 0.0 collective-permute-done.16.refs_0_
  52.6 1.3 %collective-permute-start.21 = (bf16[272,128]{1,0:T(8,128)(2,1)S(1)}, bf16[272,128]{1,0:T(8,128)(2,1)S(1)}, u32[]{:S(2)}, u32[]{:S(2)}) collective-permute-start(bf16[272,128]{1,0:T(8,128)(2,1)S(1)} %get-tuple-element.49), channel_id=1, source_target_pairs={{0,4},{1,5},{2,6},{3,7},{4,0},{5,1},{6,2},{7,3},{8,12},{9,13},{10,... | collective-permute-start | bytes 208904 | tf_op jit(solution)/shard_map/ppermute | solution.py:19
  53.9 0.0 collective-permute-done.17.refs_1_
  53.9 2.8 %collective-permute-start.22 = (bf16[272,128]{1,0:T(8,128)(2,1)S(1)}, bf16[272,128]{1,0:T(8,128)(2,1)S(1)}, u32[]{:S(2)}, u32[]{:S(2)}) collective-permute-start(bf16[272,128]{1,0:T(8,128)(2,1)S(1)} %get-tuple-element.50), channel_id=1, source_target_pairs={{0,2},{1,3},{2,0},{3,1},{4,6},{5,7},{6,4},{7,5},{8,10},{9,11},{10,... | collective-permute-start | bytes 208904 | tf_op jit(solution)/shard_map/ppermute | solution.py:19
  56.7 1.0 %shard_map.72 = f32[2,2]{1,0:T(2,128)} custom-call(bf16[6,128,128]{2,1,0:T(8,128)(2,1)S(1)} %pad_maximum_fusion.refs_0_, bf16[6,128,128]{2,1,0:T(8,128)(2,1)S(1)} %collective-permute-done.1.refs_1_, bf16[6,128,128]{2,1,0:T(8,128)(2,1)S(1)} %collective-permute-done.refs_2_, bf16[6,128,128]{2,1,0:T(8,128)(2,1)S(1)} %collective-permute-done.2.refs_3_, ...), custom_call_target="tpu_custom_call" | custom-call | tf_op jit(solution)/shard_map/pallas_call | solution.py:372
  57.7 1.2 %collective-permute-done.18.refs_2_ = bf16[272,128]{1,0:T(8,128)(2,1)S(1)} collective-permute-done((bf16[272,128]{1,0:T(8,128)(2,1)S(1)}, bf16[272,128]{1,0:T(8,128)(2,1)S(1)}, u32[]{:S(2)}, u32[]{:S(2)}) %collective-permute-start.18) | collective-permute-done | bytes 69664 | tf_op jit(solution)/shard_map/ppermute | solution.py:19
  58.9 1.6 %collective-permute-done.19.refs_3_ = bf16[272,128]{1,0:T(8,128)(2,1)S(1)} collective-permute-done((bf16[272,128]{1,0:T(8,128)(2,1)S(1)}, bf16[272,128]{1,0:T(8,128)(2,1)S(1)}, u32[]{:S(2)}, u32[]{:S(2)}) %collective-permute-start.19) | collective-permute-done | bytes 69664 | tf_op jit(solution)/shard_map/ppermute | solution.py:19
  60.5 0.0 collective-permute-done.20.refs_4_
  60.5 0.0 collective-permute-done.21.refs_5_
  60.5 0.0 collective-permute-done.22.refs_6_
  60.5 0.7 %shard_map.71 = (f32[1,2,128,128]{3,2,1,0:T(8,128)}, f32[2,2]{1,0:T(2,128)}) custom-call(f32[256,128]{1,0:T(8,128)S(1)} %get-tuple-element.42.mine_ref, f32[16,128]{1,0:T(8,128)S(1)} %get-tuple-element.43.total_ref, bf16[272,128]{1,0:T(8,128)(2,1)S(1)} %collective-permute-done.16.refs_0_, bf16[272,128]{1,0:T(8,128)(2,1)S(1)} %collective-permute-done.17.refs_1_, ...), custom_call_target="tpu_custom_call" | custom-call | tf_op jit(solution)/shard_map/pallas_call | solution.py:416
Async XLA Ops:
  1.6 3.2 %collective-permute-start.1 = (bf16[6,128,128]{2,1,0:T(8,128)(2,1)S(1)}, bf16[6,128,128]{2,1,0:T(8,128)(2,1)S(1)}, u32[]{:S(2)}, u32[]{:S(2)}) collective-permute-start(bf16[6,128,128]{2,1,0:T(8,128)(2,1)S(1)} %pad_maximum_fusion.refs_0_), channel_id=1, source_target_pairs={{0,1},{1,0},{2,3},{3,2},{4,5},{5,4},{6,7},{7,6},{8,9},{9,8},{10,11... | collective-permute-start | bytes 589832 | tf_op jit(solution)/shard_map/ppermute | solution.py:19
  2.1 6.2 %collective-permute-start = (bf16[6,128,128]{2,1,0:T(8,128)(2,1)S(1)}, bf16[6,128,128]{2,1,0:T(8,128)(2,1)S(1)}, u32[]{:S(2)}, u32[]{:S(2)}) collective-permute-start(bf16[6,128,128]{2,1,0:T(8,128)(2,1)S(1)} %pad_maximum_fusion.refs_0_), channel_id=1, source_target_pairs={{0,4},{1,3},{4,8},{5,1},{8,12},{9,5},{12,14},{13,9},{14,10},{15,13... | collective-permute-start | bytes 589832 | tf_op jit(solution)/shard_map/ppermute | solution.py:33
  4.7 5.7 %collective-permute-start.2 = (bf16[6,128,128]{2,1,0:T(8,128)(2,1)S(1)}, bf16[6,128,128]{2,1,0:T(8,128)(2,1)S(1)}, u32[]{:S(2)}, u32[]{:S(2)}) collective-permute-start(bf16[6,128,128]{2,1,0:T(8,128)(2,1)S(1)} %collective-permute-done.1.refs_1_), channel_id=1, source_target_pairs={{0,4},{1,3},{4,8},{5,1},{8,12},{9,5},{12,14},{13,9},{14,10},{15,13... | collective-permute-start | bytes 589832 | tf_op jit(solution)/shard_map/ppermute | solution.py:33
  6.3 0.7 %copy-start = (s32[256,4]{0,1:T(4,128)S(1)}, s32[256,4]{0,1:T(4,128)}, u32[]{:S(2)}) copy-start(s32[256,4]{0,1:T(4,128)} %param.7) | copy-start | bytes 12292
  8.3 5.7 %collective-permute-start.5 = (bf16[6,128,128]{2,1,0:T(8,128)(2,1)S(1)}, bf16[6,128,128]{2,1,0:T(8,128)(2,1)S(1)}, u32[]{:S(2)}, u32[]{:S(2)}) collective-permute-start(bf16[6,128,128]{2,1,0:T(8,128)(2,1)S(1)} %collective-permute-done.refs_2_), channel_id=1, source_target_pairs={{0,4},{1,3},{4,8},{5,1},{8,12},{9,5},{12,14},{13,9},{14,10},{15,13... | collective-permute-start | bytes 589832 | tf_op jit(solution)/shard_map/ppermute | solution.py:33
  10.4 5.7 %collective-permute-start.6 = (bf16[6,128,128]{2,1,0:T(8,128)(2,1)S(1)}, bf16[6,128,128]{2,1,0:T(8,128)(2,1)S(1)}, u32[]{:S(2)}, u32[]{:S(2)}) collective-permute-start(bf16[6,128,128]{2,1,0:T(8,128)(2,1)S(1)} %collective-permute-done.2.refs_3_), channel_id=1, source_target_pairs={{0,4},{1,3},{4,8},{5,1},{8,12},{9,5},{12,14},{13,9},{14,10},{15,13... | collective-permute-start | bytes 589832 | tf_op jit(solution)/shard_map/ppermute | solution.py:33
  12.5 5.7 %collective-permute-start.3 = (bf16[6,128,128]{2,1,0:T(8,128)(2,1)S(1)}, bf16[6,128,128]{2,1,0:T(8,128)(2,1)S(1)}, u32[]{:S(2)}, u32[]{:S(2)}) collective-permute-start(bf16[6,128,128]{2,1,0:T(8,128)(2,1)S(1)} %collective-permute-done.refs_2_), channel_id=1, source_target_pairs={{0,1},{1,0},{2,3},{3,2},{4,5},{5,4},{6,7},{7,6},{8,9},{9,8},{10,11... | collective-permute-start | bytes 589832 | tf_op jit(solution)/shard_map/ppermute | solution.py:19
  14.0 5.7 %collective-permute-start.9 = (bf16[6,128,128]{2,1,0:T(8,128)(2,1)S(1)}, bf16[6,128,128]{2,1,0:T(8,128)(2,1)S(1)}, u32[]{:S(2)}, u32[]{:S(2)}) collective-permute-start(bf16[6,128,128]{2,1,0:T(8,128)(2,1)S(1)} %collective-permute-done.5.refs_6_), channel_id=1, source_target_pairs={{0,4},{1,3},{4,8},{5,1},{8,12},{9,5},{12,14},{13,9},{14,10},{15,13... | collective-permute-start | bytes 589832 | tf_op jit(solution)/shard_map/ppermute | solution.py:33
  16.1 5.7 %collective-permute-start.4 = (bf16[6,128,128]{2,1,0:T(8,128)(2,1)S(1)}, bf16[6,128,128]{2,1,0:T(8,128)(2,1)S(1)}, u32[]{:S(2)}, u32[]{:S(2)}) collective-permute-start(bf16[6,128,128]{2,1,0:T(8,128)(2,1)S(1)} %collective-permute-done.2.refs_3_), channel_id=1, source_target_pairs={{0,1},{1,0},{2,3},{3,2},{4,5},{5,4},{6,7},{7,6},{8,9},{9,8},{10,11... | collective-permute-start | bytes 589832 | tf_op jit(solution)/shard_map/ppermute | solution.py:19
  16.1 5.7 %collective-permute-start.10 = (bf16[6,128,128]{2,1,0:T(8,128)(2,1)S(1)}, bf16[6,128,128]{2,1,0:T(8,128)(2,1)S(1)}, u32[]{:S(2)}, u32[]{:S(2)}) collective-permute-start(bf16[6,128,128]{2,1,0:T(8,128)(2,1)S(1)} %collective-permute-done.6.refs_7_), channel_id=1, source_target_pairs={{0,4},{1,3},{4,8},{5,1},{8,12},{9,5},{12,14},{13,9},{14,10},{15,13... | collective-permute-start | bytes 589832 | tf_op jit(solution)/shard_map/ppermute | solution.py:33
  18.2 5.7 %collective-permute-start.7 = (bf16[6,128,128]{2,1,0:T(8,128)(2,1)S(1)}, bf16[6,128,128]{2,1,0:T(8,128)(2,1)S(1)}, u32[]{:S(2)}, u32[]{:S(2)}) collective-permute-start(bf16[6,128,128]{2,1,0:T(8,128)(2,1)S(1)} %collective-permute-done.5.refs_6_), channel_id=1, source_target_pairs={{0,1},{1,0},{2,3},{3,2},{4,5},{5,4},{6,7},{7,6},{8,9},{9,8},{10,11... | collective-permute-start | bytes 589832 | tf_op jit(solution)/shard_map/ppermute | solution.py:19
  18.2 9.1 %collective-permute-start.8 = (bf16[6,128,128]{2,1,0:T(8,128)(2,1)S(1)}, bf16[6,128,128]{2,1,0:T(8,128)(2,1)S(1)}, u32[]{:S(2)}, u32[]{:S(2)}) collective-permute-start(bf16[6,128,128]{2,1,0:T(8,128)(2,1)S(1)} %collective-permute-done.6.refs_7_), channel_id=1, source_target_pairs={{0,1},{1,0},{2,3},{3,2},{4,5},{5,4},{6,7},{7,6},{8,9},{9,8},{10,11... | collective-permute-start | bytes 589832 | tf_op jit(solution)/shard_map/ppermute | solution.py:19
  19.6 7.6 %collective-permute-start.13 = (bf16[6,128,128]{2,1,0:T(8,128)(2,1)S(1)}, bf16[6,128,128]{2,1,0:T(8,128)(2,1)S(1)}, u32[]{:S(2)}, u32[]{:S(2)}) collective-permute-start(bf16[6,128,128]{2,1,0:T(8,128)(2,1)S(1)} %collective-permute-done.9.refs_10_), channel_id=1, source_target_pairs={{0,4},{1,3},{4,8},{5,1},{8,12},{9,5},{12,14},{13,9},{14,10},{15,13... | collective-permute-start | bytes 589832 | tf_op jit(solution)/shard_map/ppermute | solution.py:33
  21.7 5.5 %collective-permute-start.11 = (bf16[6,128,128]{2,1,0:T(8,128)(2,1)S(1)}, bf16[6,128,128]{2,1,0:T(8,128)(2,1)S(1)}, u32[]{:S(2)}, u32[]{:S(2)}) collective-permute-start(bf16[6,128,128]{2,1,0:T(8,128)(2,1)S(1)} %collective-permute-done.9.refs_10_), channel_id=1, source_target_pairs={{0,1},{1,0},{2,3},{3,2},{4,5},{5,4},{6,7},{7,6},{8,9},{9,8},{10,11... | collective-permute-start | bytes 589832 | tf_op jit(solution)/shard_map/ppermute | solution.py:19
  21.8 5.7 %collective-permute-start.14 = (bf16[6,128,128]{2,1,0:T(8,128)(2,1)S(1)}, bf16[6,128,128]{2,1,0:T(8,128)(2,1)S(1)}, u32[]{:S(2)}, u32[]{:S(2)}) collective-permute-start(bf16[6,128,128]{2,1,0:T(8,128)(2,1)S(1)} %collective-permute-done.10.refs_11_), channel_id=1, source_target_pairs={{0,4},{1,3},{4,8},{5,1},{8,12},{9,5},{12,14},{13,9},{14,10},{15,13... | collective-permute-start | bytes 589832 | tf_op jit(solution)/shard_map/ppermute | solution.py:33
  23.8 3.6 %collective-permute-start.12 = (bf16[6,128,128]{2,1,0:T(8,128)(2,1)S(1)}, bf16[6,128,128]{2,1,0:T(8,128)(2,1)S(1)}, u32[]{:S(2)}, u32[]{:S(2)}) collective-permute-start(bf16[6,128,128]{2,1,0:T(8,128)(2,1)S(1)} %collective-permute-done.10.refs_11_), channel_id=1, source_target_pairs={{0,1},{1,0},{2,3},{3,2},{4,5},{5,4},{6,7},{7,6},{8,9},{9,8},{10,11... | collective-permute-start | bytes 589832 | tf_op jit(solution)/shard_map/ppermute | solution.py:19
  39.6 2.0 %collective-permute-start.15 = (bf16[2064,128]{1,0:T(8,128)(2,1)S(1)}, bf16[2064,128]{1,0:T(8,128)(2,1)S(1)}, u32[]{:S(2)}, u32[]{:S(2)}) collective-permute-start(bf16[2064,128]{1,0:T(8,128)(2,1)S(1)} %get-tuple-element.41), channel_id=1, source_target_pairs={{0,1},{1,0},{2,3},{3,2},{4,5},{5,4},{6,7},{7,6},{8,9},{9,8},{10,11... | collective-permute-start | bytes 1585160 | tf_op jit(solution)/shard_map/ppermute | solution.py:19
  41.7 10.9 %collective-permute-start.16 = (bf16[272,128]{1,0:T(8,128)(2,1)S(1)}, bf16[272,128]{1,0:T(8,128)(2,1)S(1)}, u32[]{:S(2)}, u32[]{:S(2)}) collective-permute-start(bf16[272,128]{1,0:T(8,128)(2,1)S(1)} %get-tuple-element.44), channel_id=1, source_target_pairs={{0,14},{1,15},{2,12},{3,13},{4,10},{5,11},{6,8},{7,9},{8,6},{9,7},... | collective-permute-start | bytes 208904 | tf_op jit(solution)/shard_map/ppermute | solution.py:19
  45.2 8.7 %collective-permute-start.17 = (bf16[272,128]{1,0:T(8,128)(2,1)S(1)}, bf16[272,128]{1,0:T(8,128)(2,1)S(1)}, u32[]{:S(2)}, u32[]{:S(2)}) collective-permute-start(bf16[272,128]{1,0:T(8,128)(2,1)S(1)} %get-tuple-element.45), channel_id=1, source_target_pairs={{0,12},{1,13},{2,14},{3,15},{4,8},{5,9},{6,10},{7,11},{8,4},{9,5},... | collective-permute-start | bytes 208904 | tf_op jit(solution)/shard_map/ppermute | solution.py:19
  47.4 11.5 %collective-permute-start.18 = (bf16[272,128]{1,0:T(8,128)(2,1)S(1)}, bf16[272,128]{1,0:T(8,128)(2,1)S(1)}, u32[]{:S(2)}, u32[]{:S(2)}) collective-permute-start(bf16[272,128]{1,0:T(8,128)(2,1)S(1)} %get-tuple-element.46), channel_id=1, source_target_pairs={{0,10},{1,11},{2,8},{3,9},{4,14},{5,15},{6,12},{7,13},{8,2},{9,3},... | collective-permute-start | bytes 208904 | tf_op jit(solution)/shard_map/ppermute | solution.py:19
  49.3 11.2 %collective-permute-start.19 = (bf16[272,128]{1,0:T(8,128)(2,1)S(1)}, bf16[272,128]{1,0:T(8,128)(2,1)S(1)}, u32[]{:S(2)}, u32[]{:S(2)}) collective-permute-start(bf16[272,128]{1,0:T(8,128)(2,1)S(1)} %get-tuple-element.47), channel_id=1, source_target_pairs={{0,8},{1,9},{2,10},{3,11},{4,12},{5,13},{6,14},{7,15},{8,0},{9,1},... | collective-permute-start | bytes 208904 | tf_op jit(solution)/shard_map/ppermute | solution.py:19
  51.2 9.3 %collective-permute-start.20 = (bf16[272,128]{1,0:T(8,128)(2,1)S(1)}, bf16[272,128]{1,0:T(8,128)(2,1)S(1)}, u32[]{:S(2)}, u32[]{:S(2)}) collective-permute-start(bf16[272,128]{1,0:T(8,128)(2,1)S(1)} %get-tuple-element.48), channel_id=1, source_target_pairs={{0,6},{1,7},{2,4},{3,5},{4,2},{5,3},{6,0},{7,1},{8,14},{9,15},{10,... | collective-permute-start | bytes 208904 | tf_op jit(solution)/shard_map/ppermute | solution.py:19
  52.6 7.8 %collective-permute-start.21 = (bf16[272,128]{1,0:T(8,128)(2,1)S(1)}, bf16[272,128]{1,0:T(8,128)(2,1)S(1)}, u32[]{:S(2)}, u32[]{:S(2)}) collective-permute-start(bf16[272,128]{1,0:T(8,128)(2,1)S(1)} %get-tuple-element.49), channel_id=1, source_target_pairs={{0,4},{1,5},{2,6},{3,7},{4,0},{5,1},{6,2},{7,3},{8,12},{9,13},{10,... | collective-permute-start | bytes 208904 | tf_op jit(solution)/shard_map/ppermute | solution.py:19
  53.9 6.6 %collective-permute-start.22 = (bf16[272,128]{1,0:T(8,128)(2,1)S(1)}, bf16[272,128]{1,0:T(8,128)(2,1)S(1)}, u32[]{:S(2)}, u32[]{:S(2)}) collective-permute-start(bf16[272,128]{1,0:T(8,128)(2,1)S(1)} %get-tuple-element.50), channel_id=1, source_target_pairs={{0,2},{1,3},{2,0},{3,1},{4,6},{5,7},{6,4},{7,5},{8,10},{9,11},{10,... | collective-permute-start | bytes 208904 | tf_op jit(solution)/shard_map/ppermute | solution.py:19

commit v12 on v11

--- a/solution.py
+++ b/solution.py
@@ -10,8 +10,6 @@
 MIB = 1024 * 1024
 TAIL = 16
 TRIALS = 2
-CHUNK = 48
-PAIRS = 24
 AHEAD = 3
 
 
@@ -79,13 +77,18 @@
     return 1
 
 
+def chunk_of(n):
+    return 96 if fits(n) else 48
+
+
 def run_of(slots, n):
     return 4 if slots >= 8 * n else 2
 
 
 def source_places(slots, n):
-    most = slots + min(slots, n) * (run_of(slots, n) - 1) + phases_of(n) * CHUNK
-    return -(-most // CHUNK) * CHUNK
+    chunk = chunk_of(n)
+    most = slots + min(slots, n) * (run_of(slots, n) - 1)
+    return -(-most // chunk) * chunk
 
 
 def place_of(chip, chips):
@@ -134,8 +137,8 @@
             starts.append(start)
         return jnp.where(live > 0, place, -1.0), starts
 
-    by_source, source_starts = sort(source, phases, float(run_of(slots, n)), float(CHUNK))
-    by_target, target_starts = sort(target, 1, 2.0, 2.0 * PAIRS)
+    by_source, source_starts = sort(source, phases, float(run_of(slots, n)), float(chunk_of(n)))
+    by_target, target_starts = sort(target, 1, 2.0, float(chunk_of(n)))
     columns = column(by_source, by_target, lane, source, term, target)
 
     def picker(places_column):
@@ -163,7 +166,7 @@
 
 
 def make_plan(tasks, n, terms):
-    most = source_places(tasks.shape[1], n) + 2 * PAIRS
+    most = source_places(tasks.shape[1], n) + chunk_of(n)
     return pl.pallas_call(
         functools.partial(plan_kernel, n, terms),
         out_shape=jax.ShapeDtypeStruct((8, -(-most // 128) * 128), jnp.int32),
@@ -190,28 +193,31 @@
     )(left_ops)
 
 
-def block_copies(n, kinds, blocks, trial, right, sem, which):
-    copies = []
+def block_parts(n, kinds, blocks, trial, right):
+    parts = []
     for b, kind in enumerate(kinds):
-        owner = owner_of(*kind, n)
-        per = blocks[b].shape[0] - TRIALS
-        if which == 0:
-            source, to = blocks[b].at[pl.ds(0, TRIALS)], trial.at[owner]
-        else:
-            source, to = blocks[b].at[pl.ds(TRIALS, per)], right.at[pl.ds(owner * per, per)]
-        copies.append(pltpu.make_async_copy(source, to, sem.at[b, which]))
-    return copies
+        first, second, rest = blocks[3 * b : 3 * b + 3]
+        some = first.shape[0] - TRIALS
+        others = rest.shape[0] // 2
+        for half, ref in enumerate((first, second)):
+            owner = owner_of(*kind, half, n)
+            base = owner * (some + others)
+            parts.append((ref.at[pl.ds(0, TRIALS)], trial.at[owner]))
+            parts.append((ref.at[pl.ds(TRIALS, some)], right.at[pl.ds(base, some)]))
+            parts.append((rest.at[pl.ds(half * others, others)], right.at[pl.ds(base + some, others)]))
+    return parts
 
 
 def make_halves(n, plan_ref, left_ref, trial, halves, fetched):
     turns = plan_ref[5, 1]
     run = run_of(left_ref.shape[0], n)
+    chunk = chunk_of(n)
 
     def fetch(turn):
         left, left_sem = fetched
         at = lax.rem(turn, AHEAD)
-        for u in range(CHUNK):
-            slot = plan_ref[0, turn * CHUNK + u]
+        for u in range(chunk):
+            slot = plan_ref[0, turn * chunk + u]
             pltpu.make_async_copy(left_ref.at[slot], left.at[at, u], left_sem.at[at]).start()
 
     def start():
@@ -230,9 +236,9 @@
                 fetch(turn + AHEAD - 1)
 
             at = lax.rem(turn, AHEAD)
-            pltpu.make_async_copy(left_ref.at[pl.ds(0, CHUNK)], left.at[at], left_sem.at[at]).wait()
-        place = turn * CHUNK
-        for r in range(0, CHUNK, run):
+            pltpu.make_async_copy(left_ref.at[pl.ds(0, chunk)], left.at[at], left_sem.at[at]).wait()
+        place = turn * chunk
+        for r in range(0, chunk, run):
             source = plan_ref[1, place + r]
             vectors = jnp.concatenate([trial[source, 0], trial[source, 1]], axis=1)
             if fetched:
@@ -249,37 +255,32 @@
 
 
 def tasks_kernel(n, kinds, plan_ref, left_ref, *refs):
-    blocks, refs = refs[: len(kinds)], refs[len(kinds) :]
+    blocks, refs = refs[: 3 * len(kinds)], refs[3 * len(kinds) :]
     send_ref, acc, own_ref, halves, trial, right, block_sem, *fetched = refs
     start, products = make_halves(n, plan_ref, left_ref, trial, halves, fetched)
     right[right.shape[0] - 1] = jnp.zeros((128, 128), jnp.bfloat16)
     start()
-    if fits(n):
-        moves = ([], [])
-        for b, kind in enumerate(kinds):
-            owner = owner_of(*kind, n)
-            per = blocks[b].shape[0] - TRIALS
-            trial[owner] = blocks[b][0:TRIALS]
-            right[pl.ds(owner * per, per)] = blocks[b][TRIALS:]
-    else:
-        moves = [block_copies(n, kinds, blocks, trial, right, block_sem, which) for which in range(2)]
-        for copy in moves[0] + moves[1]:
-            copy.start()
+    parts = block_parts(n, kinds, blocks, trial, right)
+    copies = []
+    for index, (source, to) in enumerate(parts):
+        if fits(n):
+            to[...] = source[...]
+        else:
+            copies.append(pltpu.make_async_copy(source, to, block_sem.at[index]))
+            copies[-1].start()
 
     def clear(s, carry):
         acc[s] = jnp.zeros((256, 128), jnp.float32)
         return carry
 
     lax.fori_loop(0, n, clear, 0)
-    for copy in moves[0]:
+    for copy in copies:
         copy.wait()
     products()
-    for copy in moves[1]:
-        copy.wait()
 
     def target_turn(turn, carry):
-        first = turn * 2 * PAIRS
-        for u in range(0, 2 * PAIRS, 2):
+        first = turn * chunk_of(n)
+        for u in range(0, chunk_of(n), 2):
             place = first + u
             one = plan_ref[2, place]
             two = plan_ref[2, place + 1]
@@ -327,12 +328,13 @@
 
 def run_tasks(n, plan, left_ops, blocks):
     slots = left_ops.shape[0]
-    terms_per = blocks[0][0].shape[0] - TRIALS
+    first, unused, rest = blocks[0][0]
+    terms_per = first.shape[0] - TRIALS + rest.shape[0] // 2
     kinds = tuple(block[1:] for block in blocks)
     vmem, hbm = pl.BlockSpec(memory_space=pltpu.VMEM), pl.BlockSpec(memory_space=pltpu.HBM)
     given = vmem if fits(n) else hbm
     fetched = [] if fits(n) else [
-        pltpu.VMEM((AHEAD, CHUNK, 128, 128), jnp.bfloat16),
+        pltpu.VMEM((AHEAD, chunk_of(n), 128, 128), jnp.bfloat16),
         pltpu.SemaphoreType.DMA((AHEAD,)),
     ]
     return pl.pallas_call(
@@ -342,20 +344,20 @@
             jax.ShapeDtypeStruct((n + 1, 256, 128), jnp.float32),
             jax.ShapeDtypeStruct((8, 128), jnp.float32),
         ),
-        in_specs=[pl.BlockSpec(memory_space=pltpu.SMEM)] + [given] * (1 + len(blocks)),
+        in_specs=[pl.BlockSpec(memory_space=pltpu.SMEM)] + [given] * (1 + 3 * len(blocks)),
         out_specs=(vmem,) * 3,
         scratch_shapes=[
             pltpu.VMEM((source_places(slots, n), 2, 128, 128), jnp.bfloat16),
             pltpu.VMEM((n, TRIALS, 128, 128), jnp.bfloat16),
             pltpu.VMEM((n * terms_per + 1, 128, 128), jnp.bfloat16),
-            pltpu.SemaphoreType.DMA((len(blocks), 2)),
+            pltpu.SemaphoreType.DMA((6 * len(blocks),)),
         ]
         + fetched,
         compiler_params=pltpu.CompilerParams(vmem_limit_bytes=(30 if fits(n) else 58) * MIB),
         cost_estimate=pl.CostEstimate(
             flops=slots * 8 * 128**3, bytes_accessed=slots * 32768 + n * 450000, transcendentals=0
         ),
-    )(plan, left_ops, *[block[0] for block in blocks])
+    )(plan, left_ops, *[value for block in blocks for value in block[0]])
 
 
 def corr_kernel(*refs):
@@ -425,21 +427,26 @@
 
 def body(n, trial, left_ops, right_ops, task_list):
     steps = n // 4
-    own = jnp.concatenate([trial[0], right_ops], axis=0)
-    plan = make_plan(task_list.T, n, n * right_ops.shape[0])
     left_ops = stage(left_ops, n)
-    lines = [own, exchange(own, n, 1)]
-    blocks = [(value, 0, False, half) for half, value in enumerate(lines)]
+    some = right_ops.shape[0] // 2
+    own = jnp.concatenate([trial[0], right_ops[:some]], axis=0)
+    rest = jnp.concatenate([right_ops[some:], exchange(right_ops[some:], n, 1)], axis=0)
+    line = [own, exchange(own, n, 1), rest]
+    blocks = [(line, 0, False)]
     for step in range(1, steps + 1):
         if step == 2:
-            lines[0], plan = lax.optimization_barrier((lines[0], plan))
-        for half in range(2):
-            lines[half] = ring_step(lines[half], n)
-            blocks.append((lines[half], step, False, half))
+            tasks, first = lax.optimization_barrier((task_list.T, line[0]))
+            line = [first, *line[1:]]
+            plan = make_plan(tasks, n, n * right_ops.shape[0])
+        if step == 3:
+            last, plan = lax.optimization_barrier((line[2], plan))
+            line = [*line[:2], last]
+        line = [ring_step(value, n) for value in line]
+        blocks.append((line, step, False))
         if step < steps:
-            blocks += [(exchange(value, n, 1), step, True, half) for half, value in enumerate(lines)]
+            blocks.append(([exchange(value, n, 1) for value in line], step, True))
     send, keep, own = run_tasks(n, plan, left_ops, blocks)
-    send, arrays = lax.optimization_barrier((send, [block[0] for block in blocks]))
+    send, arrays = lax.optimization_barrier((send, [value for block in blocks for value in block[0][:2]]))
     correlation = correlate(arrays)
     mine, total, *sends = add_chip(keep, own, exchange(send, n, 1))
     received = [exchange(sends[j - 1], n, 2 * j) for j in reversed(range(1, n // 2))]

time: 61.9 us -> 63.2 us (1.021)
  waiting for transfers between devices: 7.41 us -> 5.83 us
  Pallas kernels: 18.4 us -> 19.6 us
  starting transfers between devices: 33.1 us -> 34.1 us
  local copies, waits for them, and re-layouts: 0.69 us -> 1.57 us
    ppermute x8 -> x12, starting transfers between devices: 16.7 us -> 20.8 us  [ring_step(): return lax.ppermute(value, 'op', pairs)]
    ppermute x15 -> x19, starting transfers between devices: 16.5 us -> 13.4 us  [exchange(): return lax.ppermute(value, 'op', [(i, i ^ mask) for i in range(n)])]
    ppermute x8 -> x12, waiting for transfers between devices: 3.07 us -> 0.38 us  [ring_step(): return lax.ppermute(value, 'op', pairs)]
    pallas_call x1, Pallas kernels: 12.2 us -> 13.4 us  [run_tasks(): pl.pallas_call(functools.partial(tasks_kernel, n, kinds), out_shape=(jax....]
    ppermute x15 -> x19, waiting for transfers between devices: 4.35 us -> 5.45 us  [exchange(): return lax.ppermute(value, 'op', [(i, i ^ mask) for i in range(n)])]
    slice x0 -> x1, local copies, waits for them, and re-layouts: none -> 0.88 us  [body(): own = jnp.concatenate([trial[0], right_ops[:some]], axis=0)]
  transfers between devices with their start and end apart: 23 -> 31, of which waited for: 7 -> 7; matrix products, arithmetic and copies ran while one was open for 0% -> 1% of each run, Pallas kernels for 9% -> 9%
where the time goes in v12:
time: 63.2 us; the launch traced here: 62.7 us
  starting transfers between devices  34.1 us (54%)
  Pallas kernels  19.6 us (31%)
  waiting for transfers between devices  5.83 us (9%)
  local copies, waits for them, and re-layouts  1.57 us (2%)
  other arithmetic  0.87 us (1%)
  between operations  0.75 us (1%)
    ppermute x12, starting transfers between devices, ring_step(): return lax.ppermute(value, 'op', pairs)  20.8 us
    ppermute x19, starting transfers between devices, exchange(): return lax.ppermute(value, 'op', [(i, i ^ mask) for i in range(n)])  13.4 us
    pallas_call x1, Pallas kernels, run_tasks(): pl.pallas_call(functools.partial(tasks_kernel, n, kinds), out_shape=(jax....  13.4 us
    ppermute x19, waiting for transfers between devices, exchange(): return lax.ppermute(value, 'op', [(i, i ^ mask) for i in range(n)])  5.45 us
    pallas_call x1, Pallas kernels, stage(): pl.pallas_call(stage_kernel, in_specs=[pl.BlockSpec(memory_space=pltpu.HB...  3.39 us
  transfers between devices with their start and end apart: 31, of which 7 were waited for; matrix products, arithmetic and copies ran while one was open for 1% of the time, Pallas kernels for 9%

profile of v12, /device:TPU:0, one launch (start us, length us, event | category | flops | bytes accessed | tf_op | source)
XLA Modules:
  0.0 62.7 jit_solution(3220403806910305931)
XLA Ops:
  0.6 0.9 %fusion = (bf16[2,128,128]{2,1,0:T(8,128)(2,1)S(1)}, bf16[2,128,128]{2,1,0:T(8,128)(2,1)S(1)}) fusion(bf16[4,128,128]{2,1,0:T(8,128)(2,1)} %param.6), kind=kLoop, calls=%fused_computation.2 | loop fusion | bytes 262144 | tf_op jit(solution)/shard_map/slice | solution.py:432
  1.5 0.5 collective-permute-start
  2.0 0.9 %pad_maximum_fusion.1.refs_0_ = bf16[4,128,128]{2,1,0:T(8,128)(2,1)S(1)} fusion(bf16[2,128,128]{2,1,0:T(8,128)(2,1)S(1)} %get-tuple-element.73, bf16[2,128,128]{2,1,0:T(8,128)(2,1)} %bitcast.3), kind=kLoop, calls=%fused_computation.1 | loop fusion | flops 65536 | bytes 262144 | tf_op jit(solution)/shard_map/concatenate | solution.py:432
  2.9 0.1 collective-permute-start.4
  3.0 3.0 %collective-permute-start.3 = (bf16[4,128,128]{2,1,0:T(8,128)(2,1)S(1)}, bf16[4,128,128]{2,1,0:T(8,128)(2,1)S(1)}, u32[]{:S(2)}, u32[]{:S(2)}) collective-permute-start(bf16[4,128,128]{2,1,0:T(8,128)(2,1)S(1)} %pad_maximum_fusion.1.refs_0_), channel_id=1, source_target_pairs={{0,4},{1,3},{4,8},{5,1},{8,12},{9,5},{12,14},{13,9},{14,10},{15,13... | collective-permute-start | bytes 393224 | tf_op jit(solution)/shard_map/ppermute | solution.py:31
  6.0 0.0 collective-permute-done
  6.1 1.6 %collective-permute-start.1 = (bf16[4,128,128]{2,1,0:T(8,128)(2,1)S(1)}, bf16[4,128,128]{2,1,0:T(8,128)(2,1)S(1)}, u32[]{:S(2)}, u32[]{:S(2)}) collective-permute-start(bf16[4,128,128]{2,1,0:T(8,128)(2,1)S(1)} %pad_maximum_fusion.refs_2_), channel_id=1, source_target_pairs={{0,4},{1,3},{4,8},{5,1},{8,12},{9,5},{12,14},{13,9},{14,10},{15,13... | collective-permute-start | bytes 393224 | tf_op jit(solution)/shard_map/ppermute | solution.py:31
  7.7 0.0 collective-permute-done.4.refs_1_
  7.7 1.6 %collective-permute-start.5 = (bf16[4,128,128]{2,1,0:T(8,128)(2,1)S(1)}, bf16[4,128,128]{2,1,0:T(8,128)(2,1)S(1)}, u32[]{:S(2)}, u32[]{:S(2)}) collective-permute-start(bf16[4,128,128]{2,1,0:T(8,128)(2,1)S(1)} %collective-permute-done.4.refs_1_), channel_id=1, source_target_pairs={{0,4},{1,3},{4,8},{5,1},{8,12},{9,5},{12,14},{13,9},{14,10},{15,13... | collective-permute-start | bytes 393224 | tf_op jit(solution)/shard_map/ppermute | solution.py:31
  9.3 0.0 collective-permute-done.3.refs_3_.refs_2_
  9.3 1.7 %collective-permute-start.9 = (bf16[4,128,128]{2,1,0:T(8,128)(2,1)S(1)}, bf16[4,128,128]{2,1,0:T(8,128)(2,1)S(1)}, u32[]{:S(2)}, u32[]{:S(2)}) collective-permute-start(bf16[4,128,128]{2,1,0:T(8,128)(2,1)S(1)} %collective-permute-done.3.refs_3_.refs_2_), channel_id=1, source_target_pairs={{0,4},{1,3},{4,8},{5,1},{8,12},{9,5},{12,14},{13,9},{14,10},{15,13... | collective-permute-start | bytes 393224 | tf_op jit(solution)/shard_map/ppermute | solution.py:31
  11.0 0.0 collective-permute-start.6
  11.0 0.1 collective-permute-done.1.refs_5_
  11.1 1.6 %collective-permute-start.2 = (bf16[4,128,128]{2,1,0:T(8,128)(2,1)S(1)}, bf16[4,128,128]{2,1,0:T(8,128)(2,1)S(1)}, u32[]{:S(2)}, u32[]{:S(2)}) collective-permute-start(bf16[4,128,128]{2,1,0:T(8,128)(2,1)S(1)} %collective-permute-done.1.refs_5_), channel_id=1, source_target_pairs={{0,4},{1,3},{4,8},{5,1},{8,12},{9,5},{12,14},{13,9},{14,10},{15,13... | collective-permute-start | bytes 393224 | tf_op jit(solution)/shard_map/ppermute | solution.py:31
  12.7 0.0 collective-permute-start.8
  12.7 0.0 collective-permute-done.5.refs_4_.refs_3_
  12.7 1.6 %collective-permute-start.10 = (bf16[4,128,128]{2,1,0:T(8,128)(2,1)S(1)}, bf16[4,128,128]{2,1,0:T(8,128)(2,1)S(1)}, u32[]{:S(2)}, u32[]{:S(2)}) collective-permute-start(bf16[4,128,128]{2,1,0:T(8,128)(2,1)S(1)} %collective-permute-done.5.refs_4_.refs_3_), channel_id=1, source_target_pairs={{0,4},{1,3},{4,8},{5,1},{8,12},{9,5},{12,14},{13,9},{14,10},{15,13... | collective-permute-start | bytes 393224 | tf_op jit(solution)/shard_map/ppermute | solution.py:31
  14.2 0.0 collective-permute-done.9.refs_9_.refs_6_
  14.2 0.0 collective-permute-start.7
  14.2 0.0 collective-permute-done.6.refs_6_.refs_4_
  14.3 1.7 %collective-permute-start.14 = (bf16[4,128,128]{2,1,0:T(8,128)(2,1)S(1)}, bf16[4,128,128]{2,1,0:T(8,128)(2,1)S(1)}, u32[]{:S(2)}, u32[]{:S(2)}) collective-permute-start(bf16[4,128,128]{2,1,0:T(8,128)(2,1)S(1)} %collective-permute-done.9.refs_9_.refs_6_), channel_id=1, source_target_pairs={{0,4},{1,3},{4,8},{5,1},{8,12},{9,5},{12,14},{13,9},{14,10},{15,13... | collective-permute-start | bytes 393224 | tf_op jit(solution)/shard_map/ppermute | solution.py:31
  16.0 0.1 collective-permute-done.2.refs_11_
  16.0 0.1 collective-permute-start.11
  16.2 0.7 %copy-done = s32[256,4]{0,1:T(4,128)S(1)} copy-done((s32[256,4]{0,1:T(4,128)S(1)}, s32[256,4]{0,1:T(4,128)}, u32[]{:S(2)}) %copy-start) | copy-done | bytes 4120
  16.8 1.0 %shard_map.67.plan_ref = s32[8,512]{1,0:T(8,128)S(1)} custom-call(s32[4,256]{1,0:T(4,128)S(1)} %bitcast.2), custom_call_target="tpu_custom_call" | custom-call | tf_op jit(solution)/shard_map/pallas_call | solution.py:170
  17.8 0.0 collective-permute-done.8.refs_8_
  17.8 0.5 collective-permute-start.13
  18.3 0.0 collective-permute-done.10.refs_10_.refs_7_
  18.3 1.6 %collective-permute-start.16 = (bf16[4,128,128]{2,1,0:T(8,128)(2,1)S(1)}, bf16[4,128,128]{2,1,0:T(8,128)(2,1)S(1)}, u32[]{:S(2)}, u32[]{:S(2)}) collective-permute-start(bf16[4,128,128]{2,1,0:T(8,128)(2,1)S(1)} %collective-permute-done.2.refs_11_), channel_id=1, source_target_pairs={{0,4},{1,3},{4,8},{5,1},{8,12},{9,5},{12,14},{13,9},{14,10},{15,13... | collective-permute-start | bytes 393224 | tf_op jit(solution)/shard_map/ppermute | solution.py:31
  19.9 0.0 collective-permute-done.7.refs_7_.refs_5_
  19.9 1.6 %collective-permute-start.15 = (bf16[4,128,128]{2,1,0:T(8,128)(2,1)S(1)}, bf16[4,128,128]{2,1,0:T(8,128)(2,1)S(1)}, u32[]{:S(2)}, u32[]{:S(2)}) collective-permute-start(bf16[4,128,128]{2,1,0:T(8,128)(2,1)S(1)} %collective-permute-done.10.refs_10_.refs_7_), channel_id=1, source_target_pairs={{0,4},{1,3},{4,8},{5,1},{8,12},{9,5},{12,14},{13,9},{14,10},{15,13... | collective-permute-start | bytes 393224 | tf_op jit(solution)/shard_map/ppermute | solution.py:31
  21.5 0.0 collective-permute-done.14.refs_15_.refs_10_
  21.5 0.0 collective-permute-start.12
  21.5 0.0 collective-permute-done.11.refs_12_.refs_8_
  21.5 1.6 %collective-permute-start.20 = (bf16[4,128,128]{2,1,0:T(8,128)(2,1)S(1)}, bf16[4,128,128]{2,1,0:T(8,128)(2,1)S(1)}, u32[]{:S(2)}, u32[]{:S(2)}) collective-permute-start(bf16[4,128,128]{2,1,0:T(8,128)(2,1)S(1)} %collective-permute-done.14.refs_15_.refs_10_), channel_id=1, source_target_pairs={{0,4},{1,3},{4,8},{5,1},{8,12},{9,5},{12,14},{13,9},{14,10},{15,13... | collective-permute-start | bytes 393224 | tf_op jit(solution)/shard_map/ppermute | solution.py:31
  23.0 0.0 collective-permute-done.13.refs_14_
  23.1 0.0 collective-permute-start.17
  23.1 0.2 collective-permute-done.16.refs_17_
  23.3 1.6 %collective-permute-start.22 = (bf16[4,128,128]{2,1,0:T(8,128)(2,1)S(1)}, bf16[4,128,128]{2,1,0:T(8,128)(2,1)S(1)}, u32[]{:S(2)}, u32[]{:S(2)}) collective-permute-start(bf16[4,128,128]{2,1,0:T(8,128)(2,1)S(1)} %collective-permute-done.16.refs_17_), channel_id=1, source_target_pairs={{0,4},{1,3},{4,8},{5,1},{8,12},{9,5},{12,14},{13,9},{14,10},{15,13... | collective-permute-start | bytes 393224 | tf_op jit(solution)/shard_map/ppermute | solution.py:31
  24.9 0.0 collective-permute-done.15.refs_16_.refs_11_
  24.9 0.0 collective-permute-start.19
  24.9 0.0 collective-permute-done.12.refs_13_.refs_9_
  24.9 1.6 %collective-permute-start.21 = (bf16[4,128,128]{2,1,0:T(8,128)(2,1)S(1)}, bf16[4,128,128]{2,1,0:T(8,128)(2,1)S(1)}, u32[]{:S(2)}, u32[]{:S(2)}) collective-permute-start(bf16[4,128,128]{2,1,0:T(8,128)(2,1)S(1)} %collective-permute-done.15.refs_16_.refs_11_), channel_id=1, source_target_pairs={{0,4},{1,3},{4,8},{5,1},{8,12},{9,5},{12,14},{13,9},{14,10},{15,13... | collective-permute-start | bytes 393224 | tf_op jit(solution)/shard_map/ppermute | solution.py:31
  26.5 0.0 collective-permute-done.20.refs_21_.refs_14_
  26.5 3.4 %shard_map.68.left_ref = bf16[256,128,128]{2,1,0:T(8,128)(2,1)S(1)} custom-call(bf16[256,128,128]{2,1,0:T(8,128)(2,1)} %left_ref.1), custom_call_target="tpu_custom_call" | custom-call | tf_op jit(solution)/shard_map/pallas_call | solution.py:186
  29.9 0.0 collective-permute-done.17.refs_18_.refs_12_
  29.9 0.0 collective-permute-done.21.refs_22_.refs_15_
  30.0 13.4 %shard_map.69 = (bf16[2064,128]{1,0:T(8,128)(2,1)S(1)}, f32[17,256,128]{2,1,0:T(8,128)S(1)}, f32[8,128]{1,0:T(8,128)S(1)}) custom-call(s32[8,512]{1,0:T(8,128)S(1)} %shard_map.67.plan_ref, bf16[256,128,128]{2,1,0:T(8,128)(2,1)S(1)} %shard_map.68.left_ref, bf16[4,128,128]{2,1,0:T(8,128)(2,1)S(1)} %pad_maximum_fusion.1.refs_0_, ...), custom_call_target="tpu_custom_call" | custom-call | flops 4294967296 | bytes 15588608 | tf_op jit(solution)/shard_map/pallas_call | solution.py:340
  43.3 0.6 collective-permute-start.23
  43.9 1.5 %collective-permute-done.23.received_ref = bf16[2064,128]{1,0:T(8,128)(2,1)S(1)} collective-permute-done((bf16[2064,128]{1,0:T(8,128)(2,1)S(1)}, bf16[2064,128]{1,0:T(8,128)(2,1)S(1)}, u32[]{:S(2)}, u32[]{:S(2)}) %collective-permute-start.23) | collective-permute-done | bytes 528416 | tf_op jit(solution)/shard_map/ppermute | solution.py:17
  45.4 0.1 shard_map.70
  45.5 3.9 %collective-permute-start.24 = (bf16[272,128]{1,0:T(8,128)(2,1)S(1)}, bf16[272,128]{1,0:T(8,128)(2,1)S(1)}, u32[]{:S(2)}, u32[]{:S(2)}) collective-permute-start(bf16[272,128]{1,0:T(8,128)(2,1)S(1)} %get-tuple-element.48), channel_id=1, source_target_pairs={{0,14},{1,15},{2,12},{3,13},{4,10},{5,11},{6,8},{7,9},{8,6},{9,7},... | collective-permute-start | bytes 208904 | tf_op jit(solution)/shard_map/ppermute | solution.py:17
  49.5 0.0 collective-permute-start.25
  49.5 1.4 %collective-permute-start.26 = (bf16[272,128]{1,0:T(8,128)(2,1)S(1)}, bf16[272,128]{1,0:T(8,128)(2,1)S(1)}, u32[]{:S(2)}, u32[]{:S(2)}) collective-permute-start(bf16[272,128]{1,0:T(8,128)(2,1)S(1)} %get-tuple-element.50), channel_id=1, source_target_pairs={{0,10},{1,11},{2,8},{3,9},{4,14},{5,15},{6,12},{7,13},{8,2},{9,3},... | collective-permute-start | bytes 208904 | tf_op jit(solution)/shard_map/ppermute | solution.py:17
  50.9 2.4 %collective-permute-start.27 = (bf16[272,128]{1,0:T(8,128)(2,1)S(1)}, bf16[272,128]{1,0:T(8,128)(2,1)S(1)}, u32[]{:S(2)}, u32[]{:S(2)}) collective-permute-start(bf16[272,128]{1,0:T(8,128)(2,1)S(1)} %get-tuple-element.51), channel_id=1, source_target_pairs={{0,8},{1,9},{2,10},{3,11},{4,12},{5,13},{6,14},{7,15},{8,0},{9,1},... | collective-permute-start | bytes 208904 | tf_op jit(solution)/shard_map/ppermute | solution.py:17
  53.3 1.5 %collective-permute-start.28 = (bf16[272,128]{1,0:T(8,128)(2,1)S(1)}, bf16[272,128]{1,0:T(8,128)(2,1)S(1)}, u32[]{:S(2)}, u32[]{:S(2)}) collective-permute-start(bf16[272,128]{1,0:T(8,128)(2,1)S(1)} %get-tuple-element.52), channel_id=1, source_target_pairs={{0,6},{1,7},{2,4},{3,5},{4,2},{5,3},{6,0},{7,1},{8,14},{9,15},{10,... | collective-permute-start | bytes 208904 | tf_op jit(solution)/shard_map/ppermute | solution.py:17
  54.8 0.0 collective-permute-done.24.refs_0_
  54.8 0.6 collective-permute-start.29
  55.3 0.8 %collective-permute-done.25.refs_1_ = bf16[272,128]{1,0:T(8,128)(2,1)S(1)} collective-permute-done((bf16[272,128]{1,0:T(8,128)(2,1)S(1)}, bf16[272,128]{1,0:T(8,128)(2,1)S(1)}, u32[]{:S(2)}, u32[]{:S(2)}) %collective-permute-start.25) | collective-permute-done | bytes 69664 | tf_op jit(solution)/shard_map/ppermute | solution.py:17
  56.2 1.8 %collective-permute-start.30 = (bf16[272,128]{1,0:T(8,128)(2,1)S(1)}, bf16[272,128]{1,0:T(8,128)(2,1)S(1)}, u32[]{:S(2)}, u32[]{:S(2)}) collective-permute-start(bf16[272,128]{1,0:T(8,128)(2,1)S(1)} %get-tuple-element.54), channel_id=1, source_target_pairs={{0,2},{1,3},{2,0},{3,1},{4,6},{5,7},{6,4},{7,5},{8,10},{9,11},{10,... | collective-permute-start | bytes 208904 | tf_op jit(solution)/shard_map/ppermute | solution.py:17
  58.0 1.0 %shard_map.72 = f32[2,2]{1,0:T(2,128)} custom-call(bf16[4,128,128]{2,1,0:T(8,128)(2,1)S(1)} %pad_maximum_fusion.1.refs_0_, bf16[4,128,128]{2,1,0:T(8,128)(2,1)S(1)} %collective-permute-done.4.refs_1_, bf16[4,128,128]{2,1,0:T(8,128)(2,1)S(1)} %collective-permute-done.3.refs_3_.refs_2_, bf16[4,128,128]{2,1,0:T(8,128)(2,1)S(1)} %collective-permute-done.5.refs_4_.refs_3_, ...), custom_call_target="tpu_custom_call" | custom-call | tf_op jit(solution)/shard_map/pallas_call | solution.py:374
  58.9 1.4 %collective-permute-done.26.refs_2_ = bf16[272,128]{1,0:T(8,128)(2,1)S(1)} collective-permute-done((bf16[272,128]{1,0:T(8,128)(2,1)S(1)}, bf16[272,128]{1,0:T(8,128)(2,1)S(1)}, u32[]{:S(2)}, u32[]{:S(2)}) %collective-permute-start.26) | collective-permute-done | bytes 69664 | tf_op jit(solution)/shard_map/ppermute | solution.py:17
  60.4 1.6 %collective-permute-done.27.refs_3_ = bf16[272,128]{1,0:T(8,128)(2,1)S(1)} collective-permute-done((bf16[272,128]{1,0:T(8,128)(2,1)S(1)}, bf16[272,128]{1,0:T(8,128)(2,1)S(1)}, u32[]{:S(2)}, u32[]{:S(2)}) %collective-permute-start.27) | collective-permute-done | bytes 69664 | tf_op jit(solution)/shard_map/ppermute | solution.py:17
  62.0 0.7 %shard_map.71 = (f32[1,2,128,128]{3,2,1,0:T(8,128)}, f32[2,2]{1,0:T(2,128)}) custom-call(f32[256,128]{1,0:T(8,128)S(1)} %get-tuple-element.46.mine_ref, f32[16,128]{1,0:T(8,128)S(1)} %get-tuple-element.47.total_ref, bf16[272,128]{1,0:T(8,128)(2,1)S(1)} %collective-permute-done.24.refs_0_, bf16[272,128]{1,0:T(8,128)(2,1)S(1)} %collective-permute-done.25.refs_1_, ...), custom_call_target="tpu_custom_call" | custom-call | tf_op jit(solution)/shard_map/pallas_call | solution.py:418
  (9 shorter events, 0.0 us)
Async XLA Ops:
  1.5 4.5 %collective-permute-start = (bf16[2,128,128]{2,1,0:T(8,128)(2,1)S(1)}, bf16[2,128,128]{2,1,0:T(8,128)(2,1)S(1)}, u32[]{:S(2)}, u32[]{:S(2)}) collective-permute-start(bf16[2,128,128]{2,1,0:T(8,128)(2,1)S(1)} %get-tuple-element.74), channel_id=1, source_target_pairs={{0,1},{1,0},{2,3},{3,2},{4,5},{5,4},{6,7},{7,6},{8,9},{9,8},{10,11... | collective-permute-start | bytes 196616 | tf_op jit(solution)/shard_map/ppermute | solution.py:17
  2.9 4.8 %collective-permute-start.4 = (bf16[4,128,128]{2,1,0:T(8,128)(2,1)S(1)}, bf16[4,128,128]{2,1,0:T(8,128)(2,1)S(1)}, u32[]{:S(2)}, u32[]{:S(2)}) collective-permute-start(bf16[4,128,128]{2,1,0:T(8,128)(2,1)S(1)} %pad_maximum_fusion.1.refs_0_), channel_id=1, source_target_pairs={{0,1},{1,0},{2,3},{3,2},{4,5},{5,4},{6,7},{7,6},{8,9},{9,8},{10,11... | collective-permute-start | bytes 393224 | tf_op jit(solution)/shard_map/ppermute | solution.py:17
  3.0 6.3 %collective-permute-start.3 = (bf16[4,128,128]{2,1,0:T(8,128)(2,1)S(1)}, bf16[4,128,128]{2,1,0:T(8,128)(2,1)S(1)}, u32[]{:S(2)}, u32[]{:S(2)}) collective-permute-start(bf16[4,128,128]{2,1,0:T(8,128)(2,1)S(1)} %pad_maximum_fusion.1.refs_0_), channel_id=1, source_target_pairs={{0,4},{1,3},{4,8},{5,1},{8,12},{9,5},{12,14},{13,9},{14,10},{15,13... | collective-permute-start | bytes 393224 | tf_op jit(solution)/shard_map/ppermute | solution.py:31
  6.1 5.0 %collective-permute-start.1 = (bf16[4,128,128]{2,1,0:T(8,128)(2,1)S(1)}, bf16[4,128,128]{2,1,0:T(8,128)(2,1)S(1)}, u32[]{:S(2)}, u32[]{:S(2)}) collective-permute-start(bf16[4,128,128]{2,1,0:T(8,128)(2,1)S(1)} %pad_maximum_fusion.refs_2_), channel_id=1, source_target_pairs={{0,4},{1,3},{4,8},{5,1},{8,12},{9,5},{12,14},{13,9},{14,10},{15,13... | collective-permute-start | bytes 393224 | tf_op jit(solution)/shard_map/ppermute | solution.py:31
  7.7 5.0 %collective-permute-start.5 = (bf16[4,128,128]{2,1,0:T(8,128)(2,1)S(1)}, bf16[4,128,128]{2,1,0:T(8,128)(2,1)S(1)}, u32[]{:S(2)}, u32[]{:S(2)}) collective-permute-start(bf16[4,128,128]{2,1,0:T(8,128)(2,1)S(1)} %collective-permute-done.4.refs_1_), channel_id=1, source_target_pairs={{0,4},{1,3},{4,8},{5,1},{8,12},{9,5},{12,14},{13,9},{14,10},{15,13... | collective-permute-start | bytes 393224 | tf_op jit(solution)/shard_map/ppermute | solution.py:31
  9.3 5.0 %collective-permute-start.9 = (bf16[4,128,128]{2,1,0:T(8,128)(2,1)S(1)}, bf16[4,128,128]{2,1,0:T(8,128)(2,1)S(1)}, u32[]{:S(2)}, u32[]{:S(2)}) collective-permute-start(bf16[4,128,128]{2,1,0:T(8,128)(2,1)S(1)} %collective-permute-done.3.refs_3_.refs_2_), channel_id=1, source_target_pairs={{0,4},{1,3},{4,8},{5,1},{8,12},{9,5},{12,14},{13,9},{14,10},{15,13... | collective-permute-start | bytes 393224 | tf_op jit(solution)/shard_map/ppermute | solution.py:31
  11.0 3.2 %collective-permute-start.6 = (bf16[4,128,128]{2,1,0:T(8,128)(2,1)S(1)}, bf16[4,128,128]{2,1,0:T(8,128)(2,1)S(1)}, u32[]{:S(2)}, u32[]{:S(2)}) collective-permute-start(bf16[4,128,128]{2,1,0:T(8,128)(2,1)S(1)} %collective-permute-done.3.refs_3_.refs_2_), channel_id=1, source_target_pairs={{0,1},{1,0},{2,3},{3,2},{4,5},{5,4},{6,7},{7,6},{8,9},{9,8},{10,11... | collective-permute-start | bytes 393224 | tf_op jit(solution)/shard_map/ppermute | solution.py:17
  11.1 5.0 %collective-permute-start.2 = (bf16[4,128,128]{2,1,0:T(8,128)(2,1)S(1)}, bf16[4,128,128]{2,1,0:T(8,128)(2,1)S(1)}, u32[]{:S(2)}, u32[]{:S(2)}) collective-permute-start(bf16[4,128,128]{2,1,0:T(8,128)(2,1)S(1)} %collective-permute-done.1.refs_5_), channel_id=1, source_target_pairs={{0,4},{1,3},{4,8},{5,1},{8,12},{9,5},{12,14},{13,9},{14,10},{15,13... | collective-permute-start | bytes 393224 | tf_op jit(solution)/shard_map/ppermute | solution.py:31
  12.7 5.2 %collective-permute-start.8 = (bf16[4,128,128]{2,1,0:T(8,128)(2,1)S(1)}, bf16[4,128,128]{2,1,0:T(8,128)(2,1)S(1)}, u32[]{:S(2)}, u32[]{:S(2)}) collective-permute-start(bf16[4,128,128]{2,1,0:T(8,128)(2,1)S(1)} %collective-permute-done.1.refs_5_), channel_id=1, source_target_pairs={{0,1},{1,0},{2,3},{3,2},{4,5},{5,4},{6,7},{7,6},{8,9},{9,8},{10,11... | collective-permute-start | bytes 393224 | tf_op jit(solution)/shard_map/ppermute | solution.py:17
  12.7 5.6 %collective-permute-start.10 = (bf16[4,128,128]{2,1,0:T(8,128)(2,1)S(1)}, bf16[4,128,128]{2,1,0:T(8,128)(2,1)S(1)}, u32[]{:S(2)}, u32[]{:S(2)}) collective-permute-start(bf16[4,128,128]{2,1,0:T(8,128)(2,1)S(1)} %collective-permute-done.5.refs_4_.refs_3_), channel_id=1, source_target_pairs={{0,4},{1,3},{4,8},{5,1},{8,12},{9,5},{12,14},{13,9},{14,10},{15,13... | collective-permute-start | bytes 393224 | tf_op jit(solution)/shard_map/ppermute | solution.py:31
  14.2 5.6 %collective-permute-start.7 = (bf16[4,128,128]{2,1,0:T(8,128)(2,1)S(1)}, bf16[4,128,128]{2,1,0:T(8,128)(2,1)S(1)}, u32[]{:S(2)}, u32[]{:S(2)}) collective-permute-start(bf16[4,128,128]{2,1,0:T(8,128)(2,1)S(1)} %collective-permute-done.5.refs_4_.refs_3_), channel_id=1, source_target_pairs={{0,1},{1,0},{2,3},{3,2},{4,5},{5,4},{6,7},{7,6},{8,9},{9,8},{10,11... | collective-permute-start | bytes 393224 | tf_op jit(solution)/shard_map/ppermute | solution.py:17
  14.3 7.2 %collective-permute-start.14 = (bf16[4,128,128]{2,1,0:T(8,128)(2,1)S(1)}, bf16[4,128,128]{2,1,0:T(8,128)(2,1)S(1)}, u32[]{:S(2)}, u32[]{:S(2)}) collective-permute-start(bf16[4,128,128]{2,1,0:T(8,128)(2,1)S(1)} %collective-permute-done.9.refs_9_.refs_6_), channel_id=1, source_target_pairs={{0,4},{1,3},{4,8},{5,1},{8,12},{9,5},{12,14},{13,9},{14,10},{15,13... | collective-permute-start | bytes 393224 | tf_op jit(solution)/shard_map/ppermute | solution.py:31
  16.0 5.4 %collective-permute-start.11 = (bf16[4,128,128]{2,1,0:T(8,128)(2,1)S(1)}, bf16[4,128,128]{2,1,0:T(8,128)(2,1)S(1)}, u32[]{:S(2)}, u32[]{:S(2)}) collective-permute-start(bf16[4,128,128]{2,1,0:T(8,128)(2,1)S(1)} %collective-permute-done.9.refs_9_.refs_6_), channel_id=1, source_target_pairs={{0,1},{1,0},{2,3},{3,2},{4,5},{5,4},{6,7},{7,6},{8,9},{9,8},{10,11... | collective-permute-start | bytes 393224 | tf_op jit(solution)/shard_map/ppermute | solution.py:17
  16.2 0.7 %copy-start = (s32[256,4]{0,1:T(4,128)S(1)}, s32[256,4]{0,1:T(4,128)}, u32[]{:S(2)}) copy-start(s32[256,4]{0,1:T(4,128)} %param.7) | copy-start | bytes 12292
  17.8 5.2 %collective-permute-start.13 = (bf16[4,128,128]{2,1,0:T(8,128)(2,1)S(1)}, bf16[4,128,128]{2,1,0:T(8,128)(2,1)S(1)}, u32[]{:S(2)}, u32[]{:S(2)}) collective-permute-start(bf16[4,128,128]{2,1,0:T(8,128)(2,1)S(1)} %collective-permute-done.2.refs_11_), channel_id=1, source_target_pairs={{0,1},{1,0},{2,3},{3,2},{4,5},{5,4},{6,7},{7,6},{8,9},{9,8},{10,11... | collective-permute-start | bytes 393224 | tf_op jit(solution)/shard_map/ppermute | solution.py:17
  18.3 5.0 %collective-permute-start.16 = (bf16[4,128,128]{2,1,0:T(8,128)(2,1)S(1)}, bf16[4,128,128]{2,1,0:T(8,128)(2,1)S(1)}, u32[]{:S(2)}, u32[]{:S(2)}) collective-permute-start(bf16[4,128,128]{2,1,0:T(8,128)(2,1)S(1)} %collective-permute-done.2.refs_11_), channel_id=1, source_target_pairs={{0,4},{1,3},{4,8},{5,1},{8,12},{9,5},{12,14},{13,9},{14,10},{15,13... | collective-permute-start | bytes 393224 | tf_op jit(solution)/shard_map/ppermute | solution.py:31
  19.9 5.0 %collective-permute-start.15 = (bf16[4,128,128]{2,1,0:T(8,128)(2,1)S(1)}, bf16[4,128,128]{2,1,0:T(8,128)(2,1)S(1)}, u32[]{:S(2)}, u32[]{:S(2)}) collective-permute-start(bf16[4,128,128]{2,1,0:T(8,128)(2,1)S(1)} %collective-permute-done.10.refs_10_.refs_7_), channel_id=1, source_target_pairs={{0,4},{1,3},{4,8},{5,1},{8,12},{9,5},{12,14},{13,9},{14,10},{15,13... | collective-permute-start | bytes 393224 | tf_op jit(solution)/shard_map/ppermute | solution.py:31
  21.5 3.4 %collective-permute-start.12 = (bf16[4,128,128]{2,1,0:T(8,128)(2,1)S(1)}, bf16[4,128,128]{2,1,0:T(8,128)(2,1)S(1)}, u32[]{:S(2)}, u32[]{:S(2)}) collective-permute-start(bf16[4,128,128]{2,1,0:T(8,128)(2,1)S(1)} %collective-permute-done.10.refs_10_.refs_7_), channel_id=1, source_target_pairs={{0,1},{1,0},{2,3},{3,2},{4,5},{5,4},{6,7},{7,6},{8,9},{9,8},{10,11... | collective-permute-start | bytes 393224 | tf_op jit(solution)/shard_map/ppermute | solution.py:17
  21.5 5.0 %collective-permute-start.20 = (bf16[4,128,128]{2,1,0:T(8,128)(2,1)S(1)}, bf16[4,128,128]{2,1,0:T(8,128)(2,1)S(1)}, u32[]{:S(2)}, u32[]{:S(2)}) collective-permute-start(bf16[4,128,128]{2,1,0:T(8,128)(2,1)S(1)} %collective-permute-done.14.refs_15_.refs_10_), channel_id=1, source_target_pairs={{0,4},{1,3},{4,8},{5,1},{8,12},{9,5},{12,14},{13,9},{14,10},{15,13... | collective-permute-start | bytes 393224 | tf_op jit(solution)/shard_map/ppermute | solution.py:31
  23.1 6.8 %collective-permute-start.17 = (bf16[4,128,128]{2,1,0:T(8,128)(2,1)S(1)}, bf16[4,128,128]{2,1,0:T(8,128)(2,1)S(1)}, u32[]{:S(2)}, u32[]{:S(2)}) collective-permute-start(bf16[4,128,128]{2,1,0:T(8,128)(2,1)S(1)} %collective-permute-done.14.refs_15_.refs_10_), channel_id=1, source_target_pairs={{0,1},{1,0},{2,3},{3,2},{4,5},{5,4},{6,7},{7,6},{8,9},{9,8},{10,11... | collective-permute-start | bytes 393224 | tf_op jit(solution)/shard_map/ppermute | solution.py:17
  23.3 6.6 %collective-permute-start.22 = (bf16[4,128,128]{2,1,0:T(8,128)(2,1)S(1)}, bf16[4,128,128]{2,1,0:T(8,128)(2,1)S(1)}, u32[]{:S(2)}, u32[]{:S(2)}) collective-permute-start(bf16[4,128,128]{2,1,0:T(8,128)(2,1)S(1)} %collective-permute-done.16.refs_17_), channel_id=1, source_target_pairs={{0,4},{1,3},{4,8},{5,1},{8,12},{9,5},{12,14},{13,9},{14,10},{15,13... | collective-permute-start | bytes 393224 | tf_op jit(solution)/shard_map/ppermute | solution.py:31
  24.9 5.1 %collective-permute-start.19 = (bf16[4,128,128]{2,1,0:T(8,128)(2,1)S(1)}, bf16[4,128,128]{2,1,0:T(8,128)(2,1)S(1)}, u32[]{:S(2)}, u32[]{:S(2)}) collective-permute-start(bf16[4,128,128]{2,1,0:T(8,128)(2,1)S(1)} %collective-permute-done.16.refs_17_), channel_id=1, source_target_pairs={{0,1},{1,0},{2,3},{3,2},{4,5},{5,4},{6,7},{7,6},{8,9},{9,8},{10,11... | collective-permute-start | bytes 393224 | tf_op jit(solution)/shard_map/ppermute | solution.py:17
  24.9 5.1 %collective-permute-start.21 = (bf16[4,128,128]{2,1,0:T(8,128)(2,1)S(1)}, bf16[4,128,128]{2,1,0:T(8,128)(2,1)S(1)}, u32[]{:S(2)}, u32[]{:S(2)}) collective-permute-start(bf16[4,128,128]{2,1,0:T(8,128)(2,1)S(1)} %collective-permute-done.15.refs_16_.refs_11_), channel_id=1, source_target_pairs={{0,4},{1,3},{4,8},{5,1},{8,12},{9,5},{12,14},{13,9},{14,10},{15,13... | collective-permute-start | bytes 393224 | tf_op jit(solution)/shard_map/ppermute | solution.py:31
  26.5 3.4 %collective-permute-start.18 = (bf16[4,128,128]{2,1,0:T(8,128)(2,1)S(1)}, bf16[4,128,128]{2,1,0:T(8,128)(2,1)S(1)}, u32[]{:S(2)}, u32[]{:S(2)}) collective-permute-start(bf16[4,128,128]{2,1,0:T(8,128)(2,1)S(1)} %collective-permute-done.15.refs_16_.refs_11_), channel_id=1, source_target_pairs={{0,1},{1,0},{2,3},{3,2},{4,5},{5,4},{6,7},{7,6},{8,9},{9,8},{10,11... | collective-permute-start | bytes 393224 | tf_op jit(solution)/shard_map/ppermute | solution.py:17
  43.3 2.1 %collective-permute-start.23 = (bf16[2064,128]{1,0:T(8,128)(2,1)S(1)}, bf16[2064,128]{1,0:T(8,128)(2,1)S(1)}, u32[]{:S(2)}, u32[]{:S(2)}) collective-permute-start(bf16[2064,128]{1,0:T(8,128)(2,1)S(1)} %get-tuple-element.45), channel_id=1, source_target_pairs={{0,1},{1,0},{2,3},{3,2},{4,5},{5,4},{6,7},{7,6},{8,9},{9,8},{10,11... | collective-permute-start | bytes 1585160 | tf_op jit(solution)/shard_map/ppermute | solution.py:17
  45.5 9.2 %collective-permute-start.24 = (bf16[272,128]{1,0:T(8,128)(2,1)S(1)}, bf16[272,128]{1,0:T(8,128)(2,1)S(1)}, u32[]{:S(2)}, u32[]{:S(2)}) collective-permute-start(bf16[272,128]{1,0:T(8,128)(2,1)S(1)} %get-tuple-element.48), channel_id=1, source_target_pairs={{0,14},{1,15},{2,12},{3,13},{4,10},{5,11},{6,8},{7,9},{8,6},{9,7},... | collective-permute-start | bytes 208904 | tf_op jit(solution)/shard_map/ppermute | solution.py:17
  49.5 6.7 %collective-permute-start.25 = (bf16[272,128]{1,0:T(8,128)(2,1)S(1)}, bf16[272,128]{1,0:T(8,128)(2,1)S(1)}, u32[]{:S(2)}, u32[]{:S(2)}) collective-permute-start(bf16[272,128]{1,0:T(8,128)(2,1)S(1)} %get-tuple-element.49), channel_id=1, source_target_pairs={{0,12},{1,13},{2,14},{3,15},{4,8},{5,9},{6,10},{7,11},{8,4},{9,5},... | collective-permute-start | bytes 208904 | tf_op jit(solution)/shard_map/ppermute | solution.py:17
  49.5 10.9 %collective-permute-start.26 = (bf16[272,128]{1,0:T(8,128)(2,1)S(1)}, bf16[272,128]{1,0:T(8,128)(2,1)S(1)}, u32[]{:S(2)}, u32[]{:S(2)}) collective-permute-start(bf16[272,128]{1,0:T(8,128)(2,1)S(1)} %get-tuple-element.50), channel_id=1, source_target_pairs={{0,10},{1,11},{2,8},{3,9},{4,14},{5,15},{6,12},{7,13},{8,2},{9,3},... | collective-permute-start | bytes 208904 | tf_op jit(solution)/shard_map/ppermute | solution.py:17
  50.9 11.1 %collective-permute-start.27 = (bf16[272,128]{1,0:T(8,128)(2,1)S(1)}, bf16[272,128]{1,0:T(8,128)(2,1)S(1)}, u32[]{:S(2)}, u32[]{:S(2)}) collective-permute-start(bf16[272,128]{1,0:T(8,128)(2,1)S(1)} %get-tuple-element.51), channel_id=1, source_target_pairs={{0,8},{1,9},{2,10},{3,11},{4,12},{5,13},{6,14},{7,15},{8,0},{9,1},... | collective-permute-start | bytes 208904 | tf_op jit(solution)/shard_map/ppermute | solution.py:17
  53.3 8.7 %collective-permute-start.28 = (bf16[272,128]{1,0:T(8,128)(2,1)S(1)}, bf16[272,128]{1,0:T(8,128)(2,1)S(1)}, u32[]{:S(2)}, u32[]{:S(2)}) collective-permute-start(bf16[272,128]{1,0:T(8,128)(2,1)S(1)} %get-tuple-element.52), channel_id=1, source_target_pairs={{0,6},{1,7},{2,4},{3,5},{4,2},{5,3},{6,0},{7,1},{8,14},{9,15},{10,... | collective-permute-start | bytes 208904 | tf_op jit(solution)/shard_map/ppermute | solution.py:17
  54.8 7.2 %collective-permute-start.29 = (bf16[272,128]{1,0:T(8,128)(2,1)S(1)}, bf16[272,128]{1,0:T(8,128)(2,1)S(1)}, u32[]{:S(2)}, u32[]{:S(2)}) collective-permute-start(bf16[272,128]{1,0:T(8,128)(2,1)S(1)} %get-tuple-element.53), channel_id=1, source_target_pairs={{0,4},{1,5},{2,6},{3,7},{4,0},{5,1},{6,2},{7,3},{8,12},{9,13},{10,... | collective-permute-start | bytes 208904 | tf_op jit(solution)/shard_map/ppermute | solution.py:17
  56.2 5.8 %collective-permute-start.30 = (bf16[272,128]{1,0:T(8,128)(2,1)S(1)}, bf16[272,128]{1,0:T(8,128)(2,1)S(1)}, u32[]{:S(2)}, u32[]{:S(2)}) collective-permute-start(bf16[272,128]{1,0:T(8,128)(2,1)S(1)} %get-tuple-element.54), channel_id=1, source_target_pairs={{0,2},{1,3},{2,0},{3,1},{4,6},{5,7},{6,4},{7,5},{8,10},{9,11},{10,... | collective-permute-start | bytes 208904 | tf_op jit(solution)/shard_map/ppermute | solution.py:17

commit v13 on v12

--- a/solution.py
+++ b/solution.py
@@ -165,46 +165,50 @@
     plan_ref[6:8] = jnp.zeros((2, places), jnp.int32)
 
 
-def make_plan(tasks, n, terms):
+def stage_kernel(n, terms, tasks_ref, left_ref, plan_ref, held_ref, tasks, sem):
+    copies = [
+        pltpu.make_async_copy(tasks_ref, tasks, sem.at[0]),
+        pltpu.make_async_copy(left_ref, held_ref, sem.at[1]),
+    ]
+    for copy in copies:
+        copy.start()
+    copies[0].wait()
+    plan_kernel(n, terms, tasks, plan_ref)
+    copies[1].wait()
+
+
+def make_plan(tasks, left_ops, n, terms):
     most = source_places(tasks.shape[1], n) + chunk_of(n)
-    return pl.pallas_call(
-        functools.partial(plan_kernel, n, terms),
-        out_shape=jax.ShapeDtypeStruct((8, -(-most // 128) * 128), jnp.int32),
-        compiler_params=pltpu.CompilerParams(vmem_limit_bytes=16 * MIB),
-    )(tasks)
-
-
-def stage_kernel(left_ref, held_ref, sem):
-    copy = pltpu.make_async_copy(left_ref, held_ref, sem)
-    copy.start()
-    copy.wait()
-
-
-def stage(left_ops, n):
-    if not fits(n):
-        return left_ops
-    return pl.pallas_call(
-        stage_kernel,
-        in_specs=[pl.BlockSpec(memory_space=pltpu.HBM)],
-        out_specs=pl.BlockSpec(memory_space=pltpu.VMEM),
-        out_shape=jax.ShapeDtypeStruct(left_ops.shape, left_ops.dtype),
-        scratch_shapes=[pltpu.SemaphoreType.DMA],
-        compiler_params=pltpu.CompilerParams(vmem_limit_bytes=42 * MIB),
-    )(left_ops)
+    plan = jax.ShapeDtypeStruct((8, -(-most // 128) * 128), jnp.int32)
+    vmem, hbm = pl.BlockSpec(memory_space=pltpu.VMEM), pl.BlockSpec(memory_space=pltpu.HBM)
+    if fits(n):
+        return pl.pallas_call(
+            functools.partial(stage_kernel, n, terms),
+            in_specs=[hbm, hbm],
+            out_specs=(vmem, vmem),
+            out_shape=(plan, jax.ShapeDtypeStruct(left_ops.shape, left_ops.dtype)),
+            scratch_shapes=[pltpu.VMEM(tasks.shape, jnp.int32), pltpu.SemaphoreType.DMA((2,))],
+            compiler_params=pltpu.CompilerParams(vmem_limit_bytes=42 * MIB),
+        )(tasks, left_ops)
+    return (
+        pl.pallas_call(
+            functools.partial(plan_kernel, n, terms),
+            out_shape=plan,
+            compiler_params=pltpu.CompilerParams(vmem_limit_bytes=16 * MIB),
+        )(tasks),
+        left_ops,
+    )
 
 
 def block_parts(n, kinds, blocks, trial, right):
     parts = []
     for b, kind in enumerate(kinds):
-        first, second, rest = blocks[3 * b : 3 * b + 3]
-        some = first.shape[0] - TRIALS
-        others = rest.shape[0] // 2
-        for half, ref in enumerate((first, second)):
+        vectors, *terms = blocks[3 * b : 3 * b + 3]
+        for half, ref in enumerate(terms):
             owner = owner_of(*kind, half, n)
-            base = owner * (some + others)
-            parts.append((ref.at[pl.ds(0, TRIALS)], trial.at[owner]))
-            parts.append((ref.at[pl.ds(TRIALS, some)], right.at[pl.ds(base, some)]))
-            parts.append((rest.at[pl.ds(half * others, others)], right.at[pl.ds(base + some, others)]))
+            per = ref.shape[0]
+            parts.append((vectors.at[pl.ds(half * TRIALS, TRIALS)], trial.at[owner]))
+            parts.append((ref, right.at[pl.ds(owner * per, per)]))
     return parts
 
 
@@ -328,8 +332,7 @@
 
 def run_tasks(n, plan, left_ops, blocks):
     slots = left_ops.shape[0]
-    first, unused, rest = blocks[0][0]
-    terms_per = first.shape[0] - TRIALS + rest.shape[0] // 2
+    terms_per = blocks[0][0][1].shape[0]
     kinds = tuple(block[1:] for block in blocks)
     vmem, hbm = pl.BlockSpec(memory_space=pltpu.VMEM), pl.BlockSpec(memory_space=pltpu.HBM)
     given = vmem if fits(n) else hbm
@@ -350,7 +353,7 @@
             pltpu.VMEM((source_places(slots, n), 2, 128, 128), jnp.bfloat16),
             pltpu.VMEM((n, TRIALS, 128, 128), jnp.bfloat16),
             pltpu.VMEM((n * terms_per + 1, 128, 128), jnp.bfloat16),
-            pltpu.SemaphoreType.DMA((6 * len(blocks),)),
+            pltpu.SemaphoreType.DMA((4 * len(blocks),)),
         ]
         + fetched,
         compiler_params=pltpu.CompilerParams(vmem_limit_bytes=(30 if fits(n) else 58) * MIB),
@@ -364,8 +367,9 @@
     blocks, corr_ref = refs[:-1], refs[-1]
     total = [jnp.zeros((8, 128), jnp.float32)] * 3
     for ref in blocks:
-        t0, t1 = ref[0].astype(jnp.float32), ref[1].astype(jnp.float32)
-        total = [total[0] + fold(t0 * t0), total[1] + fold(t0 * t1), total[2] + fold(t1 * t1)]
+        for start in range(0, ref.shape[0], TRIALS):
+            t0, t1 = ref[start].astype(jnp.float32), ref[start + 1].astype(jnp.float32)
+            total = [total[0] + fold(t0 * t0), total[1] + fold(t0 * t1), total[2] + fold(t1 * t1)]
     c00, c01, c11 = [jnp.sum(x) for x in total]
     corr_ref[...] = matrix_of({(0, 0): c00, (0, 1): c01, (1, 0): c01, (1, 1): c11})[0:2, 0:2]
 
@@ -427,26 +431,17 @@
 
 def body(n, trial, left_ops, right_ops, task_list):
     steps = n // 4
-    left_ops = stage(left_ops, n)
-    some = right_ops.shape[0] // 2
-    own = jnp.concatenate([trial[0], right_ops[:some]], axis=0)
-    rest = jnp.concatenate([right_ops[some:], exchange(right_ops[some:], n, 1)], axis=0)
-    line = [own, exchange(own, n, 1), rest]
+    plan, left_ops = make_plan(task_list.T, left_ops, n, n * right_ops.shape[0])
+    vectors = jnp.concatenate([trial[0], exchange(trial[0], n, 1)], axis=0)
+    line = [vectors, right_ops, exchange(right_ops, n, 1)]
     blocks = [(line, 0, False)]
     for step in range(1, steps + 1):
-        if step == 2:
-            tasks, first = lax.optimization_barrier((task_list.T, line[0]))
-            line = [first, *line[1:]]
-            plan = make_plan(tasks, n, n * right_ops.shape[0])
-        if step == 3:
-            last, plan = lax.optimization_barrier((line[2], plan))
-            line = [*line[:2], last]
         line = [ring_step(value, n) for value in line]
         blocks.append((line, step, False))
         if step < steps:
             blocks.append(([exchange(value, n, 1) for value in line], step, True))
     send, keep, own = run_tasks(n, plan, left_ops, blocks)
-    send, arrays = lax.optimization_barrier((send, [value for block in blocks for value in block[0][:2]]))
+    send, arrays = lax.optimization_barrier((send, [block[0][0] for block in blocks]))
     correlation = correlate(arrays)
     mine, total, *sends = add_chip(keep, own, exchange(send, n, 1))
     received = [exchange(sends[j - 1], n, 2 * j) for j in reversed(range(1, n // 2))]

time: 63.2 us -> 60.4 us (0.956)
  starting transfers between devices: 34.1 us -> 31.9 us
  waiting for transfers between devices: 5.83 us -> 7.42 us
  Pallas kernels: 19.6 us -> 18.5 us
  local copies, waits for them, and re-layouts: 1.57 us -> 0.69 us
    ppermute x19, starting transfers between devices: 13.4 us -> 11.5 us  [exchange(): return lax.ppermute(value, 'op', [(i, i ^ mask) for i in range(n)])]
    ppermute x19, waiting for transfers between devices: 5.45 us -> 6.64 us  [exchange(): return lax.ppermute(value, 'op', [(i, i ^ mask) for i in range(n)])]
    pallas_call x2 -> x1, Pallas kernels: 4.37 us -> 3.4 us  [make_plan(): pl.pallas_call(functools.partial(stage_kernel, n, terms), in_specs=[hbm,...]
    slice x1 -> x0, local copies, waits for them, and re-layouts: 0.88 us -> none  [body(): own = jnp.concatenate([trial[0], right_ops[:some]], axis=0)]
  transfers between devices with their start and end apart: 31 -> 31, of which waited for: 7 -> 8; matrix products, arithmetic and copies ran while one was open for 1% -> 1% of each run, Pallas kernels for 9% -> 7%
where the time goes in v13:
time: 60.4 us; the launch traced here: 60.1 us
  starting transfers between devices  31.9 us (53%)
  Pallas kernels  18.5 us (31%)
  waiting for transfers between devices  7.42 us (12%)
  other arithmetic  0.85 us (1%)
  between operations  0.76 us (1%)
  local copies, waits for them, and re-layouts  0.69 us (1%)
    ppermute x12, starting transfers between devices, ring_step(): return lax.ppermute(value, 'op', pairs)  20.4 us
    pallas_call x1, Pallas kernels, run_tasks(): pl.pallas_call(functools.partial(tasks_kernel, n, kinds), out_shape=(jax....  13.2 us
    ppermute x19, starting transfers between devices, exchange(): return lax.ppermute(value, 'op', [(i, i ^ mask) for i in range(n)])  11.5 us
    ppermute x19, waiting for transfers between devices, exchange(): return lax.ppermute(value, 'op', [(i, i ^ mask) for i in range(n)])  6.64 us
    pallas_call x1, Pallas kernels, make_plan(): pl.pallas_call(functools.partial(stage_kernel, n, terms), in_specs=[hbm,...  3.4 us
  transfers between devices with their start and end apart: 31, of which 8 were waited for; matrix products, arithmetic and copies ran while one was open for 1% of the time, Pallas kernels for 7%

profile of v13, /device:TPU:0, one launch (start us, length us, event | category | flops | bytes accessed | tf_op | source)
XLA Modules:
  0.0 60.1 jit_solution(16331689908129732886)
XLA Ops:
  0.6 0.5 collective-permute-start
  1.2 0.1 collective-permute-start.1
  1.2 3.0 %collective-permute-start.3 = (bf16[4,128,128]{2,1,0:T(8,128)(2,1)}, bf16[4,128,128]{2,1,0:T(8,128)(2,1)S(1)}, u32[]{:S(2)}, u32[]{:S(2)}) collective-permute-start(bf16[4,128,128]{2,1,0:T(8,128)(2,1)} %refs_1_.1), channel_id=1, source_target_pairs={{0,4},{1,3},{4,8},{5,1},{8,12},{9,5},{12,14},{13,9},{14,10},{15,13... | collective-permute-start | bytes 393224 | tf_op jit(solution)/shard_map/ppermute | solution.py:31
  4.2 0.0 collective-permute-done
  4.2 0.9 %pad_maximum_fusion.refs_0_ = bf16[4,128,128]{2,1,0:T(8,128)(2,1)S(1)} fusion(bf16[2,128,128]{2,1,0:T(8,128)(2,1)S(1)} %collective-permute-done, bf16[2,128,128]{2,1,0:T(8,128)(2,1)} %bitcast.4), kind=kLoop, calls=%fused_computation | loop fusion | flops 65536 | bytes 262144 | tf_op jit(solution)/shard_map/concatenate | solution.py:435
  5.1 1.6 %collective-permute-start.2 = (bf16[4,128,128]{2,1,0:T(8,128)(2,1)S(1)}, bf16[4,128,128]{2,1,0:T(8,128)(2,1)S(1)}, u32[]{:S(2)}, u32[]{:S(2)}) collective-permute-start(bf16[4,128,128]{2,1,0:T(8,128)(2,1)S(1)} %pad_maximum_fusion.refs_0_), channel_id=1, source_target_pairs={{0,4},{1,3},{4,8},{5,1},{8,12},{9,5},{12,14},{13,9},{14,10},{15,13... | collective-permute-start | bytes 393224 | tf_op jit(solution)/shard_map/ppermute | solution.py:31
  6.7 0.0 collective-permute-done.1.refs_2_
  6.7 1.6 %collective-permute-start.4 = (bf16[4,128,128]{2,1,0:T(8,128)(2,1)S(1)}, bf16[4,128,128]{2,1,0:T(8,128)(2,1)S(1)}, u32[]{:S(2)}, u32[]{:S(2)}) collective-permute-start(bf16[4,128,128]{2,1,0:T(8,128)(2,1)S(1)} %collective-permute-done.1.refs_2_), channel_id=1, source_target_pairs={{0,4},{1,3},{4,8},{5,1},{8,12},{9,5},{12,14},{13,9},{14,10},{15,13... | collective-permute-start | bytes 393224 | tf_op jit(solution)/shard_map/ppermute | solution.py:31
  8.3 0.0 collective-permute-done.3.refs_4_
  8.3 1.5 %collective-permute-start.9 = (bf16[4,128,128]{2,1,0:T(8,128)(2,1)S(1)}, bf16[4,128,128]{2,1,0:T(8,128)(2,1)S(1)}, u32[]{:S(2)}, u32[]{:S(2)}) collective-permute-start(bf16[4,128,128]{2,1,0:T(8,128)(2,1)S(1)} %collective-permute-done.3.refs_4_), channel_id=1, source_target_pairs={{0,4},{1,3},{4,8},{5,1},{8,12},{9,5},{12,14},{13,9},{14,10},{15,13... | collective-permute-start | bytes 393224 | tf_op jit(solution)/shard_map/ppermute | solution.py:31
  9.8 0.0 collective-permute-start.6
  9.8 0.3 collective-permute-done.2.refs_3_.refs_1_
  10.1 1.6 %collective-permute-start.8 = (bf16[4,128,128]{2,1,0:T(8,128)(2,1)S(1)}, bf16[4,128,128]{2,1,0:T(8,128)(2,1)S(1)}, u32[]{:S(2)}, u32[]{:S(2)}) collective-permute-start(bf16[4,128,128]{2,1,0:T(8,128)(2,1)S(1)} %collective-permute-done.2.refs_3_.refs_1_), channel_id=1, source_target_pairs={{0,4},{1,3},{4,8},{5,1},{8,12},{9,5},{12,14},{13,9},{14,10},{15,13... | collective-permute-start | bytes 393224 | tf_op jit(solution)/shard_map/ppermute | solution.py:31
  11.7 0.0 collective-permute-start.5
  11.7 0.0 collective-permute-done.4.refs_5_
  11.7 1.6 %collective-permute-start.10 = (bf16[4,128,128]{2,1,0:T(8,128)(2,1)S(1)}, bf16[4,128,128]{2,1,0:T(8,128)(2,1)S(1)}, u32[]{:S(2)}, u32[]{:S(2)}) collective-permute-start(bf16[4,128,128]{2,1,0:T(8,128)(2,1)S(1)} %collective-permute-done.4.refs_5_), channel_id=1, source_target_pairs={{0,4},{1,3},{4,8},{5,1},{8,12},{9,5},{12,14},{13,9},{14,10},{15,13... | collective-permute-start | bytes 393224 | tf_op jit(solution)/shard_map/ppermute | solution.py:31
  13.3 0.0 collective-permute-done.9.refs_10_
  13.3 0.0 collective-permute-start.7
  13.3 0.0 collective-permute-done.6.refs_7_
  13.3 1.6 %collective-permute-start.15 = (bf16[4,128,128]{2,1,0:T(8,128)(2,1)S(1)}, bf16[4,128,128]{2,1,0:T(8,128)(2,1)S(1)}, u32[]{:S(2)}, u32[]{:S(2)}) collective-permute-start(bf16[4,128,128]{2,1,0:T(8,128)(2,1)S(1)} %collective-permute-done.9.refs_10_), channel_id=1, source_target_pairs={{0,4},{1,3},{4,8},{5,1},{8,12},{9,5},{12,14},{13,9},{14,10},{15,13... | collective-permute-start | bytes 393224 | tf_op jit(solution)/shard_map/ppermute | solution.py:31
  14.9 0.2 collective-permute-done.8.refs_9_.refs_3_
  15.1 0.0 collective-permute-start.12
  15.1 0.0 collective-permute-done.5.refs_6_.refs_2_
  15.1 1.6 %collective-permute-start.14 = (bf16[4,128,128]{2,1,0:T(8,128)(2,1)S(1)}, bf16[4,128,128]{2,1,0:T(8,128)(2,1)S(1)}, u32[]{:S(2)}, u32[]{:S(2)}) collective-permute-start(bf16[4,128,128]{2,1,0:T(8,128)(2,1)S(1)} %collective-permute-done.8.refs_9_.refs_3_), channel_id=1, source_target_pairs={{0,4},{1,3},{4,8},{5,1},{8,12},{9,5},{12,14},{13,9},{14,10},{15,13... | collective-permute-start | bytes 393224 | tf_op jit(solution)/shard_map/ppermute | solution.py:31
  16.7 0.0 collective-permute-start.11
  16.7 0.0 collective-permute-done.7.refs_8_
  16.7 1.6 %collective-permute-start.16 = (bf16[4,128,128]{2,1,0:T(8,128)(2,1)S(1)}, bf16[4,128,128]{2,1,0:T(8,128)(2,1)S(1)}, u32[]{:S(2)}, u32[]{:S(2)}) collective-permute-start(bf16[4,128,128]{2,1,0:T(8,128)(2,1)S(1)} %collective-permute-done.10.refs_11_), channel_id=1, source_target_pairs={{0,4},{1,3},{4,8},{5,1},{8,12},{9,5},{12,14},{13,9},{14,10},{15,13... | collective-permute-start | bytes 393224 | tf_op jit(solution)/shard_map/ppermute | solution.py:31
  18.3 0.0 collective-permute-start.13
  18.3 0.0 collective-permute-done.12.refs_13_
  18.3 1.6 %collective-permute-start.21 = (bf16[4,128,128]{2,1,0:T(8,128)(2,1)S(1)}, bf16[4,128,128]{2,1,0:T(8,128)(2,1)S(1)}, u32[]{:S(2)}, u32[]{:S(2)}) collective-permute-start(bf16[4,128,128]{2,1,0:T(8,128)(2,1)S(1)} %collective-permute-done.15.refs_16_), channel_id=1, source_target_pairs={{0,4},{1,3},{4,8},{5,1},{8,12},{9,5},{12,14},{13,9},{14,10},{15,13... | collective-permute-start | bytes 393224 | tf_op jit(solution)/shard_map/ppermute | solution.py:31
  19.9 0.2 collective-permute-done.14.refs_15_.refs_5_
  20.1 0.0 collective-permute-done.11.refs_12_.refs_4_
  20.1 1.6 %collective-permute-start.20 = (bf16[4,128,128]{2,1,0:T(8,128)(2,1)S(1)}, bf16[4,128,128]{2,1,0:T(8,128)(2,1)S(1)}, u32[]{:S(2)}, u32[]{:S(2)}) collective-permute-start(bf16[4,128,128]{2,1,0:T(8,128)(2,1)S(1)} %collective-permute-done.14.refs_15_.refs_5_), channel_id=1, source_target_pairs={{0,4},{1,3},{4,8},{5,1},{8,12},{9,5},{12,14},{13,9},{14,10},{15,13... | collective-permute-start | bytes 393224 | tf_op jit(solution)/shard_map/ppermute | solution.py:31
  21.6 0.1 collective-permute-done.16.refs_17_
  21.7 0.0 collective-permute-start.17
  21.7 0.0 collective-permute-done.13.refs_14_
  21.7 1.6 %collective-permute-start.22 = (bf16[4,128,128]{2,1,0:T(8,128)(2,1)S(1)}, bf16[4,128,128]{2,1,0:T(8,128)(2,1)S(1)}, u32[]{:S(2)}, u32[]{:S(2)}) collective-permute-start(bf16[4,128,128]{2,1,0:T(8,128)(2,1)S(1)} %collective-permute-done.16.refs_17_), channel_id=1, source_target_pairs={{0,4},{1,3},{4,8},{5,1},{8,12},{9,5},{12,14},{13,9},{14,10},{15,13... | collective-permute-start | bytes 393224 | tf_op jit(solution)/shard_map/ppermute | solution.py:31
  23.3 0.0 collective-permute-done.21.refs_22_
  23.3 0.0 collective-permute-start.19
  23.4 0.7 %copy-done = s32[256,4]{0,1:T(4,128)S(1)} copy-done((s32[256,4]{0,1:T(4,128)S(1)}, s32[256,4]{0,1:T(4,128)}, u32[]{:S(2)}) %copy-start) | copy-done | bytes 4120
  24.0 3.4 %shard_map.67 = (s32[8,512]{1,0:T(8,128)S(1)}, bf16[256,128,128]{2,1,0:T(8,128)(2,1)S(1)}) custom-call(s32[4,256]{1,0:T(4,128)S(1)} %bitcast.2, bf16[256,128,128]{2,1,0:T(8,128)(2,1)} %left_ref.1), custom_call_target="tpu_custom_call" | custom-call | tf_op jit(solution)/shard_map/pallas_call | solution.py:185
  27.4 0.0 collective-permute-done.18.refs_19_
  27.5 0.0 collective-permute-done.17.refs_18_.refs_6_
  27.5 0.0 collective-permute-done.22.refs_23_
  27.5 13.2 %shard_map.68 = (bf16[2064,128]{1,0:T(8,128)(2,1)S(1)}, f32[17,256,128]{2,1,0:T(8,128)S(1)}, f32[8,128]{1,0:T(8,128)S(1)}) custom-call(s32[8,512]{1,0:T(8,128)S(1)} %get-tuple-element.28.plan_ref, bf16[256,128,128]{2,1,0:T(8,128)(2,1)S(1)} %get-tuple-element.29.left_ref, bf16[4,128,128]{2,1,0:T(8,128)(2,1)S(1)} %pad_maximum_fusion.refs_0_, ...), custom_call_target="tpu_custom_call" | custom-call | flops 4294967296 | bytes 15588608 | tf_op jit(solution)/shard_map/pallas_call | solution.py:343
  40.7 0.1 collective-permute-start.23
  40.8 1.9 %collective-permute-done.23.received_ref = bf16[2064,128]{1,0:T(8,128)(2,1)S(1)} collective-permute-done((bf16[2064,128]{1,0:T(8,128)(2,1)S(1)}, bf16[2064,128]{1,0:T(8,128)(2,1)S(1)}, u32[]{:S(2)}, u32[]{:S(2)}) %collective-permute-start.23) | collective-permute-done | bytes 528416 | tf_op jit(solution)/shard_map/ppermute | solution.py:17
  42.7 0.1 shard_map.69
  42.8 4.2 %collective-permute-start.24 = (bf16[272,128]{1,0:T(8,128)(2,1)S(1)}, bf16[272,128]{1,0:T(8,128)(2,1)S(1)}, u32[]{:S(2)}, u32[]{:S(2)}) collective-permute-start(bf16[272,128]{1,0:T(8,128)(2,1)S(1)} %get-tuple-element.36), channel_id=1, source_target_pairs={{0,14},{1,15},{2,12},{3,13},{4,10},{5,11},{6,8},{7,9},{8,6},{9,7},... | collective-permute-start | bytes 208904 | tf_op jit(solution)/shard_map/ppermute | solution.py:17
  47.0 0.2 collective-permute-start.25
  47.2 0.9 %collective-permute-start.26 = (bf16[272,128]{1,0:T(8,128)(2,1)S(1)}, bf16[272,128]{1,0:T(8,128)(2,1)S(1)}, u32[]{:S(2)}, u32[]{:S(2)}) collective-permute-start(bf16[272,128]{1,0:T(8,128)(2,1)S(1)} %get-tuple-element.38), channel_id=1, source_target_pairs={{0,10},{1,11},{2,8},{3,9},{4,14},{5,15},{6,12},{7,13},{8,2},{9,3},... | collective-permute-start | bytes 208904 | tf_op jit(solution)/shard_map/ppermute | solution.py:17
  48.1 2.4 %collective-permute-start.27 = (bf16[272,128]{1,0:T(8,128)(2,1)S(1)}, bf16[272,128]{1,0:T(8,128)(2,1)S(1)}, u32[]{:S(2)}, u32[]{:S(2)}) collective-permute-start(bf16[272,128]{1,0:T(8,128)(2,1)S(1)} %get-tuple-element.39), channel_id=1, source_target_pairs={{0,8},{1,9},{2,10},{3,11},{4,12},{5,13},{6,14},{7,15},{8,0},{9,1},... | collective-permute-start | bytes 208904 | tf_op jit(solution)/shard_map/ppermute | solution.py:17
  50.5 1.8 %collective-permute-start.28 = (bf16[272,128]{1,0:T(8,128)(2,1)S(1)}, bf16[272,128]{1,0:T(8,128)(2,1)S(1)}, u32[]{:S(2)}, u32[]{:S(2)}) collective-permute-start(bf16[272,128]{1,0:T(8,128)(2,1)S(1)} %get-tuple-element.40), channel_id=1, source_target_pairs={{0,6},{1,7},{2,4},{3,5},{4,2},{5,3},{6,0},{7,1},{8,14},{9,15},{10,... | collective-permute-start | bytes 208904 | tf_op jit(solution)/shard_map/ppermute | solution.py:17
  52.3 0.0 collective-permute-done.24.refs_0_
  52.3 0.8 %collective-permute-start.29 = (bf16[272,128]{1,0:T(8,128)(2,1)S(1)}, bf16[272,128]{1,0:T(8,128)(2,1)S(1)}, u32[]{:S(2)}, u32[]{:S(2)}) collective-permute-start(bf16[272,128]{1,0:T(8,128)(2,1)S(1)} %get-tuple-element.41), channel_id=1, source_target_pairs={{0,4},{1,5},{2,6},{3,7},{4,0},{5,1},{6,2},{7,3},{8,12},{9,13},{10,... | collective-permute-start | bytes 208904 | tf_op jit(solution)/shard_map/ppermute | solution.py:17
  53.1 0.8 %collective-permute-done.25.refs_1_ = bf16[272,128]{1,0:T(8,128)(2,1)S(1)} collective-permute-done((bf16[272,128]{1,0:T(8,128)(2,1)S(1)}, bf16[272,128]{1,0:T(8,128)(2,1)S(1)}, u32[]{:S(2)}, u32[]{:S(2)}) %collective-permute-start.25) | collective-permute-done | bytes 69664 | tf_op jit(solution)/shard_map/ppermute | solution.py:17
  53.9 0.6 collective-permute-start.30
  54.5 1.0 %shard_map.71 = f32[2,2]{1,0:T(2,128)} custom-call(bf16[4,128,128]{2,1,0:T(8,128)(2,1)S(1)} %pad_maximum_fusion.refs_0_, bf16[4,128,128]{2,1,0:T(8,128)(2,1)S(1)} %collective-permute-done.2.refs_3_.refs_1_, bf16[4,128,128]{2,1,0:T(8,128)(2,1)S(1)} %collective-permute-done.5.refs_6_.refs_2_, bf16[4,128,128]{2,1,0:T(8,128)(2,1)S(1)} %collective-permute-done.8.refs_9_.refs_3_, ...), custom_call_target="tpu_custom_call" | custom-call | tf_op jit(solution)/shard_map/pallas_call | solution.py:378
  55.5 2.3 %collective-permute-done.26.refs_2_ = bf16[272,128]{1,0:T(8,128)(2,1)S(1)} collective-permute-done((bf16[272,128]{1,0:T(8,128)(2,1)S(1)}, bf16[272,128]{1,0:T(8,128)(2,1)S(1)}, u32[]{:S(2)}, u32[]{:S(2)}) %collective-permute-start.26) | collective-permute-done | bytes 69664 | tf_op jit(solution)/shard_map/ppermute | solution.py:17
  57.8 1.5 %collective-permute-done.27.refs_3_ = bf16[272,128]{1,0:T(8,128)(2,1)S(1)} collective-permute-done((bf16[272,128]{1,0:T(8,128)(2,1)S(1)}, bf16[272,128]{1,0:T(8,128)(2,1)S(1)}, u32[]{:S(2)}, u32[]{:S(2)}) %collective-permute-start.27) | collective-permute-done | bytes 69664 | tf_op jit(solution)/shard_map/ppermute | solution.py:17
  59.3 0.0 collective-permute-done.28.refs_4_
  59.3 0.0 collective-permute-done.29.refs_5_
  59.3 0.0 collective-permute-done.30.refs_6_
  59.3 0.7 %shard_map.70 = (f32[1,2,128,128]{3,2,1,0:T(8,128)}, f32[2,2]{1,0:T(2,128)}) custom-call(f32[256,128]{1,0:T(8,128)S(1)} %get-tuple-element.34.mine_ref, f32[16,128]{1,0:T(8,128)S(1)} %get-tuple-element.35.total_ref, bf16[272,128]{1,0:T(8,128)(2,1)S(1)} %collective-permute-done.24.refs_0_, bf16[272,128]{1,0:T(8,128)(2,1)S(1)} %collective-permute-done.25.refs_1_, ...), custom_call_target="tpu_custom_call" | custom-call | tf_op jit(solution)/shard_map/pallas_call | solution.py:422
  (8 shorter events, 0.0 us)
Async XLA Ops:
  0.6 26.9 %copy-start.1 = (bf16[4,128,128]{2,1,0:T(8,128)(2,1)S(1)}, bf16[4,128,128]{2,1,0:T(8,128)(2,1)}, u32[]{:S(2)}) copy-start(bf16[4,128,128]{2,1,0:T(8,128)(2,1)} %refs_1_.1) | copy-start | bytes 393220
  0.6 3.6 %collective-permute-start = (bf16[2,128,128]{2,1,0:T(8,128)(2,1)}, bf16[2,128,128]{2,1,0:T(8,128)(2,1)S(1)}, u32[]{:S(2)}, u32[]{:S(2)}) collective-permute-start(bf16[2,128,128]{2,1,0:T(8,128)(2,1)} %bitcast.3), channel_id=1, source_target_pairs={{0,1},{1,0},{2,3},{3,2},{4,5},{5,4},{6,7},{7,6},{8,9},{9,8},{10,11... | collective-permute-start | bytes 196616 | tf_op jit(solution)/shard_map/ppermute | solution.py:17
  1.2 5.6 %collective-permute-start.1 = (bf16[4,128,128]{2,1,0:T(8,128)(2,1)}, bf16[4,128,128]{2,1,0:T(8,128)(2,1)S(1)}, u32[]{:S(2)}, u32[]{:S(2)}) collective-permute-start(bf16[4,128,128]{2,1,0:T(8,128)(2,1)} %refs_1_.1), channel_id=1, source_target_pairs={{0,1},{1,0},{2,3},{3,2},{4,5},{5,4},{6,7},{7,6},{8,9},{9,8},{10,11... | collective-permute-start | bytes 393224 | tf_op jit(solution)/shard_map/ppermute | solution.py:17
  1.2 7.1 %collective-permute-start.3 = (bf16[4,128,128]{2,1,0:T(8,128)(2,1)}, bf16[4,128,128]{2,1,0:T(8,128)(2,1)S(1)}, u32[]{:S(2)}, u32[]{:S(2)}) collective-permute-start(bf16[4,128,128]{2,1,0:T(8,128)(2,1)} %refs_1_.1), channel_id=1, source_target_pairs={{0,4},{1,3},{4,8},{5,1},{8,12},{9,5},{12,14},{13,9},{14,10},{15,13... | collective-permute-start | bytes 393224 | tf_op jit(solution)/shard_map/ppermute | solution.py:31
  5.1 5.0 %collective-permute-start.2 = (bf16[4,128,128]{2,1,0:T(8,128)(2,1)S(1)}, bf16[4,128,128]{2,1,0:T(8,128)(2,1)S(1)}, u32[]{:S(2)}, u32[]{:S(2)}) collective-permute-start(bf16[4,128,128]{2,1,0:T(8,128)(2,1)S(1)} %pad_maximum_fusion.refs_0_), channel_id=1, source_target_pairs={{0,4},{1,3},{4,8},{5,1},{8,12},{9,5},{12,14},{13,9},{14,10},{15,13... | collective-permute-start | bytes 393224 | tf_op jit(solution)/shard_map/ppermute | solution.py:31
  6.7 5.0 %collective-permute-start.4 = (bf16[4,128,128]{2,1,0:T(8,128)(2,1)S(1)}, bf16[4,128,128]{2,1,0:T(8,128)(2,1)S(1)}, u32[]{:S(2)}, u32[]{:S(2)}) collective-permute-start(bf16[4,128,128]{2,1,0:T(8,128)(2,1)S(1)} %collective-permute-done.1.refs_2_), channel_id=1, source_target_pairs={{0,4},{1,3},{4,8},{5,1},{8,12},{9,5},{12,14},{13,9},{14,10},{15,13... | collective-permute-start | bytes 393224 | tf_op jit(solution)/shard_map/ppermute | solution.py:31
  8.3 5.0 %collective-permute-start.9 = (bf16[4,128,128]{2,1,0:T(8,128)(2,1)S(1)}, bf16[4,128,128]{2,1,0:T(8,128)(2,1)S(1)}, u32[]{:S(2)}, u32[]{:S(2)}) collective-permute-start(bf16[4,128,128]{2,1,0:T(8,128)(2,1)S(1)} %collective-permute-done.3.refs_4_), channel_id=1, source_target_pairs={{0,4},{1,3},{4,8},{5,1},{8,12},{9,5},{12,14},{13,9},{14,10},{15,13... | collective-permute-start | bytes 393224 | tf_op jit(solution)/shard_map/ppermute | solution.py:31
  9.8 3.5 %collective-permute-start.6 = (bf16[4,128,128]{2,1,0:T(8,128)(2,1)S(1)}, bf16[4,128,128]{2,1,0:T(8,128)(2,1)S(1)}, u32[]{:S(2)}, u32[]{:S(2)}) collective-permute-start(bf16[4,128,128]{2,1,0:T(8,128)(2,1)S(1)} %collective-permute-done.3.refs_4_), channel_id=1, source_target_pairs={{0,1},{1,0},{2,3},{3,2},{4,5},{5,4},{6,7},{7,6},{8,9},{9,8},{10,11... | collective-permute-start | bytes 393224 | tf_op jit(solution)/shard_map/ppermute | solution.py:17
  10.1 5.0 %collective-permute-start.8 = (bf16[4,128,128]{2,1,0:T(8,128)(2,1)S(1)}, bf16[4,128,128]{2,1,0:T(8,128)(2,1)S(1)}, u32[]{:S(2)}, u32[]{:S(2)}) collective-permute-start(bf16[4,128,128]{2,1,0:T(8,128)(2,1)S(1)} %collective-permute-done.2.refs_3_.refs_1_), channel_id=1, source_target_pairs={{0,4},{1,3},{4,8},{5,1},{8,12},{9,5},{12,14},{13,9},{14,10},{15,13... | collective-permute-start | bytes 393224 | tf_op jit(solution)/shard_map/ppermute | solution.py:31
  11.7 3.4 %collective-permute-start.5 = (bf16[4,128,128]{2,1,0:T(8,128)(2,1)S(1)}, bf16[4,128,128]{2,1,0:T(8,128)(2,1)S(1)}, u32[]{:S(2)}, u32[]{:S(2)}) collective-permute-start(bf16[4,128,128]{2,1,0:T(8,128)(2,1)S(1)} %collective-permute-done.2.refs_3_.refs_1_), channel_id=1, source_target_pairs={{0,1},{1,0},{2,3},{3,2},{4,5},{5,4},{6,7},{7,6},{8,9},{9,8},{10,11... | collective-permute-start | bytes 393224 | tf_op jit(solution)/shard_map/ppermute | solution.py:17
  11.7 5.0 %collective-permute-start.10 = (bf16[4,128,128]{2,1,0:T(8,128)(2,1)S(1)}, bf16[4,128,128]{2,1,0:T(8,128)(2,1)S(1)}, u32[]{:S(2)}, u32[]{:S(2)}) collective-permute-start(bf16[4,128,128]{2,1,0:T(8,128)(2,1)S(1)} %collective-permute-done.4.refs_5_), channel_id=1, source_target_pairs={{0,4},{1,3},{4,8},{5,1},{8,12},{9,5},{12,14},{13,9},{14,10},{15,13... | collective-permute-start | bytes 393224 | tf_op jit(solution)/shard_map/ppermute | solution.py:31
  13.3 3.4 %collective-permute-start.7 = (bf16[4,128,128]{2,1,0:T(8,128)(2,1)S(1)}, bf16[4,128,128]{2,1,0:T(8,128)(2,1)S(1)}, u32[]{:S(2)}, u32[]{:S(2)}) collective-permute-start(bf16[4,128,128]{2,1,0:T(8,128)(2,1)S(1)} %collective-permute-done.4.refs_5_), channel_id=1, source_target_pairs={{0,1},{1,0},{2,3},{3,2},{4,5},{5,4},{6,7},{7,6},{8,9},{9,8},{10,11... | collective-permute-start | bytes 393224 | tf_op jit(solution)/shard_map/ppermute | solution.py:17
  13.3 5.0 %collective-permute-start.15 = (bf16[4,128,128]{2,1,0:T(8,128)(2,1)S(1)}, bf16[4,128,128]{2,1,0:T(8,128)(2,1)S(1)}, u32[]{:S(2)}, u32[]{:S(2)}) collective-permute-start(bf16[4,128,128]{2,1,0:T(8,128)(2,1)S(1)} %collective-permute-done.9.refs_10_), channel_id=1, source_target_pairs={{0,4},{1,3},{4,8},{5,1},{8,12},{9,5},{12,14},{13,9},{14,10},{15,13... | collective-permute-start | bytes 393224 | tf_op jit(solution)/shard_map/ppermute | solution.py:31
  15.1 3.2 %collective-permute-start.12 = (bf16[4,128,128]{2,1,0:T(8,128)(2,1)S(1)}, bf16[4,128,128]{2,1,0:T(8,128)(2,1)S(1)}, u32[]{:S(2)}, u32[]{:S(2)}) collective-permute-start(bf16[4,128,128]{2,1,0:T(8,128)(2,1)S(1)} %collective-permute-done.9.refs_10_), channel_id=1, source_target_pairs={{0,1},{1,0},{2,3},{3,2},{4,5},{5,4},{6,7},{7,6},{8,9},{9,8},{10,11... | collective-permute-start | bytes 393224 | tf_op jit(solution)/shard_map/ppermute | solution.py:17
  15.1 5.0 %collective-permute-start.14 = (bf16[4,128,128]{2,1,0:T(8,128)(2,1)S(1)}, bf16[4,128,128]{2,1,0:T(8,128)(2,1)S(1)}, u32[]{:S(2)}, u32[]{:S(2)}) collective-permute-start(bf16[4,128,128]{2,1,0:T(8,128)(2,1)S(1)} %collective-permute-done.8.refs_9_.refs_3_), channel_id=1, source_target_pairs={{0,4},{1,3},{4,8},{5,1},{8,12},{9,5},{12,14},{13,9},{14,10},{15,13... | collective-permute-start | bytes 393224 | tf_op jit(solution)/shard_map/ppermute | solution.py:31
  16.7 3.4 %collective-permute-start.11 = (bf16[4,128,128]{2,1,0:T(8,128)(2,1)S(1)}, bf16[4,128,128]{2,1,0:T(8,128)(2,1)S(1)}, u32[]{:S(2)}, u32[]{:S(2)}) collective-permute-start(bf16[4,128,128]{2,1,0:T(8,128)(2,1)S(1)} %collective-permute-done.8.refs_9_.refs_3_), channel_id=1, source_target_pairs={{0,1},{1,0},{2,3},{3,2},{4,5},{5,4},{6,7},{7,6},{8,9},{9,8},{10,11... | collective-permute-start | bytes 393224 | tf_op jit(solution)/shard_map/ppermute | solution.py:17
  16.7 5.0 %collective-permute-start.16 = (bf16[4,128,128]{2,1,0:T(8,128)(2,1)S(1)}, bf16[4,128,128]{2,1,0:T(8,128)(2,1)S(1)}, u32[]{:S(2)}, u32[]{:S(2)}) collective-permute-start(bf16[4,128,128]{2,1,0:T(8,128)(2,1)S(1)} %collective-permute-done.10.refs_11_), channel_id=1, source_target_pairs={{0,4},{1,3},{4,8},{5,1},{8,12},{9,5},{12,14},{13,9},{14,10},{15,13... | collective-permute-start | bytes 393224 | tf_op jit(solution)/shard_map/ppermute | solution.py:31
  18.3 3.4 %collective-permute-start.13 = (bf16[4,128,128]{2,1,0:T(8,128)(2,1)S(1)}, bf16[4,128,128]{2,1,0:T(8,128)(2,1)S(1)}, u32[]{:S(2)}, u32[]{:S(2)}) collective-permute-start(bf16[4,128,128]{2,1,0:T(8,128)(2,1)S(1)} %collective-permute-done.10.refs_11_), channel_id=1, source_target_pairs={{0,1},{1,0},{2,3},{3,2},{4,5},{5,4},{6,7},{7,6},{8,9},{9,8},{10,11... | collective-permute-start | bytes 393224 | tf_op jit(solution)/shard_map/ppermute | solution.py:17
  18.3 5.0 %collective-permute-start.21 = (bf16[4,128,128]{2,1,0:T(8,128)(2,1)S(1)}, bf16[4,128,128]{2,1,0:T(8,128)(2,1)S(1)}, u32[]{:S(2)}, u32[]{:S(2)}) collective-permute-start(bf16[4,128,128]{2,1,0:T(8,128)(2,1)S(1)} %collective-permute-done.15.refs_16_), channel_id=1, source_target_pairs={{0,4},{1,3},{4,8},{5,1},{8,12},{9,5},{12,14},{13,9},{14,10},{15,13... | collective-permute-start | bytes 393224 | tf_op jit(solution)/shard_map/ppermute | solution.py:31
  20.1 7.4 %collective-permute-start.18 = (bf16[4,128,128]{2,1,0:T(8,128)(2,1)S(1)}, bf16[4,128,128]{2,1,0:T(8,128)(2,1)S(1)}, u32[]{:S(2)}, u32[]{:S(2)}) collective-permute-start(bf16[4,128,128]{2,1,0:T(8,128)(2,1)S(1)} %collective-permute-done.15.refs_16_), channel_id=1, source_target_pairs={{0,1},{1,0},{2,3},{3,2},{4,5},{5,4},{6,7},{7,6},{8,9},{9,8},{10,11... | collective-permute-start | bytes 393224 | tf_op jit(solution)/shard_map/ppermute | solution.py:17
  20.1 7.4 %collective-permute-start.20 = (bf16[4,128,128]{2,1,0:T(8,128)(2,1)S(1)}, bf16[4,128,128]{2,1,0:T(8,128)(2,1)S(1)}, u32[]{:S(2)}, u32[]{:S(2)}) collective-permute-start(bf16[4,128,128]{2,1,0:T(8,128)(2,1)S(1)} %collective-permute-done.14.refs_15_.refs_5_), channel_id=1, source_target_pairs={{0,4},{1,3},{4,8},{5,1},{8,12},{9,5},{12,14},{13,9},{14,10},{15,13... | collective-permute-start | bytes 393224 | tf_op jit(solution)/shard_map/ppermute | solution.py:31
  21.7 5.8 %collective-permute-start.17 = (bf16[4,128,128]{2,1,0:T(8,128)(2,1)S(1)}, bf16[4,128,128]{2,1,0:T(8,128)(2,1)S(1)}, u32[]{:S(2)}, u32[]{:S(2)}) collective-permute-start(bf16[4,128,128]{2,1,0:T(8,128)(2,1)S(1)} %collective-permute-done.14.refs_15_.refs_5_), channel_id=1, source_target_pairs={{0,1},{1,0},{2,3},{3,2},{4,5},{5,4},{6,7},{7,6},{8,9},{9,8},{10,11... | collective-permute-start | bytes 393224 | tf_op jit(solution)/shard_map/ppermute | solution.py:17
  21.7 5.8 %collective-permute-start.22 = (bf16[4,128,128]{2,1,0:T(8,128)(2,1)S(1)}, bf16[4,128,128]{2,1,0:T(8,128)(2,1)S(1)}, u32[]{:S(2)}, u32[]{:S(2)}) collective-permute-start(bf16[4,128,128]{2,1,0:T(8,128)(2,1)S(1)} %collective-permute-done.16.refs_17_), channel_id=1, source_target_pairs={{0,4},{1,3},{4,8},{5,1},{8,12},{9,5},{12,14},{13,9},{14,10},{15,13... | collective-permute-start | bytes 393224 | tf_op jit(solution)/shard_map/ppermute | solution.py:31
  23.3 4.1 %collective-permute-start.19 = (bf16[4,128,128]{2,1,0:T(8,128)(2,1)S(1)}, bf16[4,128,128]{2,1,0:T(8,128)(2,1)S(1)}, u32[]{:S(2)}, u32[]{:S(2)}) collective-permute-start(bf16[4,128,128]{2,1,0:T(8,128)(2,1)S(1)} %collective-permute-done.16.refs_17_), channel_id=1, source_target_pairs={{0,1},{1,0},{2,3},{3,2},{4,5},{5,4},{6,7},{7,6},{8,9},{9,8},{10,11... | collective-permute-start | bytes 393224 | tf_op jit(solution)/shard_map/ppermute | solution.py:17
  23.4 0.7 %copy-start = (s32[256,4]{0,1:T(4,128)S(1)}, s32[256,4]{0,1:T(4,128)}, u32[]{:S(2)}) copy-start(s32[256,4]{0,1:T(4,128)} %param.7) | copy-start | bytes 12292
  40.7 2.0 %collective-permute-start.23 = (bf16[2064,128]{1,0:T(8,128)(2,1)S(1)}, bf16[2064,128]{1,0:T(8,128)(2,1)S(1)}, u32[]{:S(2)}, u32[]{:S(2)}) collective-permute-start(bf16[2064,128]{1,0:T(8,128)(2,1)S(1)} %get-tuple-element.33), channel_id=1, source_target_pairs={{0,1},{1,0},{2,3},{3,2},{4,5},{5,4},{6,7},{7,6},{8,9},{9,8},{10,11... | collective-permute-start | bytes 1585160 | tf_op jit(solution)/shard_map/ppermute | solution.py:17
  42.8 9.5 %collective-permute-start.24 = (bf16[272,128]{1,0:T(8,128)(2,1)S(1)}, bf16[272,128]{1,0:T(8,128)(2,1)S(1)}, u32[]{:S(2)}, u32[]{:S(2)}) collective-permute-start(bf16[272,128]{1,0:T(8,128)(2,1)S(1)} %get-tuple-element.36), channel_id=1, source_target_pairs={{0,14},{1,15},{2,12},{3,13},{4,10},{5,11},{6,8},{7,9},{8,6},{9,7},... | collective-permute-start | bytes 208904 | tf_op jit(solution)/shard_map/ppermute | solution.py:17
  47.0 6.9 %collective-permute-start.25 = (bf16[272,128]{1,0:T(8,128)(2,1)S(1)}, bf16[272,128]{1,0:T(8,128)(2,1)S(1)}, u32[]{:S(2)}, u32[]{:S(2)}) collective-permute-start(bf16[272,128]{1,0:T(8,128)(2,1)S(1)} %get-tuple-element.37), channel_id=1, source_target_pairs={{0,12},{1,13},{2,14},{3,15},{4,8},{5,9},{6,10},{7,11},{8,4},{9,5},... | collective-permute-start | bytes 208904 | tf_op jit(solution)/shard_map/ppermute | solution.py:17
  47.2 10.6 %collective-permute-start.26 = (bf16[272,128]{1,0:T(8,128)(2,1)S(1)}, bf16[272,128]{1,0:T(8,128)(2,1)S(1)}, u32[]{:S(2)}, u32[]{:S(2)}) collective-permute-start(bf16[272,128]{1,0:T(8,128)(2,1)S(1)} %get-tuple-element.38), channel_id=1, source_target_pairs={{0,10},{1,11},{2,8},{3,9},{4,14},{5,15},{6,12},{7,13},{8,2},{9,3},... | collective-permute-start | bytes 208904 | tf_op jit(solution)/shard_map/ppermute | solution.py:17
  48.1 11.2 %collective-permute-start.27 = (bf16[272,128]{1,0:T(8,128)(2,1)S(1)}, bf16[272,128]{1,0:T(8,128)(2,1)S(1)}, u32[]{:S(2)}, u32[]{:S(2)}) collective-permute-start(bf16[272,128]{1,0:T(8,128)(2,1)S(1)} %get-tuple-element.39), channel_id=1, source_target_pairs={{0,8},{1,9},{2,10},{3,11},{4,12},{5,13},{6,14},{7,15},{8,0},{9,1},... | collective-permute-start | bytes 208904 | tf_op jit(solution)/shard_map/ppermute | solution.py:17
  50.5 8.8 %collective-permute-start.28 = (bf16[272,128]{1,0:T(8,128)(2,1)S(1)}, bf16[272,128]{1,0:T(8,128)(2,1)S(1)}, u32[]{:S(2)}, u32[]{:S(2)}) collective-permute-start(bf16[272,128]{1,0:T(8,128)(2,1)S(1)} %get-tuple-element.40), channel_id=1, source_target_pairs={{0,6},{1,7},{2,4},{3,5},{4,2},{5,3},{6,0},{7,1},{8,14},{9,15},{10,... | collective-permute-start | bytes 208904 | tf_op jit(solution)/shard_map/ppermute | solution.py:17
  52.3 7.0 %collective-permute-start.29 = (bf16[272,128]{1,0:T(8,128)(2,1)S(1)}, bf16[272,128]{1,0:T(8,128)(2,1)S(1)}, u32[]{:S(2)}, u32[]{:S(2)}) collective-permute-start(bf16[272,128]{1,0:T(8,128)(2,1)S(1)} %get-tuple-element.41), channel_id=1, source_target_pairs={{0,4},{1,5},{2,6},{3,7},{4,0},{5,1},{6,2},{7,3},{8,12},{9,13},{10,... | collective-permute-start | bytes 208904 | tf_op jit(solution)/shard_map/ppermute | solution.py:17
  53.9 5.4 %collective-permute-start.30 = (bf16[272,128]{1,0:T(8,128)(2,1)S(1)}, bf16[272,128]{1,0:T(8,128)(2,1)S(1)}, u32[]{:S(2)}, u32[]{:S(2)}) collective-permute-start(bf16[272,128]{1,0:T(8,128)(2,1)S(1)} %get-tuple-element.42), channel_id=1, source_target_pairs={{0,2},{1,3},{2,0},{3,1},{4,6},{5,7},{6,4},{7,5},{8,10},{9,11},{10,... | collective-permute-start | bytes 208904 | tf_op jit(solution)/shard_map/ppermute | solution.py:17

commit v14 on v13

--- a/solution.py
+++ b/solution.py
@@ -11,6 +11,7 @@
 TAIL = 16
 TRIALS = 2
 AHEAD = 3
+STAGED = 8
 
 
 def exchange(value, n, mask):
@@ -67,6 +68,10 @@
 
 def fold(value):
     return value.reshape(16, 8, 128).sum(axis=0)
+
+
+def across(left, right):
+    return lax.dot_general(left, right, (((1,), (1,)), ((), ())), preferred_element_type=jnp.float32)
 
 
 def fits(n):
@@ -166,15 +171,17 @@
 
 
 def stage_kernel(n, terms, tasks_ref, left_ref, plan_ref, held_ref, tasks, sem):
-    copies = [
-        pltpu.make_async_copy(tasks_ref, tasks, sem.at[0]),
-        pltpu.make_async_copy(left_ref, held_ref, sem.at[1]),
-    ]
+    copies = [pltpu.make_async_copy(tasks_ref, tasks, sem.at[0])]
+    share = left_ref.shape[0] // STAGED
+    for part in range(STAGED):
+        rows = pl.ds(part * share, share)
+        copies.append(pltpu.make_async_copy(left_ref.at[rows], held_ref.at[rows], sem.at[1 + part]))
     for copy in copies:
         copy.start()
     copies[0].wait()
     plan_kernel(n, terms, tasks, plan_ref)
-    copies[1].wait()
+    for copy in copies[1:]:
+        copy.wait()
 
 
 def make_plan(tasks, left_ops, n, terms):
@@ -187,7 +194,7 @@
             in_specs=[hbm, hbm],
             out_specs=(vmem, vmem),
             out_shape=(plan, jax.ShapeDtypeStruct(left_ops.shape, left_ops.dtype)),
-            scratch_shapes=[pltpu.VMEM(tasks.shape, jnp.int32), pltpu.SemaphoreType.DMA((2,))],
+            scratch_shapes=[pltpu.VMEM(tasks.shape, jnp.int32), pltpu.SemaphoreType.DMA((1 + STAGED,))],
             compiler_params=pltpu.CompilerParams(vmem_limit_bytes=42 * MIB),
         )(tasks, left_ops)
     return (
@@ -244,12 +251,12 @@
         place = turn * chunk
         for r in range(0, chunk, run):
             source = plan_ref[1, place + r]
-            vectors = jnp.concatenate([trial[source, 0], trial[source, 1]], axis=1)
+            vectors = jnp.concatenate([trial[source, 0], trial[source, 1]], axis=0)
             if fetched:
                 rows = left[at, r : r + run].reshape(run * 128, 128)
             else:
                 rows = jnp.concatenate([left_ref[plan_ref[0, place + r + u]] for u in range(run)], axis=0)
-            half = jnp.dot(rows, vectors, preferred_element_type=jnp.float32).astype(jnp.bfloat16)
+            half = across(rows, vectors).astype(jnp.bfloat16)
             for u in range(run):
                 halves[place + r + u, 0] = half[u * 128 : (u + 1) * 128, :128]
                 halves[place + r + u, 1] = half[u * 128 : (u + 1) * 128, 128:]
@@ -297,11 +304,10 @@
                 axis=0,
             )
             rights = jnp.concatenate([right[plan_ref[3, place]], right[plan_ref[3, place + 1]]], axis=1)
-            term = lax.dot_general(
-                pair, rights, (((1,), (1,)), ((), ())), preferred_element_type=jnp.float32
-            )
+            term = across(rights, pair)
             target = plan_ref[4, place]
-            acc[target] = acc[target] + term
+            acc[target, 0:128] = acc[target, 0:128] + term[:, :128]
+            acc[target, 128:256] = acc[target, 128:256] + term[:, 128:]
         return carry
 
     lax.fori_loop(0, plan_ref[5, 2], target_turn, 0)
@@ -363,6 +369,20 @@
     )(plan, left_ops, *[value for block in blocks for value in block[0]])
 
 
+def join_kernel(own_ref, other_ref, both_ref):
+    for i, ref in enumerate((own_ref, other_ref)):
+        for v in range(TRIALS):
+            both_ref[i * TRIALS + v] = jnp.transpose(ref[v])
+
+
+def join(own, other):
+    return pl.pallas_call(
+        join_kernel,
+        out_shape=jax.ShapeDtypeStruct((2 * TRIALS, 128, 128), jnp.bfloat16),
+        compiler_params=pltpu.CompilerParams(vmem_limit_bytes=16 * MIB),
+    )(own, other)
+
+
 def corr_kernel(*refs):
     blocks, corr_ref = refs[:-1], refs[-1]
     total = [jnp.zeros((8, 128), jnp.float32)] * 3
@@ -412,8 +432,8 @@
     for ref in received:
         value = value + ref[0:256, :].astype(jnp.float32)
         total = total + ref[256:, :].astype(jnp.float32)
-    product_ref[0, 0] = value[0:128]
-    product_ref[0, 1] = value[128:256]
+    product_ref[0, 0] = jnp.transpose(value[0:128])
+    product_ref[0, 1] = jnp.transpose(value[128:256])
     total = total[0:8] + total[8:16]
     projected_ref[...] = total[0:2, 0:2] + total[0:2, 2:4] + total[0:2, 4:6]
 
@@ -432,7 +452,7 @@
 def body(n, trial, left_ops, right_ops, task_list):
     steps = n // 4
     plan, left_ops = make_plan(task_list.T, left_ops, n, n * right_ops.shape[0])
-    vectors = jnp.concatenate([trial[0], exchange(trial[0], n, 1)], axis=0)
+    vectors = join(trial[0], exchange(trial[0], n, 1))
     line = [vectors, right_ops, exchange(right_ops, n, 1)]
     blocks = [(line, 0, False)]
     for step in range(1, steps + 1):

time: 60.4 us -> 62 us (1.026)
  Pallas kernels: 18.5 us -> 19.9 us
  other arithmetic: 0.85 us -> 0 us
  local copies, waits for them, and re-layouts: 0.69 us -> 1.53 us
    pallas_call x1, Pallas kernels: 13.2 us -> 14.4 us  [run_tasks(): pl.pallas_call(functools.partial(tasks_kernel, n, kinds), out_shape=(jax....]
    concatenate x1 -> x0, other arithmetic: 0.85 us -> none  [body(): vectors = jnp.concatenate([trial[0], exchange(trial[0], n, 1)], axis=0)]
    unnamed x4 -> x6, local copies, waits for them, and re-layouts: 0.69 us -> 1.53 us
  transfers between devices with their start and end apart: 31 -> 31, of which waited for: 8 -> 9; matrix products, arithmetic and copies ran while one was open for 1% -> 0% of each run, Pallas kernels for 7% -> 7%
where the time goes in v14:
time: 62 us; the launch traced here: 61.6 us
  starting transfers between devices  32.1 us (52%)
  Pallas kernels  19.9 us (32%)
  waiting for transfers between devices  7.37 us (12%)
  local copies, waits for them, and re-layouts  1.53 us (2%)
  between operations  0.75 us (1%)
    ppermute x12, starting transfers between devices, ring_step(): return lax.ppermute(value, 'op', pairs)  20.4 us
    pallas_call x1, Pallas kernels, run_tasks(): pl.pallas_call(functools.partial(tasks_kernel, n, kinds), out_shape=(jax....  14.4 us
    ppermute x19, starting transfers between devices, exchange(): return lax.ppermute(value, 'op', [(i, i ^ mask) for i in range(n)])  11.7 us
    ppermute x19, waiting for transfers between devices, exchange(): return lax.ppermute(value, 'op', [(i, i ^ mask) for i in range(n)])  6.59 us
    pallas_call x1, Pallas kernels, make_plan(): pl.pallas_call(functools.partial(stage_kernel, n, terms), in_specs=[hbm,...  3.48 us
    unnamed x6, local copies, waits for them, and re-layouts  1.53 us
  transfers between devices with their start and end apart: 31, of which 9 were waited for; matrix products, arithmetic and copies ran while one was open for 0% of the time, Pallas kernels for 7%

profile of v14, /device:TPU:0, one launch (start us, length us, event | category | flops | bytes accessed | tf_op | source)
XLA Modules:
  0.0 61.6 jit_solution(4429817327193652755)
XLA Ops:
  0.6 0.5 collective-permute-start
  1.1 0.1 collective-permute-start.1
  1.2 3.0 %collective-permute-start.3 = (bf16[4,128,128]{2,1,0:T(8,128)(2,1)}, bf16[4,128,128]{2,1,0:T(8,128)(2,1)S(1)}, u32[]{:S(2)}, u32[]{:S(2)}) collective-permute-start(bf16[4,128,128]{2,1,0:T(8,128)(2,1)} %refs_1_.1), channel_id=1, source_target_pairs={{0,4},{1,3},{4,8},{5,1},{8,12},{9,5},{12,14},{13,9},{14,10},{15,13... | collective-permute-start | bytes 393224 | tf_op jit(solution)/shard_map/ppermute | solution.py:32
  4.2 0.0 collective-permute-done.other_ref
  4.2 0.8 %copy-done = bf16[1,2,128,128]{3,2,1,0:T(8,128)(2,1)S(1)} copy-done((bf16[1,2,128,128]{3,2,1,0:T(8,128)(2,1)S(1)}, bf16[1,2,128,128]{3,2,1,0:T(8,128)(2,1)}, u32[]{:S(2)}) %copy-start) | copy-done | bytes 65560
  5.1 0.1 shard_map.68.refs_0_
  5.2 1.6 %collective-permute-start.2 = (bf16[4,128,128]{2,1,0:T(8,128)(2,1)S(1)}, bf16[4,128,128]{2,1,0:T(8,128)(2,1)S(1)}, u32[]{:S(2)}, u32[]{:S(2)}) collective-permute-start(bf16[4,128,128]{2,1,0:T(8,128)(2,1)S(1)} %shard_map.68.refs_0_), channel_id=1, source_target_pairs={{0,4},{1,3},{4,8},{5,1},{8,12},{9,5},{12,14},{13,9},{14,10},{15,13... | collective-permute-start | bytes 393224 | tf_op jit(solution)/shard_map/ppermute | solution.py:32
  6.8 0.0 collective-permute-done.1.refs_2_
  6.8 1.6 %collective-permute-start.4 = (bf16[4,128,128]{2,1,0:T(8,128)(2,1)S(1)}, bf16[4,128,128]{2,1,0:T(8,128)(2,1)S(1)}, u32[]{:S(2)}, u32[]{:S(2)}) collective-permute-start(bf16[4,128,128]{2,1,0:T(8,128)(2,1)S(1)} %collective-permute-done.1.refs_2_), channel_id=1, source_target_pairs={{0,4},{1,3},{4,8},{5,1},{8,12},{9,5},{12,14},{13,9},{14,10},{15,13... | collective-permute-start | bytes 393224 | tf_op jit(solution)/shard_map/ppermute | solution.py:32
  8.4 0.0 collective-permute-done.3.refs_4_
  8.4 1.5 %collective-permute-start.9 = (bf16[4,128,128]{2,1,0:T(8,128)(2,1)S(1)}, bf16[4,128,128]{2,1,0:T(8,128)(2,1)S(1)}, u32[]{:S(2)}, u32[]{:S(2)}) collective-permute-start(bf16[4,128,128]{2,1,0:T(8,128)(2,1)S(1)} %collective-permute-done.3.refs_4_), channel_id=1, source_target_pairs={{0,4},{1,3},{4,8},{5,1},{8,12},{9,5},{12,14},{13,9},{14,10},{15,13... | collective-permute-start | bytes 393224 | tf_op jit(solution)/shard_map/ppermute | solution.py:32
  9.9 0.0 collective-permute-start.6
  9.9 0.3 collective-permute-done.2.refs_3_.refs_1_
  10.2 1.6 %collective-permute-start.8 = (bf16[4,128,128]{2,1,0:T(8,128)(2,1)S(1)}, bf16[4,128,128]{2,1,0:T(8,128)(2,1)S(1)}, u32[]{:S(2)}, u32[]{:S(2)}) collective-permute-start(bf16[4,128,128]{2,1,0:T(8,128)(2,1)S(1)} %collective-permute-done.2.refs_3_.refs_1_), channel_id=1, source_target_pairs={{0,4},{1,3},{4,8},{5,1},{8,12},{9,5},{12,14},{13,9},{14,10},{15,13... | collective-permute-start | bytes 393224 | tf_op jit(solution)/shard_map/ppermute | solution.py:32
  11.8 0.0 collective-permute-start.5
  11.8 0.0 collective-permute-done.4.refs_5_
  11.8 1.6 %collective-permute-start.10 = (bf16[4,128,128]{2,1,0:T(8,128)(2,1)S(1)}, bf16[4,128,128]{2,1,0:T(8,128)(2,1)S(1)}, u32[]{:S(2)}, u32[]{:S(2)}) collective-permute-start(bf16[4,128,128]{2,1,0:T(8,128)(2,1)S(1)} %collective-permute-done.4.refs_5_), channel_id=1, source_target_pairs={{0,4},{1,3},{4,8},{5,1},{8,12},{9,5},{12,14},{13,9},{14,10},{15,13... | collective-permute-start | bytes 393224 | tf_op jit(solution)/shard_map/ppermute | solution.py:32
  13.3 0.0 collective-permute-done.9.refs_10_
  13.4 0.0 collective-permute-start.7
  13.4 0.0 collective-permute-done.6.refs_7_
  13.4 1.6 %collective-permute-start.15 = (bf16[4,128,128]{2,1,0:T(8,128)(2,1)S(1)}, bf16[4,128,128]{2,1,0:T(8,128)(2,1)S(1)}, u32[]{:S(2)}, u32[]{:S(2)}) collective-permute-start(bf16[4,128,128]{2,1,0:T(8,128)(2,1)S(1)} %collective-permute-done.9.refs_10_), channel_id=1, source_target_pairs={{0,4},{1,3},{4,8},{5,1},{8,12},{9,5},{12,14},{13,9},{14,10},{15,13... | collective-permute-start | bytes 393224 | tf_op jit(solution)/shard_map/ppermute | solution.py:32
  14.9 0.2 collective-permute-done.8.refs_9_.refs_3_
  15.2 0.0 collective-permute-start.12
  15.2 0.0 collective-permute-done.5.refs_6_.refs_2_
  15.2 1.6 %collective-permute-start.14 = (bf16[4,128,128]{2,1,0:T(8,128)(2,1)S(1)}, bf16[4,128,128]{2,1,0:T(8,128)(2,1)S(1)}, u32[]{:S(2)}, u32[]{:S(2)}) collective-permute-start(bf16[4,128,128]{2,1,0:T(8,128)(2,1)S(1)} %collective-permute-done.8.refs_9_.refs_3_), channel_id=1, source_target_pairs={{0,4},{1,3},{4,8},{5,1},{8,12},{9,5},{12,14},{13,9},{14,10},{15,13... | collective-permute-start | bytes 393224 | tf_op jit(solution)/shard_map/ppermute | solution.py:32
  16.7 0.0 collective-permute-done.10.refs_11_
  16.7 0.0 collective-permute-start.11
  16.7 0.0 collective-permute-done.7.refs_8_
  16.8 1.6 %collective-permute-start.16 = (bf16[4,128,128]{2,1,0:T(8,128)(2,1)S(1)}, bf16[4,128,128]{2,1,0:T(8,128)(2,1)S(1)}, u32[]{:S(2)}, u32[]{:S(2)}) collective-permute-start(bf16[4,128,128]{2,1,0:T(8,128)(2,1)S(1)} %collective-permute-done.10.refs_11_), channel_id=1, source_target_pairs={{0,4},{1,3},{4,8},{5,1},{8,12},{9,5},{12,14},{13,9},{14,10},{15,13... | collective-permute-start | bytes 393224 | tf_op jit(solution)/shard_map/ppermute | solution.py:32
  18.4 0.0 collective-permute-done.15.refs_16_
  18.4 0.0 collective-permute-done.12.refs_13_
  18.4 1.6 %collective-permute-start.21 = (bf16[4,128,128]{2,1,0:T(8,128)(2,1)S(1)}, bf16[4,128,128]{2,1,0:T(8,128)(2,1)S(1)}, u32[]{:S(2)}, u32[]{:S(2)}) collective-permute-start(bf16[4,128,128]{2,1,0:T(8,128)(2,1)S(1)} %collective-permute-done.15.refs_16_), channel_id=1, source_target_pairs={{0,4},{1,3},{4,8},{5,1},{8,12},{9,5},{12,14},{13,9},{14,10},{15,13... | collective-permute-start | bytes 393224 | tf_op jit(solution)/shard_map/ppermute | solution.py:32
  20.0 0.2 collective-permute-done.14.refs_15_.refs_5_
  20.1 1.6 %collective-permute-start.20 = (bf16[4,128,128]{2,1,0:T(8,128)(2,1)S(1)}, bf16[4,128,128]{2,1,0:T(8,128)(2,1)S(1)}, u32[]{:S(2)}, u32[]{:S(2)}) collective-permute-start(bf16[4,128,128]{2,1,0:T(8,128)(2,1)S(1)} %collective-permute-done.14.refs_15_.refs_5_), channel_id=1, source_target_pairs={{0,4},{1,3},{4,8},{5,1},{8,12},{9,5},{12,14},{13,9},{14,10},{15,13... | collective-permute-start | bytes 393224 | tf_op jit(solution)/shard_map/ppermute | solution.py:32
  21.7 0.1 collective-permute-done.16.refs_17_
  21.8 0.0 collective-permute-start.17
  21.8 0.0 collective-permute-done.13.refs_14_
  21.8 1.6 %collective-permute-start.22 = (bf16[4,128,128]{2,1,0:T(8,128)(2,1)S(1)}, bf16[4,128,128]{2,1,0:T(8,128)(2,1)S(1)}, u32[]{:S(2)}, u32[]{:S(2)}) collective-permute-start(bf16[4,128,128]{2,1,0:T(8,128)(2,1)S(1)} %collective-permute-done.16.refs_17_), channel_id=1, source_target_pairs={{0,4},{1,3},{4,8},{5,1},{8,12},{9,5},{12,14},{13,9},{14,10},{15,13... | collective-permute-start | bytes 393224 | tf_op jit(solution)/shard_map/ppermute | solution.py:32
  23.4 0.0 collective-permute-done.21.refs_22_
  23.4 0.0 collective-permute-start.19
  23.4 0.7 %copy-done.1 = s32[256,4]{0,1:T(4,128)S(1)} copy-done((s32[256,4]{0,1:T(4,128)S(1)}, s32[256,4]{0,1:T(4,128)}, u32[]{:S(2)}) %copy-start.1) | copy-done | bytes 4120
  24.1 3.5 %shard_map.67 = (s32[8,512]{1,0:T(8,128)S(1)}, bf16[256,128,128]{2,1,0:T(8,128)(2,1)S(1)}) custom-call(s32[4,256]{1,0:T(4,128)S(1)} %bitcast.4, bf16[256,128,128]{2,1,0:T(8,128)(2,1)} %left_ref.1), custom_call_target="tpu_custom_call" | custom-call | tf_op jit(solution)/shard_map/pallas_call | solution.py:192
  27.6 0.0 collective-permute-done.18.refs_19_
  27.6 0.0 collective-permute-done.22.refs_23_
  27.6 0.0 collective-permute-done.19.refs_20_
  27.7 14.4 %shard_map.69 = (bf16[2064,128]{1,0:T(8,128)(2,1)S(1)}, f32[17,256,128]{2,1,0:T(8,128)S(1)}, f32[8,128]{1,0:T(8,128)S(1)}) custom-call(s32[8,512]{1,0:T(8,128)S(1)} %get-tuple-element.28.plan_ref, bf16[256,128,128]{2,1,0:T(8,128)(2,1)S(1)} %get-tuple-element.29.left_ref, bf16[4,128,128]{2,1,0:T(8,128)(2,1)S(1)} %shard_map.68.refs_0_, ...), custom_call_target="tpu_custom_call" | custom-call | flops 4294967296 | bytes 15588608 | tf_op jit(solution)/shard_map/pallas_call | solution.py:349
  42.1 0.6 collective-permute-start.23
  42.6 1.5 %collective-permute-done.23.received_ref = bf16[2064,128]{1,0:T(8,128)(2,1)S(1)} collective-permute-done((bf16[2064,128]{1,0:T(8,128)(2,1)S(1)}, bf16[2064,128]{1,0:T(8,128)(2,1)S(1)}, u32[]{:S(2)}, u32[]{:S(2)}) %collective-permute-start.23) | collective-permute-done | bytes 528416 | tf_op jit(solution)/shard_map/ppermute | solution.py:18
  44.2 0.1 shard_map.70
  44.3 4.0 %collective-permute-start.24 = (bf16[272,128]{1,0:T(8,128)(2,1)S(1)}, bf16[272,128]{1,0:T(8,128)(2,1)S(1)}, u32[]{:S(2)}, u32[]{:S(2)}) collective-permute-start(bf16[272,128]{1,0:T(8,128)(2,1)S(1)} %get-tuple-element.36), channel_id=1, source_target_pairs={{0,14},{1,15},{2,12},{3,13},{4,10},{5,11},{6,8},{7,9},{8,6},{9,7},... | collective-permute-start | bytes 208904 | tf_op jit(solution)/shard_map/ppermute | solution.py:18
  48.3 0.0 collective-permute-start.25
  48.3 1.3 %collective-permute-start.26 = (bf16[272,128]{1,0:T(8,128)(2,1)S(1)}, bf16[272,128]{1,0:T(8,128)(2,1)S(1)}, u32[]{:S(2)}, u32[]{:S(2)}) collective-permute-start(bf16[272,128]{1,0:T(8,128)(2,1)S(1)} %get-tuple-element.38), channel_id=1, source_target_pairs={{0,10},{1,11},{2,8},{3,9},{4,14},{5,15},{6,12},{7,13},{8,2},{9,3},... | collective-permute-start | bytes 208904 | tf_op jit(solution)/shard_map/ppermute | solution.py:18
  49.6 2.4 %collective-permute-start.27 = (bf16[272,128]{1,0:T(8,128)(2,1)S(1)}, bf16[272,128]{1,0:T(8,128)(2,1)S(1)}, u32[]{:S(2)}, u32[]{:S(2)}) collective-permute-start(bf16[272,128]{1,0:T(8,128)(2,1)S(1)} %get-tuple-element.39), channel_id=1, source_target_pairs={{0,8},{1,9},{2,10},{3,11},{4,12},{5,13},{6,14},{7,15},{8,0},{9,1},... | collective-permute-start | bytes 208904 | tf_op jit(solution)/shard_map/ppermute | solution.py:18
  52.0 1.5 %collective-permute-start.28 = (bf16[272,128]{1,0:T(8,128)(2,1)S(1)}, bf16[272,128]{1,0:T(8,128)(2,1)S(1)}, u32[]{:S(2)}, u32[]{:S(2)}) collective-permute-start(bf16[272,128]{1,0:T(8,128)(2,1)S(1)} %get-tuple-element.40), channel_id=1, source_target_pairs={{0,6},{1,7},{2,4},{3,5},{4,2},{5,3},{6,0},{7,1},{8,14},{9,15},{10,... | collective-permute-start | bytes 208904 | tf_op jit(solution)/shard_map/ppermute | solution.py:18
  53.6 0.0 collective-permute-done.24.refs_0_
  53.6 0.6 collective-permute-start.29
  54.1 1.1 %collective-permute-done.25.refs_1_ = bf16[272,128]{1,0:T(8,128)(2,1)S(1)} collective-permute-done((bf16[272,128]{1,0:T(8,128)(2,1)S(1)}, bf16[272,128]{1,0:T(8,128)(2,1)S(1)}, u32[]{:S(2)}, u32[]{:S(2)}) %collective-permute-start.25) | collective-permute-done | bytes 69664 | tf_op jit(solution)/shard_map/ppermute | solution.py:18
  55.2 0.6 %collective-permute-start.30 = (bf16[272,128]{1,0:T(8,128)(2,1)S(1)}, bf16[272,128]{1,0:T(8,128)(2,1)S(1)}, u32[]{:S(2)}, u32[]{:S(2)}) collective-permute-start(bf16[272,128]{1,0:T(8,128)(2,1)S(1)} %get-tuple-element.42), channel_id=1, source_target_pairs={{0,2},{1,3},{2,0},{3,1},{4,6},{5,7},{6,4},{7,5},{8,10},{9,11},{10,... | collective-permute-start | bytes 208904 | tf_op jit(solution)/shard_map/ppermute | solution.py:18
  55.8 1.0 %shard_map.72 = f32[2,2]{1,0:T(2,128)} custom-call(bf16[4,128,128]{2,1,0:T(8,128)(2,1)S(1)} %shard_map.68.refs_0_, bf16[4,128,128]{2,1,0:T(8,128)(2,1)S(1)} %collective-permute-done.2.refs_3_.refs_1_, bf16[4,128,128]{2,1,0:T(8,128)(2,1)S(1)} %collective-permute-done.5.refs_6_.refs_2_, bf16[4,128,128]{2,1,0:T(8,128)(2,1)S(1)} %collective-permute-done.8.refs_9_.refs_3_, ...), custom_call_target="tpu_custom_call" | custom-call | tf_op jit(solution)/shard_map/pallas_call | solution.py:398
  56.8 2.3 %collective-permute-done.26.refs_2_ = bf16[272,128]{1,0:T(8,128)(2,1)S(1)} collective-permute-done((bf16[272,128]{1,0:T(8,128)(2,1)S(1)}, bf16[272,128]{1,0:T(8,128)(2,1)S(1)}, u32[]{:S(2)}, u32[]{:S(2)}) %collective-permute-start.26) | collective-permute-done | bytes 69664 | tf_op jit(solution)/shard_map/ppermute | solution.py:18
  59.1 1.6 %collective-permute-done.27.refs_3_ = bf16[272,128]{1,0:T(8,128)(2,1)S(1)} collective-permute-done((bf16[272,128]{1,0:T(8,128)(2,1)S(1)}, bf16[272,128]{1,0:T(8,128)(2,1)S(1)}, u32[]{:S(2)}, u32[]{:S(2)}) %collective-permute-start.27) | collective-permute-done | bytes 69664 | tf_op jit(solution)/shard_map/ppermute | solution.py:18
  60.7 0.1 collective-permute-done.29.refs_5_
  60.8 0.0 collective-permute-done.30.refs_6_
  60.8 0.8 %shard_map.71 = (f32[1,2,128,128]{3,2,1,0:T(8,128)}, f32[2,2]{1,0:T(2,128)}) custom-call(f32[256,128]{1,0:T(8,128)S(1)} %get-tuple-element.34.mine_ref, f32[16,128]{1,0:T(8,128)S(1)} %get-tuple-element.35.total_ref, bf16[272,128]{1,0:T(8,128)(2,1)S(1)} %collective-permute-done.24.refs_0_, bf16[272,128]{1,0:T(8,128)(2,1)S(1)} %collective-permute-done.25.refs_1_, ...), custom_call_target="tpu_custom_call" | custom-call | tf_op jit(solution)/shard_map/pallas_call | solution.py:442
  (10 shorter events, 0.0 us)
Async XLA Ops:
  0.6 3.6 %collective-permute-start = (bf16[2,128,128]{2,1,0:T(8,128)(2,1)}, bf16[2,128,128]{2,1,0:T(8,128)(2,1)S(1)}, u32[]{:S(2)}, u32[]{:S(2)}) collective-permute-start(bf16[2,128,128]{2,1,0:T(8,128)(2,1)} %bitcast.2), channel_id=1, source_target_pairs={{0,1},{1,0},{2,3},{3,2},{4,5},{5,4},{6,7},{7,6},{8,9},{9,8},{10,11... | collective-permute-start | bytes 196616 | tf_op jit(solution)/shard_map/ppermute | solution.py:18
  1.1 5.7 %collective-permute-start.1 = (bf16[4,128,128]{2,1,0:T(8,128)(2,1)}, bf16[4,128,128]{2,1,0:T(8,128)(2,1)S(1)}, u32[]{:S(2)}, u32[]{:S(2)}) collective-permute-start(bf16[4,128,128]{2,1,0:T(8,128)(2,1)} %refs_1_.1), channel_id=1, source_target_pairs={{0,1},{1,0},{2,3},{3,2},{4,5},{5,4},{6,7},{7,6},{8,9},{9,8},{10,11... | collective-permute-start | bytes 393224 | tf_op jit(solution)/shard_map/ppermute | solution.py:18
  1.2 7.2 %collective-permute-start.3 = (bf16[4,128,128]{2,1,0:T(8,128)(2,1)}, bf16[4,128,128]{2,1,0:T(8,128)(2,1)S(1)}, u32[]{:S(2)}, u32[]{:S(2)}) collective-permute-start(bf16[4,128,128]{2,1,0:T(8,128)(2,1)} %refs_1_.1), channel_id=1, source_target_pairs={{0,4},{1,3},{4,8},{5,1},{8,12},{9,5},{12,14},{13,9},{14,10},{15,13... | collective-permute-start | bytes 393224 | tf_op jit(solution)/shard_map/ppermute | solution.py:32
  4.2 0.8 %copy-start = (bf16[1,2,128,128]{3,2,1,0:T(8,128)(2,1)S(1)}, bf16[1,2,128,128]{3,2,1,0:T(8,128)(2,1)}, u32[]{:S(2)}) copy-start(bf16[1,2,128,128]{3,2,1,0:T(8,128)(2,1)} %param.4) | copy-start | bytes 196612
  5.1 22.6 %copy-start.2 = (bf16[4,128,128]{2,1,0:T(8,128)(2,1)S(1)}, bf16[4,128,128]{2,1,0:T(8,128)(2,1)}, u32[]{:S(2)}) copy-start(bf16[4,128,128]{2,1,0:T(8,128)(2,1)} %refs_1_.1) | copy-start | bytes 393220
  5.2 5.0 %collective-permute-start.2 = (bf16[4,128,128]{2,1,0:T(8,128)(2,1)S(1)}, bf16[4,128,128]{2,1,0:T(8,128)(2,1)S(1)}, u32[]{:S(2)}, u32[]{:S(2)}) collective-permute-start(bf16[4,128,128]{2,1,0:T(8,128)(2,1)S(1)} %shard_map.68.refs_0_), channel_id=1, source_target_pairs={{0,4},{1,3},{4,8},{5,1},{8,12},{9,5},{12,14},{13,9},{14,10},{15,13... | collective-permute-start | bytes 393224 | tf_op jit(solution)/shard_map/ppermute | solution.py:32
  6.8 5.0 %collective-permute-start.4 = (bf16[4,128,128]{2,1,0:T(8,128)(2,1)S(1)}, bf16[4,128,128]{2,1,0:T(8,128)(2,1)S(1)}, u32[]{:S(2)}, u32[]{:S(2)}) collective-permute-start(bf16[4,128,128]{2,1,0:T(8,128)(2,1)S(1)} %collective-permute-done.1.refs_2_), channel_id=1, source_target_pairs={{0,4},{1,3},{4,8},{5,1},{8,12},{9,5},{12,14},{13,9},{14,10},{15,13... | collective-permute-start | bytes 393224 | tf_op jit(solution)/shard_map/ppermute | solution.py:32
  8.4 5.0 %collective-permute-start.9 = (bf16[4,128,128]{2,1,0:T(8,128)(2,1)S(1)}, bf16[4,128,128]{2,1,0:T(8,128)(2,1)S(1)}, u32[]{:S(2)}, u32[]{:S(2)}) collective-permute-start(bf16[4,128,128]{2,1,0:T(8,128)(2,1)S(1)} %collective-permute-done.3.refs_4_), channel_id=1, source_target_pairs={{0,4},{1,3},{4,8},{5,1},{8,12},{9,5},{12,14},{13,9},{14,10},{15,13... | collective-permute-start | bytes 393224 | tf_op jit(solution)/shard_map/ppermute | solution.py:32
  9.9 3.5 %collective-permute-start.6 = (bf16[4,128,128]{2,1,0:T(8,128)(2,1)S(1)}, bf16[4,128,128]{2,1,0:T(8,128)(2,1)S(1)}, u32[]{:S(2)}, u32[]{:S(2)}) collective-permute-start(bf16[4,128,128]{2,1,0:T(8,128)(2,1)S(1)} %collective-permute-done.3.refs_4_), channel_id=1, source_target_pairs={{0,1},{1,0},{2,3},{3,2},{4,5},{5,4},{6,7},{7,6},{8,9},{9,8},{10,11... | collective-permute-start | bytes 393224 | tf_op jit(solution)/shard_map/ppermute | solution.py:18
  10.2 5.0 %collective-permute-start.8 = (bf16[4,128,128]{2,1,0:T(8,128)(2,1)S(1)}, bf16[4,128,128]{2,1,0:T(8,128)(2,1)S(1)}, u32[]{:S(2)}, u32[]{:S(2)}) collective-permute-start(bf16[4,128,128]{2,1,0:T(8,128)(2,1)S(1)} %collective-permute-done.2.refs_3_.refs_1_), channel_id=1, source_target_pairs={{0,4},{1,3},{4,8},{5,1},{8,12},{9,5},{12,14},{13,9},{14,10},{15,13... | collective-permute-start | bytes 393224 | tf_op jit(solution)/shard_map/ppermute | solution.py:32
  11.8 3.4 %collective-permute-start.5 = (bf16[4,128,128]{2,1,0:T(8,128)(2,1)S(1)}, bf16[4,128,128]{2,1,0:T(8,128)(2,1)S(1)}, u32[]{:S(2)}, u32[]{:S(2)}) collective-permute-start(bf16[4,128,128]{2,1,0:T(8,128)(2,1)S(1)} %collective-permute-done.2.refs_3_.refs_1_), channel_id=1, source_target_pairs={{0,1},{1,0},{2,3},{3,2},{4,5},{5,4},{6,7},{7,6},{8,9},{9,8},{10,11... | collective-permute-start | bytes 393224 | tf_op jit(solution)/shard_map/ppermute | solution.py:18
  11.8 5.0 %collective-permute-start.10 = (bf16[4,128,128]{2,1,0:T(8,128)(2,1)S(1)}, bf16[4,128,128]{2,1,0:T(8,128)(2,1)S(1)}, u32[]{:S(2)}, u32[]{:S(2)}) collective-permute-start(bf16[4,128,128]{2,1,0:T(8,128)(2,1)S(1)} %collective-permute-done.4.refs_5_), channel_id=1, source_target_pairs={{0,4},{1,3},{4,8},{5,1},{8,12},{9,5},{12,14},{13,9},{14,10},{15,13... | collective-permute-start | bytes 393224 | tf_op jit(solution)/shard_map/ppermute | solution.py:32
  13.4 3.4 %collective-permute-start.7 = (bf16[4,128,128]{2,1,0:T(8,128)(2,1)S(1)}, bf16[4,128,128]{2,1,0:T(8,128)(2,1)S(1)}, u32[]{:S(2)}, u32[]{:S(2)}) collective-permute-start(bf16[4,128,128]{2,1,0:T(8,128)(2,1)S(1)} %collective-permute-done.4.refs_5_), channel_id=1, source_target_pairs={{0,1},{1,0},{2,3},{3,2},{4,5},{5,4},{6,7},{7,6},{8,9},{9,8},{10,11... | collective-permute-start | bytes 393224 | tf_op jit(solution)/shard_map/ppermute | solution.py:18
  13.4 5.0 %collective-permute-start.15 = (bf16[4,128,128]{2,1,0:T(8,128)(2,1)S(1)}, bf16[4,128,128]{2,1,0:T(8,128)(2,1)S(1)}, u32[]{:S(2)}, u32[]{:S(2)}) collective-permute-start(bf16[4,128,128]{2,1,0:T(8,128)(2,1)S(1)} %collective-permute-done.9.refs_10_), channel_id=1, source_target_pairs={{0,4},{1,3},{4,8},{5,1},{8,12},{9,5},{12,14},{13,9},{14,10},{15,13... | collective-permute-start | bytes 393224 | tf_op jit(solution)/shard_map/ppermute | solution.py:32
  15.2 3.2 %collective-permute-start.12 = (bf16[4,128,128]{2,1,0:T(8,128)(2,1)S(1)}, bf16[4,128,128]{2,1,0:T(8,128)(2,1)S(1)}, u32[]{:S(2)}, u32[]{:S(2)}) collective-permute-start(bf16[4,128,128]{2,1,0:T(8,128)(2,1)S(1)} %collective-permute-done.9.refs_10_), channel_id=1, source_target_pairs={{0,1},{1,0},{2,3},{3,2},{4,5},{5,4},{6,7},{7,6},{8,9},{9,8},{10,11... | collective-permute-start | bytes 393224 | tf_op jit(solution)/shard_map/ppermute | solution.py:18
  15.2 5.0 %collective-permute-start.14 = (bf16[4,128,128]{2,1,0:T(8,128)(2,1)S(1)}, bf16[4,128,128]{2,1,0:T(8,128)(2,1)S(1)}, u32[]{:S(2)}, u32[]{:S(2)}) collective-permute-start(bf16[4,128,128]{2,1,0:T(8,128)(2,1)S(1)} %collective-permute-done.8.refs_9_.refs_3_), channel_id=1, source_target_pairs={{0,4},{1,3},{4,8},{5,1},{8,12},{9,5},{12,14},{13,9},{14,10},{15,13... | collective-permute-start | bytes 393224 | tf_op jit(solution)/shard_map/ppermute | solution.py:32
  16.7 3.4 %collective-permute-start.11 = (bf16[4,128,128]{2,1,0:T(8,128)(2,1)S(1)}, bf16[4,128,128]{2,1,0:T(8,128)(2,1)S(1)}, u32[]{:S(2)}, u32[]{:S(2)}) collective-permute-start(bf16[4,128,128]{2,1,0:T(8,128)(2,1)S(1)} %collective-permute-done.8.refs_9_.refs_3_), channel_id=1, source_target_pairs={{0,1},{1,0},{2,3},{3,2},{4,5},{5,4},{6,7},{7,6},{8,9},{9,8},{10,11... | collective-permute-start | bytes 393224 | tf_op jit(solution)/shard_map/ppermute | solution.py:18
  16.8 5.0 %collective-permute-start.16 = (bf16[4,128,128]{2,1,0:T(8,128)(2,1)S(1)}, bf16[4,128,128]{2,1,0:T(8,128)(2,1)S(1)}, u32[]{:S(2)}, u32[]{:S(2)}) collective-permute-start(bf16[4,128,128]{2,1,0:T(8,128)(2,1)S(1)} %collective-permute-done.10.refs_11_), channel_id=1, source_target_pairs={{0,4},{1,3},{4,8},{5,1},{8,12},{9,5},{12,14},{13,9},{14,10},{15,13... | collective-permute-start | bytes 393224 | tf_op jit(solution)/shard_map/ppermute | solution.py:32
  18.4 3.4 %collective-permute-start.13 = (bf16[4,128,128]{2,1,0:T(8,128)(2,1)S(1)}, bf16[4,128,128]{2,1,0:T(8,128)(2,1)S(1)}, u32[]{:S(2)}, u32[]{:S(2)}) collective-permute-start(bf16[4,128,128]{2,1,0:T(8,128)(2,1)S(1)} %collective-permute-done.10.refs_11_), channel_id=1, source_target_pairs={{0,1},{1,0},{2,3},{3,2},{4,5},{5,4},{6,7},{7,6},{8,9},{9,8},{10,11... | collective-permute-start | bytes 393224 | tf_op jit(solution)/shard_map/ppermute | solution.py:18
  18.4 5.0 %collective-permute-start.21 = (bf16[4,128,128]{2,1,0:T(8,128)(2,1)S(1)}, bf16[4,128,128]{2,1,0:T(8,128)(2,1)S(1)}, u32[]{:S(2)}, u32[]{:S(2)}) collective-permute-start(bf16[4,128,128]{2,1,0:T(8,128)(2,1)S(1)} %collective-permute-done.15.refs_16_), channel_id=1, source_target_pairs={{0,4},{1,3},{4,8},{5,1},{8,12},{9,5},{12,14},{13,9},{14,10},{15,13... | collective-permute-start | bytes 393224 | tf_op jit(solution)/shard_map/ppermute | solution.py:32
  20.1 7.5 %collective-permute-start.18 = (bf16[4,128,128]{2,1,0:T(8,128)(2,1)S(1)}, bf16[4,128,128]{2,1,0:T(8,128)(2,1)S(1)}, u32[]{:S(2)}, u32[]{:S(2)}) collective-permute-start(bf16[4,128,128]{2,1,0:T(8,128)(2,1)S(1)} %collective-permute-done.15.refs_16_), channel_id=1, source_target_pairs={{0,1},{1,0},{2,3},{3,2},{4,5},{5,4},{6,7},{7,6},{8,9},{9,8},{10,11... | collective-permute-start | bytes 393224 | tf_op jit(solution)/shard_map/ppermute | solution.py:18
  20.1 7.5 %collective-permute-start.20 = (bf16[4,128,128]{2,1,0:T(8,128)(2,1)S(1)}, bf16[4,128,128]{2,1,0:T(8,128)(2,1)S(1)}, u32[]{:S(2)}, u32[]{:S(2)}) collective-permute-start(bf16[4,128,128]{2,1,0:T(8,128)(2,1)S(1)} %collective-permute-done.14.refs_15_.refs_5_), channel_id=1, source_target_pairs={{0,4},{1,3},{4,8},{5,1},{8,12},{9,5},{12,14},{13,9},{14,10},{15,13... | collective-permute-start | bytes 393224 | tf_op jit(solution)/shard_map/ppermute | solution.py:32
  21.8 5.8 %collective-permute-start.17 = (bf16[4,128,128]{2,1,0:T(8,128)(2,1)S(1)}, bf16[4,128,128]{2,1,0:T(8,128)(2,1)S(1)}, u32[]{:S(2)}, u32[]{:S(2)}) collective-permute-start(bf16[4,128,128]{2,1,0:T(8,128)(2,1)S(1)} %collective-permute-done.14.refs_15_.refs_5_), channel_id=1, source_target_pairs={{0,1},{1,0},{2,3},{3,2},{4,5},{5,4},{6,7},{7,6},{8,9},{9,8},{10,11... | collective-permute-start | bytes 393224 | tf_op jit(solution)/shard_map/ppermute | solution.py:18
  21.8 5.9 %collective-permute-start.22 = (bf16[4,128,128]{2,1,0:T(8,128)(2,1)S(1)}, bf16[4,128,128]{2,1,0:T(8,128)(2,1)S(1)}, u32[]{:S(2)}, u32[]{:S(2)}) collective-permute-start(bf16[4,128,128]{2,1,0:T(8,128)(2,1)S(1)} %collective-permute-done.16.refs_17_), channel_id=1, source_target_pairs={{0,4},{1,3},{4,8},{5,1},{8,12},{9,5},{12,14},{13,9},{14,10},{15,13... | collective-permute-start | bytes 393224 | tf_op jit(solution)/shard_map/ppermute | solution.py:32
  23.4 4.2 %collective-permute-start.19 = (bf16[4,128,128]{2,1,0:T(8,128)(2,1)S(1)}, bf16[4,128,128]{2,1,0:T(8,128)(2,1)S(1)}, u32[]{:S(2)}, u32[]{:S(2)}) collective-permute-start(bf16[4,128,128]{2,1,0:T(8,128)(2,1)S(1)} %collective-permute-done.16.refs_17_), channel_id=1, source_target_pairs={{0,1},{1,0},{2,3},{3,2},{4,5},{5,4},{6,7},{7,6},{8,9},{9,8},{10,11... | collective-permute-start | bytes 393224 | tf_op jit(solution)/shard_map/ppermute | solution.py:18
  23.4 0.7 %copy-start.1 = (s32[256,4]{0,1:T(4,128)S(1)}, s32[256,4]{0,1:T(4,128)}, u32[]{:S(2)}) copy-start(s32[256,4]{0,1:T(4,128)} %param.7) | copy-start | bytes 12292
  42.1 2.1 %collective-permute-start.23 = (bf16[2064,128]{1,0:T(8,128)(2,1)S(1)}, bf16[2064,128]{1,0:T(8,128)(2,1)S(1)}, u32[]{:S(2)}, u32[]{:S(2)}) collective-permute-start(bf16[2064,128]{1,0:T(8,128)(2,1)S(1)} %get-tuple-element.33), channel_id=1, source_target_pairs={{0,1},{1,0},{2,3},{3,2},{4,5},{5,4},{6,7},{7,6},{8,9},{9,8},{10,11... | collective-permute-start | bytes 1585160 | tf_op jit(solution)/shard_map/ppermute | solution.py:18
  44.3 9.3 %collective-permute-start.24 = (bf16[272,128]{1,0:T(8,128)(2,1)S(1)}, bf16[272,128]{1,0:T(8,128)(2,1)S(1)}, u32[]{:S(2)}, u32[]{:S(2)}) collective-permute-start(bf16[272,128]{1,0:T(8,128)(2,1)S(1)} %get-tuple-element.36), channel_id=1, source_target_pairs={{0,14},{1,15},{2,12},{3,13},{4,10},{5,11},{6,8},{7,9},{8,6},{9,7},... | collective-permute-start | bytes 208904 | tf_op jit(solution)/shard_map/ppermute | solution.py:18
  48.3 6.9 %collective-permute-start.25 = (bf16[272,128]{1,0:T(8,128)(2,1)S(1)}, bf16[272,128]{1,0:T(8,128)(2,1)S(1)}, u32[]{:S(2)}, u32[]{:S(2)}) collective-permute-start(bf16[272,128]{1,0:T(8,128)(2,1)S(1)} %get-tuple-element.37), channel_id=1, source_target_pairs={{0,12},{1,13},{2,14},{3,15},{4,8},{5,9},{6,10},{7,11},{8,4},{9,5},... | collective-permute-start | bytes 208904 | tf_op jit(solution)/shard_map/ppermute | solution.py:18
  48.3 10.8 %collective-permute-start.26 = (bf16[272,128]{1,0:T(8,128)(2,1)S(1)}, bf16[272,128]{1,0:T(8,128)(2,1)S(1)}, u32[]{:S(2)}, u32[]{:S(2)}) collective-permute-start(bf16[272,128]{1,0:T(8,128)(2,1)S(1)} %get-tuple-element.38), channel_id=1, source_target_pairs={{0,10},{1,11},{2,8},{3,9},{4,14},{5,15},{6,12},{7,13},{8,2},{9,3},... | collective-permute-start | bytes 208904 | tf_op jit(solution)/shard_map/ppermute | solution.py:18
  49.6 11.1 %collective-permute-start.27 = (bf16[272,128]{1,0:T(8,128)(2,1)S(1)}, bf16[272,128]{1,0:T(8,128)(2,1)S(1)}, u32[]{:S(2)}, u32[]{:S(2)}) collective-permute-start(bf16[272,128]{1,0:T(8,128)(2,1)S(1)} %get-tuple-element.39), channel_id=1, source_target_pairs={{0,8},{1,9},{2,10},{3,11},{4,12},{5,13},{6,14},{7,15},{8,0},{9,1},... | collective-permute-start | bytes 208904 | tf_op jit(solution)/shard_map/ppermute | solution.py:18
  52.0 8.7 %collective-permute-start.28 = (bf16[272,128]{1,0:T(8,128)(2,1)S(1)}, bf16[272,128]{1,0:T(8,128)(2,1)S(1)}, u32[]{:S(2)}, u32[]{:S(2)}) collective-permute-start(bf16[272,128]{1,0:T(8,128)(2,1)S(1)} %get-tuple-element.40), channel_id=1, source_target_pairs={{0,6},{1,7},{2,4},{3,5},{4,2},{5,3},{6,0},{7,1},{8,14},{9,15},{10,... | collective-permute-start | bytes 208904 | tf_op jit(solution)/shard_map/ppermute | solution.py:18
  53.6 7.2 %collective-permute-start.29 = (bf16[272,128]{1,0:T(8,128)(2,1)S(1)}, bf16[272,128]{1,0:T(8,128)(2,1)S(1)}, u32[]{:S(2)}, u32[]{:S(2)}) collective-permute-start(bf16[272,128]{1,0:T(8,128)(2,1)S(1)} %get-tuple-element.41), channel_id=1, source_target_pairs={{0,4},{1,5},{2,6},{3,7},{4,0},{5,1},{6,2},{7,3},{8,12},{9,13},{10,... | collective-permute-start | bytes 208904 | tf_op jit(solution)/shard_map/ppermute | solution.py:18
  55.2 5.6 %collective-permute-start.30 = (bf16[272,128]{1,0:T(8,128)(2,1)S(1)}, bf16[272,128]{1,0:T(8,128)(2,1)S(1)}, u32[]{:S(2)}, u32[]{:S(2)}) collective-permute-start(bf16[272,128]{1,0:T(8,128)(2,1)S(1)} %get-tuple-element.42), channel_id=1, source_target_pairs={{0,2},{1,3},{2,0},{3,1},{4,6},{5,7},{6,4},{7,5},{8,10},{9,11},{10,... | collective-permute-start | bytes 208904 | tf_op jit(solution)/shard_map/ppermute | solution.py:18

commit v15 on v13

--- a/solution.py
+++ b/solution.py
@@ -73,12 +73,20 @@
     return n <= 16
 
 
+def near_chips(n):
+    return n // 4
+
+
 def phases_of(n):
     return 1
 
 
 def chunk_of(n):
     return 96 if fits(n) else 48
+
+
+def pairs_of(n):
+    return 46 if fits(n) else 24
 
 
 def run_of(slots, n):
@@ -138,7 +146,7 @@
         return jnp.where(live > 0, place, -1.0), starts
 
     by_source, source_starts = sort(source, phases, float(run_of(slots, n)), float(chunk_of(n)))
-    by_target, target_starts = sort(target, 1, 2.0, float(chunk_of(n)))
+    by_target, target_starts = sort(target, 1, 2.0, 2.0 * pairs_of(n))
     columns = column(by_source, by_target, lane, source, term, target)
 
     def picker(places_column):
@@ -162,7 +170,6 @@
     for p, start in enumerate(source_starts + [target_starts[1]]):
         turns = turns + jnp.where(number == p, start, 0.0)
     plan_ref[5:6] = turns.astype(jnp.int32)
-    plan_ref[6:8] = jnp.zeros((2, places), jnp.int32)
 
 
 def stage_kernel(n, terms, tasks_ref, left_ref, plan_ref, held_ref, tasks, sem):
@@ -178,8 +185,8 @@
 
 
 def make_plan(tasks, left_ops, n, terms):
-    most = source_places(tasks.shape[1], n) + chunk_of(n)
-    plan = jax.ShapeDtypeStruct((8, -(-most // 128) * 128), jnp.int32)
+    most = source_places(tasks.shape[1], n)
+    plan = jax.ShapeDtypeStruct((6, -(-most // 128) * 128), jnp.int32)
     vmem, hbm = pl.BlockSpec(memory_space=pltpu.VMEM), pl.BlockSpec(memory_space=pltpu.HBM)
     if fits(n):
         return pl.pallas_call(
@@ -260,7 +267,7 @@
 
 def tasks_kernel(n, kinds, plan_ref, left_ref, *refs):
     blocks, refs = refs[: 3 * len(kinds)], refs[3 * len(kinds) :]
-    send_ref, acc, own_ref, halves, trial, right, block_sem, *fetched = refs
+    far_ref, near_ref, acc, own_ref, halves, trial, right, block_sem, *fetched = refs
     start, products = make_halves(n, plan_ref, left_ref, trial, halves, fetched)
     right[right.shape[0] - 1] = jnp.zeros((128, 128), jnp.bfloat16)
     start()
@@ -283,8 +290,8 @@
     products()
 
     def target_turn(turn, carry):
-        first = turn * chunk_of(n)
-        for u in range(0, chunk_of(n), 2):
+        first = turn * 2 * pairs_of(n)
+        for u in range(0, 2 * pairs_of(n), 2):
             place = first + u
             one = plan_ref[2, place]
             two = plan_ref[2, place + 1]
@@ -319,15 +326,26 @@
     sums = lax.fori_loop(0, n, dots, (zero,) * 4, unroll=4)
     p00, p01, p10, p11 = [jnp.sum(x) for x in sums]
 
+    chips = n // 2
+    near = near_chips(n)
+
     def pack(j, carry):
-        mine = jnp.bitwise_xor(me, 2 * j)
-        send_ref[pl.ds(pl.multiple_of(j * 256, 256), 256), :] = acc[jnp.bitwise_xor(mine, 1)].astype(jnp.bfloat16)
+        value = acc[jnp.bitwise_xor(me, 2 * j + 1)].astype(jnp.bfloat16)
+
+        @pl.when(j < near)
+        def _():
+            near_ref[pl.ds(pl.multiple_of(j * 256, 256), 256), :] = value
+
+        @pl.when(j >= near)
+        def _():
+            far_ref[pl.ds(pl.multiple_of((j - near) * 256, 256), 256), :] = value
+
         return carry
 
-    lax.fori_loop(0, n // 2, pack, 0, unroll=2)
+    lax.fori_loop(0, chips, pack, 0, unroll=2)
     own = split3(matrix_of({(0, 0): p00, (0, 1): p01, (1, 0): p10, (1, 1): p11}, 3))
     own_ref[...] = own
-    send_ref[n // 2 * 256 :, :] = tail_of(own, jnp.zeros_like(own))
+    far_ref[(chips - near) * 256 :, :] = tail_of(own, jnp.zeros_like(own))
 
 
 def run_tasks(n, plan, left_ops, blocks):
@@ -343,12 +361,13 @@
     return pl.pallas_call(
         functools.partial(tasks_kernel, n, kinds),
         out_shape=(
-            jax.ShapeDtypeStruct((n // 2 * 256 + TAIL, 128), jnp.bfloat16),
+            jax.ShapeDtypeStruct(((n // 2 - near_chips(n)) * 256 + TAIL, 128), jnp.bfloat16),
+            jax.ShapeDtypeStruct((near_chips(n) * 256, 128), jnp.bfloat16),
             jax.ShapeDtypeStruct((n + 1, 256, 128), jnp.float32),
             jax.ShapeDtypeStruct((8, 128), jnp.float32),
         ),
         in_specs=[pl.BlockSpec(memory_space=pltpu.SMEM)] + [given] * (1 + 3 * len(blocks)),
-        out_specs=(vmem,) * 3,
+        out_specs=(vmem,) * 4,
         scratch_shapes=[
             pltpu.VMEM((source_places(slots, n), 2, 128, 128), jnp.bfloat16),
             pltpu.VMEM((n, TRIALS, 128, 128), jnp.bfloat16),
@@ -382,28 +401,46 @@
     )(*blocks)
 
 
-def chip_kernel(chips, keep_ref, own_ref, received_ref, mine_ref, total_ref, *sends):
-    total = jnp.concatenate([own_ref[...], received_ref[chips * 256 :, :].astype(jnp.float32)[0:8]], axis=0)
+def far_kernel(n, acc_ref, own_ref, received_ref, total_ref, *sends):
+    far, near = n // 2 - near_chips(n), near_chips(n)
+    total = jnp.concatenate([own_ref[...], received_ref[far * 256 :, :].astype(jnp.float32)[0:8]], axis=0)
     total_ref[...] = total
-    tail = total.astype(jnp.bfloat16)
     me = lax.axis_index("op")
-    for j in range(chips):
-        value = keep_ref[jnp.bitwise_xor(me, 2 * j)] + received_ref[j * 256 : (j + 1) * 256, :].astype(jnp.float32)
+    for j in range(far):
+        value = acc_ref[jnp.bitwise_xor(me, 2 * (near + j))] + received_ref[j * 256 : (j + 1) * 256, :].astype(
+            jnp.float32
+        )
+        sends[j][0:256, :] = value.astype(jnp.bfloat16)
+        sends[j][256:, :] = total.astype(jnp.bfloat16)
+
+
+def add_far(n, acc, own, received):
+    return pl.pallas_call(
+        functools.partial(far_kernel, n),
+        out_shape=(jax.ShapeDtypeStruct((16, 128), jnp.float32),)
+        + (jax.ShapeDtypeStruct((256 + TAIL, 128), jnp.bfloat16),) * (n // 2 - near_chips(n)),
+        compiler_params=pltpu.CompilerParams(vmem_limit_bytes=16 * MIB),
+    )(acc, own, received)
+
+
+def near_kernel(n, acc_ref, total_ref, received_ref, mine_ref, *sends):
+    me = lax.axis_index("op")
+    for j in range(near_chips(n)):
+        value = acc_ref[jnp.bitwise_xor(me, 2 * j)] + received_ref[j * 256 : (j + 1) * 256, :].astype(jnp.float32)
         if j == 0:
             mine_ref[...] = value
         else:
             sends[j - 1][0:256, :] = value.astype(jnp.bfloat16)
-            sends[j - 1][256:, :] = tail
-
-
-def add_chip(keep, own, received):
-    chips = keep.shape[0] // 2
+            sends[j - 1][256:, :] = total_ref[...].astype(jnp.bfloat16)
+
+
+def add_near(n, acc, total, received):
     return pl.pallas_call(
-        functools.partial(chip_kernel, chips),
-        out_shape=(jax.ShapeDtypeStruct((256, 128), jnp.float32), jax.ShapeDtypeStruct((16, 128), jnp.float32))
-        + (jax.ShapeDtypeStruct((256 + TAIL, 128), jnp.bfloat16),) * (chips - 1),
+        functools.partial(near_kernel, n),
+        out_shape=(jax.ShapeDtypeStruct((256, 128), jnp.float32),)
+        + (jax.ShapeDtypeStruct((256 + TAIL, 128), jnp.bfloat16),) * (near_chips(n) - 1),
         compiler_params=pltpu.CompilerParams(vmem_limit_bytes=16 * MIB),
-    )(keep, own, received)
+    )(acc, total, received)
 
 
 def last_kernel(mine_ref, total_ref, *refs):
@@ -440,11 +477,15 @@
         blocks.append((line, step, False))
         if step < steps:
             blocks.append(([exchange(value, n, 1) for value in line], step, True))
-    send, keep, own = run_tasks(n, plan, left_ops, blocks)
-    send, arrays = lax.optimization_barrier((send, [block[0][0] for block in blocks]))
+    far, near, acc, own = run_tasks(n, plan, left_ops, blocks)
+    far, arrays = lax.optimization_barrier((far, [block[0][0] for block in blocks]))
     correlation = correlate(arrays)
-    mine, total, *sends = add_chip(keep, own, exchange(send, n, 1))
-    received = [exchange(sends[j - 1], n, 2 * j) for j in reversed(range(1, n // 2))]
+    far, near = exchange(far, n, 1), exchange(near, n, 1)
+    total, *messages = add_far(n, acc, own, far)
+    first = near_chips(n)
+    received = [exchange(messages[j], n, 2 * (first + j)) for j in reversed(range(len(messages)))]
+    mine, *messages = add_near(n, acc, total, near)
+    received += [exchange(messages[j - 1], n, 2 * j) for j in reversed(range(1, first))]
     product, projected = add_all(mine, total, received)
     return product, correlation, projected
 

time: 60.4 us -> 59.7 us (0.988)
  starting transfers between devices: 31.9 us -> 34 us
  Pallas kernels: 18.5 us -> 16.6 us
  waiting for transfers between devices: 7.42 us -> 6.34 us
    ppermute x19 -> x20, starting transfers between devices: 11.5 us -> 13.6 us  [exchange(): return lax.ppermute(value, 'op', [(i, i ^ mask) for i in range(n)])]
    pallas_call x1, Pallas kernels: 13.2 us -> 11.4 us  [run_tasks(): pl.pallas_call(functools.partial(tasks_kernel, n, kinds), out_shape=(jax....]
    ppermute x19 -> x20, waiting for transfers between devices: 6.64 us -> 5.56 us  [exchange(): return lax.ppermute(value, 'op', [(i, i ^ mask) for i in range(n)])]
  transfers between devices with their start and end apart: 31 -> 32, of which waited for: 8 -> 8; matrix products, arithmetic and copies ran while one was open for 1% -> 1% of each run, Pallas kernels for 7% -> 8%
where the time goes in v15:
time: 59.7 us; the launch traced here: 59.3 us
  starting transfers between devices  34 us (57%)
  Pallas kernels  16.6 us (28%)
  waiting for transfers between devices  6.34 us (11%)
  other arithmetic  0.85 us (1%)
  between operations  0.75 us (1%)
  local copies, waits for them, and re-layouts  0.69 us (1%)
    ppermute x12, starting transfers between devices, ring_step(): return lax.ppermute(value, 'op', pairs)  20.4 us
    ppermute x20, starting transfers between devices, exchange(): return lax.ppermute(value, 'op', [(i, i ^ mask) for i in range(n)])  13.6 us
    pallas_call x1, Pallas kernels, run_tasks(): pl.pallas_call(functools.partial(tasks_kernel, n, kinds), out_shape=(jax....  11.4 us
    ppermute x20, waiting for transfers between devices, exchange(): return lax.ppermute(value, 'op', [(i, i ^ mask) for i in range(n)])  5.56 us
    pallas_call x1, Pallas kernels, make_plan(): pl.pallas_call(functools.partial(stage_kernel, n, terms), in_specs=[hbm,...  3.4 us
  transfers between devices with their start and end apart: 32, of which 8 were waited for; matrix products, arithmetic and copies ran while one was open for 1% of the time, Pallas kernels for 8%

profile of v15, /device:TPU:0, one launch (start us, length us, event | category | flops | bytes accessed | tf_op | source)
XLA Modules:
  0.0 59.3 jit_solution(13743904561750259504)
XLA Ops:
  0.6 0.5 collective-permute-start
  1.2 0.1 collective-permute-start.1
  1.2 3.0 %collective-permute-start.3 = (bf16[4,128,128]{2,1,0:T(8,128)(2,1)}, bf16[4,128,128]{2,1,0:T(8,128)(2,1)S(1)}, u32[]{:S(2)}, u32[]{:S(2)}) collective-permute-start(bf16[4,128,128]{2,1,0:T(8,128)(2,1)} %refs_1_.1), channel_id=1, source_target_pairs={{0,4},{1,3},{4,8},{5,1},{8,12},{9,5},{12,14},{13,9},{14,10},{15,13... | collective-permute-start | bytes 393224 | tf_op jit(solution)/shard_map/ppermute | solution.py:31
  4.2 0.0 collective-permute-done
  4.2 0.9 %pad_maximum_fusion.refs_0_ = bf16[4,128,128]{2,1,0:T(8,128)(2,1)S(1)} fusion(bf16[2,128,128]{2,1,0:T(8,128)(2,1)S(1)} %collective-permute-done, bf16[2,128,128]{2,1,0:T(8,128)(2,1)} %bitcast.4), kind=kLoop, calls=%fused_computation | loop fusion | flops 65536 | bytes 262144 | tf_op jit(solution)/shard_map/concatenate | solution.py:472
  5.1 1.6 %collective-permute-start.2 = (bf16[4,128,128]{2,1,0:T(8,128)(2,1)S(1)}, bf16[4,128,128]{2,1,0:T(8,128)(2,1)S(1)}, u32[]{:S(2)}, u32[]{:S(2)}) collective-permute-start(bf16[4,128,128]{2,1,0:T(8,128)(2,1)S(1)} %pad_maximum_fusion.refs_0_), channel_id=1, source_target_pairs={{0,4},{1,3},{4,8},{5,1},{8,12},{9,5},{12,14},{13,9},{14,10},{15,13... | collective-permute-start | bytes 393224 | tf_op jit(solution)/shard_map/ppermute | solution.py:31
  6.7 0.0 collective-permute-done.1.refs_2_
  6.7 1.6 %collective-permute-start.4 = (bf16[4,128,128]{2,1,0:T(8,128)(2,1)S(1)}, bf16[4,128,128]{2,1,0:T(8,128)(2,1)S(1)}, u32[]{:S(2)}, u32[]{:S(2)}) collective-permute-start(bf16[4,128,128]{2,1,0:T(8,128)(2,1)S(1)} %collective-permute-done.1.refs_2_), channel_id=1, source_target_pairs={{0,4},{1,3},{4,8},{5,1},{8,12},{9,5},{12,14},{13,9},{14,10},{15,13... | collective-permute-start | bytes 393224 | tf_op jit(solution)/shard_map/ppermute | solution.py:31
  8.3 0.0 collective-permute-done.3.refs_4_
  8.3 1.5 %collective-permute-start.9 = (bf16[4,128,128]{2,1,0:T(8,128)(2,1)S(1)}, bf16[4,128,128]{2,1,0:T(8,128)(2,1)S(1)}, u32[]{:S(2)}, u32[]{:S(2)}) collective-permute-start(bf16[4,128,128]{2,1,0:T(8,128)(2,1)S(1)} %collective-permute-done.3.refs_4_), channel_id=1, source_target_pairs={{0,4},{1,3},{4,8},{5,1},{8,12},{9,5},{12,14},{13,9},{14,10},{15,13... | collective-permute-start | bytes 393224 | tf_op jit(solution)/shard_map/ppermute | solution.py:31
  9.8 0.0 collective-permute-start.6
  9.8 0.3 collective-permute-done.2.refs_3_.refs_1_
  10.1 1.6 %collective-permute-start.8 = (bf16[4,128,128]{2,1,0:T(8,128)(2,1)S(1)}, bf16[4,128,128]{2,1,0:T(8,128)(2,1)S(1)}, u32[]{:S(2)}, u32[]{:S(2)}) collective-permute-start(bf16[4,128,128]{2,1,0:T(8,128)(2,1)S(1)} %collective-permute-done.2.refs_3_.refs_1_), channel_id=1, source_target_pairs={{0,4},{1,3},{4,8},{5,1},{8,12},{9,5},{12,14},{13,9},{14,10},{15,13... | collective-permute-start | bytes 393224 | tf_op jit(solution)/shard_map/ppermute | solution.py:31
  11.7 0.0 collective-permute-start.5
  11.7 0.0 collective-permute-done.4.refs_5_
  11.7 1.6 %collective-permute-start.10 = (bf16[4,128,128]{2,1,0:T(8,128)(2,1)S(1)}, bf16[4,128,128]{2,1,0:T(8,128)(2,1)S(1)}, u32[]{:S(2)}, u32[]{:S(2)}) collective-permute-start(bf16[4,128,128]{2,1,0:T(8,128)(2,1)S(1)} %collective-permute-done.4.refs_5_), channel_id=1, source_target_pairs={{0,4},{1,3},{4,8},{5,1},{8,12},{9,5},{12,14},{13,9},{14,10},{15,13... | collective-permute-start | bytes 393224 | tf_op jit(solution)/shard_map/ppermute | solution.py:31
  13.3 0.0 collective-permute-done.9.refs_10_
  13.3 0.0 collective-permute-start.7
  13.3 0.0 collective-permute-done.6.refs_7_
  13.3 1.6 %collective-permute-start.15 = (bf16[4,128,128]{2,1,0:T(8,128)(2,1)S(1)}, bf16[4,128,128]{2,1,0:T(8,128)(2,1)S(1)}, u32[]{:S(2)}, u32[]{:S(2)}) collective-permute-start(bf16[4,128,128]{2,1,0:T(8,128)(2,1)S(1)} %collective-permute-done.9.refs_10_), channel_id=1, source_target_pairs={{0,4},{1,3},{4,8},{5,1},{8,12},{9,5},{12,14},{13,9},{14,10},{15,13... | collective-permute-start | bytes 393224 | tf_op jit(solution)/shard_map/ppermute | solution.py:31
  14.9 0.2 collective-permute-done.8.refs_9_.refs_3_
  15.1 0.0 collective-permute-start.12
  15.1 0.0 collective-permute-done.5.refs_6_.refs_2_
  15.1 1.6 %collective-permute-start.14 = (bf16[4,128,128]{2,1,0:T(8,128)(2,1)S(1)}, bf16[4,128,128]{2,1,0:T(8,128)(2,1)S(1)}, u32[]{:S(2)}, u32[]{:S(2)}) collective-permute-start(bf16[4,128,128]{2,1,0:T(8,128)(2,1)S(1)} %collective-permute-done.8.refs_9_.refs_3_), channel_id=1, source_target_pairs={{0,4},{1,3},{4,8},{5,1},{8,12},{9,5},{12,14},{13,9},{14,10},{15,13... | collective-permute-start | bytes 393224 | tf_op jit(solution)/shard_map/ppermute | solution.py:31
  16.7 0.0 collective-permute-done.10.refs_11_
  16.7 0.0 collective-permute-start.11
  16.7 0.0 collective-permute-done.7.refs_8_
  16.7 1.6 %collective-permute-start.16 = (bf16[4,128,128]{2,1,0:T(8,128)(2,1)S(1)}, bf16[4,128,128]{2,1,0:T(8,128)(2,1)S(1)}, u32[]{:S(2)}, u32[]{:S(2)}) collective-permute-start(bf16[4,128,128]{2,1,0:T(8,128)(2,1)S(1)} %collective-permute-done.10.refs_11_), channel_id=1, source_target_pairs={{0,4},{1,3},{4,8},{5,1},{8,12},{9,5},{12,14},{13,9},{14,10},{15,13... | collective-permute-start | bytes 393224 | tf_op jit(solution)/shard_map/ppermute | solution.py:31
  18.3 0.0 collective-permute-done.15.refs_16_
  18.3 1.6 %collective-permute-start.21 = (bf16[4,128,128]{2,1,0:T(8,128)(2,1)S(1)}, bf16[4,128,128]{2,1,0:T(8,128)(2,1)S(1)}, u32[]{:S(2)}, u32[]{:S(2)}) collective-permute-start(bf16[4,128,128]{2,1,0:T(8,128)(2,1)S(1)} %collective-permute-done.15.refs_16_), channel_id=1, source_target_pairs={{0,4},{1,3},{4,8},{5,1},{8,12},{9,5},{12,14},{13,9},{14,10},{15,13... | collective-permute-start | bytes 393224 | tf_op jit(solution)/shard_map/ppermute | solution.py:31
  19.9 0.2 collective-permute-done.14.refs_15_.refs_5_
  20.1 1.6 %collective-permute-start.20 = (bf16[4,128,128]{2,1,0:T(8,128)(2,1)S(1)}, bf16[4,128,128]{2,1,0:T(8,128)(2,1)S(1)}, u32[]{:S(2)}, u32[]{:S(2)}) collective-permute-start(bf16[4,128,128]{2,1,0:T(8,128)(2,1)S(1)} %collective-permute-done.14.refs_15_.refs_5_), channel_id=1, source_target_pairs={{0,4},{1,3},{4,8},{5,1},{8,12},{9,5},{12,14},{13,9},{14,10},{15,13... | collective-permute-start | bytes 393224 | tf_op jit(solution)/shard_map/ppermute | solution.py:31
  21.6 0.1 collective-permute-done.16.refs_17_
  21.7 0.0 collective-permute-start.17
  21.7 0.0 collective-permute-done.13.refs_14_
  21.7 1.6 %collective-permute-start.22 = (bf16[4,128,128]{2,1,0:T(8,128)(2,1)S(1)}, bf16[4,128,128]{2,1,0:T(8,128)(2,1)S(1)}, u32[]{:S(2)}, u32[]{:S(2)}) collective-permute-start(bf16[4,128,128]{2,1,0:T(8,128)(2,1)S(1)} %collective-permute-done.16.refs_17_), channel_id=1, source_target_pairs={{0,4},{1,3},{4,8},{5,1},{8,12},{9,5},{12,14},{13,9},{14,10},{15,13... | collective-permute-start | bytes 393224 | tf_op jit(solution)/shard_map/ppermute | solution.py:31
  23.3 0.0 collective-permute-done.21.refs_22_
  23.3 0.0 collective-permute-start.19
  23.4 0.7 %copy-done = s32[256,4]{0,1:T(4,128)S(1)} copy-done((s32[256,4]{0,1:T(4,128)S(1)}, s32[256,4]{0,1:T(4,128)}, u32[]{:S(2)}) %copy-start) | copy-done | bytes 4120
  24.0 3.4 %shard_map.67 = (s32[6,384]{1,0:T(8,128)S(1)}, bf16[256,128,128]{2,1,0:T(8,128)(2,1)S(1)}) custom-call(s32[4,256]{1,0:T(4,128)S(1)} %bitcast.2, bf16[256,128,128]{2,1,0:T(8,128)(2,1)} %left_ref.1), custom_call_target="tpu_custom_call" | custom-call | tf_op jit(solution)/shard_map/pallas_call | solution.py:192
  27.5 0.0 collective-permute-done.20.refs_21_.refs_7_
  27.5 0.0 collective-permute-done.17.refs_18_.refs_6_
  27.5 0.0 collective-permute-done.19.refs_20_
  27.5 11.4 %shard_map.68 = (bf16[1040,128]{1,0:T(8,128)(2,1)S(1)}, bf16[1024,128]{1,0:T(8,128)(2,1)S(1)}, f32[17,256,128]{2,1,0:T(8,128)S(1)}, f32[8,128]{1,0:T(8,128)S(1)}) custom-call(s32[6,384]{1,0:T(8,128)S(1)} %get-tuple-element.29.plan_ref, bf16[256,128,128]{2,1,0:T(8,128)(2,1)S(1)} %get-tuple-element.30.left_ref, ...), custom_call_target="tpu_custom_call" | custom-call | flops 4294967296 | bytes 15588608 | tf_op jit(solution)/shard_map/pallas_call | solution.py:361
  38.9 2.4 %collective-permute-start.23 = (bf16[1040,128]{1,0:T(8,128)(2,1)S(1)}, bf16[1040,128]{1,0:T(8,128)(2,1)S(1)}, u32[]{:S(2)}, u32[]{:S(2)}) collective-permute-start(bf16[1040,128]{1,0:T(8,128)(2,1)S(1)} %get-tuple-element.34), channel_id=1, source_target_pairs={{0,1},{1,0},{2,3},{3,2},{4,5},{5,4},{6,7},{7,6},{8,9},{9,8},{10,11... | collective-permute-start | bytes 798728 | tf_op jit(solution)/shard_map/ppermute | solution.py:17
  41.3 0.1 collective-permute-start.24
  41.4 1.1 %collective-permute-done.23.received_ref = bf16[1040,128]{1,0:T(8,128)(2,1)S(1)} collective-permute-done((bf16[1040,128]{1,0:T(8,128)(2,1)S(1)}, bf16[1040,128]{1,0:T(8,128)(2,1)S(1)}, u32[]{:S(2)}, u32[]{:S(2)}) %collective-permute-start.23) | collective-permute-done | bytes 266272 | tf_op jit(solution)/shard_map/ppermute | solution.py:17
  42.5 4.1 %collective-permute-start.25 = (bf16[272,128]{1,0:T(8,128)(2,1)S(1)}, bf16[272,128]{1,0:T(8,128)(2,1)S(1)}, u32[]{:S(2)}, u32[]{:S(2)}) collective-permute-start(bf16[272,128]{1,0:T(8,128)(2,1)S(1)} %get-tuple-element.38), channel_id=1, source_target_pairs={{0,14},{1,15},{2,12},{3,13},{4,10},{5,11},{6,8},{7,9},{8,6},{9,7},... | collective-permute-start | bytes 208904 | tf_op jit(solution)/shard_map/ppermute | solution.py:17
  46.6 0.0 collective-permute-start.26
  46.6 1.1 %collective-permute-start.27 = (bf16[272,128]{1,0:T(8,128)(2,1)S(1)}, bf16[272,128]{1,0:T(8,128)(2,1)S(1)}, u32[]{:S(2)}, u32[]{:S(2)}) collective-permute-start(bf16[272,128]{1,0:T(8,128)(2,1)S(1)} %get-tuple-element.40), channel_id=1, source_target_pairs={{0,10},{1,11},{2,8},{3,9},{4,14},{5,15},{6,12},{7,13},{8,2},{9,3},... | collective-permute-start | bytes 208904 | tf_op jit(solution)/shard_map/ppermute | solution.py:17
  47.7 2.6 %collective-permute-start.28 = (bf16[272,128]{1,0:T(8,128)(2,1)S(1)}, bf16[272,128]{1,0:T(8,128)(2,1)S(1)}, u32[]{:S(2)}, u32[]{:S(2)}) collective-permute-start(bf16[272,128]{1,0:T(8,128)(2,1)S(1)} %get-tuple-element.41), channel_id=1, source_target_pairs={{0,8},{1,9},{2,10},{3,11},{4,12},{5,13},{6,14},{7,15},{8,0},{9,1},... | collective-permute-start | bytes 208904 | tf_op jit(solution)/shard_map/ppermute | solution.py:17
  50.2 0.0 collective-permute-done.24.received_ref
  50.2 0.1 shard_map.70
  50.3 1.7 %collective-permute-start.29 = (bf16[272,128]{1,0:T(8,128)(2,1)S(1)}, bf16[272,128]{1,0:T(8,128)(2,1)S(1)}, u32[]{:S(2)}, u32[]{:S(2)}) collective-permute-start(bf16[272,128]{1,0:T(8,128)(2,1)S(1)} %get-tuple-element.42), channel_id=1, source_target_pairs={{0,6},{1,7},{2,4},{3,5},{4,2},{5,3},{6,0},{7,1},{8,14},{9,15},{10,... | collective-permute-start | bytes 208904 | tf_op jit(solution)/shard_map/ppermute | solution.py:17
  52.0 0.0 collective-permute-done.25.refs_0_
  52.0 0.6 collective-permute-start.30
  52.5 0.9 %collective-permute-done.26.refs_1_ = bf16[272,128]{1,0:T(8,128)(2,1)S(1)} collective-permute-done((bf16[272,128]{1,0:T(8,128)(2,1)S(1)}, bf16[272,128]{1,0:T(8,128)(2,1)S(1)}, u32[]{:S(2)}, u32[]{:S(2)}) %collective-permute-start.26) | collective-permute-done | bytes 69664 | tf_op jit(solution)/shard_map/ppermute | solution.py:17
  53.5 0.6 collective-permute-start.31
  54.0 1.0 %shard_map.72 = f32[2,2]{1,0:T(2,128)} custom-call(bf16[4,128,128]{2,1,0:T(8,128)(2,1)S(1)} %pad_maximum_fusion.refs_0_, bf16[4,128,128]{2,1,0:T(8,128)(2,1)S(1)} %collective-permute-done.2.refs_3_.refs_1_, bf16[4,128,128]{2,1,0:T(8,128)(2,1)S(1)} %collective-permute-done.5.refs_6_.refs_2_, bf16[4,128,128]{2,1,0:T(8,128)(2,1)S(1)} %collective-permute-done.8.refs_9_.refs_3_, ...), custom_call_target="tpu_custom_call" | custom-call | tf_op jit(solution)/shard_map/pallas_call | solution.py:397
  55.0 3.4 %collective-permute-done.27.refs_2_ = bf16[272,128]{1,0:T(8,128)(2,1)S(1)} collective-permute-done((bf16[272,128]{1,0:T(8,128)(2,1)S(1)}, bf16[272,128]{1,0:T(8,128)(2,1)S(1)}, u32[]{:S(2)}, u32[]{:S(2)}) %collective-permute-start.27) | collective-permute-done | bytes 69664 | tf_op jit(solution)/shard_map/ppermute | solution.py:17
  58.4 0.0 collective-permute-done.29.refs_4_
  58.4 0.1 collective-permute-done.30.refs_5_
  58.5 0.0 collective-permute-done.31.refs_6_
  58.5 0.7 %shard_map.71 = (f32[1,2,128,128]{3,2,1,0:T(8,128)}, f32[2,2]{1,0:T(2,128)}) custom-call(f32[256,128]{1,0:T(8,128)S(1)} %get-tuple-element.37.mine_ref, f32[16,128]{1,0:T(8,128)S(1)} %get-tuple-element.35.total_ref, bf16[272,128]{1,0:T(8,128)(2,1)S(1)} %collective-permute-done.25.refs_0_, bf16[272,128]{1,0:T(8,128)(2,1)S(1)} %collective-permute-done.26.refs_1_, ...), custom_call_target="tpu_custom_call" | custom-call | tf_op jit(solution)/shard_map/pallas_call | solution.py:459
  (11 shorter events, 0.1 us)
Async XLA Ops:
  0.6 26.9 %copy-start.1 = (bf16[4,128,128]{2,1,0:T(8,128)(2,1)S(1)}, bf16[4,128,128]{2,1,0:T(8,128)(2,1)}, u32[]{:S(2)}) copy-start(bf16[4,128,128]{2,1,0:T(8,128)(2,1)} %refs_1_.1) | copy-start | bytes 393220
  0.6 3.6 %collective-permute-start = (bf16[2,128,128]{2,1,0:T(8,128)(2,1)}, bf16[2,128,128]{2,1,0:T(8,128)(2,1)S(1)}, u32[]{:S(2)}, u32[]{:S(2)}) collective-permute-start(bf16[2,128,128]{2,1,0:T(8,128)(2,1)} %bitcast.3), channel_id=1, source_target_pairs={{0,1},{1,0},{2,3},{3,2},{4,5},{5,4},{6,7},{7,6},{8,9},{9,8},{10,11... | collective-permute-start | bytes 196616 | tf_op jit(solution)/shard_map/ppermute | solution.py:17
  1.2 5.6 %collective-permute-start.1 = (bf16[4,128,128]{2,1,0:T(8,128)(2,1)}, bf16[4,128,128]{2,1,0:T(8,128)(2,1)S(1)}, u32[]{:S(2)}, u32[]{:S(2)}) collective-permute-start(bf16[4,128,128]{2,1,0:T(8,128)(2,1)} %refs_1_.1), channel_id=1, source_target_pairs={{0,1},{1,0},{2,3},{3,2},{4,5},{5,4},{6,7},{7,6},{8,9},{9,8},{10,11... | collective-permute-start | bytes 393224 | tf_op jit(solution)/shard_map/ppermute | solution.py:17
  1.2 7.1 %collective-permute-start.3 = (bf16[4,128,128]{2,1,0:T(8,128)(2,1)}, bf16[4,128,128]{2,1,0:T(8,128)(2,1)S(1)}, u32[]{:S(2)}, u32[]{:S(2)}) collective-permute-start(bf16[4,128,128]{2,1,0:T(8,128)(2,1)} %refs_1_.1), channel_id=1, source_target_pairs={{0,4},{1,3},{4,8},{5,1},{8,12},{9,5},{12,14},{13,9},{14,10},{15,13... | collective-permute-start | bytes 393224 | tf_op jit(solution)/shard_map/ppermute | solution.py:31
  5.1 5.0 %collective-permute-start.2 = (bf16[4,128,128]{2,1,0:T(8,128)(2,1)S(1)}, bf16[4,128,128]{2,1,0:T(8,128)(2,1)S(1)}, u32[]{:S(2)}, u32[]{:S(2)}) collective-permute-start(bf16[4,128,128]{2,1,0:T(8,128)(2,1)S(1)} %pad_maximum_fusion.refs_0_), channel_id=1, source_target_pairs={{0,4},{1,3},{4,8},{5,1},{8,12},{9,5},{12,14},{13,9},{14,10},{15,13... | collective-permute-start | bytes 393224 | tf_op jit(solution)/shard_map/ppermute | solution.py:31
  6.7 5.0 %collective-permute-start.4 = (bf16[4,128,128]{2,1,0:T(8,128)(2,1)S(1)}, bf16[4,128,128]{2,1,0:T(8,128)(2,1)S(1)}, u32[]{:S(2)}, u32[]{:S(2)}) collective-permute-start(bf16[4,128,128]{2,1,0:T(8,128)(2,1)S(1)} %collective-permute-done.1.refs_2_), channel_id=1, source_target_pairs={{0,4},{1,3},{4,8},{5,1},{8,12},{9,5},{12,14},{13,9},{14,10},{15,13... | collective-permute-start | bytes 393224 | tf_op jit(solution)/shard_map/ppermute | solution.py:31
  8.3 5.0 %collective-permute-start.9 = (bf16[4,128,128]{2,1,0:T(8,128)(2,1)S(1)}, bf16[4,128,128]{2,1,0:T(8,128)(2,1)S(1)}, u32[]{:S(2)}, u32[]{:S(2)}) collective-permute-start(bf16[4,128,128]{2,1,0:T(8,128)(2,1)S(1)} %collective-permute-done.3.refs_4_), channel_id=1, source_target_pairs={{0,4},{1,3},{4,8},{5,1},{8,12},{9,5},{12,14},{13,9},{14,10},{15,13... | collective-permute-start | bytes 393224 | tf_op jit(solution)/shard_map/ppermute | solution.py:31
  9.8 3.5 %collective-permute-start.6 = (bf16[4,128,128]{2,1,0:T(8,128)(2,1)S(1)}, bf16[4,128,128]{2,1,0:T(8,128)(2,1)S(1)}, u32[]{:S(2)}, u32[]{:S(2)}) collective-permute-start(bf16[4,128,128]{2,1,0:T(8,128)(2,1)S(1)} %collective-permute-done.3.refs_4_), channel_id=1, source_target_pairs={{0,1},{1,0},{2,3},{3,2},{4,5},{5,4},{6,7},{7,6},{8,9},{9,8},{10,11... | collective-permute-start | bytes 393224 | tf_op jit(solution)/shard_map/ppermute | solution.py:17
  10.1 5.0 %collective-permute-start.8 = (bf16[4,128,128]{2,1,0:T(8,128)(2,1)S(1)}, bf16[4,128,128]{2,1,0:T(8,128)(2,1)S(1)}, u32[]{:S(2)}, u32[]{:S(2)}) collective-permute-start(bf16[4,128,128]{2,1,0:T(8,128)(2,1)S(1)} %collective-permute-done.2.refs_3_.refs_1_), channel_id=1, source_target_pairs={{0,4},{1,3},{4,8},{5,1},{8,12},{9,5},{12,14},{13,9},{14,10},{15,13... | collective-permute-start | bytes 393224 | tf_op jit(solution)/shard_map/ppermute | solution.py:31
  11.7 3.4 %collective-permute-start.5 = (bf16[4,128,128]{2,1,0:T(8,128)(2,1)S(1)}, bf16[4,128,128]{2,1,0:T(8,128)(2,1)S(1)}, u32[]{:S(2)}, u32[]{:S(2)}) collective-permute-start(bf16[4,128,128]{2,1,0:T(8,128)(2,1)S(1)} %collective-permute-done.2.refs_3_.refs_1_), channel_id=1, source_target_pairs={{0,1},{1,0},{2,3},{3,2},{4,5},{5,4},{6,7},{7,6},{8,9},{9,8},{10,11... | collective-permute-start | bytes 393224 | tf_op jit(solution)/shard_map/ppermute | solution.py:17
  11.7 5.0 %collective-permute-start.10 = (bf16[4,128,128]{2,1,0:T(8,128)(2,1)S(1)}, bf16[4,128,128]{2,1,0:T(8,128)(2,1)S(1)}, u32[]{:S(2)}, u32[]{:S(2)}) collective-permute-start(bf16[4,128,128]{2,1,0:T(8,128)(2,1)S(1)} %collective-permute-done.4.refs_5_), channel_id=1, source_target_pairs={{0,4},{1,3},{4,8},{5,1},{8,12},{9,5},{12,14},{13,9},{14,10},{15,13... | collective-permute-start | bytes 393224 | tf_op jit(solution)/shard_map/ppermute | solution.py:31
  13.3 3.4 %collective-permute-start.7 = (bf16[4,128,128]{2,1,0:T(8,128)(2,1)S(1)}, bf16[4,128,128]{2,1,0:T(8,128)(2,1)S(1)}, u32[]{:S(2)}, u32[]{:S(2)}) collective-permute-start(bf16[4,128,128]{2,1,0:T(8,128)(2,1)S(1)} %collective-permute-done.4.refs_5_), channel_id=1, source_target_pairs={{0,1},{1,0},{2,3},{3,2},{4,5},{5,4},{6,7},{7,6},{8,9},{9,8},{10,11... | collective-permute-start | bytes 393224 | tf_op jit(solution)/shard_map/ppermute | solution.py:17
  13.3 5.0 %collective-permute-start.15 = (bf16[4,128,128]{2,1,0:T(8,128)(2,1)S(1)}, bf16[4,128,128]{2,1,0:T(8,128)(2,1)S(1)}, u32[]{:S(2)}, u32[]{:S(2)}) collective-permute-start(bf16[4,128,128]{2,1,0:T(8,128)(2,1)S(1)} %collective-permute-done.9.refs_10_), channel_id=1, source_target_pairs={{0,4},{1,3},{4,8},{5,1},{8,12},{9,5},{12,14},{13,9},{14,10},{15,13... | collective-permute-start | bytes 393224 | tf_op jit(solution)/shard_map/ppermute | solution.py:31
  15.1 3.2 %collective-permute-start.12 = (bf16[4,128,128]{2,1,0:T(8,128)(2,1)S(1)}, bf16[4,128,128]{2,1,0:T(8,128)(2,1)S(1)}, u32[]{:S(2)}, u32[]{:S(2)}) collective-permute-start(bf16[4,128,128]{2,1,0:T(8,128)(2,1)S(1)} %collective-permute-done.9.refs_10_), channel_id=1, source_target_pairs={{0,1},{1,0},{2,3},{3,2},{4,5},{5,4},{6,7},{7,6},{8,9},{9,8},{10,11... | collective-permute-start | bytes 393224 | tf_op jit(solution)/shard_map/ppermute | solution.py:17
  15.1 5.0 %collective-permute-start.14 = (bf16[4,128,128]{2,1,0:T(8,128)(2,1)S(1)}, bf16[4,128,128]{2,1,0:T(8,128)(2,1)S(1)}, u32[]{:S(2)}, u32[]{:S(2)}) collective-permute-start(bf16[4,128,128]{2,1,0:T(8,128)(2,1)S(1)} %collective-permute-done.8.refs_9_.refs_3_), channel_id=1, source_target_pairs={{0,4},{1,3},{4,8},{5,1},{8,12},{9,5},{12,14},{13,9},{14,10},{15,13... | collective-permute-start | bytes 393224 | tf_op jit(solution)/shard_map/ppermute | solution.py:31
  16.7 3.4 %collective-permute-start.11 = (bf16[4,128,128]{2,1,0:T(8,128)(2,1)S(1)}, bf16[4,128,128]{2,1,0:T(8,128)(2,1)S(1)}, u32[]{:S(2)}, u32[]{:S(2)}) collective-permute-start(bf16[4,128,128]{2,1,0:T(8,128)(2,1)S(1)} %collective-permute-done.8.refs_9_.refs_3_), channel_id=1, source_target_pairs={{0,1},{1,0},{2,3},{3,2},{4,5},{5,4},{6,7},{7,6},{8,9},{9,8},{10,11... | collective-permute-start | bytes 393224 | tf_op jit(solution)/shard_map/ppermute | solution.py:17
  16.7 5.0 %collective-permute-start.16 = (bf16[4,128,128]{2,1,0:T(8,128)(2,1)S(1)}, bf16[4,128,128]{2,1,0:T(8,128)(2,1)S(1)}, u32[]{:S(2)}, u32[]{:S(2)}) collective-permute-start(bf16[4,128,128]{2,1,0:T(8,128)(2,1)S(1)} %collective-permute-done.10.refs_11_), channel_id=1, source_target_pairs={{0,4},{1,3},{4,8},{5,1},{8,12},{9,5},{12,14},{13,9},{14,10},{15,13... | collective-permute-start | bytes 393224 | tf_op jit(solution)/shard_map/ppermute | solution.py:31
  18.3 3.4 %collective-permute-start.13 = (bf16[4,128,128]{2,1,0:T(8,128)(2,1)S(1)}, bf16[4,128,128]{2,1,0:T(8,128)(2,1)S(1)}, u32[]{:S(2)}, u32[]{:S(2)}) collective-permute-start(bf16[4,128,128]{2,1,0:T(8,128)(2,1)S(1)} %collective-permute-done.10.refs_11_), channel_id=1, source_target_pairs={{0,1},{1,0},{2,3},{3,2},{4,5},{5,4},{6,7},{7,6},{8,9},{9,8},{10,11... | collective-permute-start | bytes 393224 | tf_op jit(solution)/shard_map/ppermute | solution.py:17
  18.3 5.0 %collective-permute-start.21 = (bf16[4,128,128]{2,1,0:T(8,128)(2,1)S(1)}, bf16[4,128,128]{2,1,0:T(8,128)(2,1)S(1)}, u32[]{:S(2)}, u32[]{:S(2)}) collective-permute-start(bf16[4,128,128]{2,1,0:T(8,128)(2,1)S(1)} %collective-permute-done.15.refs_16_), channel_id=1, source_target_pairs={{0,4},{1,3},{4,8},{5,1},{8,12},{9,5},{12,14},{13,9},{14,10},{15,13... | collective-permute-start | bytes 393224 | tf_op jit(solution)/shard_map/ppermute | solution.py:31
  20.1 7.4 %collective-permute-start.18 = (bf16[4,128,128]{2,1,0:T(8,128)(2,1)S(1)}, bf16[4,128,128]{2,1,0:T(8,128)(2,1)S(1)}, u32[]{:S(2)}, u32[]{:S(2)}) collective-permute-start(bf16[4,128,128]{2,1,0:T(8,128)(2,1)S(1)} %collective-permute-done.15.refs_16_), channel_id=1, source_target_pairs={{0,1},{1,0},{2,3},{3,2},{4,5},{5,4},{6,7},{7,6},{8,9},{9,8},{10,11... | collective-permute-start | bytes 393224 | tf_op jit(solution)/shard_map/ppermute | solution.py:17
  20.1 7.4 %collective-permute-start.20 = (bf16[4,128,128]{2,1,0:T(8,128)(2,1)S(1)}, bf16[4,128,128]{2,1,0:T(8,128)(2,1)S(1)}, u32[]{:S(2)}, u32[]{:S(2)}) collective-permute-start(bf16[4,128,128]{2,1,0:T(8,128)(2,1)S(1)} %collective-permute-done.14.refs_15_.refs_5_), channel_id=1, source_target_pairs={{0,4},{1,3},{4,8},{5,1},{8,12},{9,5},{12,14},{13,9},{14,10},{15,13... | collective-permute-start | bytes 393224 | tf_op jit(solution)/shard_map/ppermute | solution.py:31
  21.7 5.8 %collective-permute-start.17 = (bf16[4,128,128]{2,1,0:T(8,128)(2,1)S(1)}, bf16[4,128,128]{2,1,0:T(8,128)(2,1)S(1)}, u32[]{:S(2)}, u32[]{:S(2)}) collective-permute-start(bf16[4,128,128]{2,1,0:T(8,128)(2,1)S(1)} %collective-permute-done.14.refs_15_.refs_5_), channel_id=1, source_target_pairs={{0,1},{1,0},{2,3},{3,2},{4,5},{5,4},{6,7},{7,6},{8,9},{9,8},{10,11... | collective-permute-start | bytes 393224 | tf_op jit(solution)/shard_map/ppermute | solution.py:17
  21.7 5.8 %collective-permute-start.22 = (bf16[4,128,128]{2,1,0:T(8,128)(2,1)S(1)}, bf16[4,128,128]{2,1,0:T(8,128)(2,1)S(1)}, u32[]{:S(2)}, u32[]{:S(2)}) collective-permute-start(bf16[4,128,128]{2,1,0:T(8,128)(2,1)S(1)} %collective-permute-done.16.refs_17_), channel_id=1, source_target_pairs={{0,4},{1,3},{4,8},{5,1},{8,12},{9,5},{12,14},{13,9},{14,10},{15,13... | collective-permute-start | bytes 393224 | tf_op jit(solution)/shard_map/ppermute | solution.py:31
  23.3 4.1 %collective-permute-start.19 = (bf16[4,128,128]{2,1,0:T(8,128)(2,1)S(1)}, bf16[4,128,128]{2,1,0:T(8,128)(2,1)S(1)}, u32[]{:S(2)}, u32[]{:S(2)}) collective-permute-start(bf16[4,128,128]{2,1,0:T(8,128)(2,1)S(1)} %collective-permute-done.16.refs_17_), channel_id=1, source_target_pairs={{0,1},{1,0},{2,3},{3,2},{4,5},{5,4},{6,7},{7,6},{8,9},{9,8},{10,11... | collective-permute-start | bytes 393224 | tf_op jit(solution)/shard_map/ppermute | solution.py:17
  23.4 0.7 %copy-start = (s32[256,4]{0,1:T(4,128)S(1)}, s32[256,4]{0,1:T(4,128)}, u32[]{:S(2)}) copy-start(s32[256,4]{0,1:T(4,128)} %param.7) | copy-start | bytes 12292
  38.9 3.5 %collective-permute-start.23 = (bf16[1040,128]{1,0:T(8,128)(2,1)S(1)}, bf16[1040,128]{1,0:T(8,128)(2,1)S(1)}, u32[]{:S(2)}, u32[]{:S(2)}) collective-permute-start(bf16[1040,128]{1,0:T(8,128)(2,1)S(1)} %get-tuple-element.34), channel_id=1, source_target_pairs={{0,1},{1,0},{2,3},{3,2},{4,5},{5,4},{6,7},{7,6},{8,9},{9,8},{10,11... | collective-permute-start | bytes 798728 | tf_op jit(solution)/shard_map/ppermute | solution.py:17
  41.3 9.0 %collective-permute-start.24 = (bf16[1024,128]{1,0:T(8,128)(2,1)S(1)}, bf16[1024,128]{1,0:T(8,128)(2,1)S(1)}, u32[]{:S(2)}, u32[]{:S(2)}) collective-permute-start(bf16[1024,128]{1,0:T(8,128)(2,1)S(1)} %get-tuple-element.36), channel_id=1, source_target_pairs={{0,1},{1,0},{2,3},{3,2},{4,5},{5,4},{6,7},{7,6},{8,9},{9,8},{10,11... | collective-permute-start | bytes 786440 | tf_op jit(solution)/shard_map/ppermute | solution.py:17
  42.5 9.5 %collective-permute-start.25 = (bf16[272,128]{1,0:T(8,128)(2,1)S(1)}, bf16[272,128]{1,0:T(8,128)(2,1)S(1)}, u32[]{:S(2)}, u32[]{:S(2)}) collective-permute-start(bf16[272,128]{1,0:T(8,128)(2,1)S(1)} %get-tuple-element.38), channel_id=1, source_target_pairs={{0,14},{1,15},{2,12},{3,13},{4,10},{5,11},{6,8},{7,9},{8,6},{9,7},... | collective-permute-start | bytes 208904 | tf_op jit(solution)/shard_map/ppermute | solution.py:17
  46.6 6.9 %collective-permute-start.26 = (bf16[272,128]{1,0:T(8,128)(2,1)S(1)}, bf16[272,128]{1,0:T(8,128)(2,1)S(1)}, u32[]{:S(2)}, u32[]{:S(2)}) collective-permute-start(bf16[272,128]{1,0:T(8,128)(2,1)S(1)} %get-tuple-element.39), channel_id=1, source_target_pairs={{0,12},{1,13},{2,14},{3,15},{4,8},{5,9},{6,10},{7,11},{8,4},{9,5},... | collective-permute-start | bytes 208904 | tf_op jit(solution)/shard_map/ppermute | solution.py:17
  46.6 11.8 %collective-permute-start.27 = (bf16[272,128]{1,0:T(8,128)(2,1)S(1)}, bf16[272,128]{1,0:T(8,128)(2,1)S(1)}, u32[]{:S(2)}, u32[]{:S(2)}) collective-permute-start(bf16[272,128]{1,0:T(8,128)(2,1)S(1)} %get-tuple-element.40), channel_id=1, source_target_pairs={{0,10},{1,11},{2,8},{3,9},{4,14},{5,15},{6,12},{7,13},{8,2},{9,3},... | collective-permute-start | bytes 208904 | tf_op jit(solution)/shard_map/ppermute | solution.py:17
  47.7 10.7 %collective-permute-start.28 = (bf16[272,128]{1,0:T(8,128)(2,1)S(1)}, bf16[272,128]{1,0:T(8,128)(2,1)S(1)}, u32[]{:S(2)}, u32[]{:S(2)}) collective-permute-start(bf16[272,128]{1,0:T(8,128)(2,1)S(1)} %get-tuple-element.41), channel_id=1, source_target_pairs={{0,8},{1,9},{2,10},{3,11},{4,12},{5,13},{6,14},{7,15},{8,0},{9,1},... | collective-permute-start | bytes 208904 | tf_op jit(solution)/shard_map/ppermute | solution.py:17
  50.3 8.1 %collective-permute-start.29 = (bf16[272,128]{1,0:T(8,128)(2,1)S(1)}, bf16[272,128]{1,0:T(8,128)(2,1)S(1)}, u32[]{:S(2)}, u32[]{:S(2)}) collective-permute-start(bf16[272,128]{1,0:T(8,128)(2,1)S(1)} %get-tuple-element.42), channel_id=1, source_target_pairs={{0,6},{1,7},{2,4},{3,5},{4,2},{5,3},{6,0},{7,1},{8,14},{9,15},{10,... | collective-permute-start | bytes 208904 | tf_op jit(solution)/shard_map/ppermute | solution.py:17
  52.0 6.5 %collective-permute-start.30 = (bf16[272,128]{1,0:T(8,128)(2,1)S(1)}, bf16[272,128]{1,0:T(8,128)(2,1)S(1)}, u32[]{:S(2)}, u32[]{:S(2)}) collective-permute-start(bf16[272,128]{1,0:T(8,128)(2,1)S(1)} %get-tuple-element.43), channel_id=1, source_target_pairs={{0,4},{1,5},{2,6},{3,7},{4,0},{5,1},{6,2},{7,3},{8,12},{9,13},{10,... | collective-permute-start | bytes 208904 | tf_op jit(solution)/shard_map/ppermute | solution.py:17
  53.5 5.0 %collective-permute-start.31 = (bf16[272,128]{1,0:T(8,128)(2,1)S(1)}, bf16[272,128]{1,0:T(8,128)(2,1)S(1)}, u32[]{:S(2)}, u32[]{:S(2)}) collective-permute-start(bf16[272,128]{1,0:T(8,128)(2,1)S(1)} %get-tuple-element.44), channel_id=1, source_target_pairs={{0,2},{1,3},{2,0},{3,1},{4,6},{5,7},{6,4},{7,5},{8,10},{9,11},{10,... | collective-permute-start | bytes 208904 | tf_op jit(solution)/shard_map/ppermute | solution.py:17

commit v16 on v15

--- a/solution.py
+++ b/solution.py
@@ -82,11 +82,11 @@
 
 
 def chunk_of(n):
-    return 96 if fits(n) else 48
+    return 144 if fits(n) else 48
 
 
 def pairs_of(n):
-    return 46 if fits(n) else 24
+    return 69 if fits(n) else 24
 
 
 def run_of(slots, n):
@@ -323,7 +323,7 @@
         return p00 + fold(t0 * a0), p01 + fold(t0 * a1), p10 + fold(t1 * a0), p11 + fold(t1 * a1)
 
     zero = jnp.zeros((8, 128), jnp.float32)
-    sums = lax.fori_loop(0, n, dots, (zero,) * 4, unroll=4)
+    sums = lax.fori_loop(0, n, dots, (zero,) * 4, unroll=8)
     p00, p01, p10, p11 = [jnp.sum(x) for x in sums]
 
     chips = n // 2
@@ -375,7 +375,7 @@
             pltpu.SemaphoreType.DMA((4 * len(blocks),)),
         ]
         + fetched,
-        compiler_params=pltpu.CompilerParams(vmem_limit_bytes=(30 if fits(n) else 58) * MIB),
+        compiler_params=pltpu.CompilerParams(vmem_limit_bytes=(33 if fits(n) else 58) * MIB),
         cost_estimate=pl.CostEstimate(
             flops=slots * 8 * 128**3, bytes_accessed=slots * 32768 + n * 450000, transcendentals=0
         ),

time: 59.7 us -> 59.9 us (level)
  Pallas kernels: 16.6 us -> 18.4 us
  starting transfers between devices: 34 us -> 32.6 us
    pallas_call x1, Pallas kernels: 11.4 us -> 13.2 us  [run_tasks(): pl.pallas_call(functools.partial(tasks_kernel, n, kinds), out_shape=(jax....]
    ppermute x20, starting transfers between devices: 13.6 us -> 12.2 us  [exchange(): return lax.ppermute(value, 'op', [(i, i ^ mask) for i in range(n)])]
where the time goes in v16:
time: 59.9 us; the launch traced here: 59.7 us
  starting transfers between devices  32.6 us (54%)
  Pallas kernels  18.4 us (31%)
  waiting for transfers between devices  6.38 us (11%)
  other arithmetic  0.85 us (1%)
  between operations  0.75 us (1%)
  local copies, waits for them, and re-layouts  0.69 us (1%)
    ppermute x12, starting transfers between devices, ring_step(): return lax.ppermute(value, 'op', pairs)  20.4 us
    pallas_call x1, Pallas kernels, run_tasks(): pl.pallas_call(functools.partial(tasks_kernel, n, kinds), out_shape=(jax....  13.2 us
    ppermute x20, starting transfers between devices, exchange(): return lax.ppermute(value, 'op', [(i, i ^ mask) for i in range(n)])  12.2 us
    ppermute x20, waiting for transfers between devices, exchange(): return lax.ppermute(value, 'op', [(i, i ^ mask) for i in range(n)])  5.6 us
    pallas_call x1, Pallas kernels, make_plan(): pl.pallas_call(functools.partial(stage_kernel, n, terms), in_specs=[hbm,...  3.4 us
  transfers between devices with their start and end apart: 32, of which 8 were waited for; matrix products, arithmetic and copies ran while one was open for 1% of the time, Pallas kernels for 8%

profile of v16, /device:TPU:0, one launch (start us, length us, event | category | flops | bytes accessed | tf_op | source)
XLA Modules:
  0.0 59.7 jit_solution(9792711911232903696)
XLA Ops:
  0.6 0.5 collective-permute-start
  1.2 0.1 collective-permute-start.1
  1.2 3.0 %collective-permute-start.3 = (bf16[4,128,128]{2,1,0:T(8,128)(2,1)}, bf16[4,128,128]{2,1,0:T(8,128)(2,1)S(1)}, u32[]{:S(2)}, u32[]{:S(2)}) collective-permute-start(bf16[4,128,128]{2,1,0:T(8,128)(2,1)} %refs_1_.1), channel_id=1, source_target_pairs={{0,4},{1,3},{4,8},{5,1},{8,12},{9,5},{12,14},{13,9},{14,10},{15,13... | collective-permute-start | bytes 393224 | tf_op jit(solution)/shard_map/ppermute | solution.py:31
  4.2 0.0 collective-permute-done
  4.2 0.9 %pad_maximum_fusion.refs_0_ = bf16[4,128,128]{2,1,0:T(8,128)(2,1)S(1)} fusion(bf16[2,128,128]{2,1,0:T(8,128)(2,1)S(1)} %collective-permute-done, bf16[2,128,128]{2,1,0:T(8,128)(2,1)} %bitcast.4), kind=kLoop, calls=%fused_computation | loop fusion | flops 65536 | bytes 262144 | tf_op jit(solution)/shard_map/concatenate | solution.py:472
  5.1 1.6 %collective-permute-start.2 = (bf16[4,128,128]{2,1,0:T(8,128)(2,1)S(1)}, bf16[4,128,128]{2,1,0:T(8,128)(2,1)S(1)}, u32[]{:S(2)}, u32[]{:S(2)}) collective-permute-start(bf16[4,128,128]{2,1,0:T(8,128)(2,1)S(1)} %pad_maximum_fusion.refs_0_), channel_id=1, source_target_pairs={{0,4},{1,3},{4,8},{5,1},{8,12},{9,5},{12,14},{13,9},{14,10},{15,13... | collective-permute-start | bytes 393224 | tf_op jit(solution)/shard_map/ppermute | solution.py:31
  6.7 0.0 collective-permute-done.1.refs_2_
  6.7 1.6 %collective-permute-start.4 = (bf16[4,128,128]{2,1,0:T(8,128)(2,1)S(1)}, bf16[4,128,128]{2,1,0:T(8,128)(2,1)S(1)}, u32[]{:S(2)}, u32[]{:S(2)}) collective-permute-start(bf16[4,128,128]{2,1,0:T(8,128)(2,1)S(1)} %collective-permute-done.1.refs_2_), channel_id=1, source_target_pairs={{0,4},{1,3},{4,8},{5,1},{8,12},{9,5},{12,14},{13,9},{14,10},{15,13... | collective-permute-start | bytes 393224 | tf_op jit(solution)/shard_map/ppermute | solution.py:31
  8.3 0.0 collective-permute-done.3.refs_4_
  8.3 1.5 %collective-permute-start.9 = (bf16[4,128,128]{2,1,0:T(8,128)(2,1)S(1)}, bf16[4,128,128]{2,1,0:T(8,128)(2,1)S(1)}, u32[]{:S(2)}, u32[]{:S(2)}) collective-permute-start(bf16[4,128,128]{2,1,0:T(8,128)(2,1)S(1)} %collective-permute-done.3.refs_4_), channel_id=1, source_target_pairs={{0,4},{1,3},{4,8},{5,1},{8,12},{9,5},{12,14},{13,9},{14,10},{15,13... | collective-permute-start | bytes 393224 | tf_op jit(solution)/shard_map/ppermute | solution.py:31
  9.8 0.0 collective-permute-start.6
  9.8 0.3 collective-permute-done.2.refs_3_.refs_1_
  10.1 1.6 %collective-permute-start.8 = (bf16[4,128,128]{2,1,0:T(8,128)(2,1)S(1)}, bf16[4,128,128]{2,1,0:T(8,128)(2,1)S(1)}, u32[]{:S(2)}, u32[]{:S(2)}) collective-permute-start(bf16[4,128,128]{2,1,0:T(8,128)(2,1)S(1)} %collective-permute-done.2.refs_3_.refs_1_), channel_id=1, source_target_pairs={{0,4},{1,3},{4,8},{5,1},{8,12},{9,5},{12,14},{13,9},{14,10},{15,13... | collective-permute-start | bytes 393224 | tf_op jit(solution)/shard_map/ppermute | solution.py:31
  11.7 1.6 %collective-permute-start.10 = (bf16[4,128,128]{2,1,0:T(8,128)(2,1)S(1)}, bf16[4,128,128]{2,1,0:T(8,128)(2,1)S(1)}, u32[]{:S(2)}, u32[]{:S(2)}) collective-permute-start(bf16[4,128,128]{2,1,0:T(8,128)(2,1)S(1)} %collective-permute-done.4.refs_5_), channel_id=1, source_target_pairs={{0,4},{1,3},{4,8},{5,1},{8,12},{9,5},{12,14},{13,9},{14,10},{15,13... | collective-permute-start | bytes 393224 | tf_op jit(solution)/shard_map/ppermute | solution.py:31
  13.3 0.0 collective-permute-done.9.refs_10_
  13.3 0.0 collective-permute-start.7
  13.3 0.0 collective-permute-done.6.refs_7_
  13.3 1.6 %collective-permute-start.15 = (bf16[4,128,128]{2,1,0:T(8,128)(2,1)S(1)}, bf16[4,128,128]{2,1,0:T(8,128)(2,1)S(1)}, u32[]{:S(2)}, u32[]{:S(2)}) collective-permute-start(bf16[4,128,128]{2,1,0:T(8,128)(2,1)S(1)} %collective-permute-done.9.refs_10_), channel_id=1, source_target_pairs={{0,4},{1,3},{4,8},{5,1},{8,12},{9,5},{12,14},{13,9},{14,10},{15,13... | collective-permute-start | bytes 393224 | tf_op jit(solution)/shard_map/ppermute | solution.py:31
  14.9 0.2 collective-permute-done.8.refs_9_.refs_3_
  15.1 0.0 collective-permute-done.5.refs_6_.refs_2_
  15.1 1.6 %collective-permute-start.14 = (bf16[4,128,128]{2,1,0:T(8,128)(2,1)S(1)}, bf16[4,128,128]{2,1,0:T(8,128)(2,1)S(1)}, u32[]{:S(2)}, u32[]{:S(2)}) collective-permute-start(bf16[4,128,128]{2,1,0:T(8,128)(2,1)S(1)} %collective-permute-done.8.refs_9_.refs_3_), channel_id=1, source_target_pairs={{0,4},{1,3},{4,8},{5,1},{8,12},{9,5},{12,14},{13,9},{14,10},{15,13... | collective-permute-start | bytes 393224 | tf_op jit(solution)/shard_map/ppermute | solution.py:31
  16.7 0.0 collective-permute-done.10.refs_11_
  16.7 0.0 collective-permute-start.11
  16.7 0.0 collective-permute-done.7.refs_8_
  16.7 1.6 %collective-permute-start.16 = (bf16[4,128,128]{2,1,0:T(8,128)(2,1)S(1)}, bf16[4,128,128]{2,1,0:T(8,128)(2,1)S(1)}, u32[]{:S(2)}, u32[]{:S(2)}) collective-permute-start(bf16[4,128,128]{2,1,0:T(8,128)(2,1)S(1)} %collective-permute-done.10.refs_11_), channel_id=1, source_target_pairs={{0,4},{1,3},{4,8},{5,1},{8,12},{9,5},{12,14},{13,9},{14,10},{15,13... | collective-permute-start | bytes 393224 | tf_op jit(solution)/shard_map/ppermute | solution.py:31
  18.3 0.0 collective-permute-done.15.refs_16_
  18.3 0.0 collective-permute-start.13
  18.3 0.0 collective-permute-done.12.refs_13_
  18.3 1.6 %collective-permute-start.21 = (bf16[4,128,128]{2,1,0:T(8,128)(2,1)S(1)}, bf16[4,128,128]{2,1,0:T(8,128)(2,1)S(1)}, u32[]{:S(2)}, u32[]{:S(2)}) collective-permute-start(bf16[4,128,128]{2,1,0:T(8,128)(2,1)S(1)} %collective-permute-done.15.refs_16_), channel_id=1, source_target_pairs={{0,4},{1,3},{4,8},{5,1},{8,12},{9,5},{12,14},{13,9},{14,10},{15,13... | collective-permute-start | bytes 393224 | tf_op jit(solution)/shard_map/ppermute | solution.py:31
  19.9 0.2 collective-permute-done.14.refs_15_.refs_5_
  20.1 0.0 collective-permute-start.18
  20.1 0.0 collective-permute-done.11.refs_12_.refs_4_
  20.1 1.6 %collective-permute-start.20 = (bf16[4,128,128]{2,1,0:T(8,128)(2,1)S(1)}, bf16[4,128,128]{2,1,0:T(8,128)(2,1)S(1)}, u32[]{:S(2)}, u32[]{:S(2)}) collective-permute-start(bf16[4,128,128]{2,1,0:T(8,128)(2,1)S(1)} %collective-permute-done.14.refs_15_.refs_5_), channel_id=1, source_target_pairs={{0,4},{1,3},{4,8},{5,1},{8,12},{9,5},{12,14},{13,9},{14,10},{15,13... | collective-permute-start | bytes 393224 | tf_op jit(solution)/shard_map/ppermute | solution.py:31
  21.6 0.1 collective-permute-done.16.refs_17_
  21.7 0.0 collective-permute-start.17
  21.7 1.6 %collective-permute-start.22 = (bf16[4,128,128]{2,1,0:T(8,128)(2,1)S(1)}, bf16[4,128,128]{2,1,0:T(8,128)(2,1)S(1)}, u32[]{:S(2)}, u32[]{:S(2)}) collective-permute-start(bf16[4,128,128]{2,1,0:T(8,128)(2,1)S(1)} %collective-permute-done.16.refs_17_), channel_id=1, source_target_pairs={{0,4},{1,3},{4,8},{5,1},{8,12},{9,5},{12,14},{13,9},{14,10},{15,13... | collective-permute-start | bytes 393224 | tf_op jit(solution)/shard_map/ppermute | solution.py:31
  23.3 0.0 collective-permute-done.21.refs_22_
  23.3 0.0 collective-permute-start.19
  23.4 0.7 %copy-done = s32[256,4]{0,1:T(4,128)S(1)} copy-done((s32[256,4]{0,1:T(4,128)S(1)}, s32[256,4]{0,1:T(4,128)}, u32[]{:S(2)}) %copy-start) | copy-done | bytes 4120
  24.0 3.4 %shard_map.67 = (s32[6,512]{1,0:T(8,128)S(1)}, bf16[256,128,128]{2,1,0:T(8,128)(2,1)S(1)}) custom-call(s32[4,256]{1,0:T(4,128)S(1)} %bitcast.2, bf16[256,128,128]{2,1,0:T(8,128)(2,1)} %left_ref.1), custom_call_target="tpu_custom_call" | custom-call | tf_op jit(solution)/shard_map/pallas_call | solution.py:192
  27.4 0.0 collective-permute-done.18.refs_19_
  27.5 0.0 collective-permute-done.17.refs_18_.refs_6_
  27.5 0.0 collective-permute-done.22.refs_23_
  27.5 13.2 %shard_map.68 = (bf16[1040,128]{1,0:T(8,128)(2,1)S(1)}, bf16[1024,128]{1,0:T(8,128)(2,1)S(1)}, f32[17,256,128]{2,1,0:T(8,128)S(1)}, f32[8,128]{1,0:T(8,128)S(1)}) custom-call(s32[6,512]{1,0:T(8,128)S(1)} %get-tuple-element.29.plan_ref, bf16[256,128,128]{2,1,0:T(8,128)(2,1)S(1)} %get-tuple-element.30.left_ref, ...), custom_call_target="tpu_custom_call" | custom-call | flops 4294967296 | bytes 15588608 | tf_op jit(solution)/shard_map/pallas_call | solution.py:361
  40.7 0.6 collective-permute-start.23
  41.3 0.1 collective-permute-start.24
  41.4 1.1 %collective-permute-done.23.received_ref = bf16[1040,128]{1,0:T(8,128)(2,1)S(1)} collective-permute-done((bf16[1040,128]{1,0:T(8,128)(2,1)S(1)}, bf16[1040,128]{1,0:T(8,128)(2,1)S(1)}, u32[]{:S(2)}, u32[]{:S(2)}) %collective-permute-start.23) | collective-permute-done | bytes 266272 | tf_op jit(solution)/shard_map/ppermute | solution.py:17
  42.4 0.1 shard_map.69
  42.5 4.0 %collective-permute-start.25 = (bf16[272,128]{1,0:T(8,128)(2,1)S(1)}, bf16[272,128]{1,0:T(8,128)(2,1)S(1)}, u32[]{:S(2)}, u32[]{:S(2)}) collective-permute-start(bf16[272,128]{1,0:T(8,128)(2,1)S(1)} %get-tuple-element.38), channel_id=1, source_target_pairs={{0,14},{1,15},{2,12},{3,13},{4,10},{5,11},{6,8},{7,9},{8,6},{9,7},... | collective-permute-start | bytes 208904 | tf_op jit(solution)/shard_map/ppermute | solution.py:17
  46.6 0.4 collective-permute-start.26
  46.9 0.9 %collective-permute-start.27 = (bf16[272,128]{1,0:T(8,128)(2,1)S(1)}, bf16[272,128]{1,0:T(8,128)(2,1)S(1)}, u32[]{:S(2)}, u32[]{:S(2)}) collective-permute-start(bf16[272,128]{1,0:T(8,128)(2,1)S(1)} %get-tuple-element.40), channel_id=1, source_target_pairs={{0,10},{1,11},{2,8},{3,9},{4,14},{5,15},{6,12},{7,13},{8,2},{9,3},... | collective-permute-start | bytes 208904 | tf_op jit(solution)/shard_map/ppermute | solution.py:17
  47.8 2.4 %collective-permute-start.28 = (bf16[272,128]{1,0:T(8,128)(2,1)S(1)}, bf16[272,128]{1,0:T(8,128)(2,1)S(1)}, u32[]{:S(2)}, u32[]{:S(2)}) collective-permute-start(bf16[272,128]{1,0:T(8,128)(2,1)S(1)} %get-tuple-element.41), channel_id=1, source_target_pairs={{0,8},{1,9},{2,10},{3,11},{4,12},{5,13},{6,14},{7,15},{8,0},{9,1},... | collective-permute-start | bytes 208904 | tf_op jit(solution)/shard_map/ppermute | solution.py:17
  50.3 1.7 %collective-permute-start.29 = (bf16[272,128]{1,0:T(8,128)(2,1)S(1)}, bf16[272,128]{1,0:T(8,128)(2,1)S(1)}, u32[]{:S(2)}, u32[]{:S(2)}) collective-permute-start(bf16[272,128]{1,0:T(8,128)(2,1)S(1)} %get-tuple-element.42), channel_id=1, source_target_pairs={{0,6},{1,7},{2,4},{3,5},{4,2},{5,3},{6,0},{7,1},{8,14},{9,15},{10,... | collective-permute-start | bytes 208904 | tf_op jit(solution)/shard_map/ppermute | solution.py:17
  52.0 0.0 collective-permute-done.25.refs_0_
  52.0 0.9 %collective-permute-start.30 = (bf16[272,128]{1,0:T(8,128)(2,1)S(1)}, bf16[272,128]{1,0:T(8,128)(2,1)S(1)}, u32[]{:S(2)}, u32[]{:S(2)}) collective-permute-start(bf16[272,128]{1,0:T(8,128)(2,1)S(1)} %get-tuple-element.43), channel_id=1, source_target_pairs={{0,4},{1,5},{2,6},{3,7},{4,0},{5,1},{6,2},{7,3},{8,12},{9,13},{10,... | collective-permute-start | bytes 208904 | tf_op jit(solution)/shard_map/ppermute | solution.py:17
  52.9 0.6 collective-permute-done.26.refs_1_
  53.5 0.6 collective-permute-start.31
  54.0 1.0 %shard_map.72 = f32[2,2]{1,0:T(2,128)} custom-call(bf16[4,128,128]{2,1,0:T(8,128)(2,1)S(1)} %pad_maximum_fusion.refs_0_, bf16[4,128,128]{2,1,0:T(8,128)(2,1)S(1)} %collective-permute-done.2.refs_3_.refs_1_, bf16[4,128,128]{2,1,0:T(8,128)(2,1)S(1)} %collective-permute-done.5.refs_6_.refs_2_, bf16[4,128,128]{2,1,0:T(8,128)(2,1)S(1)} %collective-permute-done.8.refs_9_.refs_3_, ...), custom_call_target="tpu_custom_call" | custom-call | tf_op jit(solution)/shard_map/pallas_call | solution.py:397
  55.0 3.4 %collective-permute-done.27.refs_2_ = bf16[272,128]{1,0:T(8,128)(2,1)S(1)} collective-permute-done((bf16[272,128]{1,0:T(8,128)(2,1)S(1)}, bf16[272,128]{1,0:T(8,128)(2,1)S(1)}, u32[]{:S(2)}, u32[]{:S(2)}) %collective-permute-start.27) | collective-permute-done | bytes 69664 | tf_op jit(solution)/shard_map/ppermute | solution.py:17
  58.4 0.5 collective-permute-done.28.refs_3_
  58.9 0.0 collective-permute-done.29.refs_4_
  58.9 0.0 collective-permute-done.30.refs_5_
  58.9 0.0 collective-permute-done.31.refs_6_
  58.9 0.7 %shard_map.71 = (f32[1,2,128,128]{3,2,1,0:T(8,128)}, f32[2,2]{1,0:T(2,128)}) custom-call(f32[256,128]{1,0:T(8,128)S(1)} %get-tuple-element.37.mine_ref, f32[16,128]{1,0:T(8,128)S(1)} %get-tuple-element.35.total_ref, bf16[272,128]{1,0:T(8,128)(2,1)S(1)} %collective-permute-done.25.refs_0_, bf16[272,128]{1,0:T(8,128)(2,1)S(1)} %collective-permute-done.26.refs_1_, ...), custom_call_target="tpu_custom_call" | custom-call | tf_op jit(solution)/shard_map/pallas_call | solution.py:459
  (11 shorter events, 0.1 us)
Async XLA Ops:
  0.6 26.9 %copy-start.1 = (bf16[4,128,128]{2,1,0:T(8,128)(2,1)S(1)}, bf16[4,128,128]{2,1,0:T(8,128)(2,1)}, u32[]{:S(2)}) copy-start(bf16[4,128,128]{2,1,0:T(8,128)(2,1)} %refs_1_.1) | copy-start | bytes 393220
  0.6 3.6 %collective-permute-start = (bf16[2,128,128]{2,1,0:T(8,128)(2,1)}, bf16[2,128,128]{2,1,0:T(8,128)(2,1)S(1)}, u32[]{:S(2)}, u32[]{:S(2)}) collective-permute-start(bf16[2,128,128]{2,1,0:T(8,128)(2,1)} %bitcast.3), channel_id=1, source_target_pairs={{0,1},{1,0},{2,3},{3,2},{4,5},{5,4},{6,7},{7,6},{8,9},{9,8},{10,11... | collective-permute-start | bytes 196616 | tf_op jit(solution)/shard_map/ppermute | solution.py:17
  1.2 5.6 %collective-permute-start.1 = (bf16[4,128,128]{2,1,0:T(8,128)(2,1)}, bf16[4,128,128]{2,1,0:T(8,128)(2,1)S(1)}, u32[]{:S(2)}, u32[]{:S(2)}) collective-permute-start(bf16[4,128,128]{2,1,0:T(8,128)(2,1)} %refs_1_.1), channel_id=1, source_target_pairs={{0,1},{1,0},{2,3},{3,2},{4,5},{5,4},{6,7},{7,6},{8,9},{9,8},{10,11... | collective-permute-start | bytes 393224 | tf_op jit(solution)/shard_map/ppermute | solution.py:17
  1.2 7.1 %collective-permute-start.3 = (bf16[4,128,128]{2,1,0:T(8,128)(2,1)}, bf16[4,128,128]{2,1,0:T(8,128)(2,1)S(1)}, u32[]{:S(2)}, u32[]{:S(2)}) collective-permute-start(bf16[4,128,128]{2,1,0:T(8,128)(2,1)} %refs_1_.1), channel_id=1, source_target_pairs={{0,4},{1,3},{4,8},{5,1},{8,12},{9,5},{12,14},{13,9},{14,10},{15,13... | collective-permute-start | bytes 393224 | tf_op jit(solution)/shard_map/ppermute | solution.py:31
  5.1 5.0 %collective-permute-start.2 = (bf16[4,128,128]{2,1,0:T(8,128)(2,1)S(1)}, bf16[4,128,128]{2,1,0:T(8,128)(2,1)S(1)}, u32[]{:S(2)}, u32[]{:S(2)}) collective-permute-start(bf16[4,128,128]{2,1,0:T(8,128)(2,1)S(1)} %pad_maximum_fusion.refs_0_), channel_id=1, source_target_pairs={{0,4},{1,3},{4,8},{5,1},{8,12},{9,5},{12,14},{13,9},{14,10},{15,13... | collective-permute-start | bytes 393224 | tf_op jit(solution)/shard_map/ppermute | solution.py:31
  6.7 5.0 %collective-permute-start.4 = (bf16[4,128,128]{2,1,0:T(8,128)(2,1)S(1)}, bf16[4,128,128]{2,1,0:T(8,128)(2,1)S(1)}, u32[]{:S(2)}, u32[]{:S(2)}) collective-permute-start(bf16[4,128,128]{2,1,0:T(8,128)(2,1)S(1)} %collective-permute-done.1.refs_2_), channel_id=1, source_target_pairs={{0,4},{1,3},{4,8},{5,1},{8,12},{9,5},{12,14},{13,9},{14,10},{15,13... | collective-permute-start | bytes 393224 | tf_op jit(solution)/shard_map/ppermute | solution.py:31
  8.3 5.0 %collective-permute-start.9 = (bf16[4,128,128]{2,1,0:T(8,128)(2,1)S(1)}, bf16[4,128,128]{2,1,0:T(8,128)(2,1)S(1)}, u32[]{:S(2)}, u32[]{:S(2)}) collective-permute-start(bf16[4,128,128]{2,1,0:T(8,128)(2,1)S(1)} %collective-permute-done.3.refs_4_), channel_id=1, source_target_pairs={{0,4},{1,3},{4,8},{5,1},{8,12},{9,5},{12,14},{13,9},{14,10},{15,13... | collective-permute-start | bytes 393224 | tf_op jit(solution)/shard_map/ppermute | solution.py:31
  9.8 3.5 %collective-permute-start.6 = (bf16[4,128,128]{2,1,0:T(8,128)(2,1)S(1)}, bf16[4,128,128]{2,1,0:T(8,128)(2,1)S(1)}, u32[]{:S(2)}, u32[]{:S(2)}) collective-permute-start(bf16[4,128,128]{2,1,0:T(8,128)(2,1)S(1)} %collective-permute-done.3.refs_4_), channel_id=1, source_target_pairs={{0,1},{1,0},{2,3},{3,2},{4,5},{5,4},{6,7},{7,6},{8,9},{9,8},{10,11... | collective-permute-start | bytes 393224 | tf_op jit(solution)/shard_map/ppermute | solution.py:17
  10.1 5.0 %collective-permute-start.8 = (bf16[4,128,128]{2,1,0:T(8,128)(2,1)S(1)}, bf16[4,128,128]{2,1,0:T(8,128)(2,1)S(1)}, u32[]{:S(2)}, u32[]{:S(2)}) collective-permute-start(bf16[4,128,128]{2,1,0:T(8,128)(2,1)S(1)} %collective-permute-done.2.refs_3_.refs_1_), channel_id=1, source_target_pairs={{0,4},{1,3},{4,8},{5,1},{8,12},{9,5},{12,14},{13,9},{14,10},{15,13... | collective-permute-start | bytes 393224 | tf_op jit(solution)/shard_map/ppermute | solution.py:31
  11.7 3.4 %collective-permute-start.5 = (bf16[4,128,128]{2,1,0:T(8,128)(2,1)S(1)}, bf16[4,128,128]{2,1,0:T(8,128)(2,1)S(1)}, u32[]{:S(2)}, u32[]{:S(2)}) collective-permute-start(bf16[4,128,128]{2,1,0:T(8,128)(2,1)S(1)} %collective-permute-done.2.refs_3_.refs_1_), channel_id=1, source_target_pairs={{0,1},{1,0},{2,3},{3,2},{4,5},{5,4},{6,7},{7,6},{8,9},{9,8},{10,11... | collective-permute-start | bytes 393224 | tf_op jit(solution)/shard_map/ppermute | solution.py:17
  11.7 5.0 %collective-permute-start.10 = (bf16[4,128,128]{2,1,0:T(8,128)(2,1)S(1)}, bf16[4,128,128]{2,1,0:T(8,128)(2,1)S(1)}, u32[]{:S(2)}, u32[]{:S(2)}) collective-permute-start(bf16[4,128,128]{2,1,0:T(8,128)(2,1)S(1)} %collective-permute-done.4.refs_5_), channel_id=1, source_target_pairs={{0,4},{1,3},{4,8},{5,1},{8,12},{9,5},{12,14},{13,9},{14,10},{15,13... | collective-permute-start | bytes 393224 | tf_op jit(solution)/shard_map/ppermute | solution.py:31
  13.3 3.4 %collective-permute-start.7 = (bf16[4,128,128]{2,1,0:T(8,128)(2,1)S(1)}, bf16[4,128,128]{2,1,0:T(8,128)(2,1)S(1)}, u32[]{:S(2)}, u32[]{:S(2)}) collective-permute-start(bf16[4,128,128]{2,1,0:T(8,128)(2,1)S(1)} %collective-permute-done.4.refs_5_), channel_id=1, source_target_pairs={{0,1},{1,0},{2,3},{3,2},{4,5},{5,4},{6,7},{7,6},{8,9},{9,8},{10,11... | collective-permute-start | bytes 393224 | tf_op jit(solution)/shard_map/ppermute | solution.py:17
  13.3 5.0 %collective-permute-start.15 = (bf16[4,128,128]{2,1,0:T(8,128)(2,1)S(1)}, bf16[4,128,128]{2,1,0:T(8,128)(2,1)S(1)}, u32[]{:S(2)}, u32[]{:S(2)}) collective-permute-start(bf16[4,128,128]{2,1,0:T(8,128)(2,1)S(1)} %collective-permute-done.9.refs_10_), channel_id=1, source_target_pairs={{0,4},{1,3},{4,8},{5,1},{8,12},{9,5},{12,14},{13,9},{14,10},{15,13... | collective-permute-start | bytes 393224 | tf_op jit(solution)/shard_map/ppermute | solution.py:31
  15.1 3.2 %collective-permute-start.12 = (bf16[4,128,128]{2,1,0:T(8,128)(2,1)S(1)}, bf16[4,128,128]{2,1,0:T(8,128)(2,1)S(1)}, u32[]{:S(2)}, u32[]{:S(2)}) collective-permute-start(bf16[4,128,128]{2,1,0:T(8,128)(2,1)S(1)} %collective-permute-done.9.refs_10_), channel_id=1, source_target_pairs={{0,1},{1,0},{2,3},{3,2},{4,5},{5,4},{6,7},{7,6},{8,9},{9,8},{10,11... | collective-permute-start | bytes 393224 | tf_op jit(solution)/shard_map/ppermute | solution.py:17
  15.1 5.0 %collective-permute-start.14 = (bf16[4,128,128]{2,1,0:T(8,128)(2,1)S(1)}, bf16[4,128,128]{2,1,0:T(8,128)(2,1)S(1)}, u32[]{:S(2)}, u32[]{:S(2)}) collective-permute-start(bf16[4,128,128]{2,1,0:T(8,128)(2,1)S(1)} %collective-permute-done.8.refs_9_.refs_3_), channel_id=1, source_target_pairs={{0,4},{1,3},{4,8},{5,1},{8,12},{9,5},{12,14},{13,9},{14,10},{15,13... | collective-permute-start | bytes 393224 | tf_op jit(solution)/shard_map/ppermute | solution.py:31
  16.7 3.4 %collective-permute-start.11 = (bf16[4,128,128]{2,1,0:T(8,128)(2,1)S(1)}, bf16[4,128,128]{2,1,0:T(8,128)(2,1)S(1)}, u32[]{:S(2)}, u32[]{:S(2)}) collective-permute-start(bf16[4,128,128]{2,1,0:T(8,128)(2,1)S(1)} %collective-permute-done.8.refs_9_.refs_3_), channel_id=1, source_target_pairs={{0,1},{1,0},{2,3},{3,2},{4,5},{5,4},{6,7},{7,6},{8,9},{9,8},{10,11... | collective-permute-start | bytes 393224 | tf_op jit(solution)/shard_map/ppermute | solution.py:17
  16.7 5.0 %collective-permute-start.16 = (bf16[4,128,128]{2,1,0:T(8,128)(2,1)S(1)}, bf16[4,128,128]{2,1,0:T(8,128)(2,1)S(1)}, u32[]{:S(2)}, u32[]{:S(2)}) collective-permute-start(bf16[4,128,128]{2,1,0:T(8,128)(2,1)S(1)} %collective-permute-done.10.refs_11_), channel_id=1, source_target_pairs={{0,4},{1,3},{4,8},{5,1},{8,12},{9,5},{12,14},{13,9},{14,10},{15,13... | collective-permute-start | bytes 393224 | tf_op jit(solution)/shard_map/ppermute | solution.py:31
  18.3 3.4 %collective-permute-start.13 = (bf16[4,128,128]{2,1,0:T(8,128)(2,1)S(1)}, bf16[4,128,128]{2,1,0:T(8,128)(2,1)S(1)}, u32[]{:S(2)}, u32[]{:S(2)}) collective-permute-start(bf16[4,128,128]{2,1,0:T(8,128)(2,1)S(1)} %collective-permute-done.10.refs_11_), channel_id=1, source_target_pairs={{0,1},{1,0},{2,3},{3,2},{4,5},{5,4},{6,7},{7,6},{8,9},{9,8},{10,11... | collective-permute-start | bytes 393224 | tf_op jit(solution)/shard_map/ppermute | solution.py:17
  18.3 5.0 %collective-permute-start.21 = (bf16[4,128,128]{2,1,0:T(8,128)(2,1)S(1)}, bf16[4,128,128]{2,1,0:T(8,128)(2,1)S(1)}, u32[]{:S(2)}, u32[]{:S(2)}) collective-permute-start(bf16[4,128,128]{2,1,0:T(8,128)(2,1)S(1)} %collective-permute-done.15.refs_16_), channel_id=1, source_target_pairs={{0,4},{1,3},{4,8},{5,1},{8,12},{9,5},{12,14},{13,9},{14,10},{15,13... | collective-permute-start | bytes 393224 | tf_op jit(solution)/shard_map/ppermute | solution.py:31
  20.1 7.4 %collective-permute-start.18 = (bf16[4,128,128]{2,1,0:T(8,128)(2,1)S(1)}, bf16[4,128,128]{2,1,0:T(8,128)(2,1)S(1)}, u32[]{:S(2)}, u32[]{:S(2)}) collective-permute-start(bf16[4,128,128]{2,1,0:T(8,128)(2,1)S(1)} %collective-permute-done.15.refs_16_), channel_id=1, source_target_pairs={{0,1},{1,0},{2,3},{3,2},{4,5},{5,4},{6,7},{7,6},{8,9},{9,8},{10,11... | collective-permute-start | bytes 393224 | tf_op jit(solution)/shard_map/ppermute | solution.py:17
  20.1 7.4 %collective-permute-start.20 = (bf16[4,128,128]{2,1,0:T(8,128)(2,1)S(1)}, bf16[4,128,128]{2,1,0:T(8,128)(2,1)S(1)}, u32[]{:S(2)}, u32[]{:S(2)}) collective-permute-start(bf16[4,128,128]{2,1,0:T(8,128)(2,1)S(1)} %collective-permute-done.14.refs_15_.refs_5_), channel_id=1, source_target_pairs={{0,4},{1,3},{4,8},{5,1},{8,12},{9,5},{12,14},{13,9},{14,10},{15,13... | collective-permute-start | bytes 393224 | tf_op jit(solution)/shard_map/ppermute | solution.py:31
  21.7 5.8 %collective-permute-start.17 = (bf16[4,128,128]{2,1,0:T(8,128)(2,1)S(1)}, bf16[4,128,128]{2,1,0:T(8,128)(2,1)S(1)}, u32[]{:S(2)}, u32[]{:S(2)}) collective-permute-start(bf16[4,128,128]{2,1,0:T(8,128)(2,1)S(1)} %collective-permute-done.14.refs_15_.refs_5_), channel_id=1, source_target_pairs={{0,1},{1,0},{2,3},{3,2},{4,5},{5,4},{6,7},{7,6},{8,9},{9,8},{10,11... | collective-permute-start | bytes 393224 | tf_op jit(solution)/shard_map/ppermute | solution.py:17
  21.7 5.8 %collective-permute-start.22 = (bf16[4,128,128]{2,1,0:T(8,128)(2,1)S(1)}, bf16[4,128,128]{2,1,0:T(8,128)(2,1)S(1)}, u32[]{:S(2)}, u32[]{:S(2)}) collective-permute-start(bf16[4,128,128]{2,1,0:T(8,128)(2,1)S(1)} %collective-permute-done.16.refs_17_), channel_id=1, source_target_pairs={{0,4},{1,3},{4,8},{5,1},{8,12},{9,5},{12,14},{13,9},{14,10},{15,13... | collective-permute-start | bytes 393224 | tf_op jit(solution)/shard_map/ppermute | solution.py:31
  23.3 4.1 %collective-permute-start.19 = (bf16[4,128,128]{2,1,0:T(8,128)(2,1)S(1)}, bf16[4,128,128]{2,1,0:T(8,128)(2,1)S(1)}, u32[]{:S(2)}, u32[]{:S(2)}) collective-permute-start(bf16[4,128,128]{2,1,0:T(8,128)(2,1)S(1)} %collective-permute-done.16.refs_17_), channel_id=1, source_target_pairs={{0,1},{1,0},{2,3},{3,2},{4,5},{5,4},{6,7},{7,6},{8,9},{9,8},{10,11... | collective-permute-start | bytes 393224 | tf_op jit(solution)/shard_map/ppermute | solution.py:17
  23.4 0.7 %copy-start = (s32[256,4]{0,1:T(4,128)S(1)}, s32[256,4]{0,1:T(4,128)}, u32[]{:S(2)}) copy-start(s32[256,4]{0,1:T(4,128)} %param.7) | copy-start | bytes 12292
  40.7 1.7 %collective-permute-start.23 = (bf16[1040,128]{1,0:T(8,128)(2,1)S(1)}, bf16[1040,128]{1,0:T(8,128)(2,1)S(1)}, u32[]{:S(2)}, u32[]{:S(2)}) collective-permute-start(bf16[1040,128]{1,0:T(8,128)(2,1)S(1)} %get-tuple-element.34), channel_id=1, source_target_pairs={{0,1},{1,0},{2,3},{3,2},{4,5},{5,4},{6,7},{7,6},{8,9},{9,8},{10,11... | collective-permute-start | bytes 798728 | tf_op jit(solution)/shard_map/ppermute | solution.py:17
  41.3 9.0 %collective-permute-start.24 = (bf16[1024,128]{1,0:T(8,128)(2,1)S(1)}, bf16[1024,128]{1,0:T(8,128)(2,1)S(1)}, u32[]{:S(2)}, u32[]{:S(2)}) collective-permute-start(bf16[1024,128]{1,0:T(8,128)(2,1)S(1)} %get-tuple-element.36), channel_id=1, source_target_pairs={{0,1},{1,0},{2,3},{3,2},{4,5},{5,4},{6,7},{7,6},{8,9},{9,8},{10,11... | collective-permute-start | bytes 786440 | tf_op jit(solution)/shard_map/ppermute | solution.py:17
  42.5 9.5 %collective-permute-start.25 = (bf16[272,128]{1,0:T(8,128)(2,1)S(1)}, bf16[272,128]{1,0:T(8,128)(2,1)S(1)}, u32[]{:S(2)}, u32[]{:S(2)}) collective-permute-start(bf16[272,128]{1,0:T(8,128)(2,1)S(1)} %get-tuple-element.38), channel_id=1, source_target_pairs={{0,14},{1,15},{2,12},{3,13},{4,10},{5,11},{6,8},{7,9},{8,6},{9,7},... | collective-permute-start | bytes 208904 | tf_op jit(solution)/shard_map/ppermute | solution.py:17
  46.6 6.9 %collective-permute-start.26 = (bf16[272,128]{1,0:T(8,128)(2,1)S(1)}, bf16[272,128]{1,0:T(8,128)(2,1)S(1)}, u32[]{:S(2)}, u32[]{:S(2)}) collective-permute-start(bf16[272,128]{1,0:T(8,128)(2,1)S(1)} %get-tuple-element.39), channel_id=1, source_target_pairs={{0,12},{1,13},{2,14},{3,15},{4,8},{5,9},{6,10},{7,11},{8,4},{9,5},... | collective-permute-start | bytes 208904 | tf_op jit(solution)/shard_map/ppermute | solution.py:17
  46.9 11.5 %collective-permute-start.27 = (bf16[272,128]{1,0:T(8,128)(2,1)S(1)}, bf16[272,128]{1,0:T(8,128)(2,1)S(1)}, u32[]{:S(2)}, u32[]{:S(2)}) collective-permute-start(bf16[272,128]{1,0:T(8,128)(2,1)S(1)} %get-tuple-element.40), channel_id=1, source_target_pairs={{0,10},{1,11},{2,8},{3,9},{4,14},{5,15},{6,12},{7,13},{8,2},{9,3},... | collective-permute-start | bytes 208904 | tf_op jit(solution)/shard_map/ppermute | solution.py:17
  47.8 11.1 %collective-permute-start.28 = (bf16[272,128]{1,0:T(8,128)(2,1)S(1)}, bf16[272,128]{1,0:T(8,128)(2,1)S(1)}, u32[]{:S(2)}, u32[]{:S(2)}) collective-permute-start(bf16[272,128]{1,0:T(8,128)(2,1)S(1)} %get-tuple-element.41), channel_id=1, source_target_pairs={{0,8},{1,9},{2,10},{3,11},{4,12},{5,13},{6,14},{7,15},{8,0},{9,1},... | collective-permute-start | bytes 208904 | tf_op jit(solution)/shard_map/ppermute | solution.py:17
  50.3 8.6 %collective-permute-start.29 = (bf16[272,128]{1,0:T(8,128)(2,1)S(1)}, bf16[272,128]{1,0:T(8,128)(2,1)S(1)}, u32[]{:S(2)}, u32[]{:S(2)}) collective-permute-start(bf16[272,128]{1,0:T(8,128)(2,1)S(1)} %get-tuple-element.42), channel_id=1, source_target_pairs={{0,6},{1,7},{2,4},{3,5},{4,2},{5,3},{6,0},{7,1},{8,14},{9,15},{10,... | collective-permute-start | bytes 208904 | tf_op jit(solution)/shard_map/ppermute | solution.py:17
  52.0 6.9 %collective-permute-start.30 = (bf16[272,128]{1,0:T(8,128)(2,1)S(1)}, bf16[272,128]{1,0:T(8,128)(2,1)S(1)}, u32[]{:S(2)}, u32[]{:S(2)}) collective-permute-start(bf16[272,128]{1,0:T(8,128)(2,1)S(1)} %get-tuple-element.43), channel_id=1, source_target_pairs={{0,4},{1,5},{2,6},{3,7},{4,0},{5,1},{6,2},{7,3},{8,12},{9,13},{10,... | collective-permute-start | bytes 208904 | tf_op jit(solution)/shard_map/ppermute | solution.py:17
  53.5 5.5 %collective-permute-start.31 = (bf16[272,128]{1,0:T(8,128)(2,1)S(1)}, bf16[272,128]{1,0:T(8,128)(2,1)S(1)}, u32[]{:S(2)}, u32[]{:S(2)}) collective-permute-start(bf16[272,128]{1,0:T(8,128)(2,1)S(1)} %get-tuple-element.44), channel_id=1, source_target_pairs={{0,2},{1,3},{2,0},{3,1},{4,6},{5,7},{6,4},{7,5},{8,10},{9,11},{10,... | collective-permute-start | bytes 208904 | tf_op jit(solution)/shard_map/ppermute | solution.py:17

commit v17 on v16

--- a/solution.py
+++ b/solution.py
@@ -401,46 +401,49 @@
     )(*blocks)
 
 
+def sum_part(n, acc_ref, received_ref, chip, row):
+    part = acc_ref[jnp.bitwise_xor(lax.axis_index("op"), 2 * chip)]
+    return part + received_ref[row * 256 : (row + 1) * 256, :].astype(jnp.float32)
+
+
 def far_kernel(n, acc_ref, own_ref, received_ref, total_ref, *sends):
     far, near = n // 2 - near_chips(n), near_chips(n)
     total = jnp.concatenate([own_ref[...], received_ref[far * 256 :, :].astype(jnp.float32)[0:8]], axis=0)
     total_ref[...] = total
-    me = lax.axis_index("op")
-    for j in range(far):
-        value = acc_ref[jnp.bitwise_xor(me, 2 * (near + j))] + received_ref[j * 256 : (j + 1) * 256, :].astype(
-            jnp.float32
-        )
-        sends[j][0:256, :] = value.astype(jnp.bfloat16)
-        sends[j][256:, :] = total.astype(jnp.bfloat16)
+    for row, ref in zip(range(far - len(sends), far), sends):
+        ref[0:256, :] = sum_part(n, acc_ref, received_ref, near + row, row).astype(jnp.bfloat16)
+        ref[256:, :] = total.astype(jnp.bfloat16)
 
 
 def add_far(n, acc, own, received):
     return pl.pallas_call(
         functools.partial(far_kernel, n),
         out_shape=(jax.ShapeDtypeStruct((16, 128), jnp.float32),)
-        + (jax.ShapeDtypeStruct((256 + TAIL, 128), jnp.bfloat16),) * (n // 2 - near_chips(n)),
+        + (jax.ShapeDtypeStruct((256 + TAIL, 128), jnp.bfloat16),) * (near_chips(n) // 2),
         compiler_params=pltpu.CompilerParams(vmem_limit_bytes=16 * MIB),
     )(acc, own, received)
 
 
-def near_kernel(n, acc_ref, total_ref, received_ref, mine_ref, *sends):
-    me = lax.axis_index("op")
-    for j in range(near_chips(n)):
-        value = acc_ref[jnp.bitwise_xor(me, 2 * j)] + received_ref[j * 256 : (j + 1) * 256, :].astype(jnp.float32)
-        if j == 0:
-            mine_ref[...] = value
+def near_kernel(n, acc_ref, total_ref, far_ref, near_ref, mine_ref, *sends):
+    near = near_chips(n)
+    mine_ref[...] = sum_part(n, acc_ref, near_ref, 0, 0)
+    for index, ref in enumerate(sends):
+        if index < near - 1:
+            value = sum_part(n, acc_ref, near_ref, index + 1, index + 1)
         else:
-            sends[j - 1][0:256, :] = value.astype(jnp.bfloat16)
-            sends[j - 1][256:, :] = total_ref[...].astype(jnp.bfloat16)
-
-
-def add_near(n, acc, total, received):
+            value = sum_part(n, acc_ref, far_ref, index + 1, index + 1 - near)
+        ref[0:256, :] = value.astype(jnp.bfloat16)
+        ref[256:, :] = total_ref[...].astype(jnp.bfloat16)
+
+
+def add_near(n, acc, total, far, near):
+    messages = near_chips(n) - 1 + near_chips(n) // 2
     return pl.pallas_call(
         functools.partial(near_kernel, n),
         out_shape=(jax.ShapeDtypeStruct((256, 128), jnp.float32),)
-        + (jax.ShapeDtypeStruct((256 + TAIL, 128), jnp.bfloat16),) * (near_chips(n) - 1),
+        + (jax.ShapeDtypeStruct((256 + TAIL, 128), jnp.bfloat16),) * messages,
         compiler_params=pltpu.CompilerParams(vmem_limit_bytes=16 * MIB),
-    )(acc, total, received)
+    )(acc, total, far, near)
 
 
 def last_kernel(mine_ref, total_ref, *refs):
@@ -482,10 +485,10 @@
     correlation = correlate(arrays)
     far, near = exchange(far, n, 1), exchange(near, n, 1)
     total, *messages = add_far(n, acc, own, far)
-    first = near_chips(n)
-    received = [exchange(messages[j], n, 2 * (first + j)) for j in reversed(range(len(messages)))]
-    mine, *messages = add_near(n, acc, total, near)
-    received += [exchange(messages[j - 1], n, 2 * j) for j in reversed(range(1, first))]
+    last = n // 2 - len(messages)
+    received = [exchange(value, n, 2 * j) for j, value in reversed(list(enumerate(messages, last)))]
+    mine, *messages = add_near(n, acc, total, far, near)
+    received += [exchange(value, n, 2 * j) for j, value in enumerate(messages, 1)]
     product, projected = add_all(mine, total, received)
     return product, correlation, projected
 

time: 59.9 us -> 61.4 us (1.025)
  starting transfers between devices: 32.6 us -> 33.8 us
    ppermute x20, starting transfers between devices: 12.2 us -> 13.4 us  [exchange(): return lax.ppermute(value, 'op', [(i, i ^ mask) for i in range(n)])]
  transfers between devices with their start and end apart: 32 -> 32, of which waited for: 8 -> 8; matrix products, arithmetic and copies ran while one was open for 1% -> 1% of each run, Pallas kernels for 8% -> 7%
where the time goes in v17:
time: 61.4 us; the launch traced here: 61.1 us
  starting transfers between devices  33.8 us (55%)
  Pallas kernels  18.4 us (30%)
  waiting for transfers between devices  6.63 us (11%)
  other arithmetic  0.85 us (1%)
  between operations  0.75 us (1%)
  local copies, waits for them, and re-layouts  0.69 us (1%)
    ppermute x12, starting transfers between devices, ring_step(): return lax.ppermute(value, 'op', pairs)  20.4 us
    ppermute x20, starting transfers between devices, exchange(): return lax.ppermute(value, 'op', [(i, i ^ mask) for i in range(n)])  13.4 us
    pallas_call x1, Pallas kernels, run_tasks(): pl.pallas_call(functools.partial(tasks_kernel, n, kinds), out_shape=(jax....  13.2 us
    ppermute x20, waiting for transfers between devices, exchange(): return lax.ppermute(value, 'op', [(i, i ^ mask) for i in range(n)])  5.85 us
    pallas_call x1, Pallas kernels, make_plan(): pl.pallas_call(functools.partial(stage_kernel, n, terms), in_specs=[hbm,...  3.4 us
  transfers between devices with their start and end apart: 32, of which 8 were waited for; matrix products, arithmetic and copies ran while one was open for 1% of the time, Pallas kernels for 7%

profile of v17, /device:TPU:0, one launch (start us, length us, event | category | flops | bytes accessed | tf_op | source)
XLA Modules:
  0.0 61.1 jit_solution(12403478866129609866)
XLA Ops:
  0.6 0.5 collective-permute-start
  1.2 0.1 collective-permute-start.1
  1.2 3.0 %collective-permute-start.3 = (bf16[4,128,128]{2,1,0:T(8,128)(2,1)}, bf16[4,128,128]{2,1,0:T(8,128)(2,1)S(1)}, u32[]{:S(2)}, u32[]{:S(2)}) collective-permute-start(bf16[4,128,128]{2,1,0:T(8,128)(2,1)} %refs_1_.1), channel_id=1, source_target_pairs={{0,4},{1,3},{4,8},{5,1},{8,12},{9,5},{12,14},{13,9},{14,10},{15,13... | collective-permute-start | bytes 393224 | tf_op jit(solution)/shard_map/ppermute | solution.py:31
  4.2 0.0 collective-permute-done
  4.2 0.9 %pad_maximum_fusion.refs_0_ = bf16[4,128,128]{2,1,0:T(8,128)(2,1)S(1)} fusion(bf16[2,128,128]{2,1,0:T(8,128)(2,1)S(1)} %collective-permute-done, bf16[2,128,128]{2,1,0:T(8,128)(2,1)} %bitcast.4), kind=kLoop, calls=%fused_computation | loop fusion | flops 65536 | bytes 262144 | tf_op jit(solution)/shard_map/concatenate | solution.py:475
  5.1 1.6 %collective-permute-start.2 = (bf16[4,128,128]{2,1,0:T(8,128)(2,1)S(1)}, bf16[4,128,128]{2,1,0:T(8,128)(2,1)S(1)}, u32[]{:S(2)}, u32[]{:S(2)}) collective-permute-start(bf16[4,128,128]{2,1,0:T(8,128)(2,1)S(1)} %pad_maximum_fusion.refs_0_), channel_id=1, source_target_pairs={{0,4},{1,3},{4,8},{5,1},{8,12},{9,5},{12,14},{13,9},{14,10},{15,13... | collective-permute-start | bytes 393224 | tf_op jit(solution)/shard_map/ppermute | solution.py:31
  6.7 0.0 collective-permute-done.1.refs_2_
  6.7 1.6 %collective-permute-start.4 = (bf16[4,128,128]{2,1,0:T(8,128)(2,1)S(1)}, bf16[4,128,128]{2,1,0:T(8,128)(2,1)S(1)}, u32[]{:S(2)}, u32[]{:S(2)}) collective-permute-start(bf16[4,128,128]{2,1,0:T(8,128)(2,1)S(1)} %collective-permute-done.1.refs_2_), channel_id=1, source_target_pairs={{0,4},{1,3},{4,8},{5,1},{8,12},{9,5},{12,14},{13,9},{14,10},{15,13... | collective-permute-start | bytes 393224 | tf_op jit(solution)/shard_map/ppermute | solution.py:31
  8.3 0.0 collective-permute-done.3.refs_4_
  8.3 1.5 %collective-permute-start.9 = (bf16[4,128,128]{2,1,0:T(8,128)(2,1)S(1)}, bf16[4,128,128]{2,1,0:T(8,128)(2,1)S(1)}, u32[]{:S(2)}, u32[]{:S(2)}) collective-permute-start(bf16[4,128,128]{2,1,0:T(8,128)(2,1)S(1)} %collective-permute-done.3.refs_4_), channel_id=1, source_target_pairs={{0,4},{1,3},{4,8},{5,1},{8,12},{9,5},{12,14},{13,9},{14,10},{15,13... | collective-permute-start | bytes 393224 | tf_op jit(solution)/shard_map/ppermute | solution.py:31
  9.8 0.0 collective-permute-start.6
  9.8 0.3 collective-permute-done.2.refs_3_.refs_1_
  10.1 1.6 %collective-permute-start.8 = (bf16[4,128,128]{2,1,0:T(8,128)(2,1)S(1)}, bf16[4,128,128]{2,1,0:T(8,128)(2,1)S(1)}, u32[]{:S(2)}, u32[]{:S(2)}) collective-permute-start(bf16[4,128,128]{2,1,0:T(8,128)(2,1)S(1)} %collective-permute-done.2.refs_3_.refs_1_), channel_id=1, source_target_pairs={{0,4},{1,3},{4,8},{5,1},{8,12},{9,5},{12,14},{13,9},{14,10},{15,13... | collective-permute-start | bytes 393224 | tf_op jit(solution)/shard_map/ppermute | solution.py:31
  11.7 0.0 collective-permute-start.5
  11.7 0.0 collective-permute-done.4.refs_5_
  11.7 1.6 %collective-permute-start.10 = (bf16[4,128,128]{2,1,0:T(8,128)(2,1)S(1)}, bf16[4,128,128]{2,1,0:T(8,128)(2,1)S(1)}, u32[]{:S(2)}, u32[]{:S(2)}) collective-permute-start(bf16[4,128,128]{2,1,0:T(8,128)(2,1)S(1)} %collective-permute-done.4.refs_5_), channel_id=1, source_target_pairs={{0,4},{1,3},{4,8},{5,1},{8,12},{9,5},{12,14},{13,9},{14,10},{15,13... | collective-permute-start | bytes 393224 | tf_op jit(solution)/shard_map/ppermute | solution.py:31
  13.3 0.0 collective-permute-done.9.refs_10_
  13.3 0.0 collective-permute-start.7
  13.3 0.0 collective-permute-done.6.refs_7_
  13.3 1.6 %collective-permute-start.15 = (bf16[4,128,128]{2,1,0:T(8,128)(2,1)S(1)}, bf16[4,128,128]{2,1,0:T(8,128)(2,1)S(1)}, u32[]{:S(2)}, u32[]{:S(2)}) collective-permute-start(bf16[4,128,128]{2,1,0:T(8,128)(2,1)S(1)} %collective-permute-done.9.refs_10_), channel_id=1, source_target_pairs={{0,4},{1,3},{4,8},{5,1},{8,12},{9,5},{12,14},{13,9},{14,10},{15,13... | collective-permute-start | bytes 393224 | tf_op jit(solution)/shard_map/ppermute | solution.py:31
  14.9 0.2 collective-permute-done.8.refs_9_.refs_3_
  15.1 0.0 collective-permute-start.12
  15.1 0.0 collective-permute-done.5.refs_6_.refs_2_
  15.1 1.6 %collective-permute-start.14 = (bf16[4,128,128]{2,1,0:T(8,128)(2,1)S(1)}, bf16[4,128,128]{2,1,0:T(8,128)(2,1)S(1)}, u32[]{:S(2)}, u32[]{:S(2)}) collective-permute-start(bf16[4,128,128]{2,1,0:T(8,128)(2,1)S(1)} %collective-permute-done.8.refs_9_.refs_3_), channel_id=1, source_target_pairs={{0,4},{1,3},{4,8},{5,1},{8,12},{9,5},{12,14},{13,9},{14,10},{15,13... | collective-permute-start | bytes 393224 | tf_op jit(solution)/shard_map/ppermute | solution.py:31
  16.7 0.0 collective-permute-done.10.refs_11_
  16.7 0.0 collective-permute-start.11
  16.7 0.0 collective-permute-done.7.refs_8_
  16.7 1.6 %collective-permute-start.16 = (bf16[4,128,128]{2,1,0:T(8,128)(2,1)S(1)}, bf16[4,128,128]{2,1,0:T(8,128)(2,1)S(1)}, u32[]{:S(2)}, u32[]{:S(2)}) collective-permute-start(bf16[4,128,128]{2,1,0:T(8,128)(2,1)S(1)} %collective-permute-done.10.refs_11_), channel_id=1, source_target_pairs={{0,4},{1,3},{4,8},{5,1},{8,12},{9,5},{12,14},{13,9},{14,10},{15,13... | collective-permute-start | bytes 393224 | tf_op jit(solution)/shard_map/ppermute | solution.py:31
  18.3 0.0 collective-permute-done.15.refs_16_
  18.3 0.0 collective-permute-start.13
  18.3 0.0 collective-permute-done.12.refs_13_
  18.3 1.6 %collective-permute-start.21 = (bf16[4,128,128]{2,1,0:T(8,128)(2,1)S(1)}, bf16[4,128,128]{2,1,0:T(8,128)(2,1)S(1)}, u32[]{:S(2)}, u32[]{:S(2)}) collective-permute-start(bf16[4,128,128]{2,1,0:T(8,128)(2,1)S(1)} %collective-permute-done.15.refs_16_), channel_id=1, source_target_pairs={{0,4},{1,3},{4,8},{5,1},{8,12},{9,5},{12,14},{13,9},{14,10},{15,13... | collective-permute-start | bytes 393224 | tf_op jit(solution)/shard_map/ppermute | solution.py:31
  19.9 0.2 collective-permute-done.14.refs_15_.refs_5_
  20.1 0.0 collective-permute-start.18
  20.1 0.0 collective-permute-done.11.refs_12_.refs_4_
  20.1 1.6 %collective-permute-start.20 = (bf16[4,128,128]{2,1,0:T(8,128)(2,1)S(1)}, bf16[4,128,128]{2,1,0:T(8,128)(2,1)S(1)}, u32[]{:S(2)}, u32[]{:S(2)}) collective-permute-start(bf16[4,128,128]{2,1,0:T(8,128)(2,1)S(1)} %collective-permute-done.14.refs_15_.refs_5_), channel_id=1, source_target_pairs={{0,4},{1,3},{4,8},{5,1},{8,12},{9,5},{12,14},{13,9},{14,10},{15,13... | collective-permute-start | bytes 393224 | tf_op jit(solution)/shard_map/ppermute | solution.py:31
  21.6 0.1 collective-permute-done.16.refs_17_
  21.7 0.0 collective-permute-start.17
  21.7 0.0 collective-permute-done.13.refs_14_
  21.7 1.6 %collective-permute-start.22 = (bf16[4,128,128]{2,1,0:T(8,128)(2,1)S(1)}, bf16[4,128,128]{2,1,0:T(8,128)(2,1)S(1)}, u32[]{:S(2)}, u32[]{:S(2)}) collective-permute-start(bf16[4,128,128]{2,1,0:T(8,128)(2,1)S(1)} %collective-permute-done.16.refs_17_), channel_id=1, source_target_pairs={{0,4},{1,3},{4,8},{5,1},{8,12},{9,5},{12,14},{13,9},{14,10},{15,13... | collective-permute-start | bytes 393224 | tf_op jit(solution)/shard_map/ppermute | solution.py:31
  23.3 0.0 collective-permute-done.21.refs_22_
  23.3 0.0 collective-permute-start.19
  23.4 0.7 %copy-done = s32[256,4]{0,1:T(4,128)S(1)} copy-done((s32[256,4]{0,1:T(4,128)S(1)}, s32[256,4]{0,1:T(4,128)}, u32[]{:S(2)}) %copy-start) | copy-done | bytes 4120
  24.0 3.4 %shard_map.67 = (s32[6,512]{1,0:T(8,128)S(1)}, bf16[256,128,128]{2,1,0:T(8,128)(2,1)S(1)}) custom-call(s32[4,256]{1,0:T(4,128)S(1)} %bitcast.2, bf16[256,128,128]{2,1,0:T(8,128)(2,1)} %left_ref.1), custom_call_target="tpu_custom_call" | custom-call | tf_op jit(solution)/shard_map/pallas_call | solution.py:192
  27.4 0.0 collective-permute-done.18.refs_19_
  27.5 0.0 collective-permute-done.22.refs_23_
  27.5 13.2 %shard_map.68 = (bf16[1040,128]{1,0:T(8,128)(2,1)S(1)}, bf16[1024,128]{1,0:T(8,128)(2,1)S(1)}, f32[17,256,128]{2,1,0:T(8,128)S(1)}, f32[8,128]{1,0:T(8,128)S(1)}) custom-call(s32[6,512]{1,0:T(8,128)S(1)} %get-tuple-element.29.plan_ref, bf16[256,128,128]{2,1,0:T(8,128)(2,1)S(1)} %get-tuple-element.30.left_ref, ...), custom_call_target="tpu_custom_call" | custom-call | flops 4294967296 | bytes 15588608 | tf_op jit(solution)/shard_map/pallas_call | solution.py:361
  40.7 0.6 collective-permute-start.23
  41.3 0.1 collective-permute-start.24
  41.4 1.1 %collective-permute-done.23.received_ref.far_ref = bf16[1040,128]{1,0:T(8,128)(2,1)S(1)} collective-permute-done((bf16[1040,128]{1,0:T(8,128)(2,1)S(1)}, bf16[1040,128]{1,0:T(8,128)(2,1)S(1)}, u32[]{:S(2)}, u32[]{:S(2)}) %collective-permute-start.23) | collective-permute-done | bytes 266272 | tf_op jit(solution)/shard_map/ppermute | solution.py:17
  42.5 4.0 %collective-permute-start.25 = (bf16[272,128]{1,0:T(8,128)(2,1)S(1)}, bf16[272,128]{1,0:T(8,128)(2,1)S(1)}, u32[]{:S(2)}, u32[]{:S(2)}) collective-permute-start(bf16[272,128]{1,0:T(8,128)(2,1)S(1)} %get-tuple-element.38), channel_id=1, source_target_pairs={{0,14},{1,15},{2,12},{3,13},{4,10},{5,11},{6,8},{7,9},{8,6},{9,7},... | collective-permute-start | bytes 208904 | tf_op jit(solution)/shard_map/ppermute | solution.py:17
  46.5 0.4 collective-permute-start.26
  46.9 0.1 shard_map.70
  47.0 1.0 %collective-permute-start.27 = (bf16[272,128]{1,0:T(8,128)(2,1)S(1)}, bf16[272,128]{1,0:T(8,128)(2,1)S(1)}, u32[]{:S(2)}, u32[]{:S(2)}) collective-permute-start(bf16[272,128]{1,0:T(8,128)(2,1)S(1)} %get-tuple-element.40), channel_id=1, source_target_pairs={{0,2},{1,3},{2,0},{3,1},{4,6},{5,7},{6,4},{7,5},{8,10},{9,11},{10,... | collective-permute-start | bytes 208904 | tf_op jit(solution)/shard_map/ppermute | solution.py:17
  48.0 0.0 collective-permute-start.28
  48.0 2.5 %collective-permute-start.29 = (bf16[272,128]{1,0:T(8,128)(2,1)S(1)}, bf16[272,128]{1,0:T(8,128)(2,1)S(1)}, u32[]{:S(2)}, u32[]{:S(2)}) collective-permute-start(bf16[272,128]{1,0:T(8,128)(2,1)S(1)} %get-tuple-element.42), channel_id=1, source_target_pairs={{0,6},{1,7},{2,4},{3,5},{4,2},{5,3},{6,0},{7,1},{8,14},{9,15},{10,... | collective-permute-start | bytes 208904 | tf_op jit(solution)/shard_map/ppermute | solution.py:17
  50.5 0.0 collective-permute-done.25.refs_0_
  50.5 3.0 %collective-permute-start.30 = (bf16[272,128]{1,0:T(8,128)(2,1)S(1)}, bf16[272,128]{1,0:T(8,128)(2,1)S(1)}, u32[]{:S(2)}, u32[]{:S(2)}) collective-permute-start(bf16[272,128]{1,0:T(8,128)(2,1)S(1)} %get-tuple-element.43), channel_id=1, source_target_pairs={{0,8},{1,9},{2,10},{3,11},{4,12},{5,13},{6,14},{7,15},{8,0},{9,1},... | collective-permute-start | bytes 208904 | tf_op jit(solution)/shard_map/ppermute | solution.py:17
  53.5 1.2 %collective-permute-start.31 = (bf16[272,128]{1,0:T(8,128)(2,1)S(1)}, bf16[272,128]{1,0:T(8,128)(2,1)S(1)}, u32[]{:S(2)}, u32[]{:S(2)}) collective-permute-start(bf16[272,128]{1,0:T(8,128)(2,1)S(1)} %get-tuple-element.44), channel_id=1, source_target_pairs={{0,10},{1,11},{2,8},{3,9},{4,14},{5,15},{6,12},{7,13},{8,2},{9,3},... | collective-permute-start | bytes 208904 | tf_op jit(solution)/shard_map/ppermute | solution.py:17
  54.7 1.0 %shard_map.72 = f32[2,2]{1,0:T(2,128)} custom-call(bf16[4,128,128]{2,1,0:T(8,128)(2,1)S(1)} %pad_maximum_fusion.refs_0_, bf16[4,128,128]{2,1,0:T(8,128)(2,1)S(1)} %collective-permute-done.2.refs_3_.refs_1_, bf16[4,128,128]{2,1,0:T(8,128)(2,1)S(1)} %collective-permute-done.5.refs_6_.refs_2_, bf16[4,128,128]{2,1,0:T(8,128)(2,1)S(1)} %collective-permute-done.8.refs_9_.refs_3_, ...), custom_call_target="tpu_custom_call" | custom-call | tf_op jit(solution)/shard_map/pallas_call | solution.py:397
  55.7 0.2 collective-permute-done.29.refs_4_
  55.9 2.5 %collective-permute-done.30.refs_5_ = bf16[272,128]{1,0:T(8,128)(2,1)S(1)} collective-permute-done((bf16[272,128]{1,0:T(8,128)(2,1)S(1)}, bf16[272,128]{1,0:T(8,128)(2,1)S(1)}, u32[]{:S(2)}, u32[]{:S(2)}) %collective-permute-start.30) | collective-permute-done | bytes 69664 | tf_op jit(solution)/shard_map/ppermute | solution.py:17
  58.4 1.9 %collective-permute-done.31.refs_6_ = bf16[272,128]{1,0:T(8,128)(2,1)S(1)} collective-permute-done((bf16[272,128]{1,0:T(8,128)(2,1)S(1)}, bf16[272,128]{1,0:T(8,128)(2,1)S(1)}, u32[]{:S(2)}, u32[]{:S(2)}) %collective-permute-start.31) | collective-permute-done | bytes 69664 | tf_op jit(solution)/shard_map/ppermute | solution.py:17
  60.4 0.7 %shard_map.71 = (f32[1,2,128,128]{3,2,1,0:T(8,128)}, f32[2,2]{1,0:T(2,128)}) custom-call(f32[256,128]{1,0:T(8,128)S(1)} %get-tuple-element.37.mine_ref, f32[16,128]{1,0:T(8,128)S(1)} %get-tuple-element.35.total_ref, bf16[272,128]{1,0:T(8,128)(2,1)S(1)} %collective-permute-done.25.refs_0_, bf16[272,128]{1,0:T(8,128)(2,1)S(1)} %collective-permute-done.26.refs_1_, ...), custom_call_target="tpu_custom_call" | custom-call | tf_op jit(solution)/shard_map/pallas_call | solution.py:462
  (11 shorter events, 0.1 us)
Async XLA Ops:
  0.6 26.9 %copy-start.1 = (bf16[4,128,128]{2,1,0:T(8,128)(2,1)S(1)}, bf16[4,128,128]{2,1,0:T(8,128)(2,1)}, u32[]{:S(2)}) copy-start(bf16[4,128,128]{2,1,0:T(8,128)(2,1)} %refs_1_.1) | copy-start | bytes 393220
  0.6 3.6 %collective-permute-start = (bf16[2,128,128]{2,1,0:T(8,128)(2,1)}, bf16[2,128,128]{2,1,0:T(8,128)(2,1)S(1)}, u32[]{:S(2)}, u32[]{:S(2)}) collective-permute-start(bf16[2,128,128]{2,1,0:T(8,128)(2,1)} %bitcast.3), channel_id=1, source_target_pairs={{0,1},{1,0},{2,3},{3,2},{4,5},{5,4},{6,7},{7,6},{8,9},{9,8},{10,11... | collective-permute-start | bytes 196616 | tf_op jit(solution)/shard_map/ppermute | solution.py:17
  1.2 5.6 %collective-permute-start.1 = (bf16[4,128,128]{2,1,0:T(8,128)(2,1)}, bf16[4,128,128]{2,1,0:T(8,128)(2,1)S(1)}, u32[]{:S(2)}, u32[]{:S(2)}) collective-permute-start(bf16[4,128,128]{2,1,0:T(8,128)(2,1)} %refs_1_.1), channel_id=1, source_target_pairs={{0,1},{1,0},{2,3},{3,2},{4,5},{5,4},{6,7},{7,6},{8,9},{9,8},{10,11... | collective-permute-start | bytes 393224 | tf_op jit(solution)/shard_map/ppermute | solution.py:17
  1.2 7.1 %collective-permute-start.3 = (bf16[4,128,128]{2,1,0:T(8,128)(2,1)}, bf16[4,128,128]{2,1,0:T(8,128)(2,1)S(1)}, u32[]{:S(2)}, u32[]{:S(2)}) collective-permute-start(bf16[4,128,128]{2,1,0:T(8,128)(2,1)} %refs_1_.1), channel_id=1, source_target_pairs={{0,4},{1,3},{4,8},{5,1},{8,12},{9,5},{12,14},{13,9},{14,10},{15,13... | collective-permute-start | bytes 393224 | tf_op jit(solution)/shard_map/ppermute | solution.py:31
  5.1 5.0 %collective-permute-start.2 = (bf16[4,128,128]{2,1,0:T(8,128)(2,1)S(1)}, bf16[4,128,128]{2,1,0:T(8,128)(2,1)S(1)}, u32[]{:S(2)}, u32[]{:S(2)}) collective-permute-start(bf16[4,128,128]{2,1,0:T(8,128)(2,1)S(1)} %pad_maximum_fusion.refs_0_), channel_id=1, source_target_pairs={{0,4},{1,3},{4,8},{5,1},{8,12},{9,5},{12,14},{13,9},{14,10},{15,13... | collective-permute-start | bytes 393224 | tf_op jit(solution)/shard_map/ppermute | solution.py:31
  6.7 5.0 %collective-permute-start.4 = (bf16[4,128,128]{2,1,0:T(8,128)(2,1)S(1)}, bf16[4,128,128]{2,1,0:T(8,128)(2,1)S(1)}, u32[]{:S(2)}, u32[]{:S(2)}) collective-permute-start(bf16[4,128,128]{2,1,0:T(8,128)(2,1)S(1)} %collective-permute-done.1.refs_2_), channel_id=1, source_target_pairs={{0,4},{1,3},{4,8},{5,1},{8,12},{9,5},{12,14},{13,9},{14,10},{15,13... | collective-permute-start | bytes 393224 | tf_op jit(solution)/shard_map/ppermute | solution.py:31
  8.3 5.0 %collective-permute-start.9 = (bf16[4,128,128]{2,1,0:T(8,128)(2,1)S(1)}, bf16[4,128,128]{2,1,0:T(8,128)(2,1)S(1)}, u32[]{:S(2)}, u32[]{:S(2)}) collective-permute-start(bf16[4,128,128]{2,1,0:T(8,128)(2,1)S(1)} %collective-permute-done.3.refs_4_), channel_id=1, source_target_pairs={{0,4},{1,3},{4,8},{5,1},{8,12},{9,5},{12,14},{13,9},{14,10},{15,13... | collective-permute-start | bytes 393224 | tf_op jit(solution)/shard_map/ppermute | solution.py:31
  9.8 3.5 %collective-permute-start.6 = (bf16[4,128,128]{2,1,0:T(8,128)(2,1)S(1)}, bf16[4,128,128]{2,1,0:T(8,128)(2,1)S(1)}, u32[]{:S(2)}, u32[]{:S(2)}) collective-permute-start(bf16[4,128,128]{2,1,0:T(8,128)(2,1)S(1)} %collective-permute-done.3.refs_4_), channel_id=1, source_target_pairs={{0,1},{1,0},{2,3},{3,2},{4,5},{5,4},{6,7},{7,6},{8,9},{9,8},{10,11... | collective-permute-start | bytes 393224 | tf_op jit(solution)/shard_map/ppermute | solution.py:17
  10.1 5.0 %collective-permute-start.8 = (bf16[4,128,128]{2,1,0:T(8,128)(2,1)S(1)}, bf16[4,128,128]{2,1,0:T(8,128)(2,1)S(1)}, u32[]{:S(2)}, u32[]{:S(2)}) collective-permute-start(bf16[4,128,128]{2,1,0:T(8,128)(2,1)S(1)} %collective-permute-done.2.refs_3_.refs_1_), channel_id=1, source_target_pairs={{0,4},{1,3},{4,8},{5,1},{8,12},{9,5},{12,14},{13,9},{14,10},{15,13... | collective-permute-start | bytes 393224 | tf_op jit(solution)/shard_map/ppermute | solution.py:31
  11.7 3.4 %collective-permute-start.5 = (bf16[4,128,128]{2,1,0:T(8,128)(2,1)S(1)}, bf16[4,128,128]{2,1,0:T(8,128)(2,1)S(1)}, u32[]{:S(2)}, u32[]{:S(2)}) collective-permute-start(bf16[4,128,128]{2,1,0:T(8,128)(2,1)S(1)} %collective-permute-done.2.refs_3_.refs_1_), channel_id=1, source_target_pairs={{0,1},{1,0},{2,3},{3,2},{4,5},{5,4},{6,7},{7,6},{8,9},{9,8},{10,11... | collective-permute-start | bytes 393224 | tf_op jit(solution)/shard_map/ppermute | solution.py:17
  11.7 5.0 %collective-permute-start.10 = (bf16[4,128,128]{2,1,0:T(8,128)(2,1)S(1)}, bf16[4,128,128]{2,1,0:T(8,128)(2,1)S(1)}, u32[]{:S(2)}, u32[]{:S(2)}) collective-permute-start(bf16[4,128,128]{2,1,0:T(8,128)(2,1)S(1)} %collective-permute-done.4.refs_5_), channel_id=1, source_target_pairs={{0,4},{1,3},{4,8},{5,1},{8,12},{9,5},{12,14},{13,9},{14,10},{15,13... | collective-permute-start | bytes 393224 | tf_op jit(solution)/shard_map/ppermute | solution.py:31
  13.3 3.4 %collective-permute-start.7 = (bf16[4,128,128]{2,1,0:T(8,128)(2,1)S(1)}, bf16[4,128,128]{2,1,0:T(8,128)(2,1)S(1)}, u32[]{:S(2)}, u32[]{:S(2)}) collective-permute-start(bf16[4,128,128]{2,1,0:T(8,128)(2,1)S(1)} %collective-permute-done.4.refs_5_), channel_id=1, source_target_pairs={{0,1},{1,0},{2,3},{3,2},{4,5},{5,4},{6,7},{7,6},{8,9},{9,8},{10,11... | collective-permute-start | bytes 393224 | tf_op jit(solution)/shard_map/ppermute | solution.py:17
  13.3 5.0 %collective-permute-start.15 = (bf16[4,128,128]{2,1,0:T(8,128)(2,1)S(1)}, bf16[4,128,128]{2,1,0:T(8,128)(2,1)S(1)}, u32[]{:S(2)}, u32[]{:S(2)}) collective-permute-start(bf16[4,128,128]{2,1,0:T(8,128)(2,1)S(1)} %collective-permute-done.9.refs_10_), channel_id=1, source_target_pairs={{0,4},{1,3},{4,8},{5,1},{8,12},{9,5},{12,14},{13,9},{14,10},{15,13... | collective-permute-start | bytes 393224 | tf_op jit(solution)/shard_map/ppermute | solution.py:31
  15.1 3.2 %collective-permute-start.12 = (bf16[4,128,128]{2,1,0:T(8,128)(2,1)S(1)}, bf16[4,128,128]{2,1,0:T(8,128)(2,1)S(1)}, u32[]{:S(2)}, u32[]{:S(2)}) collective-permute-start(bf16[4,128,128]{2,1,0:T(8,128)(2,1)S(1)} %collective-permute-done.9.refs_10_), channel_id=1, source_target_pairs={{0,1},{1,0},{2,3},{3,2},{4,5},{5,4},{6,7},{7,6},{8,9},{9,8},{10,11... | collective-permute-start | bytes 393224 | tf_op jit(solution)/shard_map/ppermute | solution.py:17
  15.1 5.0 %collective-permute-start.14 = (bf16[4,128,128]{2,1,0:T(8,128)(2,1)S(1)}, bf16[4,128,128]{2,1,0:T(8,128)(2,1)S(1)}, u32[]{:S(2)}, u32[]{:S(2)}) collective-permute-start(bf16[4,128,128]{2,1,0:T(8,128)(2,1)S(1)} %collective-permute-done.8.refs_9_.refs_3_), channel_id=1, source_target_pairs={{0,4},{1,3},{4,8},{5,1},{8,12},{9,5},{12,14},{13,9},{14,10},{15,13... | collective-permute-start | bytes 393224 | tf_op jit(solution)/shard_map/ppermute | solution.py:31
  16.7 3.4 %collective-permute-start.11 = (bf16[4,128,128]{2,1,0:T(8,128)(2,1)S(1)}, bf16[4,128,128]{2,1,0:T(8,128)(2,1)S(1)}, u32[]{:S(2)}, u32[]{:S(2)}) collective-permute-start(bf16[4,128,128]{2,1,0:T(8,128)(2,1)S(1)} %collective-permute-done.8.refs_9_.refs_3_), channel_id=1, source_target_pairs={{0,1},{1,0},{2,3},{3,2},{4,5},{5,4},{6,7},{7,6},{8,9},{9,8},{10,11... | collective-permute-start | bytes 393224 | tf_op jit(solution)/shard_map/ppermute | solution.py:17
  16.7 5.0 %collective-permute-start.16 = (bf16[4,128,128]{2,1,0:T(8,128)(2,1)S(1)}, bf16[4,128,128]{2,1,0:T(8,128)(2,1)S(1)}, u32[]{:S(2)}, u32[]{:S(2)}) collective-permute-start(bf16[4,128,128]{2,1,0:T(8,128)(2,1)S(1)} %collective-permute-done.10.refs_11_), channel_id=1, source_target_pairs={{0,4},{1,3},{4,8},{5,1},{8,12},{9,5},{12,14},{13,9},{14,10},{15,13... | collective-permute-start | bytes 393224 | tf_op jit(solution)/shard_map/ppermute | solution.py:31
  18.3 3.4 %collective-permute-start.13 = (bf16[4,128,128]{2,1,0:T(8,128)(2,1)S(1)}, bf16[4,128,128]{2,1,0:T(8,128)(2,1)S(1)}, u32[]{:S(2)}, u32[]{:S(2)}) collective-permute-start(bf16[4,128,128]{2,1,0:T(8,128)(2,1)S(1)} %collective-permute-done.10.refs_11_), channel_id=1, source_target_pairs={{0,1},{1,0},{2,3},{3,2},{4,5},{5,4},{6,7},{7,6},{8,9},{9,8},{10,11... | collective-permute-start | bytes 393224 | tf_op jit(solution)/shard_map/ppermute | solution.py:17
  18.3 5.0 %collective-permute-start.21 = (bf16[4,128,128]{2,1,0:T(8,128)(2,1)S(1)}, bf16[4,128,128]{2,1,0:T(8,128)(2,1)S(1)}, u32[]{:S(2)}, u32[]{:S(2)}) collective-permute-start(bf16[4,128,128]{2,1,0:T(8,128)(2,1)S(1)} %collective-permute-done.15.refs_16_), channel_id=1, source_target_pairs={{0,4},{1,3},{4,8},{5,1},{8,12},{9,5},{12,14},{13,9},{14,10},{15,13... | collective-permute-start | bytes 393224 | tf_op jit(solution)/shard_map/ppermute | solution.py:31
  20.1 7.4 %collective-permute-start.18 = (bf16[4,128,128]{2,1,0:T(8,128)(2,1)S(1)}, bf16[4,128,128]{2,1,0:T(8,128)(2,1)S(1)}, u32[]{:S(2)}, u32[]{:S(2)}) collective-permute-start(bf16[4,128,128]{2,1,0:T(8,128)(2,1)S(1)} %collective-permute-done.15.refs_16_), channel_id=1, source_target_pairs={{0,1},{1,0},{2,3},{3,2},{4,5},{5,4},{6,7},{7,6},{8,9},{9,8},{10,11... | collective-permute-start | bytes 393224 | tf_op jit(solution)/shard_map/ppermute | solution.py:17
  20.1 7.4 %collective-permute-start.20 = (bf16[4,128,128]{2,1,0:T(8,128)(2,1)S(1)}, bf16[4,128,128]{2,1,0:T(8,128)(2,1)S(1)}, u32[]{:S(2)}, u32[]{:S(2)}) collective-permute-start(bf16[4,128,128]{2,1,0:T(8,128)(2,1)S(1)} %collective-permute-done.14.refs_15_.refs_5_), channel_id=1, source_target_pairs={{0,4},{1,3},{4,8},{5,1},{8,12},{9,5},{12,14},{13,9},{14,10},{15,13... | collective-permute-start | bytes 393224 | tf_op jit(solution)/shard_map/ppermute | solution.py:31
  21.7 5.8 %collective-permute-start.17 = (bf16[4,128,128]{2,1,0:T(8,128)(2,1)S(1)}, bf16[4,128,128]{2,1,0:T(8,128)(2,1)S(1)}, u32[]{:S(2)}, u32[]{:S(2)}) collective-permute-start(bf16[4,128,128]{2,1,0:T(8,128)(2,1)S(1)} %collective-permute-done.14.refs_15_.refs_5_), channel_id=1, source_target_pairs={{0,1},{1,0},{2,3},{3,2},{4,5},{5,4},{6,7},{7,6},{8,9},{9,8},{10,11... | collective-permute-start | bytes 393224 | tf_op jit(solution)/shard_map/ppermute | solution.py:17
  21.7 5.8 %collective-permute-start.22 = (bf16[4,128,128]{2,1,0:T(8,128)(2,1)S(1)}, bf16[4,128,128]{2,1,0:T(8,128)(2,1)S(1)}, u32[]{:S(2)}, u32[]{:S(2)}) collective-permute-start(bf16[4,128,128]{2,1,0:T(8,128)(2,1)S(1)} %collective-permute-done.16.refs_17_), channel_id=1, source_target_pairs={{0,4},{1,3},{4,8},{5,1},{8,12},{9,5},{12,14},{13,9},{14,10},{15,13... | collective-permute-start | bytes 393224 | tf_op jit(solution)/shard_map/ppermute | solution.py:31
  23.3 4.1 %collective-permute-start.19 = (bf16[4,128,128]{2,1,0:T(8,128)(2,1)S(1)}, bf16[4,128,128]{2,1,0:T(8,128)(2,1)S(1)}, u32[]{:S(2)}, u32[]{:S(2)}) collective-permute-start(bf16[4,128,128]{2,1,0:T(8,128)(2,1)S(1)} %collective-permute-done.16.refs_17_), channel_id=1, source_target_pairs={{0,1},{1,0},{2,3},{3,2},{4,5},{5,4},{6,7},{7,6},{8,9},{9,8},{10,11... | collective-permute-start | bytes 393224 | tf_op jit(solution)/shard_map/ppermute | solution.py:17
  23.4 0.7 %copy-start = (s32[256,4]{0,1:T(4,128)S(1)}, s32[256,4]{0,1:T(4,128)}, u32[]{:S(2)}) copy-start(s32[256,4]{0,1:T(4,128)} %param.7) | copy-start | bytes 12292
  40.7 1.7 %collective-permute-start.23 = (bf16[1040,128]{1,0:T(8,128)(2,1)S(1)}, bf16[1040,128]{1,0:T(8,128)(2,1)S(1)}, u32[]{:S(2)}, u32[]{:S(2)}) collective-permute-start(bf16[1040,128]{1,0:T(8,128)(2,1)S(1)} %get-tuple-element.34), channel_id=1, source_target_pairs={{0,1},{1,0},{2,3},{3,2},{4,5},{5,4},{6,7},{7,6},{8,9},{9,8},{10,11... | collective-permute-start | bytes 798728 | tf_op jit(solution)/shard_map/ppermute | solution.py:17
  41.3 5.6 %collective-permute-start.24 = (bf16[1024,128]{1,0:T(8,128)(2,1)S(1)}, bf16[1024,128]{1,0:T(8,128)(2,1)S(1)}, u32[]{:S(2)}, u32[]{:S(2)}) collective-permute-start(bf16[1024,128]{1,0:T(8,128)(2,1)S(1)} %get-tuple-element.36), channel_id=1, source_target_pairs={{0,1},{1,0},{2,3},{3,2},{4,5},{5,4},{6,7},{7,6},{8,9},{9,8},{10,11... | collective-permute-start | bytes 786440 | tf_op jit(solution)/shard_map/ppermute | solution.py:17
  42.5 8.1 %collective-permute-start.25 = (bf16[272,128]{1,0:T(8,128)(2,1)S(1)}, bf16[272,128]{1,0:T(8,128)(2,1)S(1)}, u32[]{:S(2)}, u32[]{:S(2)}) collective-permute-start(bf16[272,128]{1,0:T(8,128)(2,1)S(1)} %get-tuple-element.38), channel_id=1, source_target_pairs={{0,14},{1,15},{2,12},{3,13},{4,10},{5,11},{6,8},{7,9},{8,6},{9,7},... | collective-permute-start | bytes 208904 | tf_op jit(solution)/shard_map/ppermute | solution.py:17
  46.5 7.0 %collective-permute-start.26 = (bf16[272,128]{1,0:T(8,128)(2,1)S(1)}, bf16[272,128]{1,0:T(8,128)(2,1)S(1)}, u32[]{:S(2)}, u32[]{:S(2)}) collective-permute-start(bf16[272,128]{1,0:T(8,128)(2,1)S(1)} %get-tuple-element.39), channel_id=1, source_target_pairs={{0,12},{1,13},{2,14},{3,15},{4,8},{5,9},{6,10},{7,11},{8,4},{9,5},... | collective-permute-start | bytes 208904 | tf_op jit(solution)/shard_map/ppermute | solution.py:17
  47.0 8.7 %collective-permute-start.27 = (bf16[272,128]{1,0:T(8,128)(2,1)S(1)}, bf16[272,128]{1,0:T(8,128)(2,1)S(1)}, u32[]{:S(2)}, u32[]{:S(2)}) collective-permute-start(bf16[272,128]{1,0:T(8,128)(2,1)S(1)} %get-tuple-element.40), channel_id=1, source_target_pairs={{0,2},{1,3},{2,0},{3,1},{4,6},{5,7},{6,4},{7,5},{8,10},{9,11},{10,... | collective-permute-start | bytes 208904 | tf_op jit(solution)/shard_map/ppermute | solution.py:17
  48.0 7.7 %collective-permute-start.28 = (bf16[272,128]{1,0:T(8,128)(2,1)S(1)}, bf16[272,128]{1,0:T(8,128)(2,1)S(1)}, u32[]{:S(2)}, u32[]{:S(2)}) collective-permute-start(bf16[272,128]{1,0:T(8,128)(2,1)S(1)} %get-tuple-element.41), channel_id=1, source_target_pairs={{0,4},{1,5},{2,6},{3,7},{4,0},{5,1},{6,2},{7,3},{8,12},{9,13},{10,... | collective-permute-start | bytes 208904 | tf_op jit(solution)/shard_map/ppermute | solution.py:17
  48.0 7.9 %collective-permute-start.29 = (bf16[272,128]{1,0:T(8,128)(2,1)S(1)}, bf16[272,128]{1,0:T(8,128)(2,1)S(1)}, u32[]{:S(2)}, u32[]{:S(2)}) collective-permute-start(bf16[272,128]{1,0:T(8,128)(2,1)S(1)} %get-tuple-element.42), channel_id=1, source_target_pairs={{0,6},{1,7},{2,4},{3,5},{4,2},{5,3},{6,0},{7,1},{8,14},{9,15},{10,... | collective-permute-start | bytes 208904 | tf_op jit(solution)/shard_map/ppermute | solution.py:17
  50.5 7.9 %collective-permute-start.30 = (bf16[272,128]{1,0:T(8,128)(2,1)S(1)}, bf16[272,128]{1,0:T(8,128)(2,1)S(1)}, u32[]{:S(2)}, u32[]{:S(2)}) collective-permute-start(bf16[272,128]{1,0:T(8,128)(2,1)S(1)} %get-tuple-element.43), channel_id=1, source_target_pairs={{0,8},{1,9},{2,10},{3,11},{4,12},{5,13},{6,14},{7,15},{8,0},{9,1},... | collective-permute-start | bytes 208904 | tf_op jit(solution)/shard_map/ppermute | solution.py:17
  53.5 6.9 %collective-permute-start.31 = (bf16[272,128]{1,0:T(8,128)(2,1)S(1)}, bf16[272,128]{1,0:T(8,128)(2,1)S(1)}, u32[]{:S(2)}, u32[]{:S(2)}) collective-permute-start(bf16[272,128]{1,0:T(8,128)(2,1)S(1)} %get-tuple-element.44), channel_id=1, source_target_pairs={{0,10},{1,11},{2,8},{3,9},{4,14},{5,15},{6,12},{7,13},{8,2},{9,3},... | collective-permute-start | bytes 208904 | tf_op jit(solution)/shard_map/ppermute | solution.py:17

commit v18 on v16

--- a/solution.py
+++ b/solution.py
@@ -483,7 +483,7 @@
     far, near = exchange(far, n, 1), exchange(near, n, 1)
     total, *messages = add_far(n, acc, own, far)
     first = near_chips(n)
-    received = [exchange(messages[j], n, 2 * (first + j)) for j in reversed(range(len(messages)))]
+    received = [exchange(value, n, 2 * j) for j, value in enumerate(messages, first)]
     mine, *messages = add_near(n, acc, total, near)
     received += [exchange(messages[j - 1], n, 2 * j) for j in reversed(range(1, first))]
     product, projected = add_all(mine, total, received)

time: 59.9 us -> 60.7 us (1.013)
  starting transfers between devices: 32.6 us -> 34.4 us
  waiting for transfers between devices: 6.38 us -> 5.41 us
    ppermute x20, starting transfers between devices: 12.2 us -> 13.9 us  [exchange(): return lax.ppermute(value, 'op', [(i, i ^ mask) for i in range(n)])]
    ppermute x20, waiting for transfers between devices: 5.6 us -> 4.64 us  [exchange(): return lax.ppermute(value, 'op', [(i, i ^ mask) for i in range(n)])]
  transfers between devices with their start and end apart: 32 -> 32, of which waited for: 8 -> 7; matrix products, arithmetic and copies ran while one was open for 1% -> 1% of each run, Pallas kernels for 8% -> 7%
where the time goes in v18:
time: 60.7 us; the launch traced here: 60.5 us
  starting transfers between devices  34.4 us (57%)
  Pallas kernels  18.4 us (30%)
  waiting for transfers between devices  5.41 us (9%)
  other arithmetic  0.85 us (1%)
  between operations  0.76 us (1%)
  local copies, waits for them, and re-layouts  0.69 us (1%)
    ppermute x12, starting transfers between devices, ring_step(): return lax.ppermute(value, 'op', pairs)  20.4 us
    ppermute x20, starting transfers between devices, exchange(): return lax.ppermute(value, 'op', [(i, i ^ mask) for i in range(n)])  13.9 us
    pallas_call x1, Pallas kernels, run_tasks(): pl.pallas_call(functools.partial(tasks_kernel, n, kinds), out_shape=(jax....  13.2 us
    ppermute x20, waiting for transfers between devices, exchange(): return lax.ppermute(value, 'op', [(i, i ^ mask) for i in range(n)])  4.64 us
    pallas_call x1, Pallas kernels, make_plan(): pl.pallas_call(functools.partial(stage_kernel, n, terms), in_specs=[hbm,...  3.4 us
  transfers between devices with their start and end apart: 32, of which 7 were waited for; matrix products, arithmetic and copies ran while one was open for 1% of the time, Pallas kernels for 7%

profile of v18, /device:TPU:0, one launch (start us, length us, event | category | flops | bytes accessed | tf_op | source)
XLA Modules:
  0.0 60.5 jit_solution(8537107874737783969)
XLA Ops:
  0.6 0.5 collective-permute-start
  1.2 0.1 collective-permute-start.1
  1.2 3.0 %collective-permute-start.3 = (bf16[4,128,128]{2,1,0:T(8,128)(2,1)}, bf16[4,128,128]{2,1,0:T(8,128)(2,1)S(1)}, u32[]{:S(2)}, u32[]{:S(2)}) collective-permute-start(bf16[4,128,128]{2,1,0:T(8,128)(2,1)} %refs_1_.1), channel_id=1, source_target_pairs={{0,4},{1,3},{4,8},{5,1},{8,12},{9,5},{12,14},{13,9},{14,10},{15,13... | collective-permute-start | bytes 393224 | tf_op jit(solution)/shard_map/ppermute | solution.py:31
  4.2 0.0 collective-permute-done
  4.2 0.9 %pad_maximum_fusion.refs_0_ = bf16[4,128,128]{2,1,0:T(8,128)(2,1)S(1)} fusion(bf16[2,128,128]{2,1,0:T(8,128)(2,1)S(1)} %collective-permute-done, bf16[2,128,128]{2,1,0:T(8,128)(2,1)} %bitcast.4), kind=kLoop, calls=%fused_computation | loop fusion | flops 65536 | bytes 262144 | tf_op jit(solution)/shard_map/concatenate | solution.py:472
  5.1 1.6 %collective-permute-start.2 = (bf16[4,128,128]{2,1,0:T(8,128)(2,1)S(1)}, bf16[4,128,128]{2,1,0:T(8,128)(2,1)S(1)}, u32[]{:S(2)}, u32[]{:S(2)}) collective-permute-start(bf16[4,128,128]{2,1,0:T(8,128)(2,1)S(1)} %pad_maximum_fusion.refs_0_), channel_id=1, source_target_pairs={{0,4},{1,3},{4,8},{5,1},{8,12},{9,5},{12,14},{13,9},{14,10},{15,13... | collective-permute-start | bytes 393224 | tf_op jit(solution)/shard_map/ppermute | solution.py:31
  6.7 0.0 collective-permute-done.1.refs_2_
  6.7 1.6 %collective-permute-start.4 = (bf16[4,128,128]{2,1,0:T(8,128)(2,1)S(1)}, bf16[4,128,128]{2,1,0:T(8,128)(2,1)S(1)}, u32[]{:S(2)}, u32[]{:S(2)}) collective-permute-start(bf16[4,128,128]{2,1,0:T(8,128)(2,1)S(1)} %collective-permute-done.1.refs_2_), channel_id=1, source_target_pairs={{0,4},{1,3},{4,8},{5,1},{8,12},{9,5},{12,14},{13,9},{14,10},{15,13... | collective-permute-start | bytes 393224 | tf_op jit(solution)/shard_map/ppermute | solution.py:31
  8.3 0.0 collective-permute-done.3.refs_4_
  8.3 1.5 %collective-permute-start.9 = (bf16[4,128,128]{2,1,0:T(8,128)(2,1)S(1)}, bf16[4,128,128]{2,1,0:T(8,128)(2,1)S(1)}, u32[]{:S(2)}, u32[]{:S(2)}) collective-permute-start(bf16[4,128,128]{2,1,0:T(8,128)(2,1)S(1)} %collective-permute-done.3.refs_4_), channel_id=1, source_target_pairs={{0,4},{1,3},{4,8},{5,1},{8,12},{9,5},{12,14},{13,9},{14,10},{15,13... | collective-permute-start | bytes 393224 | tf_op jit(solution)/shard_map/ppermute | solution.py:31
  9.8 0.0 collective-permute-start.6
  9.8 0.3 collective-permute-done.2.refs_3_.refs_1_
  10.1 1.6 %collective-permute-start.8 = (bf16[4,128,128]{2,1,0:T(8,128)(2,1)S(1)}, bf16[4,128,128]{2,1,0:T(8,128)(2,1)S(1)}, u32[]{:S(2)}, u32[]{:S(2)}) collective-permute-start(bf16[4,128,128]{2,1,0:T(8,128)(2,1)S(1)} %collective-permute-done.2.refs_3_.refs_1_), channel_id=1, source_target_pairs={{0,4},{1,3},{4,8},{5,1},{8,12},{9,5},{12,14},{13,9},{14,10},{15,13... | collective-permute-start | bytes 393224 | tf_op jit(solution)/shard_map/ppermute | solution.py:31
  11.7 0.0 collective-permute-start.5
  11.7 0.0 collective-permute-done.4.refs_5_
  11.7 1.6 %collective-permute-start.10 = (bf16[4,128,128]{2,1,0:T(8,128)(2,1)S(1)}, bf16[4,128,128]{2,1,0:T(8,128)(2,1)S(1)}, u32[]{:S(2)}, u32[]{:S(2)}) collective-permute-start(bf16[4,128,128]{2,1,0:T(8,128)(2,1)S(1)} %collective-permute-done.4.refs_5_), channel_id=1, source_target_pairs={{0,4},{1,3},{4,8},{5,1},{8,12},{9,5},{12,14},{13,9},{14,10},{15,13... | collective-permute-start | bytes 393224 | tf_op jit(solution)/shard_map/ppermute | solution.py:31
  13.3 0.0 collective-permute-done.9.refs_10_
  13.3 0.0 collective-permute-start.7
  13.3 0.0 collective-permute-done.6.refs_7_
  13.3 1.6 %collective-permute-start.15 = (bf16[4,128,128]{2,1,0:T(8,128)(2,1)S(1)}, bf16[4,128,128]{2,1,0:T(8,128)(2,1)S(1)}, u32[]{:S(2)}, u32[]{:S(2)}) collective-permute-start(bf16[4,128,128]{2,1,0:T(8,128)(2,1)S(1)} %collective-permute-done.9.refs_10_), channel_id=1, source_target_pairs={{0,4},{1,3},{4,8},{5,1},{8,12},{9,5},{12,14},{13,9},{14,10},{15,13... | collective-permute-start | bytes 393224 | tf_op jit(solution)/shard_map/ppermute | solution.py:31
  14.9 0.2 collective-permute-done.8.refs_9_.refs_3_
  15.1 0.0 collective-permute-start.12
  15.1 0.0 collective-permute-done.5.refs_6_.refs_2_
  15.1 1.6 %collective-permute-start.14 = (bf16[4,128,128]{2,1,0:T(8,128)(2,1)S(1)}, bf16[4,128,128]{2,1,0:T(8,128)(2,1)S(1)}, u32[]{:S(2)}, u32[]{:S(2)}) collective-permute-start(bf16[4,128,128]{2,1,0:T(8,128)(2,1)S(1)} %collective-permute-done.8.refs_9_.refs_3_), channel_id=1, source_target_pairs={{0,4},{1,3},{4,8},{5,1},{8,12},{9,5},{12,14},{13,9},{14,10},{15,13... | collective-permute-start | bytes 393224 | tf_op jit(solution)/shard_map/ppermute | solution.py:31
  16.7 0.0 collective-permute-done.10.refs_11_
  16.7 0.0 collective-permute-start.11
  16.7 0.0 collective-permute-done.7.refs_8_
  16.7 1.6 %collective-permute-start.16 = (bf16[4,128,128]{2,1,0:T(8,128)(2,1)S(1)}, bf16[4,128,128]{2,1,0:T(8,128)(2,1)S(1)}, u32[]{:S(2)}, u32[]{:S(2)}) collective-permute-start(bf16[4,128,128]{2,1,0:T(8,128)(2,1)S(1)} %collective-permute-done.10.refs_11_), channel_id=1, source_target_pairs={{0,4},{1,3},{4,8},{5,1},{8,12},{9,5},{12,14},{13,9},{14,10},{15,13... | collective-permute-start | bytes 393224 | tf_op jit(solution)/shard_map/ppermute | solution.py:31
  18.3 0.0 collective-permute-done.15.refs_16_
  18.3 0.0 collective-permute-start.13
  18.3 0.0 collective-permute-done.12.refs_13_
  18.3 1.6 %collective-permute-start.21 = (bf16[4,128,128]{2,1,0:T(8,128)(2,1)S(1)}, bf16[4,128,128]{2,1,0:T(8,128)(2,1)S(1)}, u32[]{:S(2)}, u32[]{:S(2)}) collective-permute-start(bf16[4,128,128]{2,1,0:T(8,128)(2,1)S(1)} %collective-permute-done.15.refs_16_), channel_id=1, source_target_pairs={{0,4},{1,3},{4,8},{5,1},{8,12},{9,5},{12,14},{13,9},{14,10},{15,13... | collective-permute-start | bytes 393224 | tf_op jit(solution)/shard_map/ppermute | solution.py:31
  19.9 0.2 collective-permute-done.14.refs_15_.refs_5_
  20.1 0.0 collective-permute-start.18
  20.1 0.0 collective-permute-done.11.refs_12_.refs_4_
  20.1 1.6 %collective-permute-start.20 = (bf16[4,128,128]{2,1,0:T(8,128)(2,1)S(1)}, bf16[4,128,128]{2,1,0:T(8,128)(2,1)S(1)}, u32[]{:S(2)}, u32[]{:S(2)}) collective-permute-start(bf16[4,128,128]{2,1,0:T(8,128)(2,1)S(1)} %collective-permute-done.14.refs_15_.refs_5_), channel_id=1, source_target_pairs={{0,4},{1,3},{4,8},{5,1},{8,12},{9,5},{12,14},{13,9},{14,10},{15,13... | collective-permute-start | bytes 393224 | tf_op jit(solution)/shard_map/ppermute | solution.py:31
  21.6 0.1 collective-permute-done.16.refs_17_
  21.7 0.0 collective-permute-start.17
  21.7 0.0 collective-permute-done.13.refs_14_
  21.7 1.6 %collective-permute-start.22 = (bf16[4,128,128]{2,1,0:T(8,128)(2,1)S(1)}, bf16[4,128,128]{2,1,0:T(8,128)(2,1)S(1)}, u32[]{:S(2)}, u32[]{:S(2)}) collective-permute-start(bf16[4,128,128]{2,1,0:T(8,128)(2,1)S(1)} %collective-permute-done.16.refs_17_), channel_id=1, source_target_pairs={{0,4},{1,3},{4,8},{5,1},{8,12},{9,5},{12,14},{13,9},{14,10},{15,13... | collective-permute-start | bytes 393224 | tf_op jit(solution)/shard_map/ppermute | solution.py:31
  23.3 0.0 collective-permute-done.21.refs_22_
  23.3 0.0 collective-permute-start.19
  23.4 0.7 %copy-done = s32[256,4]{0,1:T(4,128)S(1)} copy-done((s32[256,4]{0,1:T(4,128)S(1)}, s32[256,4]{0,1:T(4,128)}, u32[]{:S(2)}) %copy-start) | copy-done | bytes 4120
  24.0 3.4 %shard_map.67 = (s32[6,512]{1,0:T(8,128)S(1)}, bf16[256,128,128]{2,1,0:T(8,128)(2,1)S(1)}) custom-call(s32[4,256]{1,0:T(4,128)S(1)} %bitcast.2, bf16[256,128,128]{2,1,0:T(8,128)(2,1)} %left_ref.1), custom_call_target="tpu_custom_call" | custom-call | tf_op jit(solution)/shard_map/pallas_call | solution.py:192
  27.5 0.0 collective-permute-done.20.refs_21_.refs_7_
  27.5 0.0 collective-permute-done.17.refs_18_.refs_6_
  27.5 13.2 %shard_map.68 = (bf16[1040,128]{1,0:T(8,128)(2,1)S(1)}, bf16[1024,128]{1,0:T(8,128)(2,1)S(1)}, f32[17,256,128]{2,1,0:T(8,128)S(1)}, f32[8,128]{1,0:T(8,128)S(1)}) custom-call(s32[6,512]{1,0:T(8,128)S(1)} %get-tuple-element.29.plan_ref, bf16[256,128,128]{2,1,0:T(8,128)(2,1)S(1)} %get-tuple-element.30.left_ref, ...), custom_call_target="tpu_custom_call" | custom-call | flops 4294967296 | bytes 15588608 | tf_op jit(solution)/shard_map/pallas_call | solution.py:361
  40.7 0.6 collective-permute-start.23
  41.3 0.1 collective-permute-start.24
  41.4 1.1 %collective-permute-done.23.received_ref = bf16[1040,128]{1,0:T(8,128)(2,1)S(1)} collective-permute-done((bf16[1040,128]{1,0:T(8,128)(2,1)S(1)}, bf16[1040,128]{1,0:T(8,128)(2,1)S(1)}, u32[]{:S(2)}, u32[]{:S(2)}) %collective-permute-start.23) | collective-permute-done | bytes 266272 | tf_op jit(solution)/shard_map/ppermute | solution.py:17
  42.4 0.1 shard_map.69
  42.5 2.4 %collective-permute-start.25 = (bf16[272,128]{1,0:T(8,128)(2,1)S(1)}, bf16[272,128]{1,0:T(8,128)(2,1)S(1)}, u32[]{:S(2)}, u32[]{:S(2)}) collective-permute-start(bf16[272,128]{1,0:T(8,128)(2,1)S(1)} %get-tuple-element.38), channel_id=1, source_target_pairs={{0,8},{1,9},{2,10},{3,11},{4,12},{5,13},{6,14},{7,15},{8,0},{9,1},... | collective-permute-start | bytes 208904 | tf_op jit(solution)/shard_map/ppermute | solution.py:17
  44.9 1.1 %collective-permute-start.26 = (bf16[272,128]{1,0:T(8,128)(2,1)S(1)}, bf16[272,128]{1,0:T(8,128)(2,1)S(1)}, u32[]{:S(2)}, u32[]{:S(2)}) collective-permute-start(bf16[272,128]{1,0:T(8,128)(2,1)S(1)} %get-tuple-element.39), channel_id=1, source_target_pairs={{0,10},{1,11},{2,8},{3,9},{4,14},{5,15},{6,12},{7,13},{8,2},{9,3},... | collective-permute-start | bytes 208904 | tf_op jit(solution)/shard_map/ppermute | solution.py:17
  46.0 3.5 %collective-permute-start.27 = (bf16[272,128]{1,0:T(8,128)(2,1)S(1)}, bf16[272,128]{1,0:T(8,128)(2,1)S(1)}, u32[]{:S(2)}, u32[]{:S(2)}) collective-permute-start(bf16[272,128]{1,0:T(8,128)(2,1)S(1)} %get-tuple-element.40), channel_id=1, source_target_pairs={{0,12},{1,13},{2,14},{3,15},{4,8},{5,9},{6,10},{7,11},{8,4},{9,5},... | collective-permute-start | bytes 208904 | tf_op jit(solution)/shard_map/ppermute | solution.py:17
  49.5 0.8 %collective-permute-start.28 = (bf16[272,128]{1,0:T(8,128)(2,1)S(1)}, bf16[272,128]{1,0:T(8,128)(2,1)S(1)}, u32[]{:S(2)}, u32[]{:S(2)}) collective-permute-start(bf16[272,128]{1,0:T(8,128)(2,1)S(1)} %get-tuple-element.41), channel_id=1, source_target_pairs={{0,14},{1,15},{2,12},{3,13},{4,10},{5,11},{6,8},{7,9},{8,6},{9,7},... | collective-permute-start | bytes 208904 | tf_op jit(solution)/shard_map/ppermute | solution.py:17
  50.3 0.4 collective-permute-start.29
  50.7 2.6 %collective-permute-start.30 = (bf16[272,128]{1,0:T(8,128)(2,1)S(1)}, bf16[272,128]{1,0:T(8,128)(2,1)S(1)}, u32[]{:S(2)}, u32[]{:S(2)}) collective-permute-start(bf16[272,128]{1,0:T(8,128)(2,1)S(1)} %get-tuple-element.43), channel_id=1, source_target_pairs={{0,4},{1,5},{2,6},{3,7},{4,0},{5,1},{6,2},{7,3},{8,12},{9,13},{10,... | collective-permute-start | bytes 208904 | tf_op jit(solution)/shard_map/ppermute | solution.py:17
  53.3 2.2 %collective-permute-done.26.refs_1_ = bf16[272,128]{1,0:T(8,128)(2,1)S(1)} collective-permute-done((bf16[272,128]{1,0:T(8,128)(2,1)S(1)}, bf16[272,128]{1,0:T(8,128)(2,1)S(1)}, u32[]{:S(2)}, u32[]{:S(2)}) %collective-permute-start.26) | collective-permute-done | bytes 69664 | tf_op jit(solution)/shard_map/ppermute | solution.py:17
  55.4 2.0 %collective-permute-start.31 = (bf16[272,128]{1,0:T(8,128)(2,1)S(1)}, bf16[272,128]{1,0:T(8,128)(2,1)S(1)}, u32[]{:S(2)}, u32[]{:S(2)}) collective-permute-start(bf16[272,128]{1,0:T(8,128)(2,1)S(1)} %get-tuple-element.44), channel_id=1, source_target_pairs={{0,2},{1,3},{2,0},{3,1},{4,6},{5,7},{6,4},{7,5},{8,10},{9,11},{10,... | collective-permute-start | bytes 208904 | tf_op jit(solution)/shard_map/ppermute | solution.py:17
  57.4 1.0 %shard_map.72 = f32[2,2]{1,0:T(2,128)} custom-call(bf16[4,128,128]{2,1,0:T(8,128)(2,1)S(1)} %pad_maximum_fusion.refs_0_, bf16[4,128,128]{2,1,0:T(8,128)(2,1)S(1)} %collective-permute-done.2.refs_3_.refs_1_, bf16[4,128,128]{2,1,0:T(8,128)(2,1)S(1)} %collective-permute-done.5.refs_6_.refs_2_, bf16[4,128,128]{2,1,0:T(8,128)(2,1)S(1)} %collective-permute-done.8.refs_9_.refs_3_, ...), custom_call_target="tpu_custom_call" | custom-call | tf_op jit(solution)/shard_map/pallas_call | solution.py:397
  58.4 0.0 collective-permute-done.29.refs_4_
  58.4 0.0 collective-permute-done.30.refs_5_
  58.4 1.3 %collective-permute-done.31.refs_6_ = bf16[272,128]{1,0:T(8,128)(2,1)S(1)} collective-permute-done((bf16[272,128]{1,0:T(8,128)(2,1)S(1)}, bf16[272,128]{1,0:T(8,128)(2,1)S(1)}, u32[]{:S(2)}, u32[]{:S(2)}) %collective-permute-start.31) | collective-permute-done | bytes 69664 | tf_op jit(solution)/shard_map/ppermute | solution.py:17
  59.7 0.7 %shard_map.71 = (f32[1,2,128,128]{3,2,1,0:T(8,128)}, f32[2,2]{1,0:T(2,128)}) custom-call(f32[256,128]{1,0:T(8,128)S(1)} %get-tuple-element.37.mine_ref, f32[16,128]{1,0:T(8,128)S(1)} %get-tuple-element.35.total_ref, bf16[272,128]{1,0:T(8,128)(2,1)S(1)} %collective-permute-done.25.refs_0_, bf16[272,128]{1,0:T(8,128)(2,1)S(1)} %collective-permute-done.26.refs_1_, ...), custom_call_target="tpu_custom_call" | custom-call | tf_op jit(solution)/shard_map/pallas_call | solution.py:459
  (11 shorter events, 0.1 us)
Async XLA Ops:
  0.6 26.9 %copy-start.1 = (bf16[4,128,128]{2,1,0:T(8,128)(2,1)S(1)}, bf16[4,128,128]{2,1,0:T(8,128)(2,1)}, u32[]{:S(2)}) copy-start(bf16[4,128,128]{2,1,0:T(8,128)(2,1)} %refs_1_.1) | copy-start | bytes 393220
  0.6 3.6 %collective-permute-start = (bf16[2,128,128]{2,1,0:T(8,128)(2,1)}, bf16[2,128,128]{2,1,0:T(8,128)(2,1)S(1)}, u32[]{:S(2)}, u32[]{:S(2)}) collective-permute-start(bf16[2,128,128]{2,1,0:T(8,128)(2,1)} %bitcast.3), channel_id=1, source_target_pairs={{0,1},{1,0},{2,3},{3,2},{4,5},{5,4},{6,7},{7,6},{8,9},{9,8},{10,11... | collective-permute-start | bytes 196616 | tf_op jit(solution)/shard_map/ppermute | solution.py:17
  1.2 5.6 %collective-permute-start.1 = (bf16[4,128,128]{2,1,0:T(8,128)(2,1)}, bf16[4,128,128]{2,1,0:T(8,128)(2,1)S(1)}, u32[]{:S(2)}, u32[]{:S(2)}) collective-permute-start(bf16[4,128,128]{2,1,0:T(8,128)(2,1)} %refs_1_.1), channel_id=1, source_target_pairs={{0,1},{1,0},{2,3},{3,2},{4,5},{5,4},{6,7},{7,6},{8,9},{9,8},{10,11... | collective-permute-start | bytes 393224 | tf_op jit(solution)/shard_map/ppermute | solution.py:17
  1.2 7.1 %collective-permute-start.3 = (bf16[4,128,128]{2,1,0:T(8,128)(2,1)}, bf16[4,128,128]{2,1,0:T(8,128)(2,1)S(1)}, u32[]{:S(2)}, u32[]{:S(2)}) collective-permute-start(bf16[4,128,128]{2,1,0:T(8,128)(2,1)} %refs_1_.1), channel_id=1, source_target_pairs={{0,4},{1,3},{4,8},{5,1},{8,12},{9,5},{12,14},{13,9},{14,10},{15,13... | collective-permute-start | bytes 393224 | tf_op jit(solution)/shard_map/ppermute | solution.py:31
  5.1 5.0 %collective-permute-start.2 = (bf16[4,128,128]{2,1,0:T(8,128)(2,1)S(1)}, bf16[4,128,128]{2,1,0:T(8,128)(2,1)S(1)}, u32[]{:S(2)}, u32[]{:S(2)}) collective-permute-start(bf16[4,128,128]{2,1,0:T(8,128)(2,1)S(1)} %pad_maximum_fusion.refs_0_), channel_id=1, source_target_pairs={{0,4},{1,3},{4,8},{5,1},{8,12},{9,5},{12,14},{13,9},{14,10},{15,13... | collective-permute-start | bytes 393224 | tf_op jit(solution)/shard_map/ppermute | solution.py:31
  6.7 5.0 %collective-permute-start.4 = (bf16[4,128,128]{2,1,0:T(8,128)(2,1)S(1)}, bf16[4,128,128]{2,1,0:T(8,128)(2,1)S(1)}, u32[]{:S(2)}, u32[]{:S(2)}) collective-permute-start(bf16[4,128,128]{2,1,0:T(8,128)(2,1)S(1)} %collective-permute-done.1.refs_2_), channel_id=1, source_target_pairs={{0,4},{1,3},{4,8},{5,1},{8,12},{9,5},{12,14},{13,9},{14,10},{15,13... | collective-permute-start | bytes 393224 | tf_op jit(solution)/shard_map/ppermute | solution.py:31
  8.3 5.0 %collective-permute-start.9 = (bf16[4,128,128]{2,1,0:T(8,128)(2,1)S(1)}, bf16[4,128,128]{2,1,0:T(8,128)(2,1)S(1)}, u32[]{:S(2)}, u32[]{:S(2)}) collective-permute-start(bf16[4,128,128]{2,1,0:T(8,128)(2,1)S(1)} %collective-permute-done.3.refs_4_), channel_id=1, source_target_pairs={{0,4},{1,3},{4,8},{5,1},{8,12},{9,5},{12,14},{13,9},{14,10},{15,13... | collective-permute-start | bytes 393224 | tf_op jit(solution)/shard_map/ppermute | solution.py:31
  9.8 3.5 %collective-permute-start.6 = (bf16[4,128,128]{2,1,0:T(8,128)(2,1)S(1)}, bf16[4,128,128]{2,1,0:T(8,128)(2,1)S(1)}, u32[]{:S(2)}, u32[]{:S(2)}) collective-permute-start(bf16[4,128,128]{2,1,0:T(8,128)(2,1)S(1)} %collective-permute-done.3.refs_4_), channel_id=1, source_target_pairs={{0,1},{1,0},{2,3},{3,2},{4,5},{5,4},{6,7},{7,6},{8,9},{9,8},{10,11... | collective-permute-start | bytes 393224 | tf_op jit(solution)/shard_map/ppermute | solution.py:17
  10.1 5.0 %collective-permute-start.8 = (bf16[4,128,128]{2,1,0:T(8,128)(2,1)S(1)}, bf16[4,128,128]{2,1,0:T(8,128)(2,1)S(1)}, u32[]{:S(2)}, u32[]{:S(2)}) collective-permute-start(bf16[4,128,128]{2,1,0:T(8,128)(2,1)S(1)} %collective-permute-done.2.refs_3_.refs_1_), channel_id=1, source_target_pairs={{0,4},{1,3},{4,8},{5,1},{8,12},{9,5},{12,14},{13,9},{14,10},{15,13... | collective-permute-start | bytes 393224 | tf_op jit(solution)/shard_map/ppermute | solution.py:31
  11.7 3.4 %collective-permute-start.5 = (bf16[4,128,128]{2,1,0:T(8,128)(2,1)S(1)}, bf16[4,128,128]{2,1,0:T(8,128)(2,1)S(1)}, u32[]{:S(2)}, u32[]{:S(2)}) collective-permute-start(bf16[4,128,128]{2,1,0:T(8,128)(2,1)S(1)} %collective-permute-done.2.refs_3_.refs_1_), channel_id=1, source_target_pairs={{0,1},{1,0},{2,3},{3,2},{4,5},{5,4},{6,7},{7,6},{8,9},{9,8},{10,11... | collective-permute-start | bytes 393224 | tf_op jit(solution)/shard_map/ppermute | solution.py:17
  11.7 5.0 %collective-permute-start.10 = (bf16[4,128,128]{2,1,0:T(8,128)(2,1)S(1)}, bf16[4,128,128]{2,1,0:T(8,128)(2,1)S(1)}, u32[]{:S(2)}, u32[]{:S(2)}) collective-permute-start(bf16[4,128,128]{2,1,0:T(8,128)(2,1)S(1)} %collective-permute-done.4.refs_5_), channel_id=1, source_target_pairs={{0,4},{1,3},{4,8},{5,1},{8,12},{9,5},{12,14},{13,9},{14,10},{15,13... | collective-permute-start | bytes 393224 | tf_op jit(solution)/shard_map/ppermute | solution.py:31
  13.3 3.4 %collective-permute-start.7 = (bf16[4,128,128]{2,1,0:T(8,128)(2,1)S(1)}, bf16[4,128,128]{2,1,0:T(8,128)(2,1)S(1)}, u32[]{:S(2)}, u32[]{:S(2)}) collective-permute-start(bf16[4,128,128]{2,1,0:T(8,128)(2,1)S(1)} %collective-permute-done.4.refs_5_), channel_id=1, source_target_pairs={{0,1},{1,0},{2,3},{3,2},{4,5},{5,4},{6,7},{7,6},{8,9},{9,8},{10,11... | collective-permute-start | bytes 393224 | tf_op jit(solution)/shard_map/ppermute | solution.py:17
  13.3 5.0 %collective-permute-start.15 = (bf16[4,128,128]{2,1,0:T(8,128)(2,1)S(1)}, bf16[4,128,128]{2,1,0:T(8,128)(2,1)S(1)}, u32[]{:S(2)}, u32[]{:S(2)}) collective-permute-start(bf16[4,128,128]{2,1,0:T(8,128)(2,1)S(1)} %collective-permute-done.9.refs_10_), channel_id=1, source_target_pairs={{0,4},{1,3},{4,8},{5,1},{8,12},{9,5},{12,14},{13,9},{14,10},{15,13... | collective-permute-start | bytes 393224 | tf_op jit(solution)/shard_map/ppermute | solution.py:31
  15.1 3.2 %collective-permute-start.12 = (bf16[4,128,128]{2,1,0:T(8,128)(2,1)S(1)}, bf16[4,128,128]{2,1,0:T(8,128)(2,1)S(1)}, u32[]{:S(2)}, u32[]{:S(2)}) collective-permute-start(bf16[4,128,128]{2,1,0:T(8,128)(2,1)S(1)} %collective-permute-done.9.refs_10_), channel_id=1, source_target_pairs={{0,1},{1,0},{2,3},{3,2},{4,5},{5,4},{6,7},{7,6},{8,9},{9,8},{10,11... | collective-permute-start | bytes 393224 | tf_op jit(solution)/shard_map/ppermute | solution.py:17
  15.1 5.0 %collective-permute-start.14 = (bf16[4,128,128]{2,1,0:T(8,128)(2,1)S(1)}, bf16[4,128,128]{2,1,0:T(8,128)(2,1)S(1)}, u32[]{:S(2)}, u32[]{:S(2)}) collective-permute-start(bf16[4,128,128]{2,1,0:T(8,128)(2,1)S(1)} %collective-permute-done.8.refs_9_.refs_3_), channel_id=1, source_target_pairs={{0,4},{1,3},{4,8},{5,1},{8,12},{9,5},{12,14},{13,9},{14,10},{15,13... | collective-permute-start | bytes 393224 | tf_op jit(solution)/shard_map/ppermute | solution.py:31
  16.7 3.4 %collective-permute-start.11 = (bf16[4,128,128]{2,1,0:T(8,128)(2,1)S(1)}, bf16[4,128,128]{2,1,0:T(8,128)(2,1)S(1)}, u32[]{:S(2)}, u32[]{:S(2)}) collective-permute-start(bf16[4,128,128]{2,1,0:T(8,128)(2,1)S(1)} %collective-permute-done.8.refs_9_.refs_3_), channel_id=1, source_target_pairs={{0,1},{1,0},{2,3},{3,2},{4,5},{5,4},{6,7},{7,6},{8,9},{9,8},{10,11... | collective-permute-start | bytes 393224 | tf_op jit(solution)/shard_map/ppermute | solution.py:17
  16.7 5.0 %collective-permute-start.16 = (bf16[4,128,128]{2,1,0:T(8,128)(2,1)S(1)}, bf16[4,128,128]{2,1,0:T(8,128)(2,1)S(1)}, u32[]{:S(2)}, u32[]{:S(2)}) collective-permute-start(bf16[4,128,128]{2,1,0:T(8,128)(2,1)S(1)} %collective-permute-done.10.refs_11_), channel_id=1, source_target_pairs={{0,4},{1,3},{4,8},{5,1},{8,12},{9,5},{12,14},{13,9},{14,10},{15,13... | collective-permute-start | bytes 393224 | tf_op jit(solution)/shard_map/ppermute | solution.py:31
  18.3 3.4 %collective-permute-start.13 = (bf16[4,128,128]{2,1,0:T(8,128)(2,1)S(1)}, bf16[4,128,128]{2,1,0:T(8,128)(2,1)S(1)}, u32[]{:S(2)}, u32[]{:S(2)}) collective-permute-start(bf16[4,128,128]{2,1,0:T(8,128)(2,1)S(1)} %collective-permute-done.10.refs_11_), channel_id=1, source_target_pairs={{0,1},{1,0},{2,3},{3,2},{4,5},{5,4},{6,7},{7,6},{8,9},{9,8},{10,11... | collective-permute-start | bytes 393224 | tf_op jit(solution)/shard_map/ppermute | solution.py:17
  18.3 5.0 %collective-permute-start.21 = (bf16[4,128,128]{2,1,0:T(8,128)(2,1)S(1)}, bf16[4,128,128]{2,1,0:T(8,128)(2,1)S(1)}, u32[]{:S(2)}, u32[]{:S(2)}) collective-permute-start(bf16[4,128,128]{2,1,0:T(8,128)(2,1)S(1)} %collective-permute-done.15.refs_16_), channel_id=1, source_target_pairs={{0,4},{1,3},{4,8},{5,1},{8,12},{9,5},{12,14},{13,9},{14,10},{15,13... | collective-permute-start | bytes 393224 | tf_op jit(solution)/shard_map/ppermute | solution.py:31
  20.1 7.4 %collective-permute-start.18 = (bf16[4,128,128]{2,1,0:T(8,128)(2,1)S(1)}, bf16[4,128,128]{2,1,0:T(8,128)(2,1)S(1)}, u32[]{:S(2)}, u32[]{:S(2)}) collective-permute-start(bf16[4,128,128]{2,1,0:T(8,128)(2,1)S(1)} %collective-permute-done.15.refs_16_), channel_id=1, source_target_pairs={{0,1},{1,0},{2,3},{3,2},{4,5},{5,4},{6,7},{7,6},{8,9},{9,8},{10,11... | collective-permute-start | bytes 393224 | tf_op jit(solution)/shard_map/ppermute | solution.py:17
  20.1 7.4 %collective-permute-start.20 = (bf16[4,128,128]{2,1,0:T(8,128)(2,1)S(1)}, bf16[4,128,128]{2,1,0:T(8,128)(2,1)S(1)}, u32[]{:S(2)}, u32[]{:S(2)}) collective-permute-start(bf16[4,128,128]{2,1,0:T(8,128)(2,1)S(1)} %collective-permute-done.14.refs_15_.refs_5_), channel_id=1, source_target_pairs={{0,4},{1,3},{4,8},{5,1},{8,12},{9,5},{12,14},{13,9},{14,10},{15,13... | collective-permute-start | bytes 393224 | tf_op jit(solution)/shard_map/ppermute | solution.py:31
  21.7 5.8 %collective-permute-start.17 = (bf16[4,128,128]{2,1,0:T(8,128)(2,1)S(1)}, bf16[4,128,128]{2,1,0:T(8,128)(2,1)S(1)}, u32[]{:S(2)}, u32[]{:S(2)}) collective-permute-start(bf16[4,128,128]{2,1,0:T(8,128)(2,1)S(1)} %collective-permute-done.14.refs_15_.refs_5_), channel_id=1, source_target_pairs={{0,1},{1,0},{2,3},{3,2},{4,5},{5,4},{6,7},{7,6},{8,9},{9,8},{10,11... | collective-permute-start | bytes 393224 | tf_op jit(solution)/shard_map/ppermute | solution.py:17
  21.7 5.8 %collective-permute-start.22 = (bf16[4,128,128]{2,1,0:T(8,128)(2,1)S(1)}, bf16[4,128,128]{2,1,0:T(8,128)(2,1)S(1)}, u32[]{:S(2)}, u32[]{:S(2)}) collective-permute-start(bf16[4,128,128]{2,1,0:T(8,128)(2,1)S(1)} %collective-permute-done.16.refs_17_), channel_id=1, source_target_pairs={{0,4},{1,3},{4,8},{5,1},{8,12},{9,5},{12,14},{13,9},{14,10},{15,13... | collective-permute-start | bytes 393224 | tf_op jit(solution)/shard_map/ppermute | solution.py:31
  23.3 4.1 %collective-permute-start.19 = (bf16[4,128,128]{2,1,0:T(8,128)(2,1)S(1)}, bf16[4,128,128]{2,1,0:T(8,128)(2,1)S(1)}, u32[]{:S(2)}, u32[]{:S(2)}) collective-permute-start(bf16[4,128,128]{2,1,0:T(8,128)(2,1)S(1)} %collective-permute-done.16.refs_17_), channel_id=1, source_target_pairs={{0,1},{1,0},{2,3},{3,2},{4,5},{5,4},{6,7},{7,6},{8,9},{9,8},{10,11... | collective-permute-start | bytes 393224 | tf_op jit(solution)/shard_map/ppermute | solution.py:17
  23.4 0.7 %copy-start = (s32[256,4]{0,1:T(4,128)S(1)}, s32[256,4]{0,1:T(4,128)}, u32[]{:S(2)}) copy-start(s32[256,4]{0,1:T(4,128)} %param.7) | copy-start | bytes 12292
  40.7 1.7 %collective-permute-start.23 = (bf16[1040,128]{1,0:T(8,128)(2,1)S(1)}, bf16[1040,128]{1,0:T(8,128)(2,1)S(1)}, u32[]{:S(2)}, u32[]{:S(2)}) collective-permute-start(bf16[1040,128]{1,0:T(8,128)(2,1)S(1)} %get-tuple-element.34), channel_id=1, source_target_pairs={{0,1},{1,0},{2,3},{3,2},{4,5},{5,4},{6,7},{7,6},{8,9},{9,8},{10,11... | collective-permute-start | bytes 798728 | tf_op jit(solution)/shard_map/ppermute | solution.py:17
  41.3 9.0 %collective-permute-start.24 = (bf16[1024,128]{1,0:T(8,128)(2,1)S(1)}, bf16[1024,128]{1,0:T(8,128)(2,1)S(1)}, u32[]{:S(2)}, u32[]{:S(2)}) collective-permute-start(bf16[1024,128]{1,0:T(8,128)(2,1)S(1)} %get-tuple-element.36), channel_id=1, source_target_pairs={{0,1},{1,0},{2,3},{3,2},{4,5},{5,4},{6,7},{7,6},{8,9},{9,8},{10,11... | collective-permute-start | bytes 786440 | tf_op jit(solution)/shard_map/ppermute | solution.py:17
  42.5 8.1 %collective-permute-start.25 = (bf16[272,128]{1,0:T(8,128)(2,1)S(1)}, bf16[272,128]{1,0:T(8,128)(2,1)S(1)}, u32[]{:S(2)}, u32[]{:S(2)}) collective-permute-start(bf16[272,128]{1,0:T(8,128)(2,1)S(1)} %get-tuple-element.38), channel_id=1, source_target_pairs={{0,8},{1,9},{2,10},{3,11},{4,12},{5,13},{6,14},{7,15},{8,0},{9,1},... | collective-permute-start | bytes 208904 | tf_op jit(solution)/shard_map/ppermute | solution.py:17
  44.9 10.5 %collective-permute-start.26 = (bf16[272,128]{1,0:T(8,128)(2,1)S(1)}, bf16[272,128]{1,0:T(8,128)(2,1)S(1)}, u32[]{:S(2)}, u32[]{:S(2)}) collective-permute-start(bf16[272,128]{1,0:T(8,128)(2,1)S(1)} %get-tuple-element.39), channel_id=1, source_target_pairs={{0,10},{1,11},{2,8},{3,9},{4,14},{5,15},{6,12},{7,13},{8,2},{9,3},... | collective-permute-start | bytes 208904 | tf_op jit(solution)/shard_map/ppermute | solution.py:17
  46.0 12.4 %collective-permute-start.27 = (bf16[272,128]{1,0:T(8,128)(2,1)S(1)}, bf16[272,128]{1,0:T(8,128)(2,1)S(1)}, u32[]{:S(2)}, u32[]{:S(2)}) collective-permute-start(bf16[272,128]{1,0:T(8,128)(2,1)S(1)} %get-tuple-element.40), channel_id=1, source_target_pairs={{0,12},{1,13},{2,14},{3,15},{4,8},{5,9},{6,10},{7,11},{8,4},{9,5},... | collective-permute-start | bytes 208904 | tf_op jit(solution)/shard_map/ppermute | solution.py:17
  49.5 8.9 %collective-permute-start.28 = (bf16[272,128]{1,0:T(8,128)(2,1)S(1)}, bf16[272,128]{1,0:T(8,128)(2,1)S(1)}, u32[]{:S(2)}, u32[]{:S(2)}) collective-permute-start(bf16[272,128]{1,0:T(8,128)(2,1)S(1)} %get-tuple-element.41), channel_id=1, source_target_pairs={{0,14},{1,15},{2,12},{3,13},{4,10},{5,11},{6,8},{7,9},{8,6},{9,7},... | collective-permute-start | bytes 208904 | tf_op jit(solution)/shard_map/ppermute | solution.py:17
  50.3 8.1 %collective-permute-start.29 = (bf16[272,128]{1,0:T(8,128)(2,1)S(1)}, bf16[272,128]{1,0:T(8,128)(2,1)S(1)}, u32[]{:S(2)}, u32[]{:S(2)}) collective-permute-start(bf16[272,128]{1,0:T(8,128)(2,1)S(1)} %get-tuple-element.42), channel_id=1, source_target_pairs={{0,6},{1,7},{2,4},{3,5},{4,2},{5,3},{6,0},{7,1},{8,14},{9,15},{10,... | collective-permute-start | bytes 208904 | tf_op jit(solution)/shard_map/ppermute | solution.py:17
  50.7 7.8 %collective-permute-start.30 = (bf16[272,128]{1,0:T(8,128)(2,1)S(1)}, bf16[272,128]{1,0:T(8,128)(2,1)S(1)}, u32[]{:S(2)}, u32[]{:S(2)}) collective-permute-start(bf16[272,128]{1,0:T(8,128)(2,1)S(1)} %get-tuple-element.43), channel_id=1, source_target_pairs={{0,4},{1,5},{2,6},{3,7},{4,0},{5,1},{6,2},{7,3},{8,12},{9,13},{10,... | collective-permute-start | bytes 208904 | tf_op jit(solution)/shard_map/ppermute | solution.py:17
  55.4 4.3 %collective-permute-start.31 = (bf16[272,128]{1,0:T(8,128)(2,1)S(1)}, bf16[272,128]{1,0:T(8,128)(2,1)S(1)}, u32[]{:S(2)}, u32[]{:S(2)}) collective-permute-start(bf16[272,128]{1,0:T(8,128)(2,1)S(1)} %get-tuple-element.44), channel_id=1, source_target_pairs={{0,2},{1,3},{2,0},{3,1},{4,6},{5,7},{6,4},{7,5},{8,10},{9,11},{10,... | collective-permute-start | bytes 208904 | tf_op jit(solution)/shard_map/ppermute | solution.py:17

commit v19 on v16

--- a/solution.py
+++ b/solution.py
@@ -468,7 +468,7 @@
 
 def body(n, trial, left_ops, right_ops, task_list):
     steps = n // 4
-    plan, left_ops = make_plan(task_list.T, left_ops, n, n * right_ops.shape[0])
+    plan, left_ops = make_plan(pltpu.with_memory_space_constraint(task_list.T, pltpu.HBM), left_ops, n, n * right_ops.shape[0])
     vectors = jnp.concatenate([trial[0], exchange(trial[0], n, 1)], axis=0)
     line = [vectors, right_ops, exchange(right_ops, n, 1)]
     blocks = [(line, 0, False)]

time: 59.9 us -> 59.1 us (0.987)
  local copies, waits for them, and re-layouts: 0.69 us -> 0.01 us
    unnamed x4 -> x2, local copies, waits for them, and re-layouts: 0.69 us -> 0.01 us
where the time goes in v19:
time: 59.1 us; the launch traced here: 59 us
  starting transfers between devices  32.6 us (55%)
  Pallas kernels  18.4 us (31%)
  waiting for transfers between devices  6.38 us (11%)
  other arithmetic  0.85 us (1%)
  between operations  0.75 us (1%)
    ppermute x12, starting transfers between devices, ring_step(): return lax.ppermute(value, 'op', pairs)  20.4 us
    pallas_call x1, Pallas kernels, run_tasks(): pl.pallas_call(functools.partial(tasks_kernel, n, kinds), out_shape=(jax....  13.1 us
    ppermute x20, starting transfers between devices, exchange(): return lax.ppermute(value, 'op', [(i, i ^ mask) for i in range(n)])  12.2 us
    ppermute x20, waiting for transfers between devices, exchange(): return lax.ppermute(value, 'op', [(i, i ^ mask) for i in range(n)])  5.6 us
    pallas_call x1, Pallas kernels, make_plan(): pl.pallas_call(functools.partial(stage_kernel, n, terms), in_specs=[hbm,...  3.41 us
  transfers between devices with their start and end apart: 32, of which 8 were waited for; matrix products, arithmetic and copies ran while one was open for 1% of the time, Pallas kernels for 8%

profile of v19, /device:TPU:0, one launch (start us, length us, event | category | flops | bytes accessed | tf_op | source)
XLA Modules:
  0.0 59.0 jit_solution(4020230935403960000)
XLA Ops:
  0.6 0.5 collective-permute-start
  1.2 0.1 collective-permute-start.1
  1.2 3.0 %collective-permute-start.3 = (bf16[4,128,128]{2,1,0:T(8,128)(2,1)}, bf16[4,128,128]{2,1,0:T(8,128)(2,1)S(1)}, u32[]{:S(2)}, u32[]{:S(2)}) collective-permute-start(bf16[4,128,128]{2,1,0:T(8,128)(2,1)} %refs_1_.1), channel_id=1, source_target_pairs={{0,4},{1,3},{4,8},{5,1},{8,12},{9,5},{12,14},{13,9},{14,10},{15,13... | collective-permute-start | bytes 393224 | tf_op jit(solution)/shard_map/ppermute | solution.py:31
  4.2 0.0 collective-permute-done
  4.2 0.9 %pad_maximum_fusion.refs_0_ = bf16[4,128,128]{2,1,0:T(8,128)(2,1)S(1)} fusion(bf16[2,128,128]{2,1,0:T(8,128)(2,1)S(1)} %collective-permute-done, bf16[2,128,128]{2,1,0:T(8,128)(2,1)} %bitcast.3), kind=kLoop, calls=%fused_computation | loop fusion | flops 65536 | bytes 262144 | tf_op jit(solution)/shard_map/concatenate | solution.py:472
  5.1 1.6 %collective-permute-start.2 = (bf16[4,128,128]{2,1,0:T(8,128)(2,1)S(1)}, bf16[4,128,128]{2,1,0:T(8,128)(2,1)S(1)}, u32[]{:S(2)}, u32[]{:S(2)}) collective-permute-start(bf16[4,128,128]{2,1,0:T(8,128)(2,1)S(1)} %pad_maximum_fusion.refs_0_), channel_id=1, source_target_pairs={{0,4},{1,3},{4,8},{5,1},{8,12},{9,5},{12,14},{13,9},{14,10},{15,13... | collective-permute-start | bytes 393224 | tf_op jit(solution)/shard_map/ppermute | solution.py:31
  6.7 0.0 collective-permute-done.1.refs_2_
  6.7 1.6 %collective-permute-start.4 = (bf16[4,128,128]{2,1,0:T(8,128)(2,1)S(1)}, bf16[4,128,128]{2,1,0:T(8,128)(2,1)S(1)}, u32[]{:S(2)}, u32[]{:S(2)}) collective-permute-start(bf16[4,128,128]{2,1,0:T(8,128)(2,1)S(1)} %collective-permute-done.1.refs_2_), channel_id=1, source_target_pairs={{0,4},{1,3},{4,8},{5,1},{8,12},{9,5},{12,14},{13,9},{14,10},{15,13... | collective-permute-start | bytes 393224 | tf_op jit(solution)/shard_map/ppermute | solution.py:31
  8.3 0.0 collective-permute-done.3.refs_4_
  8.3 1.5 %collective-permute-start.9 = (bf16[4,128,128]{2,1,0:T(8,128)(2,1)S(1)}, bf16[4,128,128]{2,1,0:T(8,128)(2,1)S(1)}, u32[]{:S(2)}, u32[]{:S(2)}) collective-permute-start(bf16[4,128,128]{2,1,0:T(8,128)(2,1)S(1)} %collective-permute-done.3.refs_4_), channel_id=1, source_target_pairs={{0,4},{1,3},{4,8},{5,1},{8,12},{9,5},{12,14},{13,9},{14,10},{15,13... | collective-permute-start | bytes 393224 | tf_op jit(solution)/shard_map/ppermute | solution.py:31
  9.8 0.0 collective-permute-start.6
  9.8 0.3 collective-permute-done.2.refs_3_.refs_1_
  10.1 1.6 %collective-permute-start.8 = (bf16[4,128,128]{2,1,0:T(8,128)(2,1)S(1)}, bf16[4,128,128]{2,1,0:T(8,128)(2,1)S(1)}, u32[]{:S(2)}, u32[]{:S(2)}) collective-permute-start(bf16[4,128,128]{2,1,0:T(8,128)(2,1)S(1)} %collective-permute-done.2.refs_3_.refs_1_), channel_id=1, source_target_pairs={{0,4},{1,3},{4,8},{5,1},{8,12},{9,5},{12,14},{13,9},{14,10},{15,13... | collective-permute-start | bytes 393224 | tf_op jit(solution)/shard_map/ppermute | solution.py:31
  11.7 0.0 collective-permute-start.5
  11.7 0.0 collective-permute-done.4.refs_5_
  11.7 1.6 %collective-permute-start.10 = (bf16[4,128,128]{2,1,0:T(8,128)(2,1)S(1)}, bf16[4,128,128]{2,1,0:T(8,128)(2,1)S(1)}, u32[]{:S(2)}, u32[]{:S(2)}) collective-permute-start(bf16[4,128,128]{2,1,0:T(8,128)(2,1)S(1)} %collective-permute-done.4.refs_5_), channel_id=1, source_target_pairs={{0,4},{1,3},{4,8},{5,1},{8,12},{9,5},{12,14},{13,9},{14,10},{15,13... | collective-permute-start | bytes 393224 | tf_op jit(solution)/shard_map/ppermute | solution.py:31
  13.3 0.0 collective-permute-done.9.refs_10_
  13.3 0.0 collective-permute-start.7
  13.3 0.0 collective-permute-done.6.refs_7_
  13.3 1.6 %collective-permute-start.15 = (bf16[4,128,128]{2,1,0:T(8,128)(2,1)S(1)}, bf16[4,128,128]{2,1,0:T(8,128)(2,1)S(1)}, u32[]{:S(2)}, u32[]{:S(2)}) collective-permute-start(bf16[4,128,128]{2,1,0:T(8,128)(2,1)S(1)} %collective-permute-done.9.refs_10_), channel_id=1, source_target_pairs={{0,4},{1,3},{4,8},{5,1},{8,12},{9,5},{12,14},{13,9},{14,10},{15,13... | collective-permute-start | bytes 393224 | tf_op jit(solution)/shard_map/ppermute | solution.py:31
  14.9 0.2 collective-permute-done.8.refs_9_.refs_3_
  15.1 0.0 collective-permute-start.12
  15.1 0.0 collective-permute-done.5.refs_6_.refs_2_
  15.1 1.6 %collective-permute-start.14 = (bf16[4,128,128]{2,1,0:T(8,128)(2,1)S(1)}, bf16[4,128,128]{2,1,0:T(8,128)(2,1)S(1)}, u32[]{:S(2)}, u32[]{:S(2)}) collective-permute-start(bf16[4,128,128]{2,1,0:T(8,128)(2,1)S(1)} %collective-permute-done.8.refs_9_.refs_3_), channel_id=1, source_target_pairs={{0,4},{1,3},{4,8},{5,1},{8,12},{9,5},{12,14},{13,9},{14,10},{15,13... | collective-permute-start | bytes 393224 | tf_op jit(solution)/shard_map/ppermute | solution.py:31
  16.7 0.0 collective-permute-done.10.refs_11_
  16.7 0.0 collective-permute-start.11
  16.7 0.0 collective-permute-done.7.refs_8_
  16.7 1.6 %collective-permute-start.16 = (bf16[4,128,128]{2,1,0:T(8,128)(2,1)S(1)}, bf16[4,128,128]{2,1,0:T(8,128)(2,1)S(1)}, u32[]{:S(2)}, u32[]{:S(2)}) collective-permute-start(bf16[4,128,128]{2,1,0:T(8,128)(2,1)S(1)} %collective-permute-done.10.refs_11_), channel_id=1, source_target_pairs={{0,4},{1,3},{4,8},{5,1},{8,12},{9,5},{12,14},{13,9},{14,10},{15,13... | collective-permute-start | bytes 393224 | tf_op jit(solution)/shard_map/ppermute | solution.py:31
  18.3 0.0 collective-permute-done.15.refs_16_
  18.3 0.0 collective-permute-start.13
  18.3 0.0 collective-permute-done.12.refs_13_
  18.3 1.6 %collective-permute-start.21 = (bf16[4,128,128]{2,1,0:T(8,128)(2,1)S(1)}, bf16[4,128,128]{2,1,0:T(8,128)(2,1)S(1)}, u32[]{:S(2)}, u32[]{:S(2)}) collective-permute-start(bf16[4,128,128]{2,1,0:T(8,128)(2,1)S(1)} %collective-permute-done.15.refs_16_), channel_id=1, source_target_pairs={{0,4},{1,3},{4,8},{5,1},{8,12},{9,5},{12,14},{13,9},{14,10},{15,13... | collective-permute-start | bytes 393224 | tf_op jit(solution)/shard_map/ppermute | solution.py:31
  19.9 0.2 collective-permute-done.14.refs_15_.refs_5_
  20.1 0.0 collective-permute-start.18
  20.1 1.6 %collective-permute-start.20 = (bf16[4,128,128]{2,1,0:T(8,128)(2,1)S(1)}, bf16[4,128,128]{2,1,0:T(8,128)(2,1)S(1)}, u32[]{:S(2)}, u32[]{:S(2)}) collective-permute-start(bf16[4,128,128]{2,1,0:T(8,128)(2,1)S(1)} %collective-permute-done.14.refs_15_.refs_5_), channel_id=1, source_target_pairs={{0,4},{1,3},{4,8},{5,1},{8,12},{9,5},{12,14},{13,9},{14,10},{15,13... | collective-permute-start | bytes 393224 | tf_op jit(solution)/shard_map/ppermute | solution.py:31
  21.6 0.1 collective-permute-done.16.refs_17_
  21.7 1.6 %collective-permute-start.22 = (bf16[4,128,128]{2,1,0:T(8,128)(2,1)S(1)}, bf16[4,128,128]{2,1,0:T(8,128)(2,1)S(1)}, u32[]{:S(2)}, u32[]{:S(2)}) collective-permute-start(bf16[4,128,128]{2,1,0:T(8,128)(2,1)S(1)} %collective-permute-done.16.refs_17_), channel_id=1, source_target_pairs={{0,4},{1,3},{4,8},{5,1},{8,12},{9,5},{12,14},{13,9},{14,10},{15,13... | collective-permute-start | bytes 393224 | tf_op jit(solution)/shard_map/ppermute | solution.py:31
  23.3 0.0 collective-permute-done.21.refs_22_
  23.4 3.4 %shard_map.67 = (s32[6,512]{1,0:T(8,128)S(1)}, bf16[256,128,128]{2,1,0:T(8,128)(2,1)S(1)}) custom-call(s32[4,256]{1,0:T(4,128)} %bitcast.4, bf16[256,128,128]{2,1,0:T(8,128)(2,1)} %left_ref.1), custom_call_target="tpu_custom_call" | custom-call | tf_op jit(solution)/shard_map/pallas_call | solution.py:192
  26.8 0.0 collective-permute-done.18.refs_19_
  26.8 0.0 collective-permute-done.20.refs_21_.refs_7_
  26.8 0.0 collective-permute-done.22.refs_23_
  26.8 0.0 collective-permute-done.19.refs_20_
  26.8 13.1 %shard_map.68 = (bf16[1040,128]{1,0:T(8,128)(2,1)S(1)}, bf16[1024,128]{1,0:T(8,128)(2,1)S(1)}, f32[17,256,128]{2,1,0:T(8,128)S(1)}, f32[8,128]{1,0:T(8,128)S(1)}) custom-call(s32[6,512]{1,0:T(8,128)S(1)} %get-tuple-element.29.plan_ref, bf16[256,128,128]{2,1,0:T(8,128)(2,1)S(1)} %get-tuple-element.30.left_ref, ...), custom_call_target="tpu_custom_call" | custom-call | flops 4294967296 | bytes 15588608 | tf_op jit(solution)/shard_map/pallas_call | solution.py:361
  40.0 0.6 collective-permute-start.23
  40.6 0.1 collective-permute-start.24
  40.6 1.1 %collective-permute-done.23.received_ref = bf16[1040,128]{1,0:T(8,128)(2,1)S(1)} collective-permute-done((bf16[1040,128]{1,0:T(8,128)(2,1)S(1)}, bf16[1040,128]{1,0:T(8,128)(2,1)S(1)}, u32[]{:S(2)}, u32[]{:S(2)}) %collective-permute-start.23) | collective-permute-done | bytes 266272 | tf_op jit(solution)/shard_map/ppermute | solution.py:17
  41.7 0.1 shard_map.69
  41.8 4.0 %collective-permute-start.25 = (bf16[272,128]{1,0:T(8,128)(2,1)S(1)}, bf16[272,128]{1,0:T(8,128)(2,1)S(1)}, u32[]{:S(2)}, u32[]{:S(2)}) collective-permute-start(bf16[272,128]{1,0:T(8,128)(2,1)S(1)} %get-tuple-element.38), channel_id=1, source_target_pairs={{0,14},{1,15},{2,12},{3,13},{4,10},{5,11},{6,8},{7,9},{8,6},{9,7},... | collective-permute-start | bytes 208904 | tf_op jit(solution)/shard_map/ppermute | solution.py:17
  45.8 0.4 collective-permute-start.26
  46.2 0.9 %collective-permute-start.27 = (bf16[272,128]{1,0:T(8,128)(2,1)S(1)}, bf16[272,128]{1,0:T(8,128)(2,1)S(1)}, u32[]{:S(2)}, u32[]{:S(2)}) collective-permute-start(bf16[272,128]{1,0:T(8,128)(2,1)S(1)} %get-tuple-element.40), channel_id=1, source_target_pairs={{0,10},{1,11},{2,8},{3,9},{4,14},{5,15},{6,12},{7,13},{8,2},{9,3},... | collective-permute-start | bytes 208904 | tf_op jit(solution)/shard_map/ppermute | solution.py:17
  47.1 2.4 %collective-permute-start.28 = (bf16[272,128]{1,0:T(8,128)(2,1)S(1)}, bf16[272,128]{1,0:T(8,128)(2,1)S(1)}, u32[]{:S(2)}, u32[]{:S(2)}) collective-permute-start(bf16[272,128]{1,0:T(8,128)(2,1)S(1)} %get-tuple-element.41), channel_id=1, source_target_pairs={{0,8},{1,9},{2,10},{3,11},{4,12},{5,13},{6,14},{7,15},{8,0},{9,1},... | collective-permute-start | bytes 208904 | tf_op jit(solution)/shard_map/ppermute | solution.py:17
  49.5 0.0 collective-permute-done.24.received_ref
  49.6 1.7 %collective-permute-start.29 = (bf16[272,128]{1,0:T(8,128)(2,1)S(1)}, bf16[272,128]{1,0:T(8,128)(2,1)S(1)}, u32[]{:S(2)}, u32[]{:S(2)}) collective-permute-start(bf16[272,128]{1,0:T(8,128)(2,1)S(1)} %get-tuple-element.42), channel_id=1, source_target_pairs={{0,6},{1,7},{2,4},{3,5},{4,2},{5,3},{6,0},{7,1},{8,14},{9,15},{10,... | collective-permute-start | bytes 208904 | tf_op jit(solution)/shard_map/ppermute | solution.py:17
  51.3 0.0 collective-permute-done.25.refs_0_
  51.3 0.9 %collective-permute-start.30 = (bf16[272,128]{1,0:T(8,128)(2,1)S(1)}, bf16[272,128]{1,0:T(8,128)(2,1)S(1)}, u32[]{:S(2)}, u32[]{:S(2)}) collective-permute-start(bf16[272,128]{1,0:T(8,128)(2,1)S(1)} %get-tuple-element.43), channel_id=1, source_target_pairs={{0,4},{1,5},{2,6},{3,7},{4,0},{5,1},{6,2},{7,3},{8,12},{9,13},{10,... | collective-permute-start | bytes 208904 | tf_op jit(solution)/shard_map/ppermute | solution.py:17
  52.2 0.6 collective-permute-done.26.refs_1_
  52.8 0.6 collective-permute-start.31
  53.3 1.0 %shard_map.72 = f32[2,2]{1,0:T(2,128)} custom-call(bf16[4,128,128]{2,1,0:T(8,128)(2,1)S(1)} %pad_maximum_fusion.refs_0_, bf16[4,128,128]{2,1,0:T(8,128)(2,1)S(1)} %collective-permute-done.2.refs_3_.refs_1_, bf16[4,128,128]{2,1,0:T(8,128)(2,1)S(1)} %collective-permute-done.5.refs_6_.refs_2_, bf16[4,128,128]{2,1,0:T(8,128)(2,1)S(1)} %collective-permute-done.8.refs_9_.refs_3_, ...), custom_call_target="tpu_custom_call" | custom-call | tf_op jit(solution)/shard_map/pallas_call | solution.py:397
  54.3 3.4 %collective-permute-done.27.refs_2_ = bf16[272,128]{1,0:T(8,128)(2,1)S(1)} collective-permute-done((bf16[272,128]{1,0:T(8,128)(2,1)S(1)}, bf16[272,128]{1,0:T(8,128)(2,1)S(1)}, u32[]{:S(2)}, u32[]{:S(2)}) %collective-permute-start.27) | collective-permute-done | bytes 69664 | tf_op jit(solution)/shard_map/ppermute | solution.py:17
  57.7 0.5 collective-permute-done.28.refs_3_
  58.2 0.0 collective-permute-done.29.refs_4_
  58.2 0.0 collective-permute-done.30.refs_5_
  58.2 0.7 %shard_map.71 = (f32[1,2,128,128]{3,2,1,0:T(8,128)}, f32[2,2]{1,0:T(2,128)}) custom-call(f32[256,128]{1,0:T(8,128)S(1)} %get-tuple-element.37.mine_ref, f32[16,128]{1,0:T(8,128)S(1)} %get-tuple-element.35.total_ref, bf16[272,128]{1,0:T(8,128)(2,1)S(1)} %collective-permute-done.25.refs_0_, bf16[272,128]{1,0:T(8,128)(2,1)S(1)} %collective-permute-done.26.refs_1_, ...), custom_call_target="tpu_custom_call" | custom-call | tf_op jit(solution)/shard_map/pallas_call | solution.py:459
  (9 shorter events, 0.1 us)
Async XLA Ops:
  0.6 26.2 %copy-start = (bf16[4,128,128]{2,1,0:T(8,128)(2,1)S(1)}, bf16[4,128,128]{2,1,0:T(8,128)(2,1)}, u32[]{:S(2)}) copy-start(bf16[4,128,128]{2,1,0:T(8,128)(2,1)} %refs_1_.1) | copy-start | bytes 393220
  0.6 3.6 %collective-permute-start = (bf16[2,128,128]{2,1,0:T(8,128)(2,1)}, bf16[2,128,128]{2,1,0:T(8,128)(2,1)S(1)}, u32[]{:S(2)}, u32[]{:S(2)}) collective-permute-start(bf16[2,128,128]{2,1,0:T(8,128)(2,1)} %bitcast.2), channel_id=1, source_target_pairs={{0,1},{1,0},{2,3},{3,2},{4,5},{5,4},{6,7},{7,6},{8,9},{9,8},{10,11... | collective-permute-start | bytes 196616 | tf_op jit(solution)/shard_map/ppermute | solution.py:17
  1.2 5.6 %collective-permute-start.1 = (bf16[4,128,128]{2,1,0:T(8,128)(2,1)}, bf16[4,128,128]{2,1,0:T(8,128)(2,1)S(1)}, u32[]{:S(2)}, u32[]{:S(2)}) collective-permute-start(bf16[4,128,128]{2,1,0:T(8,128)(2,1)} %refs_1_.1), channel_id=1, source_target_pairs={{0,1},{1,0},{2,3},{3,2},{4,5},{5,4},{6,7},{7,6},{8,9},{9,8},{10,11... | collective-permute-start | bytes 393224 | tf_op jit(solution)/shard_map/ppermute | solution.py:17
  1.2 7.1 %collective-permute-start.3 = (bf16[4,128,128]{2,1,0:T(8,128)(2,1)}, bf16[4,128,128]{2,1,0:T(8,128)(2,1)S(1)}, u32[]{:S(2)}, u32[]{:S(2)}) collective-permute-start(bf16[4,128,128]{2,1,0:T(8,128)(2,1)} %refs_1_.1), channel_id=1, source_target_pairs={{0,4},{1,3},{4,8},{5,1},{8,12},{9,5},{12,14},{13,9},{14,10},{15,13... | collective-permute-start | bytes 393224 | tf_op jit(solution)/shard_map/ppermute | solution.py:31
  5.1 5.0 %collective-permute-start.2 = (bf16[4,128,128]{2,1,0:T(8,128)(2,1)S(1)}, bf16[4,128,128]{2,1,0:T(8,128)(2,1)S(1)}, u32[]{:S(2)}, u32[]{:S(2)}) collective-permute-start(bf16[4,128,128]{2,1,0:T(8,128)(2,1)S(1)} %pad_maximum_fusion.refs_0_), channel_id=1, source_target_pairs={{0,4},{1,3},{4,8},{5,1},{8,12},{9,5},{12,14},{13,9},{14,10},{15,13... | collective-permute-start | bytes 393224 | tf_op jit(solution)/shard_map/ppermute | solution.py:31
  6.7 5.0 %collective-permute-start.4 = (bf16[4,128,128]{2,1,0:T(8,128)(2,1)S(1)}, bf16[4,128,128]{2,1,0:T(8,128)(2,1)S(1)}, u32[]{:S(2)}, u32[]{:S(2)}) collective-permute-start(bf16[4,128,128]{2,1,0:T(8,128)(2,1)S(1)} %collective-permute-done.1.refs_2_), channel_id=1, source_target_pairs={{0,4},{1,3},{4,8},{5,1},{8,12},{9,5},{12,14},{13,9},{14,10},{15,13... | collective-permute-start | bytes 393224 | tf_op jit(solution)/shard_map/ppermute | solution.py:31
  8.3 5.0 %collective-permute-start.9 = (bf16[4,128,128]{2,1,0:T(8,128)(2,1)S(1)}, bf16[4,128,128]{2,1,0:T(8,128)(2,1)S(1)}, u32[]{:S(2)}, u32[]{:S(2)}) collective-permute-start(bf16[4,128,128]{2,1,0:T(8,128)(2,1)S(1)} %collective-permute-done.3.refs_4_), channel_id=1, source_target_pairs={{0,4},{1,3},{4,8},{5,1},{8,12},{9,5},{12,14},{13,9},{14,10},{15,13... | collective-permute-start | bytes 393224 | tf_op jit(solution)/shard_map/ppermute | solution.py:31
  9.8 3.5 %collective-permute-start.6 = (bf16[4,128,128]{2,1,0:T(8,128)(2,1)S(1)}, bf16[4,128,128]{2,1,0:T(8,128)(2,1)S(1)}, u32[]{:S(2)}, u32[]{:S(2)}) collective-permute-start(bf16[4,128,128]{2,1,0:T(8,128)(2,1)S(1)} %collective-permute-done.3.refs_4_), channel_id=1, source_target_pairs={{0,1},{1,0},{2,3},{3,2},{4,5},{5,4},{6,7},{7,6},{8,9},{9,8},{10,11... | collective-permute-start | bytes 393224 | tf_op jit(solution)/shard_map/ppermute | solution.py:17
  10.1 5.0 %collective-permute-start.8 = (bf16[4,128,128]{2,1,0:T(8,128)(2,1)S(1)}, bf16[4,128,128]{2,1,0:T(8,128)(2,1)S(1)}, u32[]{:S(2)}, u32[]{:S(2)}) collective-permute-start(bf16[4,128,128]{2,1,0:T(8,128)(2,1)S(1)} %collective-permute-done.2.refs_3_.refs_1_), channel_id=1, source_target_pairs={{0,4},{1,3},{4,8},{5,1},{8,12},{9,5},{12,14},{13,9},{14,10},{15,13... | collective-permute-start | bytes 393224 | tf_op jit(solution)/shard_map/ppermute | solution.py:31
  11.7 3.4 %collective-permute-start.5 = (bf16[4,128,128]{2,1,0:T(8,128)(2,1)S(1)}, bf16[4,128,128]{2,1,0:T(8,128)(2,1)S(1)}, u32[]{:S(2)}, u32[]{:S(2)}) collective-permute-start(bf16[4,128,128]{2,1,0:T(8,128)(2,1)S(1)} %collective-permute-done.2.refs_3_.refs_1_), channel_id=1, source_target_pairs={{0,1},{1,0},{2,3},{3,2},{4,5},{5,4},{6,7},{7,6},{8,9},{9,8},{10,11... | collective-permute-start | bytes 393224 | tf_op jit(solution)/shard_map/ppermute | solution.py:17
  11.7 5.0 %collective-permute-start.10 = (bf16[4,128,128]{2,1,0:T(8,128)(2,1)S(1)}, bf16[4,128,128]{2,1,0:T(8,128)(2,1)S(1)}, u32[]{:S(2)}, u32[]{:S(2)}) collective-permute-start(bf16[4,128,128]{2,1,0:T(8,128)(2,1)S(1)} %collective-permute-done.4.refs_5_), channel_id=1, source_target_pairs={{0,4},{1,3},{4,8},{5,1},{8,12},{9,5},{12,14},{13,9},{14,10},{15,13... | collective-permute-start | bytes 393224 | tf_op jit(solution)/shard_map/ppermute | solution.py:31
  13.3 3.4 %collective-permute-start.7 = (bf16[4,128,128]{2,1,0:T(8,128)(2,1)S(1)}, bf16[4,128,128]{2,1,0:T(8,128)(2,1)S(1)}, u32[]{:S(2)}, u32[]{:S(2)}) collective-permute-start(bf16[4,128,128]{2,1,0:T(8,128)(2,1)S(1)} %collective-permute-done.4.refs_5_), channel_id=1, source_target_pairs={{0,1},{1,0},{2,3},{3,2},{4,5},{5,4},{6,7},{7,6},{8,9},{9,8},{10,11... | collective-permute-start | bytes 393224 | tf_op jit(solution)/shard_map/ppermute | solution.py:17
  13.3 5.0 %collective-permute-start.15 = (bf16[4,128,128]{2,1,0:T(8,128)(2,1)S(1)}, bf16[4,128,128]{2,1,0:T(8,128)(2,1)S(1)}, u32[]{:S(2)}, u32[]{:S(2)}) collective-permute-start(bf16[4,128,128]{2,1,0:T(8,128)(2,1)S(1)} %collective-permute-done.9.refs_10_), channel_id=1, source_target_pairs={{0,4},{1,3},{4,8},{5,1},{8,12},{9,5},{12,14},{13,9},{14,10},{15,13... | collective-permute-start | bytes 393224 | tf_op jit(solution)/shard_map/ppermute | solution.py:31
  15.1 3.2 %collective-permute-start.12 = (bf16[4,128,128]{2,1,0:T(8,128)(2,1)S(1)}, bf16[4,128,128]{2,1,0:T(8,128)(2,1)S(1)}, u32[]{:S(2)}, u32[]{:S(2)}) collective-permute-start(bf16[4,128,128]{2,1,0:T(8,128)(2,1)S(1)} %collective-permute-done.9.refs_10_), channel_id=1, source_target_pairs={{0,1},{1,0},{2,3},{3,2},{4,5},{5,4},{6,7},{7,6},{8,9},{9,8},{10,11... | collective-permute-start | bytes 393224 | tf_op jit(solution)/shard_map/ppermute | solution.py:17
  15.1 5.0 %collective-permute-start.14 = (bf16[4,128,128]{2,1,0:T(8,128)(2,1)S(1)}, bf16[4,128,128]{2,1,0:T(8,128)(2,1)S(1)}, u32[]{:S(2)}, u32[]{:S(2)}) collective-permute-start(bf16[4,128,128]{2,1,0:T(8,128)(2,1)S(1)} %collective-permute-done.8.refs_9_.refs_3_), channel_id=1, source_target_pairs={{0,4},{1,3},{4,8},{5,1},{8,12},{9,5},{12,14},{13,9},{14,10},{15,13... | collective-permute-start | bytes 393224 | tf_op jit(solution)/shard_map/ppermute | solution.py:31
  16.7 3.4 %collective-permute-start.11 = (bf16[4,128,128]{2,1,0:T(8,128)(2,1)S(1)}, bf16[4,128,128]{2,1,0:T(8,128)(2,1)S(1)}, u32[]{:S(2)}, u32[]{:S(2)}) collective-permute-start(bf16[4,128,128]{2,1,0:T(8,128)(2,1)S(1)} %collective-permute-done.8.refs_9_.refs_3_), channel_id=1, source_target_pairs={{0,1},{1,0},{2,3},{3,2},{4,5},{5,4},{6,7},{7,6},{8,9},{9,8},{10,11... | collective-permute-start | bytes 393224 | tf_op jit(solution)/shard_map/ppermute | solution.py:17
  16.7 5.0 %collective-permute-start.16 = (bf16[4,128,128]{2,1,0:T(8,128)(2,1)S(1)}, bf16[4,128,128]{2,1,0:T(8,128)(2,1)S(1)}, u32[]{:S(2)}, u32[]{:S(2)}) collective-permute-start(bf16[4,128,128]{2,1,0:T(8,128)(2,1)S(1)} %collective-permute-done.10.refs_11_), channel_id=1, source_target_pairs={{0,4},{1,3},{4,8},{5,1},{8,12},{9,5},{12,14},{13,9},{14,10},{15,13... | collective-permute-start | bytes 393224 | tf_op jit(solution)/shard_map/ppermute | solution.py:31
  18.3 3.4 %collective-permute-start.13 = (bf16[4,128,128]{2,1,0:T(8,128)(2,1)S(1)}, bf16[4,128,128]{2,1,0:T(8,128)(2,1)S(1)}, u32[]{:S(2)}, u32[]{:S(2)}) collective-permute-start(bf16[4,128,128]{2,1,0:T(8,128)(2,1)S(1)} %collective-permute-done.10.refs_11_), channel_id=1, source_target_pairs={{0,1},{1,0},{2,3},{3,2},{4,5},{5,4},{6,7},{7,6},{8,9},{9,8},{10,11... | collective-permute-start | bytes 393224 | tf_op jit(solution)/shard_map/ppermute | solution.py:17
  18.3 5.0 %collective-permute-start.21 = (bf16[4,128,128]{2,1,0:T(8,128)(2,1)S(1)}, bf16[4,128,128]{2,1,0:T(8,128)(2,1)S(1)}, u32[]{:S(2)}, u32[]{:S(2)}) collective-permute-start(bf16[4,128,128]{2,1,0:T(8,128)(2,1)S(1)} %collective-permute-done.15.refs_16_), channel_id=1, source_target_pairs={{0,4},{1,3},{4,8},{5,1},{8,12},{9,5},{12,14},{13,9},{14,10},{15,13... | collective-permute-start | bytes 393224 | tf_op jit(solution)/shard_map/ppermute | solution.py:31
  20.1 6.7 %collective-permute-start.18 = (bf16[4,128,128]{2,1,0:T(8,128)(2,1)S(1)}, bf16[4,128,128]{2,1,0:T(8,128)(2,1)S(1)}, u32[]{:S(2)}, u32[]{:S(2)}) collective-permute-start(bf16[4,128,128]{2,1,0:T(8,128)(2,1)S(1)} %collective-permute-done.15.refs_16_), channel_id=1, source_target_pairs={{0,1},{1,0},{2,3},{3,2},{4,5},{5,4},{6,7},{7,6},{8,9},{9,8},{10,11... | collective-permute-start | bytes 393224 | tf_op jit(solution)/shard_map/ppermute | solution.py:17
  20.1 6.7 %collective-permute-start.20 = (bf16[4,128,128]{2,1,0:T(8,128)(2,1)S(1)}, bf16[4,128,128]{2,1,0:T(8,128)(2,1)S(1)}, u32[]{:S(2)}, u32[]{:S(2)}) collective-permute-start(bf16[4,128,128]{2,1,0:T(8,128)(2,1)S(1)} %collective-permute-done.14.refs_15_.refs_5_), channel_id=1, source_target_pairs={{0,4},{1,3},{4,8},{5,1},{8,12},{9,5},{12,14},{13,9},{14,10},{15,13... | collective-permute-start | bytes 393224 | tf_op jit(solution)/shard_map/ppermute | solution.py:31
  21.7 5.1 %collective-permute-start.17 = (bf16[4,128,128]{2,1,0:T(8,128)(2,1)S(1)}, bf16[4,128,128]{2,1,0:T(8,128)(2,1)S(1)}, u32[]{:S(2)}, u32[]{:S(2)}) collective-permute-start(bf16[4,128,128]{2,1,0:T(8,128)(2,1)S(1)} %collective-permute-done.14.refs_15_.refs_5_), channel_id=1, source_target_pairs={{0,1},{1,0},{2,3},{3,2},{4,5},{5,4},{6,7},{7,6},{8,9},{9,8},{10,11... | collective-permute-start | bytes 393224 | tf_op jit(solution)/shard_map/ppermute | solution.py:17
  21.7 5.1 %collective-permute-start.22 = (bf16[4,128,128]{2,1,0:T(8,128)(2,1)S(1)}, bf16[4,128,128]{2,1,0:T(8,128)(2,1)S(1)}, u32[]{:S(2)}, u32[]{:S(2)}) collective-permute-start(bf16[4,128,128]{2,1,0:T(8,128)(2,1)S(1)} %collective-permute-done.16.refs_17_), channel_id=1, source_target_pairs={{0,4},{1,3},{4,8},{5,1},{8,12},{9,5},{12,14},{13,9},{14,10},{15,13... | collective-permute-start | bytes 393224 | tf_op jit(solution)/shard_map/ppermute | solution.py:31
  23.3 3.5 %collective-permute-start.19 = (bf16[4,128,128]{2,1,0:T(8,128)(2,1)S(1)}, bf16[4,128,128]{2,1,0:T(8,128)(2,1)S(1)}, u32[]{:S(2)}, u32[]{:S(2)}) collective-permute-start(bf16[4,128,128]{2,1,0:T(8,128)(2,1)S(1)} %collective-permute-done.16.refs_17_), channel_id=1, source_target_pairs={{0,1},{1,0},{2,3},{3,2},{4,5},{5,4},{6,7},{7,6},{8,9},{9,8},{10,11... | collective-permute-start | bytes 393224 | tf_op jit(solution)/shard_map/ppermute | solution.py:17
  40.0 1.7 %collective-permute-start.23 = (bf16[1040,128]{1,0:T(8,128)(2,1)S(1)}, bf16[1040,128]{1,0:T(8,128)(2,1)S(1)}, u32[]{:S(2)}, u32[]{:S(2)}) collective-permute-start(bf16[1040,128]{1,0:T(8,128)(2,1)S(1)} %get-tuple-element.34), channel_id=1, source_target_pairs={{0,1},{1,0},{2,3},{3,2},{4,5},{5,4},{6,7},{7,6},{8,9},{9,8},{10,11... | collective-permute-start | bytes 798728 | tf_op jit(solution)/shard_map/ppermute | solution.py:17
  40.6 9.0 %collective-permute-start.24 = (bf16[1024,128]{1,0:T(8,128)(2,1)S(1)}, bf16[1024,128]{1,0:T(8,128)(2,1)S(1)}, u32[]{:S(2)}, u32[]{:S(2)}) collective-permute-start(bf16[1024,128]{1,0:T(8,128)(2,1)S(1)} %get-tuple-element.36), channel_id=1, source_target_pairs={{0,1},{1,0},{2,3},{3,2},{4,5},{5,4},{6,7},{7,6},{8,9},{9,8},{10,11... | collective-permute-start | bytes 786440 | tf_op jit(solution)/shard_map/ppermute | solution.py:17
  41.8 9.5 %collective-permute-start.25 = (bf16[272,128]{1,0:T(8,128)(2,1)S(1)}, bf16[272,128]{1,0:T(8,128)(2,1)S(1)}, u32[]{:S(2)}, u32[]{:S(2)}) collective-permute-start(bf16[272,128]{1,0:T(8,128)(2,1)S(1)} %get-tuple-element.38), channel_id=1, source_target_pairs={{0,14},{1,15},{2,12},{3,13},{4,10},{5,11},{6,8},{7,9},{8,6},{9,7},... | collective-permute-start | bytes 208904 | tf_op jit(solution)/shard_map/ppermute | solution.py:17
  45.8 6.9 %collective-permute-start.26 = (bf16[272,128]{1,0:T(8,128)(2,1)S(1)}, bf16[272,128]{1,0:T(8,128)(2,1)S(1)}, u32[]{:S(2)}, u32[]{:S(2)}) collective-permute-start(bf16[272,128]{1,0:T(8,128)(2,1)S(1)} %get-tuple-element.39), channel_id=1, source_target_pairs={{0,12},{1,13},{2,14},{3,15},{4,8},{5,9},{6,10},{7,11},{8,4},{9,5},... | collective-permute-start | bytes 208904 | tf_op jit(solution)/shard_map/ppermute | solution.py:17
  46.2 11.5 %collective-permute-start.27 = (bf16[272,128]{1,0:T(8,128)(2,1)S(1)}, bf16[272,128]{1,0:T(8,128)(2,1)S(1)}, u32[]{:S(2)}, u32[]{:S(2)}) collective-permute-start(bf16[272,128]{1,0:T(8,128)(2,1)S(1)} %get-tuple-element.40), channel_id=1, source_target_pairs={{0,10},{1,11},{2,8},{3,9},{4,14},{5,15},{6,12},{7,13},{8,2},{9,3},... | collective-permute-start | bytes 208904 | tf_op jit(solution)/shard_map/ppermute | solution.py:17
  47.1 11.1 %collective-permute-start.28 = (bf16[272,128]{1,0:T(8,128)(2,1)S(1)}, bf16[272,128]{1,0:T(8,128)(2,1)S(1)}, u32[]{:S(2)}, u32[]{:S(2)}) collective-permute-start(bf16[272,128]{1,0:T(8,128)(2,1)S(1)} %get-tuple-element.41), channel_id=1, source_target_pairs={{0,8},{1,9},{2,10},{3,11},{4,12},{5,13},{6,14},{7,15},{8,0},{9,1},... | collective-permute-start | bytes 208904 | tf_op jit(solution)/shard_map/ppermute | solution.py:17
  49.6 8.6 %collective-permute-start.29 = (bf16[272,128]{1,0:T(8,128)(2,1)S(1)}, bf16[272,128]{1,0:T(8,128)(2,1)S(1)}, u32[]{:S(2)}, u32[]{:S(2)}) collective-permute-start(bf16[272,128]{1,0:T(8,128)(2,1)S(1)} %get-tuple-element.42), channel_id=1, source_target_pairs={{0,6},{1,7},{2,4},{3,5},{4,2},{5,3},{6,0},{7,1},{8,14},{9,15},{10,... | collective-permute-start | bytes 208904 | tf_op jit(solution)/shard_map/ppermute | solution.py:17
  51.3 6.9 %collective-permute-start.30 = (bf16[272,128]{1,0:T(8,128)(2,1)S(1)}, bf16[272,128]{1,0:T(8,128)(2,1)S(1)}, u32[]{:S(2)}, u32[]{:S(2)}) collective-permute-start(bf16[272,128]{1,0:T(8,128)(2,1)S(1)} %get-tuple-element.43), channel_id=1, source_target_pairs={{0,4},{1,5},{2,6},{3,7},{4,0},{5,1},{6,2},{7,3},{8,12},{9,13},{10,... | collective-permute-start | bytes 208904 | tf_op jit(solution)/shard_map/ppermute | solution.py:17
  52.8 5.5 %collective-permute-start.31 = (bf16[272,128]{1,0:T(8,128)(2,1)S(1)}, bf16[272,128]{1,0:T(8,128)(2,1)S(1)}, u32[]{:S(2)}, u32[]{:S(2)}) collective-permute-start(bf16[272,128]{1,0:T(8,128)(2,1)S(1)} %get-tuple-element.44), channel_id=1, source_target_pairs={{0,2},{1,3},{2,0},{3,1},{4,6},{5,7},{6,4},{7,5},{8,10},{9,11},{10,... | collective-permute-start | bytes 208904 | tf_op jit(solution)/shard_map/ppermute | solution.py:17

commit v20 on v19

--- a/solution.py
+++ b/solution.py
@@ -86,7 +86,7 @@
 
 
 def pairs_of(n):
-    return 69 if fits(n) else 24
+    return 68 if fits(n) else 24
 
 
 def run_of(slots, n):
@@ -219,7 +219,7 @@
     return parts
 
 
-def make_halves(n, plan_ref, left_ref, trial, halves, fetched):
+def make_halves(n, plan_ref, left_ref, trial, halves, fetched, beside):
     turns = plan_ref[5, 1]
     run = run_of(left_ref.shape[0], n)
     chunk = chunk_of(n)
@@ -248,6 +248,7 @@
 
             at = lax.rem(turn, AHEAD)
             pltpu.make_async_copy(left_ref.at[pl.ds(0, chunk)], left.at[at], left_sem.at[at]).wait()
+        beside()
         place = turn * chunk
         for r in range(0, chunk, run):
             source = plan_ref[1, place + r]
@@ -268,23 +269,31 @@
 def tasks_kernel(n, kinds, plan_ref, left_ref, *refs):
     blocks, refs = refs[: 3 * len(kinds)], refs[3 * len(kinds) :]
     far_ref, near_ref, acc, own_ref, halves, trial, right, block_sem, *fetched = refs
-    start, products = make_halves(n, plan_ref, left_ref, trial, halves, fetched)
+    parts = block_parts(n, kinds, blocks, trial, right)
+
+    def clear():
+        for s in range(n):
+            acc[s] = jnp.zeros((256, 128), jnp.float32)
+
+    def beside():
+        if fits(n):
+            clear()
+            for source, to in parts[1::2]:
+                to[...] = source[...]
+
+    start, products = make_halves(n, plan_ref, left_ref, trial, halves, fetched, beside)
     right[right.shape[0] - 1] = jnp.zeros((128, 128), jnp.bfloat16)
     start()
-    parts = block_parts(n, kinds, blocks, trial, right)
     copies = []
-    for index, (source, to) in enumerate(parts):
-        if fits(n):
+    if fits(n):
+        for source, to in parts[0::2]:
             to[...] = source[...]
-        else:
+        pl.when(plan_ref[5, 1] == 0)(clear)
+    else:
+        for index, (source, to) in enumerate(parts):
             copies.append(pltpu.make_async_copy(source, to, block_sem.at[index]))
             copies[-1].start()
-
-    def clear(s, carry):
-        acc[s] = jnp.zeros((256, 128), jnp.float32)
-        return carry
-
-    lax.fori_loop(0, n, clear, 0)
+        clear()
     for copy in copies:
         copy.wait()
     products()

time: 59.1 us -> 58.9 us (level)
  no operation moved by 1% of the time
where the time goes in v20:
time: 58.9 us; the launch traced here: 58.8 us
  starting transfers between devices  32.6 us (55%)
  Pallas kernels  18.2 us (31%)
  waiting for transfers between devices  6.37 us (11%)
  other arithmetic  0.85 us (1%)
  between operations  0.75 us (1%)
    ppermute x12, starting transfers between devices, ring_step(): return lax.ppermute(value, 'op', pairs)  20.4 us
    pallas_call x1, Pallas kernels, run_tasks(): pl.pallas_call(functools.partial(tasks_kernel, n, kinds), out_shape=(jax....  13 us
    ppermute x20, starting transfers between devices, exchange(): return lax.ppermute(value, 'op', [(i, i ^ mask) for i in range(n)])  12.2 us
    ppermute x20, waiting for transfers between devices, exchange(): return lax.ppermute(value, 'op', [(i, i ^ mask) for i in range(n)])  5.59 us
    pallas_call x1, Pallas kernels, make_plan(): pl.pallas_call(functools.partial(stage_kernel, n, terms), in_specs=[hbm,...  3.41 us
  transfers between devices with their start and end apart: 32, of which 8 were waited for; matrix products, arithmetic and copies ran while one was open for 1% of the time, Pallas kernels for 8%

profile of v20, /device:TPU:0, one launch (start us, length us, event | category | flops | bytes accessed | tf_op | source)
XLA Modules:
  0.0 58.8 jit_solution(14669967606052841734)
XLA Ops:
  0.6 0.5 collective-permute-start
  1.2 0.1 collective-permute-start.1
  1.2 3.0 %collective-permute-start.3 = (bf16[4,128,128]{2,1,0:T(8,128)(2,1)}, bf16[4,128,128]{2,1,0:T(8,128)(2,1)S(1)}, u32[]{:S(2)}, u32[]{:S(2)}) collective-permute-start(bf16[4,128,128]{2,1,0:T(8,128)(2,1)} %refs_1_.1), channel_id=1, source_target_pairs={{0,4},{1,3},{4,8},{5,1},{8,12},{9,5},{12,14},{13,9},{14,10},{15,13... | collective-permute-start | bytes 393224 | tf_op jit(solution)/shard_map/ppermute | solution.py:31
  4.2 0.0 collective-permute-done
  4.2 0.9 %pad_maximum_fusion.refs_0_ = bf16[4,128,128]{2,1,0:T(8,128)(2,1)S(1)} fusion(bf16[2,128,128]{2,1,0:T(8,128)(2,1)S(1)} %collective-permute-done, bf16[2,128,128]{2,1,0:T(8,128)(2,1)} %bitcast.3), kind=kLoop, calls=%fused_computation | loop fusion | flops 65536 | bytes 262144 | tf_op jit(solution)/shard_map/concatenate | solution.py:481
  5.1 1.6 %collective-permute-start.2 = (bf16[4,128,128]{2,1,0:T(8,128)(2,1)S(1)}, bf16[4,128,128]{2,1,0:T(8,128)(2,1)S(1)}, u32[]{:S(2)}, u32[]{:S(2)}) collective-permute-start(bf16[4,128,128]{2,1,0:T(8,128)(2,1)S(1)} %pad_maximum_fusion.refs_0_), channel_id=1, source_target_pairs={{0,4},{1,3},{4,8},{5,1},{8,12},{9,5},{12,14},{13,9},{14,10},{15,13... | collective-permute-start | bytes 393224 | tf_op jit(solution)/shard_map/ppermute | solution.py:31
  6.7 0.0 collective-permute-done.1.refs_2_
  6.7 1.6 %collective-permute-start.4 = (bf16[4,128,128]{2,1,0:T(8,128)(2,1)S(1)}, bf16[4,128,128]{2,1,0:T(8,128)(2,1)S(1)}, u32[]{:S(2)}, u32[]{:S(2)}) collective-permute-start(bf16[4,128,128]{2,1,0:T(8,128)(2,1)S(1)} %collective-permute-done.1.refs_2_), channel_id=1, source_target_pairs={{0,4},{1,3},{4,8},{5,1},{8,12},{9,5},{12,14},{13,9},{14,10},{15,13... | collective-permute-start | bytes 393224 | tf_op jit(solution)/shard_map/ppermute | solution.py:31
  8.3 0.0 collective-permute-done.3.refs_4_
  8.3 1.5 %collective-permute-start.9 = (bf16[4,128,128]{2,1,0:T(8,128)(2,1)S(1)}, bf16[4,128,128]{2,1,0:T(8,128)(2,1)S(1)}, u32[]{:S(2)}, u32[]{:S(2)}) collective-permute-start(bf16[4,128,128]{2,1,0:T(8,128)(2,1)S(1)} %collective-permute-done.3.refs_4_), channel_id=1, source_target_pairs={{0,4},{1,3},{4,8},{5,1},{8,12},{9,5},{12,14},{13,9},{14,10},{15,13... | collective-permute-start | bytes 393224 | tf_op jit(solution)/shard_map/ppermute | solution.py:31
  9.8 0.0 collective-permute-start.6
  9.8 0.3 collective-permute-done.2.refs_3_.refs_1_
  10.1 1.6 %collective-permute-start.8 = (bf16[4,128,128]{2,1,0:T(8,128)(2,1)S(1)}, bf16[4,128,128]{2,1,0:T(8,128)(2,1)S(1)}, u32[]{:S(2)}, u32[]{:S(2)}) collective-permute-start(bf16[4,128,128]{2,1,0:T(8,128)(2,1)S(1)} %collective-permute-done.2.refs_3_.refs_1_), channel_id=1, source_target_pairs={{0,4},{1,3},{4,8},{5,1},{8,12},{9,5},{12,14},{13,9},{14,10},{15,13... | collective-permute-start | bytes 393224 | tf_op jit(solution)/shard_map/ppermute | solution.py:31
  11.7 0.0 collective-permute-start.5
  11.7 1.6 %collective-permute-start.10 = (bf16[4,128,128]{2,1,0:T(8,128)(2,1)S(1)}, bf16[4,128,128]{2,1,0:T(8,128)(2,1)S(1)}, u32[]{:S(2)}, u32[]{:S(2)}) collective-permute-start(bf16[4,128,128]{2,1,0:T(8,128)(2,1)S(1)} %collective-permute-done.4.refs_5_), channel_id=1, source_target_pairs={{0,4},{1,3},{4,8},{5,1},{8,12},{9,5},{12,14},{13,9},{14,10},{15,13... | collective-permute-start | bytes 393224 | tf_op jit(solution)/shard_map/ppermute | solution.py:31
  13.3 0.0 collective-permute-start.7
  13.3 0.0 collective-permute-done.6.refs_7_
  13.3 1.6 %collective-permute-start.15 = (bf16[4,128,128]{2,1,0:T(8,128)(2,1)S(1)}, bf16[4,128,128]{2,1,0:T(8,128)(2,1)S(1)}, u32[]{:S(2)}, u32[]{:S(2)}) collective-permute-start(bf16[4,128,128]{2,1,0:T(8,128)(2,1)S(1)} %collective-permute-done.9.refs_10_), channel_id=1, source_target_pairs={{0,4},{1,3},{4,8},{5,1},{8,12},{9,5},{12,14},{13,9},{14,10},{15,13... | collective-permute-start | bytes 393224 | tf_op jit(solution)/shard_map/ppermute | solution.py:31
  14.9 0.2 collective-permute-done.8.refs_9_.refs_3_
  15.1 1.6 %collective-permute-start.14 = (bf16[4,128,128]{2,1,0:T(8,128)(2,1)S(1)}, bf16[4,128,128]{2,1,0:T(8,128)(2,1)S(1)}, u32[]{:S(2)}, u32[]{:S(2)}) collective-permute-start(bf16[4,128,128]{2,1,0:T(8,128)(2,1)S(1)} %collective-permute-done.8.refs_9_.refs_3_), channel_id=1, source_target_pairs={{0,4},{1,3},{4,8},{5,1},{8,12},{9,5},{12,14},{13,9},{14,10},{15,13... | collective-permute-start | bytes 393224 | tf_op jit(solution)/shard_map/ppermute | solution.py:31
  16.7 0.0 collective-permute-done.10.refs_11_
  16.7 0.0 collective-permute-start.11
  16.7 0.0 collective-permute-done.7.refs_8_
  16.7 1.6 %collective-permute-start.16 = (bf16[4,128,128]{2,1,0:T(8,128)(2,1)S(1)}, bf16[4,128,128]{2,1,0:T(8,128)(2,1)S(1)}, u32[]{:S(2)}, u32[]{:S(2)}) collective-permute-start(bf16[4,128,128]{2,1,0:T(8,128)(2,1)S(1)} %collective-permute-done.10.refs_11_), channel_id=1, source_target_pairs={{0,4},{1,3},{4,8},{5,1},{8,12},{9,5},{12,14},{13,9},{14,10},{15,13... | collective-permute-start | bytes 393224 | tf_op jit(solution)/shard_map/ppermute | solution.py:31
  18.3 0.0 collective-permute-done.15.refs_16_
  18.3 0.0 collective-permute-start.13
  18.3 0.0 collective-permute-done.12.refs_13_
  18.3 1.6 %collective-permute-start.21 = (bf16[4,128,128]{2,1,0:T(8,128)(2,1)S(1)}, bf16[4,128,128]{2,1,0:T(8,128)(2,1)S(1)}, u32[]{:S(2)}, u32[]{:S(2)}) collective-permute-start(bf16[4,128,128]{2,1,0:T(8,128)(2,1)S(1)} %collective-permute-done.15.refs_16_), channel_id=1, source_target_pairs={{0,4},{1,3},{4,8},{5,1},{8,12},{9,5},{12,14},{13,9},{14,10},{15,13... | collective-permute-start | bytes 393224 | tf_op jit(solution)/shard_map/ppermute | solution.py:31
  19.9 0.2 collective-permute-done.14.refs_15_.refs_5_
  20.1 0.0 collective-permute-start.18
  20.1 0.0 collective-permute-done.11.refs_12_.refs_4_
  20.1 1.6 %collective-permute-start.20 = (bf16[4,128,128]{2,1,0:T(8,128)(2,1)S(1)}, bf16[4,128,128]{2,1,0:T(8,128)(2,1)S(1)}, u32[]{:S(2)}, u32[]{:S(2)}) collective-permute-start(bf16[4,128,128]{2,1,0:T(8,128)(2,1)S(1)} %collective-permute-done.14.refs_15_.refs_5_), channel_id=1, source_target_pairs={{0,4},{1,3},{4,8},{5,1},{8,12},{9,5},{12,14},{13,9},{14,10},{15,13... | collective-permute-start | bytes 393224 | tf_op jit(solution)/shard_map/ppermute | solution.py:31
  21.6 0.1 collective-permute-done.16.refs_17_
  21.7 0.0 collective-permute-start.17
  21.7 0.0 collective-permute-done.13.refs_14_
  21.7 1.6 %collective-permute-start.22 = (bf16[4,128,128]{2,1,0:T(8,128)(2,1)S(1)}, bf16[4,128,128]{2,1,0:T(8,128)(2,1)S(1)}, u32[]{:S(2)}, u32[]{:S(2)}) collective-permute-start(bf16[4,128,128]{2,1,0:T(8,128)(2,1)S(1)} %collective-permute-done.16.refs_17_), channel_id=1, source_target_pairs={{0,4},{1,3},{4,8},{5,1},{8,12},{9,5},{12,14},{13,9},{14,10},{15,13... | collective-permute-start | bytes 393224 | tf_op jit(solution)/shard_map/ppermute | solution.py:31
  23.3 0.0 collective-permute-done.21.refs_22_
  23.3 0.0 collective-permute-start.19
  23.4 3.4 %shard_map.67 = (s32[6,512]{1,0:T(8,128)S(1)}, bf16[256,128,128]{2,1,0:T(8,128)(2,1)S(1)}) custom-call(s32[4,256]{1,0:T(4,128)} %bitcast.4, bf16[256,128,128]{2,1,0:T(8,128)(2,1)} %left_ref.1), custom_call_target="tpu_custom_call" | custom-call | tf_op jit(solution)/shard_map/pallas_call | solution.py:192
  26.8 0.0 collective-permute-done.18.refs_19_
  26.8 0.0 collective-permute-done.17.refs_18_.refs_6_
  26.8 0.0 collective-permute-done.22.refs_23_
  26.8 13.0 %shard_map.68 = (bf16[1040,128]{1,0:T(8,128)(2,1)S(1)}, bf16[1024,128]{1,0:T(8,128)(2,1)S(1)}, f32[17,256,128]{2,1,0:T(8,128)S(1)}, f32[8,128]{1,0:T(8,128)S(1)}) custom-call(s32[6,512]{1,0:T(8,128)S(1)} %get-tuple-element.29.plan_ref, bf16[256,128,128]{2,1,0:T(8,128)(2,1)S(1)} %get-tuple-element.30.left_ref, ...), custom_call_target="tpu_custom_call" | custom-call | flops 4294967296 | bytes 15588608 | tf_op jit(solution)/shard_map/pallas_call | solution.py:370
  39.8 0.6 collective-permute-start.23
  40.4 0.1 collective-permute-start.24
  40.4 1.1 %collective-permute-done.23.received_ref = bf16[1040,128]{1,0:T(8,128)(2,1)S(1)} collective-permute-done((bf16[1040,128]{1,0:T(8,128)(2,1)S(1)}, bf16[1040,128]{1,0:T(8,128)(2,1)S(1)}, u32[]{:S(2)}, u32[]{:S(2)}) %collective-permute-start.23) | collective-permute-done | bytes 266272 | tf_op jit(solution)/shard_map/ppermute | solution.py:17
  41.5 0.1 shard_map.69
  41.6 4.1 %collective-permute-start.25 = (bf16[272,128]{1,0:T(8,128)(2,1)S(1)}, bf16[272,128]{1,0:T(8,128)(2,1)S(1)}, u32[]{:S(2)}, u32[]{:S(2)}) collective-permute-start(bf16[272,128]{1,0:T(8,128)(2,1)S(1)} %get-tuple-element.38), channel_id=1, source_target_pairs={{0,14},{1,15},{2,12},{3,13},{4,10},{5,11},{6,8},{7,9},{8,6},{9,7},... | collective-permute-start | bytes 208904 | tf_op jit(solution)/shard_map/ppermute | solution.py:17
  45.7 0.4 collective-permute-start.26
  46.0 0.9 %collective-permute-start.27 = (bf16[272,128]{1,0:T(8,128)(2,1)S(1)}, bf16[272,128]{1,0:T(8,128)(2,1)S(1)}, u32[]{:S(2)}, u32[]{:S(2)}) collective-permute-start(bf16[272,128]{1,0:T(8,128)(2,1)S(1)} %get-tuple-element.40), channel_id=1, source_target_pairs={{0,10},{1,11},{2,8},{3,9},{4,14},{5,15},{6,12},{7,13},{8,2},{9,3},... | collective-permute-start | bytes 208904 | tf_op jit(solution)/shard_map/ppermute | solution.py:17
  46.9 2.4 %collective-permute-start.28 = (bf16[272,128]{1,0:T(8,128)(2,1)S(1)}, bf16[272,128]{1,0:T(8,128)(2,1)S(1)}, u32[]{:S(2)}, u32[]{:S(2)}) collective-permute-start(bf16[272,128]{1,0:T(8,128)(2,1)S(1)} %get-tuple-element.41), channel_id=1, source_target_pairs={{0,8},{1,9},{2,10},{3,11},{4,12},{5,13},{6,14},{7,15},{8,0},{9,1},... | collective-permute-start | bytes 208904 | tf_op jit(solution)/shard_map/ppermute | solution.py:17
  49.3 0.0 collective-permute-done.24.received_ref
  49.4 1.7 %collective-permute-start.29 = (bf16[272,128]{1,0:T(8,128)(2,1)S(1)}, bf16[272,128]{1,0:T(8,128)(2,1)S(1)}, u32[]{:S(2)}, u32[]{:S(2)}) collective-permute-start(bf16[272,128]{1,0:T(8,128)(2,1)S(1)} %get-tuple-element.42), channel_id=1, source_target_pairs={{0,6},{1,7},{2,4},{3,5},{4,2},{5,3},{6,0},{7,1},{8,14},{9,15},{10,... | collective-permute-start | bytes 208904 | tf_op jit(solution)/shard_map/ppermute | solution.py:17
  51.1 0.0 collective-permute-done.25.refs_0_
  51.1 0.9 %collective-permute-start.30 = (bf16[272,128]{1,0:T(8,128)(2,1)S(1)}, bf16[272,128]{1,0:T(8,128)(2,1)S(1)}, u32[]{:S(2)}, u32[]{:S(2)}) collective-permute-start(bf16[272,128]{1,0:T(8,128)(2,1)S(1)} %get-tuple-element.43), channel_id=1, source_target_pairs={{0,4},{1,5},{2,6},{3,7},{4,0},{5,1},{6,2},{7,3},{8,12},{9,13},{10,... | collective-permute-start | bytes 208904 | tf_op jit(solution)/shard_map/ppermute | solution.py:17
  52.0 0.6 collective-permute-done.26.refs_1_
  52.6 0.6 collective-permute-start.31
  53.1 1.0 %shard_map.72 = f32[2,2]{1,0:T(2,128)} custom-call(bf16[4,128,128]{2,1,0:T(8,128)(2,1)S(1)} %pad_maximum_fusion.refs_0_, bf16[4,128,128]{2,1,0:T(8,128)(2,1)S(1)} %collective-permute-done.2.refs_3_.refs_1_, bf16[4,128,128]{2,1,0:T(8,128)(2,1)S(1)} %collective-permute-done.5.refs_6_.refs_2_, bf16[4,128,128]{2,1,0:T(8,128)(2,1)S(1)} %collective-permute-done.8.refs_9_.refs_3_, ...), custom_call_target="tpu_custom_call" | custom-call | tf_op jit(solution)/shard_map/pallas_call | solution.py:406
  54.1 3.4 %collective-permute-done.27.refs_2_ = bf16[272,128]{1,0:T(8,128)(2,1)S(1)} collective-permute-done((bf16[272,128]{1,0:T(8,128)(2,1)S(1)}, bf16[272,128]{1,0:T(8,128)(2,1)S(1)}, u32[]{:S(2)}, u32[]{:S(2)}) %collective-permute-start.27) | collective-permute-done | bytes 69664 | tf_op jit(solution)/shard_map/ppermute | solution.py:17
  57.5 0.5 collective-permute-done.28.refs_3_
  58.0 0.0 collective-permute-done.29.refs_4_
  58.0 0.0 collective-permute-done.30.refs_5_
  58.0 0.0 collective-permute-done.31.refs_6_
  58.0 0.7 %shard_map.71 = (f32[1,2,128,128]{3,2,1,0:T(8,128)}, f32[2,2]{1,0:T(2,128)}) custom-call(f32[256,128]{1,0:T(8,128)S(1)} %get-tuple-element.37.mine_ref, f32[16,128]{1,0:T(8,128)S(1)} %get-tuple-element.35.total_ref, bf16[272,128]{1,0:T(8,128)(2,1)S(1)} %collective-permute-done.25.refs_0_, bf16[272,128]{1,0:T(8,128)(2,1)S(1)} %collective-permute-done.26.refs_1_, ...), custom_call_target="tpu_custom_call" | custom-call | tf_op jit(solution)/shard_map/pallas_call | solution.py:468
  (9 shorter events, 0.1 us)
Async XLA Ops:
  0.6 26.2 %copy-start = (bf16[4,128,128]{2,1,0:T(8,128)(2,1)S(1)}, bf16[4,128,128]{2,1,0:T(8,128)(2,1)}, u32[]{:S(2)}) copy-start(bf16[4,128,128]{2,1,0:T(8,128)(2,1)} %refs_1_.1) | copy-start | bytes 393220
  0.6 3.6 %collective-permute-start = (bf16[2,128,128]{2,1,0:T(8,128)(2,1)}, bf16[2,128,128]{2,1,0:T(8,128)(2,1)S(1)}, u32[]{:S(2)}, u32[]{:S(2)}) collective-permute-start(bf16[2,128,128]{2,1,0:T(8,128)(2,1)} %bitcast.2), channel_id=1, source_target_pairs={{0,1},{1,0},{2,3},{3,2},{4,5},{5,4},{6,7},{7,6},{8,9},{9,8},{10,11... | collective-permute-start | bytes 196616 | tf_op jit(solution)/shard_map/ppermute | solution.py:17
  1.2 5.6 %collective-permute-start.1 = (bf16[4,128,128]{2,1,0:T(8,128)(2,1)}, bf16[4,128,128]{2,1,0:T(8,128)(2,1)S(1)}, u32[]{:S(2)}, u32[]{:S(2)}) collective-permute-start(bf16[4,128,128]{2,1,0:T(8,128)(2,1)} %refs_1_.1), channel_id=1, source_target_pairs={{0,1},{1,0},{2,3},{3,2},{4,5},{5,4},{6,7},{7,6},{8,9},{9,8},{10,11... | collective-permute-start | bytes 393224 | tf_op jit(solution)/shard_map/ppermute | solution.py:17
  1.2 7.1 %collective-permute-start.3 = (bf16[4,128,128]{2,1,0:T(8,128)(2,1)}, bf16[4,128,128]{2,1,0:T(8,128)(2,1)S(1)}, u32[]{:S(2)}, u32[]{:S(2)}) collective-permute-start(bf16[4,128,128]{2,1,0:T(8,128)(2,1)} %refs_1_.1), channel_id=1, source_target_pairs={{0,4},{1,3},{4,8},{5,1},{8,12},{9,5},{12,14},{13,9},{14,10},{15,13... | collective-permute-start | bytes 393224 | tf_op jit(solution)/shard_map/ppermute | solution.py:31
  5.1 5.0 %collective-permute-start.2 = (bf16[4,128,128]{2,1,0:T(8,128)(2,1)S(1)}, bf16[4,128,128]{2,1,0:T(8,128)(2,1)S(1)}, u32[]{:S(2)}, u32[]{:S(2)}) collective-permute-start(bf16[4,128,128]{2,1,0:T(8,128)(2,1)S(1)} %pad_maximum_fusion.refs_0_), channel_id=1, source_target_pairs={{0,4},{1,3},{4,8},{5,1},{8,12},{9,5},{12,14},{13,9},{14,10},{15,13... | collective-permute-start | bytes 393224 | tf_op jit(solution)/shard_map/ppermute | solution.py:31
  6.7 5.0 %collective-permute-start.4 = (bf16[4,128,128]{2,1,0:T(8,128)(2,1)S(1)}, bf16[4,128,128]{2,1,0:T(8,128)(2,1)S(1)}, u32[]{:S(2)}, u32[]{:S(2)}) collective-permute-start(bf16[4,128,128]{2,1,0:T(8,128)(2,1)S(1)} %collective-permute-done.1.refs_2_), channel_id=1, source_target_pairs={{0,4},{1,3},{4,8},{5,1},{8,12},{9,5},{12,14},{13,9},{14,10},{15,13... | collective-permute-start | bytes 393224 | tf_op jit(solution)/shard_map/ppermute | solution.py:31
  8.3 5.0 %collective-permute-start.9 = (bf16[4,128,128]{2,1,0:T(8,128)(2,1)S(1)}, bf16[4,128,128]{2,1,0:T(8,128)(2,1)S(1)}, u32[]{:S(2)}, u32[]{:S(2)}) collective-permute-start(bf16[4,128,128]{2,1,0:T(8,128)(2,1)S(1)} %collective-permute-done.3.refs_4_), channel_id=1, source_target_pairs={{0,4},{1,3},{4,8},{5,1},{8,12},{9,5},{12,14},{13,9},{14,10},{15,13... | collective-permute-start | bytes 393224 | tf_op jit(solution)/shard_map/ppermute | solution.py:31
  9.8 3.5 %collective-permute-start.6 = (bf16[4,128,128]{2,1,0:T(8,128)(2,1)S(1)}, bf16[4,128,128]{2,1,0:T(8,128)(2,1)S(1)}, u32[]{:S(2)}, u32[]{:S(2)}) collective-permute-start(bf16[4,128,128]{2,1,0:T(8,128)(2,1)S(1)} %collective-permute-done.3.refs_4_), channel_id=1, source_target_pairs={{0,1},{1,0},{2,3},{3,2},{4,5},{5,4},{6,7},{7,6},{8,9},{9,8},{10,11... | collective-permute-start | bytes 393224 | tf_op jit(solution)/shard_map/ppermute | solution.py:17
  10.1 5.0 %collective-permute-start.8 = (bf16[4,128,128]{2,1,0:T(8,128)(2,1)S(1)}, bf16[4,128,128]{2,1,0:T(8,128)(2,1)S(1)}, u32[]{:S(2)}, u32[]{:S(2)}) collective-permute-start(bf16[4,128,128]{2,1,0:T(8,128)(2,1)S(1)} %collective-permute-done.2.refs_3_.refs_1_), channel_id=1, source_target_pairs={{0,4},{1,3},{4,8},{5,1},{8,12},{9,5},{12,14},{13,9},{14,10},{15,13... | collective-permute-start | bytes 393224 | tf_op jit(solution)/shard_map/ppermute | solution.py:31
  11.7 3.4 %collective-permute-start.5 = (bf16[4,128,128]{2,1,0:T(8,128)(2,1)S(1)}, bf16[4,128,128]{2,1,0:T(8,128)(2,1)S(1)}, u32[]{:S(2)}, u32[]{:S(2)}) collective-permute-start(bf16[4,128,128]{2,1,0:T(8,128)(2,1)S(1)} %collective-permute-done.2.refs_3_.refs_1_), channel_id=1, source_target_pairs={{0,1},{1,0},{2,3},{3,2},{4,5},{5,4},{6,7},{7,6},{8,9},{9,8},{10,11... | collective-permute-start | bytes 393224 | tf_op jit(solution)/shard_map/ppermute | solution.py:17
  11.7 5.0 %collective-permute-start.10 = (bf16[4,128,128]{2,1,0:T(8,128)(2,1)S(1)}, bf16[4,128,128]{2,1,0:T(8,128)(2,1)S(1)}, u32[]{:S(2)}, u32[]{:S(2)}) collective-permute-start(bf16[4,128,128]{2,1,0:T(8,128)(2,1)S(1)} %collective-permute-done.4.refs_5_), channel_id=1, source_target_pairs={{0,4},{1,3},{4,8},{5,1},{8,12},{9,5},{12,14},{13,9},{14,10},{15,13... | collective-permute-start | bytes 393224 | tf_op jit(solution)/shard_map/ppermute | solution.py:31
  13.3 3.4 %collective-permute-start.7 = (bf16[4,128,128]{2,1,0:T(8,128)(2,1)S(1)}, bf16[4,128,128]{2,1,0:T(8,128)(2,1)S(1)}, u32[]{:S(2)}, u32[]{:S(2)}) collective-permute-start(bf16[4,128,128]{2,1,0:T(8,128)(2,1)S(1)} %collective-permute-done.4.refs_5_), channel_id=1, source_target_pairs={{0,1},{1,0},{2,3},{3,2},{4,5},{5,4},{6,7},{7,6},{8,9},{9,8},{10,11... | collective-permute-start | bytes 393224 | tf_op jit(solution)/shard_map/ppermute | solution.py:17
  13.3 5.0 %collective-permute-start.15 = (bf16[4,128,128]{2,1,0:T(8,128)(2,1)S(1)}, bf16[4,128,128]{2,1,0:T(8,128)(2,1)S(1)}, u32[]{:S(2)}, u32[]{:S(2)}) collective-permute-start(bf16[4,128,128]{2,1,0:T(8,128)(2,1)S(1)} %collective-permute-done.9.refs_10_), channel_id=1, source_target_pairs={{0,4},{1,3},{4,8},{5,1},{8,12},{9,5},{12,14},{13,9},{14,10},{15,13... | collective-permute-start | bytes 393224 | tf_op jit(solution)/shard_map/ppermute | solution.py:31
  15.1 3.2 %collective-permute-start.12 = (bf16[4,128,128]{2,1,0:T(8,128)(2,1)S(1)}, bf16[4,128,128]{2,1,0:T(8,128)(2,1)S(1)}, u32[]{:S(2)}, u32[]{:S(2)}) collective-permute-start(bf16[4,128,128]{2,1,0:T(8,128)(2,1)S(1)} %collective-permute-done.9.refs_10_), channel_id=1, source_target_pairs={{0,1},{1,0},{2,3},{3,2},{4,5},{5,4},{6,7},{7,6},{8,9},{9,8},{10,11... | collective-permute-start | bytes 393224 | tf_op jit(solution)/shard_map/ppermute | solution.py:17
  15.1 5.0 %collective-permute-start.14 = (bf16[4,128,128]{2,1,0:T(8,128)(2,1)S(1)}, bf16[4,128,128]{2,1,0:T(8,128)(2,1)S(1)}, u32[]{:S(2)}, u32[]{:S(2)}) collective-permute-start(bf16[4,128,128]{2,1,0:T(8,128)(2,1)S(1)} %collective-permute-done.8.refs_9_.refs_3_), channel_id=1, source_target_pairs={{0,4},{1,3},{4,8},{5,1},{8,12},{9,5},{12,14},{13,9},{14,10},{15,13... | collective-permute-start | bytes 393224 | tf_op jit(solution)/shard_map/ppermute | solution.py:31
  16.7 3.4 %collective-permute-start.11 = (bf16[4,128,128]{2,1,0:T(8,128)(2,1)S(1)}, bf16[4,128,128]{2,1,0:T(8,128)(2,1)S(1)}, u32[]{:S(2)}, u32[]{:S(2)}) collective-permute-start(bf16[4,128,128]{2,1,0:T(8,128)(2,1)S(1)} %collective-permute-done.8.refs_9_.refs_3_), channel_id=1, source_target_pairs={{0,1},{1,0},{2,3},{3,2},{4,5},{5,4},{6,7},{7,6},{8,9},{9,8},{10,11... | collective-permute-start | bytes 393224 | tf_op jit(solution)/shard_map/ppermute | solution.py:17
  16.7 5.0 %collective-permute-start.16 = (bf16[4,128,128]{2,1,0:T(8,128)(2,1)S(1)}, bf16[4,128,128]{2,1,0:T(8,128)(2,1)S(1)}, u32[]{:S(2)}, u32[]{:S(2)}) collective-permute-start(bf16[4,128,128]{2,1,0:T(8,128)(2,1)S(1)} %collective-permute-done.10.refs_11_), channel_id=1, source_target_pairs={{0,4},{1,3},{4,8},{5,1},{8,12},{9,5},{12,14},{13,9},{14,10},{15,13... | collective-permute-start | bytes 393224 | tf_op jit(solution)/shard_map/ppermute | solution.py:31
  18.3 3.4 %collective-permute-start.13 = (bf16[4,128,128]{2,1,0:T(8,128)(2,1)S(1)}, bf16[4,128,128]{2,1,0:T(8,128)(2,1)S(1)}, u32[]{:S(2)}, u32[]{:S(2)}) collective-permute-start(bf16[4,128,128]{2,1,0:T(8,128)(2,1)S(1)} %collective-permute-done.10.refs_11_), channel_id=1, source_target_pairs={{0,1},{1,0},{2,3},{3,2},{4,5},{5,4},{6,7},{7,6},{8,9},{9,8},{10,11... | collective-permute-start | bytes 393224 | tf_op jit(solution)/shard_map/ppermute | solution.py:17
  18.3 5.0 %collective-permute-start.21 = (bf16[4,128,128]{2,1,0:T(8,128)(2,1)S(1)}, bf16[4,128,128]{2,1,0:T(8,128)(2,1)S(1)}, u32[]{:S(2)}, u32[]{:S(2)}) collective-permute-start(bf16[4,128,128]{2,1,0:T(8,128)(2,1)S(1)} %collective-permute-done.15.refs_16_), channel_id=1, source_target_pairs={{0,4},{1,3},{4,8},{5,1},{8,12},{9,5},{12,14},{13,9},{14,10},{15,13... | collective-permute-start | bytes 393224 | tf_op jit(solution)/shard_map/ppermute | solution.py:31
  20.1 6.7 %collective-permute-start.18 = (bf16[4,128,128]{2,1,0:T(8,128)(2,1)S(1)}, bf16[4,128,128]{2,1,0:T(8,128)(2,1)S(1)}, u32[]{:S(2)}, u32[]{:S(2)}) collective-permute-start(bf16[4,128,128]{2,1,0:T(8,128)(2,1)S(1)} %collective-permute-done.15.refs_16_), channel_id=1, source_target_pairs={{0,1},{1,0},{2,3},{3,2},{4,5},{5,4},{6,7},{7,6},{8,9},{9,8},{10,11... | collective-permute-start | bytes 393224 | tf_op jit(solution)/shard_map/ppermute | solution.py:17
  20.1 6.7 %collective-permute-start.20 = (bf16[4,128,128]{2,1,0:T(8,128)(2,1)S(1)}, bf16[4,128,128]{2,1,0:T(8,128)(2,1)S(1)}, u32[]{:S(2)}, u32[]{:S(2)}) collective-permute-start(bf16[4,128,128]{2,1,0:T(8,128)(2,1)S(1)} %collective-permute-done.14.refs_15_.refs_5_), channel_id=1, source_target_pairs={{0,4},{1,3},{4,8},{5,1},{8,12},{9,5},{12,14},{13,9},{14,10},{15,13... | collective-permute-start | bytes 393224 | tf_op jit(solution)/shard_map/ppermute | solution.py:31
  21.7 5.1 %collective-permute-start.17 = (bf16[4,128,128]{2,1,0:T(8,128)(2,1)S(1)}, bf16[4,128,128]{2,1,0:T(8,128)(2,1)S(1)}, u32[]{:S(2)}, u32[]{:S(2)}) collective-permute-start(bf16[4,128,128]{2,1,0:T(8,128)(2,1)S(1)} %collective-permute-done.14.refs_15_.refs_5_), channel_id=1, source_target_pairs={{0,1},{1,0},{2,3},{3,2},{4,5},{5,4},{6,7},{7,6},{8,9},{9,8},{10,11... | collective-permute-start | bytes 393224 | tf_op jit(solution)/shard_map/ppermute | solution.py:17
  21.7 5.1 %collective-permute-start.22 = (bf16[4,128,128]{2,1,0:T(8,128)(2,1)S(1)}, bf16[4,128,128]{2,1,0:T(8,128)(2,1)S(1)}, u32[]{:S(2)}, u32[]{:S(2)}) collective-permute-start(bf16[4,128,128]{2,1,0:T(8,128)(2,1)S(1)} %collective-permute-done.16.refs_17_), channel_id=1, source_target_pairs={{0,4},{1,3},{4,8},{5,1},{8,12},{9,5},{12,14},{13,9},{14,10},{15,13... | collective-permute-start | bytes 393224 | tf_op jit(solution)/shard_map/ppermute | solution.py:31
  23.3 3.5 %collective-permute-start.19 = (bf16[4,128,128]{2,1,0:T(8,128)(2,1)S(1)}, bf16[4,128,128]{2,1,0:T(8,128)(2,1)S(1)}, u32[]{:S(2)}, u32[]{:S(2)}) collective-permute-start(bf16[4,128,128]{2,1,0:T(8,128)(2,1)S(1)} %collective-permute-done.16.refs_17_), channel_id=1, source_target_pairs={{0,1},{1,0},{2,3},{3,2},{4,5},{5,4},{6,7},{7,6},{8,9},{9,8},{10,11... | collective-permute-start | bytes 393224 | tf_op jit(solution)/shard_map/ppermute | solution.py:17
  39.8 1.7 %collective-permute-start.23 = (bf16[1040,128]{1,0:T(8,128)(2,1)S(1)}, bf16[1040,128]{1,0:T(8,128)(2,1)S(1)}, u32[]{:S(2)}, u32[]{:S(2)}) collective-permute-start(bf16[1040,128]{1,0:T(8,128)(2,1)S(1)} %get-tuple-element.34), channel_id=1, source_target_pairs={{0,1},{1,0},{2,3},{3,2},{4,5},{5,4},{6,7},{7,6},{8,9},{9,8},{10,11... | collective-permute-start | bytes 798728 | tf_op jit(solution)/shard_map/ppermute | solution.py:17
  40.4 9.0 %collective-permute-start.24 = (bf16[1024,128]{1,0:T(8,128)(2,1)S(1)}, bf16[1024,128]{1,0:T(8,128)(2,1)S(1)}, u32[]{:S(2)}, u32[]{:S(2)}) collective-permute-start(bf16[1024,128]{1,0:T(8,128)(2,1)S(1)} %get-tuple-element.36), channel_id=1, source_target_pairs={{0,1},{1,0},{2,3},{3,2},{4,5},{5,4},{6,7},{7,6},{8,9},{9,8},{10,11... | collective-permute-start | bytes 786440 | tf_op jit(solution)/shard_map/ppermute | solution.py:17
  41.6 9.5 %collective-permute-start.25 = (bf16[272,128]{1,0:T(8,128)(2,1)S(1)}, bf16[272,128]{1,0:T(8,128)(2,1)S(1)}, u32[]{:S(2)}, u32[]{:S(2)}) collective-permute-start(bf16[272,128]{1,0:T(8,128)(2,1)S(1)} %get-tuple-element.38), channel_id=1, source_target_pairs={{0,14},{1,15},{2,12},{3,13},{4,10},{5,11},{6,8},{7,9},{8,6},{9,7},... | collective-permute-start | bytes 208904 | tf_op jit(solution)/shard_map/ppermute | solution.py:17
  45.7 6.9 %collective-permute-start.26 = (bf16[272,128]{1,0:T(8,128)(2,1)S(1)}, bf16[272,128]{1,0:T(8,128)(2,1)S(1)}, u32[]{:S(2)}, u32[]{:S(2)}) collective-permute-start(bf16[272,128]{1,0:T(8,128)(2,1)S(1)} %get-tuple-element.39), channel_id=1, source_target_pairs={{0,12},{1,13},{2,14},{3,15},{4,8},{5,9},{6,10},{7,11},{8,4},{9,5},... | collective-permute-start | bytes 208904 | tf_op jit(solution)/shard_map/ppermute | solution.py:17
  46.0 11.5 %collective-permute-start.27 = (bf16[272,128]{1,0:T(8,128)(2,1)S(1)}, bf16[272,128]{1,0:T(8,128)(2,1)S(1)}, u32[]{:S(2)}, u32[]{:S(2)}) collective-permute-start(bf16[272,128]{1,0:T(8,128)(2,1)S(1)} %get-tuple-element.40), channel_id=1, source_target_pairs={{0,10},{1,11},{2,8},{3,9},{4,14},{5,15},{6,12},{7,13},{8,2},{9,3},... | collective-permute-start | bytes 208904 | tf_op jit(solution)/shard_map/ppermute | solution.py:17
  46.9 11.1 %collective-permute-start.28 = (bf16[272,128]{1,0:T(8,128)(2,1)S(1)}, bf16[272,128]{1,0:T(8,128)(2,1)S(1)}, u32[]{:S(2)}, u32[]{:S(2)}) collective-permute-start(bf16[272,128]{1,0:T(8,128)(2,1)S(1)} %get-tuple-element.41), channel_id=1, source_target_pairs={{0,8},{1,9},{2,10},{3,11},{4,12},{5,13},{6,14},{7,15},{8,0},{9,1},... | collective-permute-start | bytes 208904 | tf_op jit(solution)/shard_map/ppermute | solution.py:17
  49.4 8.6 %collective-permute-start.29 = (bf16[272,128]{1,0:T(8,128)(2,1)S(1)}, bf16[272,128]{1,0:T(8,128)(2,1)S(1)}, u32[]{:S(2)}, u32[]{:S(2)}) collective-permute-start(bf16[272,128]{1,0:T(8,128)(2,1)S(1)} %get-tuple-element.42), channel_id=1, source_target_pairs={{0,6},{1,7},{2,4},{3,5},{4,2},{5,3},{6,0},{7,1},{8,14},{9,15},{10,... | collective-permute-start | bytes 208904 | tf_op jit(solution)/shard_map/ppermute | solution.py:17
  51.1 6.9 %collective-permute-start.30 = (bf16[272,128]{1,0:T(8,128)(2,1)S(1)}, bf16[272,128]{1,0:T(8,128)(2,1)S(1)}, u32[]{:S(2)}, u32[]{:S(2)}) collective-permute-start(bf16[272,128]{1,0:T(8,128)(2,1)S(1)} %get-tuple-element.43), channel_id=1, source_target_pairs={{0,4},{1,5},{2,6},{3,7},{4,0},{5,1},{6,2},{7,3},{8,12},{9,13},{10,... | collective-permute-start | bytes 208904 | tf_op jit(solution)/shard_map/ppermute | solution.py:17
  52.6 5.5 %collective-permute-start.31 = (bf16[272,128]{1,0:T(8,128)(2,1)S(1)}, bf16[272,128]{1,0:T(8,128)(2,1)S(1)}, u32[]{:S(2)}, u32[]{:S(2)}) collective-permute-start(bf16[272,128]{1,0:T(8,128)(2,1)S(1)} %get-tuple-element.44), channel_id=1, source_target_pairs={{0,2},{1,3},{2,0},{3,1},{4,6},{5,7},{6,4},{7,5},{8,10},{9,11},{10,... | collective-permute-start | bytes 208904 | tf_op jit(solution)/shard_map/ppermute | solution.py:17

commit v21 on v20

--- a/solution.py
+++ b/solution.py
@@ -332,7 +332,7 @@
         return p00 + fold(t0 * a0), p01 + fold(t0 * a1), p10 + fold(t1 * a0), p11 + fold(t1 * a1)
 
     zero = jnp.zeros((8, 128), jnp.float32)
-    sums = lax.fori_loop(0, n, dots, (zero,) * 4, unroll=8)
+    sums = lax.fori_loop(0, n, dots, (zero,) * 4, unroll=16)
     p00, p01, p10, p11 = [jnp.sum(x) for x in sums]
 
     chips = n // 2
@@ -351,7 +351,7 @@
 
         return carry
 
-    lax.fori_loop(0, chips, pack, 0, unroll=2)
+    lax.fori_loop(0, chips, pack, 0, unroll=8)
     own = split3(matrix_of({(0, 0): p00, (0, 1): p01, (1, 0): p10, (1, 1): p11}, 3))
     own_ref[...] = own
     far_ref[(chips - near) * 256 :, :] = tail_of(own, jnp.zeros_like(own))

time: 58.9 us -> 58.9 us (level)
  no operation moved by 1% of the time
where the time goes in v21:
time: 58.9 us; the launch traced here: 58.7 us
  starting transfers between devices  32.6 us (55%)
  Pallas kernels  18.1 us (31%)
  waiting for transfers between devices  6.37 us (11%)
  other arithmetic  0.85 us (1%)
  between operations  0.75 us (1%)
    ppermute x12, starting transfers between devices, ring_step(): return lax.ppermute(value, 'op', pairs)  20.4 us
    pallas_call x1, Pallas kernels, run_tasks(): pl.pallas_call(functools.partial(tasks_kernel, n, kinds), out_shape=(jax....  12.9 us
    ppermute x20, starting transfers between devices, exchange(): return lax.ppermute(value, 'op', [(i, i ^ mask) for i in range(n)])  12.2 us
    ppermute x20, waiting for transfers between devices, exchange(): return lax.ppermute(value, 'op', [(i, i ^ mask) for i in range(n)])  5.59 us
    pallas_call x1, Pallas kernels, make_plan(): pl.pallas_call(functools.partial(stage_kernel, n, terms), in_specs=[hbm,...  3.41 us
  transfers between devices with their start and end apart: 32, of which 8 were waited for; matrix products, arithmetic and copies ran while one was open for 1% of the time, Pallas kernels for 8%

profile of v21, /device:TPU:0, one launch (start us, length us, event | category | flops | bytes accessed | tf_op | source)
XLA Modules:
  0.0 58.7 jit_solution(15802526122084893861)
XLA Ops:
  0.6 0.5 collective-permute-start
  1.2 0.1 collective-permute-start.1
  1.2 3.0 %collective-permute-start.3 = (bf16[4,128,128]{2,1,0:T(8,128)(2,1)}, bf16[4,128,128]{2,1,0:T(8,128)(2,1)S(1)}, u32[]{:S(2)}, u32[]{:S(2)}) collective-permute-start(bf16[4,128,128]{2,1,0:T(8,128)(2,1)} %refs_1_.1), channel_id=1, source_target_pairs={{0,4},{1,3},{4,8},{5,1},{8,12},{9,5},{12,14},{13,9},{14,10},{15,13... | collective-permute-start | bytes 393224 | tf_op jit(solution)/shard_map/ppermute | solution.py:31
  4.2 0.0 collective-permute-done
  4.2 0.9 %pad_maximum_fusion.refs_0_ = bf16[4,128,128]{2,1,0:T(8,128)(2,1)S(1)} fusion(bf16[2,128,128]{2,1,0:T(8,128)(2,1)S(1)} %collective-permute-done, bf16[2,128,128]{2,1,0:T(8,128)(2,1)} %bitcast.3), kind=kLoop, calls=%fused_computation | loop fusion | flops 65536 | bytes 262144 | tf_op jit(solution)/shard_map/concatenate | solution.py:481
  5.1 1.6 %collective-permute-start.2 = (bf16[4,128,128]{2,1,0:T(8,128)(2,1)S(1)}, bf16[4,128,128]{2,1,0:T(8,128)(2,1)S(1)}, u32[]{:S(2)}, u32[]{:S(2)}) collective-permute-start(bf16[4,128,128]{2,1,0:T(8,128)(2,1)S(1)} %pad_maximum_fusion.refs_0_), channel_id=1, source_target_pairs={{0,4},{1,3},{4,8},{5,1},{8,12},{9,5},{12,14},{13,9},{14,10},{15,13... | collective-permute-start | bytes 393224 | tf_op jit(solution)/shard_map/ppermute | solution.py:31
  6.7 0.0 collective-permute-done.1.refs_2_
  6.7 1.6 %collective-permute-start.4 = (bf16[4,128,128]{2,1,0:T(8,128)(2,1)S(1)}, bf16[4,128,128]{2,1,0:T(8,128)(2,1)S(1)}, u32[]{:S(2)}, u32[]{:S(2)}) collective-permute-start(bf16[4,128,128]{2,1,0:T(8,128)(2,1)S(1)} %collective-permute-done.1.refs_2_), channel_id=1, source_target_pairs={{0,4},{1,3},{4,8},{5,1},{8,12},{9,5},{12,14},{13,9},{14,10},{15,13... | collective-permute-start | bytes 393224 | tf_op jit(solution)/shard_map/ppermute | solution.py:31
  8.3 0.0 collective-permute-done.3.refs_4_
  8.3 1.5 %collective-permute-start.9 = (bf16[4,128,128]{2,1,0:T(8,128)(2,1)S(1)}, bf16[4,128,128]{2,1,0:T(8,128)(2,1)S(1)}, u32[]{:S(2)}, u32[]{:S(2)}) collective-permute-start(bf16[4,128,128]{2,1,0:T(8,128)(2,1)S(1)} %collective-permute-done.3.refs_4_), channel_id=1, source_target_pairs={{0,4},{1,3},{4,8},{5,1},{8,12},{9,5},{12,14},{13,9},{14,10},{15,13... | collective-permute-start | bytes 393224 | tf_op jit(solution)/shard_map/ppermute | solution.py:31
  9.8 0.0 collective-permute-start.6
  9.8 0.3 collective-permute-done.2.refs_3_.refs_1_
  10.1 1.6 %collective-permute-start.8 = (bf16[4,128,128]{2,1,0:T(8,128)(2,1)S(1)}, bf16[4,128,128]{2,1,0:T(8,128)(2,1)S(1)}, u32[]{:S(2)}, u32[]{:S(2)}) collective-permute-start(bf16[4,128,128]{2,1,0:T(8,128)(2,1)S(1)} %collective-permute-done.2.refs_3_.refs_1_), channel_id=1, source_target_pairs={{0,4},{1,3},{4,8},{5,1},{8,12},{9,5},{12,14},{13,9},{14,10},{15,13... | collective-permute-start | bytes 393224 | tf_op jit(solution)/shard_map/ppermute | solution.py:31
  11.7 0.0 collective-permute-start.5
  11.7 0.0 collective-permute-done.4.refs_5_
  11.7 1.6 %collective-permute-start.10 = (bf16[4,128,128]{2,1,0:T(8,128)(2,1)S(1)}, bf16[4,128,128]{2,1,0:T(8,128)(2,1)S(1)}, u32[]{:S(2)}, u32[]{:S(2)}) collective-permute-start(bf16[4,128,128]{2,1,0:T(8,128)(2,1)S(1)} %collective-permute-done.4.refs_5_), channel_id=1, source_target_pairs={{0,4},{1,3},{4,8},{5,1},{8,12},{9,5},{12,14},{13,9},{14,10},{15,13... | collective-permute-start | bytes 393224 | tf_op jit(solution)/shard_map/ppermute | solution.py:31
  13.3 0.0 collective-permute-done.9.refs_10_
  13.3 0.0 collective-permute-start.7
  13.3 0.0 collective-permute-done.6.refs_7_
  13.3 1.6 %collective-permute-start.15 = (bf16[4,128,128]{2,1,0:T(8,128)(2,1)S(1)}, bf16[4,128,128]{2,1,0:T(8,128)(2,1)S(1)}, u32[]{:S(2)}, u32[]{:S(2)}) collective-permute-start(bf16[4,128,128]{2,1,0:T(8,128)(2,1)S(1)} %collective-permute-done.9.refs_10_), channel_id=1, source_target_pairs={{0,4},{1,3},{4,8},{5,1},{8,12},{9,5},{12,14},{13,9},{14,10},{15,13... | collective-permute-start | bytes 393224 | tf_op jit(solution)/shard_map/ppermute | solution.py:31
  14.9 0.2 collective-permute-done.8.refs_9_.refs_3_
  15.1 0.0 collective-permute-start.12
  15.1 0.0 collective-permute-done.5.refs_6_.refs_2_
  15.1 1.6 %collective-permute-start.14 = (bf16[4,128,128]{2,1,0:T(8,128)(2,1)S(1)}, bf16[4,128,128]{2,1,0:T(8,128)(2,1)S(1)}, u32[]{:S(2)}, u32[]{:S(2)}) collective-permute-start(bf16[4,128,128]{2,1,0:T(8,128)(2,1)S(1)} %collective-permute-done.8.refs_9_.refs_3_), channel_id=1, source_target_pairs={{0,4},{1,3},{4,8},{5,1},{8,12},{9,5},{12,14},{13,9},{14,10},{15,13... | collective-permute-start | bytes 393224 | tf_op jit(solution)/shard_map/ppermute | solution.py:31
  16.7 0.0 collective-permute-done.10.refs_11_
  16.7 0.0 collective-permute-start.11
  16.7 0.0 collective-permute-done.7.refs_8_
  16.7 1.6 %collective-permute-start.16 = (bf16[4,128,128]{2,1,0:T(8,128)(2,1)S(1)}, bf16[4,128,128]{2,1,0:T(8,128)(2,1)S(1)}, u32[]{:S(2)}, u32[]{:S(2)}) collective-permute-start(bf16[4,128,128]{2,1,0:T(8,128)(2,1)S(1)} %collective-permute-done.10.refs_11_), channel_id=1, source_target_pairs={{0,4},{1,3},{4,8},{5,1},{8,12},{9,5},{12,14},{13,9},{14,10},{15,13... | collective-permute-start | bytes 393224 | tf_op jit(solution)/shard_map/ppermute | solution.py:31
  18.3 0.0 collective-permute-done.15.refs_16_
  18.3 0.0 collective-permute-start.13
  18.3 0.0 collective-permute-done.12.refs_13_
  18.3 1.6 %collective-permute-start.21 = (bf16[4,128,128]{2,1,0:T(8,128)(2,1)S(1)}, bf16[4,128,128]{2,1,0:T(8,128)(2,1)S(1)}, u32[]{:S(2)}, u32[]{:S(2)}) collective-permute-start(bf16[4,128,128]{2,1,0:T(8,128)(2,1)S(1)} %collective-permute-done.15.refs_16_), channel_id=1, source_target_pairs={{0,4},{1,3},{4,8},{5,1},{8,12},{9,5},{12,14},{13,9},{14,10},{15,13... | collective-permute-start | bytes 393224 | tf_op jit(solution)/shard_map/ppermute | solution.py:31
  19.9 0.2 collective-permute-done.14.refs_15_.refs_5_
  20.1 0.0 collective-permute-start.18
  20.1 0.0 collective-permute-done.11.refs_12_.refs_4_
  20.1 1.6 %collective-permute-start.20 = (bf16[4,128,128]{2,1,0:T(8,128)(2,1)S(1)}, bf16[4,128,128]{2,1,0:T(8,128)(2,1)S(1)}, u32[]{:S(2)}, u32[]{:S(2)}) collective-permute-start(bf16[4,128,128]{2,1,0:T(8,128)(2,1)S(1)} %collective-permute-done.14.refs_15_.refs_5_), channel_id=1, source_target_pairs={{0,4},{1,3},{4,8},{5,1},{8,12},{9,5},{12,14},{13,9},{14,10},{15,13... | collective-permute-start | bytes 393224 | tf_op jit(solution)/shard_map/ppermute | solution.py:31
  21.6 0.1 collective-permute-done.16.refs_17_
  21.7 0.0 collective-permute-start.17
  21.7 0.0 collective-permute-done.13.refs_14_
  21.7 1.6 %collective-permute-start.22 = (bf16[4,128,128]{2,1,0:T(8,128)(2,1)S(1)}, bf16[4,128,128]{2,1,0:T(8,128)(2,1)S(1)}, u32[]{:S(2)}, u32[]{:S(2)}) collective-permute-start(bf16[4,128,128]{2,1,0:T(8,128)(2,1)S(1)} %collective-permute-done.16.refs_17_), channel_id=1, source_target_pairs={{0,4},{1,3},{4,8},{5,1},{8,12},{9,5},{12,14},{13,9},{14,10},{15,13... | collective-permute-start | bytes 393224 | tf_op jit(solution)/shard_map/ppermute | solution.py:31
  23.3 0.0 collective-permute-done.21.refs_22_
  23.3 0.0 collective-permute-start.19
  23.4 3.4 %shard_map.67 = (s32[6,512]{1,0:T(8,128)S(1)}, bf16[256,128,128]{2,1,0:T(8,128)(2,1)S(1)}) custom-call(s32[4,256]{1,0:T(4,128)} %bitcast.4, bf16[256,128,128]{2,1,0:T(8,128)(2,1)} %left_ref.1), custom_call_target="tpu_custom_call" | custom-call | tf_op jit(solution)/shard_map/pallas_call | solution.py:192
  26.8 0.0 collective-permute-done.18.refs_19_
  26.8 0.0 collective-permute-done.17.refs_18_.refs_6_
  26.8 0.0 collective-permute-done.22.refs_23_
  26.8 12.9 %shard_map.68 = (bf16[1040,128]{1,0:T(8,128)(2,1)S(1)}, bf16[1024,128]{1,0:T(8,128)(2,1)S(1)}, f32[17,256,128]{2,1,0:T(8,128)S(1)}, f32[8,128]{1,0:T(8,128)S(1)}) custom-call(s32[6,512]{1,0:T(8,128)S(1)} %get-tuple-element.29.plan_ref, bf16[256,128,128]{2,1,0:T(8,128)(2,1)S(1)} %get-tuple-element.30.left_ref, ...), custom_call_target="tpu_custom_call" | custom-call | flops 4294967296 | bytes 15588608 | tf_op jit(solution)/shard_map/pallas_call | solution.py:370
  39.8 0.6 collective-permute-start.23
  40.3 0.1 collective-permute-start.24
  40.4 1.1 %collective-permute-done.23.received_ref = bf16[1040,128]{1,0:T(8,128)(2,1)S(1)} collective-permute-done((bf16[1040,128]{1,0:T(8,128)(2,1)S(1)}, bf16[1040,128]{1,0:T(8,128)(2,1)S(1)}, u32[]{:S(2)}, u32[]{:S(2)}) %collective-permute-start.23) | collective-permute-done | bytes 266272 | tf_op jit(solution)/shard_map/ppermute | solution.py:17
  41.5 0.1 shard_map.69
  41.5 4.1 %collective-permute-start.25 = (bf16[272,128]{1,0:T(8,128)(2,1)S(1)}, bf16[272,128]{1,0:T(8,128)(2,1)S(1)}, u32[]{:S(2)}, u32[]{:S(2)}) collective-permute-start(bf16[272,128]{1,0:T(8,128)(2,1)S(1)} %get-tuple-element.38), channel_id=1, source_target_pairs={{0,14},{1,15},{2,12},{3,13},{4,10},{5,11},{6,8},{7,9},{8,6},{9,7},... | collective-permute-start | bytes 208904 | tf_op jit(solution)/shard_map/ppermute | solution.py:17
  45.6 0.4 collective-permute-start.26
  46.0 0.9 %collective-permute-start.27 = (bf16[272,128]{1,0:T(8,128)(2,1)S(1)}, bf16[272,128]{1,0:T(8,128)(2,1)S(1)}, u32[]{:S(2)}, u32[]{:S(2)}) collective-permute-start(bf16[272,128]{1,0:T(8,128)(2,1)S(1)} %get-tuple-element.40), channel_id=1, source_target_pairs={{0,10},{1,11},{2,8},{3,9},{4,14},{5,15},{6,12},{7,13},{8,2},{9,3},... | collective-permute-start | bytes 208904 | tf_op jit(solution)/shard_map/ppermute | solution.py:17
  46.9 2.4 %collective-permute-start.28 = (bf16[272,128]{1,0:T(8,128)(2,1)S(1)}, bf16[272,128]{1,0:T(8,128)(2,1)S(1)}, u32[]{:S(2)}, u32[]{:S(2)}) collective-permute-start(bf16[272,128]{1,0:T(8,128)(2,1)S(1)} %get-tuple-element.41), channel_id=1, source_target_pairs={{0,8},{1,9},{2,10},{3,11},{4,12},{5,13},{6,14},{7,15},{8,0},{9,1},... | collective-permute-start | bytes 208904 | tf_op jit(solution)/shard_map/ppermute | solution.py:17
  49.3 1.7 %collective-permute-start.29 = (bf16[272,128]{1,0:T(8,128)(2,1)S(1)}, bf16[272,128]{1,0:T(8,128)(2,1)S(1)}, u32[]{:S(2)}, u32[]{:S(2)}) collective-permute-start(bf16[272,128]{1,0:T(8,128)(2,1)S(1)} %get-tuple-element.42), channel_id=1, source_target_pairs={{0,6},{1,7},{2,4},{3,5},{4,2},{5,3},{6,0},{7,1},{8,14},{9,15},{10,... | collective-permute-start | bytes 208904 | tf_op jit(solution)/shard_map/ppermute | solution.py:17
  51.0 0.0 collective-permute-done.25.refs_0_
  51.0 0.9 %collective-permute-start.30 = (bf16[272,128]{1,0:T(8,128)(2,1)S(1)}, bf16[272,128]{1,0:T(8,128)(2,1)S(1)}, u32[]{:S(2)}, u32[]{:S(2)}) collective-permute-start(bf16[272,128]{1,0:T(8,128)(2,1)S(1)} %get-tuple-element.43), channel_id=1, source_target_pairs={{0,4},{1,5},{2,6},{3,7},{4,0},{5,1},{6,2},{7,3},{8,12},{9,13},{10,... | collective-permute-start | bytes 208904 | tf_op jit(solution)/shard_map/ppermute | solution.py:17
  52.0 0.6 collective-permute-done.26.refs_1_
  52.5 0.6 collective-permute-start.31
  53.1 1.0 %shard_map.72 = f32[2,2]{1,0:T(2,128)} custom-call(bf16[4,128,128]{2,1,0:T(8,128)(2,1)S(1)} %pad_maximum_fusion.refs_0_, bf16[4,128,128]{2,1,0:T(8,128)(2,1)S(1)} %collective-permute-done.2.refs_3_.refs_1_, bf16[4,128,128]{2,1,0:T(8,128)(2,1)S(1)} %collective-permute-done.5.refs_6_.refs_2_, bf16[4,128,128]{2,1,0:T(8,128)(2,1)S(1)} %collective-permute-done.8.refs_9_.refs_3_, ...), custom_call_target="tpu_custom_call" | custom-call | tf_op jit(solution)/shard_map/pallas_call | solution.py:406
  54.1 3.4 %collective-permute-done.27.refs_2_ = bf16[272,128]{1,0:T(8,128)(2,1)S(1)} collective-permute-done((bf16[272,128]{1,0:T(8,128)(2,1)S(1)}, bf16[272,128]{1,0:T(8,128)(2,1)S(1)}, u32[]{:S(2)}, u32[]{:S(2)}) %collective-permute-start.27) | collective-permute-done | bytes 69664 | tf_op jit(solution)/shard_map/ppermute | solution.py:17
  57.4 0.5 collective-permute-done.28.refs_3_
  58.0 0.7 %shard_map.71 = (f32[1,2,128,128]{3,2,1,0:T(8,128)}, f32[2,2]{1,0:T(2,128)}) custom-call(f32[256,128]{1,0:T(8,128)S(1)} %get-tuple-element.37.mine_ref, f32[16,128]{1,0:T(8,128)S(1)} %get-tuple-element.35.total_ref, bf16[272,128]{1,0:T(8,128)(2,1)S(1)} %collective-permute-done.25.refs_0_, bf16[272,128]{1,0:T(8,128)(2,1)S(1)} %collective-permute-done.26.refs_1_, ...), custom_call_target="tpu_custom_call" | custom-call | tf_op jit(solution)/shard_map/pallas_call | solution.py:468
  (9 shorter events, 0.1 us)
Async XLA Ops:
  0.6 26.2 %copy-start = (bf16[4,128,128]{2,1,0:T(8,128)(2,1)S(1)}, bf16[4,128,128]{2,1,0:T(8,128)(2,1)}, u32[]{:S(2)}) copy-start(bf16[4,128,128]{2,1,0:T(8,128)(2,1)} %refs_1_.1) | copy-start | bytes 393220
  0.6 3.6 %collective-permute-start = (bf16[2,128,128]{2,1,0:T(8,128)(2,1)}, bf16[2,128,128]{2,1,0:T(8,128)(2,1)S(1)}, u32[]{:S(2)}, u32[]{:S(2)}) collective-permute-start(bf16[2,128,128]{2,1,0:T(8,128)(2,1)} %bitcast.2), channel_id=1, source_target_pairs={{0,1},{1,0},{2,3},{3,2},{4,5},{5,4},{6,7},{7,6},{8,9},{9,8},{10,11... | collective-permute-start | bytes 196616 | tf_op jit(solution)/shard_map/ppermute | solution.py:17
  1.2 5.6 %collective-permute-start.1 = (bf16[4,128,128]{2,1,0:T(8,128)(2,1)}, bf16[4,128,128]{2,1,0:T(8,128)(2,1)S(1)}, u32[]{:S(2)}, u32[]{:S(2)}) collective-permute-start(bf16[4,128,128]{2,1,0:T(8,128)(2,1)} %refs_1_.1), channel_id=1, source_target_pairs={{0,1},{1,0},{2,3},{3,2},{4,5},{5,4},{6,7},{7,6},{8,9},{9,8},{10,11... | collective-permute-start | bytes 393224 | tf_op jit(solution)/shard_map/ppermute | solution.py:17
  1.2 7.1 %collective-permute-start.3 = (bf16[4,128,128]{2,1,0:T(8,128)(2,1)}, bf16[4,128,128]{2,1,0:T(8,128)(2,1)S(1)}, u32[]{:S(2)}, u32[]{:S(2)}) collective-permute-start(bf16[4,128,128]{2,1,0:T(8,128)(2,1)} %refs_1_.1), channel_id=1, source_target_pairs={{0,4},{1,3},{4,8},{5,1},{8,12},{9,5},{12,14},{13,9},{14,10},{15,13... | collective-permute-start | bytes 393224 | tf_op jit(solution)/shard_map/ppermute | solution.py:31
  5.1 5.0 %collective-permute-start.2 = (bf16[4,128,128]{2,1,0:T(8,128)(2,1)S(1)}, bf16[4,128,128]{2,1,0:T(8,128)(2,1)S(1)}, u32[]{:S(2)}, u32[]{:S(2)}) collective-permute-start(bf16[4,128,128]{2,1,0:T(8,128)(2,1)S(1)} %pad_maximum_fusion.refs_0_), channel_id=1, source_target_pairs={{0,4},{1,3},{4,8},{5,1},{8,12},{9,5},{12,14},{13,9},{14,10},{15,13... | collective-permute-start | bytes 393224 | tf_op jit(solution)/shard_map/ppermute | solution.py:31
  6.7 5.0 %collective-permute-start.4 = (bf16[4,128,128]{2,1,0:T(8,128)(2,1)S(1)}, bf16[4,128,128]{2,1,0:T(8,128)(2,1)S(1)}, u32[]{:S(2)}, u32[]{:S(2)}) collective-permute-start(bf16[4,128,128]{2,1,0:T(8,128)(2,1)S(1)} %collective-permute-done.1.refs_2_), channel_id=1, source_target_pairs={{0,4},{1,3},{4,8},{5,1},{8,12},{9,5},{12,14},{13,9},{14,10},{15,13... | collective-permute-start | bytes 393224 | tf_op jit(solution)/shard_map/ppermute | solution.py:31
  8.3 5.0 %collective-permute-start.9 = (bf16[4,128,128]{2,1,0:T(8,128)(2,1)S(1)}, bf16[4,128,128]{2,1,0:T(8,128)(2,1)S(1)}, u32[]{:S(2)}, u32[]{:S(2)}) collective-permute-start(bf16[4,128,128]{2,1,0:T(8,128)(2,1)S(1)} %collective-permute-done.3.refs_4_), channel_id=1, source_target_pairs={{0,4},{1,3},{4,8},{5,1},{8,12},{9,5},{12,14},{13,9},{14,10},{15,13... | collective-permute-start | bytes 393224 | tf_op jit(solution)/shard_map/ppermute | solution.py:31
  9.8 3.5 %collective-permute-start.6 = (bf16[4,128,128]{2,1,0:T(8,128)(2,1)S(1)}, bf16[4,128,128]{2,1,0:T(8,128)(2,1)S(1)}, u32[]{:S(2)}, u32[]{:S(2)}) collective-permute-start(bf16[4,128,128]{2,1,0:T(8,128)(2,1)S(1)} %collective-permute-done.3.refs_4_), channel_id=1, source_target_pairs={{0,1},{1,0},{2,3},{3,2},{4,5},{5,4},{6,7},{7,6},{8,9},{9,8},{10,11... | collective-permute-start | bytes 393224 | tf_op jit(solution)/shard_map/ppermute | solution.py:17
  10.1 5.0 %collective-permute-start.8 = (bf16[4,128,128]{2,1,0:T(8,128)(2,1)S(1)}, bf16[4,128,128]{2,1,0:T(8,128)(2,1)S(1)}, u32[]{:S(2)}, u32[]{:S(2)}) collective-permute-start(bf16[4,128,128]{2,1,0:T(8,128)(2,1)S(1)} %collective-permute-done.2.refs_3_.refs_1_), channel_id=1, source_target_pairs={{0,4},{1,3},{4,8},{5,1},{8,12},{9,5},{12,14},{13,9},{14,10},{15,13... | collective-permute-start | bytes 393224 | tf_op jit(solution)/shard_map/ppermute | solution.py:31
  11.7 3.4 %collective-permute-start.5 = (bf16[4,128,128]{2,1,0:T(8,128)(2,1)S(1)}, bf16[4,128,128]{2,1,0:T(8,128)(2,1)S(1)}, u32[]{:S(2)}, u32[]{:S(2)}) collective-permute-start(bf16[4,128,128]{2,1,0:T(8,128)(2,1)S(1)} %collective-permute-done.2.refs_3_.refs_1_), channel_id=1, source_target_pairs={{0,1},{1,0},{2,3},{3,2},{4,5},{5,4},{6,7},{7,6},{8,9},{9,8},{10,11... | collective-permute-start | bytes 393224 | tf_op jit(solution)/shard_map/ppermute | solution.py:17
  11.7 5.0 %collective-permute-start.10 = (bf16[4,128,128]{2,1,0:T(8,128)(2,1)S(1)}, bf16[4,128,128]{2,1,0:T(8,128)(2,1)S(1)}, u32[]{:S(2)}, u32[]{:S(2)}) collective-permute-start(bf16[4,128,128]{2,1,0:T(8,128)(2,1)S(1)} %collective-permute-done.4.refs_5_), channel_id=1, source_target_pairs={{0,4},{1,3},{4,8},{5,1},{8,12},{9,5},{12,14},{13,9},{14,10},{15,13... | collective-permute-start | bytes 393224 | tf_op jit(solution)/shard_map/ppermute | solution.py:31
  13.3 3.4 %collective-permute-start.7 = (bf16[4,128,128]{2,1,0:T(8,128)(2,1)S(1)}, bf16[4,128,128]{2,1,0:T(8,128)(2,1)S(1)}, u32[]{:S(2)}, u32[]{:S(2)}) collective-permute-start(bf16[4,128,128]{2,1,0:T(8,128)(2,1)S(1)} %collective-permute-done.4.refs_5_), channel_id=1, source_target_pairs={{0,1},{1,0},{2,3},{3,2},{4,5},{5,4},{6,7},{7,6},{8,9},{9,8},{10,11... | collective-permute-start | bytes 393224 | tf_op jit(solution)/shard_map/ppermute | solution.py:17
  13.3 5.0 %collective-permute-start.15 = (bf16[4,128,128]{2,1,0:T(8,128)(2,1)S(1)}, bf16[4,128,128]{2,1,0:T(8,128)(2,1)S(1)}, u32[]{:S(2)}, u32[]{:S(2)}) collective-permute-start(bf16[4,128,128]{2,1,0:T(8,128)(2,1)S(1)} %collective-permute-done.9.refs_10_), channel_id=1, source_target_pairs={{0,4},{1,3},{4,8},{5,1},{8,12},{9,5},{12,14},{13,9},{14,10},{15,13... | collective-permute-start | bytes 393224 | tf_op jit(solution)/shard_map/ppermute | solution.py:31
  15.1 3.2 %collective-permute-start.12 = (bf16[4,128,128]{2,1,0:T(8,128)(2,1)S(1)}, bf16[4,128,128]{2,1,0:T(8,128)(2,1)S(1)}, u32[]{:S(2)}, u32[]{:S(2)}) collective-permute-start(bf16[4,128,128]{2,1,0:T(8,128)(2,1)S(1)} %collective-permute-done.9.refs_10_), channel_id=1, source_target_pairs={{0,1},{1,0},{2,3},{3,2},{4,5},{5,4},{6,7},{7,6},{8,9},{9,8},{10,11... | collective-permute-start | bytes 393224 | tf_op jit(solution)/shard_map/ppermute | solution.py:17
  15.1 5.0 %collective-permute-start.14 = (bf16[4,128,128]{2,1,0:T(8,128)(2,1)S(1)}, bf16[4,128,128]{2,1,0:T(8,128)(2,1)S(1)}, u32[]{:S(2)}, u32[]{:S(2)}) collective-permute-start(bf16[4,128,128]{2,1,0:T(8,128)(2,1)S(1)} %collective-permute-done.8.refs_9_.refs_3_), channel_id=1, source_target_pairs={{0,4},{1,3},{4,8},{5,1},{8,12},{9,5},{12,14},{13,9},{14,10},{15,13... | collective-permute-start | bytes 393224 | tf_op jit(solution)/shard_map/ppermute | solution.py:31
  16.7 3.4 %collective-permute-start.11 = (bf16[4,128,128]{2,1,0:T(8,128)(2,1)S(1)}, bf16[4,128,128]{2,1,0:T(8,128)(2,1)S(1)}, u32[]{:S(2)}, u32[]{:S(2)}) collective-permute-start(bf16[4,128,128]{2,1,0:T(8,128)(2,1)S(1)} %collective-permute-done.8.refs_9_.refs_3_), channel_id=1, source_target_pairs={{0,1},{1,0},{2,3},{3,2},{4,5},{5,4},{6,7},{7,6},{8,9},{9,8},{10,11... | collective-permute-start | bytes 393224 | tf_op jit(solution)/shard_map/ppermute | solution.py:17
  16.7 5.0 %collective-permute-start.16 = (bf16[4,128,128]{2,1,0:T(8,128)(2,1)S(1)}, bf16[4,128,128]{2,1,0:T(8,128)(2,1)S(1)}, u32[]{:S(2)}, u32[]{:S(2)}) collective-permute-start(bf16[4,128,128]{2,1,0:T(8,128)(2,1)S(1)} %collective-permute-done.10.refs_11_), channel_id=1, source_target_pairs={{0,4},{1,3},{4,8},{5,1},{8,12},{9,5},{12,14},{13,9},{14,10},{15,13... | collective-permute-start | bytes 393224 | tf_op jit(solution)/shard_map/ppermute | solution.py:31
  18.3 3.4 %collective-permute-start.13 = (bf16[4,128,128]{2,1,0:T(8,128)(2,1)S(1)}, bf16[4,128,128]{2,1,0:T(8,128)(2,1)S(1)}, u32[]{:S(2)}, u32[]{:S(2)}) collective-permute-start(bf16[4,128,128]{2,1,0:T(8,128)(2,1)S(1)} %collective-permute-done.10.refs_11_), channel_id=1, source_target_pairs={{0,1},{1,0},{2,3},{3,2},{4,5},{5,4},{6,7},{7,6},{8,9},{9,8},{10,11... | collective-permute-start | bytes 393224 | tf_op jit(solution)/shard_map/ppermute | solution.py:17
  18.3 5.0 %collective-permute-start.21 = (bf16[4,128,128]{2,1,0:T(8,128)(2,1)S(1)}, bf16[4,128,128]{2,1,0:T(8,128)(2,1)S(1)}, u32[]{:S(2)}, u32[]{:S(2)}) collective-permute-start(bf16[4,128,128]{2,1,0:T(8,128)(2,1)S(1)} %collective-permute-done.15.refs_16_), channel_id=1, source_target_pairs={{0,4},{1,3},{4,8},{5,1},{8,12},{9,5},{12,14},{13,9},{14,10},{15,13... | collective-permute-start | bytes 393224 | tf_op jit(solution)/shard_map/ppermute | solution.py:31
  20.1 6.7 %collective-permute-start.18 = (bf16[4,128,128]{2,1,0:T(8,128)(2,1)S(1)}, bf16[4,128,128]{2,1,0:T(8,128)(2,1)S(1)}, u32[]{:S(2)}, u32[]{:S(2)}) collective-permute-start(bf16[4,128,128]{2,1,0:T(8,128)(2,1)S(1)} %collective-permute-done.15.refs_16_), channel_id=1, source_target_pairs={{0,1},{1,0},{2,3},{3,2},{4,5},{5,4},{6,7},{7,6},{8,9},{9,8},{10,11... | collective-permute-start | bytes 393224 | tf_op jit(solution)/shard_map/ppermute | solution.py:17
  20.1 6.7 %collective-permute-start.20 = (bf16[4,128,128]{2,1,0:T(8,128)(2,1)S(1)}, bf16[4,128,128]{2,1,0:T(8,128)(2,1)S(1)}, u32[]{:S(2)}, u32[]{:S(2)}) collective-permute-start(bf16[4,128,128]{2,1,0:T(8,128)(2,1)S(1)} %collective-permute-done.14.refs_15_.refs_5_), channel_id=1, source_target_pairs={{0,4},{1,3},{4,8},{5,1},{8,12},{9,5},{12,14},{13,9},{14,10},{15,13... | collective-permute-start | bytes 393224 | tf_op jit(solution)/shard_map/ppermute | solution.py:31
  21.7 5.1 %collective-permute-start.17 = (bf16[4,128,128]{2,1,0:T(8,128)(2,1)S(1)}, bf16[4,128,128]{2,1,0:T(8,128)(2,1)S(1)}, u32[]{:S(2)}, u32[]{:S(2)}) collective-permute-start(bf16[4,128,128]{2,1,0:T(8,128)(2,1)S(1)} %collective-permute-done.14.refs_15_.refs_5_), channel_id=1, source_target_pairs={{0,1},{1,0},{2,3},{3,2},{4,5},{5,4},{6,7},{7,6},{8,9},{9,8},{10,11... | collective-permute-start | bytes 393224 | tf_op jit(solution)/shard_map/ppermute | solution.py:17
  21.7 5.1 %collective-permute-start.22 = (bf16[4,128,128]{2,1,0:T(8,128)(2,1)S(1)}, bf16[4,128,128]{2,1,0:T(8,128)(2,1)S(1)}, u32[]{:S(2)}, u32[]{:S(2)}) collective-permute-start(bf16[4,128,128]{2,1,0:T(8,128)(2,1)S(1)} %collective-permute-done.16.refs_17_), channel_id=1, source_target_pairs={{0,4},{1,3},{4,8},{5,1},{8,12},{9,5},{12,14},{13,9},{14,10},{15,13... | collective-permute-start | bytes 393224 | tf_op jit(solution)/shard_map/ppermute | solution.py:31
  23.3 3.5 %collective-permute-start.19 = (bf16[4,128,128]{2,1,0:T(8,128)(2,1)S(1)}, bf16[4,128,128]{2,1,0:T(8,128)(2,1)S(1)}, u32[]{:S(2)}, u32[]{:S(2)}) collective-permute-start(bf16[4,128,128]{2,1,0:T(8,128)(2,1)S(1)} %collective-permute-done.16.refs_17_), channel_id=1, source_target_pairs={{0,1},{1,0},{2,3},{3,2},{4,5},{5,4},{6,7},{7,6},{8,9},{9,8},{10,11... | collective-permute-start | bytes 393224 | tf_op jit(solution)/shard_map/ppermute | solution.py:17
  39.8 1.7 %collective-permute-start.23 = (bf16[1040,128]{1,0:T(8,128)(2,1)S(1)}, bf16[1040,128]{1,0:T(8,128)(2,1)S(1)}, u32[]{:S(2)}, u32[]{:S(2)}) collective-permute-start(bf16[1040,128]{1,0:T(8,128)(2,1)S(1)} %get-tuple-element.34), channel_id=1, source_target_pairs={{0,1},{1,0},{2,3},{3,2},{4,5},{5,4},{6,7},{7,6},{8,9},{9,8},{10,11... | collective-permute-start | bytes 798728 | tf_op jit(solution)/shard_map/ppermute | solution.py:17
  40.3 9.0 %collective-permute-start.24 = (bf16[1024,128]{1,0:T(8,128)(2,1)S(1)}, bf16[1024,128]{1,0:T(8,128)(2,1)S(1)}, u32[]{:S(2)}, u32[]{:S(2)}) collective-permute-start(bf16[1024,128]{1,0:T(8,128)(2,1)S(1)} %get-tuple-element.36), channel_id=1, source_target_pairs={{0,1},{1,0},{2,3},{3,2},{4,5},{5,4},{6,7},{7,6},{8,9},{9,8},{10,11... | collective-permute-start | bytes 786440 | tf_op jit(solution)/shard_map/ppermute | solution.py:17
  41.5 9.5 %collective-permute-start.25 = (bf16[272,128]{1,0:T(8,128)(2,1)S(1)}, bf16[272,128]{1,0:T(8,128)(2,1)S(1)}, u32[]{:S(2)}, u32[]{:S(2)}) collective-permute-start(bf16[272,128]{1,0:T(8,128)(2,1)S(1)} %get-tuple-element.38), channel_id=1, source_target_pairs={{0,14},{1,15},{2,12},{3,13},{4,10},{5,11},{6,8},{7,9},{8,6},{9,7},... | collective-permute-start | bytes 208904 | tf_op jit(solution)/shard_map/ppermute | solution.py:17
  45.6 6.9 %collective-permute-start.26 = (bf16[272,128]{1,0:T(8,128)(2,1)S(1)}, bf16[272,128]{1,0:T(8,128)(2,1)S(1)}, u32[]{:S(2)}, u32[]{:S(2)}) collective-permute-start(bf16[272,128]{1,0:T(8,128)(2,1)S(1)} %get-tuple-element.39), channel_id=1, source_target_pairs={{0,12},{1,13},{2,14},{3,15},{4,8},{5,9},{6,10},{7,11},{8,4},{9,5},... | collective-permute-start | bytes 208904 | tf_op jit(solution)/shard_map/ppermute | solution.py:17
  46.0 11.5 %collective-permute-start.27 = (bf16[272,128]{1,0:T(8,128)(2,1)S(1)}, bf16[272,128]{1,0:T(8,128)(2,1)S(1)}, u32[]{:S(2)}, u32[]{:S(2)}) collective-permute-start(bf16[272,128]{1,0:T(8,128)(2,1)S(1)} %get-tuple-element.40), channel_id=1, source_target_pairs={{0,10},{1,11},{2,8},{3,9},{4,14},{5,15},{6,12},{7,13},{8,2},{9,3},... | collective-permute-start | bytes 208904 | tf_op jit(solution)/shard_map/ppermute | solution.py:17
  46.9 11.1 %collective-permute-start.28 = (bf16[272,128]{1,0:T(8,128)(2,1)S(1)}, bf16[272,128]{1,0:T(8,128)(2,1)S(1)}, u32[]{:S(2)}, u32[]{:S(2)}) collective-permute-start(bf16[272,128]{1,0:T(8,128)(2,1)S(1)} %get-tuple-element.41), channel_id=1, source_target_pairs={{0,8},{1,9},{2,10},{3,11},{4,12},{5,13},{6,14},{7,15},{8,0},{9,1},... | collective-permute-start | bytes 208904 | tf_op jit(solution)/shard_map/ppermute | solution.py:17
  49.3 8.6 %collective-permute-start.29 = (bf16[272,128]{1,0:T(8,128)(2,1)S(1)}, bf16[272,128]{1,0:T(8,128)(2,1)S(1)}, u32[]{:S(2)}, u32[]{:S(2)}) collective-permute-start(bf16[272,128]{1,0:T(8,128)(2,1)S(1)} %get-tuple-element.42), channel_id=1, source_target_pairs={{0,6},{1,7},{2,4},{3,5},{4,2},{5,3},{6,0},{7,1},{8,14},{9,15},{10,... | collective-permute-start | bytes 208904 | tf_op jit(solution)/shard_map/ppermute | solution.py:17
  51.0 6.9 %collective-permute-start.30 = (bf16[272,128]{1,0:T(8,128)(2,1)S(1)}, bf16[272,128]{1,0:T(8,128)(2,1)S(1)}, u32[]{:S(2)}, u32[]{:S(2)}) collective-permute-start(bf16[272,128]{1,0:T(8,128)(2,1)S(1)} %get-tuple-element.43), channel_id=1, source_target_pairs={{0,4},{1,5},{2,6},{3,7},{4,0},{5,1},{6,2},{7,3},{8,12},{9,13},{10,... | collective-permute-start | bytes 208904 | tf_op jit(solution)/shard_map/ppermute | solution.py:17
  52.5 5.5 %collective-permute-start.31 = (bf16[272,128]{1,0:T(8,128)(2,1)S(1)}, bf16[272,128]{1,0:T(8,128)(2,1)S(1)}, u32[]{:S(2)}, u32[]{:S(2)}) collective-permute-start(bf16[272,128]{1,0:T(8,128)(2,1)S(1)} %get-tuple-element.44), channel_id=1, source_target_pairs={{0,2},{1,3},{2,0},{3,1},{4,6},{5,7},{6,4},{7,5},{8,10},{9,11},{10,... | collective-permute-start | bytes 208904 | tf_op jit(solution)/shard_map/ppermute | solution.py:17
